TPU v7x, 32 devices: a whole 2x2x4 slice. The times are simulated.
32 devices in a mesh: dp: 4 (over z), row: 4 (over y, core), col: 2 (over x).
Axes of the slice: x: 2, y: 2, z: 4, core: 2. Of those that a mesh axis runs over, the one named last changes fastest.
Arguments:
- tokens: bfloat16 [768, 4096], P('dp', ('row', 'col')), may hold values from -6 to 6
- in_weight: bfloat16 [4096, 3, 4096], P('dp', None, ('row', 'col')), may hold values from -0.09375 to 0.09375
- short_filter: float32 [3, 3, 4096], P(None, None, ('row', 'col')), may hold values from -3 to 3
- long_filter: bfloat16 [256, 128], P(('row', 'col')), may hold values from -0.59765625 to 0.59765625
- grad_out: bfloat16 [768, 4096], P('dp', ('row', 'col')), may hold values from -6 to 6
Outputs:
- mixed: bfloat16 [768, 4096], P('dp', ('row', 'col'))
- grad_in: bfloat16 [768, 4096], P('dp', ('row', 'col'))
- grad_weight: float32 [4096, 3, 4096], P('dp', None, ('row', 'col'))
- grad_long: float32 [256, 128], P(('row', 'col'))
- grad_short: float32 [3, 3, 4096], P(None, None, ('row', 'col'))
All inputs are finite; a program needn't handle non-finite values.
Results may differ from a plain program's by a relative error of at most 0.019.
Values may be sent and summed in bfloat16 or wider, within the bound.
No kernel may reach another device: no remote copies, remote signals or barrier semaphores. Data moves between devices by JAX's collectives and lax.ppermute only.
A program may use at most 128 MiB of HBM per device.

v0:
```python
import jax
import jax.numpy as jnp
from jax import lax
from jax.sharding import PartitionSpec as P


def from_behind(block, axis, distance):
    devices = range(lax.axis_size(axis))
    route = [(i - distance, i) for i in devices if i - distance in devices]
    return lax.ppermute(block, axis, route)


def toeplitz(leading, rows, span):
    groups = leading.shape[0]
    width = rows + span
    seed_row = jnp.concatenate(
        [leading, jnp.zeros((groups, width - leading.shape[1]), leading.dtype)], axis=1
    )
    tiled = jnp.tile(seed_row, (1, rows))
    skewed = tiled[:, : rows * (width - 1)].reshape(groups, rows, width - 1)
    return skewed[:, :, :span]


def to_groups(values, ngroups, members):
    count = values.shape[0]
    return values.reshape(count, ngroups, members).transpose(1, 2, 0)


def from_groups(values):
    groups, members, count = values.shape
    return values.transpose(2, 0, 1).reshape(count, groups * members)


def per_device(tokens, in_weight, short_filter, long_filter, grad_out):
    rows = tokens.shape[0]
    local = grad_out.shape[1]
    nshort = short_filter.shape[0]
    ntaps = long_filter.shape[1]
    ngroups = long_filter.shape[0]
    members = local // ngroups
    margin = ntaps - 1
    span = rows + margin
    scale = float(rows * lax.axis_size("dp")) ** (-0.5)
    whole = lax.all_gather(tokens, ("row", "col"), axis=1, tiled=True)
    full_w = lax.all_gather(in_weight, "dp", axis=0, tiled=True)
    mixed_in = jnp.einsum("sd,dic->sic", whole, full_w, preferred_element_type=jnp.float32).astype(
        jnp.bfloat16
    )
    before = from_behind(mixed_in[rows - margin - nshort + 1 :], "dp", 1)
    extended = jnp.concatenate([before, mixed_in], axis=0).astype(jnp.float32)
    long_feats = jnp.zeros((span, 3, local), jnp.float32)
    for j in range(nshort):
        long_feats = (
            long_feats + short_filter[j][None] * extended[nshort - 1 - j : nshort - 1 - j + span]
        )
    product_ext = (long_feats[:, 1] * long_feats[:, 2]).astype(jnp.bfloat16)
    feats = long_feats[margin:]
    short_rows = extended[margin:]
    product_cols = to_groups(product_ext, ngroups, members)
    causal = toeplitz(long_filter[:, ::-1], rows, span)
    conv = from_groups(
        jnp.einsum("gst,gct->gcs", causal, product_cols, preferred_element_type=jnp.float32)
    )
    mixed = (feats[:, 0] * conv).astype(jnp.bfloat16)
    upstream = grad_out.astype(jnp.float32)
    grad_query = upstream * conv
    grad_conv = (upstream * feats[:, 0]).astype(jnp.bfloat16)
    after = from_behind(grad_conv[:margin], "dp", -1)
    grad_ext = jnp.concatenate([grad_conv, after], axis=0)
    anti = toeplitz(long_filter, rows, span)
    grad_product = from_groups(
        jnp.einsum(
            "gst,gct->gcs",
            anti,
            to_groups(grad_ext, ngroups, members),
            preferred_element_type=jnp.float32,
        )
    )
    reversed_cols = jnp.concatenate(
        [product_cols[:, :, ::-1], jnp.zeros((ngroups, members, rows), product_cols.dtype)], axis=2
    )
    width = span + rows
    pairs = jnp.einsum(
        "gcs,gcu->gsu",
        to_groups(grad_conv, ngroups, members),
        reversed_cols,
        preferred_element_type=jnp.float32,
    )
    diagonal = pairs.reshape(ngroups, rows * width)[:, : rows * (width - 1)].reshape(
        ngroups, rows, width - 1
    )
    filter_part = jnp.sum(diagonal[:, :, rows - 1 : rows - 1 + ntaps], axis=1)
    grad_feats = jnp.stack(
        [grad_query, grad_product * feats[:, 2], grad_product * feats[:, 1]], axis=1
    )
    later = from_behind(grad_feats[: nshort - 1], "dp", -1)
    feats_ext = jnp.concatenate([grad_feats, later], axis=0)
    grad_acc = jnp.zeros((rows, 3, local), jnp.float32)
    for j in range(nshort):
        grad_acc = grad_acc + short_filter[j][None] * feats_ext[j : j + rows]
    grad_mixed = grad_acc.astype(jnp.bfloat16)
    short_part = jnp.stack(
        [
            jnp.sum(grad_feats * short_rows[nshort - 1 - j : nshort - 1 - j + rows], axis=0)
            for j in range(nshort)
        ]
    )
    filter_total, short_total = (
        lax.psum(filter_part.astype(jnp.bfloat16), "dp").astype(jnp.float32),
        lax.psum(short_part.astype(jnp.bfloat16), "dp").astype(jnp.float32),
    )
    grad_long = filter_total * scale
    grad_short = short_total * scale
    partial_in = jnp.einsum("sic,dic->sd", grad_mixed, full_w, preferred_element_type=jnp.float32)
    summed_in = lax.psum_scatter(
        partial_in.astype(jnp.bfloat16), ("row", "col"), scatter_dimension=1, tiled=True
    )
    weight_term = (
        jnp.einsum("sd,sic->dic", whole, grad_mixed, preferred_element_type=jnp.float32) * scale
    )
    grad_weight = lax.psum_scatter(
        weight_term.astype(jnp.bfloat16), "dp", scatter_dimension=0, tiled=True
    ).astype(jnp.float32)
    return (mixed, summed_in, grad_weight, grad_long, grad_short)


def solution(mesh):
    placed = (
        P("dp", ("row", "col")),
        P("dp", None, ("row", "col")),
        P(None, None, ("row", "col")),
        P(("row", "col"), None),
        P("dp", ("row", "col")),
    )
    return jax.shard_map(
        per_device,
        mesh=mesh,
        in_specs=placed,
        out_specs=(
            P("dp", ("row", "col")),
            P("dp", ("row", "col")),
            P("dp", None, ("row", "col")),
            P(("row", "col"), None),
            P(None, None, ("row", "col")),
        ),
        check_vma=False,
    )
```

profile of v0, /device:TPU:1, one launch (start us, length us, event | category | flops | bytes accessed | tf_op | source)
XLA Modules:
  0.0 635.3 jit_solution(2712296209382541438)
XLA Ops:
  8.7 29.6 %all-gather.3.cloned.1.call-done = bf16[192,4096]{1,0:T(8,128)(2,1)} async-done(((bf16[192,512]{1,0:T(8,128)(2,1)}), bf16[192,4096]{1,0:T(8,128)(2,1)}) %all-gather.3.cloned.1.call-update) | async-done | bytes 1572880 | tf_op jit(solution)/shard_map/all_gather | solution.py:44
  38.3 219.6 %all-gather.5.cloned.1.call-done = bf16[4096,3,512]{2,0,1:T(8,128)(2,1)} async-done(((bf16[1024,3,512]{2,0,1:T(8,128)(2,1)}), bf16[4096,3,512]{2,0,1:T(8,128)(2,1)}) %all-gather.5.cloned.1.call-update) | async-done | bytes 12582928 | tf_op jit(solution)/shard_map/all_gather | solution.py:45
  257.9 7.7 %fusion.11 = bf16[192,3,512]{2,0,1:T(8,128)(2,1)S(1)} fusion(bf16[4096,3,512]{2,0,1:T(8,128)(2,1)} %all-gather.5.cloned.1.call-done, bf16[192,4096]{1,0:T(8,128)(2,1)} %all-gather.3.cloned.1.call-done), kind=kOutput, calls=%fused_computation.17 | convolution fusion | flops 2416214016 | bytes 14745600 | tf_op jit(solution)/shard_map/sd,dic->sic/dot_general | solution.py:46
  267.1 3.2 tile.8
  270.3 11.6 %tile.9 = bf16[32,98112]{1,0:T(8,128)(2,1)} reshape(bf16[32,192,511]{2,1,0:T(8,128)(2,1)} %tile.8) | data formatting | bytes 12558336 | tf_op jit(solution)/shard_map/tile | solution.py:19
  281.9 5.8 slice.119
  287.7 15.3 %reshape.49 = bf16[32,192,510]{2,1,0:T(8,128)(2,1)} reshape(bf16[32,97920]{1,0:T(8,128)(2,1)} %slice.119) | data formatting | bytes 12533760 | tf_op jit(solution)/shard_map/reshape | solution.py:20
  305.5 4.1 fusion.4
  317.2 11.6 %tile.21 = bf16[32,98112]{1,0:T(8,128)(2,1)} reshape(bf16[32,192,511]{2,1,0:T(8,128)(2,1)} %tile.20) | data formatting | bytes 12558336 | tf_op jit(solution)/shard_map/tile | solution.py:19
  328.8 5.8 slice.122
  334.6 15.3 %reshape.52 = bf16[32,192,510]{2,1,0:T(8,128)(2,1)} reshape(bf16[32,97920]{1,0:T(8,128)(2,1)} %slice.122) | data formatting | bytes 12533760 | tf_op jit(solution)/shard_map/reshape | solution.py:20
  350.9 4.2 fusion.2
  358.8 3.8 collective-permute-done.2
  364.3 6.4 %fusion = bf16[4096,3,512]{0,2,1:T(8,128)(2,1)} fusion(bf16[192,3,512]{2,0,1:T(8,128)(2,1)S(1)} %get-tuple-element.24, bf16[192,4096]{1,0:T(8,128)(2,1)S(1)} %copy-done.6), kind=kOutput, calls=%fused_computation.1 | convolution fusion | flops 2428502016 | bytes 14745600 | tf_op jit(solution)/shard_map/sd,sic->dic/dot_general | solution.py:119
  371.8 10.0 %fusion.1 = bf16[192,4096]{1,0:T(8,128)(2,1)} fusion(bf16[192,3,512]{2,0,1:T(8,128)(2,1)S(1)} %copy-done.2, bf16[4096,3,512]{2,0,1:T(8,128)(2,1)} %all-gather.5.cloned.1.call-done), kind=kOutput, calls=%fused_computation.3 | convolution fusion | flops 2416705536 | bytes 14745600 | tf_op jit(solution)/shard_map/sic,dic->sd/dot_general | solution.py:114
  382.6 6.3 fusion.21
  388.9 12.6 %reshape.55 = f32[32,98112]{1,0:T(8,128)} reshape(f32[32,192,511]{2,1,0:T(8,128)} %fusion.21) | data formatting | bytes 25116672 | tf_op jit(solution)/shard_map/reshape | solution.py:89
  401.5 9.8 %slice.129 = f32[32,97920]{1,0:T(8,128)} slice(f32[32,98112]{1,0:T(8,128)} %reshape.55), slice={[0:32], [0:97920]} | slice | bytes 25067520 | tf_op jit(solution)/shard_map/slice | solution.py:89
  411.3 14.9 %reshape.56 = f32[32,192,510]{2,1,0:T(8,128)} reshape(f32[32,97920]{1,0:T(8,128)} %slice.129) | data formatting | bytes 25067520 | tf_op jit(solution)/shard_map/reshape | solution.py:89
  426.2 3.7 slice_reduce_fusion
  430.0 19.7 %all-reduce.3 = (bf16[32,128]{1,0:T(8,128)(2,1)S(1)}, bf16[3,3,512]{2,1,0:T(4,128)(2,1)S(1)}) all-reduce(bf16[32,128]{1,0:T(8,128)(2,1)S(1)} %slice_reduce_fusion, bf16[3,3,512]{2,1,0:T(4,128)(2,1)S(1)} %pad_maximum_fusion.3), channel_id=1, replica_groups=mesh['dp'=4,'row'=4,'col'=2] {'dp'}, use_global_device_ids=true, to_apply=%region_3.0 | all-reduce | flops 8704 | bytes 34816 | tf_op jit(solution)/shard_map/psum | solution.py:109
  450.9 134.7 %reduce-scatter.5.cloned.1.call-done = bf16[1024,3,512]{0,2,1:T(8,128)(2,1)} async-done(((bf16[4096,3,512]{0,2,1:T(8,128)(2,1)}), bf16[1024,3,512]{0,2,1:T(8,128)(2,1)}) %reduce-scatter.5.cloned.1.call-update) | async-done | bytes 3145744 | tf_op jit(solution)/shard_map/reduce_scatter | solution.py:121
  585.6 5.4 copy.23
  591.0 37.8 %reduce-scatter.3.cloned.1.call-done = bf16[192,512]{1,0:T(8,128)(2,1)} async-done(((bf16[192,4096]{1,0:T(8,128)(2,1)}), bf16[192,512]{1,0:T(8,128)(2,1)}) %reduce-scatter.3.cloned.1.call-update) | async-done | bytes 196624 | tf_op jit(solution)/shard_map/reduce_scatter | solution.py:115
  (54 shorter events, 22.5 us)
Async XLA Ops:
  7.2 31.1 %all-gather.3.cloned.1.call-start = ((), (), s32[]{:S(2)}) async-start(), calls=%async_computation.2 | async-start | bytes 1769472 | tf_op jit(solution)/shard_map/all_gather | solution.py:44
  7.9 250.0 %all-gather.5.cloned.1.call-start = ((), (), s32[]{:S(2)}) async-start(), calls=%async_computation.3 | async-start | bytes 15728640 | tf_op jit(solution)/shard_map/all_gather | solution.py:45
  8.6 258.3 %copy-start.4 = (bf16[32,128]{1,0:T(8,128)(2,1)S(1)}, bf16[32,128]{1,0:T(8,128)(2,1)}, u32[]{:S(2)}) copy-start(bf16[32,128]{1,0:T(8,128)(2,1)} %param.8) | copy-start | bytes 24580
  8.7 577.0 %reduce-scatter.5.cloned.1.call-start = ((), (), s32[]{:S(2)}) async-start(), calls=%async_computation.5 | async-start | bytes 15728640 | tf_op jit(solution)/shard_map/reduce_scatter | solution.py:121
  265.7 37.4 %collective-permute-start = (bf16[129,3,512]{2,0,1:T(8,128)(2,1)S(1)}, bf16[129,3,512]{2,0,1:T(8,128)(2,1)S(1)}, u32[]{:S(2)}, u32[]{:S(2)}) collective-permute-start(bf16[129,3,512]{2,0,1:T(8,128)(2,1)S(1)} %slice.112), channel_id=1, source_target_pairs={{0,8},{8,16},{16,24},{1,9},{9,17},{17,25},{2,10},{10,18},{18,26},{... | collective-permute-start | bytes 1188872 | tf_op jit(solution)/shard_map/ppermute | solution.py:10
  287.7 15.3 %copy-start.5 = (f32[3,3,512]{2,1,0:T(4,128)S(1)}, f32[3,3,512]{2,1,0:T(4,128)}, u32[]{:S(2)}) copy-start(f32[3,3,512]{2,1,0:T(4,128)} %param.7) | copy-start | bytes 55300
  303.9 1.3 copy-start
  305.5 5.1 copy-start.3
  312.5 37.4 %collective-permute-start.1 = (bf16[127,512]{1,0:T(8,128)(2,1)S(1)}, bf16[127,512]{1,0:T(8,128)(2,1)S(1)}, u32[]{:S(2)}, u32[]{:S(2)}) collective-permute-start(bf16[127,512]{1,0:T(8,128)(2,1)S(1)} %slice.121), channel_id=1, source_target_pairs={{8,0},{16,8},{24,16},{9,1},{17,9},{25,17},{10,2},{18,10},{26,18},{... | collective-permute-start | bytes 390152 | tf_op jit(solution)/shard_map/ppermute | solution.py:10
  357.5 5.1 collective-permute-start.2
  362.7 1.6 copy-start.6
  363.5 0.8 copy-start.1
  370.7 1.1 copy-start.2
  370.8 258.0 %reduce-scatter.3.cloned.1.call-start = ((), (), s32[]{:S(2)}) async-start(), calls=%async_computation.4 | async-start | bytes 1769472 | tf_op jit(solution)/shard_map/reduce_scatter | solution.py:115
Sparse Core Ops, SparseCore 0:
  9.9 28.3 all-gather.2
  39.9 217.9 all-gather.4
  370.9 214.6 reduce-scatter.4
  589.3 39.3 reduce-scatter.2
where the time goes:
time: 637 us; the launch traced here: 635 us
  waiting for transfers between devices  427 us (67%)
  local copies, waits for them, and re-layouts  121 us (19%)
  matrix products  38.6 us (6%)
  blocking collectives  19.7 us (3%)
  between operations  14 us (2%)
  other arithmetic  10.2 us (2%)
    all_gather x1, waiting for transfers between devices, per_device(): full_w = lax.all_gather(in_weight, 'dp', axis=0, tiled=True)  220 us
    reduce_scatter x1, waiting for transfers between devices, per_device(): lax.psum_scatter(weight_term.astype(jnp.bfloat16), 'dp', scatter_dimensio...  135 us
    reduce_scatter x1, waiting for transfers between devices, per_device(): lax.psum_scatter(partial_in.astype(jnp.bfloat16), ('row', 'col'), scatter...  37.8 us
    reshape x2, local copies, waits for them, and re-layouts, toeplitz(): skewed = tiled[:, :rows * (width - 1)].reshape(groups, rows, width - 1)  30.6 us
    all_gather x1, waiting for transfers between devices, per_device(): whole = lax.all_gather(tokens, ('row', 'col'), axis=1, tiled=True)  29.6 us
    another operation x4, local copies, waits for them, and re-layouts, toeplitz(): tiled = jnp.tile(seed_row, (1, rows))  29.6 us
    reshape x2, local copies, waits for them, and re-layouts, per_device(): pairs.reshape(ngroups, rows * width)[:, :rows * (width - 1)]  27.5 us
    psum x1, blocking collectives, per_device(): lax.psum(filter_part.astype(jnp.bfloat16), 'dp').astype(jnp.float32)  19.7 us
  transfers between devices with their start and end apart: 7, of which 5 were waited for; matrix products, arithmetic and copies ran while one was open for 22% of the time, Pallas kernels for 0%

commit v1 on v0

--- a/solution.py
+++ b/solution.py
@@ -1,7 +1,270 @@
+import functools
+
 import jax
 import jax.numpy as jnp
 from jax import lax
+from jax.experimental import pallas as pl
+from jax.experimental.pallas import tpu as pltpu
 from jax.sharding import PartitionSpec as P
+
+VMEM_BYTES = 48 * 2**20
+F32 = jnp.float32
+BF16 = jnp.bfloat16
+
+
+def kernel_call(body, outs, grid=None, in_specs=None, out_specs=None, flops=0, nbytes=0):
+    kwargs = {}
+    if grid is not None:
+        kwargs = dict(grid=grid, in_specs=in_specs, out_specs=out_specs)
+    return pl.pallas_call(
+        body,
+        out_shape=outs,
+        compiler_params=pltpu.CompilerParams(vmem_limit_bytes=VMEM_BYTES),
+        cost_estimate=pl.CostEstimate(flops=flops, bytes_accessed=nbytes, transcendentals=0),
+        **kwargs,
+    )
+
+
+def shaped(shape, dtype):
+    return jax.ShapeDtypeStruct(shape, dtype)
+
+
+def bands_body(base_ref, out_ref):
+    groups, wide = base_ref.shape
+    rows = out_ref.shape[1]
+    row = lax.broadcasted_iota(jnp.int32, (8, wide), 0)
+    for g in range(groups):
+        band = jnp.broadcast_to(base_ref[g : g + 1, :], (8, wide))
+        for bit in (1, 2, 4):
+            band = jnp.where((row & bit) != 0, pltpu.roll(band, bit, 1), band)
+        count = 8
+        while count < rows:
+            band = jnp.concatenate([band, pltpu.roll(band, count, 1)], axis=0)
+            count *= 2
+        out_ref[g] = band.astype(out_ref.dtype)
+
+
+def project_body(x_ref, w_ref, out_ref):
+    parts, pieces, rows, depth = x_ref.shape
+    owners, _, tokens, width = out_ref.shape
+    total = jnp.zeros((tokens, w_ref.shape[2]), F32)
+    for e in range(pieces):
+        total += jnp.dot(
+            x_ref[:, e].reshape(tokens, depth),
+            w_ref[0, e * depth : (e + 1) * depth],
+            preferred_element_type=F32,
+        )
+    for z in range(owners):
+        out_ref[z, 0] = total[:, z * width : (z + 1) * width].astype(BF16)
+
+
+def input_grad_body(gm_ref, w_ref, out_ref):
+    parts, _, rows, depth = out_ref.shape
+    owners = gm_ref.shape[0]
+    tokens = parts * rows
+    total = jnp.zeros((tokens, depth), F32)
+    for i in range(w_ref.shape[0]):
+        gm = jnp.concatenate([gm_ref[z, i * tokens : (i + 1) * tokens] for z in range(owners)], axis=1)
+        total += lax.dot_general(gm, w_ref[i], (((1,), (1,)), ((), ())), preferred_element_type=F32)
+    out_ref[:, 0] = total.reshape(parts, rows, depth).astype(BF16)
+
+
+def weight_grad_body(scale, x_ref, gm_ref, out_ref):
+    parts, _, rows, depth = x_ref.shape
+    owners, tokens, width = gm_ref.shape
+    gm = jnp.concatenate([gm_ref[z] for z in range(owners)], axis=1)
+    x = x_ref[:, 0].reshape(tokens, depth)
+    out_ref[0] = scale * lax.dot_general(x, gm, (((0,), (0,)), ((), ())), preferred_element_type=F32)
+
+
+def delayed(values, count):
+    row = lax.broadcasted_iota(jnp.int32, values.shape, 0)
+    return jnp.where(row >= count, pltpu.roll(values, count, 0), 0.0)
+
+
+def advanced(values, count):
+    rows = values.shape[0]
+    row = lax.broadcasted_iota(jnp.int32, values.shape, 0)
+    return jnp.where(row < rows - count, pltpu.roll(values, rows - count, 0), 0.0)
+
+
+def middle_body(scale, nshort, m_ref, sf_ref, causal_ref, anti_ref, go_ref, gm_ref, mixed_ref):
+    tokens, width = go_ref.shape
+    groups, block, span = causal_ref.shape
+    members = width // groups
+    nblocks = tokens // block
+    lane = lax.broadcasted_iota(jnp.int32, (block, width), 1) // members
+    lanes = lax.broadcasted_iota(jnp.int32, (block, 2 * width), 1) % width // members
+
+    def past(i, j):
+        held = m_ref[i * tokens : (i + 1) * tokens].astype(F32)
+        return held if j == 0 else delayed(held, j)
+
+    def taps(j, i):
+        return sf_ref[3 * j + i : 3 * j + i + 1, :]
+
+    feats = [sum(taps(j, i) * past(i, j) for j in range(nshort)) for i in range(3)]
+    product = (feats[1] * feats[2]).astype(BF16)
+    zero = jnp.zeros((block, width), BF16)
+    p_blocks = [zero] + [product[b * block : (b + 1) * block] for b in range(nblocks)]
+    p_pairs = [jnp.concatenate(p_blocks[b : b + 2], axis=0) for b in range(nblocks)]
+
+    def filtered(band_ref, pairs):
+        bands = band_ref[...].reshape(groups * block, span)
+        out = []
+        for b in range(0, nblocks, 2):
+            both = jnp.dot(bands, jnp.concatenate(pairs[b : b + 2], axis=1), preferred_element_type=F32)
+            for h in range(2):
+                part = both[:, h * width : (h + 1) * width]
+                picked = part[:block]
+                for g in range(1, groups):
+                    picked = jnp.where(lane == g, part[g * block : (g + 1) * block], picked)
+                out.append(picked)
+        return jnp.concatenate(out, axis=0)
+
+    conv = filtered(causal_ref, p_pairs)
+    upstream = go_ref[...].astype(F32)
+    mixed_ref[...] = (feats[0] * conv).astype(BF16)
+    grad_conv = (upstream * feats[0]).astype(BF16)
+    c_blocks = [grad_conv[b * block : (b + 1) * block] for b in range(nblocks)] + [zero]
+    c_pairs = [jnp.concatenate(c_blocks[b : b + 2], axis=0) for b in range(nblocks)]
+    grad_product = filtered(anti_ref, c_pairs)
+
+    corr = jnp.zeros((groups * block, span), F32)
+    for b in range(0, nblocks, 2):
+        left = jnp.concatenate(c_blocks[b : b + 2], axis=1)
+        stacked = jnp.concatenate(
+            [jnp.where(lanes == g, left, jnp.zeros_like(left)) for g in range(groups)], axis=0
+        )
+        right = jnp.concatenate(p_pairs[b : b + 2], axis=1)
+        corr += lax.dot_general(stacked, right, (((1,), (1,)), ((), ())), preferred_element_type=F32)
+    row = lax.broadcasted_iota(jnp.int32, (8, span), 0)
+    sums = []
+    for g in range(groups):
+        part = corr[g * block : (g + 1) * block]
+        count = block
+        while count > 8:
+            count //= 2
+            part = part[:count] + pltpu.roll(part[count:], span - count, 1)
+        for bit in (1, 2, 4):
+            part = jnp.where((row & bit) != 0, pltpu.roll(part, span - bit, 1), part)
+        sums.append(jnp.sum(part, axis=0, keepdims=True))
+    by_lag = jnp.concatenate(sums, axis=0)
+    by_lag = scale * pltpu.roll(by_lag, span - 1, 1)[:, :block]
+
+    grad_feats = [upstream * conv, grad_product * feats[2], grad_product * feats[1]]
+    short_rows = []
+    for j in range(nshort):
+        for i in range(3):
+            short_rows.append(scale * jnp.sum(grad_feats[i] * past(i, j), axis=0, keepdims=True))
+    for i in range(3):
+        total = taps(0, i) * grad_feats[i]
+        for j in range(1, nshort):
+            total += taps(j, i) * advanced(grad_feats[i], j)
+        gm_ref[i * tokens : (i + 1) * tokens] = total.astype(BF16)
+    tail = gm_ref.shape[0] - 3 * tokens - groups - 3 * nshort
+    small = jnp.concatenate([by_lag] + short_rows + [jnp.zeros((tail, width), F32)], axis=0)
+    gm_ref[3 * tokens :] = small.astype(BF16)
+
+
+def move_activations(tokens, in_weight, short_filter, long_filter, grad_out):
+    ndp, nrow, ncol = (lax.axis_size(a) for a in ("dp", "row", "col"))
+    z = lax.axis_index("dp")
+    rows, dcol = tokens.shape
+    local = grad_out.shape[1]
+    nshort = short_filter.shape[0]
+    ngroups, ntaps = long_filter.shape
+    seq = rows * ndp
+    width, groups = local // ndp, ngroups // ndp
+    drow = in_weight.shape[0]
+    scale = float(seq) ** -0.5
+    swap = [(a * nrow + b, b * nrow + a) for a in range(ndp) for b in range(nrow)]
+
+    w = jnp.transpose(in_weight, (1, 0, 2))
+    moved = lax.ppermute(tokens, ("dp", "row"), swap)
+    x = lax.all_gather(moved, ("row", "col"), axis=0).reshape(nrow, ncol, rows, dcol)
+    upstream = lax.all_to_all(grad_out, "dp", split_axis=1, concat_axis=0, tiled=True)
+
+    sf = lax.dynamic_slice_in_dim(short_filter, z * width, width, 2).reshape(3 * nshort, width)
+    lf = lax.dynamic_slice_in_dim(long_filter, z * groups, groups, 0).astype(F32)
+    zeros = functools.partial(jnp.zeros, dtype=F32)
+    bases = jnp.concatenate(
+        [
+            jnp.concatenate([zeros((groups, 1)), lf[:, ::-1], zeros((groups, ntaps - 1))], axis=1),
+            jnp.concatenate([lf, zeros((groups, ntaps))], axis=1),
+        ],
+        axis=0,
+    )
+    bands = kernel_call(bands_body, shaped((2 * groups, ntaps, 2 * ntaps), BF16))(bases)
+
+    mm_flops = 2 * seq * drow * 3 * local
+    partial = kernel_call(
+        project_body,
+        shaped((ndp, 3, seq, width), BF16),
+        grid=(3,),
+        in_specs=[
+            pl.BlockSpec((nrow, ncol, rows, dcol), lambda i: (0, 0, 0, 0)),
+            pl.BlockSpec((1, drow, local), lambda i: (i, 0, 0)),
+        ],
+        out_specs=pl.BlockSpec((ndp, 1, seq, width), lambda i: (0, i, 0, 0)),
+        flops=mm_flops,
+        nbytes=2 * (seq * drow + 3 * drow * local + 3 * seq * local),
+    )(x, w)
+    mixed_in = lax.psum_scatter(partial.reshape(ndp, 3 * seq, width), "dp", scatter_dimension=0)
+
+    extra = -(-(groups + 3 * nshort) // 16) * 16
+    half = pl.BlockSpec((groups, ntaps, 2 * ntaps), lambda i: (0, 0, 0))
+    other = pl.BlockSpec((groups, ntaps, 2 * ntaps), lambda i: (1, 0, 0))
+    whole = lambda shape: pl.BlockSpec(shape, lambda i: (0,) * len(shape))
+    gm_rows = 3 * seq + extra
+    grad_mixed, mixed = kernel_call(
+        functools.partial(middle_body, scale, nshort),
+        (shaped((gm_rows, width), BF16), shaped((seq, width), BF16)),
+        grid=(1,),
+        in_specs=[whole((3 * seq, width)), whole((3 * nshort, width)), half, other, whole((seq, width))],
+        out_specs=(whole((gm_rows, width)), whole((seq, width))),
+        flops=3 * 2 * groups * ntaps * 2 * ntaps * width * (seq // ntaps),
+        nbytes=2 * width * seq * 10,
+    )(mixed_in, sf, bands, bands, upstream)
+    gathered = lax.all_gather(grad_mixed, "dp", axis=0)
+    mixed = lax.all_to_all(mixed, "dp", split_axis=0, concat_axis=1, tiled=True)
+
+    partial_in = kernel_call(
+        input_grad_body,
+        shaped((nrow, ncol, rows, dcol), BF16),
+        grid=(ncol,),
+        in_specs=[
+            pl.BlockSpec((ndp, gm_rows, width), lambda e: (0, 0, 0)),
+            pl.BlockSpec((3, dcol, local), lambda e: (0, e, 0)),
+        ],
+        out_specs=pl.BlockSpec((nrow, 1, rows, dcol), lambda e: (0, e, 0, 0)),
+        flops=mm_flops,
+        nbytes=2 * (seq * drow + 3 * drow * local + 3 * seq * local),
+    )(gathered, w)
+    summed = lax.psum_scatter(
+        partial_in.reshape(nrow * ncol, rows, dcol), ("row", "col"), scatter_dimension=0
+    )
+    grad_in = lax.ppermute(summed, ("dp", "row"), swap)
+
+    grad_weight = kernel_call(
+        functools.partial(weight_grad_body, scale),
+        shaped((3, drow, local), F32),
+        grid=(3, ncol),
+        in_specs=[
+            pl.BlockSpec((nrow, 1, rows, dcol), lambda i, e: (0, e, 0, 0)),
+            pl.BlockSpec((ndp, seq, width), lambda i, e: (0, i, 0)),
+        ],
+        out_specs=pl.BlockSpec((1, dcol, local), lambda i, e: (i, e, 0)),
+        flops=mm_flops,
+        nbytes=2 * (seq * drow + 6 * drow * local + 3 * seq * local),
+    )(x, gathered)
+    grad_weight = jnp.transpose(grad_weight, (1, 0, 2))
+    small = gathered[:, 3 * seq :].astype(F32)
+    grad_long = small[:, :groups, ::-1].reshape(ngroups, ntaps)
+    grad_short = (
+        small[:, groups : groups + 3 * nshort].transpose(1, 0, 2).reshape(nshort, 3, local)
+    )
+    return (mixed, grad_in, grad_weight, grad_long, grad_short)
 
 
 def from_behind(block, axis, distance):
@@ -31,7 +294,7 @@
     return values.transpose(2, 0, 1).reshape(count, groups * members)
 
 
-def per_device(tokens, in_weight, short_filter, long_filter, grad_out):
+def move_weights(tokens, in_weight, short_filter, long_filter, grad_out):
     rows = tokens.shape[0]
     local = grad_out.shape[1]
     nshort = short_filter.shape[0]
@@ -124,6 +387,22 @@
     return (mixed, summed_in, grad_weight, grad_long, grad_short)
 
 
+def fits_whole_sequences(mesh, tokens, in_weight, short_filter, long_filter, grad_out):
+    ndp, nrow, ncol = (mesh.shape[a] for a in ("dp", "row", "col"))
+    seq, channels = grad_out.shape
+    groups, ntaps = long_filter.shape
+    local = channels // (nrow * ncol)
+    width, rows = local // ndp, seq // ndp
+    return (
+        seq < tokens.shape[1]
+        and ndp == nrow
+        and ntaps == width == 128
+        and seq % (2 * ntaps) == 0
+        and rows % 16 == 0
+        and groups % (8 * ndp * nrow * ncol) == 0
+    )
+
+
 def solution(mesh):
     placed = (
         P("dp", ("row", "col")),
@@ -132,16 +411,18 @@
         P(("row", "col"), None),
         P("dp", ("row", "col")),
     )
-    return jax.shard_map(
-        per_device,
-        mesh=mesh,
-        in_specs=placed,
-        out_specs=(
-            P("dp", ("row", "col")),
-            P("dp", ("row", "col")),
-            P("dp", None, ("row", "col")),
-            P(("row", "col"), None),
-            P(None, None, ("row", "col")),
-        ),
-        check_vma=False,
-    )
+    gives = (
+        P("dp", ("row", "col")),
+        P("dp", ("row", "col")),
+        P("dp", None, ("row", "col")),
+        P(("row", "col"), None),
+        P(None, None, ("row", "col")),
+    )
+
+    def run(*arrays):
+        plan = move_activations if fits_whole_sequences(mesh, *arrays) else move_weights
+        return jax.shard_map(
+            plan, mesh=mesh, in_specs=placed, out_specs=gives, check_vma=False
+        )(*arrays)
+
+    return run

time: 637 us -> 229 us (0.36)
  waiting for transfers between devices: 427 us -> 157 us
  local copies, waits for them, and re-layouts: 121 us -> 11.6 us
  matrix products: 38.6 us -> 0 us
  Pallas kernels: 0 us -> 20.4 us
  blocking collectives: 19.7 us -> 8.34 us
  other arithmetic: 10.2 us -> 0.78 us
  starting transfers between devices: 4.46 us -> 12.9 us
    all_gather x2, waiting for transfers between devices: 249 us -> 82.7 us  [the longest x1 49.7 us: move_activations(): gathered = lax.all_gather(grad_mixed, 'dp', axis=0)]
    reduce_scatter x2, waiting for transfers between devices: 173 us -> 59.8 us  [the longest x1 32.7 us: move_activations(): lax.psum_scatter(partial.reshape(ndp, 3 * seq, width), 'dp', scatter_dime...]
    reshape x6 -> x2, local copies, waits for them, and re-layouts: 60 us -> 0.64 us  [the longest x1 0.63 us: move_activations(): small[:, groups:groups + 3 * nshort].transpose(1, 0, 2)]
    dot_general x6 -> x0, matrix products: 38.6 us -> none  [the longest x1 9.96 us: per_device(): jnp.einsum('sic,dic->sd', grad_mixed, full_w, preferred_element_type=jnp....]
    another operation x4 -> x1, local copies, waits for them, and re-layouts: 29.6 us -> 0.01 us  [run(): jax.shard_map(plan, mesh=mesh, in_specs=placed, out_specs=gives, check_vm...]
    slice x6 -> x1, local copies, waits for them, and re-layouts: 21.6 us -> 0.01 us  [move_activations(): grad_long = small[:, :groups, ::-1].reshape(ngroups, ntaps)]
    pallas_call x0 -> x5, Pallas kernels: none -> 20.4 us  [the longest x1 6.11 us: move_activations(): kernel_call(functools.partial(weight_grad_body, scale), shaped((3, drow,...]
    psum x1 -> x0, blocking collectives: 19.7 us -> none  [per_device(): lax.psum(filter_part.astype(jnp.bfloat16), 'dp').astype(jnp.float32)]
  transfers between devices with their start and end apart: 7 -> 7, of which waited for: 5 -> 6; matrix products, arithmetic and copies ran while one was open for 22% -> 2% of each run, Pallas kernels for 0% -> 3%
where the time goes in v1:
time: 229 us; the launch traced here: 225 us
  waiting for transfers between devices  157 us (69%)
  Pallas kernels  20.4 us (9%)
  between operations  13.8 us (6%)
  starting transfers between devices  12.9 us (6%)
  local copies, waits for them, and re-layouts  11.6 us (5%)
  blocking collectives  8.34 us (4%)
    all_gather x1, waiting for transfers between devices, move_activations(): gathered = lax.all_gather(grad_mixed, 'dp', axis=0)  49.7 us
    all_gather x1, waiting for transfers between devices, move_activations(): lax.all_gather(moved, ('row', 'col'), axis=0)  33 us
    reduce_scatter x1, waiting for transfers between devices, move_activations(): lax.psum_scatter(partial.reshape(ndp, 3 * seq, width), 'dp', scatter_dime...  32.7 us
    reduce_scatter x1, waiting for transfers between devices, move_activations(): lax.psum_scatter(partial_in.reshape(nrow * ncol, rows, dcol), ('row', 'co...  27.1 us
    all_to_all x1, waiting for transfers between devices, move_activations(): lax.all_to_all(grad_out, 'dp', split_axis=1, concat_axis=0, tiled=True)  10.9 us
    all_to_all x1, blocking collectives, move_activations(): mixed = lax.all_to_all(mixed, 'dp', split_axis=0, concat_axis=1, tiled=True)  8.34 us
    unnamed x17, local copies, waits for them, and re-layouts  8.05 us
    pallas_call x1, Pallas kernels, move_activations(): kernel_call(functools.partial(weight_grad_body, scale), shaped((3, drow,...  6.11 us
  transfers between devices with their start and end apart: 7, of which 6 were waited for; matrix products, arithmetic and copies ran while one was open for 2% of the time, Pallas kernels for 3%

profile of v1, /device:TPU:1, one launch (start us, length us, event | category | flops | bytes accessed | tf_op | source)
XLA Modules:
  0.0 224.7 jit_solution(12855208199446682461)
XLA Ops:
  7.2 4.7 %collective-permute-start = (bf16[192,512]{1,0:T(8,128)(2,1)}, bf16[192,512]{1,0:T(8,128)(2,1)S(1)}, u32[]{:S(2)}, u32[]{:S(2)}) collective-permute-start(bf16[192,512]{1,0:T(8,128)(2,1)} %param.5), channel_id=1, source_target_pairs={{0,0},{2,8},{4,16},{6,24},{8,2},{10,10},{12,18},{14,26},{16,4},{18... | collective-permute-start | bytes 589832 | tf_op jit(solution)/shard_map/ppermute | solution.py:184
  12.0 3.5 %collective-permute-done = bf16[192,512]{1,0:T(8,128)(2,1)S(1)} collective-permute-done((bf16[192,512]{1,0:T(8,128)(2,1)}, bf16[192,512]{1,0:T(8,128)(2,1)S(1)}, u32[]{:S(2)}, u32[]{:S(2)}) %collective-permute-start) | collective-permute-done | bytes 196640 | tf_op jit(solution)/shard_map/ppermute | solution.py:184
  16.3 33.0 %all-gather.5.cloned.1.call-done = bf16[1536,512]{1,0:T(8,128)(2,1)} async-done(((bf16[192,512]{1,0:T(8,128)(2,1)}), bf16[1536,512]{1,0:T(8,128)(2,1)}) %all-gather.5.cloned.1.call-update) | async-done | bytes 1572880 | tf_op jit(solution)/shard_map/all_gather | solution.py:185
  49.3 1.4 copy-done.3
  50.7 5.6 %shard_map.92 = bf16[4,3,768,128]{3,2,1,0:T(8,128)(2,1)} custom-call(bf16[4,2,192,512]{3,2,1,0:T(8,128)(2,1)S(1)} %bitcast.29, bf16[3,1024,512]{2,1,0:T(8,128)(2,1)} %bitcast.37), custom_call_target="tpu_custom_call" | custom-call | flops 2415919104 | bytes 7077888 | tf_op jit(solution)/shard_map/pallas_call | solution.py:201
  56.3 0.7 copy_bitcast_fusion.1
  57.0 4.3 %all-to-all-start = ((bf16[192,4,128]{2,0,1:T(8,128)(2,1)}), bf16[192,4,128]{2,0,1:T(8,128)(2,1)S(1)}, u32[]{:S(2)}, u32[]{:S(2)}) async-start(bf16[192,4,128]{2,0,1:T(8,128)(2,1)} %copy_bitcast_fusion.1), calls=%async_computation.1 | async-start | bytes 393216 | tf_op jit(solution)/shard_map/all_to_all | solution.py:186
  61.3 0.7 constant_dynamic-slice_fusion
  62.0 0.7 dynamic-slice_convert_fusion
  63.5 10.9 %all-to-all-done = bf16[192,4,128]{2,0,1:T(8,128)(2,1)S(1)} async-done(((bf16[192,4,128]{2,0,1:T(8,128)(2,1)}), bf16[192,4,128]{2,0,1:T(8,128)(2,1)S(1)}, u32[]{:S(2)}, u32[]{:S(2)}) %all-to-all-start) | async-done | bytes 196640 | tf_op jit(solution)/shard_map/all_to_all | solution.py:186
  74.4 32.7 %reduce-scatter.3.cloned.1.call-done = bf16[1,2304,128]{2,1,0:T(8,128)(2,1)} async-done(((bf16[4,2304,128]{2,1,0:T(8,128)(2,1)}), bf16[1,2304,128]{2,1,0:T(8,128)(2,1)}) %reduce-scatter.3.cloned.1.call-update) | async-done | bytes 589840 | tf_op jit(solution)/shard_map/reduce_scatter | solution.py:213
  107.1 1.1 copy-done.6
  108.2 3.6 %shard_map.94 = (bf16[2336,128]{1,0:T(8,128)(2,1)}, bf16[768,128]{1,0:T(8,128)(2,1)S(1)}) custom-call(bf16[2304,128]{1,0:T(8,128)(2,1)S(1)} %bitcast.34, f32[9,128]{1,0:T(8,128)S(1)} %reshape.36.sf_ref, bf16[16,128,256]{2,1,0:T(8,128)(2,1)S(1)} %shard_map.93.causal_ref.anti_ref, bf16[16,128,256]{2,1,0:T(8,128)(2,1)S(1)} %shard_map.93.causal_ref.anti_ref, ...), custom_call_target="tpu_custom_call" | custom-call | flops 1207959552 | bytes 1966080 | tf_op jit(solution)/shard_map/pallas_call | solution.py:220
  111.8 49.7 %all-gather.7.cloned.1.call-done = bf16[9344,128]{1,0:T(8,128)(2,1)} async-done(((bf16[2336,128]{1,0:T(8,128)(2,1)}), bf16[9344,128]{1,0:T(8,128)(2,1)}) %all-gather.7.cloned.1.call-update) | async-done | bytes 2392080 | tf_op jit(solution)/shard_map/all_gather | solution.py:229
  161.5 1.7 copy-done.1
  163.2 4.5 %shard_map.95 = bf16[4,2,192,512]{3,2,1,0:T(8,128)(2,1)S(1)} custom-call(bf16[4,2336,128]{2,1,0:T(8,128)(2,1)S(1)} %bitcast.26, bf16[3,1024,512]{2,1,0:T(8,128)(2,1)} %bitcast.38), custom_call_target="tpu_custom_call" | custom-call | flops 2415919104 | bytes 7077888 | tf_op jit(solution)/shard_map/pallas_call | solution.py:232
  167.7 1.1 copy-done.5
  168.8 8.3 %all_to_all.38 = bf16[4,192,128]{2,1,0:T(8,128)(2,1)S(1)} all-to-all(bf16[4,192,128]{2,1,0:T(8,128)(2,1)S(1)} %bitcast.33), channel_id=1, replica_groups=mesh['dp'=4,'row'=4,'col'=2] {'dp'}, dimensions={0} | all-to-all | bytes 393216 | tf_op jit(solution)/shard_map/all_to_all | solution.py:230
  177.2 0.7 copy_bitcast_fusion
  177.9 0.7 rev.7
  179.2 27.1 %reduce-scatter.5.cloned.1.call-done = bf16[1,192,512]{2,1,0:T(8,128)(2,1)} async-done(((bf16[8,192,512]{2,1,0:T(8,128)(2,1)}), bf16[1,192,512]{2,1,0:T(8,128)(2,1)}) %reduce-scatter.5.cloned.1.call-update) | async-done | bytes 196624 | tf_op jit(solution)/shard_map/reduce_scatter | solution.py:244
  206.3 3.7 %collective-permute-start.1 = (bf16[192,512]{1,0:T(8,128)(2,1)}, bf16[192,512]{1,0:T(8,128)(2,1)S(1)}, u32[]{:S(2)}, u32[]{:S(2)}) collective-permute-start(bf16[192,512]{1,0:T(8,128)(2,1)} %bitcast.39), channel_id=1, source_target_pairs={{0,0},{2,8},{4,16},{6,24},{8,2},{10,10},{12,18},{14,26},{16,4},{18... | collective-permute-start | bytes 589832 | tf_op jit(solution)/shard_map/ppermute | solution.py:247
  210.0 1.4 copy-done.4
  211.4 6.1 %shard_map.96 = f32[3,1024,512]{2,1,0:T(8,128)} custom-call(bf16[4,2,192,512]{3,2,1,0:T(8,128)(2,1)S(1)} %bitcast.30, bf16[4,2336,128]{2,1,0:T(8,128)(2,1)S(1)} %bitcast.28), custom_call_target="tpu_custom_call" | custom-call | flops 2415919104 | bytes 10223616 | tf_op jit(solution)/shard_map/pallas_call | solution.py:249
  (32 shorter events, 3.0 us)
Async XLA Ops:
  7.2 49.1 %copy-start = (bf16[192,512]{1,0:T(8,128)(2,1)S(1)}, bf16[192,512]{1,0:T(8,128)(2,1)}, u32[]{:S(2)}) copy-start(bf16[192,512]{1,0:T(8,128)(2,1)} %param.9) | copy-start | bytes 589828
  7.2 42.1 %all-gather.5.cloned.1.call-start = ((), (), s32[]{:S(2)}) async-start(), calls=%async_computation.6 | async-start | bytes 1769472 | tf_op jit(solution)/shard_map/all_gather | solution.py:185
  7.2 8.3 %collective-permute-start = (bf16[192,512]{1,0:T(8,128)(2,1)}, bf16[192,512]{1,0:T(8,128)(2,1)S(1)}, u32[]{:S(2)}, u32[]{:S(2)}) collective-permute-start(bf16[192,512]{1,0:T(8,128)(2,1)} %param.5), channel_id=1, source_target_pairs={{0,0},{2,8},{4,16},{6,24},{8,2},{10,10},{12,18},{14,26},{16,4},{18... | collective-permute-start | bytes 589832 | tf_op jit(solution)/shard_map/ppermute | solution.py:184
  15.5 0.7 copy-start.7
  16.2 90.9 %reduce-scatter.3.cloned.1.call-start = ((), (), s32[]{:S(2)}) async-start(), calls=%async_computation.4 | async-start | bytes 2949120 | tf_op jit(solution)/shard_map/reduce_scatter | solution.py:213
  49.3 1.4 copy-start.3
  57.0 17.4 %all-to-all-start = ((bf16[192,4,128]{2,0,1:T(8,128)(2,1)}), bf16[192,4,128]{2,0,1:T(8,128)(2,1)S(1)}, u32[]{:S(2)}, u32[]{:S(2)}) async-start(bf16[192,4,128]{2,0,1:T(8,128)(2,1)} %copy_bitcast_fusion.1), calls=%async_computation.1 | async-start | bytes 393216 | tf_op jit(solution)/shard_map/all_to_all | solution.py:186
  61.3 100.2 %all-gather.7.cloned.1.call-start = ((), (), s32[]{:S(2)}) async-start(), calls=%async_computation.7 | async-start | bytes 2990080 | tf_op jit(solution)/shard_map/all_gather | solution.py:229
  107.1 1.1 copy-start.6
  111.8 94.5 %reduce-scatter.5.cloned.1.call-start = ((), (), s32[]{:S(2)}) async-start(), calls=%async_computation.5 | async-start | bytes 1769472 | tf_op jit(solution)/shard_map/reduce_scatter | solution.py:244
  161.5 1.7 copy-start.1
  163.2 14.7 %copy-start.2 = (bf16[9344,128]{1,0:T(8,128)(2,1)S(1)}, bf16[9344,128]{1,0:T(8,128)(2,1)}, u32[]{:S(2)}) copy-start(bf16[9344,128]{1,0:T(8,128)(2,1)} %all-gather.7.cloned.1.call-done) | copy-start | bytes 7176196
  167.7 1.1 copy-start.5
  206.3 11.2 %collective-permute-start.1 = (bf16[192,512]{1,0:T(8,128)(2,1)}, bf16[192,512]{1,0:T(8,128)(2,1)S(1)}, u32[]{:S(2)}, u32[]{:S(2)}) collective-permute-start(bf16[192,512]{1,0:T(8,128)(2,1)} %bitcast.39), channel_id=1, source_target_pairs={{0,0},{2,8},{4,16},{6,24},{8,2},{10,10},{12,18},{14,26},{16,4},{18... | collective-permute-start | bytes 589832 | tf_op jit(solution)/shard_map/ppermute | solution.py:247
  210.0 1.4 copy-start.4
Sparse Core Ops, SparseCore 0:
  16.3 32.8 all-gather.4
  56.4 50.6 reduce-scatter.2
  111.9 49.5 all-gather.6
  169.0 37.2 reduce-scatter.4

commit v2 on v1

--- a/solution.py
+++ b/solution.py
@@ -241,9 +241,10 @@
         flops=mm_flops,
         nbytes=2 * (seq * drow + 3 * drow * local + 3 * seq * local),
     )(gathered, w)
-    summed = lax.psum_scatter(
-        partial_in.reshape(nrow * ncol, rows, dcol), ("row", "col"), scatter_dimension=0
-    )
+    spread = lax.all_to_all(
+        partial_in.reshape(nrow * ncol, rows, dcol), ("row", "col"), split_axis=0, concat_axis=0, tiled=True
+    )
+    summed = jnp.sum(spread.astype(F32), axis=0).astype(BF16)
     grad_in = lax.ppermute(summed, ("dp", "row"), swap)
 
     grad_weight = kernel_call(

time: 229 us -> 215 us (0.939)
  waiting for transfers between devices: 157 us -> 145 us
  blocking collectives: 8.34 us -> 0 us
  starting transfers between devices: 12.9 us -> 19.2 us
    reduce_scatter x1 -> x0, waiting for transfers between devices: 27.1 us -> none  [move_activations(): lax.psum_scatter(partial_in.reshape(nrow * ncol, rows, dcol), ('row', 'co...]
    all_to_all x0 -> x2, waiting for transfers between devices: none -> 17.8 us  [the longest x1 17.8 us: move_activations(): lax.all_to_all(partial_in.reshape(nrow * ncol, rows, dcol), ('row', 'col'...]
    all_to_all x1 -> x0, blocking collectives: 8.34 us -> none  [move_activations(): mixed = lax.all_to_all(mixed, 'dp', split_axis=0, concat_axis=1, tiled=True)]
    all_to_all x0 -> x2, starting transfers between devices: none -> 8.17 us  [the longest x1 4.79 us: move_activations(): lax.all_to_all(partial_in.reshape(nrow * ncol, rows, dcol), ('row', 'col'...]
    all_gather x1, waiting for transfers between devices: 49.7 us -> 47.2 us  [move_activations(): gathered = lax.all_gather(grad_mixed, 'dp', axis=0)]
  transfers between devices with their start and end apart: 7 -> 8, of which waited for: 6 -> 6; matrix products, arithmetic and copies ran while one was open for 2% -> 2% of each run, Pallas kernels for 3% -> 5%
where the time goes in v2:
time: 215 us; the launch traced here: 212 us
  waiting for transfers between devices  145 us (67%)
  Pallas kernels  20.3 us (9%)
  starting transfers between devices  19.2 us (9%)
  between operations  13.8 us (6%)
  local copies, waits for them, and re-layouts  11.6 us (5%)
  other arithmetic  2.43 us (1%)
    all_gather x1, waiting for transfers between devices, move_activations(): gathered = lax.all_gather(grad_mixed, 'dp', axis=0)  47.2 us
    all_gather x1, waiting for transfers between devices, move_activations(): lax.all_gather(moved, ('row', 'col'), axis=0)  33 us
    reduce_scatter x1, waiting for transfers between devices, move_activations(): lax.psum_scatter(partial.reshape(ndp, 3 * seq, width), 'dp', scatter_dime...  32.7 us
    all_to_all x1, waiting for transfers between devices, move_activations(): lax.all_to_all(partial_in.reshape(nrow * ncol, rows, dcol), ('row', 'col'...  17.8 us
    all_to_all x1, waiting for transfers between devices, move_activations(): lax.all_to_all(grad_out, 'dp', split_axis=1, concat_axis=0, tiled=True)  10.9 us
    unnamed x17, local copies, waits for them, and re-layouts  8.05 us
    pallas_call x1, Pallas kernels, move_activations(): kernel_call(functools.partial(weight_grad_body, scale), shaped((3, drow,...  6.1 us
    pallas_call x1, Pallas kernels, move_activations(): kernel_call(project_body, shaped((ndp, 3, seq, width), BF16), grid=(3,),...  5.57 us
  transfers between devices with their start and end apart: 8, of which 6 were waited for; matrix products, arithmetic and copies ran while one was open for 2% of the time, Pallas kernels for 5%

profile of v2, /device:TPU:1, one launch (start us, length us, event | category | flops | bytes accessed | tf_op | source)
XLA Modules:
  0.0 212.5 jit_solution(6129278867318607737)
XLA Ops:
  7.2 4.7 %collective-permute-start = (bf16[192,512]{1,0:T(8,128)(2,1)}, bf16[192,512]{1,0:T(8,128)(2,1)S(1)}, u32[]{:S(2)}, u32[]{:S(2)}) collective-permute-start(bf16[192,512]{1,0:T(8,128)(2,1)} %param.5), channel_id=1, source_target_pairs={{0,0},{2,8},{4,16},{6,24},{8,2},{10,10},{12,18},{14,26},{16,4},{18... | collective-permute-start | bytes 589832 | tf_op jit(solution)/shard_map/ppermute | solution.py:184
  12.0 3.5 %collective-permute-done = bf16[192,512]{1,0:T(8,128)(2,1)S(1)} collective-permute-done((bf16[192,512]{1,0:T(8,128)(2,1)}, bf16[192,512]{1,0:T(8,128)(2,1)S(1)}, u32[]{:S(2)}, u32[]{:S(2)}) %collective-permute-start) | collective-permute-done | bytes 196640 | tf_op jit(solution)/shard_map/ppermute | solution.py:184
  16.3 33.0 %all-gather.5.cloned.1.call-done = bf16[1536,512]{1,0:T(8,128)(2,1)} async-done(((bf16[192,512]{1,0:T(8,128)(2,1)}), bf16[1536,512]{1,0:T(8,128)(2,1)}) %all-gather.5.cloned.1.call-update) | async-done | bytes 1572880 | tf_op jit(solution)/shard_map/all_gather | solution.py:185
  49.3 1.4 copy-done.3
  50.7 5.6 %shard_map.92 = bf16[4,3,768,128]{3,2,1,0:T(8,128)(2,1)} custom-call(bf16[4,2,192,512]{3,2,1,0:T(8,128)(2,1)S(1)} %bitcast.28, bf16[3,1024,512]{2,1,0:T(8,128)(2,1)} %bitcast.35), custom_call_target="tpu_custom_call" | custom-call | flops 2415919104 | bytes 7077888 | tf_op jit(solution)/shard_map/pallas_call | solution.py:201
  56.3 0.7 copy_bitcast_fusion.1
  57.0 4.3 %all-to-all-start = ((bf16[192,4,128]{2,0,1:T(8,128)(2,1)}), bf16[192,4,128]{2,0,1:T(8,128)(2,1)S(1)}, u32[]{:S(2)}, u32[]{:S(2)}) async-start(bf16[192,4,128]{2,0,1:T(8,128)(2,1)} %copy_bitcast_fusion.1), calls=%async_computation.1 | async-start | bytes 393216 | tf_op jit(solution)/shard_map/all_to_all | solution.py:186
  61.3 0.7 constant_dynamic-slice_fusion
  63.5 10.9 %all-to-all-done = bf16[192,4,128]{2,0,1:T(8,128)(2,1)S(1)} async-done(((bf16[192,4,128]{2,0,1:T(8,128)(2,1)}), bf16[192,4,128]{2,0,1:T(8,128)(2,1)S(1)}, u32[]{:S(2)}, u32[]{:S(2)}) %all-to-all-start) | async-done | bytes 196640 | tf_op jit(solution)/shard_map/all_to_all | solution.py:186
  74.4 32.7 %reduce-scatter.2.cloned.1.call-done = bf16[1,2304,128]{2,1,0:T(8,128)(2,1)} async-done(((bf16[4,2304,128]{2,1,0:T(8,128)(2,1)}), bf16[1,2304,128]{2,1,0:T(8,128)(2,1)}) %reduce-scatter.2.cloned.1.call-update) | async-done | bytes 589840 | tf_op jit(solution)/shard_map/reduce_scatter | solution.py:213
  107.1 1.1 copy-done.6
  108.2 3.6 %shard_map.94 = (bf16[2336,128]{1,0:T(8,128)(2,1)}, bf16[768,128]{1,0:T(8,128)(2,1)}) custom-call(bf16[2304,128]{1,0:T(8,128)(2,1)S(1)} %bitcast.32, f32[9,128]{1,0:T(8,128)S(1)} %reshape.36.sf_ref, bf16[16,128,256]{2,1,0:T(8,128)(2,1)S(1)} %shard_map.93.causal_ref.anti_ref, bf16[16,128,256]{2,1,0:T(8,128)(2,1)S(1)} %shard_map.93.causal_ref.anti_ref, ...), custom_call_target="tpu_custom_call" | custom-call | flops 1207959552 | bytes 1966080 | tf_op jit(solution)/shard_map/pallas_call | solution.py:220
  111.8 3.4 %all-to-all-start.1 = ((bf16[4,192,128]{2,1,0:T(8,128)(2,1)}), bf16[4,192,128]{2,1,0:T(8,128)(2,1)S(1)}, u32[]{:S(2)}, u32[]{:S(2)}) async-start(bf16[4,192,128]{2,1,0:T(8,128)(2,1)} %bitcast.6), calls=%async_computation.2 | async-start | bytes 393216 | tf_op jit(solution)/shard_map/all_to_all | solution.py:230
  115.2 47.2 %all-gather.7.cloned.1.call-done = bf16[9344,128]{1,0:T(8,128)(2,1)} async-done(((bf16[2336,128]{1,0:T(8,128)(2,1)}), bf16[9344,128]{1,0:T(8,128)(2,1)}) %all-gather.7.cloned.1.call-update) | async-done | bytes 2392080 | tf_op jit(solution)/shard_map/all_gather | solution.py:229
  162.4 1.7 copy-done.1
  164.1 4.3 %shard_map.95 = bf16[4,2,192,512]{3,2,1,0:T(8,128)(2,1)S(1)} custom-call(bf16[4,2336,128]{2,1,0:T(8,128)(2,1)S(1)} %bitcast.25, bf16[3,1024,512]{2,1,0:T(8,128)(2,1)} %bitcast.36), custom_call_target="tpu_custom_call" | custom-call | flops 2415919104 | bytes 7077888 | tf_op jit(solution)/shard_map/pallas_call | solution.py:232
  168.4 1.1 copy-done.5
  169.6 4.8 %all-to-all-start.2 = ((bf16[8,192,512]{2,1,0:T(8,128)(2,1)}), bf16[8,192,512]{2,1,0:T(8,128)(2,1)}, u32[]{:S(2)}, u32[]{:S(2)}) async-start(bf16[8,192,512]{2,1,0:T(8,128)(2,1)} %bitcast.30), calls=%async_computation.3 | async-start | bytes 3145728 | tf_op jit(solution)/shard_map/all_to_all | solution.py:244
  174.3 0.7 copy_bitcast_fusion
  176.4 17.8 %all-to-all-done.2 = bf16[8,192,512]{2,1,0:T(8,128)(2,1)} async-done(((bf16[8,192,512]{2,1,0:T(8,128)(2,1)}), bf16[8,192,512]{2,1,0:T(8,128)(2,1)}, u32[]{:S(2)}, u32[]{:S(2)}) %all-to-all-start.2) | async-done | bytes 1572896 | tf_op jit(solution)/shard_map/all_to_all | solution.py:244
  194.2 1.7 reduce_sum.12
  195.8 1.9 collective-permute-start.1
  197.8 1.4 copy-done.4
  199.2 6.1 %shard_map.96 = f32[3,1024,512]{2,1,0:T(8,128)} custom-call(bf16[4,2,192,512]{3,2,1,0:T(8,128)(2,1)S(1)} %bitcast.29, bf16[4,2336,128]{2,1,0:T(8,128)(2,1)S(1)} %bitcast.27), custom_call_target="tpu_custom_call" | custom-call | flops 2415919104 | bytes 10223616 | tf_op jit(solution)/shard_map/pallas_call | solution.py:250
  (33 shorter events, 4.4 us)
Async XLA Ops:
  7.2 49.1 %copy-start = (bf16[192,512]{1,0:T(8,128)(2,1)S(1)}, bf16[192,512]{1,0:T(8,128)(2,1)}, u32[]{:S(2)}) copy-start(bf16[192,512]{1,0:T(8,128)(2,1)} %param.9) | copy-start | bytes 589828
  7.2 42.1 %all-gather.5.cloned.1.call-start = ((), (), s32[]{:S(2)}) async-start(), calls=%async_computation.5 | async-start | bytes 1769472 | tf_op jit(solution)/shard_map/all_gather | solution.py:185
  7.2 8.3 %collective-permute-start = (bf16[192,512]{1,0:T(8,128)(2,1)}, bf16[192,512]{1,0:T(8,128)(2,1)S(1)}, u32[]{:S(2)}, u32[]{:S(2)}) collective-permute-start(bf16[192,512]{1,0:T(8,128)(2,1)} %param.5), channel_id=1, source_target_pairs={{0,0},{2,8},{4,16},{6,24},{8,2},{10,10},{12,18},{14,26},{16,4},{18... | collective-permute-start | bytes 589832 | tf_op jit(solution)/shard_map/ppermute | solution.py:184
  15.5 0.7 copy-start.7
  16.2 90.9 %reduce-scatter.2.cloned.1.call-start = ((), (), s32[]{:S(2)}) async-start(), calls=%async_computation.4 | async-start | bytes 2949120 | tf_op jit(solution)/shard_map/reduce_scatter | solution.py:213
  49.3 1.4 copy-start.3
  57.0 17.4 %all-to-all-start = ((bf16[192,4,128]{2,0,1:T(8,128)(2,1)}), bf16[192,4,128]{2,0,1:T(8,128)(2,1)S(1)}, u32[]{:S(2)}, u32[]{:S(2)}) async-start(bf16[192,4,128]{2,0,1:T(8,128)(2,1)} %copy_bitcast_fusion.1), calls=%async_computation.1 | async-start | bytes 393216 | tf_op jit(solution)/shard_map/all_to_all | solution.py:186
  61.3 101.1 %all-gather.7.cloned.1.call-start = ((), (), s32[]{:S(2)}) async-start(), calls=%async_computation.6 | async-start | bytes 2990080 | tf_op jit(solution)/shard_map/all_gather | solution.py:229
  107.1 1.1 copy-start.6
  111.8 57.8 %all-to-all-start.1 = ((bf16[4,192,128]{2,1,0:T(8,128)(2,1)}), bf16[4,192,128]{2,1,0:T(8,128)(2,1)S(1)}, u32[]{:S(2)}, u32[]{:S(2)}) async-start(bf16[4,192,128]{2,1,0:T(8,128)(2,1)} %bitcast.6), calls=%async_computation.2 | async-start | bytes 393216 | tf_op jit(solution)/shard_map/all_to_all | solution.py:230
  162.4 1.7 copy-start.1
  168.4 1.1 copy-start.5
  169.5 5.5 %copy-start.2 = (bf16[9344,128]{1,0:T(8,128)(2,1)S(1)}, bf16[9344,128]{1,0:T(8,128)(2,1)}, u32[]{:S(2)}) copy-start(bf16[9344,128]{1,0:T(8,128)(2,1)} %all-gather.7.cloned.1.call-done) | copy-start | bytes 7176196
  169.6 24.6 %all-to-all-start.2 = ((bf16[8,192,512]{2,1,0:T(8,128)(2,1)}), bf16[8,192,512]{2,1,0:T(8,128)(2,1)}, u32[]{:S(2)}, u32[]{:S(2)}) async-start(bf16[8,192,512]{2,1,0:T(8,128)(2,1)} %bitcast.30), calls=%async_computation.3 | async-start | bytes 3145728 | tf_op jit(solution)/shard_map/all_to_all | solution.py:244
  195.8 9.4 %collective-permute-start.1 = (bf16[192,512]{1,0:T(8,128)(2,1)S(1)}, bf16[192,512]{1,0:T(8,128)(2,1)S(1)}, u32[]{:S(2)}, u32[]{:S(2)}) collective-permute-start(bf16[192,512]{1,0:T(8,128)(2,1)S(1)} %reduce_sum.12), channel_id=1, source_target_pairs={{0,0},{2,8},{4,16},{6,24},{8,2},{10,10},{12,18},{14,26},{16,4},{18... | collective-permute-start | bytes 589832 | tf_op jit(solution)/shard_map/ppermute | solution.py:248
  197.8 1.4 copy-start.4
Sparse Core Ops, SparseCore 0:
  16.3 32.8 all-gather.4
  56.4 50.6 reduce-scatter.1
  111.9 50.4 all-gather.6

commit v3 on v1

--- a/solution.py
+++ b/solution.py
@@ -12,13 +12,14 @@
 BF16 = jnp.bfloat16
 
 
-def kernel_call(body, outs, grid=None, in_specs=None, out_specs=None, flops=0, nbytes=0):
+def kernel_call(body, outs, grid=None, in_specs=None, out_specs=None, scratch=(), flops=0, nbytes=0):
     kwargs = {}
     if grid is not None:
         kwargs = dict(grid=grid, in_specs=in_specs, out_specs=out_specs)
     return pl.pallas_call(
         body,
         out_shape=outs,
+        scratch_shapes=scratch,
         compiler_params=pltpu.CompilerParams(vmem_limit_bytes=VMEM_BYTES),
         cost_estimate=pl.CostEstimate(flops=flops, bytes_accessed=nbytes, transcendentals=0),
         **kwargs,
@@ -44,37 +45,96 @@
         out_ref[g] = band.astype(out_ref.dtype)
 
 
-def project_body(x_ref, w_ref, out_ref):
-    parts, pieces, rows, depth = x_ref.shape
-    owners, _, tokens, width = out_ref.shape
-    total = jnp.zeros((tokens, w_ref.shape[2]), F32)
-    for e in range(pieces):
+def wrapped(value, size):
+    return lax.rem(value + 2 * size, size)
+
+
+def project_body(x_ref, w_ref, *refs):
+    *out_refs, held = refs
+    z, col = lax.axis_index("dp"), lax.axis_index("col")
+    nblocks, ncol, rows, depth = x_ref.shape
+    width = held.shape[2]
+    total = jnp.zeros((nblocks * rows, w_ref.shape[2]), F32)
+    for dx in range(ncol):
+        start = pl.multiple_of(wrapped(col - dx, ncol) * depth, depth)
         total += jnp.dot(
-            x_ref[:, e].reshape(tokens, depth),
-            w_ref[0, e * depth : (e + 1) * depth],
+            x_ref[:, dx].reshape(nblocks * rows, depth),
+            w_ref[0, pl.ds(start, depth), :],
             preferred_element_type=F32,
         )
-    for z in range(owners):
-        out_ref[z, 0] = total[:, z * width : (z + 1) * width].astype(BF16)
-
-
-def input_grad_body(gm_ref, w_ref, out_ref):
-    parts, _, rows, depth = out_ref.shape
-    owners = gm_ref.shape[0]
-    tokens = parts * rows
-    total = jnp.zeros((tokens, depth), F32)
-    for i in range(w_ref.shape[0]):
-        gm = jnp.concatenate([gm_ref[z, i * tokens : (i + 1) * tokens] for z in range(owners)], axis=1)
-        total += lax.dot_general(gm, w_ref[i], (((1,), (1,)), ((), ())), preferred_element_type=F32)
-    out_ref[:, 0] = total.reshape(parts, rows, depth).astype(BF16)
-
-
-def weight_grad_body(scale, x_ref, gm_ref, out_ref):
-    parts, _, rows, depth = x_ref.shape
-    owners, tokens, width = gm_ref.shape
-    gm = jnp.concatenate([gm_ref[z] for z in range(owners)], axis=1)
-    x = x_ref[:, 0].reshape(tokens, depth)
-    out_ref[0] = scale * lax.dot_general(x, gm, (((0,), (0,)), ((), ())), preferred_element_type=F32)
+    for owner in range(len(out_refs)):
+        held[owner] = total[:, owner * width : (owner + 1) * width].astype(BF16)
+    for ahead, out_ref in enumerate(out_refs):
+        out_ref[0] = held[wrapped(z + ahead, len(out_refs))]
+
+
+def assemble(pieces, held, ndp):
+    z = lax.axis_index("dp")
+    own, before, after, far_before, far_after = pieces
+    held[z] = own[...]
+    held[wrapped(z - 1, ndp)] = before[...]
+    held[wrapped(z + 1, ndp)] = after[...]
+
+    @pl.when(z >= ndp // 2)
+    def _():
+        held[z - ndp // 2] = far_before[...]
+
+    @pl.when(z < ndp // 2)
+    def _():
+        held[z + ndp // 2] = far_after[...]
+
+
+def input_grads(held, w_ref, all_ref, ncol):
+    ndp = held.shape[0]
+    tokens, depth = all_ref.shape[1], w_ref.shape[1] // ncol
+    col = lax.axis_index("col")
+    for i in range(3):
+        for owner in range(ndp):
+            width = held.shape[2]
+            all_ref[i, :, owner * width : (owner + 1) * width] = held[owner, i * tokens : (i + 1) * tokens]
+    for dx in range(ncol):
+        start = pl.multiple_of(wrapped(col - dx, ncol) * depth, depth)
+        total = jnp.zeros((tokens, depth), F32)
+        for i in range(3):
+            total += lax.dot_general(
+                all_ref[i],
+                w_ref[i, pl.ds(start, depth), :],
+                (((1,), (1,)), ((), ())),
+                preferred_element_type=F32,
+            )
+        yield dx, total
+
+
+def first_grad_body(own, before, after, far_before, far_after, w_ref, out_ref, all_ref, small_ref, held):
+    nblocks, ncol, rows, depth = out_ref.shape
+    assemble((own, before, after, far_before, far_after), held, held.shape[0])
+    small_ref[...] = held[:, 3 * nblocks * rows :]
+    for dx, total in input_grads(held, w_ref, all_ref, ncol):
+        out_ref[:, dx] = total.reshape(nblocks, rows, depth).astype(BF16)
+
+
+def second_grad_body(own, before, after, far_before, far_after, w_ref, other_ref, all_ref, *refs):
+    *out_refs, held = refs
+    nblocks, ncol, rows, depth = other_ref.shape
+    assemble((own, before, after, far_before, far_after), held, held.shape[0])
+    for dx, total in input_grads(held, w_ref, all_ref, ncol):
+        for block in range(nblocks):
+            both = total[block * rows : (block + 1) * rows] + other_ref[block, dx].astype(F32)
+            out_refs[block * ncol + dx][...] = both.astype(BF16)
+
+
+def weight_grad_body(scale, x0_ref, x1_ref, g0_ref, g1_ref, out_ref):
+    nblocks, ncol, rows, depth = x0_ref.shape
+    col = lax.axis_index("col")
+    gm = jnp.concatenate([g0_ref[0], g1_ref[0]], axis=0)
+    for dx in range(ncol):
+        start = pl.multiple_of(wrapped(col - dx, ncol) * depth, depth)
+        x = jnp.concatenate(
+            [x_ref[:, dx].reshape(nblocks * rows, depth) for x_ref in (x0_ref, x1_ref)], axis=0
+        )
+        out_ref[0, pl.ds(start, depth), :] = scale * lax.dot_general(
+            x, gm, (((0,), (0,)), ((), ())), preferred_element_type=F32
+        )
 
 
 def delayed(values, count):
@@ -88,16 +148,32 @@
     return jnp.where(row < rows - count, pltpu.roll(values, rows - count, 0), 0.0)
 
 
-def middle_body(scale, nshort, m_ref, sf_ref, causal_ref, anti_ref, go_ref, gm_ref, mixed_ref):
+def middle_body(scale, nshort, nrow, *refs):
+    sums, refs = (refs[:3], refs[3:6]), refs[6:]
+    sf_ref, causal_ref, anti_ref, go_ref, near_ref, other_ref, mixed_ref, m_ref, gm_ref = refs
     tokens, width = go_ref.shape
+    row = lax.axis_index("row")
+    nblocks = nrow // 2
+    rows = tokens // nrow
+
+    def places():
+        for chunk, start in enumerate((row, row + 1 - 2 * lax.rem(row, 2))):
+            for block in range(nblocks):
+                at = wrapped(start - 2 * block, nrow) * rows
+                for i in range(3):
+                    yield chunk, (i * nblocks + block) * rows, pl.multiple_of(i * tokens + at, 16)
+
+    for chunk, place, at in places():
+        held = [ref[place : place + rows].astype(F32) for ref in sums[chunk]]
+        m_ref[pl.ds(at, rows)] = held[0] + held[1] + held[2]
     groups, block, span = causal_ref.shape
     members = width // groups
-    nblocks = tokens // block
+    nspans = tokens // block
     lane = lax.broadcasted_iota(jnp.int32, (block, width), 1) // members
     lanes = lax.broadcasted_iota(jnp.int32, (block, 2 * width), 1) % width // members
 
     def past(i, j):
-        held = m_ref[i * tokens : (i + 1) * tokens].astype(F32)
+        held = m_ref[i * tokens : (i + 1) * tokens]
         return held if j == 0 else delayed(held, j)
 
     def taps(j, i):
@@ -106,13 +182,13 @@
     feats = [sum(taps(j, i) * past(i, j) for j in range(nshort)) for i in range(3)]
     product = (feats[1] * feats[2]).astype(BF16)
     zero = jnp.zeros((block, width), BF16)
-    p_blocks = [zero] + [product[b * block : (b + 1) * block] for b in range(nblocks)]
-    p_pairs = [jnp.concatenate(p_blocks[b : b + 2], axis=0) for b in range(nblocks)]
+    p_blocks = [zero] + [product[b * block : (b + 1) * block] for b in range(nspans)]
+    p_pairs = [jnp.concatenate(p_blocks[b : b + 2], axis=0) for b in range(nspans)]
 
     def filtered(band_ref, pairs):
         bands = band_ref[...].reshape(groups * block, span)
         out = []
-        for b in range(0, nblocks, 2):
+        for b in range(0, nspans, 2):
             both = jnp.dot(bands, jnp.concatenate(pairs[b : b + 2], axis=1), preferred_element_type=F32)
             for h in range(2):
                 part = both[:, h * width : (h + 1) * width]
@@ -126,19 +202,19 @@
     upstream = go_ref[...].astype(F32)
     mixed_ref[...] = (feats[0] * conv).astype(BF16)
     grad_conv = (upstream * feats[0]).astype(BF16)
-    c_blocks = [grad_conv[b * block : (b + 1) * block] for b in range(nblocks)] + [zero]
-    c_pairs = [jnp.concatenate(c_blocks[b : b + 2], axis=0) for b in range(nblocks)]
+    c_blocks = [grad_conv[b * block : (b + 1) * block] for b in range(nspans)] + [zero]
+    c_pairs = [jnp.concatenate(c_blocks[b : b + 2], axis=0) for b in range(nspans)]
     grad_product = filtered(anti_ref, c_pairs)
 
     corr = jnp.zeros((groups * block, span), F32)
-    for b in range(0, nblocks, 2):
+    for b in range(0, nspans, 2):
         left = jnp.concatenate(c_blocks[b : b + 2], axis=1)
         stacked = jnp.concatenate(
             [jnp.where(lanes == g, left, jnp.zeros_like(left)) for g in range(groups)], axis=0
         )
         right = jnp.concatenate(p_pairs[b : b + 2], axis=1)
         corr += lax.dot_general(stacked, right, (((1,), (1,)), ((), ())), preferred_element_type=F32)
-    row = lax.broadcasted_iota(jnp.int32, (8, span), 0)
+    turn = lax.broadcasted_iota(jnp.int32, (8, span), 0)
     sums = []
     for g in range(groups):
         part = corr[g * block : (g + 1) * block]
@@ -147,7 +223,7 @@
             count //= 2
             part = part[:count] + pltpu.roll(part[count:], span - count, 1)
         for bit in (1, 2, 4):
-            part = jnp.where((row & bit) != 0, pltpu.roll(part, span - bit, 1), part)
+            part = jnp.where((turn & bit) != 0, pltpu.roll(part, span - bit, 1), part)
         sums.append(jnp.sum(part, axis=0, keepdims=True))
     by_lag = jnp.concatenate(sums, axis=0)
     by_lag = scale * pltpu.roll(by_lag, span - 1, 1)[:, :block]
@@ -162,9 +238,29 @@
         for j in range(1, nshort):
             total += taps(j, i) * advanced(grad_feats[i], j)
         gm_ref[i * tokens : (i + 1) * tokens] = total.astype(BF16)
-    tail = gm_ref.shape[0] - 3 * tokens - groups - 3 * nshort
+    for chunk, place, at in places():
+        (near_ref, other_ref)[chunk][place : place + rows] = gm_ref[pl.ds(at, rows)]
+    tail = other_ref.shape[0] - 3 * tokens // 2 - groups - 3 * nshort
     small = jnp.concatenate([by_lag] + short_rows + [jnp.zeros((tail, width), F32)], axis=0)
-    gm_ref[3 * tokens :] = small.astype(BF16)
+    other_ref[3 * tokens // 2 :] = small.astype(BF16)
+
+
+def sum_over_line(own, right, far, left):
+    ndp = lax.axis_size("dp")
+    from_left = lax.ppermute(far, "dp", [(a, a + 1) for a in range(ndp // 2)])
+    from_right = lax.ppermute(far, "dp", [(a, a - 1) for a in range(ndp // 2, ndp)])
+    rightward = lax.ppermute(right + from_left, "dp", [(a, (a + 1) % ndp) for a in range(ndp)])
+    leftward = lax.ppermute(left + from_right, "dp", [(a, (a - 1) % ndp) for a in range(ndp)])
+    return own, rightward, leftward
+
+
+def gather_over_line(own):
+    ndp = lax.axis_size("dp")
+    before = lax.ppermute(own, "dp", [(a, (a + 1) % ndp) for a in range(ndp)])
+    after = lax.ppermute(own, "dp", [(a, (a - 1) % ndp) for a in range(ndp)])
+    far_before = lax.ppermute(before, "dp", [(a - 1, a) for a in range(ndp // 2, ndp)])
+    far_after = lax.ppermute(after, "dp", [(a + 1, a) for a in range(ndp // 2)])
+    return own, before, after, far_before, far_after
 
 
 def move_activations(tokens, in_weight, short_filter, long_filter, grad_out):
@@ -178,11 +274,22 @@
     width, groups = local // ndp, ngroups // ndp
     drow = in_weight.shape[0]
     scale = float(seq) ** -0.5
+    nblocks = nrow // 2
+    chunk = nblocks * rows
     swap = [(a * nrow + b, b * nrow + a) for a in range(ndp) for b in range(nrow)]
+    partner = [(a, a + 1 - 2 * (a % 2)) for a in range(nrow)]
+    places = [(dy, dx) for dy in range(nblocks) for dx in range(ncol)]
+
+    def offset(dy, dx):
+        return [
+            (a * ncol + b, (a + 2 * dy) % nrow * ncol + (b + dx) % ncol) for a in range(nrow) for b in range(ncol)
+        ]
 
     w = jnp.transpose(in_weight, (1, 0, 2))
     moved = lax.ppermute(tokens, ("dp", "row"), swap)
-    x = lax.all_gather(moved, ("row", "col"), axis=0).reshape(nrow, ncol, rows, dcol)
+    near = [moved] + [lax.ppermute(moved, ("row", "col"), offset(*p)) for p in places[1:]]
+    x0 = jnp.stack(near).reshape(nblocks, ncol, rows, dcol)
+    x1 = lax.ppermute(x0, "row", partner)
     upstream = lax.all_to_all(grad_out, "dp", split_axis=1, concat_axis=0, tiled=True)
 
     sf = lax.dynamic_slice_in_dim(short_filter, z * width, width, 2).reshape(3 * nshort, width)
@@ -197,69 +304,82 @@
     )
     bands = kernel_call(bands_body, shaped((2 * groups, ntaps, 2 * ntaps), BF16))(bases)
 
-    mm_flops = 2 * seq * drow * 3 * local
-    partial = kernel_call(
-        project_body,
-        shaped((ndp, 3, seq, width), BF16),
-        grid=(3,),
-        in_specs=[
-            pl.BlockSpec((nrow, ncol, rows, dcol), lambda i: (0, 0, 0, 0)),
-            pl.BlockSpec((1, drow, local), lambda i: (i, 0, 0)),
-        ],
-        out_specs=pl.BlockSpec((ndp, 1, seq, width), lambda i: (0, i, 0, 0)),
-        flops=mm_flops,
-        nbytes=2 * (seq * drow + 3 * drow * local + 3 * seq * local),
-    )(x, w)
-    mixed_in = lax.psum_scatter(partial.reshape(ndp, 3 * seq, width), "dp", scatter_dimension=0)
+    mm_flops = seq * drow * 3 * local
+    mm_bytes = seq * drow + 6 * drow * local + 3 * seq * local
+    sums = []
+    for x in (x0, x1):
+        parts = kernel_call(
+            project_body,
+            [shaped((3, chunk, width), BF16)] * ndp,
+            grid=(3,),
+            in_specs=[
+                pl.BlockSpec((nblocks, ncol, rows, dcol), lambda i: (0, 0, 0, 0)),
+                pl.BlockSpec((1, drow, local), lambda i: (i, 0, 0)),
+            ],
+            out_specs=[pl.BlockSpec((1, chunk, width), lambda i: (i, 0, 0))] * ndp,
+            scratch=[pltpu.VMEM((ndp, chunk, width), BF16)],
+            flops=mm_flops,
+            nbytes=mm_bytes,
+        )(x, w)
+        sums += sum_over_line(*(p.reshape(3 * chunk, width) for p in parts))
 
     extra = -(-(groups + 3 * nshort) // 16) * 16
     half = pl.BlockSpec((groups, ntaps, 2 * ntaps), lambda i: (0, 0, 0))
     other = pl.BlockSpec((groups, ntaps, 2 * ntaps), lambda i: (1, 0, 0))
-    whole = lambda shape: pl.BlockSpec(shape, lambda i: (0,) * len(shape))
-    gm_rows = 3 * seq + extra
-    grad_mixed, mixed = kernel_call(
-        functools.partial(middle_body, scale, nshort),
-        (shaped((gm_rows, width), BF16), shaped((seq, width), BF16)),
+    whole = lambda *shape: pl.BlockSpec(shape, lambda i: (0,) * len(shape))
+    grad_near, grad_other, mixed = kernel_call(
+        functools.partial(middle_body, scale, nshort, nrow),
+        (
+            shaped((3 * chunk, width), BF16),
+            shaped((3 * chunk + extra, width), BF16),
+            shaped((seq, width), BF16),
+        ),
         grid=(1,),
-        in_specs=[whole((3 * seq, width)), whole((3 * nshort, width)), half, other, whole((seq, width))],
-        out_specs=(whole((gm_rows, width)), whole((seq, width))),
+        in_specs=[whole(3 * chunk, width)] * 6
+        + [whole(3 * nshort, width), half, other, whole(seq, width)],
+        out_specs=(whole(3 * chunk, width), whole(3 * chunk + extra, width), whole(seq, width)),
+        scratch=[pltpu.VMEM((3 * seq, width), F32), pltpu.VMEM((3 * seq, width), BF16)],
         flops=3 * 2 * groups * ntaps * 2 * ntaps * width * (seq // ntaps),
-        nbytes=2 * width * seq * 10,
-    )(mixed_in, sf, bands, bands, upstream)
-    gathered = lax.all_gather(grad_mixed, "dp", axis=0)
+        nbytes=2 * width * seq * 14,
+    )(*sums, sf, bands, bands, upstream)
     mixed = lax.all_to_all(mixed, "dp", split_axis=0, concat_axis=1, tiled=True)
 
-    partial_in = kernel_call(
-        input_grad_body,
-        shaped((nrow, ncol, rows, dcol), BF16),
-        grid=(ncol,),
-        in_specs=[
-            pl.BlockSpec((ndp, gm_rows, width), lambda e: (0, 0, 0)),
-            pl.BlockSpec((3, dcol, local), lambda e: (0, e, 0)),
-        ],
-        out_specs=pl.BlockSpec((nrow, 1, rows, dcol), lambda e: (0, e, 0, 0)),
+    block = shaped((rows, dcol), BF16)
+    all_shape = shaped((3, chunk, local), BF16)
+    out_first, all_other, small = kernel_call(
+        first_grad_body,
+        (shaped((nblocks, ncol, rows, dcol), BF16), all_shape, shaped((ndp, extra, width), BF16)),
+        scratch=[pltpu.VMEM((ndp, 3 * chunk + extra, width), BF16)],
         flops=mm_flops,
-        nbytes=2 * (seq * drow + 3 * drow * local + 3 * seq * local),
-    )(gathered, w)
-    summed = lax.psum_scatter(
-        partial_in.reshape(nrow * ncol, rows, dcol), ("row", "col"), scatter_dimension=0
-    )
-    grad_in = lax.ppermute(summed, ("dp", "row"), swap)
-
+        nbytes=mm_bytes,
+    )(*gather_over_line(grad_other), w)
+    from_partner = lax.ppermute(out_first, "row", partner)
+    all_near, *blocks = kernel_call(
+        second_grad_body,
+        [all_shape] + [block] * len(places),
+        scratch=[pltpu.VMEM((ndp, 3 * chunk, width), BF16)],
+        flops=mm_flops,
+        nbytes=mm_bytes,
+    )(*gather_over_line(grad_near), w, from_partner)
+    arrived = blocks[0].astype(F32)
+    for (dy, dx), sent in zip(places[1:], blocks[1:]):
+        back = [(b, a) for a, b in offset(dy, dx)]
+        arrived += lax.ppermute(sent, ("row", "col"), back).astype(F32)
+    grad_in = lax.ppermute(arrived.astype(BF16), ("dp", "row"), swap)
+
+    x_spec = pl.BlockSpec((nblocks, ncol, rows, dcol), lambda i: (0, 0, 0, 0))
+    g_spec = pl.BlockSpec((1, chunk, local), lambda i: (i, 0, 0))
     grad_weight = kernel_call(
         functools.partial(weight_grad_body, scale),
         shaped((3, drow, local), F32),
-        grid=(3, ncol),
-        in_specs=[
-            pl.BlockSpec((nrow, 1, rows, dcol), lambda i, e: (0, e, 0, 0)),
-            pl.BlockSpec((ndp, seq, width), lambda i, e: (0, i, 0)),
-        ],
-        out_specs=pl.BlockSpec((1, dcol, local), lambda i, e: (i, e, 0)),
-        flops=mm_flops,
-        nbytes=2 * (seq * drow + 6 * drow * local + 3 * seq * local),
-    )(x, gathered)
+        grid=(3,),
+        in_specs=[x_spec, x_spec, g_spec, g_spec],
+        out_specs=pl.BlockSpec((1, drow, local), lambda i: (i, 0, 0)),
+        flops=2 * mm_flops,
+        nbytes=2 * mm_bytes,
+    )(x0, x1, all_near, all_other)
     grad_weight = jnp.transpose(grad_weight, (1, 0, 2))
-    small = gathered[:, 3 * seq :].astype(F32)
+    small = small.astype(F32)
     grad_long = small[:, :groups, ::-1].reshape(ngroups, ntaps)
     grad_short = (
         small[:, groups : groups + 3 * nshort].transpose(1, 0, 2).reshape(nshort, 3, local)
@@ -395,7 +515,8 @@
     width, rows = local // ndp, seq // ndp
     return (
         seq < tokens.shape[1]
-        and ndp == nrow
+        and ndp == nrow == 4
+        and ncol * (tokens.shape[1] // (nrow * ncol)) == in_weight.shape[0] // ndp
         and ntaps == width == 128
         and seq % (2 * ntaps) == 0
         and rows % 16 == 0

time: 229 us -> 187 us (0.82)
  the two profiles are of different devices: /device:TPU:1 before, /device:TPU:4 now
where the time goes in v3:
time: 187 us; the launch traced here: 186 us
  waiting for transfers between devices  75.9 us (41%)
  starting transfers between devices  61.9 us (33%)
  Pallas kernels  26.3 us (14%)
  local copies, waits for them, and re-layouts  16.4 us (9%)
  other arithmetic  4.44 us (2%)
    ppermute x2, waiting for transfers between devices, gather_over_line(): far_after = lax.ppermute(after, 'dp', [(a + 1, a) for a in range(ndp // 2)])  13.1 us
    ppermute x2, waiting for transfers between devices, gather_over_line(): before = lax.ppermute(own, 'dp', [(a, (a + 1) % ndp) for a in range(ndp)])  12 us
    unnamed x39, local copies, waits for them, and re-layouts  11.9 us
    ppermute x1, waiting for transfers between devices, move_activations(): moved = lax.ppermute(tokens, ('dp', 'row'), swap)  11.5 us
    ppermute x2, starting transfers between devices, sum_over_line(): lax.ppermute(left + from_right, 'dp', [(a, (a - 1) % ndp) for a in range(...  11.1 us
    ppermute x2, waiting for transfers between devices, gather_over_line(): after = lax.ppermute(own, 'dp', [(a, (a - 1) % ndp) for a in range(ndp)])  7.72 us
    ppermute x2, waiting for transfers between devices, sum_over_line(): from_left = lax.ppermute(far, 'dp', [(a, a + 1) for a in range(ndp // 2)])  7.57 us
    ppermute x2, starting transfers between devices, sum_over_line(): from_left = lax.ppermute(far, 'dp', [(a, a + 1) for a in range(ndp // 2)])  7.53 us
  transfers between devices with their start and end apart: 28, of which 17 were waited for; matrix products, arithmetic and copies ran while one was open for 4% of the time, Pallas kernels for 7%

profile of v3, /device:TPU:4, one launch (start us, length us, event | category | flops | bytes accessed | tf_op | source)
XLA Modules:
  0.0 185.8 jit_solution(4319113824397508397)
XLA Ops:
  0.6 4.6 %collective-permute-start = (bf16[192,512]{1,0:T(8,128)(2,1)}, bf16[192,512]{1,0:T(8,128)(2,1)S(1)}, u32[]{:S(2)}, u32[]{:S(2)}) collective-permute-start(bf16[192,512]{1,0:T(8,128)(2,1)} %param.5), channel_id=1, source_target_pairs={{0,0},{2,8},{4,16},{6,24},{8,2},{10,10},{12,18},{14,26},{16,4},{18... | collective-permute-start | bytes 589832 | tf_op jit(solution)/shard_map/ppermute | solution.py:289
  5.2 11.5 %collective-permute-done = bf16[192,512]{1,0:T(8,128)(2,1)S(1)} collective-permute-done((bf16[192,512]{1,0:T(8,128)(2,1)}, bf16[192,512]{1,0:T(8,128)(2,1)S(1)}, u32[]{:S(2)}, u32[]{:S(2)}) %collective-permute-start) | collective-permute-done | bytes 196640 | tf_op jit(solution)/shard_map/ppermute | solution.py:289
  28.3 4.0 %shard_map.92 = (bf16[3,384,128]{2,1,0:T(8,128)(2,1)S(1)}, bf16[3,384,128]{2,1,0:T(8,128)(2,1)S(1)}, bf16[3,384,128]{2,1,0:T(8,128)(2,1)}, bf16[3,384,128]{2,1,0:T(8,128)(2,1)S(1)}) custom-call(bf16[2,2,192,512]{3,2,1,0:T(8,128)(2,1)} %bitcast.4.x_ref.x0_ref, bf16[3,1024,512]{2,1,0:T(8,128)(2,1)S(1)} %bitcast.39), custom_call_target="tpu_custom_call" | custom-call | flops 1207959552 | bytes 5111808 | tf_op jit(solution)/shard_map/pallas_call | solution.py:311
  34.4 4.3 %collective-permute-start.4 = (bf16[1152,128]{1,0:T(8,128)(2,1)}, bf16[1152,128]{1,0:T(8,128)(2,1)}, u32[]{:S(2)}, u32[]{:S(2)}) collective-permute-start(bf16[1152,128]{1,0:T(8,128)(2,1)} %bitcast.8), channel_id=1, source_target_pairs={{0,8},{8,16},{1,9},{9,17},{2,10},{10,18},{3,11},{11,19},{4,12},{12... | collective-permute-start | bytes 884744 | tf_op jit(solution)/shard_map/ppermute | solution.py:250
  39.5 3.4 %all-to-all-start = ((bf16[192,4,128]{2,0,1:T(8,128)(2,1)}), bf16[192,4,128]{2,0,1:T(8,128)(2,1)S(1)}, u32[]{:S(2)}, u32[]{:S(2)}) async-start(bf16[192,4,128]{2,0,1:T(8,128)(2,1)} %copy_bitcast_fusion.1), calls=%async_computation | async-start | bytes 393216 | tf_op jit(solution)/shard_map/all_to_all | solution.py:293
  58.2 5.6 %collective-permute-done.9 = bf16[1152,128]{1,0:T(8,128)(2,1)S(1)} collective-permute-done((bf16[1152,128]{1,0:T(8,128)(2,1)S(1)}, bf16[1152,128]{1,0:T(8,128)(2,1)S(1)}, u32[]{:S(2)}, u32[]{:S(2)}) %collective-permute-start.9) | collective-permute-done | bytes 294944 | tf_op jit(solution)/shard_map/ppermute | solution.py:250
  66.5 10.0 %collective-permute-start.12 = (bf16[1152,128]{1,0:T(8,128)(2,1)S(1)}, bf16[1152,128]{1,0:T(8,128)(2,1)S(1)}, u32[]{:S(2)}, u32[]{:S(2)}) collective-permute-start(bf16[1152,128]{1,0:T(8,128)(2,1)S(1)} %bitcast_add_fusion), channel_id=1, source_target_pairs={{0,24},{8,0},{16,8},{24,16},{1,25},{9,1},{17,9},{25,17},{2,26},{10... | collective-permute-start | bytes 884744 | tf_op jit(solution)/shard_map/ppermute | solution.py:253
  78.7 4.5 %collective-permute-done.10.refs_4_ = bf16[1152,128]{1,0:T(8,128)(2,1)S(1)} collective-permute-done((bf16[1152,128]{1,0:T(8,128)(2,1)S(1)}, bf16[1152,128]{1,0:T(8,128)(2,1)S(1)}, u32[]{:S(2)}, u32[]{:S(2)}) %collective-permute-start.10) | collective-permute-done | bytes 294944 | tf_op jit(solution)/shard_map/ppermute | solution.py:252
  83.2 4.2 %collective-permute-done.12.refs_5_ = bf16[1152,128]{1,0:T(8,128)(2,1)S(1)} collective-permute-done((bf16[1152,128]{1,0:T(8,128)(2,1)S(1)}, bf16[1152,128]{1,0:T(8,128)(2,1)S(1)}, u32[]{:S(2)}, u32[]{:S(2)}) %collective-permute-start.12) | collective-permute-done | bytes 294944 | tf_op jit(solution)/shard_map/ppermute | solution.py:253
  89.4 3.9 %shard_map.95 = (bf16[1152,128]{1,0:T(8,128)(2,1)S(1)}, bf16[1184,128]{1,0:T(8,128)(2,1)S(1)}, bf16[768,128]{1,0:T(8,128)(2,1)}) custom-call(bf16[1152,128]{1,0:T(8,128)(2,1)S(1)} %bitcast.44, bf16[1152,128]{1,0:T(8,128)(2,1)} %collective-permute-done.5.refs_1_, bf16[1152,128]{1,0:T(8,128)(2,1)S(1)} %collective-permute-done.7.refs_2_, ...), custom_call_target="tpu_custom_call" | custom-call | flops 1207959552 | bytes 2752512 | tf_op jit(solution)/shard_map/pallas_call | solution.py:330
  97.1 8.1 %collective-permute-done.17.before = bf16[1184,128]{1,0:T(8,128)(2,1)S(1)} collective-permute-done((bf16[1184,128]{1,0:T(8,128)(2,1)S(1)}, bf16[1184,128]{1,0:T(8,128)(2,1)S(1)}, u32[]{:S(2)}, u32[]{:S(2)}) %collective-permute-start.17) | collective-permute-done | bytes 303136 | tf_op jit(solution)/shard_map/ppermute | solution.py:259
  106.0 3.3 %collective-permute-done.18.after = bf16[1184,128]{1,0:T(8,128)(2,1)S(1)} collective-permute-done((bf16[1184,128]{1,0:T(8,128)(2,1)S(1)}, bf16[1184,128]{1,0:T(8,128)(2,1)S(1)}, u32[]{:S(2)}, u32[]{:S(2)}) %collective-permute-start.18) | collective-permute-done | bytes 303136 | tf_op jit(solution)/shard_map/ppermute | solution.py:260
  110.6 9.7 %collective-permute-done.20.far_after = bf16[1184,128]{1,0:T(8,128)(2,1)S(1)} collective-permute-done((bf16[1184,128]{1,0:T(8,128)(2,1)S(1)}, bf16[1184,128]{1,0:T(8,128)(2,1)S(1)}, u32[]{:S(2)}, u32[]{:S(2)}) %collective-permute-start.20) | collective-permute-done | bytes 303136 | tf_op jit(solution)/shard_map/ppermute | solution.py:262
  120.3 4.3 %shard_map.96 = (bf16[2,2,192,512]{3,2,1,0:T(8,128)(2,1)}, bf16[3,384,512]{2,1,0:T(8,128)(2,1)S(1)}, bf16[4,32,128]{2,1,0:T(8,128)(2,1)S(1)}) custom-call(bf16[1184,128]{1,0:T(8,128)(2,1)S(1)} %get-tuple-element.34.own, bf16[1184,128]{1,0:T(8,128)(2,1)S(1)} %collective-permute-done.17.before, bf16[1184,128]{1,0:T(8,128)(2,1)S(1)} %collective-permute-done.18.after, ...), custom_call_target="tpu_custom_call" | custom-call | flops 1207959552 | bytes 5111808 | tf_op jit(solution)/shard_map/pallas_call | solution.py:349
  125.1 3.2 %collective-permute-start.14 = (bf16[1152,128]{1,0:T(8,128)(2,1)S(1)}, bf16[1152,128]{1,0:T(8,128)(2,1)S(1)}, u32[]{:S(2)}, u32[]{:S(2)}) collective-permute-start(bf16[1152,128]{1,0:T(8,128)(2,1)S(1)} %get-tuple-element.33.own), channel_id=1, source_target_pairs={{0,24},{8,0},{16,8},{24,16},{1,25},{9,1},{17,9},{25,17},{2,26},{10... | collective-permute-start | bytes 884744 | tf_op jit(solution)/shard_map/ppermute | solution.py:260
  128.4 4.0 %all-to-all-start.1 = ((bf16[4,192,128]{2,1,0:T(8,128)(2,1)}), bf16[4,192,128]{2,1,0:T(8,128)(2,1)}, u32[]{:S(2)}, u32[]{:S(2)}) async-start(bf16[4,192,128]{2,1,0:T(8,128)(2,1)} %bitcast.16), calls=%async_computation.1 | async-start | bytes 393216 | tf_op jit(solution)/shard_map/all_to_all | solution.py:345
  132.4 3.8 %collective-permute-done.13.before = bf16[1152,128]{1,0:T(8,128)(2,1)S(1)} collective-permute-done((bf16[1152,128]{1,0:T(8,128)(2,1)S(1)}, bf16[1152,128]{1,0:T(8,128)(2,1)S(1)}, u32[]{:S(2)}, u32[]{:S(2)}) %collective-permute-start.13) | collective-permute-done | bytes 294944 | tf_op jit(solution)/shard_map/ppermute | solution.py:259
  136.9 4.4 %collective-permute-done.14.after = bf16[1152,128]{1,0:T(8,128)(2,1)S(1)} collective-permute-done((bf16[1152,128]{1,0:T(8,128)(2,1)S(1)}, bf16[1152,128]{1,0:T(8,128)(2,1)S(1)}, u32[]{:S(2)}, u32[]{:S(2)}) %collective-permute-start.14) | collective-permute-done | bytes 294944 | tf_op jit(solution)/shard_map/ppermute | solution.py:260
  147.5 3.4 %collective-permute-done.16.far_after = bf16[1152,128]{1,0:T(8,128)(2,1)} collective-permute-done((bf16[1152,128]{1,0:T(8,128)(2,1)S(1)}, bf16[1152,128]{1,0:T(8,128)(2,1)}, u32[]{:S(2)}, u32[]{:S(2)}) %collective-permute-start.16) | collective-permute-done | bytes 294944 | tf_op jit(solution)/shard_map/ppermute | solution.py:262
  154.8 4.2 %shard_map.97 = (bf16[3,384,512]{2,1,0:T(8,128)(2,1)S(1)}, bf16[192,512]{1,0:T(8,128)(2,1)S(1)}, bf16[192,512]{1,0:T(8,128)(2,1)}, bf16[192,512]{1,0:T(8,128)(2,1)}, bf16[192,512]{1,0:T(8,128)(2,1)}) custom-call(bf16[1152,128]{1,0:T(8,128)(2,1)S(1)} %copy-done.7, bf16[1152,128]{1,0:T(8,128)(2,1)S(1)} %copy-done.9, bf16[1152,128]{1,0:T(8,128)(2,1)S(1)} %copy-done.11, ...), custom_call_target="tpu_custom_call" | custom-call | flops 1207959552 | bytes 5111808 | tf_op jit(solution)/shard_map/pallas_call | solution.py:357
  163.1 3.8 %collective-permute-done.24 = bf16[192,512]{1,0:T(8,128)(2,1)S(1)} collective-permute-done((bf16[192,512]{1,0:T(8,128)(2,1)}, bf16[192,512]{1,0:T(8,128)(2,1)S(1)}, u32[]{:S(2)}, u32[]{:S(2)}) %collective-permute-start.24) | collective-permute-done | bytes 196640 | tf_op jit(solution)/shard_map/ppermute | solution.py:367
  169.0 6.3 %collective-permute-start.25 = (bf16[192,512]{1,0:T(8,128)(2,1)S(1)}, bf16[192,512]{1,0:T(8,128)(2,1)S(1)}, u32[]{:S(2)}, u32[]{:S(2)}) collective-permute-start(bf16[192,512]{1,0:T(8,128)(2,1)S(1)} %add_convert_fusion), channel_id=1, source_target_pairs={{0,0},{2,8},{4,16},{6,24},{8,2},{10,10},{12,18},{14,26},{16,4},{18... | collective-permute-start | bytes 589832 | tf_op jit(solution)/shard_map/ppermute | solution.py:368
  175.3 6.1 %shard_map.98 = f32[3,1024,512]{2,1,0:T(8,128)} custom-call(bf16[2,2,192,512]{3,2,1,0:T(8,128)(2,1)} %bitcast.4.x_ref.x0_ref, bf16[2,2,192,512]{3,2,1,0:T(8,128)(2,1)} %collective-permute-done.8.x_ref.x1_ref, bf16[3,384,512]{2,1,0:T(8,128)(2,1)S(1)} %get-tuple-element.40.g0_ref, bf16[3,384,512]{2,1,0:T(8,128)(2,1)S(1)} %get-tuple-element.41.g1_ref), custom_call_target="tpu_custom_call" | custom-call | flops 2415919104 | bytes 10223616 | tf_op jit(solution)/shard_map/pallas_call | solution.py:372
  181.4 3.7 %collective-permute-done.25 = bf16[192,512]{1,0:T(8,128)(2,1)S(1)} collective-permute-done((bf16[192,512]{1,0:T(8,128)(2,1)S(1)}, bf16[192,512]{1,0:T(8,128)(2,1)S(1)}, u32[]{:S(2)}, u32[]{:S(2)}) %collective-permute-start.25) | collective-permute-done | bytes 196640 | tf_op jit(solution)/shard_map/ppermute | solution.py:368
  (99 shorter events, 60.5 us)
Async XLA Ops:
  0.6 16.1 %collective-permute-start = (bf16[192,512]{1,0:T(8,128)(2,1)}, bf16[192,512]{1,0:T(8,128)(2,1)S(1)}, u32[]{:S(2)}, u32[]{:S(2)}) collective-permute-start(bf16[192,512]{1,0:T(8,128)(2,1)} %param.5), channel_id=1, source_target_pairs={{0,0},{2,8},{4,16},{6,24},{8,2},{10,10},{12,18},{14,26},{16,4},{18... | collective-permute-start | bytes 589832 | tf_op jit(solution)/shard_map/ppermute | solution.py:289
  16.7 8.7 %collective-permute-start.2 = (bf16[192,512]{1,0:T(8,128)(2,1)S(1)}, bf16[192,512]{1,0:T(8,128)(2,1)S(1)}, u32[]{:S(2)}, u32[]{:S(2)}) collective-permute-start(bf16[192,512]{1,0:T(8,128)(2,1)S(1)} %collective-permute-done), channel_id=1, source_target_pairs={{0,4},{1,5},{2,6},{3,7},{4,0},{5,1},{6,2},{7,3},{8,12},{9,13},{10,... | collective-permute-start | bytes 589832 | tf_op jit(solution)/shard_map/ppermute | solution.py:290
  26.4 23.6 %collective-permute-start.8 = (bf16[2,2,192,512]{3,2,1,0:T(8,128)(2,1)}, bf16[2,2,192,512]{3,2,1,0:T(8,128)(2,1)}, u32[]{:S(2)}, u32[]{:S(2)}) collective-permute-start(bf16[2,2,192,512]{3,2,1,0:T(8,128)(2,1)} %bitcast.4.x_ref.x0_ref), channel_id=1, source_target_pairs={{0,2},{2,0},{4,6},{6,4},{1,3},{3,1},{5,7},{7,5},{8,10},{10,8},{12,... | collective-permute-start | bytes 2359304 | tf_op jit(solution)/shard_map/ppermute | solution.py:292
  34.4 11.2 %collective-permute-start.4 = (bf16[1152,128]{1,0:T(8,128)(2,1)}, bf16[1152,128]{1,0:T(8,128)(2,1)}, u32[]{:S(2)}, u32[]{:S(2)}) collective-permute-start(bf16[1152,128]{1,0:T(8,128)(2,1)} %bitcast.8), channel_id=1, source_target_pairs={{0,8},{8,16},{1,9},{9,17},{2,10},{10,18},{3,11},{11,19},{4,12},{12... | collective-permute-start | bytes 884744 | tf_op jit(solution)/shard_map/ppermute | solution.py:250
  39.5 39.3 %all-to-all-start = ((bf16[192,4,128]{2,0,1:T(8,128)(2,1)}), bf16[192,4,128]{2,0,1:T(8,128)(2,1)S(1)}, u32[]{:S(2)}, u32[]{:S(2)}) async-start(bf16[192,4,128]{2,0,1:T(8,128)(2,1)} %copy_bitcast_fusion.1), calls=%async_computation | async-start | bytes 393216 | tf_op jit(solution)/shard_map/all_to_all | solution.py:293
  42.9 13.6 %collective-permute-start.6 = (bf16[1152,128]{1,0:T(8,128)(2,1)}, bf16[1152,128]{1,0:T(8,128)(2,1)S(1)}, u32[]{:S(2)}, u32[]{:S(2)}) collective-permute-start(bf16[1152,128]{1,0:T(8,128)(2,1)} %bitcast.8), channel_id=1, source_target_pairs={{16,8},{24,16},{17,9},{25,17},{18,10},{26,18},{19,11},{27,19},{20,... | collective-permute-start | bytes 884744 | tf_op jit(solution)/shard_map/ppermute | solution.py:251
  47.5 31.3 %collective-permute-start.5 = (bf16[1152,128]{1,0:T(8,128)(2,1)}, bf16[1152,128]{1,0:T(8,128)(2,1)}, u32[]{:S(2)}, u32[]{:S(2)}) collective-permute-start(bf16[1152,128]{1,0:T(8,128)(2,1)} %bitcast_add_fusion.3), channel_id=1, source_target_pairs={{0,8},{8,16},{16,24},{24,0},{1,9},{9,17},{17,25},{25,1},{2,10},{10... | collective-permute-start | bytes 884744 | tf_op jit(solution)/shard_map/ppermute | solution.py:252
  53.2 10.7 %collective-permute-start.9 = (bf16[1152,128]{1,0:T(8,128)(2,1)S(1)}, bf16[1152,128]{1,0:T(8,128)(2,1)S(1)}, u32[]{:S(2)}, u32[]{:S(2)}) collective-permute-start(bf16[1152,128]{1,0:T(8,128)(2,1)S(1)} %bitcast.42), channel_id=1, source_target_pairs={{0,8},{8,16},{1,9},{9,17},{2,10},{10,18},{3,11},{11,19},{4,12},{12... | collective-permute-start | bytes 884744 | tf_op jit(solution)/shard_map/ppermute | solution.py:250
  56.5 22.3 %collective-permute-start.7 = (bf16[1152,128]{1,0:T(8,128)(2,1)S(1)}, bf16[1152,128]{1,0:T(8,128)(2,1)S(1)}, u32[]{:S(2)}, u32[]{:S(2)}) collective-permute-start(bf16[1152,128]{1,0:T(8,128)(2,1)S(1)} %bitcast_add_fusion.2), channel_id=1, source_target_pairs={{0,24},{8,0},{16,8},{24,16},{1,25},{9,1},{17,9},{25,17},{2,26},{10... | collective-permute-start | bytes 884744 | tf_op jit(solution)/shard_map/ppermute | solution.py:253
  57.6 8.9 %collective-permute-start.11 = (bf16[1152,128]{1,0:T(8,128)(2,1)S(1)}, bf16[1152,128]{1,0:T(8,128)(2,1)S(1)}, u32[]{:S(2)}, u32[]{:S(2)}) collective-permute-start(bf16[1152,128]{1,0:T(8,128)(2,1)S(1)} %bitcast.43), channel_id=1, source_target_pairs={{16,8},{24,16},{17,9},{25,17},{18,10},{26,18},{19,11},{27,19},{20,... | collective-permute-start | bytes 884744 | tf_op jit(solution)/shard_map/ppermute | solution.py:251
  63.9 19.3 %collective-permute-start.10 = (bf16[1152,128]{1,0:T(8,128)(2,1)S(1)}, bf16[1152,128]{1,0:T(8,128)(2,1)S(1)}, u32[]{:S(2)}, u32[]{:S(2)}) collective-permute-start(bf16[1152,128]{1,0:T(8,128)(2,1)S(1)} %bitcast_add_fusion.1), channel_id=1, source_target_pairs={{0,8},{8,16},{16,24},{24,0},{1,9},{9,17},{17,25},{25,1},{2,10},{10... | collective-permute-start | bytes 884744 | tf_op jit(solution)/shard_map/ppermute | solution.py:252
  66.5 21.0 %collective-permute-start.12 = (bf16[1152,128]{1,0:T(8,128)(2,1)S(1)}, bf16[1152,128]{1,0:T(8,128)(2,1)S(1)}, u32[]{:S(2)}, u32[]{:S(2)}) collective-permute-start(bf16[1152,128]{1,0:T(8,128)(2,1)S(1)} %bitcast_add_fusion), channel_id=1, source_target_pairs={{0,24},{8,0},{16,8},{24,16},{1,25},{9,1},{17,9},{25,17},{2,26},{10... | collective-permute-start | bytes 884744 | tf_op jit(solution)/shard_map/ppermute | solution.py:253
  93.3 12.0 %collective-permute-start.17 = (bf16[1184,128]{1,0:T(8,128)(2,1)S(1)}, bf16[1184,128]{1,0:T(8,128)(2,1)S(1)}, u32[]{:S(2)}, u32[]{:S(2)}) collective-permute-start(bf16[1184,128]{1,0:T(8,128)(2,1)S(1)} %get-tuple-element.34.own), channel_id=1, source_target_pairs={{0,8},{8,16},{16,24},{24,0},{1,9},{9,17},{17,25},{25,1},{2,10},{10... | collective-permute-start | bytes 909320 | tf_op jit(solution)/shard_map/ppermute | solution.py:259
  95.3 14.0 %collective-permute-start.18 = (bf16[1184,128]{1,0:T(8,128)(2,1)S(1)}, bf16[1184,128]{1,0:T(8,128)(2,1)S(1)}, u32[]{:S(2)}, u32[]{:S(2)}) collective-permute-start(bf16[1184,128]{1,0:T(8,128)(2,1)S(1)} %get-tuple-element.34.own), channel_id=1, source_target_pairs={{0,24},{8,0},{16,8},{24,16},{1,25},{9,1},{17,9},{25,17},{2,26},{10... | collective-permute-start | bytes 909320 | tf_op jit(solution)/shard_map/ppermute | solution.py:260
  109.3 11.0 %collective-permute-start.20 = (bf16[1184,128]{1,0:T(8,128)(2,1)S(1)}, bf16[1184,128]{1,0:T(8,128)(2,1)S(1)}, u32[]{:S(2)}, u32[]{:S(2)}) collective-permute-start(bf16[1184,128]{1,0:T(8,128)(2,1)S(1)} %collective-permute-done.18.after), channel_id=1, source_target_pairs={{8,0},{16,8},{9,1},{17,9},{10,2},{18,10},{11,3},{19,11},{12,4},{20... | collective-permute-start | bytes 909320 | tf_op jit(solution)/shard_map/ppermute | solution.py:262
  124.5 26.4 %collective-permute-start.21 = (bf16[2,2,192,512]{3,2,1,0:T(8,128)(2,1)}, bf16[2,2,192,512]{3,2,1,0:T(8,128)(2,1)S(1)}, u32[]{:S(2)}, u32[]{:S(2)}) collective-permute-start(bf16[2,2,192,512]{3,2,1,0:T(8,128)(2,1)} %get-tuple-element.35), channel_id=1, source_target_pairs={{0,2},{2,0},{4,6},{6,4},{1,3},{3,1},{5,7},{7,5},{8,10},{10,8},{12,... | collective-permute-start | bytes 2359304 | tf_op jit(solution)/shard_map/ppermute | solution.py:356
  124.5 11.6 %collective-permute-start.13 = (bf16[1152,128]{1,0:T(8,128)(2,1)S(1)}, bf16[1152,128]{1,0:T(8,128)(2,1)S(1)}, u32[]{:S(2)}, u32[]{:S(2)}) collective-permute-start(bf16[1152,128]{1,0:T(8,128)(2,1)S(1)} %get-tuple-element.33.own), channel_id=1, source_target_pairs={{0,8},{8,16},{16,24},{24,0},{1,9},{9,17},{17,25},{25,1},{2,10},{10... | collective-permute-start | bytes 884744 | tf_op jit(solution)/shard_map/ppermute | solution.py:259
  125.1 16.1 %collective-permute-start.14 = (bf16[1152,128]{1,0:T(8,128)(2,1)S(1)}, bf16[1152,128]{1,0:T(8,128)(2,1)S(1)}, u32[]{:S(2)}, u32[]{:S(2)}) collective-permute-start(bf16[1152,128]{1,0:T(8,128)(2,1)S(1)} %get-tuple-element.33.own), channel_id=1, source_target_pairs={{0,24},{8,0},{16,8},{24,16},{1,25},{9,1},{17,9},{25,17},{2,26},{10... | collective-permute-start | bytes 884744 | tf_op jit(solution)/shard_map/ppermute | solution.py:260
  128.4 15.5 %all-to-all-start.1 = ((bf16[4,192,128]{2,1,0:T(8,128)(2,1)}), bf16[4,192,128]{2,1,0:T(8,128)(2,1)}, u32[]{:S(2)}, u32[]{:S(2)}) async-start(bf16[4,192,128]{2,1,0:T(8,128)(2,1)} %bitcast.16), calls=%async_computation.1 | async-start | bytes 393216 | tf_op jit(solution)/shard_map/all_to_all | solution.py:345
  136.2 10.6 %collective-permute-start.15 = (bf16[1152,128]{1,0:T(8,128)(2,1)S(1)}, bf16[1152,128]{1,0:T(8,128)(2,1)S(1)}, u32[]{:S(2)}, u32[]{:S(2)}) collective-permute-start(bf16[1152,128]{1,0:T(8,128)(2,1)S(1)} %collective-permute-done.13.before), channel_id=1, source_target_pairs={{8,16},{16,24},{9,17},{17,25},{10,18},{18,26},{11,19},{19,27},{12,... | collective-permute-start | bytes 884744 | tf_op jit(solution)/shard_map/ppermute | solution.py:261
  141.2 9.6 %collective-permute-start.16 = (bf16[1152,128]{1,0:T(8,128)(2,1)S(1)}, bf16[1152,128]{1,0:T(8,128)(2,1)}, u32[]{:S(2)}, u32[]{:S(2)}) collective-permute-start(bf16[1152,128]{1,0:T(8,128)(2,1)S(1)} %collective-permute-done.14.after), channel_id=1, source_target_pairs={{8,0},{16,8},{9,1},{17,9},{10,2},{18,10},{11,3},{19,11},{12,4},{20... | collective-permute-start | bytes 884744 | tf_op jit(solution)/shard_map/ppermute | solution.py:262
  159.0 8.0 %collective-permute-start.24 = (bf16[192,512]{1,0:T(8,128)(2,1)}, bf16[192,512]{1,0:T(8,128)(2,1)S(1)}, u32[]{:S(2)}, u32[]{:S(2)}) collective-permute-start(bf16[192,512]{1,0:T(8,128)(2,1)} %get-tuple-element.39), channel_id=1, source_target_pairs={{5,0},{4,1},{7,2},{6,3},{1,4},{0,5},{3,6},{2,7},{13,8},{12,9},{15,... | collective-permute-start | bytes 589832 | tf_op jit(solution)/shard_map/ppermute | solution.py:367
  160.5 8.4 %collective-permute-start.23 = (bf16[192,512]{1,0:T(8,128)(2,1)}, bf16[192,512]{1,0:T(8,128)(2,1)S(1)}, u32[]{:S(2)}, u32[]{:S(2)}) collective-permute-start(bf16[192,512]{1,0:T(8,128)(2,1)} %get-tuple-element.38), channel_id=1, source_target_pairs={{4,0},{5,1},{6,2},{7,3},{0,4},{1,5},{2,6},{3,7},{12,8},{13,9},{14,... | collective-permute-start | bytes 589832 | tf_op jit(solution)/shard_map/ppermute | solution.py:367
  169.0 16.1 %collective-permute-start.25 = (bf16[192,512]{1,0:T(8,128)(2,1)S(1)}, bf16[192,512]{1,0:T(8,128)(2,1)S(1)}, u32[]{:S(2)}, u32[]{:S(2)}) collective-permute-start(bf16[192,512]{1,0:T(8,128)(2,1)S(1)} %add_convert_fusion), channel_id=1, source_target_pairs={{0,0},{2,8},{4,16},{6,24},{8,2},{10,10},{12,18},{14,26},{16,4},{18... | collective-permute-start | bytes 589832 | tf_op jit(solution)/shard_map/ppermute | solution.py:368
  (23 other events, 213.6 us)

commit v4 on v3

--- a/solution.py
+++ b/solution.py
@@ -7,7 +7,7 @@
 from jax.experimental.pallas import tpu as pltpu
 from jax.sharding import PartitionSpec as P
 
-VMEM_BYTES = 48 * 2**20
+VMEM_BYTES = 20 * 2**20
 F32 = jnp.float32
 BF16 = jnp.bfloat16
 
@@ -53,7 +53,7 @@
     *out_refs, held = refs
     z, col = lax.axis_index("dp"), lax.axis_index("col")
     nblocks, ncol, rows, depth = x_ref.shape
-    width = held.shape[2]
+    width = out_refs[0].shape[-1]
     total = jnp.zeros((nblocks * rows, w_ref.shape[2]), F32)
     for dx in range(ncol):
         start = pl.multiple_of(wrapped(col - dx, ncol) * depth, depth)
@@ -62,10 +62,13 @@
             w_ref[0, pl.ds(start, depth), :],
             preferred_element_type=F32,
         )
-    for owner in range(len(out_refs)):
+    if len(out_refs) == 1:
+        (held,) = (ref.at[:, 0] for ref in out_refs)
+    for owner in range(held.shape[0]):
         held[owner] = total[:, owner * width : (owner + 1) * width].astype(BF16)
-    for ahead, out_ref in enumerate(out_refs):
-        out_ref[0] = held[wrapped(z + ahead, len(out_refs))]
+    if len(out_refs) > 1:
+        for ahead, out_ref in enumerate(out_refs):
+            out_ref[0] = held[wrapped(z + ahead, len(out_refs))]
 
 
 def assemble(pieces, held, ndp):
@@ -113,10 +116,8 @@
         out_ref[:, dx] = total.reshape(nblocks, rows, depth).astype(BF16)
 
 
-def second_grad_body(own, before, after, far_before, far_after, w_ref, other_ref, all_ref, *refs):
-    *out_refs, held = refs
+def second_grad_body(held, w_ref, other_ref, all_ref, *out_refs):
     nblocks, ncol, rows, depth = other_ref.shape
-    assemble((own, before, after, far_before, far_after), held, held.shape[0])
     for dx, total in input_grads(held, w_ref, all_ref, ncol):
         for block in range(nblocks):
             both = total[block * rows : (block + 1) * rows] + other_ref[block, dx].astype(F32)
@@ -149,7 +150,7 @@
 
 
 def middle_body(scale, nshort, nrow, *refs):
-    sums, refs = (refs[:3], refs[3:6]), refs[6:]
+    sums, refs = (refs[:3], refs[3:4]), refs[4:]
     sf_ref, causal_ref, anti_ref, go_ref, near_ref, other_ref, mixed_ref, m_ref, gm_ref = refs
     tokens, width = go_ref.shape
     row = lax.axis_index("row")
@@ -164,8 +165,7 @@
                     yield chunk, (i * nblocks + block) * rows, pl.multiple_of(i * tokens + at, 16)
 
     for chunk, place, at in places():
-        held = [ref[place : place + rows].astype(F32) for ref in sums[chunk]]
-        m_ref[pl.ds(at, rows)] = held[0] + held[1] + held[2]
+        m_ref[pl.ds(at, rows)] = sum(ref[place : place + rows].astype(F32) for ref in sums[chunk])
     groups, block, span = causal_ref.shape
     members = width // groups
     nspans = tokens // block
@@ -287,10 +287,12 @@
 
     w = jnp.transpose(in_weight, (1, 0, 2))
     moved = lax.ppermute(tokens, ("dp", "row"), swap)
+    moved, grad_out = lax.optimization_barrier((moved, grad_out))
     near = [moved] + [lax.ppermute(moved, ("row", "col"), offset(*p)) for p in places[1:]]
+    upstream = lax.all_to_all(grad_out, "dp", split_axis=1, concat_axis=0, tiled=True)
     x0 = jnp.stack(near).reshape(nblocks, ncol, rows, dcol)
     x1 = lax.ppermute(x0, "row", partner)
-    upstream = lax.all_to_all(grad_out, "dp", split_axis=1, concat_axis=0, tiled=True)
+    x0, upstream = lax.optimization_barrier((x0, upstream))
 
     sf = lax.dynamic_slice_in_dim(short_filter, z * width, width, 2).reshape(3 * nshort, width)
     lf = lax.dynamic_slice_in_dim(long_filter, z * groups, groups, 0).astype(F32)
@@ -307,21 +309,32 @@
     mm_flops = seq * drow * 3 * local
     mm_bytes = seq * drow + 6 * drow * local + 3 * seq * local
     sums = []
-    for x in (x0, x1):
-        parts = kernel_call(
-            project_body,
-            [shaped((3, chunk, width), BF16)] * ndp,
-            grid=(3,),
-            in_specs=[
-                pl.BlockSpec((nblocks, ncol, rows, dcol), lambda i: (0, 0, 0, 0)),
-                pl.BlockSpec((1, drow, local), lambda i: (i, 0, 0)),
-            ],
-            out_specs=[pl.BlockSpec((1, chunk, width), lambda i: (i, 0, 0))] * ndp,
-            scratch=[pltpu.VMEM((ndp, chunk, width), BF16)],
-            flops=mm_flops,
-            nbytes=mm_bytes,
-        )(x, w)
-        sums += sum_over_line(*(p.reshape(3 * chunk, width) for p in parts))
+    project_specs = [
+        pl.BlockSpec((nblocks, ncol, rows, dcol), lambda i: (0, 0, 0, 0)),
+        pl.BlockSpec((1, drow, local), lambda i: (i, 0, 0)),
+    ]
+    parts = kernel_call(
+        project_body,
+        [shaped((3, chunk, width), BF16)] * ndp,
+        grid=(3,),
+        in_specs=project_specs,
+        out_specs=[pl.BlockSpec((1, chunk, width), lambda i: (i, 0, 0))] * ndp,
+        scratch=[pltpu.VMEM((ndp, chunk, width), BF16)],
+        flops=mm_flops,
+        nbytes=mm_bytes,
+    )(x0, w)
+    sums = [*sum_over_line(*(p.reshape(3 * chunk, width) for p in parts))]
+    part = kernel_call(
+        project_body,
+        [shaped((ndp, 3, chunk, width), BF16)],
+        grid=(3,),
+        in_specs=project_specs,
+        out_specs=[pl.BlockSpec((ndp, 1, chunk, width), lambda i: (0, i, 0, 0))],
+        scratch=[pltpu.VMEM((8, width), BF16)],
+        flops=mm_flops,
+        nbytes=mm_bytes,
+    )(x1, w)[0]
+    sums.append(lax.psum_scatter(part.reshape(ndp, 3 * chunk, width), "dp", scatter_dimension=0))
 
     extra = -(-(groups + 3 * nshort) // 16) * 16
     half = pl.BlockSpec((groups, ntaps, 2 * ntaps), lambda i: (0, 0, 0))
@@ -335,7 +348,7 @@
             shaped((seq, width), BF16),
         ),
         grid=(1,),
-        in_specs=[whole(3 * chunk, width)] * 6
+        in_specs=[whole(3 * chunk, width)] * 4
         + [whole(3 * nshort, width), half, other, whole(seq, width)],
         out_specs=(whole(3 * chunk, width), whole(3 * chunk + extra, width), whole(seq, width)),
         scratch=[pltpu.VMEM((3 * seq, width), F32), pltpu.VMEM((3 * seq, width), BF16)],
@@ -344,23 +357,25 @@
     )(*sums, sf, bands, bands, upstream)
     mixed = lax.all_to_all(mixed, "dp", split_axis=0, concat_axis=1, tiled=True)
 
+    gathered = lax.all_gather(grad_near, "dp", axis=0)
     block = shaped((rows, dcol), BF16)
     all_shape = shaped((3, chunk, local), BF16)
+    pieces = gather_over_line(grad_other)
+    gathered, *pieces = lax.optimization_barrier((gathered, *pieces))
     out_first, all_other, small = kernel_call(
         first_grad_body,
         (shaped((nblocks, ncol, rows, dcol), BF16), all_shape, shaped((ndp, extra, width), BF16)),
         scratch=[pltpu.VMEM((ndp, 3 * chunk + extra, width), BF16)],
-        flops=mm_flops,
-        nbytes=mm_bytes,
-    )(*gather_over_line(grad_other), w)
+        flops=0,
+        nbytes=0,
+    )(*pieces, w)
     from_partner = lax.ppermute(out_first, "row", partner)
     all_near, *blocks = kernel_call(
         second_grad_body,
         [all_shape] + [block] * len(places),
-        scratch=[pltpu.VMEM((ndp, 3 * chunk, width), BF16)],
         flops=mm_flops,
         nbytes=mm_bytes,
-    )(*gather_over_line(grad_near), w, from_partner)
+    )(gathered, w, from_partner)
     arrived = blocks[0].astype(F32)
     for (dy, dx), sent in zip(places[1:], blocks[1:]):
         back = [(b, a) for a, b in offset(dy, dx)]

time: 187 us -> 203 us (1.086)
  the two profiles are of different devices: /device:TPU:4 before, /device:TPU:1 now
where the time goes in v4:
time: 203 us; the launch traced here: 201 us
  waiting for transfers between devices  68.3 us (34%)
  starting transfers between devices  39.8 us (20%)
  local copies, waits for them, and re-layouts  31.9 us (16%)
  blocking collectives  21.7 us (11%)
  Pallas kernels  19.5 us (10%)
  between operations  14.2 us (7%)
  other arithmetic  5.15 us (3%)
    unnamed x71, local copies, waits for them, and re-layouts  29.1 us
    ppermute x1, waiting for transfers between devices, gather_over_line(): far_after = lax.ppermute(after, 'dp', [(a + 1, a) for a in range(ndp // 2)])  17.5 us
    all_to_all x1, blocking collectives, move_activations(): lax.all_to_all(grad_out, 'dp', split_axis=1, concat_axis=0, tiled=True)  11.8 us
    all_to_all x1, blocking collectives, move_activations(): mixed = lax.all_to_all(mixed, 'dp', split_axis=0, concat_axis=1, tiled=True)  9.87 us
    ppermute x1, waiting for transfers between devices, sum_over_line(): from_left = lax.ppermute(far, 'dp', [(a, a + 1) for a in range(ndp // 2)])  9.43 us
    ppermute x1, waiting for transfers between devices, sum_over_line(): lax.ppermute(left + from_right, 'dp', [(a, (a - 1) % ndp) for a in range(...  8.31 us
    ppermute x1, waiting for transfers between devices, gather_over_line(): after = lax.ppermute(own, 'dp', [(a, (a - 1) % ndp) for a in range(ndp)])  7.89 us
    ppermute x3, waiting for transfers between devices, move_activations(): arrived += lax.ppermute(sent, ('row', 'col'), back).astype(F32)  7.31 us
  transfers between devices with their start and end apart: 20, of which 13 were waited for; matrix products, arithmetic and copies ran while one was open for 4% of the time, Pallas kernels for 4%

profile of v4, /device:TPU:1, one launch (start us, length us, event | category | flops | bytes accessed | tf_op | source)
XLA Modules:
  0.0 200.5 jit_solution(7520897437372326382)
XLA Ops:
  7.2 4.7 %collective-permute-start = (bf16[192,512]{1,0:T(8,128)(2,1)}, bf16[192,512]{1,0:T(8,128)(2,1)S(1)}, u32[]{:S(2)}, u32[]{:S(2)}) collective-permute-start(bf16[192,512]{1,0:T(8,128)(2,1)} %param.5), channel_id=1, source_target_pairs={{0,0},{2,8},{4,16},{6,24},{8,2},{10,10},{12,18},{14,26},{16,4},{18... | collective-permute-start | bytes 589832 | tf_op jit(solution)/shard_map/ppermute | solution.py:289
  12.0 3.5 %collective-permute-done = bf16[192,512]{1,0:T(8,128)(2,1)S(1)} collective-permute-done((bf16[192,512]{1,0:T(8,128)(2,1)}, bf16[192,512]{1,0:T(8,128)(2,1)S(1)}, u32[]{:S(2)}, u32[]{:S(2)}) %collective-permute-start) | collective-permute-done | bytes 196640 | tf_op jit(solution)/shard_map/ppermute | solution.py:289
  15.5 6.5 %collective-permute-start.3 = (bf16[192,512]{1,0:T(8,128)(2,1)S(1)}, bf16[192,512]{1,0:T(8,128)(2,1)S(1)}, u32[]{:S(2)}, u32[]{:S(2)}) collective-permute-start(bf16[192,512]{1,0:T(8,128)(2,1)S(1)} %collective-permute-done), channel_id=1, source_target_pairs={{0,5},{1,4},{2,7},{3,6},{4,1},{5,0},{6,3},{7,2},{8,13},{9,12},{10,... | collective-permute-start | bytes 589832 | tf_op jit(solution)/shard_map/ppermute | solution.py:291
  22.3 2.8 %collective-permute-done.3 = bf16[192,512]{1,0:T(8,128)(2,1)S(1)} collective-permute-done((bf16[192,512]{1,0:T(8,128)(2,1)S(1)}, bf16[192,512]{1,0:T(8,128)(2,1)S(1)}, u32[]{:S(2)}, u32[]{:S(2)}) %collective-permute-start.3) | collective-permute-done | bytes 196640 | tf_op jit(solution)/shard_map/ppermute | solution.py:291
  28.0 5.8 %collective-permute-start.8 = (bf16[2,2,192,512]{3,2,1,0:T(8,128)(2,1)S(1)}, bf16[2,2,192,512]{3,2,1,0:T(8,128)(2,1)S(1)}, u32[]{:S(2)}, u32[]{:S(2)}) collective-permute-start(bf16[2,2,192,512]{3,2,1,0:T(8,128)(2,1)S(1)} %bitcast.39), channel_id=1, source_target_pairs={{0,2},{2,0},{4,6},{6,4},{1,3},{3,1},{5,7},{7,5},{8,10},{10,8},{12,... | collective-permute-start | bytes 2359304 | tf_op jit(solution)/shard_map/ppermute | solution.py:294
  40.8 11.8 %all_to_all.38 = bf16[192,4,128]{2,0,1:T(8,128)(2,1)S(1)} all-to-all(bf16[192,4,128]{2,0,1:T(8,128)(2,1)S(1)} %copy_bitcast_fusion.1), channel_id=1, replica_groups=mesh['dp'=4,'row'=4,'col'=2] {'dp'}, dimensions={1} | all-to-all | bytes 393216 | tf_op jit(solution)/shard_map/all_to_all | solution.py:292
  53.8 2.7 %shard_map.92 = (bf16[3,384,128]{2,1,0:T(8,128)(2,1)S(1)}, bf16[3,384,128]{2,1,0:T(8,128)(2,1)S(1)}, bf16[3,384,128]{2,1,0:T(8,128)(2,1)}, bf16[3,384,128]{2,1,0:T(8,128)(2,1)S(1)}) custom-call(bf16[2,2,192,512]{3,2,1,0:T(8,128)(2,1)S(1)} %bitcast.40, bf16[3,1024,512]{2,1,0:T(8,128)(2,1)S(1)} %bitcast.35), custom_call_target="tpu_custom_call" | custom-call | flops 1207959552 | bytes 5111808 | tf_op jit(solution)/shard_map/pallas_call | solution.py:316
  58.7 4.1 %collective-permute-start.4 = (bf16[1152,128]{1,0:T(8,128)(2,1)}, bf16[1152,128]{1,0:T(8,128)(2,1)}, u32[]{:S(2)}, u32[]{:S(2)}) collective-permute-start(bf16[1152,128]{1,0:T(8,128)(2,1)} %bitcast.10), channel_id=1, source_target_pairs={{0,8},{8,16},{1,9},{9,17},{2,10},{10,18},{3,11},{11,19},{4,12},{12... | collective-permute-start | bytes 884744 | tf_op jit(solution)/shard_map/ppermute | solution.py:250
  63.5 9.4 %collective-permute-done.4 = bf16[1152,128]{1,0:T(8,128)(2,1)} collective-permute-done((bf16[1152,128]{1,0:T(8,128)(2,1)}, bf16[1152,128]{1,0:T(8,128)(2,1)}, u32[]{:S(2)}, u32[]{:S(2)}) %collective-permute-start.4) | collective-permute-done | bytes 294944 | tf_op jit(solution)/shard_map/ppermute | solution.py:250
  74.7 3.3 %collective-permute-start.5 = (bf16[1152,128]{1,0:T(8,128)(2,1)}, bf16[1152,128]{1,0:T(8,128)(2,1)}, u32[]{:S(2)}, u32[]{:S(2)}) collective-permute-start(bf16[1152,128]{1,0:T(8,128)(2,1)} %bitcast_add_fusion.1), channel_id=1, source_target_pairs={{0,8},{8,16},{16,24},{24,0},{1,9},{9,17},{17,25},{25,1},{2,10},{10... | collective-permute-start | bytes 884744 | tf_op jit(solution)/shard_map/ppermute | solution.py:252
  83.6 8.3 %collective-permute-done.7.refs_2_ = bf16[1152,128]{1,0:T(8,128)(2,1)} collective-permute-done((bf16[1152,128]{1,0:T(8,128)(2,1)}, bf16[1152,128]{1,0:T(8,128)(2,1)}, u32[]{:S(2)}, u32[]{:S(2)}) %collective-permute-start.7) | collective-permute-done | bytes 294944 | tf_op jit(solution)/shard_map/ppermute | solution.py:253
  95.1 4.0 %shard_map.95 = (bf16[1152,128]{1,0:T(8,128)(2,1)S(1)}, bf16[1184,128]{1,0:T(8,128)(2,1)S(1)}, bf16[768,128]{1,0:T(8,128)(2,1)S(1)}) custom-call(bf16[1152,128]{1,0:T(8,128)(2,1)S(1)} %bitcast.46, bf16[1152,128]{1,0:T(8,128)(2,1)} %collective-permute-done.5.refs_1_, bf16[1152,128]{1,0:T(8,128)(2,1)} %collective-permute-done.7.refs_2_, ...), custom_call_target="tpu_custom_call" | custom-call | flops 1207959552 | bytes 2752512 | tf_op jit(solution)/shard_map/pallas_call | solution.py:343
  101.2 3.3 %collective-permute-start.10 = (bf16[1184,128]{1,0:T(8,128)(2,1)}, bf16[1184,128]{1,0:T(8,128)(2,1)S(1)}, u32[]{:S(2)}, u32[]{:S(2)}) collective-permute-start(bf16[1184,128]{1,0:T(8,128)(2,1)} %copy-done.16), channel_id=1, source_target_pairs={{0,24},{8,0},{16,8},{24,16},{1,25},{9,1},{17,9},{25,17},{2,26},{10... | collective-permute-start | bytes 909320 | tf_op jit(solution)/shard_map/ppermute | solution.py:260
  104.5 7.0 %collective-permute-done.9.before = bf16[1184,128]{1,0:T(8,128)(2,1)S(1)} collective-permute-done((bf16[1184,128]{1,0:T(8,128)(2,1)}, bf16[1184,128]{1,0:T(8,128)(2,1)S(1)}, u32[]{:S(2)}, u32[]{:S(2)}) %collective-permute-start.9) | collective-permute-done | bytes 303136 | tf_op jit(solution)/shard_map/ppermute | solution.py:259
  112.8 7.9 %collective-permute-done.10.after = bf16[1184,128]{1,0:T(8,128)(2,1)S(1)} collective-permute-done((bf16[1184,128]{1,0:T(8,128)(2,1)}, bf16[1184,128]{1,0:T(8,128)(2,1)S(1)}, u32[]{:S(2)}, u32[]{:S(2)}) %collective-permute-start.10) | collective-permute-done | bytes 303136 | tf_op jit(solution)/shard_map/ppermute | solution.py:260
  123.5 17.5 %collective-permute-done.12.far_after = bf16[1184,128]{1,0:T(8,128)(2,1)S(1)} collective-permute-done((bf16[1184,128]{1,0:T(8,128)(2,1)S(1)}, bf16[1184,128]{1,0:T(8,128)(2,1)S(1)}, u32[]{:S(2)}, u32[]{:S(2)}) %collective-permute-start.12) | collective-permute-done | bytes 303136 | tf_op jit(solution)/shard_map/ppermute | solution.py:262
  146.5 2.4 %shard_map.96 = (bf16[2,2,192,512]{3,2,1,0:T(8,128)(2,1)}, bf16[3,384,512]{2,1,0:T(8,128)(2,1)S(1)}, bf16[4,32,128]{2,1,0:T(8,128)(2,1)S(1)}) custom-call(bf16[1184,128]{1,0:T(8,128)(2,1)S(1)} %copy-done.17, bf16[1184,128]{1,0:T(8,128)(2,1)S(1)} %copy-done.19, bf16[1184,128]{1,0:T(8,128)(2,1)S(1)} %copy-done.21, bf16[1184,128]{1,0:T(8,128)(2,1)S(1)} %copy-done.23, ...), custom_call_target="tpu_custom_call" | custom-call | tf_op jit(solution)/shard_map/pallas_call | solution.py:365
  152.0 9.9 %all_to_all.39 = bf16[4,192,128]{2,1,0:T(8,128)(2,1)S(1)} all-to-all(bf16[4,192,128]{2,1,0:T(8,128)(2,1)S(1)} %bitcast.44), channel_id=1, replica_groups=mesh['dp'=4,'row'=4,'col'=2] {'dp'}, dimensions={0} | all-to-all | bytes 393216 | tf_op jit(solution)/shard_map/all_to_all | solution.py:358
  165.2 3.3 %shard_map.97 = (bf16[3,384,512]{2,1,0:T(8,128)(2,1)S(1)}, bf16[192,512]{1,0:T(8,128)(2,1)S(1)}, bf16[192,512]{1,0:T(8,128)(2,1)}, bf16[192,512]{1,0:T(8,128)(2,1)}, bf16[192,512]{1,0:T(8,128)(2,1)}) custom-call(bf16[4,1152,128]{2,1,0:T(8,128)(2,1)S(1)} %bitcast.42, bf16[3,1024,512]{2,1,0:T(8,128)(2,1)S(1)} %bitcast.37, ...), custom_call_target="tpu_custom_call" | custom-call | flops 1207959552 | bytes 5111808 | tf_op jit(solution)/shard_map/pallas_call | solution.py:373
  170.0 2.2 %collective-permute-start.14 = (bf16[192,512]{1,0:T(8,128)(2,1)}, bf16[192,512]{1,0:T(8,128)(2,1)S(1)}, u32[]{:S(2)}, u32[]{:S(2)}) collective-permute-start(bf16[192,512]{1,0:T(8,128)(2,1)} %get-tuple-element.49), channel_id=1, source_target_pairs={{1,0},{0,1},{3,2},{2,3},{5,4},{4,5},{7,6},{6,7},{9,8},{8,9},{11,10... | collective-permute-start | bytes 589832 | tf_op jit(solution)/shard_map/ppermute | solution.py:382
  172.8 2.4 %collective-permute-done.16 = bf16[192,512]{1,0:T(8,128)(2,1)S(1)} collective-permute-done((bf16[192,512]{1,0:T(8,128)(2,1)}, bf16[192,512]{1,0:T(8,128)(2,1)S(1)}, u32[]{:S(2)}, u32[]{:S(2)}) %collective-permute-start.16) | collective-permute-done | bytes 196640 | tf_op jit(solution)/shard_map/ppermute | solution.py:382
  175.2 4.9 %collective-permute-done.15 = bf16[192,512]{1,0:T(8,128)(2,1)S(1)} collective-permute-done((bf16[192,512]{1,0:T(8,128)(2,1)}, bf16[192,512]{1,0:T(8,128)(2,1)S(1)}, u32[]{:S(2)}, u32[]{:S(2)}) %collective-permute-start.15) | collective-permute-done | bytes 196640 | tf_op jit(solution)/shard_map/ppermute | solution.py:382
  180.2 4.4 %collective-permute-start.17 = (bf16[192,512]{1,0:T(8,128)(2,1)S(1)}, bf16[192,512]{1,0:T(8,128)(2,1)S(1)}, u32[]{:S(2)}, u32[]{:S(2)}) collective-permute-start(bf16[192,512]{1,0:T(8,128)(2,1)S(1)} %add_convert_fusion), channel_id=1, source_target_pairs={{0,0},{2,8},{4,16},{6,24},{8,2},{10,10},{12,18},{14,26},{16,4},{18... | collective-permute-start | bytes 589832 | tf_op jit(solution)/shard_map/ppermute | solution.py:383
  188.3 4.7 %shard_map.98 = f32[3,1024,512]{2,1,0:T(8,128)} custom-call(bf16[2,2,192,512]{3,2,1,0:T(8,128)(2,1)S(1)} %bitcast.41, bf16[2,2,192,512]{3,2,1,0:T(8,128)(2,1)S(1)} %copy-done.5, bf16[3,384,512]{2,1,0:T(8,128)(2,1)S(1)} %copy-done.12, bf16[3,384,512]{2,1,0:T(8,128)(2,1)S(1)} %copy-done.10), custom_call_target="tpu_custom_call" | custom-call | flops 2415919104 | bytes 10223616 | tf_op jit(solution)/shard_map/pallas_call | solution.py:387
  (117 shorter events, 49.6 us)
Async XLA Ops:
  7.2 33.6 %copy-start = (bf16[192,512]{1,0:T(8,128)(2,1)S(1)}, bf16[192,512]{1,0:T(8,128)(2,1)}, u32[]{:S(2)}) copy-start(bf16[192,512]{1,0:T(8,128)(2,1)} %param.9) | copy-start | bytes 589828
  7.2 84.7 %reduce-scatter.2.cloned.1.call-start = ((), (), s32[]{:S(2)}) async-start(), calls=%async_computation.3 | async-start | bytes 1474560 | tf_op jit(solution)/shard_map/reduce_scatter | solution.py:337
  7.2 8.3 %collective-permute-start = (bf16[192,512]{1,0:T(8,128)(2,1)}, bf16[192,512]{1,0:T(8,128)(2,1)S(1)}, u32[]{:S(2)}, u32[]{:S(2)}) collective-permute-start(bf16[192,512]{1,0:T(8,128)(2,1)} %param.5), channel_id=1, source_target_pairs={{0,0},{2,8},{4,16},{6,24},{8,2},{10,10},{12,18},{14,26},{16,4},{18... | collective-permute-start | bytes 589832 | tf_op jit(solution)/shard_map/ppermute | solution.py:289
  15.5 9.6 %collective-permute-start.3 = (bf16[192,512]{1,0:T(8,128)(2,1)S(1)}, bf16[192,512]{1,0:T(8,128)(2,1)S(1)}, u32[]{:S(2)}, u32[]{:S(2)}) collective-permute-start(bf16[192,512]{1,0:T(8,128)(2,1)S(1)} %collective-permute-done), channel_id=1, source_target_pairs={{0,5},{1,4},{2,7},{3,6},{4,1},{5,0},{6,3},{7,2},{8,13},{9,12},{10,... | collective-permute-start | bytes 589832 | tf_op jit(solution)/shard_map/ppermute | solution.py:291
  22.0 5.2 %collective-permute-start.2 = (bf16[192,512]{1,0:T(8,128)(2,1)S(1)}, bf16[192,512]{1,0:T(8,128)(2,1)S(1)}, u32[]{:S(2)}, u32[]{:S(2)}) collective-permute-start(bf16[192,512]{1,0:T(8,128)(2,1)S(1)} %collective-permute-done), channel_id=1, source_target_pairs={{0,4},{1,5},{2,6},{3,7},{4,0},{5,1},{6,2},{7,3},{8,12},{9,13},{10,... | collective-permute-start | bytes 589832 | tf_op jit(solution)/shard_map/ppermute | solution.py:291
  22.0 5.9 %collective-permute-start.1 = (bf16[192,512]{1,0:T(8,128)(2,1)S(1)}, bf16[192,512]{1,0:T(8,128)(2,1)S(1)}, u32[]{:S(2)}, u32[]{:S(2)}) collective-permute-start(bf16[192,512]{1,0:T(8,128)(2,1)S(1)} %collective-permute-done), channel_id=1, source_target_pairs={{0,1},{1,0},{2,3},{3,2},{4,5},{5,4},{6,7},{7,6},{8,9},{9,8},{10,11... | collective-permute-start | bytes 589832 | tf_op jit(solution)/shard_map/ppermute | solution.py:291
  28.0 7.7 %collective-permute-start.8 = (bf16[2,2,192,512]{3,2,1,0:T(8,128)(2,1)S(1)}, bf16[2,2,192,512]{3,2,1,0:T(8,128)(2,1)S(1)}, u32[]{:S(2)}, u32[]{:S(2)}) collective-permute-start(bf16[2,2,192,512]{3,2,1,0:T(8,128)(2,1)S(1)} %bitcast.39), channel_id=1, source_target_pairs={{0,2},{2,0},{4,6},{6,4},{1,3},{3,1},{5,7},{7,5},{8,10},{10,8},{12,... | collective-permute-start | bytes 2359304 | tf_op jit(solution)/shard_map/ppermute | solution.py:294
  37.8 14.8 %copy-start.2 = (bf16[1024,3,512]{2,0,1:T(8,128)(2,1)S(1)}, bf16[1024,3,512]{2,0,1:T(8,128)(2,1)}, u32[]{:S(2)}) copy-start(bf16[1024,3,512]{2,0,1:T(8,128)(2,1)} %param.6) | copy-start | bytes 9437188
  40.7 101.0 %all-gather.3.cloned.1.call-start = ((), (), s32[]{:S(2)}) async-start(), calls=%async_computation.4 | async-start | bytes 1474560 | tf_op jit(solution)/shard_map/all_gather | solution.py:360
  58.7 14.2 %collective-permute-start.4 = (bf16[1152,128]{1,0:T(8,128)(2,1)}, bf16[1152,128]{1,0:T(8,128)(2,1)}, u32[]{:S(2)}, u32[]{:S(2)}) collective-permute-start(bf16[1152,128]{1,0:T(8,128)(2,1)} %bitcast.10), channel_id=1, source_target_pairs={{0,8},{8,16},{1,9},{9,17},{2,10},{10,18},{3,11},{11,19},{4,12},{12... | collective-permute-start | bytes 884744 | tf_op jit(solution)/shard_map/ppermute | solution.py:250
  62.8 15.2 %collective-permute-start.6 = (bf16[1152,128]{1,0:T(8,128)(2,1)}, bf16[1152,128]{1,0:T(8,128)(2,1)S(1)}, u32[]{:S(2)}, u32[]{:S(2)}) collective-permute-start(bf16[1152,128]{1,0:T(8,128)(2,1)} %bitcast.10), channel_id=1, source_target_pairs={{16,8},{24,16},{17,9},{25,17},{18,10},{26,18},{19,11},{27,19},{20,... | collective-permute-start | bytes 884744 | tf_op jit(solution)/shard_map/ppermute | solution.py:251
  74.7 8.9 %collective-permute-start.5 = (bf16[1152,128]{1,0:T(8,128)(2,1)}, bf16[1152,128]{1,0:T(8,128)(2,1)}, u32[]{:S(2)}, u32[]{:S(2)}) collective-permute-start(bf16[1152,128]{1,0:T(8,128)(2,1)} %bitcast_add_fusion.1), channel_id=1, source_target_pairs={{0,8},{8,16},{16,24},{24,0},{1,9},{9,17},{17,25},{25,1},{2,10},{10... | collective-permute-start | bytes 884744 | tf_op jit(solution)/shard_map/ppermute | solution.py:252
  79.7 12.2 %collective-permute-start.7 = (bf16[1152,128]{1,0:T(8,128)(2,1)}, bf16[1152,128]{1,0:T(8,128)(2,1)}, u32[]{:S(2)}, u32[]{:S(2)}) collective-permute-start(bf16[1152,128]{1,0:T(8,128)(2,1)} %bitcast_add_fusion), channel_id=1, source_target_pairs={{0,24},{8,0},{16,8},{24,16},{1,25},{9,1},{17,9},{25,17},{2,26},{10... | collective-permute-start | bytes 884744 | tf_op jit(solution)/shard_map/ppermute | solution.py:253
  101.2 10.3 %collective-permute-start.9 = (bf16[1184,128]{1,0:T(8,128)(2,1)}, bf16[1184,128]{1,0:T(8,128)(2,1)S(1)}, u32[]{:S(2)}, u32[]{:S(2)}) collective-permute-start(bf16[1184,128]{1,0:T(8,128)(2,1)} %copy-done.16), channel_id=1, source_target_pairs={{0,8},{8,16},{16,24},{24,0},{1,9},{9,17},{17,25},{25,1},{2,10},{10... | collective-permute-start | bytes 909320 | tf_op jit(solution)/shard_map/ppermute | solution.py:259
  101.2 19.5 %collective-permute-start.10 = (bf16[1184,128]{1,0:T(8,128)(2,1)}, bf16[1184,128]{1,0:T(8,128)(2,1)S(1)}, u32[]{:S(2)}, u32[]{:S(2)}) collective-permute-start(bf16[1184,128]{1,0:T(8,128)(2,1)} %copy-done.16), channel_id=1, source_target_pairs={{0,24},{8,0},{16,8},{24,16},{1,25},{9,1},{17,9},{25,17},{2,26},{10... | collective-permute-start | bytes 909320 | tf_op jit(solution)/shard_map/ppermute | solution.py:260
  111.4 11.3 %collective-permute-start.11 = (bf16[1184,128]{1,0:T(8,128)(2,1)S(1)}, bf16[1184,128]{1,0:T(8,128)(2,1)S(1)}, u32[]{:S(2)}, u32[]{:S(2)}) collective-permute-start(bf16[1184,128]{1,0:T(8,128)(2,1)S(1)} %collective-permute-done.9.before), channel_id=1, source_target_pairs={{8,16},{16,24},{9,17},{17,25},{10,18},{18,26},{11,19},{19,27},{12,... | collective-permute-start | bytes 909320 | tf_op jit(solution)/shard_map/ppermute | solution.py:261
  120.7 20.2 %collective-permute-start.12 = (bf16[1184,128]{1,0:T(8,128)(2,1)S(1)}, bf16[1184,128]{1,0:T(8,128)(2,1)S(1)}, u32[]{:S(2)}, u32[]{:S(2)}) collective-permute-start(bf16[1184,128]{1,0:T(8,128)(2,1)S(1)} %collective-permute-done.10.after), channel_id=1, source_target_pairs={{8,0},{16,8},{9,1},{17,9},{10,2},{18,10},{11,3},{19,11},{12,4},{20... | collective-permute-start | bytes 909320 | tf_op jit(solution)/shard_map/ppermute | solution.py:262
  150.0 14.0 %collective-permute-start.13 = (bf16[2,2,192,512]{3,2,1,0:T(8,128)(2,1)}, bf16[2,2,192,512]{3,2,1,0:T(8,128)(2,1)}, u32[]{:S(2)}, u32[]{:S(2)}) collective-permute-start(bf16[2,2,192,512]{3,2,1,0:T(8,128)(2,1)} %get-tuple-element.47), channel_id=1, source_target_pairs={{0,2},{2,0},{4,6},{6,4},{1,3},{3,1},{5,7},{7,5},{8,10},{10,8},{12,... | collective-permute-start | bytes 2359304 | tf_op jit(solution)/shard_map/ppermute | solution.py:372
  165.2 7.0 %copy-start.34 = (f32[4,32,128]{2,1,0:T(8,128)S(1)}, f32[4,32,128]{2,1,0:T(8,128)}, u32[]{:S(2)}) copy-start(f32[4,32,128]{2,1,0:T(8,128)} %convert_element_type.27) | copy-start | bytes 196612
  169.5 15.2 %copy-start.8 = (bf16[4,192,512]{2,1,0:T(8,128)(2,1)S(1)}, bf16[4,192,512]{2,1,0:T(8,128)(2,1)}, u32[]{:S(2)}) copy-start(bf16[4,192,512]{2,1,0:T(8,128)(2,1)} %copy-done.6) | copy-start | bytes 2359300
  169.5 5.7 %collective-permute-start.16 = (bf16[192,512]{1,0:T(8,128)(2,1)}, bf16[192,512]{1,0:T(8,128)(2,1)S(1)}, u32[]{:S(2)}, u32[]{:S(2)}) collective-permute-start(bf16[192,512]{1,0:T(8,128)(2,1)} %get-tuple-element.51), channel_id=1, source_target_pairs={{5,0},{4,1},{7,2},{6,3},{1,4},{0,5},{3,6},{2,7},{13,8},{12,9},{15,... | collective-permute-start | bytes 589832 | tf_op jit(solution)/shard_map/ppermute | solution.py:382
  169.7 10.4 %collective-permute-start.15 = (bf16[192,512]{1,0:T(8,128)(2,1)}, bf16[192,512]{1,0:T(8,128)(2,1)S(1)}, u32[]{:S(2)}, u32[]{:S(2)}) collective-permute-start(bf16[192,512]{1,0:T(8,128)(2,1)} %get-tuple-element.50), channel_id=1, source_target_pairs={{4,0},{5,1},{6,2},{7,3},{0,4},{1,5},{2,6},{3,7},{12,8},{13,9},{14,... | collective-permute-start | bytes 589832 | tf_op jit(solution)/shard_map/ppermute | solution.py:382
  170.0 10.2 %collective-permute-start.14 = (bf16[192,512]{1,0:T(8,128)(2,1)}, bf16[192,512]{1,0:T(8,128)(2,1)S(1)}, u32[]{:S(2)}, u32[]{:S(2)}) collective-permute-start(bf16[192,512]{1,0:T(8,128)(2,1)} %get-tuple-element.49), channel_id=1, source_target_pairs={{1,0},{0,1},{3,2},{2,3},{5,4},{4,5},{7,6},{6,7},{9,8},{8,9},{11,10... | collective-permute-start | bytes 589832 | tf_op jit(solution)/shard_map/ppermute | solution.py:382
  180.2 12.8 %collective-permute-start.17 = (bf16[192,512]{1,0:T(8,128)(2,1)S(1)}, bf16[192,512]{1,0:T(8,128)(2,1)S(1)}, u32[]{:S(2)}, u32[]{:S(2)}) collective-permute-start(bf16[192,512]{1,0:T(8,128)(2,1)S(1)} %add_convert_fusion), channel_id=1, source_target_pairs={{0,0},{2,8},{4,16},{6,24},{8,2},{10,10},{12,18},{14,26},{16,4},{18... | collective-permute-start | bytes 589832 | tf_op jit(solution)/shard_map/ppermute | solution.py:383
  (31 other events, 37.9 us)
Sparse Core Ops, SparseCore 0:
  40.8 33.1 reduce-scatter.1
  101.3 37.7 all-gather.2

commit v5 on v3

--- a/solution.py
+++ b/solution.py
@@ -7,7 +7,7 @@
 from jax.experimental.pallas import tpu as pltpu
 from jax.sharding import PartitionSpec as P
 
-VMEM_BYTES = 48 * 2**20
+VMEM_BYTES = 20 * 2**20
 F32 = jnp.float32
 BF16 = jnp.bfloat16
 
@@ -16,7 +16,7 @@
     kwargs = {}
     if grid is not None:
         kwargs = dict(grid=grid, in_specs=in_specs, out_specs=out_specs)
-    return pl.pallas_call(
+    call = pl.pallas_call(
         body,
         out_shape=outs,
         scratch_shapes=scratch,
@@ -24,10 +24,19 @@
         cost_estimate=pl.CostEstimate(flops=flops, bytes_accessed=nbytes, transcendentals=0),
         **kwargs,
     )
+    return lambda *args: call(*(pltpu.with_memory_space_constraint(arg, pltpu.VMEM) for arg in args))
 
 
 def shaped(shape, dtype):
     return jax.ShapeDtypeStruct(shape, dtype)
+
+
+def near_core(shape, dtype):
+    return pltpu.VMEM(shape, dtype)
+
+
+def bring_body(far_ref, near_ref):
+    pltpu.sync_copy(far_ref, near_ref)
 
 
 def bands_body(base_ref, out_ref):
@@ -113,10 +122,8 @@
         out_ref[:, dx] = total.reshape(nblocks, rows, depth).astype(BF16)
 
 
-def second_grad_body(own, before, after, far_before, far_after, w_ref, other_ref, all_ref, *refs):
-    *out_refs, held = refs
+def second_grad_body(held, w_ref, other_ref, all_ref, *out_refs):
     nblocks, ncol, rows, depth = other_ref.shape
-    assemble((own, before, after, far_before, far_after), held, held.shape[0])
     for dx, total in input_grads(held, w_ref, all_ref, ncol):
         for block in range(nblocks):
             both = total[block * rows : (block + 1) * rows] + other_ref[block, dx].astype(F32)
@@ -287,10 +294,18 @@
 
     w = jnp.transpose(in_weight, (1, 0, 2))
     moved = lax.ppermute(tokens, ("dp", "row"), swap)
+    w = pl.pallas_call(
+        bring_body,
+        out_shape=near_core(w.shape, BF16),
+        in_specs=[pl.BlockSpec(memory_space=pl.ANY)],
+        compiler_params=pltpu.CompilerParams(vmem_limit_bytes=VMEM_BYTES),
+    )(w)
+    moved, grad_out, w = lax.optimization_barrier((moved, grad_out, w))
     near = [moved] + [lax.ppermute(moved, ("row", "col"), offset(*p)) for p in places[1:]]
+    upstream = lax.all_to_all(grad_out, "dp", split_axis=1, concat_axis=0, tiled=True)
+    upstream, *near = lax.optimization_barrier((upstream, *near))
     x0 = jnp.stack(near).reshape(nblocks, ncol, rows, dcol)
     x1 = lax.ppermute(x0, "row", partner)
-    upstream = lax.all_to_all(grad_out, "dp", split_axis=1, concat_axis=0, tiled=True)
 
     sf = lax.dynamic_slice_in_dim(short_filter, z * width, width, 2).reshape(3 * nshort, width)
     lf = lax.dynamic_slice_in_dim(long_filter, z * groups, groups, 0).astype(F32)
@@ -302,7 +317,7 @@
         ],
         axis=0,
     )
-    bands = kernel_call(bands_body, shaped((2 * groups, ntaps, 2 * ntaps), BF16))(bases)
+    bands = kernel_call(bands_body, near_core((2 * groups, ntaps, 2 * ntaps), BF16))(bases)
 
     mm_flops = seq * drow * 3 * local
     mm_bytes = seq * drow + 6 * drow * local + 3 * seq * local
@@ -310,7 +325,7 @@
     for x in (x0, x1):
         parts = kernel_call(
             project_body,
-            [shaped((3, chunk, width), BF16)] * ndp,
+            [near_core((3, chunk, width), BF16)] * ndp,
             grid=(3,),
             in_specs=[
                 pl.BlockSpec((nblocks, ncol, rows, dcol), lambda i: (0, 0, 0, 0)),
@@ -331,7 +346,7 @@
         functools.partial(middle_body, scale, nshort, nrow),
         (
             shaped((3 * chunk, width), BF16),
-            shaped((3 * chunk + extra, width), BF16),
+            near_core((3 * chunk + extra, width), BF16),
             shaped((seq, width), BF16),
         ),
         grid=(1,),
@@ -343,24 +358,25 @@
         nbytes=2 * width * seq * 14,
     )(*sums, sf, bands, bands, upstream)
     mixed = lax.all_to_all(mixed, "dp", split_axis=0, concat_axis=1, tiled=True)
-
-    block = shaped((rows, dcol), BF16)
-    all_shape = shaped((3, chunk, local), BF16)
+    mixed, *pieces = lax.optimization_barrier((mixed, *gather_over_line(grad_other)))
+    block = near_core((rows, dcol), BF16)
+    all_shape = near_core((3, chunk, local), BF16)
     out_first, all_other, small = kernel_call(
         first_grad_body,
-        (shaped((nblocks, ncol, rows, dcol), BF16), all_shape, shaped((ndp, extra, width), BF16)),
+        (near_core((nblocks, ncol, rows, dcol), BF16), all_shape, near_core((ndp, extra, width), BF16)),
         scratch=[pltpu.VMEM((ndp, 3 * chunk + extra, width), BF16)],
         flops=mm_flops,
         nbytes=mm_bytes,
-    )(*gather_over_line(grad_other), w)
+    )(*pieces, w)
+    gathered = lax.all_gather(grad_near, "dp", axis=0)
+    gathered, out_first = lax.optimization_barrier((gathered, out_first))
     from_partner = lax.ppermute(out_first, "row", partner)
     all_near, *blocks = kernel_call(
         second_grad_body,
         [all_shape] + [block] * len(places),
-        scratch=[pltpu.VMEM((ndp, 3 * chunk, width), BF16)],
         flops=mm_flops,
         nbytes=mm_bytes,
-    )(*gather_over_line(grad_near), w, from_partner)
+    )(gathered, w, from_partner)
     arrived = blocks[0].astype(F32)
     for (dy, dx), sent in zip(places[1:], blocks[1:]):
         back = [(b, a) for a, b in offset(dy, dx)]

time: 187 us -> 197 us (1.053)
  the two profiles are of different devices: /device:TPU:4 before, /device:TPU:1 now
where the time goes in v5:
time: 197 us; the launch traced here: 196 us
  waiting for transfers between devices  67.1 us (34%)
  starting transfers between devices  62.1 us (32%)
  Pallas kernels  24.2 us (12%)
  local copies, waits for them, and re-layouts  20.6 us (10%)
  between operations  14.2 us (7%)
  other arithmetic  7.78 us (4%)
    pallas_call x7, Pallas kernels, kernel_call(): call(*(pltpu.with_memory_space_constraint(arg, pltpu.VMEM) for arg in args))  24 us
    unnamed x45, local copies, waits for them, and re-layouts  17.1 us
    all_to_all x1, waiting for transfers between devices, move_activations(): mixed = lax.all_to_all(mixed, 'dp', split_axis=0, concat_axis=1, tiled=True)  16.4 us
    ppermute x1, waiting for transfers between devices, gather_over_line(): far_after = lax.ppermute(after, 'dp', [(a + 1, a) for a in range(ndp // 2)])  12.4 us
    all_to_all x1, starting transfers between devices, move_activations(): lax.all_to_all(grad_out, 'dp', split_axis=1, concat_axis=0, tiled=True)  11.6 us
    ppermute x2, waiting for transfers between devices, sum_over_line(): from_left = lax.ppermute(far, 'dp', [(a, a + 1) for a in range(ndp // 2)])  9.3 us
    ppermute x3, waiting for transfers between devices, move_activations(): lax.ppermute(moved, ('row', 'col'), offset(*p))  8.98 us
    ppermute x3, waiting for transfers between devices, move_activations(): arrived += lax.ppermute(sent, ('row', 'col'), back).astype(F32)  7.62 us
  transfers between devices with their start and end apart: 25, of which 15 were waited for; matrix products, arithmetic and copies ran while one was open for 4% of the time, Pallas kernels for 9%

profile of v5, /device:TPU:1, one launch (start us, length us, event | category | flops | bytes accessed | tf_op | source)
XLA Modules:
  0.0 196.0 jit_solution(7777687383845227974)
XLA Ops:
  7.2 4.7 %collective-permute-start = (bf16[192,512]{1,0:T(8,128)(2,1)}, bf16[192,512]{1,0:T(8,128)(2,1)}, u32[]{:S(2)}, u32[]{:S(2)}) collective-permute-start(bf16[192,512]{1,0:T(8,128)(2,1)} %param.5), channel_id=1, source_target_pairs={{0,0},{2,8},{4,16},{6,24},{8,2},{10,10},{12,18},{14,26},{16,4},{18... | collective-permute-start | bytes 589832 | tf_op jit(solution)/shard_map/ppermute | solution.py:296
  16.3 11.6 %all-to-all-start = ((bf16[192,4,128]{2,0,1:T(8,128)(2,1)}), bf16[192,4,128]{2,0,1:T(8,128)(2,1)S(1)}, u32[]{:S(2)}, u32[]{:S(2)}) async-start(bf16[192,4,128]{2,0,1:T(8,128)(2,1)} %copy_bitcast_fusion.1), calls=%async_computation | async-start | bytes 393216 | tf_op jit(solution)/shard_map/all_to_all | solution.py:305
  30.5 3.3 %collective-permute-done.1 = bf16[192,512]{1,0:T(8,128)(2,1)S(1)} collective-permute-done((bf16[192,512]{1,0:T(8,128)(2,1)}, bf16[192,512]{1,0:T(8,128)(2,1)S(1)}, u32[]{:S(2)}, u32[]{:S(2)}) %collective-permute-start.1) | collective-permute-done | bytes 196640 | tf_op jit(solution)/shard_map/ppermute | solution.py:304
  33.8 5.7 %collective-permute-done.2 = bf16[192,512]{1,0:T(8,128)(2,1)S(1)} collective-permute-done((bf16[192,512]{1,0:T(8,128)(2,1)}, bf16[192,512]{1,0:T(8,128)(2,1)S(1)}, u32[]{:S(2)}, u32[]{:S(2)}) %collective-permute-start.2) | collective-permute-done | bytes 196640 | tf_op jit(solution)/shard_map/ppermute | solution.py:304
  43.7 3.9 %shard_map.93 = (bf16[3,384,128]{2,1,0:T(8,128)(2,1)S(1)}, bf16[3,384,128]{2,1,0:T(8,128)(2,1)S(1)}, bf16[3,384,128]{2,1,0:T(8,128)(2,1)}, bf16[3,384,128]{2,1,0:T(8,128)(2,1)S(1)}) custom-call(bf16[2,2,192,512]{3,2,1,0:T(8,128)(2,1)} %bitcast.7.x_ref.x0_ref, bf16[3,1024,512]{2,1,0:T(8,128)(2,1)S(1)} %shard_map.92.w_ref), custom_call_target="tpu_custom_call" | custom-call | flops 1207959552 | bytes 5111808 | tf_op jit(solution)/shard_map/pallas_call | solution.py:27
  49.7 4.1 %collective-permute-start.4 = (bf16[1152,128]{1,0:T(8,128)(2,1)}, bf16[1152,128]{1,0:T(8,128)(2,1)}, u32[]{:S(2)}, u32[]{:S(2)}) collective-permute-start(bf16[1152,128]{1,0:T(8,128)(2,1)} %bitcast.10), channel_id=1, source_target_pairs={{0,8},{8,16},{1,9},{9,17},{2,10},{10,18},{3,11},{11,19},{4,12},{12... | collective-permute-start | bytes 884744 | tf_op jit(solution)/shard_map/ppermute | solution.py:257
  54.6 5.2 %collective-permute-done.4 = bf16[1152,128]{1,0:T(8,128)(2,1)} collective-permute-done((bf16[1152,128]{1,0:T(8,128)(2,1)}, bf16[1152,128]{1,0:T(8,128)(2,1)}, u32[]{:S(2)}, u32[]{:S(2)}) %collective-permute-start.4) | collective-permute-done | bytes 294944 | tf_op jit(solution)/shard_map/ppermute | solution.py:257
  63.8 3.2 %shard_map.94 = (bf16[3,384,128]{2,1,0:T(8,128)(2,1)S(1)}, bf16[3,384,128]{2,1,0:T(8,128)(2,1)S(1)}, bf16[3,384,128]{2,1,0:T(8,128)(2,1)S(1)}, bf16[3,384,128]{2,1,0:T(8,128)(2,1)S(1)}) custom-call(bf16[2,2,192,512]{3,2,1,0:T(8,128)(2,1)} %collective-permute-done.8.x_ref.x1_ref, bf16[3,1024,512]{2,1,0:T(8,128)(2,1)S(1)} %shard_map.92.w_ref), custom_call_target="tpu_custom_call" | custom-call | flops 1207959552 | bytes 5111808 | tf_op jit(solution)/shard_map/pallas_call | solution.py:27
  67.0 3.1 %collective-permute-start.9 = (bf16[1152,128]{1,0:T(8,128)(2,1)S(1)}, bf16[1152,128]{1,0:T(8,128)(2,1)S(1)}, u32[]{:S(2)}, u32[]{:S(2)}) collective-permute-start(bf16[1152,128]{1,0:T(8,128)(2,1)S(1)} %bitcast.42), channel_id=1, source_target_pairs={{0,8},{8,16},{1,9},{9,17},{2,10},{10,18},{3,11},{11,19},{4,12},{12... | collective-permute-start | bytes 884744 | tf_op jit(solution)/shard_map/ppermute | solution.py:257
  71.7 4.1 %collective-permute-done.9 = bf16[1152,128]{1,0:T(8,128)(2,1)S(1)} collective-permute-done((bf16[1152,128]{1,0:T(8,128)(2,1)S(1)}, bf16[1152,128]{1,0:T(8,128)(2,1)S(1)}, u32[]{:S(2)}, u32[]{:S(2)}) %collective-permute-start.9) | collective-permute-done | bytes 294944 | tf_op jit(solution)/shard_map/ppermute | solution.py:257
  79.6 4.5 %collective-permute-start.12 = (bf16[1152,128]{1,0:T(8,128)(2,1)}, bf16[1152,128]{1,0:T(8,128)(2,1)}, u32[]{:S(2)}, u32[]{:S(2)}) collective-permute-start(bf16[1152,128]{1,0:T(8,128)(2,1)} %bitcast_add_fusion), channel_id=1, source_target_pairs={{0,24},{8,0},{16,8},{24,16},{1,25},{9,1},{17,9},{25,17},{2,26},{10... | collective-permute-start | bytes 884744 | tf_op jit(solution)/shard_map/ppermute | solution.py:260
  86.4 4.2 %collective-permute-done.10.refs_4_ = bf16[1152,128]{1,0:T(8,128)(2,1)} collective-permute-done((bf16[1152,128]{1,0:T(8,128)(2,1)}, bf16[1152,128]{1,0:T(8,128)(2,1)}, u32[]{:S(2)}, u32[]{:S(2)}) %collective-permute-start.10) | collective-permute-done | bytes 294944 | tf_op jit(solution)/shard_map/ppermute | solution.py:259
  90.6 4.3 %collective-permute-done.12.refs_5_ = bf16[1152,128]{1,0:T(8,128)(2,1)} collective-permute-done((bf16[1152,128]{1,0:T(8,128)(2,1)}, bf16[1152,128]{1,0:T(8,128)(2,1)}, u32[]{:S(2)}, u32[]{:S(2)}) %collective-permute-start.12) | collective-permute-done | bytes 294944 | tf_op jit(solution)/shard_map/ppermute | solution.py:260
  96.8 4.2 %shard_map.96 = (bf16[1152,128]{1,0:T(8,128)(2,1)S(1)}, bf16[1184,128]{1,0:T(8,128)(2,1)S(1)}, bf16[768,128]{1,0:T(8,128)(2,1)S(1)}) custom-call(bf16[1152,128]{1,0:T(8,128)(2,1)S(1)} %bitcast.44, bf16[1152,128]{1,0:T(8,128)(2,1)} %collective-permute-done.5.refs_1_, bf16[1152,128]{1,0:T(8,128)(2,1)} %collective-permute-done.7.refs_2_, ...), custom_call_target="tpu_custom_call" | custom-call | flops 1207959552 | bytes 2752512 | tf_op jit(solution)/shard_map/pallas_call | solution.py:27
  104.2 3.1 %collective-permute-start.14 = (bf16[1184,128]{1,0:T(8,128)(2,1)}, bf16[1184,128]{1,0:T(8,128)(2,1)}, u32[]{:S(2)}, u32[]{:S(2)}) collective-permute-start(bf16[1184,128]{1,0:T(8,128)(2,1)} %copy-done.7), channel_id=1, source_target_pairs={{0,24},{8,0},{16,8},{24,16},{1,25},{9,1},{17,9},{25,17},{2,26},{10... | collective-permute-start | bytes 909320 | tf_op jit(solution)/shard_map/ppermute | solution.py:267
  107.2 3.4 %all-to-all-start.1 = ((bf16[4,192,128]{2,1,0:T(8,128)(2,1)}), bf16[4,192,128]{2,1,0:T(8,128)(2,1)S(1)}, u32[]{:S(2)}, u32[]{:S(2)}) async-start(bf16[4,192,128]{2,1,0:T(8,128)(2,1)} %bitcast.41), calls=%async_computation.1 | async-start | bytes 393216 | tf_op jit(solution)/shard_map/all_to_all | solution.py:360
  114.7 16.4 %all-to-all-done.1 = bf16[4,192,128]{2,1,0:T(8,128)(2,1)S(1)} async-done(((bf16[4,192,128]{2,1,0:T(8,128)(2,1)}), bf16[4,192,128]{2,1,0:T(8,128)(2,1)S(1)}, u32[]{:S(2)}, u32[]{:S(2)}) %all-to-all-start.1) | async-done | bytes 196640 | tf_op jit(solution)/shard_map/all_to_all | solution.py:360
  131.7 12.4 %collective-permute-done.16.far_after = bf16[1184,128]{1,0:T(8,128)(2,1)} collective-permute-done((bf16[1184,128]{1,0:T(8,128)(2,1)}, bf16[1184,128]{1,0:T(8,128)(2,1)}, u32[]{:S(2)}, u32[]{:S(2)}) %collective-permute-start.16) | collective-permute-done | bytes 303136 | tf_op jit(solution)/shard_map/ppermute | solution.py:269
  149.8 4.6 %collective-permute-start.17 = (bf16[2,2,192,512]{3,2,1,0:T(8,128)(2,1)}, bf16[2,2,192,512]{3,2,1,0:T(8,128)(2,1)}, u32[]{:S(2)}, u32[]{:S(2)}) collective-permute-start(bf16[2,2,192,512]{3,2,1,0:T(8,128)(2,1)} %copy-done.14), channel_id=1, source_target_pairs={{0,2},{2,0},{4,6},{6,4},{1,3},{3,1},{5,7},{7,5},{8,10},{10,8},{12,... | collective-permute-start | bytes 2359304 | tf_op jit(solution)/shard_map/ppermute | solution.py:373
  157.9 3.3 %shard_map.98 = (bf16[3,384,512]{2,1,0:T(8,128)(2,1)S(1)}, bf16[192,512]{1,0:T(8,128)(2,1)S(1)}, bf16[192,512]{1,0:T(8,128)(2,1)}, bf16[192,512]{1,0:T(8,128)(2,1)}, bf16[192,512]{1,0:T(8,128)(2,1)}) custom-call(bf16[4,1152,128]{2,1,0:T(8,128)(2,1)S(1)} %bitcast.39, bf16[3,1024,512]{2,1,0:T(8,128)(2,1)S(1)} %shard_map.92.w_ref, ...), custom_call_target="tpu_custom_call" | custom-call | flops 1207959552 | bytes 5111808 | tf_op jit(solution)/shard_map/pallas_call | solution.py:27
  165.5 4.0 %collective-permute-done.20 = bf16[192,512]{1,0:T(8,128)(2,1)S(1)} collective-permute-done((bf16[192,512]{1,0:T(8,128)(2,1)}, bf16[192,512]{1,0:T(8,128)(2,1)S(1)}, u32[]{:S(2)}, u32[]{:S(2)}) %collective-permute-start.20) | collective-permute-done | bytes 196640 | tf_op jit(solution)/shard_map/ppermute | solution.py:383
  169.5 3.4 %collective-permute-done.19 = bf16[192,512]{1,0:T(8,128)(2,1)S(1)} collective-permute-done((bf16[192,512]{1,0:T(8,128)(2,1)}, bf16[192,512]{1,0:T(8,128)(2,1)S(1)}, u32[]{:S(2)}, u32[]{:S(2)}) %collective-permute-start.19) | collective-permute-done | bytes 196640 | tf_op jit(solution)/shard_map/ppermute | solution.py:383
  173.2 6.7 %collective-permute-start.21 = (bf16[192,512]{1,0:T(8,128)(2,1)S(1)}, bf16[192,512]{1,0:T(8,128)(2,1)S(1)}, u32[]{:S(2)}, u32[]{:S(2)}) collective-permute-start(bf16[192,512]{1,0:T(8,128)(2,1)S(1)} %add_convert_fusion), channel_id=1, source_target_pairs={{0,0},{2,8},{4,16},{6,24},{8,2},{10,10},{12,18},{14,26},{16,4},{18... | collective-permute-start | bytes 589832 | tf_op jit(solution)/shard_map/ppermute | solution.py:384
  182.5 6.0 %shard_map.99 = f32[3,1024,512]{2,1,0:T(8,128)} custom-call(bf16[2,2,192,512]{3,2,1,0:T(8,128)(2,1)} %bitcast.7.x_ref.x0_ref, bf16[2,2,192,512]{3,2,1,0:T(8,128)(2,1)} %collective-permute-done.8.x_ref.x1_ref, bf16[3,384,512]{2,1,0:T(8,128)(2,1)S(1)} %copy-done.5, bf16[3,384,512]{2,1,0:T(8,128)(2,1)S(1)} %copy-done.3), custom_call_target="tpu_custom_call" | custom-call | flops 2415919104 | bytes 10223616 | tf_op jit(solution)/shard_map/pallas_call | solution.py:27
  (101 shorter events, 52.5 us)
Async XLA Ops:
  7.2 8.4 %collective-permute-start = (bf16[192,512]{1,0:T(8,128)(2,1)}, bf16[192,512]{1,0:T(8,128)(2,1)}, u32[]{:S(2)}, u32[]{:S(2)}) collective-permute-start(bf16[192,512]{1,0:T(8,128)(2,1)} %param.5), channel_id=1, source_target_pairs={{0,0},{2,8},{4,16},{6,24},{8,2},{10,10},{12,18},{14,26},{16,4},{18... | collective-permute-start | bytes 589832 | tf_op jit(solution)/shard_map/ppermute | solution.py:296
  16.3 23.9 %all-to-all-start = ((bf16[192,4,128]{2,0,1:T(8,128)(2,1)}), bf16[192,4,128]{2,0,1:T(8,128)(2,1)S(1)}, u32[]{:S(2)}, u32[]{:S(2)}) async-start(bf16[192,4,128]{2,0,1:T(8,128)(2,1)} %copy_bitcast_fusion.1), calls=%async_computation | async-start | bytes 393216 | tf_op jit(solution)/shard_map/all_to_all | solution.py:305
  27.9 121.9 %all-gather.3.cloned.1.call-start = ((), (), s32[]{:S(2)}) async-start(), calls=%async_computation.2 | async-start | bytes 1474560 | tf_op jit(solution)/shard_map/all_gather | solution.py:371
  29.1 10.4 %collective-permute-start.2 = (bf16[192,512]{1,0:T(8,128)(2,1)}, bf16[192,512]{1,0:T(8,128)(2,1)S(1)}, u32[]{:S(2)}, u32[]{:S(2)}) collective-permute-start(bf16[192,512]{1,0:T(8,128)(2,1)} %collective-permute-done), channel_id=1, source_target_pairs={{0,4},{1,5},{2,6},{3,7},{4,0},{5,1},{6,2},{7,3},{8,12},{9,13},{10,... | collective-permute-start | bytes 589832 | tf_op jit(solution)/shard_map/ppermute | solution.py:304
  29.1 11.1 %collective-permute-start.3 = (bf16[192,512]{1,0:T(8,128)(2,1)}, bf16[192,512]{1,0:T(8,128)(2,1)}, u32[]{:S(2)}, u32[]{:S(2)}) collective-permute-start(bf16[192,512]{1,0:T(8,128)(2,1)} %collective-permute-done), channel_id=1, source_target_pairs={{0,5},{1,4},{2,7},{3,6},{4,1},{5,0},{6,3},{7,2},{8,13},{9,12},{10,... | collective-permute-start | bytes 589832 | tf_op jit(solution)/shard_map/ppermute | solution.py:304
  42.4 21.4 %collective-permute-start.8 = (bf16[2,2,192,512]{3,2,1,0:T(8,128)(2,1)}, bf16[2,2,192,512]{3,2,1,0:T(8,128)(2,1)}, u32[]{:S(2)}, u32[]{:S(2)}) collective-permute-start(bf16[2,2,192,512]{3,2,1,0:T(8,128)(2,1)} %bitcast.7.x_ref.x0_ref), channel_id=1, source_target_pairs={{0,2},{2,0},{4,6},{6,4},{1,3},{3,1},{5,7},{7,5},{8,10},{10,8},{12,... | collective-permute-start | bytes 2359304 | tf_op jit(solution)/shard_map/ppermute | solution.py:308
  49.7 10.1 %collective-permute-start.4 = (bf16[1152,128]{1,0:T(8,128)(2,1)}, bf16[1152,128]{1,0:T(8,128)(2,1)}, u32[]{:S(2)}, u32[]{:S(2)}) collective-permute-start(bf16[1152,128]{1,0:T(8,128)(2,1)} %bitcast.10), channel_id=1, source_target_pairs={{0,8},{8,16},{1,9},{9,17},{2,10},{10,18},{3,11},{11,19},{4,12},{12... | collective-permute-start | bytes 884744 | tf_op jit(solution)/shard_map/ppermute | solution.py:257
  53.8 16.4 %collective-permute-start.6 = (bf16[1152,128]{1,0:T(8,128)(2,1)}, bf16[1152,128]{1,0:T(8,128)(2,1)S(1)}, u32[]{:S(2)}, u32[]{:S(2)}) collective-permute-start(bf16[1152,128]{1,0:T(8,128)(2,1)} %bitcast.10), channel_id=1, source_target_pairs={{16,8},{24,16},{17,9},{25,17},{18,10},{26,18},{19,11},{27,19},{20,... | collective-permute-start | bytes 884744 | tf_op jit(solution)/shard_map/ppermute | solution.py:258
  61.6 24.7 %collective-permute-start.5 = (bf16[1152,128]{1,0:T(8,128)(2,1)}, bf16[1152,128]{1,0:T(8,128)(2,1)}, u32[]{:S(2)}, u32[]{:S(2)}) collective-permute-start(bf16[1152,128]{1,0:T(8,128)(2,1)} %bitcast_add_fusion.3), channel_id=1, source_target_pairs={{0,8},{8,16},{16,24},{24,0},{1,9},{9,17},{17,25},{25,1},{2,10},{10... | collective-permute-start | bytes 884744 | tf_op jit(solution)/shard_map/ppermute | solution.py:259
  67.0 8.7 %collective-permute-start.9 = (bf16[1152,128]{1,0:T(8,128)(2,1)S(1)}, bf16[1152,128]{1,0:T(8,128)(2,1)S(1)}, u32[]{:S(2)}, u32[]{:S(2)}) collective-permute-start(bf16[1152,128]{1,0:T(8,128)(2,1)S(1)} %bitcast.42), channel_id=1, source_target_pairs={{0,8},{8,16},{1,9},{9,17},{2,10},{10,18},{3,11},{11,19},{4,12},{12... | collective-permute-start | bytes 884744 | tf_op jit(solution)/shard_map/ppermute | solution.py:257
  71.0 15.4 %collective-permute-start.7 = (bf16[1152,128]{1,0:T(8,128)(2,1)}, bf16[1152,128]{1,0:T(8,128)(2,1)}, u32[]{:S(2)}, u32[]{:S(2)}) collective-permute-start(bf16[1152,128]{1,0:T(8,128)(2,1)} %bitcast_add_fusion.2), channel_id=1, source_target_pairs={{0,24},{8,0},{16,8},{24,16},{1,25},{9,1},{17,9},{25,17},{2,26},{10... | collective-permute-start | bytes 884744 | tf_op jit(solution)/shard_map/ppermute | solution.py:260
  71.0 7.9 %collective-permute-start.11 = (bf16[1152,128]{1,0:T(8,128)(2,1)S(1)}, bf16[1152,128]{1,0:T(8,128)(2,1)S(1)}, u32[]{:S(2)}, u32[]{:S(2)}) collective-permute-start(bf16[1152,128]{1,0:T(8,128)(2,1)S(1)} %bitcast.43), channel_id=1, source_target_pairs={{16,8},{24,16},{17,9},{25,17},{18,10},{26,18},{19,11},{27,19},{20,... | collective-permute-start | bytes 884744 | tf_op jit(solution)/shard_map/ppermute | solution.py:258
  76.6 14.1 %collective-permute-start.10 = (bf16[1152,128]{1,0:T(8,128)(2,1)}, bf16[1152,128]{1,0:T(8,128)(2,1)}, u32[]{:S(2)}, u32[]{:S(2)}) collective-permute-start(bf16[1152,128]{1,0:T(8,128)(2,1)} %bitcast_add_fusion.1), channel_id=1, source_target_pairs={{0,8},{8,16},{16,24},{24,0},{1,9},{9,17},{17,25},{25,1},{2,10},{10... | collective-permute-start | bytes 884744 | tf_op jit(solution)/shard_map/ppermute | solution.py:259
  79.6 15.2 %collective-permute-start.12 = (bf16[1152,128]{1,0:T(8,128)(2,1)}, bf16[1152,128]{1,0:T(8,128)(2,1)}, u32[]{:S(2)}, u32[]{:S(2)}) collective-permute-start(bf16[1152,128]{1,0:T(8,128)(2,1)} %bitcast_add_fusion), channel_id=1, source_target_pairs={{0,24},{8,0},{16,8},{24,16},{1,25},{9,1},{17,9},{25,17},{2,26},{10... | collective-permute-start | bytes 884744 | tf_op jit(solution)/shard_map/ppermute | solution.py:260
  103.1 8.7 %collective-permute-start.13 = (bf16[1184,128]{1,0:T(8,128)(2,1)}, bf16[1184,128]{1,0:T(8,128)(2,1)}, u32[]{:S(2)}, u32[]{:S(2)}) collective-permute-start(bf16[1184,128]{1,0:T(8,128)(2,1)} %copy-done.7), channel_id=1, source_target_pairs={{0,8},{8,16},{16,24},{24,0},{1,9},{9,17},{17,25},{25,1},{2,10},{10... | collective-permute-start | bytes 909320 | tf_op jit(solution)/shard_map/ppermute | solution.py:266
  104.2 9.2 %collective-permute-start.14 = (bf16[1184,128]{1,0:T(8,128)(2,1)}, bf16[1184,128]{1,0:T(8,128)(2,1)}, u32[]{:S(2)}, u32[]{:S(2)}) collective-permute-start(bf16[1184,128]{1,0:T(8,128)(2,1)} %copy-done.7), channel_id=1, source_target_pairs={{0,24},{8,0},{16,8},{24,16},{1,25},{9,1},{17,9},{25,17},{2,26},{10... | collective-permute-start | bytes 909320 | tf_op jit(solution)/shard_map/ppermute | solution.py:267
  107.2 23.8 %all-to-all-start.1 = ((bf16[4,192,128]{2,1,0:T(8,128)(2,1)}), bf16[4,192,128]{2,1,0:T(8,128)(2,1)S(1)}, u32[]{:S(2)}, u32[]{:S(2)}) async-start(bf16[4,192,128]{2,1,0:T(8,128)(2,1)} %bitcast.41), calls=%async_computation.1 | async-start | bytes 393216 | tf_op jit(solution)/shard_map/all_to_all | solution.py:360
  111.9 19.9 %collective-permute-start.15 = (bf16[1184,128]{1,0:T(8,128)(2,1)}, bf16[1184,128]{1,0:T(8,128)(2,1)}, u32[]{:S(2)}, u32[]{:S(2)}) collective-permute-start(bf16[1184,128]{1,0:T(8,128)(2,1)} %collective-permute-done.13.before), channel_id=1, source_target_pairs={{8,16},{16,24},{9,17},{17,25},{10,18},{18,26},{11,19},{19,27},{12,... | collective-permute-start | bytes 909320 | tf_op jit(solution)/shard_map/ppermute | solution.py:268
  113.4 30.8 %collective-permute-start.16 = (bf16[1184,128]{1,0:T(8,128)(2,1)}, bf16[1184,128]{1,0:T(8,128)(2,1)}, u32[]{:S(2)}, u32[]{:S(2)}) collective-permute-start(bf16[1184,128]{1,0:T(8,128)(2,1)} %collective-permute-done.14.after), channel_id=1, source_target_pairs={{8,0},{16,8},{9,1},{17,9},{10,2},{18,10},{11,3},{19,11},{12,4},{20... | collective-permute-start | bytes 909320 | tf_op jit(solution)/shard_map/ppermute | solution.py:269
  149.8 6.8 %collective-permute-start.17 = (bf16[2,2,192,512]{3,2,1,0:T(8,128)(2,1)}, bf16[2,2,192,512]{3,2,1,0:T(8,128)(2,1)}, u32[]{:S(2)}, u32[]{:S(2)}) collective-permute-start(bf16[2,2,192,512]{3,2,1,0:T(8,128)(2,1)} %copy-done.14), channel_id=1, source_target_pairs={{0,2},{2,0},{4,6},{6,4},{1,3},{3,1},{5,7},{7,5},{8,10},{10,8},{12,... | collective-permute-start | bytes 2359304 | tf_op jit(solution)/shard_map/ppermute | solution.py:373
  162.2 7.3 %collective-permute-start.20 = (bf16[192,512]{1,0:T(8,128)(2,1)}, bf16[192,512]{1,0:T(8,128)(2,1)S(1)}, u32[]{:S(2)}, u32[]{:S(2)}) collective-permute-start(bf16[192,512]{1,0:T(8,128)(2,1)} %get-tuple-element.71), channel_id=1, source_target_pairs={{5,0},{4,1},{7,2},{6,3},{1,4},{0,5},{3,6},{2,7},{13,8},{12,9},{15,... | collective-permute-start | bytes 589832 | tf_op jit(solution)/shard_map/ppermute | solution.py:383
  162.4 10.5 %collective-permute-start.19 = (bf16[192,512]{1,0:T(8,128)(2,1)}, bf16[192,512]{1,0:T(8,128)(2,1)S(1)}, u32[]{:S(2)}, u32[]{:S(2)}) collective-permute-start(bf16[192,512]{1,0:T(8,128)(2,1)} %get-tuple-element.70), channel_id=1, source_target_pairs={{4,0},{5,1},{6,2},{7,3},{0,4},{1,5},{2,6},{3,7},{12,8},{13,9},{14,... | collective-permute-start | bytes 589832 | tf_op jit(solution)/shard_map/ppermute | solution.py:383
  163.3 9.8 %collective-permute-start.18 = (bf16[192,512]{1,0:T(8,128)(2,1)}, bf16[192,512]{1,0:T(8,128)(2,1)S(1)}, u32[]{:S(2)}, u32[]{:S(2)}) collective-permute-start(bf16[192,512]{1,0:T(8,128)(2,1)} %get-tuple-element.69), channel_id=1, source_target_pairs={{1,0},{0,1},{3,2},{2,3},{5,4},{4,5},{7,6},{6,7},{9,8},{8,9},{11,10... | collective-permute-start | bytes 589832 | tf_op jit(solution)/shard_map/ppermute | solution.py:383
  173.2 15.3 %collective-permute-start.21 = (bf16[192,512]{1,0:T(8,128)(2,1)S(1)}, bf16[192,512]{1,0:T(8,128)(2,1)S(1)}, u32[]{:S(2)}, u32[]{:S(2)}) collective-permute-start(bf16[192,512]{1,0:T(8,128)(2,1)S(1)} %add_convert_fusion), channel_id=1, source_target_pairs={{0,0},{2,8},{4,16},{6,24},{8,2},{10,10},{12,18},{14,26},{16,4},{18... | collective-permute-start | bytes 589832 | tf_op jit(solution)/shard_map/ppermute | solution.py:384
  (23 other events, 76.9 us)
Sparse Core Ops, SparseCore 0:
  103.2 46.1 all-gather.2

commit v6 on v3

--- a/solution.py
+++ b/solution.py
@@ -84,43 +84,34 @@
         held[z + ndp // 2] = far_after[...]
 
 
-def input_grads(held, w_ref, all_ref, ncol):
-    ndp = held.shape[0]
-    tokens, depth = all_ref.shape[1], w_ref.shape[1] // ncol
+def input_grad_body(*refs):
+    pieces, (w_ref, partner_w_ref, near_ref, far_ref, small_ref), refs = refs[:10], refs[10:15], refs[15:]
+    *out_refs, near_held, far_held = refs
+    tokens = near_ref.shape[1]
+    rows, depth = out_refs[0].shape
+    ndp, _, width = near_held.shape
+    ncol = w_ref.shape[1] // depth
     col = lax.axis_index("col")
-    for i in range(3):
-        for owner in range(ndp):
-            width = held.shape[2]
-            all_ref[i, :, owner * width : (owner + 1) * width] = held[owner, i * tokens : (i + 1) * tokens]
+    assemble(pieces[:5], near_held, ndp)
+    assemble(pieces[5:], far_held, ndp)
+    small_ref[...] = near_held[:, 3 * tokens :]
+    for held, all_ref in ((near_held, near_ref), (far_held, far_ref)):
+        for i in range(3):
+            for owner in range(ndp):
+                all_ref[i, :, owner * width : (owner + 1) * width] = held[owner, i * tokens : (i + 1) * tokens]
     for dx in range(ncol):
         start = pl.multiple_of(wrapped(col - dx, ncol) * depth, depth)
         total = jnp.zeros((tokens, depth), F32)
-        for i in range(3):
-            total += lax.dot_general(
-                all_ref[i],
-                w_ref[i, pl.ds(start, depth), :],
-                (((1,), (1,)), ((), ())),
-                preferred_element_type=F32,
-            )
-        yield dx, total
-
-
-def first_grad_body(own, before, after, far_before, far_after, w_ref, out_ref, all_ref, small_ref, held):
-    nblocks, ncol, rows, depth = out_ref.shape
-    assemble((own, before, after, far_before, far_after), held, held.shape[0])
-    small_ref[...] = held[:, 3 * nblocks * rows :]
-    for dx, total in input_grads(held, w_ref, all_ref, ncol):
-        out_ref[:, dx] = total.reshape(nblocks, rows, depth).astype(BF16)
-
-
-def second_grad_body(own, before, after, far_before, far_after, w_ref, other_ref, all_ref, *refs):
-    *out_refs, held = refs
-    nblocks, ncol, rows, depth = other_ref.shape
-    assemble((own, before, after, far_before, far_after), held, held.shape[0])
-    for dx, total in input_grads(held, w_ref, all_ref, ncol):
-        for block in range(nblocks):
-            both = total[block * rows : (block + 1) * rows] + other_ref[block, dx].astype(F32)
-            out_refs[block * ncol + dx][...] = both.astype(BF16)
+        for all_ref, weights in ((near_ref, w_ref), (far_ref, partner_w_ref)):
+            for i in range(3):
+                total += lax.dot_general(
+                    all_ref[i],
+                    weights[i, pl.ds(start, depth), :],
+                    (((1,), (1,)), ((), ())),
+                    preferred_element_type=F32,
+                )
+        for block in range(tokens // rows):
+            out_refs[block * ncol + dx][...] = total[block * rows : (block + 1) * rows].astype(BF16)
 
 
 def weight_grad_body(scale, x0_ref, x1_ref, g0_ref, g1_ref, out_ref):
@@ -240,9 +231,9 @@
         gm_ref[i * tokens : (i + 1) * tokens] = total.astype(BF16)
     for chunk, place, at in places():
         (near_ref, other_ref)[chunk][place : place + rows] = gm_ref[pl.ds(at, rows)]
-    tail = other_ref.shape[0] - 3 * tokens // 2 - groups - 3 * nshort
+    tail = near_ref.shape[0] - 3 * tokens // 2 - groups - 3 * nshort
     small = jnp.concatenate([by_lag] + short_rows + [jnp.zeros((tail, width), F32)], axis=0)
-    other_ref[3 * tokens // 2 :] = small.astype(BF16)
+    near_ref[3 * tokens // 2 :] = small.astype(BF16)
 
 
 def sum_over_line(own, right, far, left):
@@ -254,13 +245,22 @@
     return own, rightward, leftward
 
 
-def gather_over_line(own):
-    ndp = lax.axis_size("dp")
-    before = lax.ppermute(own, "dp", [(a, (a + 1) % ndp) for a in range(ndp)])
-    after = lax.ppermute(own, "dp", [(a, (a - 1) % ndp) for a in range(ndp)])
+def gather_over_line(own, across):
+    ndp, nrow = lax.axis_size("dp"), lax.axis_size("row")
+
+    def shift(count):
+        return [
+            (a * nrow + r, (a + count) % ndp * nrow + (r + 1 - 2 * (r % 2) if across else r))
+            for a in range(ndp)
+            for r in range(nrow)
+        ]
+
+    before = lax.ppermute(own, ("dp", "row"), shift(1))
+    after = lax.ppermute(own, ("dp", "row"), shift(-1))
+    here = lax.ppermute(own, ("dp", "row"), shift(0)) if across else own
     far_before = lax.ppermute(before, "dp", [(a - 1, a) for a in range(ndp // 2, ndp)])
     far_after = lax.ppermute(after, "dp", [(a + 1, a) for a in range(ndp // 2)])
-    return own, before, after, far_before, far_after
+    return here, before, after, far_before, far_after
 
 
 def move_activations(tokens, in_weight, short_filter, long_filter, grad_out):
@@ -288,9 +288,10 @@
     w = jnp.transpose(in_weight, (1, 0, 2))
     moved = lax.ppermute(tokens, ("dp", "row"), swap)
     near = [moved] + [lax.ppermute(moved, ("row", "col"), offset(*p)) for p in places[1:]]
+    upstream = lax.all_to_all(grad_out, "dp", split_axis=1, concat_axis=0, tiled=True)
+    upstream, *near = lax.optimization_barrier((upstream, *near))
     x0 = jnp.stack(near).reshape(nblocks, ncol, rows, dcol)
     x1 = lax.ppermute(x0, "row", partner)
-    upstream = lax.all_to_all(grad_out, "dp", split_axis=1, concat_axis=0, tiled=True)
 
     sf = lax.dynamic_slice_in_dim(short_filter, z * width, width, 2).reshape(3 * nshort, width)
     lf = lax.dynamic_slice_in_dim(long_filter, z * groups, groups, 0).astype(F32)
@@ -330,42 +331,41 @@
     grad_near, grad_other, mixed = kernel_call(
         functools.partial(middle_body, scale, nshort, nrow),
         (
+            shaped((3 * chunk + extra, width), BF16),
             shaped((3 * chunk, width), BF16),
-            shaped((3 * chunk + extra, width), BF16),
             shaped((seq, width), BF16),
         ),
         grid=(1,),
         in_specs=[whole(3 * chunk, width)] * 6
         + [whole(3 * nshort, width), half, other, whole(seq, width)],
-        out_specs=(whole(3 * chunk, width), whole(3 * chunk + extra, width), whole(seq, width)),
+        out_specs=(whole(3 * chunk + extra, width), whole(3 * chunk, width), whole(seq, width)),
         scratch=[pltpu.VMEM((3 * seq, width), F32), pltpu.VMEM((3 * seq, width), BF16)],
         flops=3 * 2 * groups * ntaps * 2 * ntaps * width * (seq // ntaps),
         nbytes=2 * width * seq * 14,
     )(*sums, sf, bands, bands, upstream)
     mixed = lax.all_to_all(mixed, "dp", split_axis=0, concat_axis=1, tiled=True)
-
+    pieces = (*gather_over_line(grad_near, False), *gather_over_line(grad_other, True))
+    mixed, *pieces = lax.optimization_barrier((mixed, *pieces))
     block = shaped((rows, dcol), BF16)
     all_shape = shaped((3, chunk, local), BF16)
-    out_first, all_other, small = kernel_call(
-        first_grad_body,
-        (shaped((nblocks, ncol, rows, dcol), BF16), all_shape, shaped((ndp, extra, width), BF16)),
-        scratch=[pltpu.VMEM((ndp, 3 * chunk + extra, width), BF16)],
-        flops=mm_flops,
-        nbytes=mm_bytes,
-    )(*gather_over_line(grad_other), w)
-    from_partner = lax.ppermute(out_first, "row", partner)
-    all_near, *blocks = kernel_call(
-        second_grad_body,
-        [all_shape] + [block] * len(places),
-        scratch=[pltpu.VMEM((ndp, 3 * chunk, width), BF16)],
-        flops=mm_flops,
-        nbytes=mm_bytes,
-    )(*gather_over_line(grad_near), w, from_partner)
-    arrived = blocks[0].astype(F32)
-    for (dy, dx), sent in zip(places[1:], blocks[1:]):
-        back = [(b, a) for a, b in offset(dy, dx)]
-        arrived += lax.ppermute(sent, ("row", "col"), back).astype(F32)
-    grad_in = lax.ppermute(arrived.astype(BF16), ("dp", "row"), swap)
+    all_near, all_far, small, *blocks = kernel_call(
+        input_grad_body,
+        [all_shape, all_shape, shaped((ndp, extra, width), BF16)] + [block] * len(places),
+        scratch=[
+            pltpu.VMEM((ndp, 3 * chunk + extra, width), BF16),
+            pltpu.VMEM((ndp, 3 * chunk, width), BF16),
+        ],
+        flops=2 * mm_flops,
+        nbytes=2 * mm_bytes,
+    )(*pieces, w, lax.ppermute(w, "row", partner))
+    arrivals = [
+        lax.ppermute(sent, ("row", "col"), [(b, a) for a, b in offset(*p)])
+        for p, sent in zip(places[1:], blocks[1:])
+    ]
+    arrived = sum((a.astype(F32) for a in arrivals), blocks[0].astype(F32)).astype(BF16)
+    all_other = lax.ppermute(all_far, "row", partner)
+    arrived, all_other = lax.optimization_barrier((arrived, all_other))
+    grad_in = lax.ppermute(arrived, ("dp", "row"), swap)
 
     x_spec = pl.BlockSpec((nblocks, ncol, rows, dcol), lambda i: (0, 0, 0, 0))
     g_spec = pl.BlockSpec((1, chunk, local), lambda i: (i, 0, 0))

time: 187 us -> 176 us (0.941)
  waiting for transfers between devices: 75.9 us -> 64.9 us
  Pallas kernels: 26.3 us -> 22.4 us
  starting transfers between devices: 61.9 us -> 65.4 us
    ppermute x9 -> x11, starting transfers between devices: 17.4 us -> 12 us  [the longest x1 3.99 us: move_activations(): grad_in = lax.ppermute(arrived, ('dp', 'row'), swap)]
    ppermute x2, waiting for transfers between devices: 7.57 us -> 2.98 us  [sum_over_line(): from_left = lax.ppermute(far, 'dp', [(a, a + 1) for a in range(ndp // 2)])]
    ppermute x2, waiting for transfers between devices: 4.23 us -> 0.01 us  [sum_over_line(): lax.ppermute(left + from_right, 'dp', [(a, (a - 1) % ndp) for a in range(...]
    ppermute x2, starting transfers between devices: 5.02 us -> 8.82 us  [sum_over_line(): lax.ppermute(right + from_left, 'dp', [(a, (a + 1) % ndp) for a in range(...]
    ppermute x9 -> x11, waiting for transfers between devices: 29.2 us -> 32 us  [the longest x2 14.2 us: gather_over_line(): before = lax.ppermute(own, ('dp', 'row'), shift(1))]
    pallas_call x2 -> x1, Pallas kernels: 8.51 us -> 5.93 us  [move_activations(): kernel_call(input_grad_body, [all_shape, all_shape, shaped((ndp, extra, w...]
    ppermute x2, waiting for transfers between devices: 13.1 us -> 10.9 us  [gather_over_line(): far_after = lax.ppermute(after, 'dp', [(a + 1, a) for a in range(ndp // 2)])]
    unnamed x39 -> x35, local copies, waits for them, and re-layouts: 11.9 us -> 10.8 us
  transfers between devices with their start and end apart: 28 -> 30, of which waited for: 17 -> 12; matrix products, arithmetic and copies ran while one was open for 4% -> 6% of each run, Pallas kernels for 7% -> 9%
where the time goes in v6:
time: 176 us; the launch traced here: 175 us
  starting transfers between devices  65.4 us (37%)
  waiting for transfers between devices  64.9 us (37%)
  Pallas kernels  22.4 us (13%)
  local copies, waits for them, and re-layouts  16.4 us (9%)
  other arithmetic  5.1 us (3%)
    ppermute x2, waiting for transfers between devices, gather_over_line(): before = lax.ppermute(own, ('dp', 'row'), shift(1))  14.2 us
    ppermute x2, starting transfers between devices, sum_over_line(): lax.ppermute(left + from_right, 'dp', [(a, (a - 1) % ndp) for a in range(...  12.9 us
    ppermute x2, waiting for transfers between devices, gather_over_line(): far_after = lax.ppermute(after, 'dp', [(a + 1, a) for a in range(ndp // 2)])  10.9 us
    unnamed x35, local copies, waits for them, and re-layouts  10.8 us
    ppermute x1, waiting for transfers between devices, move_activations(): moved = lax.ppermute(tokens, ('dp', 'row'), swap)  9.89 us
    ppermute x2, starting transfers between devices, sum_over_line(): lax.ppermute(right + from_left, 'dp', [(a, (a + 1) % ndp) for a in range(...  8.82 us
    ppermute x2, starting transfers between devices, sum_over_line(): from_left = lax.ppermute(far, 'dp', [(a, a + 1) for a in range(ndp // 2)])  8.74 us
    pallas_call x2, Pallas kernels, move_activations(): kernel_call(project_body, [shaped((3, chunk, width), BF16)] * ndp, grid=(...  7.94 us
  transfers between devices with their start and end apart: 30, of which 12 were waited for; matrix products, arithmetic and copies ran while one was open for 6% of the time, Pallas kernels for 9%

profile of v6, /device:TPU:4, one launch (start us, length us, event | category | flops | bytes accessed | tf_op | source)
XLA Modules:
  0.0 175.0 jit_solution(3534718362476317462)
XLA Ops:
  0.6 4.6 %collective-permute-start = (bf16[192,512]{1,0:T(8,128)(2,1)}, bf16[192,512]{1,0:T(8,128)(2,1)S(1)}, u32[]{:S(2)}, u32[]{:S(2)}) collective-permute-start(bf16[192,512]{1,0:T(8,128)(2,1)} %param.5), channel_id=1, source_target_pairs={{0,0},{2,8},{4,16},{6,24},{8,2},{10,10},{12,18},{14,26},{16,4},{18... | collective-permute-start | bytes 589832 | tf_op jit(solution)/shard_map/ppermute | solution.py:289
  5.9 3.4 %all-to-all-start = ((bf16[192,4,128]{2,0,1:T(8,128)(2,1)}), bf16[192,4,128]{2,0,1:T(8,128)(2,1)S(1)}, u32[]{:S(2)}, u32[]{:S(2)}) async-start(bf16[192,4,128]{2,0,1:T(8,128)(2,1)} %copy_bitcast_fusion.1), calls=%async_computation | async-start | bytes 393216 | tf_op jit(solution)/shard_map/all_to_all | solution.py:291
  9.3 9.9 %collective-permute-done = bf16[192,512]{1,0:T(8,128)(2,1)S(1)} collective-permute-done((bf16[192,512]{1,0:T(8,128)(2,1)}, bf16[192,512]{1,0:T(8,128)(2,1)S(1)}, u32[]{:S(2)}, u32[]{:S(2)}) %collective-permute-start) | collective-permute-done | bytes 196640 | tf_op jit(solution)/shard_map/ppermute | solution.py:289
  22.7 3.2 %collective-permute-done.3 = bf16[192,512]{1,0:T(8,128)(2,1)S(1)} collective-permute-done((bf16[192,512]{1,0:T(8,128)(2,1)S(1)}, bf16[192,512]{1,0:T(8,128)(2,1)S(1)}, u32[]{:S(2)}, u32[]{:S(2)}) %collective-permute-start.3) | collective-permute-done | bytes 196640 | tf_op jit(solution)/shard_map/ppermute | solution.py:290
  28.1 3.8 %shard_map.92 = (bf16[3,384,128]{2,1,0:T(8,128)(2,1)S(1)}, bf16[3,384,128]{2,1,0:T(8,128)(2,1)S(1)}, bf16[3,384,128]{2,1,0:T(8,128)(2,1)S(1)}, bf16[3,384,128]{2,1,0:T(8,128)(2,1)S(1)}) custom-call(bf16[2,2,192,512]{3,2,1,0:T(8,128)(2,1)S(1)} %bitcast.38, bf16[3,1024,512]{2,1,0:T(8,128)(2,1)} %bitcast.7.w_ref.refs_10_), custom_call_target="tpu_custom_call" | custom-call | flops 1207959552 | bytes 5111808 | tf_op jit(solution)/shard_map/pallas_call | solution.py:312
  33.9 4.2 %collective-permute-start.4 = (bf16[1152,128]{1,0:T(8,128)(2,1)S(1)}, bf16[1152,128]{1,0:T(8,128)(2,1)S(1)}, u32[]{:S(2)}, u32[]{:S(2)}) collective-permute-start(bf16[1152,128]{1,0:T(8,128)(2,1)S(1)} %bitcast.42), channel_id=1, source_target_pairs={{0,8},{8,16},{1,9},{9,17},{2,10},{10,18},{3,11},{11,19},{4,12},{12... | collective-permute-start | bytes 884744 | tf_op jit(solution)/shard_map/ppermute | solution.py:241
  38.8 7.3 %collective-permute-start.7 = (bf16[1152,128]{1,0:T(8,128)(2,1)}, bf16[1152,128]{1,0:T(8,128)(2,1)S(1)}, u32[]{:S(2)}, u32[]{:S(2)}) collective-permute-start(bf16[1152,128]{1,0:T(8,128)(2,1)} %bitcast_add_fusion.2), channel_id=1, source_target_pairs={{0,24},{8,0},{16,8},{24,16},{1,25},{9,1},{17,9},{25,17},{2,26},{10... | collective-permute-start | bytes 884744 | tf_op jit(solution)/shard_map/ppermute | solution.py:244
  46.1 4.1 %shard_map.93 = (bf16[3,384,128]{2,1,0:T(8,128)(2,1)S(1)}, bf16[3,384,128]{2,1,0:T(8,128)(2,1)S(1)}, bf16[3,384,128]{2,1,0:T(8,128)(2,1)S(1)}, bf16[3,384,128]{2,1,0:T(8,128)(2,1)S(1)}) custom-call(bf16[2,2,192,512]{3,2,1,0:T(8,128)(2,1)S(1)} %collective-permute-done.8.x_ref.x1_ref, bf16[3,1024,512]{2,1,0:T(8,128)(2,1)} %bitcast.7.w_ref.refs_10_), custom_call_target="tpu_custom_call" | custom-call | flops 1207959552 | bytes 5111808 | tf_op jit(solution)/shard_map/pallas_call | solution.py:312
  52.6 4.6 %collective-permute-start.9 = (bf16[1152,128]{1,0:T(8,128)(2,1)S(1)}, bf16[1152,128]{1,0:T(8,128)(2,1)S(1)}, u32[]{:S(2)}, u32[]{:S(2)}) collective-permute-start(bf16[1152,128]{1,0:T(8,128)(2,1)S(1)} %bitcast.44), channel_id=1, source_target_pairs={{0,8},{8,16},{1,9},{9,17},{2,10},{10,18},{3,11},{11,19},{4,12},{12... | collective-permute-start | bytes 884744 | tf_op jit(solution)/shard_map/ppermute | solution.py:241
  57.9 5.6 %collective-permute-start.12 = (bf16[1152,128]{1,0:T(8,128)(2,1)}, bf16[1152,128]{1,0:T(8,128)(2,1)S(1)}, u32[]{:S(2)}, u32[]{:S(2)}) collective-permute-start(bf16[1152,128]{1,0:T(8,128)(2,1)} %bitcast_add_fusion), channel_id=1, source_target_pairs={{0,24},{8,0},{16,8},{24,16},{1,25},{9,1},{17,9},{25,17},{2,26},{10... | collective-permute-start | bytes 884744 | tf_op jit(solution)/shard_map/ppermute | solution.py:244
  63.6 3.0 %collective-permute-done.9 = bf16[1152,128]{1,0:T(8,128)(2,1)S(1)} collective-permute-done((bf16[1152,128]{1,0:T(8,128)(2,1)S(1)}, bf16[1152,128]{1,0:T(8,128)(2,1)S(1)}, u32[]{:S(2)}, u32[]{:S(2)}) %collective-permute-start.9) | collective-permute-done | bytes 294944 | tf_op jit(solution)/shard_map/ppermute | solution.py:241
  66.6 8.0 %collective-permute-start.10 = (bf16[1152,128]{1,0:T(8,128)(2,1)S(1)}, bf16[1152,128]{1,0:T(8,128)(2,1)S(1)}, u32[]{:S(2)}, u32[]{:S(2)}) collective-permute-start(bf16[1152,128]{1,0:T(8,128)(2,1)S(1)} %bitcast_add_fusion.1), channel_id=1, source_target_pairs={{0,8},{8,16},{16,24},{24,0},{1,9},{9,17},{17,25},{25,1},{2,10},{10... | collective-permute-start | bytes 884744 | tf_op jit(solution)/shard_map/ppermute | solution.py:243
  76.8 3.8 %collective-permute-done.10.refs_4_ = bf16[1152,128]{1,0:T(8,128)(2,1)S(1)} collective-permute-done((bf16[1152,128]{1,0:T(8,128)(2,1)S(1)}, bf16[1152,128]{1,0:T(8,128)(2,1)S(1)}, u32[]{:S(2)}, u32[]{:S(2)}) %collective-permute-start.10) | collective-permute-done | bytes 294944 | tf_op jit(solution)/shard_map/ppermute | solution.py:243
  82.6 3.2 %shard_map.95 = (bf16[1184,128]{1,0:T(8,128)(2,1)S(1)}, bf16[1152,128]{1,0:T(8,128)(2,1)}, bf16[768,128]{1,0:T(8,128)(2,1)}) custom-call(bf16[1152,128]{1,0:T(8,128)(2,1)S(1)} %bitcast.45, bf16[1152,128]{1,0:T(8,128)(2,1)S(1)} %collective-permute-done.5.refs_1_, bf16[1152,128]{1,0:T(8,128)(2,1)S(1)} %collective-permute-done.7.refs_2_, ...), custom_call_target="tpu_custom_call" | custom-call | flops 1207959552 | bytes 2752512 | tf_op jit(solution)/shard_map/pallas_call | solution.py:331
  89.5 5.7 %collective-permute-done.19.refs_7_ = bf16[1152,128]{1,0:T(8,128)(2,1)S(1)} collective-permute-done((bf16[1152,128]{1,0:T(8,128)(2,1)}, bf16[1152,128]{1,0:T(8,128)(2,1)S(1)}, u32[]{:S(2)}, u32[]{:S(2)}) %collective-permute-start.19) | collective-permute-done | bytes 294944 | tf_op jit(solution)/shard_map/ppermute | solution.py:259
  95.4 5.4 %all-to-all-start.1 = ((bf16[4,192,128]{2,1,0:T(8,128)(2,1)}), bf16[4,192,128]{2,1,0:T(8,128)(2,1)S(1)}, u32[]{:S(2)}, u32[]{:S(2)}) async-start(bf16[4,192,128]{2,1,0:T(8,128)(2,1)} %bitcast.16), calls=%async_computation.1 | async-start | bytes 393216 | tf_op jit(solution)/shard_map/all_to_all | solution.py:346
  102.1 5.6 %collective-permute-done.13.refs_1_ = bf16[1184,128]{1,0:T(8,128)(2,1)S(1)} collective-permute-done((bf16[1184,128]{1,0:T(8,128)(2,1)S(1)}, bf16[1184,128]{1,0:T(8,128)(2,1)S(1)}, u32[]{:S(2)}, u32[]{:S(2)}) %collective-permute-start.13) | collective-permute-done | bytes 303136 | tf_op jit(solution)/shard_map/ppermute | solution.py:258
  108.4 8.6 %collective-permute-done.18.refs_6_ = bf16[1152,128]{1,0:T(8,128)(2,1)S(1)} collective-permute-done((bf16[1152,128]{1,0:T(8,128)(2,1)}, bf16[1152,128]{1,0:T(8,128)(2,1)S(1)}, u32[]{:S(2)}, u32[]{:S(2)}) %collective-permute-start.18) | collective-permute-done | bytes 294944 | tf_op jit(solution)/shard_map/ppermute | solution.py:258
  120.4 10.9 %collective-permute-done.21.refs_9_ = bf16[1152,128]{1,0:T(8,128)(2,1)} collective-permute-done((bf16[1152,128]{1,0:T(8,128)(2,1)S(1)}, bf16[1152,128]{1,0:T(8,128)(2,1)}, u32[]{:S(2)}, u32[]{:S(2)}) %collective-permute-start.21) | collective-permute-done | bytes 294944 | tf_op jit(solution)/shard_map/ppermute | solution.py:262
  135.0 5.9 %shard_map.96 = (bf16[3,384,512]{2,1,0:T(8,128)(2,1)S(1)}, bf16[3,384,512]{2,1,0:T(8,128)(2,1)}, bf16[4,32,128]{2,1,0:T(8,128)(2,1)S(1)}, bf16[192,512]{1,0:T(8,...) custom-call(bf16[1184,128]{1,0:T(8,128)(2,1)S(1)} %get-tuple-element.58.refs, ...), custom_call_target="tpu_custom_call" | custom-call | flops 2415919104 | bytes 10223616 | tf_op jit(solution)/shard_map/pallas_call | solution.py:351
  152.9 4.9 %collective-permute-done.24 = bf16[192,512]{1,0:T(8,128)(2,1)} collective-permute-done((bf16[192,512]{1,0:T(8,128)(2,1)}, bf16[192,512]{1,0:T(8,128)(2,1)}, u32[]{:S(2)}, u32[]{:S(2)}) %collective-permute-start.24) | collective-permute-done | bytes 196640 | tf_op jit(solution)/shard_map/ppermute | solution.py:362
  159.0 4.0 %collective-permute-start.27 = (bf16[192,512]{1,0:T(8,128)(2,1)S(1)}, bf16[192,512]{1,0:T(8,128)(2,1)S(1)}, u32[]{:S(2)}, u32[]{:S(2)}) collective-permute-start(bf16[192,512]{1,0:T(8,128)(2,1)S(1)} %add_convert_fusion), channel_id=1, source_target_pairs={{0,0},{2,8},{4,16},{6,24},{8,2},{10,10},{12,18},{14,26},{16,4},{18... | collective-permute-start | bytes 589832 | tf_op jit(solution)/shard_map/ppermute | solution.py:368
  164.2 4.7 %shard_map.97 = f32[3,1024,512]{2,1,0:T(8,128)} custom-call(bf16[2,2,192,512]{3,2,1,0:T(8,128)(2,1)S(1)} %bitcast.39, bf16[2,2,192,512]{3,2,1,0:T(8,128)(2,1)S(1)} %copy-done.2, bf16[3,384,512]{2,1,0:T(8,128)(2,1)S(1)} %get-tuple-element.74.g0_ref, bf16[3,384,512]{2,1,0:T(8,128)(2,1)S(1)} %collective-permute-done.26.g1_ref), custom_call_target="tpu_custom_call" | custom-call | flops 2415919104 | bytes 10223616 | tf_op jit(solution)/shard_map/pallas_call | solution.py:372
  168.8 5.5 %collective-permute-done.27 = bf16[192,512]{1,0:T(8,128)(2,1)S(1)} collective-permute-done((bf16[192,512]{1,0:T(8,128)(2,1)S(1)}, bf16[192,512]{1,0:T(8,128)(2,1)S(1)}, u32[]{:S(2)}, u32[]{:S(2)}) %collective-permute-start.27) | collective-permute-done | bytes 196640 | tf_op jit(solution)/shard_map/ppermute | solution.py:368
  (98 shorter events, 44.2 us)
Async XLA Ops:
  0.6 18.6 %collective-permute-start = (bf16[192,512]{1,0:T(8,128)(2,1)}, bf16[192,512]{1,0:T(8,128)(2,1)S(1)}, u32[]{:S(2)}, u32[]{:S(2)}) collective-permute-start(bf16[192,512]{1,0:T(8,128)(2,1)} %param.5), channel_id=1, source_target_pairs={{0,0},{2,8},{4,16},{6,24},{8,2},{10,10},{12,18},{14,26},{16,4},{18... | collective-permute-start | bytes 589832 | tf_op jit(solution)/shard_map/ppermute | solution.py:289
  5.9 16.8 %all-to-all-start = ((bf16[192,4,128]{2,0,1:T(8,128)(2,1)}), bf16[192,4,128]{2,0,1:T(8,128)(2,1)S(1)}, u32[]{:S(2)}, u32[]{:S(2)}) async-start(bf16[192,4,128]{2,0,1:T(8,128)(2,1)} %copy_bitcast_fusion.1), calls=%async_computation | async-start | bytes 393216 | tf_op jit(solution)/shard_map/all_to_all | solution.py:291
  28.0 18.1 %collective-permute-start.8 = (bf16[2,2,192,512]{3,2,1,0:T(8,128)(2,1)S(1)}, bf16[2,2,192,512]{3,2,1,0:T(8,128)(2,1)S(1)}, u32[]{:S(2)}, u32[]{:S(2)}) collective-permute-start(bf16[2,2,192,512]{3,2,1,0:T(8,128)(2,1)S(1)} %bitcast.37), channel_id=1, source_target_pairs={{0,2},{2,0},{4,6},{6,4},{1,3},{3,1},{5,7},{7,5},{8,10},{10,8},{12,... | collective-permute-start | bytes 2359304 | tf_op jit(solution)/shard_map/ppermute | solution.py:294
  33.3 98.8 %collective-permute-start.22 = (bf16[3,1024,512]{2,1,0:T(8,128)(2,1)}, bf16[3,1024,512]{2,1,0:T(8,128)(2,1)}, u32[]{:S(2)}, u32[]{:S(2)}) collective-permute-start(bf16[3,1024,512]{2,1,0:T(8,128)(2,1)} %bitcast.7.w_ref.refs_10_), channel_id=1, source_target_pairs={{0,2},{2,0},{4,6},{6,4},{1,3},{3,1},{5,7},{7,5},{8,10},{10,8},{12,... | collective-permute-start | bytes 9437192 | tf_op jit(solution)/shard_map/ppermute | solution.py:360
  33.9 17.1 %collective-permute-start.4 = (bf16[1152,128]{1,0:T(8,128)(2,1)S(1)}, bf16[1152,128]{1,0:T(8,128)(2,1)S(1)}, u32[]{:S(2)}, u32[]{:S(2)}) collective-permute-start(bf16[1152,128]{1,0:T(8,128)(2,1)S(1)} %bitcast.42), channel_id=1, source_target_pairs={{0,8},{8,16},{1,9},{9,17},{2,10},{10,18},{3,11},{11,19},{4,12},{12... | collective-permute-start | bytes 884744 | tf_op jit(solution)/shard_map/ppermute | solution.py:241
  38.8 38.0 %collective-permute-start.7 = (bf16[1152,128]{1,0:T(8,128)(2,1)}, bf16[1152,128]{1,0:T(8,128)(2,1)S(1)}, u32[]{:S(2)}, u32[]{:S(2)}) collective-permute-start(bf16[1152,128]{1,0:T(8,128)(2,1)} %bitcast_add_fusion.2), channel_id=1, source_target_pairs={{0,24},{8,0},{16,8},{24,16},{1,25},{9,1},{17,9},{25,17},{2,26},{10... | collective-permute-start | bytes 884744 | tf_op jit(solution)/shard_map/ppermute | solution.py:244
  51.7 25.1 %collective-permute-start.5 = (bf16[1152,128]{1,0:T(8,128)(2,1)}, bf16[1152,128]{1,0:T(8,128)(2,1)S(1)}, u32[]{:S(2)}, u32[]{:S(2)}) collective-permute-start(bf16[1152,128]{1,0:T(8,128)(2,1)} %bitcast_add_fusion.3), channel_id=1, source_target_pairs={{0,8},{8,16},{16,24},{24,0},{1,9},{9,17},{17,25},{25,1},{2,10},{10... | collective-permute-start | bytes 884744 | tf_op jit(solution)/shard_map/ppermute | solution.py:243
  52.6 14.0 %collective-permute-start.9 = (bf16[1152,128]{1,0:T(8,128)(2,1)S(1)}, bf16[1152,128]{1,0:T(8,128)(2,1)S(1)}, u32[]{:S(2)}, u32[]{:S(2)}) collective-permute-start(bf16[1152,128]{1,0:T(8,128)(2,1)S(1)} %bitcast.44), channel_id=1, source_target_pairs={{0,8},{8,16},{1,9},{9,17},{2,10},{10,18},{3,11},{11,19},{4,12},{12... | collective-permute-start | bytes 884744 | tf_op jit(solution)/shard_map/ppermute | solution.py:241
  57.9 18.9 %collective-permute-start.12 = (bf16[1152,128]{1,0:T(8,128)(2,1)}, bf16[1152,128]{1,0:T(8,128)(2,1)S(1)}, u32[]{:S(2)}, u32[]{:S(2)}) collective-permute-start(bf16[1152,128]{1,0:T(8,128)(2,1)} %bitcast_add_fusion), channel_id=1, source_target_pairs={{0,24},{8,0},{16,8},{24,16},{1,25},{9,1},{17,9},{25,17},{2,26},{10... | collective-permute-start | bytes 884744 | tf_op jit(solution)/shard_map/ppermute | solution.py:244
  66.6 14.0 %collective-permute-start.10 = (bf16[1152,128]{1,0:T(8,128)(2,1)S(1)}, bf16[1152,128]{1,0:T(8,128)(2,1)S(1)}, u32[]{:S(2)}, u32[]{:S(2)}) collective-permute-start(bf16[1152,128]{1,0:T(8,128)(2,1)S(1)} %bitcast_add_fusion.1), channel_id=1, source_target_pairs={{0,8},{8,16},{16,24},{24,0},{1,9},{9,17},{17,25},{25,1},{2,10},{10... | collective-permute-start | bytes 884744 | tf_op jit(solution)/shard_map/ppermute | solution.py:243
  85.7 9.5 %collective-permute-start.19 = (bf16[1152,128]{1,0:T(8,128)(2,1)}, bf16[1152,128]{1,0:T(8,128)(2,1)S(1)}, u32[]{:S(2)}, u32[]{:S(2)}) collective-permute-start(bf16[1152,128]{1,0:T(8,128)(2,1)} %get-tuple-element.56), channel_id=1, source_target_pairs={{0,26},{2,24},{4,30},{6,28},{8,2},{10,0},{12,6},{14,4},{16,10},{18... | collective-permute-start | bytes 884744 | tf_op jit(solution)/shard_map/ppermute | solution.py:259
  85.7 15.1 %collective-permute-start.14 = (bf16[1184,128]{1,0:T(8,128)(2,1)S(1)}, bf16[1184,128]{1,0:T(8,128)(2,1)S(1)}, u32[]{:S(2)}, u32[]{:S(2)}) collective-permute-start(bf16[1184,128]{1,0:T(8,128)(2,1)S(1)} %get-tuple-element.58.refs_0_), channel_id=1, source_target_pairs={{0,24},{2,26},{4,28},{6,30},{8,0},{10,2},{12,4},{14,6},{16,8},{18,... | collective-permute-start | bytes 909320 | tf_op jit(solution)/shard_map/ppermute | solution.py:259
  88.0 19.7 %collective-permute-start.13 = (bf16[1184,128]{1,0:T(8,128)(2,1)S(1)}, bf16[1184,128]{1,0:T(8,128)(2,1)S(1)}, u32[]{:S(2)}, u32[]{:S(2)}) collective-permute-start(bf16[1184,128]{1,0:T(8,128)(2,1)S(1)} %get-tuple-element.58.refs_0_), channel_id=1, source_target_pairs={{0,8},{2,10},{4,12},{6,14},{8,16},{10,18},{12,20},{14,22},{16,24},... | collective-permute-start | bytes 909320 | tf_op jit(solution)/shard_map/ppermute | solution.py:258
  88.0 28.9 %collective-permute-start.18 = (bf16[1152,128]{1,0:T(8,128)(2,1)}, bf16[1152,128]{1,0:T(8,128)(2,1)S(1)}, u32[]{:S(2)}, u32[]{:S(2)}) collective-permute-start(bf16[1152,128]{1,0:T(8,128)(2,1)} %get-tuple-element.56), channel_id=1, source_target_pairs={{0,10},{2,8},{4,14},{6,12},{8,18},{10,16},{12,22},{14,20},{16,26},... | collective-permute-start | bytes 884744 | tf_op jit(solution)/shard_map/ppermute | solution.py:258
  95.2 23.1 %collective-permute-start.17 = (bf16[1152,128]{1,0:T(8,128)(2,1)}, bf16[1152,128]{1,0:T(8,128)(2,1)}, u32[]{:S(2)}, u32[]{:S(2)}) collective-permute-start(bf16[1152,128]{1,0:T(8,128)(2,1)} %get-tuple-element.56), channel_id=1, source_target_pairs={{0,2},{2,0},{4,6},{6,4},{8,10},{10,8},{12,14},{14,12},{16,18},{18,... | collective-permute-start | bytes 884744 | tf_op jit(solution)/shard_map/ppermute | solution.py:260
  95.4 24.3 %all-to-all-start.1 = ((bf16[4,192,128]{2,1,0:T(8,128)(2,1)}), bf16[4,192,128]{2,1,0:T(8,128)(2,1)S(1)}, u32[]{:S(2)}, u32[]{:S(2)}) async-start(bf16[4,192,128]{2,1,0:T(8,128)(2,1)} %bitcast.16), calls=%async_computation.1 | async-start | bytes 393216 | tf_op jit(solution)/shard_map/all_to_all | solution.py:346
  100.8 30.5 %collective-permute-start.16 = (bf16[1184,128]{1,0:T(8,128)(2,1)S(1)}, bf16[1184,128]{1,0:T(8,128)(2,1)S(1)}, u32[]{:S(2)}, u32[]{:S(2)}) collective-permute-start(bf16[1184,128]{1,0:T(8,128)(2,1)S(1)} %collective-permute-done.14.refs_2_), channel_id=1, source_target_pairs={{8,0},{16,8},{9,1},{17,9},{10,2},{18,10},{11,3},{19,11},{12,4},{20... | collective-permute-start | bytes 909320 | tf_op jit(solution)/shard_map/ppermute | solution.py:262
  107.7 23.6 %collective-permute-start.15 = (bf16[1184,128]{1,0:T(8,128)(2,1)S(1)}, bf16[1184,128]{1,0:T(8,128)(2,1)S(1)}, u32[]{:S(2)}, u32[]{:S(2)}) collective-permute-start(bf16[1184,128]{1,0:T(8,128)(2,1)S(1)} %collective-permute-done.13.refs_1_), channel_id=1, source_target_pairs={{8,16},{16,24},{9,17},{17,25},{10,18},{18,26},{11,19},{19,27},{12,... | collective-permute-start | bytes 909320 | tf_op jit(solution)/shard_map/ppermute | solution.py:261
  117.0 14.4 %collective-permute-start.21 = (bf16[1152,128]{1,0:T(8,128)(2,1)S(1)}, bf16[1152,128]{1,0:T(8,128)(2,1)}, u32[]{:S(2)}, u32[]{:S(2)}) collective-permute-start(bf16[1152,128]{1,0:T(8,128)(2,1)S(1)} %collective-permute-done.19.refs_7_), channel_id=1, source_target_pairs={{8,0},{16,8},{9,1},{17,9},{10,2},{18,10},{11,3},{19,11},{12,4},{20... | collective-permute-start | bytes 884744 | tf_op jit(solution)/shard_map/ppermute | solution.py:262
  118.3 13.1 %collective-permute-start.20 = (bf16[1152,128]{1,0:T(8,128)(2,1)S(1)}, bf16[1152,128]{1,0:T(8,128)(2,1)}, u32[]{:S(2)}, u32[]{:S(2)}) collective-permute-start(bf16[1152,128]{1,0:T(8,128)(2,1)S(1)} %collective-permute-done.18.refs_6_), channel_id=1, source_target_pairs={{8,16},{16,24},{9,17},{17,25},{10,18},{18,26},{11,19},{19,27},{12,... | collective-permute-start | bytes 884744 | tf_op jit(solution)/shard_map/ppermute | solution.py:261
  143.7 15.4 %collective-permute-start.26 = (bf16[3,384,512]{2,1,0:T(8,128)(2,1)}, bf16[3,384,512]{2,1,0:T(8,128)(2,1)S(1)}, u32[]{:S(2)}, u32[]{:S(2)}) collective-permute-start(bf16[3,384,512]{2,1,0:T(8,128)(2,1)} %get-tuple-element.72), channel_id=1, source_target_pairs={{0,2},{2,0},{4,6},{6,4},{1,3},{3,1},{5,7},{7,5},{8,10},{10,8},{12,... | collective-permute-start | bytes 3538952 | tf_op jit(solution)/shard_map/ppermute | solution.py:366
  146.2 11.6 %collective-permute-start.24 = (bf16[192,512]{1,0:T(8,128)(2,1)}, bf16[192,512]{1,0:T(8,128)(2,1)}, u32[]{:S(2)}, u32[]{:S(2)}) collective-permute-start(bf16[192,512]{1,0:T(8,128)(2,1)} %copy-done.11), channel_id=1, source_target_pairs={{4,0},{5,1},{6,2},{7,3},{0,4},{1,5},{2,6},{3,7},{12,8},{13,9},{14,... | collective-permute-start | bytes 589832 | tf_op jit(solution)/shard_map/ppermute | solution.py:362
  147.1 10.7 %collective-permute-start.25 = (bf16[192,512]{1,0:T(8,128)(2,1)}, bf16[192,512]{1,0:T(8,128)(2,1)}, u32[]{:S(2)}, u32[]{:S(2)}) collective-permute-start(bf16[192,512]{1,0:T(8,128)(2,1)} %copy-done.10), channel_id=1, source_target_pairs={{5,0},{4,1},{7,2},{6,3},{1,4},{0,5},{3,6},{2,7},{13,8},{12,9},{15,... | collective-permute-start | bytes 589832 | tf_op jit(solution)/shard_map/ppermute | solution.py:362
  159.0 15.3 %collective-permute-start.27 = (bf16[192,512]{1,0:T(8,128)(2,1)S(1)}, bf16[192,512]{1,0:T(8,128)(2,1)S(1)}, u32[]{:S(2)}, u32[]{:S(2)}) collective-permute-start(bf16[192,512]{1,0:T(8,128)(2,1)S(1)} %add_convert_fusion), channel_id=1, source_target_pairs={{0,0},{2,8},{4,16},{6,24},{8,2},{10,10},{12,18},{14,26},{16,4},{18... | collective-permute-start | bytes 589832 | tf_op jit(solution)/shard_map/ppermute | solution.py:368
  (23 other events, 151.3 us)

commit v7 on v6

--- a/solution.py
+++ b/solution.py
@@ -12,7 +12,7 @@
 BF16 = jnp.bfloat16
 
 
-def kernel_call(body, outs, grid=None, in_specs=None, out_specs=None, scratch=(), flops=0, nbytes=0):
+def kernel_call(body, outs, grid=None, in_specs=None, out_specs=None, scratch=(), flops=0, nbytes=0, vmem=VMEM_BYTES):
     kwargs = {}
     if grid is not None:
         kwargs = dict(grid=grid, in_specs=in_specs, out_specs=out_specs)
@@ -20,7 +20,7 @@
         body,
         out_shape=outs,
         scratch_shapes=scratch,
-        compiler_params=pltpu.CompilerParams(vmem_limit_bytes=VMEM_BYTES),
+        compiler_params=pltpu.CompilerParams(vmem_limit_bytes=vmem),
         cost_estimate=pl.CostEstimate(flops=flops, bytes_accessed=nbytes, transcendentals=0),
         **kwargs,
     )
@@ -43,6 +43,10 @@
             band = jnp.concatenate([band, pltpu.roll(band, count, 1)], axis=0)
             count *= 2
         out_ref[g] = band.astype(out_ref.dtype)
+
+
+def tokens_of(row, nrow):
+    return row % 2 * (nrow // 2) + row // 2
 
 
 def wrapped(value, size):
@@ -85,7 +89,7 @@
 
 
 def input_grad_body(*refs):
-    pieces, (w_ref, partner_w_ref, near_ref, far_ref, small_ref), refs = refs[:10], refs[10:15], refs[15:]
+    pieces, (w_ref, partner_w_ref, near_ref, far_ref, long_ref, short_ref), refs = refs[:10], refs[10:16], refs[16:]
     *out_refs, near_held, far_held = refs
     tokens = near_ref.shape[1]
     rows, depth = out_refs[0].shape
@@ -94,7 +98,11 @@
     col = lax.axis_index("col")
     assemble(pieces[:5], near_held, ndp)
     assemble(pieces[5:], far_held, ndp)
-    small_ref[...] = near_held[:, 3 * tokens :]
+    groups = long_ref.shape[0] // ndp
+    for owner in range(ndp):
+        small = near_held[owner, 3 * tokens :].astype(F32)
+        long_ref[owner * groups : (owner + 1) * groups] = small[:groups]
+        short_ref[:, owner * width : (owner + 1) * width] = small[groups : groups + short_ref.shape[0]]
     for held, all_ref in ((near_held, near_ref), (far_held, far_ref)):
         for i in range(3):
             for owner in range(ndp):
@@ -150,7 +158,7 @@
     def places():
         for chunk, start in enumerate((row, row + 1 - 2 * lax.rem(row, 2))):
             for block in range(nblocks):
-                at = wrapped(start - 2 * block, nrow) * rows
+                at = tokens_of(wrapped(start - 2 * block, nrow), nrow) * rows
                 for i in range(3):
                     yield chunk, (i * nblocks + block) * rows, pl.multiple_of(i * tokens + at, 16)
 
@@ -217,7 +225,11 @@
             part = jnp.where((turn & bit) != 0, pltpu.roll(part, span - bit, 1), part)
         sums.append(jnp.sum(part, axis=0, keepdims=True))
     by_lag = jnp.concatenate(sums, axis=0)
-    by_lag = scale * pltpu.roll(by_lag, span - 1, 1)[:, :block]
+    by_lag = (scale * pltpu.roll(by_lag, span - 1, 1)[:, :block]).astype(BF16)
+    ahead = lax.broadcasted_iota(jnp.int32, (block, block), 0)
+    back = lax.broadcasted_iota(jnp.int32, (block, block), 1)
+    turned = jnp.where(ahead + back == block - 1, 1.0, 0.0).astype(BF16)
+    by_lag = jnp.dot(by_lag, turned, preferred_element_type=F32)
 
     grad_feats = [upstream * conv, grad_product * feats[2], grad_product * feats[1]]
     short_rows = []
@@ -276,7 +288,8 @@
     scale = float(seq) ** -0.5
     nblocks = nrow // 2
     chunk = nblocks * rows
-    swap = [(a * nrow + b, b * nrow + a) for a in range(ndp) for b in range(nrow)]
+    swap = [(tokens_of(b, nrow) * nrow + a, a * nrow + b) for a in range(ndp) for b in range(nrow)]
+    swap_back = [(b, a) for a, b in swap]
     partner = [(a, a + 1 - 2 * (a % 2)) for a in range(nrow)]
     places = [(dy, dx) for dy in range(nblocks) for dx in range(ncol)]
 
@@ -348,15 +361,17 @@
     mixed, *pieces = lax.optimization_barrier((mixed, *pieces))
     block = shaped((rows, dcol), BF16)
     all_shape = shaped((3, chunk, local), BF16)
-    all_near, all_far, small, *blocks = kernel_call(
+    all_near, all_far, grad_long, grad_short, *blocks = kernel_call(
         input_grad_body,
-        [all_shape, all_shape, shaped((ndp, extra, width), BF16)] + [block] * len(places),
+        [all_shape, all_shape, shaped((ngroups, ntaps), F32), shaped((3 * nshort, local), F32)]
+        + [block] * len(places),
         scratch=[
             pltpu.VMEM((ndp, 3 * chunk + extra, width), BF16),
             pltpu.VMEM((ndp, 3 * chunk, width), BF16),
         ],
         flops=2 * mm_flops,
         nbytes=2 * mm_bytes,
+        vmem=62 * 2**20,
     )(*pieces, w, lax.ppermute(w, "row", partner))
     arrivals = [
         lax.ppermute(sent, ("row", "col"), [(b, a) for a, b in offset(*p)])
@@ -365,7 +380,7 @@
     arrived = sum((a.astype(F32) for a in arrivals), blocks[0].astype(F32)).astype(BF16)
     all_other = lax.ppermute(all_far, "row", partner)
     arrived, all_other = lax.optimization_barrier((arrived, all_other))
-    grad_in = lax.ppermute(arrived, ("dp", "row"), swap)
+    grad_in = lax.ppermute(arrived, ("dp", "row"), swap_back)
 
     x_spec = pl.BlockSpec((nblocks, ncol, rows, dcol), lambda i: (0, 0, 0, 0))
     g_spec = pl.BlockSpec((1, chunk, local), lambda i: (i, 0, 0))
@@ -379,11 +394,7 @@
         nbytes=2 * mm_bytes,
     )(x0, x1, all_near, all_other)
     grad_weight = jnp.transpose(grad_weight, (1, 0, 2))
-    small = small.astype(F32)
-    grad_long = small[:, :groups, ::-1].reshape(ngroups, ntaps)
-    grad_short = (
-        small[:, groups : groups + 3 * nshort].transpose(1, 0, 2).reshape(nshort, 3, local)
-    )
+    grad_short = grad_short.reshape(nshort, 3, local)
     return (mixed, grad_in, grad_weight, grad_long, grad_short)
 
 

time: 176 us -> 173 us (0.983)
  the two profiles are of different devices: /device:TPU:4 before, /device:TPU:1 now
where the time goes in v7:
time: 173 us
  waiting for transfers between devices  66 us (38%)
  starting transfers between devices  64.9 us (38%)
  Pallas kernels  24.5 us (14%)
  local copies, waits for them, and re-layouts  11.3 us (7%)
  other arithmetic  4.97 us (3%)
    ppermute x2, starting transfers between devices, sum_over_line(): from_left = lax.ppermute(far, 'dp', [(a, a + 1) for a in range(ndp // 2)])  11.9 us
    ppermute x2, waiting for transfers between devices, gather_over_line(): before = lax.ppermute(own, ('dp', 'row'), shift(1))  10.8 us
    ppermute x2, waiting for transfers between devices, gather_over_line(): far_after = lax.ppermute(after, 'dp', [(a + 1, a) for a in range(ndp // 2)])  10.6 us
    ppermute x2, starting transfers between devices, sum_over_line(): lax.ppermute(right + from_left, 'dp', [(a, (a + 1) % ndp) for a in range(...  8.72 us
    ppermute x2, starting transfers between devices, gather_over_line(): after = lax.ppermute(own, ('dp', 'row'), shift(-1))  8.53 us
    ppermute x1, waiting for transfers between devices, move_activations(): moved = lax.ppermute(tokens, ('dp', 'row'), swap)  8.53 us
    ppermute x3, waiting for transfers between devices, move_activations(): lax.ppermute(sent, ('row', 'col'), [(b, a) for a, b in offset(*p)])  7.9 us
    unnamed x29, local copies, waits for them, and re-layouts  7.69 us
  transfers between devices with their start and end apart: 30, of which 16 were waited for; matrix products, arithmetic and copies ran while one was open for 5% of the time, Pallas kernels for 10%

profile of v7, /device:TPU:1, one launch (start us, length us, event | category | flops | bytes accessed | tf_op | source)
XLA Modules:
  0.0 172.5 jit_solution(6167854937579561164)
XLA Ops:
  0.6 4.7 %collective-permute-start = (bf16[192,512]{1,0:T(8,128)(2,1)}, bf16[192,512]{1,0:T(8,128)(2,1)S(1)}, u32[]{:S(2)}, u32[]{:S(2)}) collective-permute-start(bf16[192,512]{1,0:T(8,128)(2,1)} %param.5), channel_id=1, source_target_pairs={{0,0},{16,2},{8,4},{24,6},{2,8},{18,10},{10,12},{26,14},{4,16},{20... | collective-permute-start | bytes 589832 | tf_op jit(solution)/shard_map/ppermute | solution.py:302
  6.1 3.7 %all-to-all-start = ((bf16[192,4,128]{2,0,1:T(8,128)(2,1)}), bf16[192,4,128]{2,0,1:T(8,128)(2,1)S(1)}, u32[]{:S(2)}, u32[]{:S(2)}) async-start(bf16[192,4,128]{2,0,1:T(8,128)(2,1)} %copy_bitcast_fusion.1), calls=%async_computation | async-start | bytes 393216 | tf_op jit(solution)/shard_map/all_to_all | solution.py:304
  9.8 8.5 %collective-permute-done = bf16[192,512]{1,0:T(8,128)(2,1)S(1)} collective-permute-done((bf16[192,512]{1,0:T(8,128)(2,1)}, bf16[192,512]{1,0:T(8,128)(2,1)S(1)}, u32[]{:S(2)}, u32[]{:S(2)}) %collective-permute-start) | collective-permute-done | bytes 196640 | tf_op jit(solution)/shard_map/ppermute | solution.py:302
  21.0 2.9 %collective-permute-done.3 = bf16[192,512]{1,0:T(8,128)(2,1)S(1)} collective-permute-done((bf16[192,512]{1,0:T(8,128)(2,1)S(1)}, bf16[192,512]{1,0:T(8,128)(2,1)S(1)}, u32[]{:S(2)}, u32[]{:S(2)}) %collective-permute-start.3) | collective-permute-done | bytes 196640 | tf_op jit(solution)/shard_map/ppermute | solution.py:303
  26.1 3.8 %shard_map.92 = (bf16[3,384,128]{2,1,0:T(8,128)(2,1)S(1)}, bf16[3,384,128]{2,1,0:T(8,128)(2,1)S(1)}, bf16[3,384,128]{2,1,0:T(8,128)(2,1)S(1)}, bf16[3,384,128]{2,1,0:T(8,128)(2,1)S(1)}) custom-call(bf16[2,2,192,512]{3,2,1,0:T(8,128)(2,1)S(1)} %bitcast.35, bf16[3,1024,512]{2,1,0:T(8,128)(2,1)} %bitcast.7.w_ref.refs_10_), custom_call_target="tpu_custom_call" | custom-call | flops 1207959552 | bytes 5111808 | tf_op jit(solution)/shard_map/pallas_call | solution.py:325
  31.9 7.6 %collective-permute-start.4 = (bf16[1152,128]{1,0:T(8,128)(2,1)S(1)}, bf16[1152,128]{1,0:T(8,128)(2,1)S(1)}, u32[]{:S(2)}, u32[]{:S(2)}) collective-permute-start(bf16[1152,128]{1,0:T(8,128)(2,1)S(1)} %bitcast.39), channel_id=1, source_target_pairs={{0,8},{8,16},{1,9},{9,17},{2,10},{10,18},{3,11},{11,19},{4,12},{12... | collective-permute-start | bytes 884744 | tf_op jit(solution)/shard_map/ppermute | solution.py:253
  40.3 3.9 %collective-permute-start.7 = (bf16[1152,128]{1,0:T(8,128)(2,1)}, bf16[1152,128]{1,0:T(8,128)(2,1)S(1)}, u32[]{:S(2)}, u32[]{:S(2)}) collective-permute-start(bf16[1152,128]{1,0:T(8,128)(2,1)} %bitcast_add_fusion.2), channel_id=1, source_target_pairs={{0,24},{8,0},{16,8},{24,16},{1,25},{9,1},{17,9},{25,17},{2,26},{10... | collective-permute-start | bytes 884744 | tf_op jit(solution)/shard_map/ppermute | solution.py:256
  44.2 3.8 %shard_map.93 = (bf16[3,384,128]{2,1,0:T(8,128)(2,1)S(1)}, bf16[3,384,128]{2,1,0:T(8,128)(2,1)S(1)}, bf16[3,384,128]{2,1,0:T(8,128)(2,1)S(1)}, bf16[3,384,128]{2,1,0:T(8,128)(2,1)S(1)}) custom-call(bf16[2,2,192,512]{3,2,1,0:T(8,128)(2,1)S(1)} %collective-permute-done.8.x_ref.x1_ref, bf16[3,1024,512]{2,1,0:T(8,128)(2,1)} %bitcast.7.w_ref.refs_10_), custom_call_target="tpu_custom_call" | custom-call | flops 1207959552 | bytes 5111808 | tf_op jit(solution)/shard_map/pallas_call | solution.py:325
  49.5 5.4 %collective-permute-start.5 = (bf16[1152,128]{1,0:T(8,128)(2,1)}, bf16[1152,128]{1,0:T(8,128)(2,1)S(1)}, u32[]{:S(2)}, u32[]{:S(2)}) collective-permute-start(bf16[1152,128]{1,0:T(8,128)(2,1)} %bitcast_add_fusion.3), channel_id=1, source_target_pairs={{0,8},{8,16},{16,24},{24,0},{1,9},{9,17},{17,25},{25,1},{2,10},{10... | collective-permute-start | bytes 884744 | tf_op jit(solution)/shard_map/ppermute | solution.py:255
  55.0 4.3 %collective-permute-start.9 = (bf16[1152,128]{1,0:T(8,128)(2,1)S(1)}, bf16[1152,128]{1,0:T(8,128)(2,1)S(1)}, u32[]{:S(2)}, u32[]{:S(2)}) collective-permute-start(bf16[1152,128]{1,0:T(8,128)(2,1)S(1)} %bitcast.41), channel_id=1, source_target_pairs={{0,8},{8,16},{1,9},{9,17},{2,10},{10,18},{3,11},{11,19},{4,12},{12... | collective-permute-start | bytes 884744 | tf_op jit(solution)/shard_map/ppermute | solution.py:253
  61.6 5.0 %collective-permute-done.9 = bf16[1152,128]{1,0:T(8,128)(2,1)S(1)} collective-permute-done((bf16[1152,128]{1,0:T(8,128)(2,1)S(1)}, bf16[1152,128]{1,0:T(8,128)(2,1)S(1)}, u32[]{:S(2)}, u32[]{:S(2)}) %collective-permute-start.9) | collective-permute-done | bytes 294944 | tf_op jit(solution)/shard_map/ppermute | solution.py:253
  67.4 3.3 %collective-permute-start.10 = (bf16[1152,128]{1,0:T(8,128)(2,1)}, bf16[1152,128]{1,0:T(8,128)(2,1)}, u32[]{:S(2)}, u32[]{:S(2)}) collective-permute-start(bf16[1152,128]{1,0:T(8,128)(2,1)} %bitcast_add_fusion.1), channel_id=1, source_target_pairs={{0,8},{8,16},{16,24},{24,0},{1,9},{9,17},{17,25},{25,1},{2,10},{10... | collective-permute-start | bytes 884744 | tf_op jit(solution)/shard_map/ppermute | solution.py:255
  72.9 4.2 %collective-permute-done.12.refs_5_ = bf16[1152,128]{1,0:T(8,128)(2,1)S(1)} collective-permute-done((bf16[1152,128]{1,0:T(8,128)(2,1)}, bf16[1152,128]{1,0:T(8,128)(2,1)S(1)}, u32[]{:S(2)}, u32[]{:S(2)}) %collective-permute-start.12) | collective-permute-done | bytes 294944 | tf_op jit(solution)/shard_map/ppermute | solution.py:256
  83.5 4.1 %shard_map.95 = (bf16[1184,128]{1,0:T(8,128)(2,1)S(1)}, bf16[1152,128]{1,0:T(8,128)(2,1)}, bf16[768,128]{1,0:T(8,128)(2,1)}) custom-call(bf16[1152,128]{1,0:T(8,128)(2,1)S(1)} %bitcast.42, bf16[1152,128]{1,0:T(8,128)(2,1)S(1)} %collective-permute-done.5.refs_1_, bf16[1152,128]{1,0:T(8,128)(2,1)S(1)} %collective-permute-done.7.refs_2_, ...), custom_call_target="tpu_custom_call" | custom-call | flops 1207959552 | bytes 2752512 | tf_op jit(solution)/shard_map/pallas_call | solution.py:344
  87.7 6.8 %collective-permute-start.19 = (bf16[1152,128]{1,0:T(8,128)(2,1)}, bf16[1152,128]{1,0:T(8,128)(2,1)S(1)}, u32[]{:S(2)}, u32[]{:S(2)}) collective-permute-start(bf16[1152,128]{1,0:T(8,128)(2,1)} %get-tuple-element.57), channel_id=1, source_target_pairs={{0,26},{2,24},{4,30},{6,28},{8,2},{10,0},{12,6},{14,4},{16,10},{18... | collective-permute-start | bytes 884744 | tf_op jit(solution)/shard_map/ppermute | solution.py:271
  96.3 5.0 %collective-permute-done.19.refs_7_ = bf16[1152,128]{1,0:T(8,128)(2,1)S(1)} collective-permute-done((bf16[1152,128]{1,0:T(8,128)(2,1)}, bf16[1152,128]{1,0:T(8,128)(2,1)S(1)}, u32[]{:S(2)}, u32[]{:S(2)}) %collective-permute-start.19) | collective-permute-done | bytes 294944 | tf_op jit(solution)/shard_map/ppermute | solution.py:271
  101.3 5.7 %all-to-all-start.1 = ((bf16[4,192,128]{2,1,0:T(8,128)(2,1)}), bf16[4,192,128]{2,1,0:T(8,128)(2,1)S(1)}, u32[]{:S(2)}, u32[]{:S(2)}) async-start(bf16[4,192,128]{2,1,0:T(8,128)(2,1)} %bitcast.16), calls=%async_computation.1 | async-start | bytes 393216 | tf_op jit(solution)/shard_map/all_to_all | solution.py:359
  109.0 7.9 %collective-permute-done.13.refs_1_ = bf16[1184,128]{1,0:T(8,128)(2,1)S(1)} collective-permute-done((bf16[1184,128]{1,0:T(8,128)(2,1)S(1)}, bf16[1184,128]{1,0:T(8,128)(2,1)S(1)}, u32[]{:S(2)}, u32[]{:S(2)}) %collective-permute-start.13) | collective-permute-done | bytes 303136 | tf_op jit(solution)/shard_map/ppermute | solution.py:270
  117.6 2.9 %collective-permute-done.18.refs_6_ = bf16[1152,128]{1,0:T(8,128)(2,1)} collective-permute-done((bf16[1152,128]{1,0:T(8,128)(2,1)}, bf16[1152,128]{1,0:T(8,128)(2,1)}, u32[]{:S(2)}, u32[]{:S(2)}) %collective-permute-start.18) | collective-permute-done | bytes 294944 | tf_op jit(solution)/shard_map/ppermute | solution.py:270
  126.7 10.6 %collective-permute-done.21.refs_9_ = bf16[1152,128]{1,0:T(8,128)(2,1)} collective-permute-done((bf16[1152,128]{1,0:T(8,128)(2,1)S(1)}, bf16[1152,128]{1,0:T(8,128)(2,1)}, u32[]{:S(2)}, u32[]{:S(2)}) %collective-permute-start.21) | collective-permute-done | bytes 294944 | tf_op jit(solution)/shard_map/ppermute | solution.py:274
  138.7 7.4 %shard_map.96 = (bf16[3,384,512]{2,1,0:T(8,128)(2,1)}, bf16[3,384,512]{2,1,0:T(8,128)(2,1)}, f32[32,128]{1,0:T(8,128)}, f32[9,512]{1,0:T(8,128)}, bf16[192,512]{...) custom-call(bf16[1184,128]{1,0:T(8,128)(2,1)} %copy-done.2, ...), custom_call_target="tpu_custom_call" | custom-call | flops 2415919104 | bytes 10223616 | tf_op jit(solution)/shard_map/pallas_call | solution.py:364
  154.4 4.3 %collective-permute-done.25 = bf16[192,512]{1,0:T(8,128)(2,1)S(1)} collective-permute-done((bf16[192,512]{1,0:T(8,128)(2,1)}, bf16[192,512]{1,0:T(8,128)(2,1)S(1)}, u32[]{:S(2)}, u32[]{:S(2)}) %collective-permute-start.25) | collective-permute-done | bytes 196640 | tf_op jit(solution)/shard_map/ppermute | solution.py:377
  159.8 3.4 %collective-permute-start.27 = (bf16[192,512]{1,0:T(8,128)(2,1)S(1)}, bf16[192,512]{1,0:T(8,128)(2,1)S(1)}, u32[]{:S(2)}, u32[]{:S(2)}) collective-permute-start(bf16[192,512]{1,0:T(8,128)(2,1)S(1)} %add_convert_fusion), channel_id=1, source_target_pairs={{0,0},{2,16},{4,8},{6,24},{8,2},{10,18},{12,10},{14,26},{16,4},{18... | collective-permute-start | bytes 589832 | tf_op jit(solution)/shard_map/ppermute | solution.py:383
  164.4 4.7 %shard_map.97 = f32[3,1024,512]{2,1,0:T(8,128)} custom-call(bf16[2,2,192,512]{3,2,1,0:T(8,128)(2,1)S(1)} %bitcast.36, bf16[2,2,192,512]{3,2,1,0:T(8,128)(2,1)S(1)} %collective-permute-done.8.x_ref.x1_ref, bf16[3,384,512]{2,1,0:T(8,128)(2,1)S(1)} %copy-done.1, bf16[3,384,512]{2,1,0:T(8,128)(2,1)S(1)} %collective-permute-done.26.g1_ref), custom_call_target="tpu_custom_call" | custom-call | flops 2415919104 | bytes 10223616 | tf_op jit(solution)/shard_map/pallas_call | solution.py:387
  (87 shorter events, 47.6 us)
Async XLA Ops:
  0.6 17.7 %collective-permute-start = (bf16[192,512]{1,0:T(8,128)(2,1)}, bf16[192,512]{1,0:T(8,128)(2,1)S(1)}, u32[]{:S(2)}, u32[]{:S(2)}) collective-permute-start(bf16[192,512]{1,0:T(8,128)(2,1)} %param.5), channel_id=1, source_target_pairs={{0,0},{16,2},{8,4},{24,6},{2,8},{18,10},{10,12},{26,14},{4,16},{20... | collective-permute-start | bytes 589832 | tf_op jit(solution)/shard_map/ppermute | solution.py:302
  6.1 14.9 %all-to-all-start = ((bf16[192,4,128]{2,0,1:T(8,128)(2,1)}), bf16[192,4,128]{2,0,1:T(8,128)(2,1)S(1)}, u32[]{:S(2)}, u32[]{:S(2)}) async-start(bf16[192,4,128]{2,0,1:T(8,128)(2,1)} %copy_bitcast_fusion.1), calls=%async_computation | async-start | bytes 393216 | tf_op jit(solution)/shard_map/all_to_all | solution.py:304
  26.0 18.2 %collective-permute-start.8 = (bf16[2,2,192,512]{3,2,1,0:T(8,128)(2,1)S(1)}, bf16[2,2,192,512]{3,2,1,0:T(8,128)(2,1)S(1)}, u32[]{:S(2)}, u32[]{:S(2)}) collective-permute-start(bf16[2,2,192,512]{3,2,1,0:T(8,128)(2,1)S(1)} %bitcast.34), channel_id=1, source_target_pairs={{0,2},{2,0},{4,6},{6,4},{1,3},{3,1},{5,7},{7,5},{8,10},{10,8},{12,... | collective-permute-start | bytes 2359304 | tf_op jit(solution)/shard_map/ppermute | solution.py:307
  31.3 107.4 %collective-permute-start.22 = (bf16[3,1024,512]{2,1,0:T(8,128)(2,1)}, bf16[3,1024,512]{2,1,0:T(8,128)(2,1)}, u32[]{:S(2)}, u32[]{:S(2)}) collective-permute-start(bf16[3,1024,512]{2,1,0:T(8,128)(2,1)} %bitcast.7.w_ref.refs_10_), channel_id=1, source_target_pairs={{0,2},{2,0},{4,6},{6,4},{1,3},{3,1},{5,7},{7,5},{8,10},{10,8},{12,... | collective-permute-start | bytes 9437192 | tf_op jit(solution)/shard_map/ppermute | solution.py:375
  31.9 16.9 %collective-permute-start.4 = (bf16[1152,128]{1,0:T(8,128)(2,1)S(1)}, bf16[1152,128]{1,0:T(8,128)(2,1)S(1)}, u32[]{:S(2)}, u32[]{:S(2)}) collective-permute-start(bf16[1152,128]{1,0:T(8,128)(2,1)S(1)} %bitcast.39), channel_id=1, source_target_pairs={{0,8},{8,16},{1,9},{9,17},{2,10},{10,18},{3,11},{11,19},{4,12},{12... | collective-permute-start | bytes 884744 | tf_op jit(solution)/shard_map/ppermute | solution.py:253
  40.3 32.6 %collective-permute-start.7 = (bf16[1152,128]{1,0:T(8,128)(2,1)}, bf16[1152,128]{1,0:T(8,128)(2,1)S(1)}, u32[]{:S(2)}, u32[]{:S(2)}) collective-permute-start(bf16[1152,128]{1,0:T(8,128)(2,1)} %bitcast_add_fusion.2), channel_id=1, source_target_pairs={{0,24},{8,0},{16,8},{24,16},{1,25},{9,1},{17,9},{25,17},{2,26},{10... | collective-permute-start | bytes 884744 | tf_op jit(solution)/shard_map/ppermute | solution.py:256
  48.1 11.2 %collective-permute-start.11 = (bf16[1152,128]{1,0:T(8,128)(2,1)S(1)}, bf16[1152,128]{1,0:T(8,128)(2,1)S(1)}, u32[]{:S(2)}, u32[]{:S(2)}) collective-permute-start(bf16[1152,128]{1,0:T(8,128)(2,1)S(1)} %bitcast.40), channel_id=1, source_target_pairs={{16,8},{24,16},{17,9},{25,17},{18,10},{26,18},{19,11},{27,19},{20,... | collective-permute-start | bytes 884744 | tf_op jit(solution)/shard_map/ppermute | solution.py:254
  49.5 23.4 %collective-permute-start.5 = (bf16[1152,128]{1,0:T(8,128)(2,1)}, bf16[1152,128]{1,0:T(8,128)(2,1)S(1)}, u32[]{:S(2)}, u32[]{:S(2)}) collective-permute-start(bf16[1152,128]{1,0:T(8,128)(2,1)} %bitcast_add_fusion.3), channel_id=1, source_target_pairs={{0,8},{8,16},{16,24},{24,0},{1,9},{9,17},{17,25},{25,1},{2,10},{10... | collective-permute-start | bytes 884744 | tf_op jit(solution)/shard_map/ppermute | solution.py:255
  55.0 11.7 %collective-permute-start.9 = (bf16[1152,128]{1,0:T(8,128)(2,1)S(1)}, bf16[1152,128]{1,0:T(8,128)(2,1)S(1)}, u32[]{:S(2)}, u32[]{:S(2)}) collective-permute-start(bf16[1152,128]{1,0:T(8,128)(2,1)S(1)} %bitcast.41), channel_id=1, source_target_pairs={{0,8},{8,16},{1,9},{9,17},{2,10},{10,18},{3,11},{11,19},{4,12},{12... | collective-permute-start | bytes 884744 | tf_op jit(solution)/shard_map/ppermute | solution.py:253
  60.0 17.1 %collective-permute-start.12 = (bf16[1152,128]{1,0:T(8,128)(2,1)}, bf16[1152,128]{1,0:T(8,128)(2,1)S(1)}, u32[]{:S(2)}, u32[]{:S(2)}) collective-permute-start(bf16[1152,128]{1,0:T(8,128)(2,1)} %bitcast_add_fusion), channel_id=1, source_target_pairs={{0,24},{8,0},{16,8},{24,16},{1,25},{9,1},{17,9},{25,17},{2,26},{10... | collective-permute-start | bytes 884744 | tf_op jit(solution)/shard_map/ppermute | solution.py:256
  67.4 13.2 %collective-permute-start.10 = (bf16[1152,128]{1,0:T(8,128)(2,1)}, bf16[1152,128]{1,0:T(8,128)(2,1)}, u32[]{:S(2)}, u32[]{:S(2)}) collective-permute-start(bf16[1152,128]{1,0:T(8,128)(2,1)} %bitcast_add_fusion.1), channel_id=1, source_target_pairs={{0,8},{8,16},{16,24},{24,0},{1,9},{9,17},{17,25},{25,1},{2,10},{10... | collective-permute-start | bytes 884744 | tf_op jit(solution)/shard_map/ppermute | solution.py:255
  87.7 13.7 %collective-permute-start.19 = (bf16[1152,128]{1,0:T(8,128)(2,1)}, bf16[1152,128]{1,0:T(8,128)(2,1)S(1)}, u32[]{:S(2)}, u32[]{:S(2)}) collective-permute-start(bf16[1152,128]{1,0:T(8,128)(2,1)} %get-tuple-element.57), channel_id=1, source_target_pairs={{0,26},{2,24},{4,30},{6,28},{8,2},{10,0},{12,6},{14,4},{16,10},{18... | collective-permute-start | bytes 884744 | tf_op jit(solution)/shard_map/ppermute | solution.py:271
  94.5 13.3 %collective-permute-start.14 = (bf16[1184,128]{1,0:T(8,128)(2,1)S(1)}, bf16[1184,128]{1,0:T(8,128)(2,1)S(1)}, u32[]{:S(2)}, u32[]{:S(2)}) collective-permute-start(bf16[1184,128]{1,0:T(8,128)(2,1)S(1)} %get-tuple-element.59.refs_0_), channel_id=1, source_target_pairs={{0,24},{2,26},{4,28},{6,30},{8,0},{10,2},{12,4},{14,6},{16,8},{18,... | collective-permute-start | bytes 909320 | tf_op jit(solution)/shard_map/ppermute | solution.py:271
  96.2 20.7 %collective-permute-start.13 = (bf16[1184,128]{1,0:T(8,128)(2,1)S(1)}, bf16[1184,128]{1,0:T(8,128)(2,1)S(1)}, u32[]{:S(2)}, u32[]{:S(2)}) collective-permute-start(bf16[1184,128]{1,0:T(8,128)(2,1)S(1)} %get-tuple-element.59.refs_0_), channel_id=1, source_target_pairs={{0,8},{2,10},{4,12},{6,14},{8,16},{10,18},{12,20},{14,22},{16,24},... | collective-permute-start | bytes 909320 | tf_op jit(solution)/shard_map/ppermute | solution.py:270
  96.2 24.3 %collective-permute-start.18 = (bf16[1152,128]{1,0:T(8,128)(2,1)}, bf16[1152,128]{1,0:T(8,128)(2,1)}, u32[]{:S(2)}, u32[]{:S(2)}) collective-permute-start(bf16[1152,128]{1,0:T(8,128)(2,1)} %get-tuple-element.57), channel_id=1, source_target_pairs={{0,10},{2,8},{4,14},{6,12},{8,18},{10,16},{12,22},{14,20},{16,26},... | collective-permute-start | bytes 884744 | tf_op jit(solution)/shard_map/ppermute | solution.py:270
  101.3 20.4 %collective-permute-start.17 = (bf16[1152,128]{1,0:T(8,128)(2,1)}, bf16[1152,128]{1,0:T(8,128)(2,1)}, u32[]{:S(2)}, u32[]{:S(2)}) collective-permute-start(bf16[1152,128]{1,0:T(8,128)(2,1)} %get-tuple-element.57), channel_id=1, source_target_pairs={{0,2},{2,0},{4,6},{6,4},{8,10},{10,8},{12,14},{14,12},{16,18},{18,... | collective-permute-start | bytes 884744 | tf_op jit(solution)/shard_map/ppermute | solution.py:272
  101.3 24.6 %all-to-all-start.1 = ((bf16[4,192,128]{2,1,0:T(8,128)(2,1)}), bf16[4,192,128]{2,1,0:T(8,128)(2,1)S(1)}, u32[]{:S(2)}, u32[]{:S(2)}) async-start(bf16[4,192,128]{2,1,0:T(8,128)(2,1)} %bitcast.16), calls=%async_computation.1 | async-start | bytes 393216 | tf_op jit(solution)/shard_map/all_to_all | solution.py:359
  107.7 29.5 %collective-permute-start.16 = (bf16[1184,128]{1,0:T(8,128)(2,1)S(1)}, bf16[1184,128]{1,0:T(8,128)(2,1)S(1)}, u32[]{:S(2)}, u32[]{:S(2)}) collective-permute-start(bf16[1184,128]{1,0:T(8,128)(2,1)S(1)} %collective-permute-done.14.refs_2_), channel_id=1, source_target_pairs={{8,0},{16,8},{9,1},{17,9},{10,2},{18,10},{11,3},{19,11},{12,4},{20... | collective-permute-start | bytes 909320 | tf_op jit(solution)/shard_map/ppermute | solution.py:274
  116.9 20.4 %collective-permute-start.15 = (bf16[1184,128]{1,0:T(8,128)(2,1)S(1)}, bf16[1184,128]{1,0:T(8,128)(2,1)S(1)}, u32[]{:S(2)}, u32[]{:S(2)}) collective-permute-start(bf16[1184,128]{1,0:T(8,128)(2,1)S(1)} %collective-permute-done.13.refs_1_), channel_id=1, source_target_pairs={{8,16},{16,24},{9,17},{17,25},{10,18},{18,26},{11,19},{19,27},{12,... | collective-permute-start | bytes 909320 | tf_op jit(solution)/shard_map/ppermute | solution.py:273
  120.5 16.8 %collective-permute-start.21 = (bf16[1152,128]{1,0:T(8,128)(2,1)S(1)}, bf16[1152,128]{1,0:T(8,128)(2,1)}, u32[]{:S(2)}, u32[]{:S(2)}) collective-permute-start(bf16[1152,128]{1,0:T(8,128)(2,1)S(1)} %collective-permute-done.19.refs_7_), channel_id=1, source_target_pairs={{8,0},{16,8},{9,1},{17,9},{10,2},{18,10},{11,3},{19,11},{12,4},{20... | collective-permute-start | bytes 884744 | tf_op jit(solution)/shard_map/ppermute | solution.py:274
  121.8 15.5 %collective-permute-start.20 = (bf16[1152,128]{1,0:T(8,128)(2,1)}, bf16[1152,128]{1,0:T(8,128)(2,1)}, u32[]{:S(2)}, u32[]{:S(2)}) collective-permute-start(bf16[1152,128]{1,0:T(8,128)(2,1)} %collective-permute-done.18.refs_6_), channel_id=1, source_target_pairs={{8,16},{16,24},{9,17},{17,25},{10,18},{18,26},{11,19},{19,27},{12,... | collective-permute-start | bytes 884744 | tf_op jit(solution)/shard_map/ppermute | solution.py:273
  146.1 13.7 %collective-permute-start.26 = (bf16[3,384,512]{2,1,0:T(8,128)(2,1)}, bf16[3,384,512]{2,1,0:T(8,128)(2,1)S(1)}, u32[]{:S(2)}, u32[]{:S(2)}) collective-permute-start(bf16[3,384,512]{2,1,0:T(8,128)(2,1)} %get-tuple-element.73), channel_id=1, source_target_pairs={{0,2},{2,0},{4,6},{6,4},{1,3},{3,1},{5,7},{7,5},{8,10},{10,8},{12,... | collective-permute-start | bytes 3538952 | tf_op jit(solution)/shard_map/ppermute | solution.py:381
  148.3 10.5 %collective-permute-start.25 = (bf16[192,512]{1,0:T(8,128)(2,1)}, bf16[192,512]{1,0:T(8,128)(2,1)S(1)}, u32[]{:S(2)}, u32[]{:S(2)}) collective-permute-start(bf16[192,512]{1,0:T(8,128)(2,1)} %get-tuple-element.72), channel_id=1, source_target_pairs={{5,0},{4,1},{7,2},{6,3},{1,4},{0,5},{3,6},{2,7},{13,8},{12,9},{15,... | collective-permute-start | bytes 589832 | tf_op jit(solution)/shard_map/ppermute | solution.py:377
  159.8 12.0 %collective-permute-start.27 = (bf16[192,512]{1,0:T(8,128)(2,1)S(1)}, bf16[192,512]{1,0:T(8,128)(2,1)S(1)}, u32[]{:S(2)}, u32[]{:S(2)}) collective-permute-start(bf16[192,512]{1,0:T(8,128)(2,1)S(1)} %add_convert_fusion), channel_id=1, source_target_pairs={{0,0},{2,16},{4,8},{6,24},{8,2},{10,18},{12,10},{14,26},{16,4},{18... | collective-permute-start | bytes 589832 | tf_op jit(solution)/shard_map/ppermute | solution.py:383
  (20 other events, 155.0 us)

commit v8 on v7

--- a/solution.py
+++ b/solution.py
@@ -8,13 +8,14 @@
 from jax.sharding import PartitionSpec as P
 
 VMEM_BYTES = 48 * 2**20
+MOST_VMEM_BYTES = 62 * 2**20
 F32 = jnp.float32
 BF16 = jnp.bfloat16
 
 
-def kernel_call(body, outs, grid=None, in_specs=None, out_specs=None, scratch=(), flops=0, nbytes=0, vmem=VMEM_BYTES):
+def kernel_call(body, outs, grid=(), in_specs=None, out_specs=None, scratch=(), flops=0, nbytes=0, vmem=VMEM_BYTES):
     kwargs = {}
-    if grid is not None:
+    if in_specs is not None:
         kwargs = dict(grid=grid, in_specs=in_specs, out_specs=out_specs)
     return pl.pallas_call(
         body,
@@ -72,64 +73,110 @@
         out_ref[0] = held[wrapped(z + ahead, len(out_refs))]
 
 
-def assemble(pieces, held, ndp):
-    z = lax.axis_index("dp")
-    own, before, after, far_before, far_after = pieces
-    held[z] = own[...]
-    held[wrapped(z - 1, ndp)] = before[...]
-    held[wrapped(z + 1, ndp)] = after[...]
-
-    @pl.when(z >= ndp // 2)
-    def _():
-        held[z - ndp // 2] = far_before[...]
-
-    @pl.when(z < ndp // 2)
-    def _():
-        held[z + ndp // 2] = far_after[...]
-
-
-def input_grad_body(*refs):
-    pieces, (w_ref, partner_w_ref, near_ref, far_ref, long_ref, short_ref), refs = refs[:10], refs[10:16], refs[16:]
-    *out_refs, near_held, far_held = refs
-    tokens = near_ref.shape[1]
-    rows, depth = out_refs[0].shape
-    ndp, _, width = near_held.shape
-    ncol = w_ref.shape[1] // depth
-    col = lax.axis_index("col")
-    assemble(pieces[:5], near_held, ndp)
-    assemble(pieces[5:], far_held, ndp)
-    groups = long_ref.shape[0] // ndp
-    for owner in range(ndp):
-        small = near_held[owner, 3 * tokens :].astype(F32)
-        long_ref[owner * groups : (owner + 1) * groups] = small[:groups]
-        short_ref[:, owner * width : (owner + 1) * width] = small[groups : groups + short_ref.shape[0]]
-    for held, all_ref in ((near_held, near_ref), (far_held, far_ref)):
-        for i in range(3):
-            for owner in range(ndp):
-                all_ref[i, :, owner * width : (owner + 1) * width] = held[owner, i * tokens : (i + 1) * tokens]
-    for dx in range(ncol):
-        start = pl.multiple_of(wrapped(col - dx, ncol) * depth, depth)
-        total = jnp.zeros((tokens, depth), F32)
-        for all_ref, weights in ((near_ref, w_ref), (far_ref, partner_w_ref)):
+def first_grad_body(near, near_before, near_after, far, far_before, far_after, w_ref, partner_w_ref, out_ref, far_ref, held):
+    ndp, _, width = held.shape
+    ncol, tokens, depth = out_ref.shape
+    z, col = lax.axis_index("dp"), lax.axis_index("col")
+    far_ref[0], far_ref[1], far_ref[2] = far[...], far_before[...], far_after[...]
+    for pieces, weights, first in (
+        ((near, near_before, near_after), w_ref, True),
+        ((far, far_before, far_after), partner_w_ref, False),
+    ):
+        held[wrapped(z + ndp // 2, ndp)] = jnp.zeros(held.shape[1:], BF16)
+        for ahead, piece in zip((0, -1, 1), pieces):
+            held[wrapped(z + ahead, ndp)] = piece[: 3 * tokens]
+        for dx in range(ncol):
+            start = pl.multiple_of(wrapped(col - dx, ncol) * depth, depth)
+            total = jnp.zeros((tokens, depth), F32) if first else out_ref[dx]
             for i in range(3):
+                rows = slice(i * tokens, (i + 1) * tokens)
                 total += lax.dot_general(
-                    all_ref[i],
+                    jnp.concatenate([held[owner, rows] for owner in range(ndp)], axis=1),
                     weights[i, pl.ds(start, depth), :],
                     (((1,), (1,)), ((), ())),
                     preferred_element_type=F32,
                 )
+            out_ref[dx] = total
+
+
+def second_grad_body(ndp, part_ref, *refs):
+    arrived, weights, refs = (refs[:2], refs[2:4]), refs[4:6], refs[6:]
+    (near_ref, far_ref), refs = refs[:2], refs[2:]
+    *out_refs, held_w, held_part, sems = refs
+    ncol, tokens, depth = held_part.shape
+    rows = out_refs[0].shape[0]
+    width = near_ref.shape[1]
+    z, col = lax.axis_index("dp"), lax.axis_index("col")
+    lanes = pl.ds(pl.multiple_of(wrapped(z + ndp // 2, ndp) * width, width), width)
+    copies = [
+        pltpu.make_async_copy(w_ref.at[:, :, lanes], held_w.at[k], sems.at[k]) for k, w_ref in enumerate(weights)
+    ]
+    copies.append(pltpu.make_async_copy(part_ref, held_part, sems.at[2]))
+    for copy in copies:
+        copy.start()
+    for k, (pair, target) in enumerate(zip(arrived, (near_ref, far_ref))):
+        for source, here in zip(pair, (z >= ndp // 2, z < ndp // 2)):
+
+            @pl.when(here)
+            def _(source=source, target=target, k=k):
+                copy = pltpu.make_async_copy(source, target, sems.at[3 + k])
+                copy.start()
+                copy.wait()
+
+    for copy in copies:
+        copy.wait()
+    left = jnp.concatenate(
+        [ref[i * tokens : (i + 1) * tokens] for ref in (near_ref, far_ref) for i in range(3)], axis=1
+    )
+    for dx in range(ncol):
+        start = pl.multiple_of(wrapped(col - dx, ncol) * depth, depth)
+        right = jnp.concatenate([held_w[k, i, pl.ds(start, depth), :] for k in range(2) for i in range(3)], axis=1)
+        total = held_part[dx] + lax.dot_general(
+            left, right, (((1,), (1,)), ((), ())), preferred_element_type=F32
+        )
         for block in range(tokens // rows):
             out_refs[block * ncol + dx][...] = total[block * rows : (block + 1) * rows].astype(BF16)
 
 
-def weight_grad_body(scale, x0_ref, x1_ref, g0_ref, g1_ref, out_ref):
+def weight_grad_body(scale, *refs):
+    (x0_ref, x1_ref), near_refs, (far_ref, far_last_ref), mixed_refs, refs = (
+        refs[:2],
+        refs[2:6],
+        refs[6:8],
+        refs[8:12],
+        refs[12:],
+    )
+    out_ref, mixed_ref, long_ref, short_ref, held, held_mixed = refs
     nblocks, ncol, rows, depth = x0_ref.shape
-    col = lax.axis_index("col")
-    gm = jnp.concatenate([g0_ref[0], g1_ref[0]], axis=0)
+    _, ndp, _, width = held.shape
+    tokens = nblocks * rows
+    i = pl.program_id(0)
+    z, col = lax.axis_index("dp"), lax.axis_index("col")
+
+    @pl.when(i == 0)
+    def _():
+        groups = long_ref.shape[0] // ndp
+        for k, ahead in enumerate((0, -1, 1, 2)):
+            owner = wrapped(z + ahead, ndp)
+            held[0, owner] = near_refs[k][...]
+            held[1, owner, : 3 * tokens] = far_ref[k] if k < 3 else far_last_ref[...]
+        for back in range(ndp):
+            held_mixed[wrapped(z - back, ndp)] = mixed_refs[back][...]
+        for owner in range(ndp):
+            lanes = slice(owner * width, (owner + 1) * width)
+            mixed_ref[:, lanes] = held_mixed[owner]
+            small = held[0, owner, 3 * tokens :].astype(F32)
+            long_ref[owner * groups : (owner + 1) * groups] = small[:groups]
+            short_ref[:, lanes] = small[groups : groups + short_ref.shape[0]]
+
+    at = pl.ds(pl.multiple_of(i * tokens, 16), tokens)
+    gm = jnp.concatenate(
+        [jnp.concatenate([held[k, owner, at, :] for owner in range(ndp)], axis=1) for k in range(2)], axis=0
+    )
     for dx in range(ncol):
         start = pl.multiple_of(wrapped(col - dx, ncol) * depth, depth)
         x = jnp.concatenate(
-            [x_ref[:, dx].reshape(nblocks * rows, depth) for x_ref in (x0_ref, x1_ref)], axis=0
+            [x_ref[:, dx].reshape(tokens, depth) for x_ref in (x0_ref, x1_ref)], axis=0
         )
         out_ref[0, pl.ds(start, depth), :] = scale * lax.dot_general(
             x, gm, (((0,), (0,)), ((), ())), preferred_element_type=F32
@@ -149,7 +196,7 @@
 
 def middle_body(scale, nshort, nrow, *refs):
     sums, refs = (refs[:3], refs[3:6]), refs[6:]
-    sf_ref, causal_ref, anti_ref, go_ref, near_ref, other_ref, mixed_ref, m_ref, gm_ref = refs
+    sf_ref, causal_ref, anti_ref, go_ref, near_ref, other_ref, *mixed_refs, m_ref, gm_ref, mixed_ref = refs
     tokens, width = go_ref.shape
     row = lax.axis_index("row")
     nblocks = nrow // 2
@@ -200,6 +247,10 @@
     conv = filtered(causal_ref, p_pairs)
     upstream = go_ref[...].astype(F32)
     mixed_ref[...] = (feats[0] * conv).astype(BF16)
+    ndp = len(mixed_refs)
+    for ahead, out_ref in enumerate(mixed_refs):
+        at = pl.multiple_of(wrapped(lax.axis_index("dp") + ahead, ndp) * (tokens // ndp), 16)
+        out_ref[...] = mixed_ref[pl.ds(at, tokens // ndp)]
     grad_conv = (upstream * feats[0]).astype(BF16)
     c_blocks = [grad_conv[b * block : (b + 1) * block] for b in range(nspans)] + [zero]
     c_pairs = [jnp.concatenate(c_blocks[b : b + 2], axis=0) for b in range(nspans)]
@@ -341,58 +392,93 @@
     half = pl.BlockSpec((groups, ntaps, 2 * ntaps), lambda i: (0, 0, 0))
     other = pl.BlockSpec((groups, ntaps, 2 * ntaps), lambda i: (1, 0, 0))
     whole = lambda *shape: pl.BlockSpec(shape, lambda i: (0,) * len(shape))
-    grad_near, grad_other, mixed = kernel_call(
+    grad_near, grad_other, *mixed = kernel_call(
         functools.partial(middle_body, scale, nshort, nrow),
-        (
-            shaped((3 * chunk + extra, width), BF16),
-            shaped((3 * chunk, width), BF16),
-            shaped((seq, width), BF16),
-        ),
+        [shaped((3 * chunk + extra, width), BF16), shaped((3 * chunk, width), BF16)]
+        + [shaped((rows, width), BF16)] * ndp,
         grid=(1,),
         in_specs=[whole(3 * chunk, width)] * 6
         + [whole(3 * nshort, width), half, other, whole(seq, width)],
-        out_specs=(whole(3 * chunk + extra, width), whole(3 * chunk, width), whole(seq, width)),
-        scratch=[pltpu.VMEM((3 * seq, width), F32), pltpu.VMEM((3 * seq, width), BF16)],
+        out_specs=[whole(3 * chunk + extra, width), whole(3 * chunk, width)] + [whole(rows, width)] * ndp,
+        scratch=[
+            pltpu.VMEM((3 * seq, width), F32),
+            pltpu.VMEM((3 * seq, width), BF16),
+            pltpu.VMEM((seq, width), BF16),
+        ],
         flops=3 * 2 * groups * ntaps * 2 * ntaps * width * (seq // ntaps),
         nbytes=2 * width * seq * 14,
+        vmem=MOST_VMEM_BYTES,
     )(*sums, sf, bands, bands, upstream)
-    mixed = lax.all_to_all(mixed, "dp", split_axis=0, concat_axis=1, tiled=True)
-    pieces = (*gather_over_line(grad_near, False), *gather_over_line(grad_other, True))
-    mixed, *pieces = lax.optimization_barrier((mixed, *pieces))
-    block = shaped((rows, dcol), BF16)
-    all_shape = shaped((3, chunk, local), BF16)
-    all_near, all_far, grad_long, grad_short, *blocks = kernel_call(
-        input_grad_body,
-        [all_shape, all_shape, shaped((ngroups, ntaps), F32), shaped((3 * nshort, local), F32)]
-        + [block] * len(places),
-        scratch=[
-            pltpu.VMEM((ndp, 3 * chunk + extra, width), BF16),
-            pltpu.VMEM((ndp, 3 * chunk, width), BF16),
-        ],
+    mixed = [mixed[0]] + [
+        lax.ppermute(part, "dp", [(a, (a + ahead) % ndp) for a in range(ndp)])
+        for ahead, part in enumerate(mixed)
+        if ahead
+    ]
+    *near, near_far_before, near_far_after = gather_over_line(grad_near, False)
+    *far, far_far_before, far_far_after = gather_over_line(grad_other, True)
+    partner_w = lax.ppermute(w, "row", partner)
+    part, far_three = kernel_call(
+        first_grad_body,
+        [shaped((ncol, chunk, dcol), F32), shaped((3, 3 * chunk, width), BF16)],
+        scratch=[pltpu.VMEM((ndp, 3 * chunk, width), BF16)],
         flops=2 * mm_flops,
         nbytes=2 * mm_bytes,
-        vmem=62 * 2**20,
-    )(*pieces, w, lax.ppermute(w, "row", partner))
+    )(*near, *far, w, partner_w)
+    everywhere = pl.BlockSpec(memory_space=pl.ANY)
+    in_vmem = pl.BlockSpec(memory_space=pltpu.VMEM)
+    near_last, far_last, *blocks = kernel_call(
+        functools.partial(second_grad_body, ndp),
+        [shaped(grad_near.shape, BF16), shaped(grad_other.shape, BF16)]
+        + [shaped((rows, dcol), BF16)] * len(places),
+        grid=(),
+        in_specs=[everywhere] * 7,
+        out_specs=[in_vmem] * (2 + len(places)),
+        scratch=[
+            pltpu.VMEM((2, 3, drow, width), BF16),
+            pltpu.VMEM((ncol, chunk, dcol), F32),
+            pltpu.SemaphoreType.DMA((5,)),
+        ],
+        flops=mm_flops // 2,
+        nbytes=mm_bytes // 2,
+        vmem=MOST_VMEM_BYTES,
+    )(part, near_far_before, near_far_after, far_far_before, far_far_after, w, partner_w)
+    far_three, far_last = lax.optimization_barrier((far_three, far_last))
+    far_three, far_last = (lax.ppermute(part, "row", partner) for part in (far_three, far_last))
     arrivals = [
         lax.ppermute(sent, ("row", "col"), [(b, a) for a, b in offset(*p)])
         for p, sent in zip(places[1:], blocks[1:])
     ]
     arrived = sum((a.astype(F32) for a in arrivals), blocks[0].astype(F32)).astype(BF16)
-    all_other = lax.ppermute(all_far, "row", partner)
-    arrived, all_other = lax.optimization_barrier((arrived, all_other))
+    arrived, far_three, far_last, *mixed = lax.optimization_barrier((arrived, far_three, far_last, *mixed))
     grad_in = lax.ppermute(arrived, ("dp", "row"), swap_back)
 
-    x_spec = pl.BlockSpec((nblocks, ncol, rows, dcol), lambda i: (0, 0, 0, 0))
-    g_spec = pl.BlockSpec((1, chunk, local), lambda i: (i, 0, 0))
-    grad_weight = kernel_call(
+    grad_weight, mixed, grad_long, grad_short = kernel_call(
         functools.partial(weight_grad_body, scale),
-        shaped((3, drow, local), F32),
+        [
+            shaped((3, drow, local), F32),
+            shaped((rows, local), BF16),
+            shaped((ngroups, ntaps), F32),
+            shaped((3 * nshort, local), F32),
+        ],
         grid=(3,),
-        in_specs=[x_spec, x_spec, g_spec, g_spec],
-        out_specs=pl.BlockSpec((1, drow, local), lambda i: (i, 0, 0)),
+        in_specs=[whole(nblocks, ncol, rows, dcol)] * 2
+        + [whole(*grad_near.shape)] * 4
+        + [whole(*far_three.shape), whole(*far_last.shape)]
+        + [whole(rows, width)] * ndp,
+        out_specs=[
+            pl.BlockSpec((1, drow, local), lambda i: (i, 0, 0)),
+            whole(rows, local),
+            whole(ngroups, ntaps),
+            whole(3 * nshort, local),
+        ],
+        scratch=[
+            pltpu.VMEM((2, ndp, 3 * chunk + extra, width), BF16),
+            pltpu.VMEM((ndp, rows, width), BF16),
+        ],
         flops=2 * mm_flops,
         nbytes=2 * mm_bytes,
-    )(x0, x1, all_near, all_other)
+        vmem=MOST_VMEM_BYTES,
+    )(x0, x1, *near, near_last, far_three, far_last, *mixed)
     grad_weight = jnp.transpose(grad_weight, (1, 0, 2))
     grad_short = grad_short.reshape(nshort, 3, local)
     return (mixed, grad_in, grad_weight, grad_long, grad_short)

time: 173 us -> 171 us (0.988)
  Pallas kernels: 24.5 us -> 31.4 us
  waiting for transfers between devices: 66 us -> 62.3 us
  starting transfers between devices: 64.9 us -> 61.9 us
  other arithmetic: 4.97 us -> 2.82 us
  local copies, waits for them, and re-layouts: 11.3 us -> 9.54 us
    pallas_call x3 -> x4, Pallas kernels: 16.2 us -> 22.6 us  [the longest x1 7.06 us: move_activations(): kernel_call(functools.partial(weight_grad_body, scale), [shaped((3, drow,...]
    ppermute x2, waiting for transfers between devices: 10.6 us -> 4.51 us  [gather_over_line(): far_after = lax.ppermute(after, 'dp', [(a + 1, a) for a in range(ndp // 2)])]
    all_to_all x1 -> x0, starting transfers between devices: 5.66 us -> none  [move_activations(): mixed = lax.all_to_all(mixed, 'dp', split_axis=0, concat_axis=1, tiled=True)]
    ppermute x2, waiting for transfers between devices: 5.77 us -> 11.3 us  [gather_over_line(): after = lax.ppermute(own, ('dp', 'row'), shift(-1))]
    ppermute x2, waiting for transfers between devices: 4.22 us -> 0.07 us  [sum_over_line(): lax.ppermute(left + from_right, 'dp', [(a, (a - 1) % ndp) for a in range(...]
    ppermute x2, waiting for transfers between devices: 2.78 us -> 6.76 us  [sum_over_line(): lax.ppermute(right + from_left, 'dp', [(a, (a + 1) % ndp) for a in range(...]
    ppermute x1, starting transfers between devices: 3.36 us -> 6.77 us  [move_activations(): grad_in = lax.ppermute(arrived, ('dp', 'row'), swap_back)]
    all_to_all x1 -> x0, waiting for transfers between devices: 2.83 us -> none  [move_activations(): mixed = lax.all_to_all(mixed, 'dp', split_axis=0, concat_axis=1, tiled=True)]
  transfers between devices with their start and end apart: 30 -> 33, of which waited for: 16 -> 15; matrix products, arithmetic and copies ran while one was open for 5% -> 4% of each run, Pallas kernels for 10% -> 16%
where the time goes in v8:
time: 171 us; the launch traced here: 169 us
  waiting for transfers between devices  62.3 us (36%)
  starting transfers between devices  61.9 us (36%)
  Pallas kernels  31.4 us (18%)
  local copies, waits for them, and re-layouts  9.54 us (6%)
  other arithmetic  2.82 us (2%)
    ppermute x2, starting transfers between devices, sum_over_line(): from_left = lax.ppermute(far, 'dp', [(a, a + 1) for a in range(ndp // 2)])  12.1 us
    ppermute x2, waiting for transfers between devices, gather_over_line(): after = lax.ppermute(own, ('dp', 'row'), shift(-1))  11.3 us
    ppermute x2, waiting for transfers between devices, gather_over_line(): before = lax.ppermute(own, ('dp', 'row'), shift(1))  10.9 us
    ppermute x2, starting transfers between devices, sum_over_line(): lax.ppermute(right + from_left, 'dp', [(a, (a + 1) % ndp) for a in range(...  9.17 us
    ppermute x1, waiting for transfers between devices, move_activations(): moved = lax.ppermute(tokens, ('dp', 'row'), swap)  8.53 us
    pallas_call x2, Pallas kernels, move_activations(): kernel_call(project_body, [shaped((3, chunk, width), BF16)] * ndp, grid=(...  8.13 us
    ppermute x3, waiting for transfers between devices, move_activations(): lax.ppermute(sent, ('row', 'col'), [(b, a) for a, b in offset(*p)])  7.94 us
    ppermute x2, starting transfers between devices, gather_over_line(): after = lax.ppermute(own, ('dp', 'row'), shift(-1))  7.37 us
  transfers between devices with their start and end apart: 33, of which 15 were waited for; matrix products, arithmetic and copies ran while one was open for 4% of the time, Pallas kernels for 16%

profile of v8, /device:TPU:1, one launch (start us, length us, event | category | flops | bytes accessed | tf_op | source)
XLA Modules:
  0.0 169.0 jit_solution(11355872949659707581)
XLA Ops:
  0.6 4.7 %collective-permute-start = (bf16[192,512]{1,0:T(8,128)(2,1)}, bf16[192,512]{1,0:T(8,128)(2,1)S(1)}, u32[]{:S(2)}, u32[]{:S(2)}) collective-permute-start(bf16[192,512]{1,0:T(8,128)(2,1)} %param.5), channel_id=1, source_target_pairs={{0,0},{16,2},{8,4},{24,6},{2,8},{18,10},{10,12},{26,14},{4,16},{20... | collective-permute-start | bytes 589832 | tf_op jit(solution)/shard_map/ppermute | solution.py:353
  6.1 3.7 %all-to-all-start = ((bf16[192,4,128]{2,0,1:T(8,128)(2,1)}), bf16[192,4,128]{2,0,1:T(8,128)(2,1)S(1)}, u32[]{:S(2)}, u32[]{:S(2)}) async-start(bf16[192,4,128]{2,0,1:T(8,128)(2,1)} %copy_bitcast_fusion), calls=%async_computation | async-start | bytes 393216 | tf_op jit(solution)/shard_map/all_to_all | solution.py:355
  9.8 8.5 %collective-permute-done = bf16[192,512]{1,0:T(8,128)(2,1)S(1)} collective-permute-done((bf16[192,512]{1,0:T(8,128)(2,1)}, bf16[192,512]{1,0:T(8,128)(2,1)S(1)}, u32[]{:S(2)}, u32[]{:S(2)}) %collective-permute-start) | collective-permute-done | bytes 196640 | tf_op jit(solution)/shard_map/ppermute | solution.py:353
  26.1 4.0 %shard_map.92 = (bf16[3,384,128]{2,1,0:T(8,128)(2,1)S(1)}, bf16[3,384,128]{2,1,0:T(8,128)(2,1)S(1)}, bf16[3,384,128]{2,1,0:T(8,128)(2,1)S(1)}, bf16[3,384,128]{2,1,0:T(8,128)(2,1)S(1)}) custom-call(bf16[2,2,192,512]{3,2,1,0:T(8,128)(2,1)S(1)} %bitcast.28, bf16[3,1024,512]{2,1,0:T(8,128)(2,1)} %bitcast.7.w_ref.refs_4_), custom_call_target="tpu_custom_call" | custom-call | flops 1207959552 | bytes 5111808 | tf_op jit(solution)/shard_map/pallas_call | solution.py:376
  31.2 7.8 %collective-permute-start.5 = (bf16[1152,128]{1,0:T(8,128)(2,1)S(1)}, bf16[1152,128]{1,0:T(8,128)(2,1)S(1)}, u32[]{:S(2)}, u32[]{:S(2)}) collective-permute-start(bf16[1152,128]{1,0:T(8,128)(2,1)S(1)} %bitcast.31), channel_id=1, source_target_pairs={{0,8},{8,16},{1,9},{9,17},{2,10},{10,18},{3,11},{11,19},{4,12},{12... | collective-permute-start | bytes 884744 | tf_op jit(solution)/shard_map/ppermute | solution.py:304
  39.8 3.5 %collective-permute-start.8 = (bf16[1152,128]{1,0:T(8,128)(2,1)}, bf16[1152,128]{1,0:T(8,128)(2,1)}, u32[]{:S(2)}, u32[]{:S(2)}) collective-permute-start(bf16[1152,128]{1,0:T(8,128)(2,1)} %bitcast_add_fusion.2), channel_id=1, source_target_pairs={{0,24},{8,0},{16,8},{24,16},{1,25},{9,1},{17,9},{25,17},{2,26},{10... | collective-permute-start | bytes 884744 | tf_op jit(solution)/shard_map/ppermute | solution.py:307
  43.3 4.1 %shard_map.93 = (bf16[3,384,128]{2,1,0:T(8,128)(2,1)S(1)}, bf16[3,384,128]{2,1,0:T(8,128)(2,1)S(1)}, bf16[3,384,128]{2,1,0:T(8,128)(2,1)S(1)}, bf16[3,384,128]{2,1,0:T(8,128)(2,1)S(1)}) custom-call(bf16[2,2,192,512]{3,2,1,0:T(8,128)(2,1)S(1)} %collective-permute-done.4.x_ref.refs_1_, bf16[3,1024,512]{2,1,0:T(8,128)(2,1)} %bitcast.7.w_ref.refs_4_), custom_call_target="tpu_custom_call" | custom-call | flops 1207959552 | bytes 5111808 | tf_op jit(solution)/shard_map/pallas_call | solution.py:376
  48.2 5.8 %collective-permute-start.6 = (bf16[1152,128]{1,0:T(8,128)(2,1)S(1)}, bf16[1152,128]{1,0:T(8,128)(2,1)S(1)}, u32[]{:S(2)}, u32[]{:S(2)}) collective-permute-start(bf16[1152,128]{1,0:T(8,128)(2,1)S(1)} %bitcast_add_fusion.3), channel_id=1, source_target_pairs={{0,8},{8,16},{16,24},{24,0},{1,9},{9,17},{17,25},{25,1},{2,10},{10... | collective-permute-start | bytes 884744 | tf_op jit(solution)/shard_map/ppermute | solution.py:306
  54.0 4.3 %collective-permute-start.9 = (bf16[1152,128]{1,0:T(8,128)(2,1)S(1)}, bf16[1152,128]{1,0:T(8,128)(2,1)S(1)}, u32[]{:S(2)}, u32[]{:S(2)}) collective-permute-start(bf16[1152,128]{1,0:T(8,128)(2,1)S(1)} %bitcast.33), channel_id=1, source_target_pairs={{0,8},{8,16},{1,9},{9,17},{2,10},{10,18},{3,11},{11,19},{4,12},{12... | collective-permute-start | bytes 884744 | tf_op jit(solution)/shard_map/ppermute | solution.py:304
  60.1 5.6 %collective-permute-done.9 = bf16[1152,128]{1,0:T(8,128)(2,1)S(1)} collective-permute-done((bf16[1152,128]{1,0:T(8,128)(2,1)S(1)}, bf16[1152,128]{1,0:T(8,128)(2,1)S(1)}, u32[]{:S(2)}, u32[]{:S(2)}) %collective-permute-start.9) | collective-permute-done | bytes 294944 | tf_op jit(solution)/shard_map/ppermute | solution.py:304
  65.7 3.4 %collective-permute-start.10 = (bf16[1152,128]{1,0:T(8,128)(2,1)S(1)}, bf16[1152,128]{1,0:T(8,128)(2,1)S(1)}, u32[]{:S(2)}, u32[]{:S(2)}) collective-permute-start(bf16[1152,128]{1,0:T(8,128)(2,1)S(1)} %bitcast_add_fusion.1), channel_id=1, source_target_pairs={{0,8},{8,16},{16,24},{24,0},{1,9},{9,17},{17,25},{25,1},{2,10},{10... | collective-permute-start | bytes 884744 | tf_op jit(solution)/shard_map/ppermute | solution.py:306
  73.0 6.8 %collective-permute-done.10.refs_4_ = bf16[1152,128]{1,0:T(8,128)(2,1)S(1)} collective-permute-done((bf16[1152,128]{1,0:T(8,128)(2,1)S(1)}, bf16[1152,128]{1,0:T(8,128)(2,1)S(1)}, u32[]{:S(2)}, u32[]{:S(2)}) %collective-permute-start.10) | collective-permute-done | bytes 294944 | tf_op jit(solution)/shard_map/ppermute | solution.py:306
  80.4 5.4 %shard_map.95 = (bf16[1184,128]{1,0:T(8,128)(2,1)}, bf16[1152,128]{1,0:T(8,128)(2,1)}, bf16[192,128]{1,0:T(8,128)(2,1)}, bf16[192,128]{1,0:T(8,128)(2,1)}, bf16[...) custom-call(bf16[1152,128]{1,0:T(8,128)(2,1)} %bitcast.34, bf16[1152,128]{1,0:T(8,128)(2,1)} %copy-done.16, ...), custom_call_target="tpu_custom_call" | custom-call | flops 1207959552 | bytes 2752512 | tf_op jit(solution)/shard_map/pallas_call | solution.py:395
  85.9 5.6 %collective-permute-start.17 = (bf16[1152,128]{1,0:T(8,128)(2,1)}, bf16[1152,128]{1,0:T(8,128)(2,1)S(1)}, u32[]{:S(2)}, u32[]{:S(2)}) collective-permute-start(bf16[1152,128]{1,0:T(8,128)(2,1)} %get-tuple-element.59), channel_id=1, source_target_pairs={{0,26},{2,24},{4,30},{6,28},{8,2},{10,0},{12,6},{14,4},{16,10},{18... | collective-permute-start | bytes 884744 | tf_op jit(solution)/shard_map/ppermute | solution.py:322
  93.2 4.9 %collective-permute-done.17.far_after = bf16[1152,128]{1,0:T(8,128)(2,1)S(1)} collective-permute-done((bf16[1152,128]{1,0:T(8,128)(2,1)}, bf16[1152,128]{1,0:T(8,128)(2,1)S(1)}, u32[]{:S(2)}, u32[]{:S(2)}) %collective-permute-start.17) | collective-permute-done | bytes 294944 | tf_op jit(solution)/shard_map/ppermute | solution.py:322
  98.1 6.5 %collective-permute-done.14.near_after.refs_4_ = bf16[1184,128]{1,0:T(8,128)(2,1)S(1)} collective-permute-done((bf16[1184,128]{1,0:T(8,128)(2,1)}, bf16[1184,128]{1,0:T(8,128)(2,1)S(1)}, u32[]{:S(2)}, u32[]{:S(2)}) %collective-permute-start.14) | collective-permute-done | bytes 303136 | tf_op jit(solution)/shard_map/ppermute | solution.py:322
  105.9 8.0 %collective-permute-done.13.near_before.refs_3_ = bf16[1184,128]{1,0:T(8,128)(2,1)S(1)} collective-permute-done((bf16[1184,128]{1,0:T(8,128)(2,1)}, bf16[1184,128]{1,0:T(8,128)(2,1)S(1)}, u32[]{:S(2)}, u32[]{:S(2)}) %collective-permute-start.13) | collective-permute-done | bytes 303136 | tf_op jit(solution)/shard_map/ppermute | solution.py:321
  120.4 5.5 %shard_map.96 = (f32[2,384,512]{2,1,0:T(8,128)S(1)}, bf16[3,1152,128]{2,1,0:T(8,128)(2,1)S(1)}) custom-call(bf16[1184,128]{1,0:T(8,128)(2,1)S(1)} %copy-done.5, bf16[1184,128]{1,0:T(8,128)(2,1)S(1)} %collective-permute-done.13.near_before.refs_3_, bf16[1184,128]{1,0:T(8,128)(2,1)S(1)} %collective-permute-done.14.near_after.refs_4_, ...), custom_call_target="tpu_custom_call" | custom-call | flops 2415919104 | bytes 10223616 | tf_op jit(solution)/shard_map/pallas_call | solution.py:420
  127.1 4.5 %collective-permute-done.22.refs_3_ = bf16[1152,128]{1,0:T(8,128)(2,1)S(1)} collective-permute-done((bf16[1152,128]{1,0:T(8,128)(2,1)S(1)}, bf16[1152,128]{1,0:T(8,128)(2,1)S(1)}, u32[]{:S(2)}, u32[]{:S(2)}) %collective-permute-start.22) | collective-permute-done | bytes 294944 | tf_op jit(solution)/shard_map/ppermute | solution.py:325
  133.2 4.6 %shard_map.97 = (bf16[1184,128]{1,0:T(8,128)(2,1)}, bf16[1152,128]{1,0:T(8,128)(2,1)}, bf16[192,512]{1,0:T(8,128)(2,1)}, bf16[192,512]{1,0:T(8,128)(2,1)}, bf16[...) custom-call(f32[2,384,512]{2,1,0:T(8,128)} %copy-done.1, bf16[1184,128]{1,0:T(8,128)(2,1)} %copy-done.11, ...), custom_call_target="tpu_custom_call" | custom-call | flops 603979776 | bytes 2555904 | tf_op jit(solution)/shard_map/pallas_call | solution.py:429
  141.9 3.1 %collective-permute-done.23 = bf16[192,512]{1,0:T(8,128)(2,1)S(1)} collective-permute-done((bf16[192,512]{1,0:T(8,128)(2,1)}, bf16[192,512]{1,0:T(8,128)(2,1)S(1)}, u32[]{:S(2)}, u32[]{:S(2)}) %collective-permute-start.23) | collective-permute-done | bytes 196640 | tf_op jit(solution)/shard_map/ppermute | solution.py:448
  145.9 4.2 %collective-permute-done.25 = bf16[192,512]{1,0:T(8,128)(2,1)S(1)} collective-permute-done((bf16[192,512]{1,0:T(8,128)(2,1)}, bf16[192,512]{1,0:T(8,128)(2,1)S(1)}, u32[]{:S(2)}, u32[]{:S(2)}) %collective-permute-start.25) | collective-permute-done | bytes 196640 | tf_op jit(solution)/shard_map/ppermute | solution.py:448
  153.1 6.8 %collective-permute-start.31 = (bf16[192,512]{1,0:T(8,128)(2,1)S(1)}, bf16[192,512]{1,0:T(8,128)(2,1)S(1)}, u32[]{:S(2)}, u32[]{:S(2)}) collective-permute-start(bf16[192,512]{1,0:T(8,128)(2,1)S(1)} %add_convert_fusion), channel_id=1, source_target_pairs={{0,0},{2,16},{4,8},{6,24},{8,2},{10,18},{12,10},{14,26},{16,4},{18... | collective-permute-start | bytes 589832 | tf_op jit(solution)/shard_map/ppermute | solution.py:453
  159.9 7.1 %shard_map.98 = (f32[3,1024,512]{2,1,0:T(8,128)}, bf16[192,512]{1,0:T(8,128)(2,1)}, f32[32,128]{1,0:T(8,128)}, f32[9,512]{1,0:T(8,128)}) custom-call(bf16[2,2,192,512]{3,2,1,0:T(8,128)(2,1)} %bitcast.29, bf16[2,2,192,512]{3,2,1,0:T(8,128)(2,1)} %copy-done.4, bf16[1184,128]{1,0:T(8,128)(2,1)} %get-tuple-element.58.near.refs_2_, bf16[1184,128]{1,0:T(8,128)(2,1)} %copy-done.7, ...), custom_call_target="tpu_custom_call" | custom-call | flops 2415919104 | bytes 10223616 | tf_op jit(solution)/shard_map/pallas_call | solution.py:455
  (115 shorter events, 39.6 us)
Async XLA Ops:
  0.6 17.7 %collective-permute-start = (bf16[192,512]{1,0:T(8,128)(2,1)}, bf16[192,512]{1,0:T(8,128)(2,1)S(1)}, u32[]{:S(2)}, u32[]{:S(2)}) collective-permute-start(bf16[192,512]{1,0:T(8,128)(2,1)} %param.5), channel_id=1, source_target_pairs={{0,0},{16,2},{8,4},{24,6},{2,8},{18,10},{10,12},{26,14},{4,16},{20... | collective-permute-start | bytes 589832 | tf_op jit(solution)/shard_map/ppermute | solution.py:353
  6.1 14.9 %all-to-all-start = ((bf16[192,4,128]{2,0,1:T(8,128)(2,1)}), bf16[192,4,128]{2,0,1:T(8,128)(2,1)S(1)}, u32[]{:S(2)}, u32[]{:S(2)}) async-start(bf16[192,4,128]{2,0,1:T(8,128)(2,1)} %copy_bitcast_fusion), calls=%async_computation | async-start | bytes 393216 | tf_op jit(solution)/shard_map/all_to_all | solution.py:355
  26.0 17.3 %collective-permute-start.4 = (bf16[2,2,192,512]{3,2,1,0:T(8,128)(2,1)S(1)}, bf16[2,2,192,512]{3,2,1,0:T(8,128)(2,1)S(1)}, u32[]{:S(2)}, u32[]{:S(2)}) collective-permute-start(bf16[2,2,192,512]{3,2,1,0:T(8,128)(2,1)S(1)} %bitcast.27), channel_id=1, source_target_pairs={{0,2},{2,0},{4,6},{6,4},{1,3},{3,1},{5,7},{7,5},{8,10},{10,8},{12,... | collective-permute-start | bytes 2359304 | tf_op jit(solution)/shard_map/ppermute | solution.py:358
  30.8 88.6 %collective-permute-start.18 = (bf16[3,1024,512]{2,1,0:T(8,128)(2,1)}, bf16[3,1024,512]{2,1,0:T(8,128)(2,1)}, u32[]{:S(2)}, u32[]{:S(2)}) collective-permute-start(bf16[3,1024,512]{2,1,0:T(8,128)(2,1)} %bitcast.7.w_ref.refs_4_), channel_id=1, source_target_pairs={{0,2},{2,0},{4,6},{6,4},{1,3},{3,1},{5,7},{7,5},{8,10},{10,8},{12,... | collective-permute-start | bytes 9437192 | tf_op jit(solution)/shard_map/ppermute | solution.py:419
  31.2 17.0 %collective-permute-start.5 = (bf16[1152,128]{1,0:T(8,128)(2,1)S(1)}, bf16[1152,128]{1,0:T(8,128)(2,1)S(1)}, u32[]{:S(2)}, u32[]{:S(2)}) collective-permute-start(bf16[1152,128]{1,0:T(8,128)(2,1)S(1)} %bitcast.31), channel_id=1, source_target_pairs={{0,8},{8,16},{1,9},{9,17},{2,10},{10,18},{3,11},{11,19},{4,12},{12... | collective-permute-start | bytes 884744 | tf_op jit(solution)/shard_map/ppermute | solution.py:304
  39.8 33.1 %collective-permute-start.8 = (bf16[1152,128]{1,0:T(8,128)(2,1)}, bf16[1152,128]{1,0:T(8,128)(2,1)}, u32[]{:S(2)}, u32[]{:S(2)}) collective-permute-start(bf16[1152,128]{1,0:T(8,128)(2,1)} %bitcast_add_fusion.2), channel_id=1, source_target_pairs={{0,24},{8,0},{16,8},{24,16},{1,25},{9,1},{17,9},{25,17},{2,26},{10... | collective-permute-start | bytes 884744 | tf_op jit(solution)/shard_map/ppermute | solution.py:307
  47.5 10.8 %collective-permute-start.11 = (bf16[1152,128]{1,0:T(8,128)(2,1)S(1)}, bf16[1152,128]{1,0:T(8,128)(2,1)S(1)}, u32[]{:S(2)}, u32[]{:S(2)}) collective-permute-start(bf16[1152,128]{1,0:T(8,128)(2,1)S(1)} %bitcast.32), channel_id=1, source_target_pairs={{16,8},{24,16},{17,9},{25,17},{18,10},{26,18},{19,11},{27,19},{20,... | collective-permute-start | bytes 884744 | tf_op jit(solution)/shard_map/ppermute | solution.py:305
  48.2 24.7 %collective-permute-start.6 = (bf16[1152,128]{1,0:T(8,128)(2,1)S(1)}, bf16[1152,128]{1,0:T(8,128)(2,1)S(1)}, u32[]{:S(2)}, u32[]{:S(2)}) collective-permute-start(bf16[1152,128]{1,0:T(8,128)(2,1)S(1)} %bitcast_add_fusion.3), channel_id=1, source_target_pairs={{0,8},{8,16},{16,24},{24,0},{1,9},{9,17},{17,25},{25,1},{2,10},{10... | collective-permute-start | bytes 884744 | tf_op jit(solution)/shard_map/ppermute | solution.py:306
  54.0 11.7 %collective-permute-start.9 = (bf16[1152,128]{1,0:T(8,128)(2,1)S(1)}, bf16[1152,128]{1,0:T(8,128)(2,1)S(1)}, u32[]{:S(2)}, u32[]{:S(2)}) collective-permute-start(bf16[1152,128]{1,0:T(8,128)(2,1)S(1)} %bitcast.33), channel_id=1, source_target_pairs={{0,8},{8,16},{1,9},{9,17},{2,10},{10,18},{3,11},{11,19},{4,12},{12... | collective-permute-start | bytes 884744 | tf_op jit(solution)/shard_map/ppermute | solution.py:304
  58.3 14.6 %collective-permute-start.12 = (bf16[1152,128]{1,0:T(8,128)(2,1)S(1)}, bf16[1152,128]{1,0:T(8,128)(2,1)S(1)}, u32[]{:S(2)}, u32[]{:S(2)}) collective-permute-start(bf16[1152,128]{1,0:T(8,128)(2,1)S(1)} %bitcast_add_fusion), channel_id=1, source_target_pairs={{0,24},{8,0},{16,8},{24,16},{1,25},{9,1},{17,9},{25,17},{2,26},{10... | collective-permute-start | bytes 884744 | tf_op jit(solution)/shard_map/ppermute | solution.py:307
  65.7 14.0 %collective-permute-start.10 = (bf16[1152,128]{1,0:T(8,128)(2,1)S(1)}, bf16[1152,128]{1,0:T(8,128)(2,1)S(1)}, u32[]{:S(2)}, u32[]{:S(2)}) collective-permute-start(bf16[1152,128]{1,0:T(8,128)(2,1)S(1)} %bitcast_add_fusion.1), channel_id=1, source_target_pairs={{0,8},{8,16},{16,24},{24,0},{1,9},{9,17},{17,25},{25,1},{2,10},{10... | collective-permute-start | bytes 884744 | tf_op jit(solution)/shard_map/ppermute | solution.py:306
  85.9 12.2 %collective-permute-start.17 = (bf16[1152,128]{1,0:T(8,128)(2,1)}, bf16[1152,128]{1,0:T(8,128)(2,1)S(1)}, u32[]{:S(2)}, u32[]{:S(2)}) collective-permute-start(bf16[1152,128]{1,0:T(8,128)(2,1)} %get-tuple-element.59), channel_id=1, source_target_pairs={{0,26},{2,24},{4,30},{6,28},{8,2},{10,0},{12,6},{14,4},{16,10},{18... | collective-permute-start | bytes 884744 | tf_op jit(solution)/shard_map/ppermute | solution.py:322
  91.5 13.1 %collective-permute-start.14 = (bf16[1184,128]{1,0:T(8,128)(2,1)}, bf16[1184,128]{1,0:T(8,128)(2,1)S(1)}, u32[]{:S(2)}, u32[]{:S(2)}) collective-permute-start(bf16[1184,128]{1,0:T(8,128)(2,1)} %get-tuple-element.58.near.refs_2_), channel_id=1, source_target_pairs={{0,24},{2,26},{4,28},{6,30},{8,0},{10,2},{12,4},{14,6},{16,8},{18,... | collective-permute-start | bytes 909320 | tf_op jit(solution)/shard_map/ppermute | solution.py:322
  93.2 20.7 %collective-permute-start.13 = (bf16[1184,128]{1,0:T(8,128)(2,1)}, bf16[1184,128]{1,0:T(8,128)(2,1)S(1)}, u32[]{:S(2)}, u32[]{:S(2)}) collective-permute-start(bf16[1184,128]{1,0:T(8,128)(2,1)} %get-tuple-element.58.near.refs_2_), channel_id=1, source_target_pairs={{0,8},{2,10},{4,12},{6,14},{8,16},{10,18},{12,20},{14,22},{16,24},... | collective-permute-start | bytes 909320 | tf_op jit(solution)/shard_map/ppermute | solution.py:321
  93.2 24.2 %collective-permute-start.16 = (bf16[1152,128]{1,0:T(8,128)(2,1)}, bf16[1152,128]{1,0:T(8,128)(2,1)S(1)}, u32[]{:S(2)}, u32[]{:S(2)}) collective-permute-start(bf16[1152,128]{1,0:T(8,128)(2,1)} %get-tuple-element.59), channel_id=1, source_target_pairs={{0,10},{2,8},{4,14},{6,12},{8,18},{10,16},{12,22},{14,20},{16,26},... | collective-permute-start | bytes 884744 | tf_op jit(solution)/shard_map/ppermute | solution.py:321
  98.1 20.6 %collective-permute-start.15 = (bf16[1152,128]{1,0:T(8,128)(2,1)}, bf16[1152,128]{1,0:T(8,128)(2,1)S(1)}, u32[]{:S(2)}, u32[]{:S(2)}) collective-permute-start(bf16[1152,128]{1,0:T(8,128)(2,1)} %get-tuple-element.59), channel_id=1, source_target_pairs={{0,2},{2,0},{4,6},{6,4},{8,10},{10,8},{12,14},{14,12},{16,18},{18,... | collective-permute-start | bytes 884744 | tf_op jit(solution)/shard_map/ppermute | solution.py:323
  104.6 27.0 %collective-permute-start.20 = (bf16[1184,128]{1,0:T(8,128)(2,1)S(1)}, bf16[1184,128]{1,0:T(8,128)(2,1)S(1)}, u32[]{:S(2)}, u32[]{:S(2)}) collective-permute-start(bf16[1184,128]{1,0:T(8,128)(2,1)S(1)} %collective-permute-done.14.near_after.refs_4_), channel_id=1, source_target_pairs={{8,0},{16,8},{9,1},{17,9},{10,2},{18,10},{11,3},{19,11},{12,4},{20... | collective-permute-start | bytes 909320 | tf_op jit(solution)/shard_map/ppermute | solution.py:325
  113.9 17.7 %collective-permute-start.19 = (bf16[1184,128]{1,0:T(8,128)(2,1)S(1)}, bf16[1184,128]{1,0:T(8,128)(2,1)S(1)}, u32[]{:S(2)}, u32[]{:S(2)}) collective-permute-start(bf16[1184,128]{1,0:T(8,128)(2,1)S(1)} %collective-permute-done.13.near_before.refs_3_), channel_id=1, source_target_pairs={{8,16},{16,24},{9,17},{17,25},{10,18},{18,26},{11,19},{19,27},{12,... | collective-permute-start | bytes 909320 | tf_op jit(solution)/shard_map/ppermute | solution.py:324
  117.4 14.2 %collective-permute-start.22 = (bf16[1152,128]{1,0:T(8,128)(2,1)S(1)}, bf16[1152,128]{1,0:T(8,128)(2,1)S(1)}, u32[]{:S(2)}, u32[]{:S(2)}) collective-permute-start(bf16[1152,128]{1,0:T(8,128)(2,1)S(1)} %collective-permute-done.17.far_after), channel_id=1, source_target_pairs={{8,0},{16,8},{9,1},{17,9},{10,2},{18,10},{11,3},{19,11},{12,4},{20... | collective-permute-start | bytes 884744 | tf_op jit(solution)/shard_map/ppermute | solution.py:325
  118.7 12.9 %collective-permute-start.21 = (bf16[1152,128]{1,0:T(8,128)(2,1)S(1)}, bf16[1152,128]{1,0:T(8,128)(2,1)S(1)}, u32[]{:S(2)}, u32[]{:S(2)}) collective-permute-start(bf16[1152,128]{1,0:T(8,128)(2,1)S(1)} %collective-permute-done.16.far_before), channel_id=1, source_target_pairs={{8,16},{16,24},{9,17},{17,25},{10,18},{18,26},{11,19},{19,27},{12,... | collective-permute-start | bytes 884744 | tf_op jit(solution)/shard_map/ppermute | solution.py:324
  137.8 15.3 %collective-permute-start.26 = (bf16[3,1152,128]{2,1,0:T(8,128)(2,1)S(1)}, bf16[3,1152,128]{2,1,0:T(8,128)(2,1)S(1)}, u32[]{:S(2)}, u32[]{:S(2)}) collective-permute-start(bf16[3,1152,128]{2,1,0:T(8,128)(2,1)S(1)} %get-tuple-element.68), channel_id=1, source_target_pairs={{0,2},{2,0},{4,6},{6,4},{1,3},{3,1},{5,7},{7,5},{8,10},{10,8},{12,... | collective-permute-start | bytes 2654216 | tf_op jit(solution)/shard_map/ppermute | solution.py:446
  139.8 10.3 %collective-permute-start.25 = (bf16[192,512]{1,0:T(8,128)(2,1)}, bf16[192,512]{1,0:T(8,128)(2,1)S(1)}, u32[]{:S(2)}, u32[]{:S(2)}) collective-permute-start(bf16[192,512]{1,0:T(8,128)(2,1)} %get-tuple-element.65), channel_id=1, source_target_pairs={{5,0},{4,1},{7,2},{6,3},{1,4},{0,5},{3,6},{2,7},{13,8},{12,9},{15,... | collective-permute-start | bytes 589832 | tf_op jit(solution)/shard_map/ppermute | solution.py:448
  141.0 12.1 %collective-permute-start.27 = (bf16[1152,128]{1,0:T(8,128)(2,1)}, bf16[1152,128]{1,0:T(8,128)(2,1)S(1)}, u32[]{:S(2)}, u32[]{:S(2)}) collective-permute-start(bf16[1152,128]{1,0:T(8,128)(2,1)} %get-tuple-element.69), channel_id=1, source_target_pairs={{0,2},{2,0},{4,6},{6,4},{1,3},{3,1},{5,7},{7,5},{8,10},{10,8},{12,... | collective-permute-start | bytes 884744 | tf_op jit(solution)/shard_map/ppermute | solution.py:446
  153.1 15.3 %collective-permute-start.31 = (bf16[192,512]{1,0:T(8,128)(2,1)S(1)}, bf16[192,512]{1,0:T(8,128)(2,1)S(1)}, u32[]{:S(2)}, u32[]{:S(2)}) collective-permute-start(bf16[192,512]{1,0:T(8,128)(2,1)S(1)} %add_convert_fusion), channel_id=1, source_target_pairs={{0,0},{2,16},{4,8},{6,24},{8,2},{10,18},{12,10},{14,26},{16,4},{18... | collective-permute-start | bytes 589832 | tf_op jit(solution)/shard_map/ppermute | solution.py:453
  (34 other events, 268.0 us)

commit v9 on v8

--- a/solution.py
+++ b/solution.py
@@ -54,23 +54,31 @@
     return lax.rem(value + 2 * size, size)
 
 
-def project_body(x_ref, w_ref, *refs):
+def split_body(all_ref, *out_refs):
+    width = out_refs[0].shape[1]
+    for ahead, out_ref in enumerate(out_refs):
+        at = wrapped(lax.axis_index("dp") + ahead, len(out_refs)) * width
+        out_ref[...] = all_ref[:, pl.ds(pl.multiple_of(at, width), width)]
+
+
+def project_body(x_ref, w_ref, partner_w_ref, *refs):
     *out_refs, held = refs
+    ndp, _, width = held.shape
     z, col = lax.axis_index("dp"), lax.axis_index("col")
     nblocks, ncol, rows, depth = x_ref.shape
-    width = held.shape[2]
-    total = jnp.zeros((nblocks * rows, w_ref.shape[2]), F32)
-    for dx in range(ncol):
-        start = pl.multiple_of(wrapped(col - dx, ncol) * depth, depth)
-        total += jnp.dot(
-            x_ref[:, dx].reshape(nblocks * rows, depth),
-            w_ref[0, pl.ds(start, depth), :],
-            preferred_element_type=F32,
-        )
-    for owner in range(len(out_refs)):
-        held[owner] = total[:, owner * width : (owner + 1) * width].astype(BF16)
-    for ahead, out_ref in enumerate(out_refs):
-        out_ref[0] = held[wrapped(z + ahead, len(out_refs))]
+    for weights, targets in ((w_ref, out_refs[:ndp]), (partner_w_ref, out_refs[ndp:])):
+        total = jnp.zeros((nblocks * rows, w_ref.shape[2]), F32)
+        for dx in range(ncol):
+            start = pl.multiple_of(wrapped(col - dx, ncol) * depth, depth)
+            total += jnp.dot(
+                x_ref[:, dx].reshape(nblocks * rows, depth),
+                weights[0, pl.ds(start, depth), :],
+                preferred_element_type=F32,
+            )
+        for owner in range(ndp):
+            held[owner] = total[:, owner * width : (owner + 1) * width].astype(BF16)
+        for ahead, out_ref in enumerate(targets):
+            out_ref[0] = held[wrapped(z + ahead, ndp)]
 
 
 def first_grad_body(near, near_before, near_after, far, far_before, far_after, w_ref, partner_w_ref, out_ref, far_ref, held):
@@ -99,10 +107,10 @@
             out_ref[dx] = total
 
 
-def second_grad_body(ndp, part_ref, *refs):
+def second_grad_body(ndp, part_ref, far_three_ref, *refs):
     arrived, weights, refs = (refs[:2], refs[2:4]), refs[4:6], refs[6:]
-    (near_ref, far_ref), refs = refs[:2], refs[2:]
-    *out_refs, held_w, held_part, sems = refs
+    (near_ref, far_all_ref), refs = refs[:2], refs[2:]
+    *out_refs, held_w, held_part, far_ref, sems = refs
     ncol, tokens, depth = held_part.shape
     rows = out_refs[0].shape[0]
     width = near_ref.shape[1]
@@ -114,6 +122,8 @@
     copies.append(pltpu.make_async_copy(part_ref, held_part, sems.at[2]))
     for copy in copies:
         copy.start()
+    handed_on = pltpu.make_async_copy(far_three_ref, far_all_ref.at[pl.ds(0, ndp - 1)], sems.at[5])
+    handed_on.start()
     for k, (pair, target) in enumerate(zip(arrived, (near_ref, far_ref))):
         for source, here in zip(pair, (z >= ndp // 2, z < ndp // 2)):
 
@@ -123,6 +133,8 @@
                 copy.start()
                 copy.wait()
 
+    last_on = pltpu.make_async_copy(far_ref, far_all_ref.at[ndp - 1], sems.at[6])
+    last_on.start()
     for copy in copies:
         copy.wait()
     left = jnp.concatenate(
@@ -136,16 +148,12 @@
         )
         for block in range(tokens // rows):
             out_refs[block * ncol + dx][...] = total[block * rows : (block + 1) * rows].astype(BF16)
+    handed_on.wait()
+    last_on.wait()
 
 
 def weight_grad_body(scale, *refs):
-    (x0_ref, x1_ref), near_refs, (far_ref, far_last_ref), mixed_refs, refs = (
-        refs[:2],
-        refs[2:6],
-        refs[6:8],
-        refs[8:12],
-        refs[12:],
-    )
+    (x0_ref, x1_ref), near_refs, far_ref, mixed_refs, refs = refs[:2], refs[2:6], refs[6], refs[7:11], refs[11:]
     out_ref, mixed_ref, long_ref, short_ref, held, held_mixed = refs
     nblocks, ncol, rows, depth = x0_ref.shape
     _, ndp, _, width = held.shape
@@ -159,7 +167,7 @@
         for k, ahead in enumerate((0, -1, 1, 2)):
             owner = wrapped(z + ahead, ndp)
             held[0, owner] = near_refs[k][...]
-            held[1, owner, : 3 * tokens] = far_ref[k] if k < 3 else far_last_ref[...]
+            held[1, owner, : 3 * tokens] = far_ref[k]
         for back in range(ndp):
             held_mixed[wrapped(z - back, ndp)] = mixed_refs[back][...]
         for owner in range(ndp):
@@ -167,7 +175,9 @@
             mixed_ref[:, lanes] = held_mixed[owner]
             small = held[0, owner, 3 * tokens :].astype(F32)
             long_ref[owner * groups : (owner + 1) * groups] = small[:groups]
-            short_ref[:, lanes] = small[groups : groups + short_ref.shape[0]]
+            nshort, three, _ = short_ref.shape
+            for j in range(nshort):
+                short_ref[j, :, lanes] = small[groups + three * j : groups + three * (j + 1)]
 
     at = pl.ds(pl.multiple_of(i * tokens, 16), tokens)
     gm = jnp.concatenate(
@@ -196,8 +206,14 @@
 
 def middle_body(scale, nshort, nrow, *refs):
     sums, refs = (refs[:3], refs[3:6]), refs[6:]
-    sf_ref, causal_ref, anti_ref, go_ref, near_ref, other_ref, *mixed_refs, m_ref, gm_ref, mixed_ref = refs
+    (sf_ref, causal_ref, anti_ref), refs = refs[:3], refs[3:]
+    *refs, m_ref, gm_ref, mixed_ref, go_ref = refs
+    ndp = len(refs) // 2 - 1
+    go_refs, (near_ref, other_ref), mixed_refs = refs[:ndp], refs[ndp : ndp + 2], refs[ndp + 2 :]
     tokens, width = go_ref.shape
+    for behind, piece in enumerate(go_refs):
+        at = wrapped(lax.axis_index("dp") - behind, ndp) * (tokens // ndp)
+        go_ref[pl.ds(pl.multiple_of(at, 16), tokens // ndp)] = piece[...]
     row = lax.axis_index("row")
     nblocks = nrow // 2
     rows = tokens // nrow
@@ -247,7 +263,6 @@
     conv = filtered(causal_ref, p_pairs)
     upstream = go_ref[...].astype(F32)
     mixed_ref[...] = (feats[0] * conv).astype(BF16)
-    ndp = len(mixed_refs)
     for ahead, out_ref in enumerate(mixed_refs):
         at = pl.multiple_of(wrapped(lax.axis_index("dp") + ahead, ndp) * (tokens // ndp), 16)
         out_ref[...] = mixed_ref[pl.ds(at, tokens // ndp)]
@@ -299,28 +314,35 @@
     near_ref[3 * tokens // 2 :] = small.astype(BF16)
 
 
-def sum_over_line(own, right, far, left):
+def shift(count, across):
+    ndp, nrow = lax.axis_size("dp"), lax.axis_size("row")
+    return [
+        (a * nrow + r, (a + count) % ndp * nrow + (r + 1 - 2 * (r % 2) if across else r))
+        for a in range(ndp)
+        for r in range(nrow)
+    ]
+
+
+def first_hop(far):
     ndp = lax.axis_size("dp")
-    from_left = lax.ppermute(far, "dp", [(a, a + 1) for a in range(ndp // 2)])
-    from_right = lax.ppermute(far, "dp", [(a, a - 1) for a in range(ndp // 2, ndp)])
-    rightward = lax.ppermute(right + from_left, "dp", [(a, (a + 1) % ndp) for a in range(ndp)])
-    leftward = lax.ppermute(left + from_right, "dp", [(a, (a - 1) % ndp) for a in range(ndp)])
-    return own, rightward, leftward
+    return (
+        lax.ppermute(far, "dp", [(a, a + 1) for a in range(ndp // 2)]),
+        lax.ppermute(far, "dp", [(a, a - 1) for a in range(ndp // 2, ndp)]),
+    )
+
+
+def second_hop(own, right, left, from_left, from_right, across):
+    rightward = lax.ppermute(right + from_left, ("dp", "row"), shift(1, across))
+    leftward = lax.ppermute(left + from_right, ("dp", "row"), shift(-1, across))
+    here = lax.ppermute(own, ("dp", "row"), shift(0, across)) if across else own
+    return here, rightward, leftward
 
 
 def gather_over_line(own, across):
-    ndp, nrow = lax.axis_size("dp"), lax.axis_size("row")
-
-    def shift(count):
-        return [
-            (a * nrow + r, (a + count) % ndp * nrow + (r + 1 - 2 * (r % 2) if across else r))
-            for a in range(ndp)
-            for r in range(nrow)
-        ]
-
-    before = lax.ppermute(own, ("dp", "row"), shift(1))
-    after = lax.ppermute(own, ("dp", "row"), shift(-1))
-    here = lax.ppermute(own, ("dp", "row"), shift(0)) if across else own
+    ndp = lax.axis_size("dp")
+    before = lax.ppermute(own, ("dp", "row"), shift(1, across))
+    after = lax.ppermute(own, ("dp", "row"), shift(-1, across))
+    here = lax.ppermute(own, ("dp", "row"), shift(0, across)) if across else own
     far_before = lax.ppermute(before, "dp", [(a - 1, a) for a in range(ndp // 2, ndp)])
     far_after = lax.ppermute(after, "dp", [(a + 1, a) for a in range(ndp // 2)])
     return here, before, after, far_before, far_after
@@ -351,11 +373,16 @@
 
     w = jnp.transpose(in_weight, (1, 0, 2))
     moved = lax.ppermute(tokens, ("dp", "row"), swap)
+    partner_w = lax.ppermute(w, "row", partner)
+    upstream = [*kernel_call(split_body, [shaped((rows, width), BF16)] * ndp)(grad_out)]
+    turn = [[(a, (a + ahead) % ndp) for a in range(ndp)] for ahead in range(ndp)]
+    upstream[2] = lax.ppermute(upstream[2], "dp", turn[2])
+    moved, partner_w, upstream = lax.optimization_barrier((moved, partner_w, upstream))
     near = [moved] + [lax.ppermute(moved, ("row", "col"), offset(*p)) for p in places[1:]]
-    upstream = lax.all_to_all(grad_out, "dp", split_axis=1, concat_axis=0, tiled=True)
-    upstream, *near = lax.optimization_barrier((upstream, *near))
+    for ahead in (1, 3):
+        upstream[ahead] = lax.ppermute(upstream[ahead], "dp", turn[ahead])
+    upstream[1::2], near[1:] = lax.optimization_barrier((upstream[1::2], near[1:]))
     x0 = jnp.stack(near).reshape(nblocks, ncol, rows, dcol)
-    x1 = lax.ppermute(x0, "row", partner)
 
     sf = lax.dynamic_slice_in_dim(short_filter, z * width, width, 2).reshape(3 * nshort, width)
     lf = lax.dynamic_slice_in_dim(long_filter, z * groups, groups, 0).astype(F32)
@@ -371,22 +398,26 @@
 
     mm_flops = seq * drow * 3 * local
     mm_bytes = seq * drow + 6 * drow * local + 3 * seq * local
+    parts = kernel_call(
+        project_body,
+        [shaped((3, chunk, width), BF16)] * (2 * ndp),
+        grid=(3,),
+        in_specs=[pl.BlockSpec((nblocks, ncol, rows, dcol), lambda i: (0, 0, 0, 0))]
+        + [pl.BlockSpec((1, drow, local), lambda i: (i, 0, 0))] * 2,
+        out_specs=[pl.BlockSpec((1, chunk, width), lambda i: (i, 0, 0))] * (2 * ndp),
+        scratch=[pltpu.VMEM((ndp, chunk, width), BF16)],
+        flops=2 * mm_flops,
+        nbytes=2 * mm_bytes,
+    )(x0, w, partner_w)
+    parts = [p.reshape(3 * chunk, width) for p in parts]
+    x1 = lax.ppermute(x0, "row", partner)
     sums = []
-    for x in (x0, x1):
-        parts = kernel_call(
-            project_body,
-            [shaped((3, chunk, width), BF16)] * ndp,
-            grid=(3,),
-            in_specs=[
-                pl.BlockSpec((nblocks, ncol, rows, dcol), lambda i: (0, 0, 0, 0)),
-                pl.BlockSpec((1, drow, local), lambda i: (i, 0, 0)),
-            ],
-            out_specs=[pl.BlockSpec((1, chunk, width), lambda i: (i, 0, 0))] * ndp,
-            scratch=[pltpu.VMEM((ndp, chunk, width), BF16)],
-            flops=mm_flops,
-            nbytes=mm_bytes,
-        )(x, w)
-        sums += sum_over_line(*(p.reshape(3 * chunk, width) for p in parts))
+    for across in (False, True):
+        own, right, far, left = parts[ndp * across :][:ndp]
+        from_left, from_right = first_hop(far)
+        if not across:
+            x1, from_left = lax.optimization_barrier((x1, from_left))
+        sums += second_hop(own, right, left, from_left, from_right, across)
 
     extra = -(-(groups + 3 * nshort) // 16) * 16
     half = pl.BlockSpec((groups, ntaps, 2 * ntaps), lambda i: (0, 0, 0))
@@ -398,25 +429,24 @@
         + [shaped((rows, width), BF16)] * ndp,
         grid=(1,),
         in_specs=[whole(3 * chunk, width)] * 6
-        + [whole(3 * nshort, width), half, other, whole(seq, width)],
+        + [whole(3 * nshort, width), half, other]
+        + [whole(rows, width)] * ndp,
         out_specs=[whole(3 * chunk + extra, width), whole(3 * chunk, width)] + [whole(rows, width)] * ndp,
         scratch=[
             pltpu.VMEM((3 * seq, width), F32),
             pltpu.VMEM((3 * seq, width), BF16),
             pltpu.VMEM((seq, width), BF16),
+            pltpu.VMEM((seq, width), BF16),
         ],
         flops=3 * 2 * groups * ntaps * 2 * ntaps * width * (seq // ntaps),
         nbytes=2 * width * seq * 14,
         vmem=MOST_VMEM_BYTES,
-    )(*sums, sf, bands, bands, upstream)
-    mixed = [mixed[0]] + [
-        lax.ppermute(part, "dp", [(a, (a + ahead) % ndp) for a in range(ndp)])
-        for ahead, part in enumerate(mixed)
-        if ahead
-    ]
+    )(*sums, sf, bands, bands, *upstream)
+    for ahead in range(1, ndp):
+        mixed[ahead] = lax.ppermute(mixed[ahead], "dp", turn[ahead])
     *near, near_far_before, near_far_after = gather_over_line(grad_near, False)
     *far, far_far_before, far_far_after = gather_over_line(grad_other, True)
-    partner_w = lax.ppermute(w, "row", partner)
+    mixed[2:], near_far_before = lax.optimization_barrier((mixed[2:], near_far_before))
     part, far_three = kernel_call(
         first_grad_body,
         [shaped((ncol, chunk, dcol), F32), shaped((3, 3 * chunk, width), BF16)],
@@ -426,30 +456,30 @@
     )(*near, *far, w, partner_w)
     everywhere = pl.BlockSpec(memory_space=pl.ANY)
     in_vmem = pl.BlockSpec(memory_space=pltpu.VMEM)
-    near_last, far_last, *blocks = kernel_call(
+    near_last, far_all, *blocks = kernel_call(
         functools.partial(second_grad_body, ndp),
-        [shaped(grad_near.shape, BF16), shaped(grad_other.shape, BF16)]
+        [shaped(grad_near.shape, BF16), shaped((ndp, *grad_other.shape), BF16)]
         + [shaped((rows, dcol), BF16)] * len(places),
         grid=(),
-        in_specs=[everywhere] * 7,
-        out_specs=[in_vmem] * (2 + len(places)),
+        in_specs=[everywhere] * 8,
+        out_specs=[in_vmem, everywhere] + [in_vmem] * len(places),
         scratch=[
             pltpu.VMEM((2, 3, drow, width), BF16),
             pltpu.VMEM((ncol, chunk, dcol), F32),
-            pltpu.SemaphoreType.DMA((5,)),
+            pltpu.VMEM(grad_other.shape, BF16),
+            pltpu.SemaphoreType.DMA((7,)),
         ],
         flops=mm_flops // 2,
         nbytes=mm_bytes // 2,
         vmem=MOST_VMEM_BYTES,
-    )(part, near_far_before, near_far_after, far_far_before, far_far_after, w, partner_w)
-    far_three, far_last = lax.optimization_barrier((far_three, far_last))
-    far_three, far_last = (lax.ppermute(part, "row", partner) for part in (far_three, far_last))
+    )(part, far_three, near_far_before, near_far_after, far_far_before, far_far_after, w, partner_w)
     arrivals = [
         lax.ppermute(sent, ("row", "col"), [(b, a) for a, b in offset(*p)])
         for p, sent in zip(places[1:], blocks[1:])
     ]
+    far_all = lax.ppermute(far_all, "row", partner)
     arrived = sum((a.astype(F32) for a in arrivals), blocks[0].astype(F32)).astype(BF16)
-    arrived, far_three, far_last, *mixed = lax.optimization_barrier((arrived, far_three, far_last, *mixed))
+    arrived, far_all, mixed[1] = lax.optimization_barrier((arrived, far_all, mixed[1]))
     grad_in = lax.ppermute(arrived, ("dp", "row"), swap_back)
 
     grad_weight, mixed, grad_long, grad_short = kernel_call(
@@ -458,18 +488,18 @@
             shaped((3, drow, local), F32),
             shaped((rows, local), BF16),
             shaped((ngroups, ntaps), F32),
-            shaped((3 * nshort, local), F32),
+            shaped((nshort, 3, local), F32),
         ],
         grid=(3,),
         in_specs=[whole(nblocks, ncol, rows, dcol)] * 2
         + [whole(*grad_near.shape)] * 4
-        + [whole(*far_three.shape), whole(*far_last.shape)]
+        + [whole(*far_all.shape)]
         + [whole(rows, width)] * ndp,
         out_specs=[
             pl.BlockSpec((1, drow, local), lambda i: (i, 0, 0)),
             whole(rows, local),
             whole(ngroups, ntaps),
-            whole(3 * nshort, local),
+            whole(nshort, 3, local),
         ],
         scratch=[
             pltpu.VMEM((2, ndp, 3 * chunk + extra, width), BF16),
@@ -478,9 +508,8 @@
         flops=2 * mm_flops,
         nbytes=2 * mm_bytes,
         vmem=MOST_VMEM_BYTES,
-    )(x0, x1, *near, near_last, far_three, far_last, *mixed)
+    )(x0, x1, *near, near_last, far_all, *mixed)
     grad_weight = jnp.transpose(grad_weight, (1, 0, 2))
-    grad_short = grad_short.reshape(nshort, 3, local)
     return (mixed, grad_in, grad_weight, grad_long, grad_short)
 
 

time: 171 us -> 206 us (1.20)
  Pallas kernels: 31.4 us -> 53.5 us
  waiting for transfers between devices: 62.3 us -> 71.7 us
  starting transfers between devices: 61.9 us -> 67.9 us
    pallas_call x1, Pallas kernels: 4.56 us -> 28.9 us  [move_activations(): kernel_call(functools.partial(second_grad_body, ndp), [shaped(grad_near.s...]
    ppermute x18 -> x21, waiting for transfers between devices: 36.5 us -> 59 us  [the longest x3 28.4 us: move_activations(): mixed[ahead] = lax.ppermute(mixed[ahead], 'dp', turn[ahead])]
    ppermute x18 -> x21, starting transfers between devices: 37 us -> 49.4 us  [the longest x2 14.9 us: second_hop(): rightward = lax.ppermute(right + from_left, ('dp', 'row'), shift(1, across))]
    ppermute x1, waiting for transfers between devices: 8.53 us -> 0.01 us  [move_activations(): moved = lax.ppermute(tokens, ('dp', 'row'), swap)]
    ppermute x2, waiting for transfers between devices: 4.51 us -> 0.01 us  [gather_over_line(): far_after = lax.ppermute(after, 'dp', [(a + 1, a) for a in range(ndp // 2)])]
    all_to_all x1 -> x0, starting transfers between devices: 3.75 us -> none  [move_activations(): lax.all_to_all(grad_out, 'dp', split_axis=1, concat_axis=0, tiled=True)]
    ppermute x1, starting transfers between devices: 6.77 us -> 3.58 us  [move_activations(): grad_in = lax.ppermute(arrived, ('dp', 'row'), swap_back)]
    pallas_call x2, Pallas kernels: 8.13 us -> 5.89 us  [the longest x1 5.85 us: move_activations(): kernel_call(project_body, [shaped((3, chunk, width), BF16)] * (2 * ndp),...]
  transfers between devices with their start and end apart: 33 -> 35, of which waited for: 15 -> 13; matrix products, arithmetic and copies ran while one was open for 4% -> 1% of each run, Pallas kernels for 16% -> 6%
where the time goes in v9:
time: 206 us; the launch traced here: 205 us
  waiting for transfers between devices  71.7 us (35%)
  starting transfers between devices  67.9 us (33%)
  Pallas kernels  53.5 us (26%)
  local copies, waits for them, and re-layouts  8.95 us (4%)
  other arithmetic  2.14 us (1%)
    pallas_call x1, Pallas kernels, move_activations(): kernel_call(functools.partial(second_grad_body, ndp), [shaped(grad_near.s...  28.9 us
    ppermute x3, waiting for transfers between devices, move_activations(): mixed[ahead] = lax.ppermute(mixed[ahead], 'dp', turn[ahead])  28.4 us
    ppermute x2, waiting for transfers between devices, second_hop(): rightward = lax.ppermute(right + from_left, ('dp', 'row'), shift(1, across))  16.6 us
    ppermute x2, starting transfers between devices, second_hop(): rightward = lax.ppermute(right + from_left, ('dp', 'row'), shift(1, across))  14.9 us
    ppermute x1, waiting for transfers between devices, move_activations(): upstream[2] = lax.ppermute(upstream[2], 'dp', turn[2])  10.9 us
    ppermute x2, starting transfers between devices, second_hop(): leftward = lax.ppermute(left + from_right, ('dp', 'row'), shift(-1, across))  8.76 us
    unnamed x59, local copies, waits for them, and re-layouts  8.26 us
    ppermute x2, starting transfers between devices, first_hop(): lax.ppermute(far, 'dp', [(a, a + 1) for a in range(ndp // 2)])  7.78 us
  transfers between devices with their start and end apart: 35, of which 13 were waited for; matrix products, arithmetic and copies ran while one was open for 1% of the time, Pallas kernels for 6%

profile of v9, /device:TPU:1, one launch (start us, length us, event | category | flops | bytes accessed | tf_op | source)
XLA Modules:
  0.0 205.3 jit_solution(14906057094490909986)
XLA Ops:
  0.8 4.6 %collective-permute-start = (bf16[192,512]{1,0:T(8,128)(2,1)}, bf16[192,512]{1,0:T(8,128)(2,1)S(1)}, u32[]{:S(2)}, u32[]{:S(2)}) collective-permute-start(bf16[192,512]{1,0:T(8,128)(2,1)} %param.5), channel_id=1, source_target_pairs={{0,0},{16,2},{8,4},{24,6},{2,8},{18,10},{10,12},{26,14},{4,16},{20... | collective-permute-start | bytes 589832 | tf_op jit(solution)/shard_map/ppermute | solution.py:375
  7.6 10.9 %collective-permute-done.2.refs_11_ = bf16[192,128]{1,0:T(8,128)(2,1)S(1)} collective-permute-done((bf16[192,128]{1,0:T(8,128)(2,1)S(1)}, bf16[192,128]{1,0:T(8,128)(2,1)S(1)}, u32[]{:S(2)}, u32[]{:S(2)}) %collective-permute-start.2) | collective-permute-done | bytes 49184 | tf_op jit(solution)/shard_map/ppermute | solution.py:379
  21.2 3.3 %collective-permute-start.4 = (bf16[192,128]{1,0:T(8,128)(2,1)S(1)}, bf16[192,128]{1,0:T(8,128)(2,1)S(1)}, u32[]{:S(2)}, u32[]{:S(2)}) collective-permute-start(bf16[192,128]{1,0:T(8,128)(2,1)S(1)} %get-tuple-element.60), channel_id=1, source_target_pairs={{0,24},{8,0},{16,8},{24,16},{1,25},{9,1},{17,9},{25,17},{2,26},{10... | collective-permute-start | bytes 147464 | tf_op jit(solution)/shard_map/ppermute | solution.py:383
  26.1 3.8 %collective-permute-done.6 = bf16[192,512]{1,0:T(8,128)(2,1)S(1)} collective-permute-done((bf16[192,512]{1,0:T(8,128)(2,1)S(1)}, bf16[192,512]{1,0:T(8,128)(2,1)S(1)}, u32[]{:S(2)}, u32[]{:S(2)}) %collective-permute-start.6) | collective-permute-done | bytes 196640 | tf_op jit(solution)/shard_map/ppermute | solution.py:381
  30.0 5.9 %shard_map.93 = (bf16[3,384,128]{2,1,0:T(8,128)(2,1)S(1)}, bf16[3,384,128]{2,1,0:T(8,128)(2,1)S(1)}, bf16[3,384,128]{2,1,0:T(8,128)(2,1)S(1)}, bf16[3,384,128]{2...) custom-call(bf16[2,2,192,512]{3,2,1,0:T(8,128)(2,1)S(1)} %bitcast.19, ...), custom_call_target="tpu_custom_call" | custom-call | flops 2415919104 | bytes 10223616 | tf_op jit(solution)/shard_map/pallas_call | solution.py:401
  38.2 2.9 %collective-permute-start.9 = (bf16[1152,128]{1,0:T(8,128)(2,1)S(1)}, bf16[1152,128]{1,0:T(8,128)(2,1)S(1)}, u32[]{:S(2)}, u32[]{:S(2)}) collective-permute-start(bf16[1152,128]{1,0:T(8,128)(2,1)S(1)} %bitcast.24), channel_id=1, source_target_pairs={{0,8},{8,16},{1,9},{9,17},{2,10},{10,18},{3,11},{11,19},{4,12},{12... | collective-permute-start | bytes 884744 | tf_op jit(solution)/shard_map/ppermute | solution.py:329
  41.8 4.9 %collective-permute-start.14 = (bf16[1152,128]{1,0:T(8,128)(2,1)S(1)}, bf16[1152,128]{1,0:T(8,128)(2,1)S(1)}, u32[]{:S(2)}, u32[]{:S(2)}) collective-permute-start(bf16[1152,128]{1,0:T(8,128)(2,1)S(1)} %bitcast.26), channel_id=1, source_target_pairs={{0,8},{8,16},{1,9},{9,17},{2,10},{10,18},{3,11},{11,19},{4,12},{12... | collective-permute-start | bytes 884744 | tf_op jit(solution)/shard_map/ppermute | solution.py:329
  47.4 5.7 %collective-permute-start.12 = (bf16[1152,128]{1,0:T(8,128)(2,1)S(1)}, bf16[1152,128]{1,0:T(8,128)(2,1)S(1)}, u32[]{:S(2)}, u32[]{:S(2)}) collective-permute-start(bf16[1152,128]{1,0:T(8,128)(2,1)S(1)} %bitcast_add_fusion.2), channel_id=1, source_target_pairs={{0,24},{2,26},{4,28},{6,30},{8,0},{10,2},{12,4},{14,6},{16,8},{18,... | collective-permute-start | bytes 884744 | tf_op jit(solution)/shard_map/ppermute | solution.py:336
  53.8 3.1 %collective-permute-start.17 = (bf16[1152,128]{1,0:T(8,128)(2,1)S(1)}, bf16[1152,128]{1,0:T(8,128)(2,1)S(1)}, u32[]{:S(2)}, u32[]{:S(2)}) collective-permute-start(bf16[1152,128]{1,0:T(8,128)(2,1)S(1)} %bitcast_add_fusion), channel_id=1, source_target_pairs={{0,26},{2,24},{4,30},{6,28},{8,2},{10,0},{12,6},{14,4},{16,10},{18... | collective-permute-start | bytes 884744 | tf_op jit(solution)/shard_map/ppermute | solution.py:336
  57.0 12.6 %collective-permute-start.15 = (bf16[1152,128]{1,0:T(8,128)(2,1)S(1)}, bf16[1152,128]{1,0:T(8,128)(2,1)S(1)}, u32[]{:S(2)}, u32[]{:S(2)}) collective-permute-start(bf16[1152,128]{1,0:T(8,128)(2,1)S(1)} %bitcast_add_fusion.1), channel_id=1, source_target_pairs={{0,10},{2,8},{4,14},{6,12},{8,18},{10,16},{12,22},{14,20},{16,26},... | collective-permute-start | bytes 884744 | tf_op jit(solution)/shard_map/ppermute | solution.py:335
  69.7 2.3 %collective-permute-start.10 = (bf16[1152,128]{1,0:T(8,128)(2,1)S(1)}, bf16[1152,128]{1,0:T(8,128)(2,1)S(1)}, u32[]{:S(2)}, u32[]{:S(2)}) collective-permute-start(bf16[1152,128]{1,0:T(8,128)(2,1)S(1)} %bitcast_add_fusion.3), channel_id=1, source_target_pairs={{0,8},{2,10},{4,12},{6,14},{8,16},{10,18},{12,20},{14,22},{16,24},... | collective-permute-start | bytes 884744 | tf_op jit(solution)/shard_map/ppermute | solution.py:335
  76.0 10.3 %collective-permute-done.15.refs_4_ = bf16[1152,128]{1,0:T(8,128)(2,1)S(1)} collective-permute-done((bf16[1152,128]{1,0:T(8,128)(2,1)S(1)}, bf16[1152,128]{1,0:T(8,128)(2,1)S(1)}, u32[]{:S(2)}, u32[]{:S(2)}) %collective-permute-start.15) | collective-permute-done | bytes 294944 | tf_op jit(solution)/shard_map/ppermute | solution.py:335
  86.3 6.3 %collective-permute-done.10.refs_1_ = bf16[1152,128]{1,0:T(8,128)(2,1)S(1)} collective-permute-done((bf16[1152,128]{1,0:T(8,128)(2,1)S(1)}, bf16[1152,128]{1,0:T(8,128)(2,1)S(1)}, u32[]{:S(2)}, u32[]{:S(2)}) %collective-permute-start.10) | collective-permute-done | bytes 294944 | tf_op jit(solution)/shard_map/ppermute | solution.py:335
  93.3 5.4 %shard_map.95 = (bf16[1184,128]{1,0:T(8,128)(2,1)}, bf16[1152,128]{1,0:T(8,128)(2,1)}, bf16[192,128]{1,0:T(8,128)(2,1)}, bf16[192,128]{1,0:T(8,128)(2,1)}, bf16[...) custom-call(bf16[1152,128]{1,0:T(8,128)(2,1)} %bitcast.27, bf16[1152,128]{1,0:T(8,128)(2,1)} %copy-done.21, ...), custom_call_target="tpu_custom_call" | custom-call | flops 1207959552 | bytes 2752512 | tf_op jit(solution)/shard_map/pallas_call | solution.py:426
  98.8 3.3 %collective-permute-start.19 = (bf16[1184,128]{1,0:T(8,128)(2,1)}, bf16[1184,128]{1,0:T(8,128)(2,1)S(1)}, u32[]{:S(2)}, u32[]{:S(2)}) collective-permute-start(bf16[1184,128]{1,0:T(8,128)(2,1)} %get-tuple-element.79.near.refs_2_), channel_id=1, source_target_pairs={{0,24},{2,26},{4,28},{6,30},{8,0},{10,2},{12,4},{14,6},{16,8},{18,... | collective-permute-start | bytes 909320 | tf_op jit(solution)/shard_map/ppermute | solution.py:344
  103.8 22.0 %collective-permute-done.23.refs_9_ = bf16[192,128]{1,0:T(8,128)(2,1)S(1)} collective-permute-done((bf16[192,128]{1,0:T(8,128)(2,1)}, bf16[192,128]{1,0:T(8,128)(2,1)S(1)}, u32[]{:S(2)}, u32[]{:S(2)}) %collective-permute-start.23) | collective-permute-done | bytes 49184 | tf_op jit(solution)/shard_map/ppermute | solution.py:446
  130.8 3.3 %collective-permute-start.24 = (bf16[192,128]{1,0:T(8,128)(2,1)}, bf16[192,128]{1,0:T(8,128)(2,1)S(1)}, u32[]{:S(2)}, u32[]{:S(2)}) collective-permute-start(bf16[192,128]{1,0:T(8,128)(2,1)} %get-tuple-element.84), channel_id=1, source_target_pairs={{0,24},{8,0},{16,8},{24,16},{1,25},{9,1},{17,9},{25,17},{2,26},{10... | collective-permute-start | bytes 147464 | tf_op jit(solution)/shard_map/ppermute | solution.py:446
  135.0 5.5 %shard_map.96 = (f32[2,384,512]{2,1,0:T(8,128)S(1)}, bf16[3,1152,128]{2,1,0:T(8,128)(2,1)S(1)}) custom-call(bf16[1184,128]{1,0:T(8,128)(2,1)S(1)} %copy-done.6, bf16[1184,128]{1,0:T(8,128)(2,1)S(1)} %collective-permute-done.18.near_before.refs_3_, bf16[1184,128]{1,0:T(8,128)(2,1)S(1)} %collective-permute-done.19.near_after.refs_4_, ...), custom_call_target="tpu_custom_call" | custom-call | flops 2415919104 | bytes 10223616 | tf_op jit(solution)/shard_map/pallas_call | solution.py:450
  142.7 6.3 %collective-permute-done.24.refs_10_ = bf16[192,128]{1,0:T(8,128)(2,1)S(1)} collective-permute-done((bf16[192,128]{1,0:T(8,128)(2,1)}, bf16[192,128]{1,0:T(8,128)(2,1)S(1)}, u32[]{:S(2)}, u32[]{:S(2)}) %collective-permute-start.24) | collective-permute-done | bytes 49184 | tf_op jit(solution)/shard_map/ppermute | solution.py:446
  150.2 28.9 %shard_map.97 = (bf16[1184,128]{1,0:T(8,128)(2,1)}, bf16[4,1152,128]{2,1,0:T(8,128)(2,1)}, bf16[192,512]{1,0:T(8,128)(2,1)}, bf16[192,512]{1,0:T(8,128)(2,1)}, b...) custom-call(f32[2,384,512]{2,1,0:T(8,128)} %copy-done.1, bf16[3,1152,128]{2,1,0:T(8,128)(2,1)} %copy-done.3, ...), custom_call_target="tpu_custom_call" | custom-call | flops 603979776 | bytes 2555904 | tf_op jit(solution)/shard_map/pallas_call | solution.py:459
  183.9 2.6 %collective-permute-done.29 = bf16[192,512]{1,0:T(8,128)(2,1)S(1)} collective-permute-done((bf16[192,512]{1,0:T(8,128)(2,1)}, bf16[192,512]{1,0:T(8,128)(2,1)S(1)}, u32[]{:S(2)}, u32[]{:S(2)}) %collective-permute-start.29) | collective-permute-done | bytes 196640 | tf_op jit(solution)/shard_map/ppermute | solution.py:477
  187.4 4.2 %collective-permute-done.31 = bf16[192,512]{1,0:T(8,128)(2,1)S(1)} collective-permute-done((bf16[192,512]{1,0:T(8,128)(2,1)}, bf16[192,512]{1,0:T(8,128)(2,1)S(1)}, u32[]{:S(2)}, u32[]{:S(2)}) %collective-permute-start.31) | collective-permute-done | bytes 196640 | tf_op jit(solution)/shard_map/ppermute | solution.py:477
  192.7 3.6 %collective-permute-start.34 = (bf16[192,512]{1,0:T(8,128)(2,1)S(1)}, bf16[192,512]{1,0:T(8,128)(2,1)S(1)}, u32[]{:S(2)}, u32[]{:S(2)}) collective-permute-start(bf16[192,512]{1,0:T(8,128)(2,1)S(1)} %add_convert_fusion), channel_id=1, source_target_pairs={{0,0},{2,16},{4,8},{6,24},{8,2},{10,18},{12,10},{14,26},{16,4},{18... | collective-permute-start | bytes 589832 | tf_op jit(solution)/shard_map/ppermute | solution.py:483
  196.3 7.1 %shard_map.98 = (f32[3,1024,512]{2,1,0:T(8,128)}, bf16[192,512]{1,0:T(8,128)(2,1)}, f32[32,128]{1,0:T(8,128)}, f32[3,3,512]{2,1,0:T(4,128)}) custom-call(bf16[2,2,192,512]{3,2,1,0:T(8,128)(2,1)} %bitcast.21, bf16[2,2,192,512]{3,2,1,0:T(8,128)(2,1)} %copy-done.17, bf16[1184,128]{1,0:T(8,128)(2,1)} %get-tuple-element.79.near.refs_2_, ...), custom_call_target="tpu_custom_call" | custom-call | flops 2415919104 | bytes 10223616 | tf_op jit(solution)/shard_map/pallas_call | solution.py:485
  (125 shorter events, 35.6 us)
Async XLA Ops:
  0.6 17.9 %collective-permute-start.1 = (bf16[3,1024,512]{2,1,0:T(8,128)(2,1)}, bf16[3,1024,512]{2,1,0:T(8,128)(2,1)S(1)}, u32[]{:S(2)}, u32[]{:S(2)}) collective-permute-start(bf16[3,1024,512]{2,1,0:T(8,128)(2,1)} %bitcast.28), channel_id=1, source_target_pairs={{0,2},{2,0},{4,6},{6,4},{1,3},{3,1},{5,7},{7,5},{8,10},{10,8},{12,... | collective-permute-start | bytes 9437192 | tf_op jit(solution)/shard_map/ppermute | solution.py:376
  0.8 17.7 %collective-permute-start = (bf16[192,512]{1,0:T(8,128)(2,1)}, bf16[192,512]{1,0:T(8,128)(2,1)S(1)}, u32[]{:S(2)}, u32[]{:S(2)}) collective-permute-start(bf16[192,512]{1,0:T(8,128)(2,1)} %param.5), channel_id=1, source_target_pairs={{0,0},{16,2},{8,4},{24,6},{2,8},{18,10},{10,12},{26,14},{4,16},{20... | collective-permute-start | bytes 589832 | tf_op jit(solution)/shard_map/ppermute | solution.py:375
  6.3 12.2 %collective-permute-start.2 = (bf16[192,128]{1,0:T(8,128)(2,1)S(1)}, bf16[192,128]{1,0:T(8,128)(2,1)S(1)}, u32[]{:S(2)}, u32[]{:S(2)}) collective-permute-start(bf16[192,128]{1,0:T(8,128)(2,1)S(1)} %get-tuple-element.56), channel_id=1, source_target_pairs={{0,16},{8,24},{16,0},{24,8},{1,17},{9,25},{17,1},{25,9},{2,18},{10... | collective-permute-start | bytes 147464 | tf_op jit(solution)/shard_map/ppermute | solution.py:379
  18.6 11.3 %collective-permute-start.6 = (bf16[192,512]{1,0:T(8,128)(2,1)S(1)}, bf16[192,512]{1,0:T(8,128)(2,1)S(1)}, u32[]{:S(2)}, u32[]{:S(2)}) collective-permute-start(bf16[192,512]{1,0:T(8,128)(2,1)S(1)} %collective-permute-done), channel_id=1, source_target_pairs={{0,4},{1,5},{2,6},{3,7},{4,0},{5,1},{6,2},{7,3},{8,12},{9,13},{10,... | collective-permute-start | bytes 589832 | tf_op jit(solution)/shard_map/ppermute | solution.py:381
  37.3 32.3 %collective-permute-start.8 = (bf16[2,2,192,512]{3,2,1,0:T(8,128)(2,1)S(1)}, bf16[2,2,192,512]{3,2,1,0:T(8,128)(2,1)S(1)}, u32[]{:S(2)}, u32[]{:S(2)}) collective-permute-start(bf16[2,2,192,512]{3,2,1,0:T(8,128)(2,1)S(1)} %bitcast.20), channel_id=1, source_target_pairs={{0,2},{2,0},{4,6},{6,4},{1,3},{3,1},{5,7},{7,5},{8,10},{10,8},{12,... | collective-permute-start | bytes 2359304 | tf_op jit(solution)/shard_map/ppermute | solution.py:413
  38.2 18.8 %collective-permute-start.9 = (bf16[1152,128]{1,0:T(8,128)(2,1)S(1)}, bf16[1152,128]{1,0:T(8,128)(2,1)S(1)}, u32[]{:S(2)}, u32[]{:S(2)}) collective-permute-start(bf16[1152,128]{1,0:T(8,128)(2,1)S(1)} %bitcast.24), channel_id=1, source_target_pairs={{0,8},{8,16},{1,9},{9,17},{2,10},{10,18},{3,11},{11,19},{4,12},{12... | collective-permute-start | bytes 884744 | tf_op jit(solution)/shard_map/ppermute | solution.py:329
  41.8 12.0 %collective-permute-start.14 = (bf16[1152,128]{1,0:T(8,128)(2,1)S(1)}, bf16[1152,128]{1,0:T(8,128)(2,1)S(1)}, u32[]{:S(2)}, u32[]{:S(2)}) collective-permute-start(bf16[1152,128]{1,0:T(8,128)(2,1)S(1)} %bitcast.26), channel_id=1, source_target_pairs={{0,8},{8,16},{1,9},{9,17},{2,10},{10,18},{3,11},{11,19},{4,12},{12... | collective-permute-start | bytes 884744 | tf_op jit(solution)/shard_map/ppermute | solution.py:329
  46.7 28.4 %collective-permute-start.13 = (bf16[1152,128]{1,0:T(8,128)(2,1)S(1)}, bf16[1152,128]{1,0:T(8,128)(2,1)}, u32[]{:S(2)}, u32[]{:S(2)}) collective-permute-start(bf16[1152,128]{1,0:T(8,128)(2,1)S(1)} %bitcast.22), channel_id=1, source_target_pairs={{0,2},{2,0},{4,6},{6,4},{8,10},{10,8},{12,14},{14,12},{16,18},{18,... | collective-permute-start | bytes 884744 | tf_op jit(solution)/shard_map/ppermute | solution.py:337
  47.4 27.7 %collective-permute-start.12 = (bf16[1152,128]{1,0:T(8,128)(2,1)S(1)}, bf16[1152,128]{1,0:T(8,128)(2,1)S(1)}, u32[]{:S(2)}, u32[]{:S(2)}) collective-permute-start(bf16[1152,128]{1,0:T(8,128)(2,1)S(1)} %bitcast_add_fusion.2), channel_id=1, source_target_pairs={{0,24},{2,26},{4,28},{6,30},{8,0},{10,2},{12,4},{14,6},{16,8},{18,... | collective-permute-start | bytes 884744 | tf_op jit(solution)/shard_map/ppermute | solution.py:336
  53.8 22.1 %collective-permute-start.17 = (bf16[1152,128]{1,0:T(8,128)(2,1)S(1)}, bf16[1152,128]{1,0:T(8,128)(2,1)S(1)}, u32[]{:S(2)}, u32[]{:S(2)}) collective-permute-start(bf16[1152,128]{1,0:T(8,128)(2,1)S(1)} %bitcast_add_fusion), channel_id=1, source_target_pairs={{0,26},{2,24},{4,30},{6,28},{8,2},{10,0},{12,6},{14,4},{16,10},{18... | collective-permute-start | bytes 884744 | tf_op jit(solution)/shard_map/ppermute | solution.py:336
  57.0 29.3 %collective-permute-start.15 = (bf16[1152,128]{1,0:T(8,128)(2,1)S(1)}, bf16[1152,128]{1,0:T(8,128)(2,1)S(1)}, u32[]{:S(2)}, u32[]{:S(2)}) collective-permute-start(bf16[1152,128]{1,0:T(8,128)(2,1)S(1)} %bitcast_add_fusion.1), channel_id=1, source_target_pairs={{0,10},{2,8},{4,14},{6,12},{8,18},{10,16},{12,22},{14,20},{16,26},... | collective-permute-start | bytes 884744 | tf_op jit(solution)/shard_map/ppermute | solution.py:335
  69.7 22.9 %collective-permute-start.10 = (bf16[1152,128]{1,0:T(8,128)(2,1)S(1)}, bf16[1152,128]{1,0:T(8,128)(2,1)S(1)}, u32[]{:S(2)}, u32[]{:S(2)}) collective-permute-start(bf16[1152,128]{1,0:T(8,128)(2,1)S(1)} %bitcast_add_fusion.3), channel_id=1, source_target_pairs={{0,8},{2,10},{4,12},{6,14},{8,16},{10,18},{12,20},{14,22},{16,24},... | collective-permute-start | bytes 884744 | tf_op jit(solution)/shard_map/ppermute | solution.py:335
  98.7 28.0 %collective-permute-start.18 = (bf16[1184,128]{1,0:T(8,128)(2,1)}, bf16[1184,128]{1,0:T(8,128)(2,1)S(1)}, u32[]{:S(2)}, u32[]{:S(2)}) collective-permute-start(bf16[1184,128]{1,0:T(8,128)(2,1)} %get-tuple-element.79.near.refs_2_), channel_id=1, source_target_pairs={{0,8},{2,10},{4,12},{6,14},{8,16},{10,18},{12,20},{14,22},{16,24},... | collective-permute-start | bytes 909320 | tf_op jit(solution)/shard_map/ppermute | solution.py:343
  98.8 28.6 %collective-permute-start.19 = (bf16[1184,128]{1,0:T(8,128)(2,1)}, bf16[1184,128]{1,0:T(8,128)(2,1)S(1)}, u32[]{:S(2)}, u32[]{:S(2)}) collective-permute-start(bf16[1184,128]{1,0:T(8,128)(2,1)} %get-tuple-element.79.near.refs_2_), channel_id=1, source_target_pairs={{0,24},{2,26},{4,28},{6,30},{8,0},{10,2},{12,4},{14,6},{16,8},{18,... | collective-permute-start | bytes 909320 | tf_op jit(solution)/shard_map/ppermute | solution.py:344
  102.1 26.7 %collective-permute-start.22 = (bf16[1152,128]{1,0:T(8,128)(2,1)}, bf16[1152,128]{1,0:T(8,128)(2,1)S(1)}, u32[]{:S(2)}, u32[]{:S(2)}) collective-permute-start(bf16[1152,128]{1,0:T(8,128)(2,1)} %get-tuple-element.80), channel_id=1, source_target_pairs={{0,26},{2,24},{4,30},{6,28},{8,2},{10,0},{12,6},{14,4},{16,10},{18... | collective-permute-start | bytes 884744 | tf_op jit(solution)/shard_map/ppermute | solution.py:344
  102.6 27.4 %collective-permute-start.21 = (bf16[1152,128]{1,0:T(8,128)(2,1)}, bf16[1152,128]{1,0:T(8,128)(2,1)S(1)}, u32[]{:S(2)}, u32[]{:S(2)}) collective-permute-start(bf16[1152,128]{1,0:T(8,128)(2,1)} %get-tuple-element.80), channel_id=1, source_target_pairs={{0,10},{2,8},{4,14},{6,12},{8,18},{10,16},{12,22},{14,20},{16,26},... | collective-permute-start | bytes 884744 | tf_op jit(solution)/shard_map/ppermute | solution.py:343
  103.8 22.0 %collective-permute-start.23 = (bf16[192,128]{1,0:T(8,128)(2,1)}, bf16[192,128]{1,0:T(8,128)(2,1)S(1)}, u32[]{:S(2)}, u32[]{:S(2)}) collective-permute-start(bf16[192,128]{1,0:T(8,128)(2,1)} %get-tuple-element.83), channel_id=1, source_target_pairs={{0,16},{8,24},{16,0},{24,8},{1,17},{9,25},{17,1},{25,9},{2,18},{10... | collective-permute-start | bytes 147464 | tf_op jit(solution)/shard_map/ppermute | solution.py:446
  126.7 22.3 %collective-permute-start.25 = (bf16[1184,128]{1,0:T(8,128)(2,1)S(1)}, bf16[1184,128]{1,0:T(8,128)(2,1)S(1)}, u32[]{:S(2)}, u32[]{:S(2)}) collective-permute-start(bf16[1184,128]{1,0:T(8,128)(2,1)S(1)} %collective-permute-done.18.near_before.refs_3_), channel_id=1, source_target_pairs={{8,16},{16,24},{9,17},{17,25},{10,18},{18,26},{11,19},{19,27},{12,... | collective-permute-start | bytes 909320 | tf_op jit(solution)/shard_map/ppermute | solution.py:346
  127.4 21.7 %collective-permute-start.26 = (bf16[1184,128]{1,0:T(8,128)(2,1)S(1)}, bf16[1184,128]{1,0:T(8,128)(2,1)S(1)}, u32[]{:S(2)}, u32[]{:S(2)}) collective-permute-start(bf16[1184,128]{1,0:T(8,128)(2,1)S(1)} %collective-permute-done.19.near_after.refs_4_), channel_id=1, source_target_pairs={{8,0},{16,8},{9,1},{17,9},{10,2},{18,10},{11,3},{19,11},{12,4},{20... | collective-permute-start | bytes 909320 | tf_op jit(solution)/shard_map/ppermute | solution.py:347
  128.8 20.3 %collective-permute-start.28 = (bf16[1152,128]{1,0:T(8,128)(2,1)S(1)}, bf16[1152,128]{1,0:T(8,128)(2,1)S(1)}, u32[]{:S(2)}, u32[]{:S(2)}) collective-permute-start(bf16[1152,128]{1,0:T(8,128)(2,1)S(1)} %collective-permute-done.22.far_after), channel_id=1, source_target_pairs={{8,0},{16,8},{9,1},{17,9},{10,2},{18,10},{11,3},{19,11},{12,4},{20... | collective-permute-start | bytes 884744 | tf_op jit(solution)/shard_map/ppermute | solution.py:347
  130.1 19.0 %collective-permute-start.27 = (bf16[1152,128]{1,0:T(8,128)(2,1)S(1)}, bf16[1152,128]{1,0:T(8,128)(2,1)S(1)}, u32[]{:S(2)}, u32[]{:S(2)}) collective-permute-start(bf16[1152,128]{1,0:T(8,128)(2,1)S(1)} %collective-permute-done.21.far_before), channel_id=1, source_target_pairs={{8,16},{16,24},{9,17},{17,25},{10,18},{18,26},{11,19},{19,27},{12,... | collective-permute-start | bytes 884744 | tf_op jit(solution)/shard_map/ppermute | solution.py:346
  130.8 18.3 %collective-permute-start.24 = (bf16[192,128]{1,0:T(8,128)(2,1)}, bf16[192,128]{1,0:T(8,128)(2,1)S(1)}, u32[]{:S(2)}, u32[]{:S(2)}) collective-permute-start(bf16[192,128]{1,0:T(8,128)(2,1)} %get-tuple-element.84), channel_id=1, source_target_pairs={{0,24},{8,0},{16,8},{24,16},{1,25},{9,1},{17,9},{25,17},{2,26},{10... | collective-permute-start | bytes 147464 | tf_op jit(solution)/shard_map/ppermute | solution.py:446
  179.1 13.5 %collective-permute-start.32 = (bf16[4,1152,128]{2,1,0:T(8,128)(2,1)}, bf16[4,1152,128]{2,1,0:T(8,128)(2,1)S(1)}, u32[]{:S(2)}, u32[]{:S(2)}) collective-permute-start(bf16[4,1152,128]{2,1,0:T(8,128)(2,1)} %get-tuple-element.91), channel_id=1, source_target_pairs={{0,2},{2,0},{4,6},{6,4},{1,3},{3,1},{5,7},{7,5},{8,10},{10,8},{12,... | collective-permute-start | bytes 3538952 | tf_op jit(solution)/shard_map/ppermute | solution.py:480
  192.7 12.0 %collective-permute-start.34 = (bf16[192,512]{1,0:T(8,128)(2,1)S(1)}, bf16[192,512]{1,0:T(8,128)(2,1)S(1)}, u32[]{:S(2)}, u32[]{:S(2)}) collective-permute-start(bf16[192,512]{1,0:T(8,128)(2,1)S(1)} %add_convert_fusion), channel_id=1, source_target_pairs={{0,0},{2,16},{4,8},{6,24},{8,2},{10,18},{12,10},{14,26},{16,4},{18... | collective-permute-start | bytes 589832 | tf_op jit(solution)/shard_map/ppermute | solution.py:483
  (40 other events, 402.6 us)

commit v10 on v8

--- a/solution.py
+++ b/solution.py
@@ -52,6 +52,13 @@
 
 def wrapped(value, size):
     return lax.rem(value + 2 * size, size)
+
+
+def split_body(all_ref, *out_refs):
+    width = out_refs[0].shape[1]
+    for ahead, out_ref in enumerate(out_refs):
+        at = wrapped(lax.axis_index("dp") + ahead, len(out_refs)) * width
+        out_ref[...] = all_ref[:, pl.ds(pl.multiple_of(at, width), width)]
 
 
 def project_body(x_ref, w_ref, *refs):
@@ -167,7 +174,9 @@
             mixed_ref[:, lanes] = held_mixed[owner]
             small = held[0, owner, 3 * tokens :].astype(F32)
             long_ref[owner * groups : (owner + 1) * groups] = small[:groups]
-            short_ref[:, lanes] = small[groups : groups + short_ref.shape[0]]
+            nshort, three, _ = short_ref.shape
+            for j in range(nshort):
+                short_ref[j, :, lanes] = small[groups + three * j : groups + three * (j + 1)]
 
     at = pl.ds(pl.multiple_of(i * tokens, 16), tokens)
     gm = jnp.concatenate(
@@ -196,8 +205,14 @@
 
 def middle_body(scale, nshort, nrow, *refs):
     sums, refs = (refs[:3], refs[3:6]), refs[6:]
-    sf_ref, causal_ref, anti_ref, go_ref, near_ref, other_ref, *mixed_refs, m_ref, gm_ref, mixed_ref = refs
+    (sf_ref, causal_ref, anti_ref), refs = refs[:3], refs[3:]
+    *refs, m_ref, gm_ref, mixed_ref, go_ref = refs
+    ndp = len(refs) // 2 - 1
+    go_refs, (near_ref, other_ref), mixed_refs = refs[:ndp], refs[ndp : ndp + 2], refs[ndp + 2 :]
     tokens, width = go_ref.shape
+    for behind, piece in enumerate(go_refs):
+        at = wrapped(lax.axis_index("dp") - behind, ndp) * (tokens // ndp)
+        go_ref[pl.ds(pl.multiple_of(at, 16), tokens // ndp)] = piece[...]
     row = lax.axis_index("row")
     nblocks = nrow // 2
     rows = tokens // nrow
@@ -247,7 +262,6 @@
     conv = filtered(causal_ref, p_pairs)
     upstream = go_ref[...].astype(F32)
     mixed_ref[...] = (feats[0] * conv).astype(BF16)
-    ndp = len(mixed_refs)
     for ahead, out_ref in enumerate(mixed_refs):
         at = pl.multiple_of(wrapped(lax.axis_index("dp") + ahead, ndp) * (tokens // ndp), 16)
         out_ref[...] = mixed_ref[pl.ds(at, tokens // ndp)]
@@ -351,9 +365,14 @@
 
     w = jnp.transpose(in_weight, (1, 0, 2))
     moved = lax.ppermute(tokens, ("dp", "row"), swap)
+    turn = [[(a, (a + ahead) % ndp) for a in range(ndp)] for ahead in range(ndp)]
+    upstream = [*kernel_call(split_body, [shaped((rows, width), BF16)] * ndp)(grad_out)]
+    upstream[2] = lax.ppermute(upstream[2], "dp", turn[2])
+    moved, upstream = lax.optimization_barrier((moved, upstream))
     near = [moved] + [lax.ppermute(moved, ("row", "col"), offset(*p)) for p in places[1:]]
-    upstream = lax.all_to_all(grad_out, "dp", split_axis=1, concat_axis=0, tiled=True)
-    upstream, *near = lax.optimization_barrier((upstream, *near))
+    for ahead in (1, 3):
+        upstream[ahead] = lax.ppermute(upstream[ahead], "dp", turn[ahead])
+    upstream[1::2], near[1:] = lax.optimization_barrier((upstream[1::2], near[1:]))
     x0 = jnp.stack(near).reshape(nblocks, ncol, rows, dcol)
     x1 = lax.ppermute(x0, "row", partner)
 
@@ -398,17 +417,19 @@
         + [shaped((rows, width), BF16)] * ndp,
         grid=(1,),
         in_specs=[whole(3 * chunk, width)] * 6
-        + [whole(3 * nshort, width), half, other, whole(seq, width)],
+        + [whole(3 * nshort, width), half, other]
+        + [whole(rows, width)] * ndp,
         out_specs=[whole(3 * chunk + extra, width), whole(3 * chunk, width)] + [whole(rows, width)] * ndp,
         scratch=[
             pltpu.VMEM((3 * seq, width), F32),
             pltpu.VMEM((3 * seq, width), BF16),
             pltpu.VMEM((seq, width), BF16),
+            pltpu.VMEM((seq, width), BF16),
         ],
         flops=3 * 2 * groups * ntaps * 2 * ntaps * width * (seq // ntaps),
         nbytes=2 * width * seq * 14,
         vmem=MOST_VMEM_BYTES,
-    )(*sums, sf, bands, bands, upstream)
+    )(*sums, sf, bands, bands, *upstream)
     mixed = [mixed[0]] + [
         lax.ppermute(part, "dp", [(a, (a + ahead) % ndp) for a in range(ndp)])
         for ahead, part in enumerate(mixed)
@@ -458,7 +479,7 @@
             shaped((3, drow, local), F32),
             shaped((rows, local), BF16),
             shaped((ngroups, ntaps), F32),
-            shaped((3 * nshort, local), F32),
+            shaped((nshort, 3, local), F32),
         ],
         grid=(3,),
         in_specs=[whole(nblocks, ncol, rows, dcol)] * 2
@@ -469,7 +490,7 @@
             pl.BlockSpec((1, drow, local), lambda i: (i, 0, 0)),
             whole(rows, local),
             whole(ngroups, ntaps),
-            whole(3 * nshort, local),
+            whole(nshort, 3, local),
         ],
         scratch=[
             pltpu.VMEM((2, ndp, 3 * chunk + extra, width), BF16),
@@ -480,7 +501,6 @@
         vmem=MOST_VMEM_BYTES,
     )(x0, x1, *near, near_last, far_three, far_last, *mixed)
     grad_weight = jnp.transpose(grad_weight, (1, 0, 2))
-    grad_short = grad_short.reshape(nshort, 3, local)
     return (mixed, grad_in, grad_weight, grad_long, grad_short)
 
 

time: 171 us -> 168 us (0.982)
  starting transfers between devices: 61.9 us -> 58.7 us
  waiting for transfers between devices: 62.3 us -> 64.5 us
    ppermute x0 -> x3, waiting for transfers between devices: none -> 11.5 us  [the longest x1 9.96 us: move_activations(): upstream[2] = lax.ppermute(upstream[2], 'dp', turn[2])]
    ppermute x1, waiting for transfers between devices: 8.53 us -> 0.13 us  [move_activations(): moved = lax.ppermute(tokens, ('dp', 'row'), swap)]
    ppermute x2, starting transfers between devices: 9.17 us -> 2.91 us  [sum_over_line(): lax.ppermute(right + from_left, 'dp', [(a, (a + 1) % ndp) for a in range(...]
    ppermute x2, starting transfers between devices: 5.28 us -> 11 us  [sum_over_line(): lax.ppermute(left + from_right, 'dp', [(a, (a - 1) % ndp) for a in range(...]
    ppermute x0 -> x3, starting transfers between devices: none -> 4.42 us  [the longest x2 3.74 us: move_activations(): upstream[ahead] = lax.ppermute(upstream[ahead], 'dp', turn[ahead])]
    ppermute x2, starting transfers between devices: 12.1 us -> 7.96 us  [sum_over_line(): from_left = lax.ppermute(far, 'dp', [(a, a + 1) for a in range(ndp // 2)])]
    ppermute x2, waiting for transfers between devices: 0.07 us -> 3.94 us  [sum_over_line(): lax.ppermute(left + from_right, 'dp', [(a, (a - 1) % ndp) for a in range(...]
    all_to_all x1 -> x0, starting transfers between devices: 3.75 us -> none  [move_activations(): lax.all_to_all(grad_out, 'dp', split_axis=1, concat_axis=0, tiled=True)]
  transfers between devices with their start and end apart: 33 -> 35, of which waited for: 15 -> 16; matrix products, arithmetic and copies ran while one was open for 4% -> 2% of each run, Pallas kernels for 16% -> 16%
where the time goes in v10:
time: 168 us; the launch traced here: 166 us
  waiting for transfers between devices  64.5 us (38%)
  starting transfers between devices  58.7 us (35%)
  Pallas kernels  31.2 us (19%)
  local copies, waits for them, and re-layouts  8.37 us (5%)
  other arithmetic  2.19 us (1%)
    ppermute x2, waiting for transfers between devices, gather_over_line(): after = lax.ppermute(own, ('dp', 'row'), shift(-1))  11.6 us
    ppermute x2, starting transfers between devices, sum_over_line(): lax.ppermute(left + from_right, 'dp', [(a, (a - 1) % ndp) for a in range(...  11 us
    ppermute x2, waiting for transfers between devices, gather_over_line(): before = lax.ppermute(own, ('dp', 'row'), shift(1))  10.2 us
    ppermute x1, waiting for transfers between devices, move_activations(): upstream[2] = lax.ppermute(upstream[2], 'dp', turn[2])  9.96 us
    ppermute x2, starting transfers between devices, sum_over_line(): from_left = lax.ppermute(far, 'dp', [(a, a + 1) for a in range(ndp // 2)])  7.96 us
    pallas_call x2, Pallas kernels, move_activations(): kernel_call(project_body, [shaped((3, chunk, width), BF16)] * ndp, grid=(...  7.93 us
    unnamed x55, local copies, waits for them, and re-layouts  7.68 us
    ppermute x3, waiting for transfers between devices, move_activations(): lax.ppermute(sent, ('row', 'col'), [(b, a) for a, b in offset(*p)])  7.37 us
  transfers between devices with their start and end apart: 35, of which 16 were waited for; matrix products, arithmetic and copies ran while one was open for 2% of the time, Pallas kernels for 16%

profile of v10, /device:TPU:1, one launch (start us, length us, event | category | flops | bytes accessed | tf_op | source)
XLA Modules:
  0.0 165.9 jit_solution(8125772214405450336)
XLA Ops:
  0.6 4.6 %collective-permute-start = (bf16[192,512]{1,0:T(8,128)(2,1)}, bf16[192,512]{1,0:T(8,128)(2,1)S(1)}, u32[]{:S(2)}, u32[]{:S(2)}) collective-permute-start(bf16[192,512]{1,0:T(8,128)(2,1)} %param.5), channel_id=1, source_target_pairs={{0,0},{16,2},{8,4},{24,6},{2,8},{18,10},{10,12},{26,14},{4,16},{20... | collective-permute-start | bytes 589832 | tf_op jit(solution)/shard_map/ppermute | solution.py:367
  6.9 10.0 %collective-permute-done.1.refs_11_ = bf16[192,128]{1,0:T(8,128)(2,1)S(1)} collective-permute-done((bf16[192,128]{1,0:T(8,128)(2,1)S(1)}, bf16[192,128]{1,0:T(8,128)(2,1)S(1)}, u32[]{:S(2)}, u32[]{:S(2)}) %collective-permute-start.1) | collective-permute-done | bytes 49184 | tf_op jit(solution)/shard_map/ppermute | solution.py:370
  24.9 4.0 %collective-permute-done.5 = bf16[192,512]{1,0:T(8,128)(2,1)S(1)} collective-permute-done((bf16[192,512]{1,0:T(8,128)(2,1)S(1)}, bf16[192,512]{1,0:T(8,128)(2,1)S(1)}, u32[]{:S(2)}, u32[]{:S(2)}) %collective-permute-start.5) | collective-permute-done | bytes 196640 | tf_op jit(solution)/shard_map/ppermute | solution.py:372
  29.6 3.8 %shard_map.93 = (bf16[3,384,128]{2,1,0:T(8,128)(2,1)S(1)}, bf16[3,384,128]{2,1,0:T(8,128)(2,1)S(1)}, bf16[3,384,128]{2,1,0:T(8,128)(2,1)S(1)}, bf16[3,384,128]{2,1,0:T(8,128)(2,1)S(1)}) custom-call(bf16[2,2,192,512]{3,2,1,0:T(8,128)(2,1)S(1)} %bitcast.20, bf16[3,1024,512]{2,1,0:T(8,128)(2,1)} %bitcast.5.w_ref.refs_4_), custom_call_target="tpu_custom_call" | custom-call | flops 1207959552 | bytes 5111808 | tf_op jit(solution)/shard_map/pallas_call | solution.py:395
  35.1 4.0 %collective-permute-start.8 = (bf16[1152,128]{1,0:T(8,128)(2,1)S(1)}, bf16[1152,128]{1,0:T(8,128)(2,1)S(1)}, u32[]{:S(2)}, u32[]{:S(2)}) collective-permute-start(bf16[1152,128]{1,0:T(8,128)(2,1)S(1)} %bitcast.23), channel_id=1, source_target_pairs={{0,8},{8,16},{1,9},{9,17},{2,10},{10,18},{3,11},{11,19},{4,12},{12... | collective-permute-start | bytes 884744 | tf_op jit(solution)/shard_map/ppermute | solution.py:318
  39.2 6.9 %collective-permute-start.11 = (bf16[1152,128]{1,0:T(8,128)(2,1)S(1)}, bf16[1152,128]{1,0:T(8,128)(2,1)}, u32[]{:S(2)}, u32[]{:S(2)}) collective-permute-start(bf16[1152,128]{1,0:T(8,128)(2,1)S(1)} %bitcast_add_fusion.2), channel_id=1, source_target_pairs={{0,24},{8,0},{16,8},{24,16},{1,25},{9,1},{17,9},{25,17},{2,26},{10... | collective-permute-start | bytes 884744 | tf_op jit(solution)/shard_map/ppermute | solution.py:321
  46.1 4.1 %shard_map.94 = (bf16[3,384,128]{2,1,0:T(8,128)(2,1)S(1)}, bf16[3,384,128]{2,1,0:T(8,128)(2,1)S(1)}, bf16[3,384,128]{2,1,0:T(8,128)(2,1)S(1)}, bf16[3,384,128]{2,1,0:T(8,128)(2,1)S(1)}) custom-call(bf16[2,2,192,512]{3,2,1,0:T(8,128)(2,1)S(1)} %collective-permute-done.7.x_ref.refs_1_, bf16[3,1024,512]{2,1,0:T(8,128)(2,1)} %bitcast.5.w_ref.refs_4_), custom_call_target="tpu_custom_call" | custom-call | flops 1207959552 | bytes 5111808 | tf_op jit(solution)/shard_map/pallas_call | solution.py:395
  51.7 4.0 %collective-permute-start.12 = (bf16[1152,128]{1,0:T(8,128)(2,1)S(1)}, bf16[1152,128]{1,0:T(8,128)(2,1)S(1)}, u32[]{:S(2)}, u32[]{:S(2)}) collective-permute-start(bf16[1152,128]{1,0:T(8,128)(2,1)S(1)} %bitcast.25), channel_id=1, source_target_pairs={{0,8},{8,16},{1,9},{9,17},{2,10},{10,18},{3,11},{11,19},{4,12},{12... | collective-permute-start | bytes 884744 | tf_op jit(solution)/shard_map/ppermute | solution.py:318
  55.7 4.1 %collective-permute-start.15 = (bf16[1152,128]{1,0:T(8,128)(2,1)S(1)}, bf16[1152,128]{1,0:T(8,128)(2,1)S(1)}, u32[]{:S(2)}, u32[]{:S(2)}) collective-permute-start(bf16[1152,128]{1,0:T(8,128)(2,1)S(1)} %bitcast_add_fusion), channel_id=1, source_target_pairs={{0,24},{8,0},{16,8},{24,16},{1,25},{9,1},{17,9},{25,17},{2,26},{10... | collective-permute-start | bytes 884744 | tf_op jit(solution)/shard_map/ppermute | solution.py:321
  59.9 3.0 %collective-permute-done.12 = bf16[1152,128]{1,0:T(8,128)(2,1)S(1)} collective-permute-done((bf16[1152,128]{1,0:T(8,128)(2,1)S(1)}, bf16[1152,128]{1,0:T(8,128)(2,1)S(1)}, u32[]{:S(2)}, u32[]{:S(2)}) %collective-permute-start.12) | collective-permute-done | bytes 294944 | tf_op jit(solution)/shard_map/ppermute | solution.py:318
  68.3 3.9 %collective-permute-done.15.refs_5_ = bf16[1152,128]{1,0:T(8,128)(2,1)S(1)} collective-permute-done((bf16[1152,128]{1,0:T(8,128)(2,1)S(1)}, bf16[1152,128]{1,0:T(8,128)(2,1)S(1)}, u32[]{:S(2)}, u32[]{:S(2)}) %collective-permute-start.15) | collective-permute-done | bytes 294944 | tf_op jit(solution)/shard_map/ppermute | solution.py:321
  72.3 7.2 %collective-permute-done.13.refs_4_ = bf16[1152,128]{1,0:T(8,128)(2,1)S(1)} collective-permute-done((bf16[1152,128]{1,0:T(8,128)(2,1)S(1)}, bf16[1152,128]{1,0:T(8,128)(2,1)S(1)}, u32[]{:S(2)}, u32[]{:S(2)}) %collective-permute-start.13) | collective-permute-done | bytes 294944 | tf_op jit(solution)/shard_map/ppermute | solution.py:320
  80.2 5.4 %shard_map.96 = (bf16[1184,128]{1,0:T(8,128)(2,1)}, bf16[1152,128]{1,0:T(8,128)(2,1)}, bf16[192,128]{1,0:T(8,128)(2,1)}, bf16[192,128]{1,0:T(8,128)(2,1)}, bf16[...) custom-call(bf16[1152,128]{1,0:T(8,128)(2,1)} %bitcast.26, bf16[1152,128]{1,0:T(8,128)(2,1)} %copy-done.17, ...), custom_call_target="tpu_custom_call" | custom-call | flops 1207959552 | bytes 2752512 | tf_op jit(solution)/shard_map/pallas_call | solution.py:414
  85.6 4.0 %collective-permute-start.20 = (bf16[1152,128]{1,0:T(8,128)(2,1)}, bf16[1152,128]{1,0:T(8,128)(2,1)S(1)}, u32[]{:S(2)}, u32[]{:S(2)}) collective-permute-start(bf16[1152,128]{1,0:T(8,128)(2,1)} %get-tuple-element.77), channel_id=1, source_target_pairs={{0,26},{2,24},{4,30},{6,28},{8,2},{10,0},{12,6},{14,4},{16,10},{18... | collective-permute-start | bytes 884744 | tf_op jit(solution)/shard_map/ppermute | solution.py:336
  91.3 5.5 %collective-permute-done.20.far_after = bf16[1152,128]{1,0:T(8,128)(2,1)S(1)} collective-permute-done((bf16[1152,128]{1,0:T(8,128)(2,1)}, bf16[1152,128]{1,0:T(8,128)(2,1)S(1)}, u32[]{:S(2)}, u32[]{:S(2)}) %collective-permute-start.20) | collective-permute-done | bytes 294944 | tf_op jit(solution)/shard_map/ppermute | solution.py:336
  97.2 6.1 %collective-permute-done.17.near_after.refs_4_ = bf16[1184,128]{1,0:T(8,128)(2,1)S(1)} collective-permute-done((bf16[1184,128]{1,0:T(8,128)(2,1)}, bf16[1184,128]{1,0:T(8,128)(2,1)S(1)}, u32[]{:S(2)}, u32[]{:S(2)}) %collective-permute-start.17) | collective-permute-done | bytes 303136 | tf_op jit(solution)/shard_map/ppermute | solution.py:336
  104.6 7.4 %collective-permute-done.16.near_before.refs_3_ = bf16[1184,128]{1,0:T(8,128)(2,1)S(1)} collective-permute-done((bf16[1184,128]{1,0:T(8,128)(2,1)}, bf16[1184,128]{1,0:T(8,128)(2,1)S(1)}, u32[]{:S(2)}, u32[]{:S(2)}) %collective-permute-start.16) | collective-permute-done | bytes 303136 | tf_op jit(solution)/shard_map/ppermute | solution.py:335
  118.4 5.5 %shard_map.97 = (f32[2,384,512]{2,1,0:T(8,128)S(1)}, bf16[3,1152,128]{2,1,0:T(8,128)(2,1)S(1)}) custom-call(bf16[1184,128]{1,0:T(8,128)(2,1)S(1)} %copy-done.6, bf16[1184,128]{1,0:T(8,128)(2,1)S(1)} %collective-permute-done.16.near_before.refs_3_, bf16[1184,128]{1,0:T(8,128)(2,1)S(1)} %collective-permute-done.17.near_after.refs_4_, ...), custom_call_target="tpu_custom_call" | custom-call | flops 2415919104 | bytes 10223616 | tf_op jit(solution)/shard_map/pallas_call | solution.py:441
  125.2 4.5 %collective-permute-done.25.refs_3_ = bf16[1152,128]{1,0:T(8,128)(2,1)S(1)} collective-permute-done((bf16[1152,128]{1,0:T(8,128)(2,1)S(1)}, bf16[1152,128]{1,0:T(8,128)(2,1)S(1)}, u32[]{:S(2)}, u32[]{:S(2)}) %collective-permute-start.25) | collective-permute-done | bytes 294944 | tf_op jit(solution)/shard_map/ppermute | solution.py:339
  131.3 4.5 %shard_map.98 = (bf16[1184,128]{1,0:T(8,128)(2,1)}, bf16[1152,128]{1,0:T(8,128)(2,1)}, bf16[192,512]{1,0:T(8,128)(2,1)}, bf16[192,512]{1,0:T(8,128)(2,1)}, bf16[...) custom-call(f32[2,384,512]{2,1,0:T(8,128)} %copy-done.1, bf16[1184,128]{1,0:T(8,128)(2,1)} %copy-done.13, ...), custom_call_target="tpu_custom_call" | custom-call | flops 603979776 | bytes 2555904 | tf_op jit(solution)/shard_map/pallas_call | solution.py:450
  139.9 3.1 %collective-permute-done.26 = bf16[192,512]{1,0:T(8,128)(2,1)S(1)} collective-permute-done((bf16[192,512]{1,0:T(8,128)(2,1)}, bf16[192,512]{1,0:T(8,128)(2,1)S(1)}, u32[]{:S(2)}, u32[]{:S(2)}) %collective-permute-start.26) | collective-permute-done | bytes 196640 | tf_op jit(solution)/shard_map/ppermute | solution.py:469
  144.5 3.6 %collective-permute-done.28 = bf16[192,512]{1,0:T(8,128)(2,1)S(1)} collective-permute-done((bf16[192,512]{1,0:T(8,128)(2,1)}, bf16[192,512]{1,0:T(8,128)(2,1)S(1)}, u32[]{:S(2)}, u32[]{:S(2)}) %collective-permute-start.28) | collective-permute-done | bytes 196640 | tf_op jit(solution)/shard_map/ppermute | solution.py:469
  151.3 6.8 %collective-permute-start.34 = (bf16[192,512]{1,0:T(8,128)(2,1)S(1)}, bf16[192,512]{1,0:T(8,128)(2,1)S(1)}, u32[]{:S(2)}, u32[]{:S(2)}) collective-permute-start(bf16[192,512]{1,0:T(8,128)(2,1)S(1)} %add_convert_fusion), channel_id=1, source_target_pairs={{0,0},{2,16},{4,8},{6,24},{8,2},{10,18},{12,10},{14,26},{16,4},{18... | collective-permute-start | bytes 589832 | tf_op jit(solution)/shard_map/ppermute | solution.py:474
  158.2 7.1 %shard_map.99 = (f32[3,1024,512]{2,1,0:T(8,128)}, bf16[192,512]{1,0:T(8,128)(2,1)}, f32[32,128]{1,0:T(8,128)}, f32[3,3,512]{2,1,0:T(4,128)}) custom-call(bf16[2,2,192,512]{3,2,1,0:T(8,128)(2,1)} %bitcast.21, bf16[2,2,192,512]{3,2,1,0:T(8,128)(2,1)} %copy-done.5, bf16[1184,128]{1,0:T(8,128)(2,1)} %get-tuple-element.76.near.refs_2_, ...), custom_call_target="tpu_custom_call" | custom-call | flops 2415919104 | bytes 10223616 | tf_op jit(solution)/shard_map/pallas_call | solution.py:476
  (122 shorter events, 41.6 us)
Async XLA Ops:
  0.6 16.4 %collective-permute-start = (bf16[192,512]{1,0:T(8,128)(2,1)}, bf16[192,512]{1,0:T(8,128)(2,1)S(1)}, u32[]{:S(2)}, u32[]{:S(2)}) collective-permute-start(bf16[192,512]{1,0:T(8,128)(2,1)} %param.5), channel_id=1, source_target_pairs={{0,0},{16,2},{8,4},{24,6},{2,8},{18,10},{10,12},{26,14},{4,16},{20... | collective-permute-start | bytes 589832 | tf_op jit(solution)/shard_map/ppermute | solution.py:367
  6.2 10.7 %collective-permute-start.1 = (bf16[192,128]{1,0:T(8,128)(2,1)S(1)}, bf16[192,128]{1,0:T(8,128)(2,1)S(1)}, u32[]{:S(2)}, u32[]{:S(2)}) collective-permute-start(bf16[192,128]{1,0:T(8,128)(2,1)S(1)} %get-tuple-element.56), channel_id=1, source_target_pairs={{0,16},{8,24},{16,0},{24,8},{1,17},{9,25},{17,1},{25,9},{2,18},{10... | collective-permute-start | bytes 147464 | tf_op jit(solution)/shard_map/ppermute | solution.py:370
  17.0 11.9 %collective-permute-start.5 = (bf16[192,512]{1,0:T(8,128)(2,1)S(1)}, bf16[192,512]{1,0:T(8,128)(2,1)S(1)}, u32[]{:S(2)}, u32[]{:S(2)}) collective-permute-start(bf16[192,512]{1,0:T(8,128)(2,1)S(1)} %collective-permute-done), channel_id=1, source_target_pairs={{0,4},{1,5},{2,6},{3,7},{4,0},{5,1},{6,2},{7,3},{8,12},{9,13},{10,... | collective-permute-start | bytes 589832 | tf_op jit(solution)/shard_map/ppermute | solution.py:372
  29.1 17.0 %collective-permute-start.7 = (bf16[2,2,192,512]{3,2,1,0:T(8,128)(2,1)S(1)}, bf16[2,2,192,512]{3,2,1,0:T(8,128)(2,1)S(1)}, u32[]{:S(2)}, u32[]{:S(2)}) collective-permute-start(bf16[2,2,192,512]{3,2,1,0:T(8,128)(2,1)S(1)} %bitcast.19), channel_id=1, source_target_pairs={{0,2},{2,0},{4,6},{6,4},{1,3},{3,1},{5,7},{7,5},{8,10},{10,8},{12,... | collective-permute-start | bytes 2359304 | tf_op jit(solution)/shard_map/ppermute | solution.py:377
  34.8 82.6 %collective-permute-start.21 = (bf16[3,1024,512]{2,1,0:T(8,128)(2,1)}, bf16[3,1024,512]{2,1,0:T(8,128)(2,1)}, u32[]{:S(2)}, u32[]{:S(2)}) collective-permute-start(bf16[3,1024,512]{2,1,0:T(8,128)(2,1)} %bitcast.5.w_ref.refs_4_), channel_id=1, source_target_pairs={{0,2},{2,0},{4,6},{6,4},{1,3},{3,1},{5,7},{7,5},{8,10},{10,8},{12,... | collective-permute-start | bytes 9437192 | tf_op jit(solution)/shard_map/ppermute | solution.py:440
  35.1 15.8 %collective-permute-start.8 = (bf16[1152,128]{1,0:T(8,128)(2,1)S(1)}, bf16[1152,128]{1,0:T(8,128)(2,1)S(1)}, u32[]{:S(2)}, u32[]{:S(2)}) collective-permute-start(bf16[1152,128]{1,0:T(8,128)(2,1)S(1)} %bitcast.23), channel_id=1, source_target_pairs={{0,8},{8,16},{1,9},{9,17},{2,10},{10,18},{3,11},{11,19},{4,12},{12... | collective-permute-start | bytes 884744 | tf_op jit(solution)/shard_map/ppermute | solution.py:318
  39.2 29.1 %collective-permute-start.11 = (bf16[1152,128]{1,0:T(8,128)(2,1)S(1)}, bf16[1152,128]{1,0:T(8,128)(2,1)}, u32[]{:S(2)}, u32[]{:S(2)}) collective-permute-start(bf16[1152,128]{1,0:T(8,128)(2,1)S(1)} %bitcast_add_fusion.2), channel_id=1, source_target_pairs={{0,24},{8,0},{16,8},{24,16},{1,25},{9,1},{17,9},{25,17},{2,26},{10... | collective-permute-start | bytes 884744 | tf_op jit(solution)/shard_map/ppermute | solution.py:321
  51.0 17.3 %collective-permute-start.9 = (bf16[1152,128]{1,0:T(8,128)(2,1)S(1)}, bf16[1152,128]{1,0:T(8,128)(2,1)S(1)}, u32[]{:S(2)}, u32[]{:S(2)}) collective-permute-start(bf16[1152,128]{1,0:T(8,128)(2,1)S(1)} %bitcast_add_fusion.3), channel_id=1, source_target_pairs={{0,8},{8,16},{16,24},{24,0},{1,9},{9,17},{17,25},{25,1},{2,10},{10... | collective-permute-start | bytes 884744 | tf_op jit(solution)/shard_map/ppermute | solution.py:320
  51.7 11.2 %collective-permute-start.12 = (bf16[1152,128]{1,0:T(8,128)(2,1)S(1)}, bf16[1152,128]{1,0:T(8,128)(2,1)S(1)}, u32[]{:S(2)}, u32[]{:S(2)}) collective-permute-start(bf16[1152,128]{1,0:T(8,128)(2,1)S(1)} %bitcast.25), channel_id=1, source_target_pairs={{0,8},{8,16},{1,9},{9,17},{2,10},{10,18},{3,11},{11,19},{4,12},{12... | collective-permute-start | bytes 884744 | tf_op jit(solution)/shard_map/ppermute | solution.py:318
  55.7 16.5 %collective-permute-start.15 = (bf16[1152,128]{1,0:T(8,128)(2,1)S(1)}, bf16[1152,128]{1,0:T(8,128)(2,1)S(1)}, u32[]{:S(2)}, u32[]{:S(2)}) collective-permute-start(bf16[1152,128]{1,0:T(8,128)(2,1)S(1)} %bitcast_add_fusion), channel_id=1, source_target_pairs={{0,24},{8,0},{16,8},{24,16},{1,25},{9,1},{17,9},{25,17},{2,26},{10... | collective-permute-start | bytes 884744 | tf_op jit(solution)/shard_map/ppermute | solution.py:321
  63.0 16.5 %collective-permute-start.13 = (bf16[1152,128]{1,0:T(8,128)(2,1)S(1)}, bf16[1152,128]{1,0:T(8,128)(2,1)S(1)}, u32[]{:S(2)}, u32[]{:S(2)}) collective-permute-start(bf16[1152,128]{1,0:T(8,128)(2,1)S(1)} %bitcast_add_fusion.1), channel_id=1, source_target_pairs={{0,8},{8,16},{16,24},{24,0},{1,9},{9,17},{17,25},{25,1},{2,10},{10... | collective-permute-start | bytes 884744 | tf_op jit(solution)/shard_map/ppermute | solution.py:320
  85.6 11.2 %collective-permute-start.20 = (bf16[1152,128]{1,0:T(8,128)(2,1)}, bf16[1152,128]{1,0:T(8,128)(2,1)S(1)}, u32[]{:S(2)}, u32[]{:S(2)}) collective-permute-start(bf16[1152,128]{1,0:T(8,128)(2,1)} %get-tuple-element.77), channel_id=1, source_target_pairs={{0,26},{2,24},{4,30},{6,28},{8,2},{10,0},{12,6},{14,4},{16,10},{18... | collective-permute-start | bytes 884744 | tf_op jit(solution)/shard_map/ppermute | solution.py:336
  89.6 13.7 %collective-permute-start.17 = (bf16[1184,128]{1,0:T(8,128)(2,1)}, bf16[1184,128]{1,0:T(8,128)(2,1)S(1)}, u32[]{:S(2)}, u32[]{:S(2)}) collective-permute-start(bf16[1184,128]{1,0:T(8,128)(2,1)} %get-tuple-element.76.near.refs_2_), channel_id=1, source_target_pairs={{0,24},{2,26},{4,28},{6,30},{8,0},{10,2},{12,4},{14,6},{16,8},{18,... | collective-permute-start | bytes 909320 | tf_op jit(solution)/shard_map/ppermute | solution.py:336
  91.3 20.7 %collective-permute-start.16 = (bf16[1184,128]{1,0:T(8,128)(2,1)}, bf16[1184,128]{1,0:T(8,128)(2,1)S(1)}, u32[]{:S(2)}, u32[]{:S(2)}) collective-permute-start(bf16[1184,128]{1,0:T(8,128)(2,1)} %get-tuple-element.76.near.refs_2_), channel_id=1, source_target_pairs={{0,8},{2,10},{4,12},{6,14},{8,16},{10,18},{12,20},{14,22},{16,24},... | collective-permute-start | bytes 909320 | tf_op jit(solution)/shard_map/ppermute | solution.py:335
  91.3 24.2 %collective-permute-start.19 = (bf16[1152,128]{1,0:T(8,128)(2,1)}, bf16[1152,128]{1,0:T(8,128)(2,1)S(1)}, u32[]{:S(2)}, u32[]{:S(2)}) collective-permute-start(bf16[1152,128]{1,0:T(8,128)(2,1)} %get-tuple-element.77), channel_id=1, source_target_pairs={{0,10},{2,8},{4,14},{6,12},{8,18},{10,16},{12,22},{14,20},{16,26},... | collective-permute-start | bytes 884744 | tf_op jit(solution)/shard_map/ppermute | solution.py:335
  96.8 20.0 %collective-permute-start.18 = (bf16[1152,128]{1,0:T(8,128)(2,1)}, bf16[1152,128]{1,0:T(8,128)(2,1)S(1)}, u32[]{:S(2)}, u32[]{:S(2)}) collective-permute-start(bf16[1152,128]{1,0:T(8,128)(2,1)} %get-tuple-element.77), channel_id=1, source_target_pairs={{0,2},{2,0},{4,6},{6,4},{8,10},{10,8},{12,14},{14,12},{16,18},{18,... | collective-permute-start | bytes 884744 | tf_op jit(solution)/shard_map/ppermute | solution.py:337
  103.3 26.4 %collective-permute-start.23 = (bf16[1184,128]{1,0:T(8,128)(2,1)S(1)}, bf16[1184,128]{1,0:T(8,128)(2,1)S(1)}, u32[]{:S(2)}, u32[]{:S(2)}) collective-permute-start(bf16[1184,128]{1,0:T(8,128)(2,1)S(1)} %collective-permute-done.17.near_after.refs_4_), channel_id=1, source_target_pairs={{8,0},{16,8},{9,1},{17,9},{10,2},{18,10},{11,3},{19,11},{12,4},{20... | collective-permute-start | bytes 909320 | tf_op jit(solution)/shard_map/ppermute | solution.py:339
  112.0 17.7 %collective-permute-start.22 = (bf16[1184,128]{1,0:T(8,128)(2,1)S(1)}, bf16[1184,128]{1,0:T(8,128)(2,1)S(1)}, u32[]{:S(2)}, u32[]{:S(2)}) collective-permute-start(bf16[1184,128]{1,0:T(8,128)(2,1)S(1)} %collective-permute-done.16.near_before.refs_3_), channel_id=1, source_target_pairs={{8,16},{16,24},{9,17},{17,25},{10,18},{18,26},{11,19},{19,27},{12,... | collective-permute-start | bytes 909320 | tf_op jit(solution)/shard_map/ppermute | solution.py:338
  115.5 14.2 %collective-permute-start.25 = (bf16[1152,128]{1,0:T(8,128)(2,1)S(1)}, bf16[1152,128]{1,0:T(8,128)(2,1)S(1)}, u32[]{:S(2)}, u32[]{:S(2)}) collective-permute-start(bf16[1152,128]{1,0:T(8,128)(2,1)S(1)} %collective-permute-done.20.far_after), channel_id=1, source_target_pairs={{8,0},{16,8},{9,1},{17,9},{10,2},{18,10},{11,3},{19,11},{12,4},{20... | collective-permute-start | bytes 884744 | tf_op jit(solution)/shard_map/ppermute | solution.py:339
  116.8 12.9 %collective-permute-start.24 = (bf16[1152,128]{1,0:T(8,128)(2,1)S(1)}, bf16[1152,128]{1,0:T(8,128)(2,1)S(1)}, u32[]{:S(2)}, u32[]{:S(2)}) collective-permute-start(bf16[1152,128]{1,0:T(8,128)(2,1)S(1)} %collective-permute-done.19.far_before), channel_id=1, source_target_pairs={{8,16},{16,24},{9,17},{17,25},{10,18},{18,26},{11,19},{19,27},{12,... | collective-permute-start | bytes 884744 | tf_op jit(solution)/shard_map/ppermute | solution.py:338
  135.8 15.5 %collective-permute-start.29 = (bf16[3,1152,128]{2,1,0:T(8,128)(2,1)S(1)}, bf16[3,1152,128]{2,1,0:T(8,128)(2,1)S(1)}, u32[]{:S(2)}, u32[]{:S(2)}) collective-permute-start(bf16[3,1152,128]{2,1,0:T(8,128)(2,1)S(1)} %get-tuple-element.86), channel_id=1, source_target_pairs={{0,2},{2,0},{4,6},{6,4},{1,3},{3,1},{5,7},{7,5},{8,10},{10,8},{12,... | collective-permute-start | bytes 2654216 | tf_op jit(solution)/shard_map/ppermute | solution.py:467
  137.9 10.3 %collective-permute-start.28 = (bf16[192,512]{1,0:T(8,128)(2,1)}, bf16[192,512]{1,0:T(8,128)(2,1)S(1)}, u32[]{:S(2)}, u32[]{:S(2)}) collective-permute-start(bf16[192,512]{1,0:T(8,128)(2,1)} %get-tuple-element.83), channel_id=1, source_target_pairs={{5,0},{4,1},{7,2},{6,3},{1,4},{0,5},{3,6},{2,7},{13,8},{12,9},{15,... | collective-permute-start | bytes 589832 | tf_op jit(solution)/shard_map/ppermute | solution.py:469
  139.0 12.3 %collective-permute-start.30 = (bf16[1152,128]{1,0:T(8,128)(2,1)}, bf16[1152,128]{1,0:T(8,128)(2,1)S(1)}, u32[]{:S(2)}, u32[]{:S(2)}) collective-permute-start(bf16[1152,128]{1,0:T(8,128)(2,1)} %get-tuple-element.87), channel_id=1, source_target_pairs={{0,2},{2,0},{4,6},{6,4},{1,3},{3,1},{5,7},{7,5},{8,10},{10,8},{12,... | collective-permute-start | bytes 884744 | tf_op jit(solution)/shard_map/ppermute | solution.py:467
  151.3 13.9 %collective-permute-start.34 = (bf16[192,512]{1,0:T(8,128)(2,1)S(1)}, bf16[192,512]{1,0:T(8,128)(2,1)S(1)}, u32[]{:S(2)}, u32[]{:S(2)}) collective-permute-start(bf16[192,512]{1,0:T(8,128)(2,1)S(1)} %add_convert_fusion), channel_id=1, source_target_pairs={{0,0},{2,16},{4,8},{6,24},{8,2},{10,18},{12,10},{14,26},{16,4},{18... | collective-permute-start | bytes 589832 | tf_op jit(solution)/shard_map/ppermute | solution.py:474
  (38 other events, 362.9 us)

commit v11 on v10

--- a/solution.py
+++ b/solution.py
@@ -367,7 +367,6 @@
     moved = lax.ppermute(tokens, ("dp", "row"), swap)
     turn = [[(a, (a + ahead) % ndp) for a in range(ndp)] for ahead in range(ndp)]
     upstream = [*kernel_call(split_body, [shaped((rows, width), BF16)] * ndp)(grad_out)]
-    upstream[2] = lax.ppermute(upstream[2], "dp", turn[2])
     moved, upstream = lax.optimization_barrier((moved, upstream))
     near = [moved] + [lax.ppermute(moved, ("row", "col"), offset(*p)) for p in places[1:]]
     for ahead in (1, 3):
@@ -375,6 +374,8 @@
     upstream[1::2], near[1:] = lax.optimization_barrier((upstream[1::2], near[1:]))
     x0 = jnp.stack(near).reshape(nblocks, ncol, rows, dcol)
     x1 = lax.ppermute(x0, "row", partner)
+    upstream[2] = lax.ppermute(upstream[2], "dp", turn[2])
+    upstream[2], x1 = lax.optimization_barrier((upstream[2], x1))
 
     sf = lax.dynamic_slice_in_dim(short_filter, z * width, width, 2).reshape(3 * nshort, width)
     lf = lax.dynamic_slice_in_dim(long_filter, z * groups, groups, 0).astype(F32)
@@ -463,14 +464,14 @@
         nbytes=mm_bytes // 2,
         vmem=MOST_VMEM_BYTES,
     )(part, near_far_before, near_far_after, far_far_before, far_far_after, w, partner_w)
-    far_three, far_last = lax.optimization_barrier((far_three, far_last))
+    far_three, far_last, mixed[1:] = lax.optimization_barrier((far_three, far_last, mixed[1:]))
     far_three, far_last = (lax.ppermute(part, "row", partner) for part in (far_three, far_last))
     arrivals = [
         lax.ppermute(sent, ("row", "col"), [(b, a) for a, b in offset(*p)])
         for p, sent in zip(places[1:], blocks[1:])
     ]
     arrived = sum((a.astype(F32) for a in arrivals), blocks[0].astype(F32)).astype(BF16)
-    arrived, far_three, far_last, *mixed = lax.optimization_barrier((arrived, far_three, far_last, *mixed))
+    arrived, far_three, far_last = lax.optimization_barrier((arrived, far_three, far_last))
     grad_in = lax.ppermute(arrived, ("dp", "row"), swap_back)
 
     grad_weight, mixed, grad_long, grad_short = kernel_call(

time: 168 us -> 164 us (0.976)
  waiting for transfers between devices: 64.5 us -> 59.9 us
    ppermute x1, waiting for transfers between devices: 0.13 us -> 9.2 us  [move_activations(): moved = lax.ppermute(tokens, ('dp', 'row'), swap)]
    ppermute x1, waiting for transfers between devices: 9.96 us -> 4.07 us  [move_activations(): upstream[2] = lax.ppermute(upstream[2], 'dp', turn[2])]
    ppermute x1, starting transfers between devices: 0.69 us -> 6.46 us  [move_activations(): upstream[2] = lax.ppermute(upstream[2], 'dp', turn[2])]
    ppermute x3, starting transfers between devices: 2.07 us -> 7.6 us  [move_activations(): lax.ppermute(part, 'dp', [(a, (a + ahead) % ndp) for a in range(ndp)])]
    ppermute x2, starting transfers between devices: 11 us -> 5.97 us  [sum_over_line(): lax.ppermute(left + from_right, 'dp', [(a, (a - 1) % ndp) for a in range(...]
    ppermute x2, waiting for transfers between devices: 4.53 us -> 0.12 us  [gather_over_line(): far_after = lax.ppermute(after, 'dp', [(a + 1, a) for a in range(ndp // 2)])]
    ppermute x1, starting transfers between devices: 6.79 us -> 3.79 us  [move_activations(): grad_in = lax.ppermute(arrived, ('dp', 'row'), swap_back)]
    ppermute x2, starting transfers between devices: 7.96 us -> 5.3 us  [sum_over_line(): from_left = lax.ppermute(far, 'dp', [(a, a + 1) for a in range(ndp // 2)])]
  transfers between devices with their start and end apart: 35 -> 35, of which waited for: 16 -> 16; matrix products, arithmetic and copies ran while one was open for 2% -> 2% of each run, Pallas kernels for 16% -> 19%
where the time goes in v11:
time: 164 us; the launch traced here: 163 us
  starting transfers between devices  60 us (37%)
  waiting for transfers between devices  59.9 us (37%)
  Pallas kernels  31.3 us (19%)
  local copies, waits for them, and re-layouts  8.35 us (5%)
  other arithmetic  2.19 us (1%)
    ppermute x2, waiting for transfers between devices, gather_over_line(): before = lax.ppermute(own, ('dp', 'row'), shift(1))  10.6 us
    ppermute x2, waiting for transfers between devices, gather_over_line(): after = lax.ppermute(own, ('dp', 'row'), shift(-1))  9.89 us
    ppermute x1, waiting for transfers between devices, move_activations(): moved = lax.ppermute(tokens, ('dp', 'row'), swap)  9.2 us
    ppermute x3, waiting for transfers between devices, move_activations(): lax.ppermute(sent, ('row', 'col'), [(b, a) for a, b in offset(*p)])  8.32 us
    pallas_call x2, Pallas kernels, move_activations(): kernel_call(project_body, [shaped((3, chunk, width), BF16)] * ndp, grid=(...  8.12 us
    ppermute x2, waiting for transfers between devices, sum_over_line(): lax.ppermute(right + from_left, 'dp', [(a, (a + 1) % ndp) for a in range(...  7.75 us
    unnamed x59, local copies, waits for them, and re-layouts  7.67 us
    ppermute x3, starting transfers between devices, move_activations(): lax.ppermute(part, 'dp', [(a, (a + ahead) % ndp) for a in range(ndp)])  7.6 us
  transfers between devices with their start and end apart: 35, of which 16 were waited for; matrix products, arithmetic and copies ran while one was open for 2% of the time, Pallas kernels for 19%

profile of v11, /device:TPU:1, one launch (start us, length us, event | category | flops | bytes accessed | tf_op | source)
XLA Modules:
  0.0 162.9 jit_solution(8325891321819709850)
XLA Ops:
  0.6 4.6 %collective-permute-start = (bf16[192,512]{1,0:T(8,128)(2,1)}, bf16[192,512]{1,0:T(8,128)(2,1)S(1)}, u32[]{:S(2)}, u32[]{:S(2)}) collective-permute-start(bf16[192,512]{1,0:T(8,128)(2,1)} %param.5), channel_id=1, source_target_pairs={{0,0},{16,2},{8,4},{24,6},{2,8},{18,10},{10,12},{26,14},{4,16},{20... | collective-permute-start | bytes 589832 | tf_op jit(solution)/shard_map/ppermute | solution.py:367
  6.2 9.2 %collective-permute-done = bf16[192,512]{1,0:T(8,128)(2,1)S(1)} collective-permute-done((bf16[192,512]{1,0:T(8,128)(2,1)}, bf16[192,512]{1,0:T(8,128)(2,1)S(1)}, u32[]{:S(2)}, u32[]{:S(2)}) %collective-permute-start) | collective-permute-done | bytes 196640 | tf_op jit(solution)/shard_map/ppermute | solution.py:367
  15.4 2.7 %collective-permute-start.4 = (bf16[192,512]{1,0:T(8,128)(2,1)S(1)}, bf16[192,512]{1,0:T(8,128)(2,1)S(1)}, u32[]{:S(2)}, u32[]{:S(2)}) collective-permute-start(bf16[192,512]{1,0:T(8,128)(2,1)S(1)} %collective-permute-done), channel_id=1, source_target_pairs={{0,4},{1,5},{2,6},{3,7},{4,0},{5,1},{6,2},{7,3},{8,12},{9,13},{10,... | collective-permute-start | bytes 589832 | tf_op jit(solution)/shard_map/ppermute | solution.py:371
  25.1 4.0 %shard_map.93 = (bf16[3,384,128]{2,1,0:T(8,128)(2,1)S(1)}, bf16[3,384,128]{2,1,0:T(8,128)(2,1)S(1)}, bf16[3,384,128]{2,1,0:T(8,128)(2,1)S(1)}, bf16[3,384,128]{2,1,0:T(8,128)(2,1)S(1)}) custom-call(bf16[2,2,192,512]{3,2,1,0:T(8,128)(2,1)S(1)} %bitcast.20, bf16[3,1024,512]{2,1,0:T(8,128)(2,1)} %bitcast.5.w_ref.refs_4_), custom_call_target="tpu_custom_call" | custom-call | flops 1207959552 | bytes 5111808 | tf_op jit(solution)/shard_map/pallas_call | solution.py:396
  30.8 6.5 %collective-permute-start.6 = (bf16[192,128]{1,0:T(8,128)(2,1)S(1)}, bf16[192,128]{1,0:T(8,128)(2,1)S(1)}, u32[]{:S(2)}, u32[]{:S(2)}) collective-permute-start(bf16[192,128]{1,0:T(8,128)(2,1)S(1)} %get-tuple-element.65), channel_id=1, source_target_pairs={{0,16},{8,24},{16,0},{24,8},{1,17},{9,25},{17,1},{25,9},{2,18},{10... | collective-permute-start | bytes 147464 | tf_op jit(solution)/shard_map/ppermute | solution.py:377
  41.4 4.1 %collective-permute-done.6.refs_11_ = bf16[192,128]{1,0:T(8,128)(2,1)S(1)} collective-permute-done((bf16[192,128]{1,0:T(8,128)(2,1)S(1)}, bf16[192,128]{1,0:T(8,128)(2,1)S(1)}, u32[]{:S(2)}, u32[]{:S(2)}) %collective-permute-start.6) | collective-permute-done | bytes 49184 | tf_op jit(solution)/shard_map/ppermute | solution.py:377
  45.4 4.1 %shard_map.94 = (bf16[3,384,128]{2,1,0:T(8,128)(2,1)S(1)}, bf16[3,384,128]{2,1,0:T(8,128)(2,1)S(1)}, bf16[3,384,128]{2,1,0:T(8,128)(2,1)S(1)}, bf16[3,384,128]{2,1,0:T(8,128)(2,1)S(1)}) custom-call(bf16[2,2,192,512]{3,2,1,0:T(8,128)(2,1)S(1)} %collective-permute-done.7.x_ref.refs_1_, bf16[3,1024,512]{2,1,0:T(8,128)(2,1)} %bitcast.5.w_ref.refs_4_), custom_call_target="tpu_custom_call" | custom-call | flops 1207959552 | bytes 5111808 | tf_op jit(solution)/shard_map/pallas_call | solution.py:396
  50.7 4.0 %collective-permute-start.12 = (bf16[1152,128]{1,0:T(8,128)(2,1)S(1)}, bf16[1152,128]{1,0:T(8,128)(2,1)S(1)}, u32[]{:S(2)}, u32[]{:S(2)}) collective-permute-start(bf16[1152,128]{1,0:T(8,128)(2,1)S(1)} %bitcast.25), channel_id=1, source_target_pairs={{0,8},{8,16},{1,9},{9,17},{2,10},{10,18},{3,11},{11,19},{4,12},{12... | collective-permute-start | bytes 884744 | tf_op jit(solution)/shard_map/ppermute | solution.py:318
  54.8 3.3 %collective-permute-start.15 = (bf16[1152,128]{1,0:T(8,128)(2,1)S(1)}, bf16[1152,128]{1,0:T(8,128)(2,1)S(1)}, u32[]{:S(2)}, u32[]{:S(2)}) collective-permute-start(bf16[1152,128]{1,0:T(8,128)(2,1)S(1)} %bitcast_add_fusion), channel_id=1, source_target_pairs={{0,24},{8,0},{16,8},{24,16},{1,25},{9,1},{17,9},{25,17},{2,26},{10... | collective-permute-start | bytes 884744 | tf_op jit(solution)/shard_map/ppermute | solution.py:321
  58.1 4.6 %collective-permute-done.12 = bf16[1152,128]{1,0:T(8,128)(2,1)S(1)} collective-permute-done((bf16[1152,128]{1,0:T(8,128)(2,1)S(1)}, bf16[1152,128]{1,0:T(8,128)(2,1)S(1)}, u32[]{:S(2)}, u32[]{:S(2)}) %collective-permute-start.12) | collective-permute-done | bytes 294944 | tf_op jit(solution)/shard_map/ppermute | solution.py:318
  70.0 7.7 %collective-permute-done.13.refs_4_ = bf16[1152,128]{1,0:T(8,128)(2,1)S(1)} collective-permute-done((bf16[1152,128]{1,0:T(8,128)(2,1)S(1)}, bf16[1152,128]{1,0:T(8,128)(2,1)S(1)}, u32[]{:S(2)}, u32[]{:S(2)}) %collective-permute-start.13) | collective-permute-done | bytes 294944 | tf_op jit(solution)/shard_map/ppermute | solution.py:320
  78.5 5.4 %shard_map.96 = (bf16[1184,128]{1,0:T(8,128)(2,1)}, bf16[1152,128]{1,0:T(8,128)(2,1)}, bf16[192,128]{1,0:T(8,128)(2,1)}, bf16[192,128]{1,0:T(8,128)(2,1)}, bf16[...) custom-call(bf16[1152,128]{1,0:T(8,128)(2,1)} %bitcast.26, bf16[1152,128]{1,0:T(8,128)(2,1)} %copy-done.17, ...), custom_call_target="tpu_custom_call" | custom-call | flops 1207959552 | bytes 2752512 | tf_op jit(solution)/shard_map/pallas_call | solution.py:415
  83.9 3.4 %collective-permute-start.20 = (bf16[1152,128]{1,0:T(8,128)(2,1)}, bf16[1152,128]{1,0:T(8,128)(2,1)S(1)}, u32[]{:S(2)}, u32[]{:S(2)}) collective-permute-start(bf16[1152,128]{1,0:T(8,128)(2,1)} %get-tuple-element.80), channel_id=1, source_target_pairs={{0,26},{2,24},{4,30},{6,28},{8,2},{10,0},{12,6},{14,4},{16,10},{18... | collective-permute-start | bytes 884744 | tf_op jit(solution)/shard_map/ppermute | solution.py:336
  89.0 5.4 %collective-permute-done.20.far_after = bf16[1152,128]{1,0:T(8,128)(2,1)S(1)} collective-permute-done((bf16[1152,128]{1,0:T(8,128)(2,1)}, bf16[1152,128]{1,0:T(8,128)(2,1)S(1)}, u32[]{:S(2)}, u32[]{:S(2)}) %collective-permute-start.20) | collective-permute-done | bytes 294944 | tf_op jit(solution)/shard_map/ppermute | solution.py:336
  96.3 4.5 %collective-permute-done.17.near_after.refs_4_ = bf16[1184,128]{1,0:T(8,128)(2,1)S(1)} collective-permute-done((bf16[1184,128]{1,0:T(8,128)(2,1)}, bf16[1184,128]{1,0:T(8,128)(2,1)S(1)}, u32[]{:S(2)}, u32[]{:S(2)}) %collective-permute-start.17) | collective-permute-done | bytes 303136 | tf_op jit(solution)/shard_map/ppermute | solution.py:336
  102.2 7.5 %collective-permute-done.16.near_before.refs_3_ = bf16[1184,128]{1,0:T(8,128)(2,1)S(1)} collective-permute-done((bf16[1184,128]{1,0:T(8,128)(2,1)}, bf16[1184,128]{1,0:T(8,128)(2,1)S(1)}, u32[]{:S(2)}, u32[]{:S(2)}) %collective-permute-start.16) | collective-permute-done | bytes 303136 | tf_op jit(solution)/shard_map/ppermute | solution.py:335
  110.4 3.1 %collective-permute-done.19.far_before = bf16[1152,128]{1,0:T(8,128)(2,1)S(1)} collective-permute-done((bf16[1152,128]{1,0:T(8,128)(2,1)}, bf16[1152,128]{1,0:T(8,128)(2,1)S(1)}, u32[]{:S(2)}, u32[]{:S(2)}) %collective-permute-start.19) | collective-permute-done | bytes 294944 | tf_op jit(solution)/shard_map/ppermute | solution.py:335
  115.4 5.2 %collective-permute-start.29 = (bf16[192,128]{1,0:T(8,128)(2,1)}, bf16[192,128]{1,0:T(8,128)(2,1)S(1)}, u32[]{:S(2)}, u32[]{:S(2)}) collective-permute-start(bf16[192,128]{1,0:T(8,128)(2,1)} %get-tuple-element.89), channel_id=1, source_target_pairs={{0,8},{8,16},{16,24},{24,0},{1,9},{9,17},{17,25},{25,1},{2,10},{10... | collective-permute-start | bytes 147464 | tf_op jit(solution)/shard_map/ppermute | solution.py:435
  121.6 5.5 %shard_map.97 = (f32[2,384,512]{2,1,0:T(8,128)S(1)}, bf16[3,1152,128]{2,1,0:T(8,128)(2,1)S(1)}) custom-call(bf16[1184,128]{1,0:T(8,128)(2,1)S(1)} %copy-done.6, bf16[1184,128]{1,0:T(8,128)(2,1)S(1)} %collective-permute-done.16.near_before.refs_3_, bf16[1184,128]{1,0:T(8,128)(2,1)S(1)} %collective-permute-done.17.near_after.refs_4_, ...), custom_call_target="tpu_custom_call" | custom-call | flops 2415919104 | bytes 10223616 | tf_op jit(solution)/shard_map/pallas_call | solution.py:442
  131.7 4.5 %shard_map.98 = (bf16[1184,128]{1,0:T(8,128)(2,1)}, bf16[1152,128]{1,0:T(8,128)(2,1)}, bf16[192,512]{1,0:T(8,128)(2,1)}, bf16[192,512]{1,0:T(8,128)(2,1)}, bf16[...) custom-call(f32[2,384,512]{2,1,0:T(8,128)} %copy-done.1, bf16[1184,128]{1,0:T(8,128)(2,1)} %copy-done.13, ...), custom_call_target="tpu_custom_call" | custom-call | flops 603979776 | bytes 2555904 | tf_op jit(solution)/shard_map/pallas_call | solution.py:451
  141.9 3.2 %collective-permute-done.26 = bf16[192,512]{1,0:T(8,128)(2,1)S(1)} collective-permute-done((bf16[192,512]{1,0:T(8,128)(2,1)}, bf16[192,512]{1,0:T(8,128)(2,1)S(1)}, u32[]{:S(2)}, u32[]{:S(2)}) %collective-permute-start.26) | collective-permute-done | bytes 196640 | tf_op jit(solution)/shard_map/ppermute | solution.py:470
  146.0 4.2 %collective-permute-done.28 = bf16[192,512]{1,0:T(8,128)(2,1)S(1)} collective-permute-done((bf16[192,512]{1,0:T(8,128)(2,1)}, bf16[192,512]{1,0:T(8,128)(2,1)S(1)}, u32[]{:S(2)}, u32[]{:S(2)}) %collective-permute-start.28) | collective-permute-done | bytes 196640 | tf_op jit(solution)/shard_map/ppermute | solution.py:470
  151.3 3.8 %collective-permute-start.34 = (bf16[192,512]{1,0:T(8,128)(2,1)S(1)}, bf16[192,512]{1,0:T(8,128)(2,1)S(1)}, u32[]{:S(2)}, u32[]{:S(2)}) collective-permute-start(bf16[192,512]{1,0:T(8,128)(2,1)S(1)} %add_convert_fusion), channel_id=1, source_target_pairs={{0,0},{2,16},{4,8},{6,24},{8,2},{10,18},{12,10},{14,26},{16,4},{18... | collective-permute-start | bytes 589832 | tf_op jit(solution)/shard_map/ppermute | solution.py:475
  155.1 7.1 %shard_map.99 = (f32[3,1024,512]{2,1,0:T(8,128)}, bf16[192,512]{1,0:T(8,128)(2,1)}, f32[32,128]{1,0:T(8,128)}, f32[3,3,512]{2,1,0:T(4,128)}) custom-call(bf16[2,2,192,512]{3,2,1,0:T(8,128)(2,1)} %bitcast.21, bf16[2,2,192,512]{3,2,1,0:T(8,128)(2,1)} %copy-done.5, bf16[1184,128]{1,0:T(8,128)(2,1)} %get-tuple-element.79.near.refs_2_, ...), custom_call_target="tpu_custom_call" | custom-call | flops 2415919104 | bytes 10223616 | tf_op jit(solution)/shard_map/pallas_call | solution.py:477
  (126 shorter events, 44.2 us)
Async XLA Ops:
  0.6 14.8 %collective-permute-start = (bf16[192,512]{1,0:T(8,128)(2,1)}, bf16[192,512]{1,0:T(8,128)(2,1)S(1)}, u32[]{:S(2)}, u32[]{:S(2)}) collective-permute-start(bf16[192,512]{1,0:T(8,128)(2,1)} %param.5), channel_id=1, source_target_pairs={{0,0},{16,2},{8,4},{24,6},{2,8},{18,10},{10,12},{26,14},{4,16},{20... | collective-permute-start | bytes 589832 | tf_op jit(solution)/shard_map/ppermute | solution.py:367
  25.0 20.5 %collective-permute-start.7 = (bf16[2,2,192,512]{3,2,1,0:T(8,128)(2,1)S(1)}, bf16[2,2,192,512]{3,2,1,0:T(8,128)(2,1)S(1)}, u32[]{:S(2)}, u32[]{:S(2)}) collective-permute-start(bf16[2,2,192,512]{3,2,1,0:T(8,128)(2,1)S(1)} %bitcast.19), channel_id=1, source_target_pairs={{0,2},{2,0},{4,6},{6,4},{1,3},{3,1},{5,7},{7,5},{8,10},{10,8},{12,... | collective-permute-start | bytes 2359304 | tf_op jit(solution)/shard_map/ppermute | solution.py:376
  30.5 85.0 %collective-permute-start.21 = (bf16[3,1024,512]{2,1,0:T(8,128)(2,1)}, bf16[3,1024,512]{2,1,0:T(8,128)(2,1)}, u32[]{:S(2)}, u32[]{:S(2)}) collective-permute-start(bf16[3,1024,512]{2,1,0:T(8,128)(2,1)} %bitcast.5.w_ref.refs_4_), channel_id=1, source_target_pairs={{0,2},{2,0},{4,6},{6,4},{1,3},{3,1},{5,7},{7,5},{8,10},{10,8},{12,... | collective-permute-start | bytes 9437192 | tf_op jit(solution)/shard_map/ppermute | solution.py:441
  30.8 14.6 %collective-permute-start.6 = (bf16[192,128]{1,0:T(8,128)(2,1)S(1)}, bf16[192,128]{1,0:T(8,128)(2,1)S(1)}, u32[]{:S(2)}, u32[]{:S(2)}) collective-permute-start(bf16[192,128]{1,0:T(8,128)(2,1)S(1)} %get-tuple-element.65), channel_id=1, source_target_pairs={{0,16},{8,24},{16,0},{24,8},{1,17},{9,25},{17,1},{25,9},{2,18},{10... | collective-permute-start | bytes 147464 | tf_op jit(solution)/shard_map/ppermute | solution.py:377
  37.3 13.0 %collective-permute-start.8 = (bf16[1152,128]{1,0:T(8,128)(2,1)S(1)}, bf16[1152,128]{1,0:T(8,128)(2,1)S(1)}, u32[]{:S(2)}, u32[]{:S(2)}) collective-permute-start(bf16[1152,128]{1,0:T(8,128)(2,1)S(1)} %bitcast.23), channel_id=1, source_target_pairs={{0,8},{8,16},{1,9},{9,17},{2,10},{10,18},{3,11},{11,19},{4,12},{12... | collective-permute-start | bytes 884744 | tf_op jit(solution)/shard_map/ppermute | solution.py:318
  38.7 29.5 %collective-permute-start.11 = (bf16[1152,128]{1,0:T(8,128)(2,1)S(1)}, bf16[1152,128]{1,0:T(8,128)(2,1)}, u32[]{:S(2)}, u32[]{:S(2)}) collective-permute-start(bf16[1152,128]{1,0:T(8,128)(2,1)S(1)} %bitcast_add_fusion.2), channel_id=1, source_target_pairs={{0,24},{8,0},{16,8},{24,16},{1,25},{9,1},{17,9},{25,17},{2,26},{10... | collective-permute-start | bytes 884744 | tf_op jit(solution)/shard_map/ppermute | solution.py:321
  50.4 17.8 %collective-permute-start.9 = (bf16[1152,128]{1,0:T(8,128)(2,1)S(1)}, bf16[1152,128]{1,0:T(8,128)(2,1)S(1)}, u32[]{:S(2)}, u32[]{:S(2)}) collective-permute-start(bf16[1152,128]{1,0:T(8,128)(2,1)S(1)} %bitcast_add_fusion.3), channel_id=1, source_target_pairs={{0,8},{8,16},{16,24},{24,0},{1,9},{9,17},{17,25},{25,1},{2,10},{10... | collective-permute-start | bytes 884744 | tf_op jit(solution)/shard_map/ppermute | solution.py:320
  50.7 12.0 %collective-permute-start.12 = (bf16[1152,128]{1,0:T(8,128)(2,1)S(1)}, bf16[1152,128]{1,0:T(8,128)(2,1)S(1)}, u32[]{:S(2)}, u32[]{:S(2)}) collective-permute-start(bf16[1152,128]{1,0:T(8,128)(2,1)S(1)} %bitcast.25), channel_id=1, source_target_pairs={{0,8},{8,16},{1,9},{9,17},{2,10},{10,18},{3,11},{11,19},{4,12},{12... | collective-permute-start | bytes 884744 | tf_op jit(solution)/shard_map/ppermute | solution.py:318
  54.8 15.2 %collective-permute-start.15 = (bf16[1152,128]{1,0:T(8,128)(2,1)S(1)}, bf16[1152,128]{1,0:T(8,128)(2,1)S(1)}, u32[]{:S(2)}, u32[]{:S(2)}) collective-permute-start(bf16[1152,128]{1,0:T(8,128)(2,1)S(1)} %bitcast_add_fusion), channel_id=1, source_target_pairs={{0,24},{8,0},{16,8},{24,16},{1,25},{9,1},{17,9},{25,17},{2,26},{10... | collective-permute-start | bytes 884744 | tf_op jit(solution)/shard_map/ppermute | solution.py:321
  62.8 14.9 %collective-permute-start.13 = (bf16[1152,128]{1,0:T(8,128)(2,1)S(1)}, bf16[1152,128]{1,0:T(8,128)(2,1)S(1)}, u32[]{:S(2)}, u32[]{:S(2)}) collective-permute-start(bf16[1152,128]{1,0:T(8,128)(2,1)S(1)} %bitcast_add_fusion.1), channel_id=1, source_target_pairs={{0,8},{8,16},{16,24},{24,0},{1,9},{9,17},{17,25},{25,1},{2,10},{10... | collective-permute-start | bytes 884744 | tf_op jit(solution)/shard_map/ppermute | solution.py:320
  83.9 10.4 %collective-permute-start.20 = (bf16[1152,128]{1,0:T(8,128)(2,1)}, bf16[1152,128]{1,0:T(8,128)(2,1)S(1)}, u32[]{:S(2)}, u32[]{:S(2)}) collective-permute-start(bf16[1152,128]{1,0:T(8,128)(2,1)} %get-tuple-element.80), channel_id=1, source_target_pairs={{0,26},{2,24},{4,30},{6,28},{8,2},{10,0},{12,6},{14,4},{16,10},{18... | collective-permute-start | bytes 884744 | tf_op jit(solution)/shard_map/ppermute | solution.py:336
  87.3 13.6 %collective-permute-start.17 = (bf16[1184,128]{1,0:T(8,128)(2,1)}, bf16[1184,128]{1,0:T(8,128)(2,1)S(1)}, u32[]{:S(2)}, u32[]{:S(2)}) collective-permute-start(bf16[1184,128]{1,0:T(8,128)(2,1)} %get-tuple-element.79.near.refs_2_), channel_id=1, source_target_pairs={{0,24},{2,26},{4,28},{6,30},{8,0},{10,2},{12,4},{14,6},{16,8},{18,... | collective-permute-start | bytes 909320 | tf_op jit(solution)/shard_map/ppermute | solution.py:336
  89.0 20.7 %collective-permute-start.16 = (bf16[1184,128]{1,0:T(8,128)(2,1)}, bf16[1184,128]{1,0:T(8,128)(2,1)S(1)}, u32[]{:S(2)}, u32[]{:S(2)}) collective-permute-start(bf16[1184,128]{1,0:T(8,128)(2,1)} %get-tuple-element.79.near.refs_2_), channel_id=1, source_target_pairs={{0,8},{2,10},{4,12},{6,14},{8,16},{10,18},{12,20},{14,22},{16,24},... | collective-permute-start | bytes 909320 | tf_op jit(solution)/shard_map/ppermute | solution.py:335
  89.0 24.4 %collective-permute-start.19 = (bf16[1152,128]{1,0:T(8,128)(2,1)}, bf16[1152,128]{1,0:T(8,128)(2,1)S(1)}, u32[]{:S(2)}, u32[]{:S(2)}) collective-permute-start(bf16[1152,128]{1,0:T(8,128)(2,1)} %get-tuple-element.80), channel_id=1, source_target_pairs={{0,10},{2,8},{4,14},{6,12},{8,18},{10,16},{12,22},{14,20},{16,26},... | collective-permute-start | bytes 884744 | tf_op jit(solution)/shard_map/ppermute | solution.py:335
  94.4 20.3 %collective-permute-start.18 = (bf16[1152,128]{1,0:T(8,128)(2,1)}, bf16[1152,128]{1,0:T(8,128)(2,1)S(1)}, u32[]{:S(2)}, u32[]{:S(2)}) collective-permute-start(bf16[1152,128]{1,0:T(8,128)(2,1)} %get-tuple-element.80), channel_id=1, source_target_pairs={{0,2},{2,0},{4,6},{6,4},{8,10},{10,8},{12,14},{14,12},{16,18},{18,... | collective-permute-start | bytes 884744 | tf_op jit(solution)/shard_map/ppermute | solution.py:337
  100.9 30.0 %collective-permute-start.23 = (bf16[1184,128]{1,0:T(8,128)(2,1)S(1)}, bf16[1184,128]{1,0:T(8,128)(2,1)S(1)}, u32[]{:S(2)}, u32[]{:S(2)}) collective-permute-start(bf16[1184,128]{1,0:T(8,128)(2,1)S(1)} %collective-permute-done.17.near_after.refs_4_), channel_id=1, source_target_pairs={{8,0},{16,8},{9,1},{17,9},{10,2},{18,10},{11,3},{19,11},{12,4},{20... | collective-permute-start | bytes 909320 | tf_op jit(solution)/shard_map/ppermute | solution.py:339
  109.7 21.2 %collective-permute-start.22 = (bf16[1184,128]{1,0:T(8,128)(2,1)S(1)}, bf16[1184,128]{1,0:T(8,128)(2,1)S(1)}, u32[]{:S(2)}, u32[]{:S(2)}) collective-permute-start(bf16[1184,128]{1,0:T(8,128)(2,1)S(1)} %collective-permute-done.16.near_before.refs_3_), channel_id=1, source_target_pairs={{8,16},{16,24},{9,17},{17,25},{10,18},{18,26},{11,19},{19,27},{12,... | collective-permute-start | bytes 909320 | tf_op jit(solution)/shard_map/ppermute | solution.py:338
  113.4 15.0 %collective-permute-start.25 = (bf16[1152,128]{1,0:T(8,128)(2,1)S(1)}, bf16[1152,128]{1,0:T(8,128)(2,1)S(1)}, u32[]{:S(2)}, u32[]{:S(2)}) collective-permute-start(bf16[1152,128]{1,0:T(8,128)(2,1)S(1)} %collective-permute-done.20.far_after), channel_id=1, source_target_pairs={{8,0},{16,8},{9,1},{17,9},{10,2},{18,10},{11,3},{19,11},{12,4},{20... | collective-permute-start | bytes 884744 | tf_op jit(solution)/shard_map/ppermute | solution.py:339
  114.7 13.7 %collective-permute-start.24 = (bf16[1152,128]{1,0:T(8,128)(2,1)S(1)}, bf16[1152,128]{1,0:T(8,128)(2,1)S(1)}, u32[]{:S(2)}, u32[]{:S(2)}) collective-permute-start(bf16[1152,128]{1,0:T(8,128)(2,1)S(1)} %collective-permute-done.19.far_before), channel_id=1, source_target_pairs={{8,16},{16,24},{9,17},{17,25},{10,18},{18,26},{11,19},{19,27},{12,... | collective-permute-start | bytes 884744 | tf_op jit(solution)/shard_map/ppermute | solution.py:338
  115.4 20.8 %collective-permute-start.29 = (bf16[192,128]{1,0:T(8,128)(2,1)}, bf16[192,128]{1,0:T(8,128)(2,1)S(1)}, u32[]{:S(2)}, u32[]{:S(2)}) collective-permute-start(bf16[192,128]{1,0:T(8,128)(2,1)} %get-tuple-element.89), channel_id=1, source_target_pairs={{0,8},{8,16},{16,24},{24,0},{1,9},{9,17},{17,25},{25,1},{2,10},{10... | collective-permute-start | bytes 147464 | tf_op jit(solution)/shard_map/ppermute | solution.py:435
  137.0 14.4 %collective-permute-start.32 = (bf16[3,1152,128]{2,1,0:T(8,128)(2,1)S(1)}, bf16[3,1152,128]{2,1,0:T(8,128)(2,1)S(1)}, u32[]{:S(2)}, u32[]{:S(2)}) collective-permute-start(bf16[3,1152,128]{2,1,0:T(8,128)(2,1)S(1)} %get-tuple-element.92), channel_id=1, source_target_pairs={{0,2},{2,0},{4,6},{6,4},{1,3},{3,1},{5,7},{7,5},{8,10},{10,8},{12,... | collective-permute-start | bytes 2654216 | tf_op jit(solution)/shard_map/ppermute | solution.py:468
  140.4 9.9 %collective-permute-start.28 = (bf16[192,512]{1,0:T(8,128)(2,1)}, bf16[192,512]{1,0:T(8,128)(2,1)S(1)}, u32[]{:S(2)}, u32[]{:S(2)}) collective-permute-start(bf16[192,512]{1,0:T(8,128)(2,1)} %get-tuple-element.86), channel_id=1, source_target_pairs={{5,0},{4,1},{7,2},{6,3},{1,4},{0,5},{3,6},{2,7},{13,8},{12,9},{15,... | collective-permute-start | bytes 589832 | tf_op jit(solution)/shard_map/ppermute | solution.py:470
  141.1 10.2 %collective-permute-start.33 = (bf16[1152,128]{1,0:T(8,128)(2,1)}, bf16[1152,128]{1,0:T(8,128)(2,1)S(1)}, u32[]{:S(2)}, u32[]{:S(2)}) collective-permute-start(bf16[1152,128]{1,0:T(8,128)(2,1)} %get-tuple-element.93), channel_id=1, source_target_pairs={{0,2},{2,0},{4,6},{6,4},{1,3},{3,1},{5,7},{7,5},{8,10},{10,8},{12,... | collective-permute-start | bytes 884744 | tf_op jit(solution)/shard_map/ppermute | solution.py:468
  151.3 10.9 %collective-permute-start.34 = (bf16[192,512]{1,0:T(8,128)(2,1)S(1)}, bf16[192,512]{1,0:T(8,128)(2,1)S(1)}, u32[]{:S(2)}, u32[]{:S(2)}) collective-permute-start(bf16[192,512]{1,0:T(8,128)(2,1)S(1)} %add_convert_fusion), channel_id=1, source_target_pairs={{0,0},{2,16},{4,8},{6,24},{8,2},{10,18},{12,10},{14,26},{16,4},{18... | collective-permute-start | bytes 589832 | tf_op jit(solution)/shard_map/ppermute | solution.py:475
  (40 other events, 368.4 us)

commit v12 on v11

--- a/solution.py
+++ b/solution.py
@@ -313,13 +313,19 @@
     near_ref[3 * tokens // 2 :] = small.astype(BF16)
 
 
-def sum_over_line(own, right, far, left):
+def first_hop(far):
     ndp = lax.axis_size("dp")
-    from_left = lax.ppermute(far, "dp", [(a, a + 1) for a in range(ndp // 2)])
-    from_right = lax.ppermute(far, "dp", [(a, a - 1) for a in range(ndp // 2, ndp)])
+    return (
+        lax.ppermute(far, "dp", [(a, a + 1) for a in range(ndp // 2)]),
+        lax.ppermute(far, "dp", [(a, a - 1) for a in range(ndp // 2, ndp)]),
+    )
+
+
+def second_hop(right, left, from_left, from_right):
+    ndp = lax.axis_size("dp")
     rightward = lax.ppermute(right + from_left, "dp", [(a, (a + 1) % ndp) for a in range(ndp)])
     leftward = lax.ppermute(left + from_right, "dp", [(a, (a - 1) % ndp) for a in range(ndp)])
-    return own, rightward, leftward
+    return rightward, leftward
 
 
 def gather_over_line(own, across):
@@ -367,15 +373,14 @@
     moved = lax.ppermute(tokens, ("dp", "row"), swap)
     turn = [[(a, (a + ahead) % ndp) for a in range(ndp)] for ahead in range(ndp)]
     upstream = [*kernel_call(split_body, [shaped((rows, width), BF16)] * ndp)(grad_out)]
+    upstream[1] = lax.ppermute(upstream[1], "dp", turn[1])
     moved, upstream = lax.optimization_barrier((moved, upstream))
     near = [moved] + [lax.ppermute(moved, ("row", "col"), offset(*p)) for p in places[1:]]
-    for ahead in (1, 3):
-        upstream[ahead] = lax.ppermute(upstream[ahead], "dp", turn[ahead])
-    upstream[1::2], near[1:] = lax.optimization_barrier((upstream[1::2], near[1:]))
+    upstream[3] = lax.ppermute(upstream[3], "dp", turn[3])
+    partner_w = lax.ppermute(w, "row", partner)
+    upstream[3], near[1:], partner_w = lax.optimization_barrier((upstream[3], near[1:], partner_w))
     x0 = jnp.stack(near).reshape(nblocks, ncol, rows, dcol)
     x1 = lax.ppermute(x0, "row", partner)
-    upstream[2] = lax.ppermute(upstream[2], "dp", turn[2])
-    upstream[2], x1 = lax.optimization_barrier((upstream[2], x1))
 
     sf = lax.dynamic_slice_in_dim(short_filter, z * width, width, 2).reshape(3 * nshort, width)
     lf = lax.dynamic_slice_in_dim(long_filter, z * groups, groups, 0).astype(F32)
@@ -406,7 +411,11 @@
             flops=mm_flops,
             nbytes=mm_bytes,
         )(x, w)
-        sums += sum_over_line(*(p.reshape(3 * chunk, width) for p in parts))
+        own, right, far, left = (p.reshape(3 * chunk, width) for p in parts)
+        passed = first_hop(far)
+        sums += [own, *second_hop(right, left, *passed)]
+    passed, upstream[2] = lax.optimization_barrier((passed, upstream[2]))
+    upstream[2] = lax.ppermute(upstream[2], "dp", turn[2])
 
     extra = -(-(groups + 3 * nshort) // 16) * 16
     half = pl.BlockSpec((groups, ntaps, 2 * ntaps), lambda i: (0, 0, 0))
@@ -431,14 +440,8 @@
         nbytes=2 * width * seq * 14,
         vmem=MOST_VMEM_BYTES,
     )(*sums, sf, bands, bands, *upstream)
-    mixed = [mixed[0]] + [
-        lax.ppermute(part, "dp", [(a, (a + ahead) % ndp) for a in range(ndp)])
-        for ahead, part in enumerate(mixed)
-        if ahead
-    ]
     *near, near_far_before, near_far_after = gather_over_line(grad_near, False)
     *far, far_far_before, far_far_after = gather_over_line(grad_other, True)
-    partner_w = lax.ppermute(w, "row", partner)
     part, far_three = kernel_call(
         first_grad_body,
         [shaped((ncol, chunk, dcol), F32), shaped((3, 3 * chunk, width), BF16)],
@@ -446,6 +449,9 @@
         flops=2 * mm_flops,
         nbytes=2 * mm_bytes,
     )(*near, *far, w, partner_w)
+    part, mixed = lax.optimization_barrier((part, mixed))
+    for ahead in range(1, ndp):
+        mixed[ahead] = lax.ppermute(mixed[ahead], "dp", turn[ahead])
     everywhere = pl.BlockSpec(memory_space=pl.ANY)
     in_vmem = pl.BlockSpec(memory_space=pltpu.VMEM)
     near_last, far_last, *blocks = kernel_call(

time: 164 us -> 168 us (1.024)
  local copies, waits for them, and re-layouts: 8.35 us -> 13.7 us
  Pallas kernels: 31.3 us -> 27.4 us
  waiting for transfers between devices: 59.9 us -> 63.2 us
    ppermute x2, waiting for transfers between devices: 9.89 us -> 19.8 us  [gather_over_line(): after = lax.ppermute(own, ('dp', 'row'), shift(-1))]
    ppermute x2, waiting for transfers between devices: 10.6 us -> 1.07 us  [gather_over_line(): before = lax.ppermute(own, ('dp', 'row'), shift(1))]
    ppermute x1, waiting for transfers between devices: 4.07 us -> 11.6 us  [move_activations(): upstream[2] = lax.ppermute(upstream[2], 'dp', turn[2])]
    ppermute x1, waiting for transfers between devices: 9.2 us -> 2.4 us  [move_activations(): moved = lax.ppermute(tokens, ('dp', 'row'), swap)]
    unnamed x59 -> x63, local copies, waits for them, and re-layouts: 7.67 us -> 13 us
    ppermute x1, starting transfers between devices: 6.46 us -> 1.18 us  [move_activations(): upstream[2] = lax.ppermute(upstream[2], 'dp', turn[2])]
    ppermute x13, starting transfers between devices: 26.1 us -> 31.2 us  [the longest x2 12.7 us: second_hop(): lax.ppermute(left + from_right, 'dp', [(a, (a - 1) % ndp) for a in range(...]
    pallas_call x2, Pallas kernels: 8.12 us -> 4.13 us  [move_activations(): kernel_call(project_body, [shaped((3, chunk, width), BF16)] * ndp, grid=(...]
  transfers between devices with their start and end apart: 35 -> 35, of which waited for: 16 -> 14; matrix products, arithmetic and copies ran while one was open for 2% -> 2% of each run, Pallas kernels for 19% -> 13%
where the time goes in v12:
time: 168 us; the launch traced here: 167 us
  waiting for transfers between devices  63.2 us (38%)
  starting transfers between devices  59.8 us (36%)
  Pallas kernels  27.4 us (16%)
  local copies, waits for them, and re-layouts  13.7 us (8%)
  other arithmetic  2.19 us (1%)
    ppermute x2, waiting for transfers between devices, gather_over_line(): after = lax.ppermute(own, ('dp', 'row'), shift(-1))  19.8 us
    unnamed x63, local copies, waits for them, and re-layouts  13 us
    ppermute x2, starting transfers between devices, second_hop(): lax.ppermute(left + from_right, 'dp', [(a, (a - 1) % ndp) for a in range(...  12.7 us
    ppermute x1, waiting for transfers between devices, move_activations(): upstream[2] = lax.ppermute(upstream[2], 'dp', turn[2])  11.6 us
    ppermute x3, waiting for transfers between devices, move_activations(): lax.ppermute(sent, ('row', 'col'), [(b, a) for a, b in offset(*p)])  8.28 us
    ppermute x2, starting transfers between devices, first_hop(): lax.ppermute(far, 'dp', [(a, a + 1) for a in range(ndp // 2)])  8.01 us
    ppermute x1, waiting for transfers between devices, move_activations(): upstream[1] = lax.ppermute(upstream[1], 'dp', turn[1])  7.21 us
    pallas_call x1, Pallas kernels, move_activations(): kernel_call(functools.partial(weight_grad_body, scale), [shaped((3, drow,...  7.06 us
  transfers between devices with their start and end apart: 35, of which 14 were waited for; matrix products, arithmetic and copies ran while one was open for 2% of the time, Pallas kernels for 13%

profile of v12, /device:TPU:1, one launch (start us, length us, event | category | flops | bytes accessed | tf_op | source)
XLA Modules:
  0.0 167.3 jit_solution(5603370991458344089)
XLA Ops:
  0.8 4.6 %collective-permute-start = (bf16[192,512]{1,0:T(8,128)(2,1)}, bf16[192,512]{1,0:T(8,128)(2,1)S(1)}, u32[]{:S(2)}, u32[]{:S(2)}) collective-permute-start(bf16[192,512]{1,0:T(8,128)(2,1)} %param.5), channel_id=1, source_target_pairs={{0,0},{16,2},{8,4},{24,6},{2,8},{18,10},{10,12},{26,14},{4,16},{20... | collective-permute-start | bytes 589832 | tf_op jit(solution)/shard_map/ppermute | solution.py:373
  7.6 7.2 %collective-permute-done.1.refs_10_ = bf16[192,128]{1,0:T(8,128)(2,1)S(1)} collective-permute-done((bf16[192,128]{1,0:T(8,128)(2,1)S(1)}, bf16[192,128]{1,0:T(8,128)(2,1)S(1)}, u32[]{:S(2)}, u32[]{:S(2)}) %collective-permute-start.1) | collective-permute-done | bytes 49184 | tf_op jit(solution)/shard_map/ppermute | solution.py:376
  14.8 2.4 %collective-permute-done = bf16[192,512]{1,0:T(8,128)(2,1)S(1)} collective-permute-done((bf16[192,512]{1,0:T(8,128)(2,1)}, bf16[192,512]{1,0:T(8,128)(2,1)S(1)}, u32[]{:S(2)}, u32[]{:S(2)}) %collective-permute-start) | collective-permute-done | bytes 196640 | tf_op jit(solution)/shard_map/ppermute | solution.py:373
  17.2 2.4 %collective-permute-start.4 = (bf16[192,512]{1,0:T(8,128)(2,1)S(1)}, bf16[192,512]{1,0:T(8,128)(2,1)S(1)}, u32[]{:S(2)}, u32[]{:S(2)}) collective-permute-start(bf16[192,512]{1,0:T(8,128)(2,1)S(1)} %collective-permute-done), channel_id=1, source_target_pairs={{0,4},{1,5},{2,6},{3,7},{4,0},{5,1},{6,2},{7,3},{8,12},{9,13},{10,... | collective-permute-start | bytes 589832 | tf_op jit(solution)/shard_map/ppermute | solution.py:378
  19.9 3.5 %collective-permute-done.2.refs_12_ = bf16[192,128]{1,0:T(8,128)(2,1)S(1)} collective-permute-done((bf16[192,128]{1,0:T(8,128)(2,1)S(1)}, bf16[192,128]{1,0:T(8,128)(2,1)S(1)}, u32[]{:S(2)}, u32[]{:S(2)}) %collective-permute-start.2) | collective-permute-done | bytes 49184 | tf_op jit(solution)/shard_map/ppermute | solution.py:379
  24.8 3.3 %collective-permute-done.4 = bf16[192,512]{1,0:T(8,128)(2,1)S(1)} collective-permute-done((bf16[192,512]{1,0:T(8,128)(2,1)S(1)}, bf16[192,512]{1,0:T(8,128)(2,1)S(1)}, u32[]{:S(2)}, u32[]{:S(2)}) %collective-permute-start.4) | collective-permute-done | bytes 196640 | tf_op jit(solution)/shard_map/ppermute | solution.py:378
  35.5 4.0 %collective-permute-start.8 = (bf16[1152,128]{1,0:T(8,128)(2,1)S(1)}, bf16[1152,128]{1,0:T(8,128)(2,1)S(1)}, u32[]{:S(2)}, u32[]{:S(2)}) collective-permute-start(bf16[1152,128]{1,0:T(8,128)(2,1)S(1)} %bitcast.28), channel_id=1, source_target_pairs={{0,8},{8,16},{1,9},{9,17},{2,10},{10,18},{3,11},{11,19},{4,12},{12... | collective-permute-start | bytes 884744 | tf_op jit(solution)/shard_map/ppermute | solution.py:319
  39.6 8.0 %collective-permute-start.11 = (bf16[1152,128]{1,0:T(8,128)(2,1)S(1)}, bf16[1152,128]{1,0:T(8,128)(2,1)}, u32[]{:S(2)}, u32[]{:S(2)}) collective-permute-start(bf16[1152,128]{1,0:T(8,128)(2,1)S(1)} %bitcast_add_fusion.2), channel_id=1, source_target_pairs={{0,24},{8,0},{16,8},{24,16},{1,25},{9,1},{17,9},{25,17},{2,26},{10... | collective-permute-start | bytes 884744 | tf_op jit(solution)/shard_map/ppermute | solution.py:327
  53.1 4.0 %collective-permute-start.12 = (bf16[1152,128]{1,0:T(8,128)(2,1)S(1)}, bf16[1152,128]{1,0:T(8,128)(2,1)S(1)}, u32[]{:S(2)}, u32[]{:S(2)}) collective-permute-start(bf16[1152,128]{1,0:T(8,128)(2,1)S(1)} %bitcast.30), channel_id=1, source_target_pairs={{0,8},{8,16},{1,9},{9,17},{2,10},{10,18},{3,11},{11,19},{4,12},{12... | collective-permute-start | bytes 884744 | tf_op jit(solution)/shard_map/ppermute | solution.py:319
  57.2 4.7 %collective-permute-start.15 = (bf16[1152,128]{1,0:T(8,128)(2,1)S(1)}, bf16[1152,128]{1,0:T(8,128)(2,1)S(1)}, u32[]{:S(2)}, u32[]{:S(2)}) collective-permute-start(bf16[1152,128]{1,0:T(8,128)(2,1)S(1)} %bitcast_add_fusion), channel_id=1, source_target_pairs={{0,24},{8,0},{16,8},{24,16},{1,25},{9,1},{17,9},{25,17},{2,26},{10... | collective-permute-start | bytes 884744 | tf_op jit(solution)/shard_map/ppermute | solution.py:327
  61.9 4.4 %collective-permute-done.12 = bf16[1152,128]{1,0:T(8,128)(2,1)S(1)} collective-permute-done((bf16[1152,128]{1,0:T(8,128)(2,1)S(1)}, bf16[1152,128]{1,0:T(8,128)(2,1)S(1)}, u32[]{:S(2)}, u32[]{:S(2)}) %collective-permute-start.12) | collective-permute-done | bytes 294944 | tf_op jit(solution)/shard_map/ppermute | solution.py:319
  66.4 2.3 %collective-permute-start.13 = (bf16[1152,128]{1,0:T(8,128)(2,1)S(1)}, bf16[1152,128]{1,0:T(8,128)(2,1)S(1)}, u32[]{:S(2)}, u32[]{:S(2)}) collective-permute-start(bf16[1152,128]{1,0:T(8,128)(2,1)S(1)} %bitcast_add_fusion.1), channel_id=1, source_target_pairs={{0,8},{8,16},{16,24},{24,0},{1,9},{9,17},{17,25},{25,1},{2,10},{10... | collective-permute-start | bytes 884744 | tf_op jit(solution)/shard_map/ppermute | solution.py:326
  72.9 11.6 %collective-permute-done.16.refs_11_ = bf16[192,128]{1,0:T(8,128)(2,1)S(1)} collective-permute-done((bf16[192,128]{1,0:T(8,128)(2,1)S(1)}, bf16[192,128]{1,0:T(8,128)(2,1)S(1)}, u32[]{:S(2)}, u32[]{:S(2)}) %collective-permute-start.16) | collective-permute-done | bytes 49184 | tf_op jit(solution)/shard_map/ppermute | solution.py:418
  85.3 5.4 %shard_map.96 = (bf16[1184,128]{1,0:T(8,128)(2,1)}, bf16[1152,128]{1,0:T(8,128)(2,1)}, bf16[192,128]{1,0:T(8,128)(2,1)}, bf16[192,128]{1,0:T(8,128)(2,1)}, bf16[...) custom-call(bf16[1152,128]{1,0:T(8,128)(2,1)} %bitcast.31, bf16[1152,128]{1,0:T(8,128)(2,1)} %collective-permute-done.9.refs_1_, ...), custom_call_target="tpu_custom_call" | custom-call | flops 1207959552 | bytes 2752512 | tf_op jit(solution)/shard_map/pallas_call | solution.py:424
  92.3 4.3 %collective-permute-start.21 = (bf16[1152,128]{1,0:T(8,128)(2,1)}, bf16[1152,128]{1,0:T(8,128)(2,1)S(1)}, u32[]{:S(2)}, u32[]{:S(2)}) collective-permute-start(bf16[1152,128]{1,0:T(8,128)(2,1)} %get-tuple-element.82), channel_id=1, source_target_pairs={{0,26},{2,24},{4,30},{6,28},{8,2},{10,0},{12,6},{14,4},{16,10},{18... | collective-permute-start | bytes 884744 | tf_op jit(solution)/shard_map/ppermute | solution.py:342
  96.6 4.6 %collective-permute-done.18.near_after.refs_4_ = bf16[1184,128]{1,0:T(8,128)(2,1)S(1)} collective-permute-done((bf16[1184,128]{1,0:T(8,128)(2,1)}, bf16[1184,128]{1,0:T(8,128)(2,1)S(1)}, u32[]{:S(2)}, u32[]{:S(2)}) %collective-permute-start.18) | collective-permute-done | bytes 303136 | tf_op jit(solution)/shard_map/ppermute | solution.py:342
  104.9 15.2 %collective-permute-done.21.far_after = bf16[1152,128]{1,0:T(8,128)(2,1)S(1)} collective-permute-done((bf16[1152,128]{1,0:T(8,128)(2,1)}, bf16[1152,128]{1,0:T(8,128)(2,1)S(1)}, u32[]{:S(2)}, u32[]{:S(2)}) %collective-permute-start.21) | collective-permute-done | bytes 294944 | tf_op jit(solution)/shard_map/ppermute | solution.py:342
  123.1 5.5 %shard_map.97 = (f32[2,384,512]{2,1,0:T(8,128)S(1)}, bf16[3,1152,128]{2,1,0:T(8,128)(2,1)S(1)}) custom-call(bf16[1184,128]{1,0:T(8,128)(2,1)S(1)} %copy-done.8, bf16[1184,128]{1,0:T(8,128)(2,1)S(1)} %collective-permute-done.17.near_before.refs_3_, bf16[1184,128]{1,0:T(8,128)(2,1)S(1)} %collective-permute-done.18.near_after.refs_4_, ...), custom_call_target="tpu_custom_call" | custom-call | flops 2415919104 | bytes 10223616 | tf_op jit(solution)/shard_map/pallas_call | solution.py:445
  129.9 2.7 %collective-permute-start.29 = (bf16[192,128]{1,0:T(8,128)(2,1)S(1)}, bf16[192,128]{1,0:T(8,128)(2,1)S(1)}, u32[]{:S(2)}, u32[]{:S(2)}) collective-permute-start(bf16[192,128]{1,0:T(8,128)(2,1)S(1)} %copy-done.26), channel_id=1, source_target_pairs={{0,8},{8,16},{16,24},{24,0},{1,9},{9,17},{17,25},{25,1},{2,10},{10... | collective-permute-start | bytes 147464 | tf_op jit(solution)/shard_map/ppermute | solution.py:454
  135.5 4.5 %shard_map.98 = (bf16[1184,128]{1,0:T(8,128)(2,1)}, bf16[1152,128]{1,0:T(8,128)(2,1)}, bf16[192,512]{1,0:T(8,128)(2,1)}, bf16[192,512]{1,0:T(8,128)(2,1)}, bf16[...) custom-call(f32[2,384,512]{2,1,0:T(8,128)} %copy-done.3, bf16[1184,128]{1,0:T(8,128)(2,1)} %collective-permute-done.22.refs_0_, ...), custom_call_target="tpu_custom_call" | custom-call | flops 603979776 | bytes 2555904 | tf_op jit(solution)/shard_map/pallas_call | solution.py:457
  146.1 3.2 %collective-permute-done.26 = bf16[192,512]{1,0:T(8,128)(2,1)S(1)} collective-permute-done((bf16[192,512]{1,0:T(8,128)(2,1)}, bf16[192,512]{1,0:T(8,128)(2,1)S(1)}, u32[]{:S(2)}, u32[]{:S(2)}) %collective-permute-start.26) | collective-permute-done | bytes 196640 | tf_op jit(solution)/shard_map/ppermute | solution.py:476
  150.2 4.1 %collective-permute-done.28 = bf16[192,512]{1,0:T(8,128)(2,1)S(1)} collective-permute-done((bf16[192,512]{1,0:T(8,128)(2,1)}, bf16[192,512]{1,0:T(8,128)(2,1)S(1)}, u32[]{:S(2)}, u32[]{:S(2)}) %collective-permute-start.28) | collective-permute-done | bytes 196640 | tf_op jit(solution)/shard_map/ppermute | solution.py:476
  155.4 3.9 %collective-permute-start.34 = (bf16[192,512]{1,0:T(8,128)(2,1)S(1)}, bf16[192,512]{1,0:T(8,128)(2,1)S(1)}, u32[]{:S(2)}, u32[]{:S(2)}) collective-permute-start(bf16[192,512]{1,0:T(8,128)(2,1)S(1)} %add_convert_fusion), channel_id=1, source_target_pairs={{0,0},{2,16},{4,8},{6,24},{8,2},{10,18},{12,10},{14,26},{16,4},{18... | collective-permute-start | bytes 589832 | tf_op jit(solution)/shard_map/ppermute | solution.py:481
  159.4 7.1 %shard_map.99 = (f32[3,1024,512]{2,1,0:T(8,128)}, bf16[192,512]{1,0:T(8,128)(2,1)}, f32[32,128]{1,0:T(8,128)}, f32[3,3,512]{2,1,0:T(4,128)}) custom-call(bf16[2,2,192,512]{3,2,1,0:T(8,128)(2,1)} %bitcast.26, bf16[2,2,192,512]{3,2,1,0:T(8,128)(2,1)} %copy-done.7, bf16[1184,128]{1,0:T(8,128)(2,1)} %get-tuple-element.81.near.refs_2_, ...), custom_call_target="tpu_custom_call" | custom-call | flops 2415919104 | bytes 10223616 | tf_op jit(solution)/shard_map/pallas_call | solution.py:483
  (130 shorter events, 43.4 us)
Async XLA Ops:
  0.6 27.4 %collective-permute-start.6 = (bf16[3,1024,512]{2,1,0:T(8,128)(2,1)}, bf16[3,1024,512]{2,1,0:T(8,128)(2,1)S(1)}, u32[]{:S(2)}, u32[]{:S(2)}) collective-permute-start(bf16[3,1024,512]{2,1,0:T(8,128)(2,1)} %bitcast.19), channel_id=1, source_target_pairs={{0,2},{2,0},{4,6},{6,4},{1,3},{3,1},{5,7},{7,5},{8,10},{10,8},{12,... | collective-permute-start | bytes 9437192 | tf_op jit(solution)/shard_map/ppermute | solution.py:380
  0.8 16.4 %collective-permute-start = (bf16[192,512]{1,0:T(8,128)(2,1)}, bf16[192,512]{1,0:T(8,128)(2,1)S(1)}, u32[]{:S(2)}, u32[]{:S(2)}) collective-permute-start(bf16[192,512]{1,0:T(8,128)(2,1)} %param.5), channel_id=1, source_target_pairs={{0,0},{16,2},{8,4},{24,6},{2,8},{18,10},{10,12},{26,14},{4,16},{20... | collective-permute-start | bytes 589832 | tf_op jit(solution)/shard_map/ppermute | solution.py:373
  17.2 10.8 %collective-permute-start.4 = (bf16[192,512]{1,0:T(8,128)(2,1)S(1)}, bf16[192,512]{1,0:T(8,128)(2,1)S(1)}, u32[]{:S(2)}, u32[]{:S(2)}) collective-permute-start(bf16[192,512]{1,0:T(8,128)(2,1)S(1)} %collective-permute-done), channel_id=1, source_target_pairs={{0,4},{1,5},{2,6},{3,7},{4,0},{5,1},{6,2},{7,3},{8,12},{9,13},{10,... | collective-permute-start | bytes 589832 | tf_op jit(solution)/shard_map/ppermute | solution.py:378
  29.7 17.8 %collective-permute-start.7 = (bf16[2,2,192,512]{3,2,1,0:T(8,128)(2,1)S(1)}, bf16[2,2,192,512]{3,2,1,0:T(8,128)(2,1)S(1)}, u32[]{:S(2)}, u32[]{:S(2)}) collective-permute-start(bf16[2,2,192,512]{3,2,1,0:T(8,128)(2,1)S(1)} %bitcast.24), channel_id=1, source_target_pairs={{0,2},{2,0},{4,6},{6,4},{1,3},{3,1},{5,7},{7,5},{8,10},{10,8},{12,... | collective-permute-start | bytes 2359304 | tf_op jit(solution)/shard_map/ppermute | solution.py:383
  35.5 16.8 %collective-permute-start.8 = (bf16[1152,128]{1,0:T(8,128)(2,1)S(1)}, bf16[1152,128]{1,0:T(8,128)(2,1)S(1)}, u32[]{:S(2)}, u32[]{:S(2)}) collective-permute-start(bf16[1152,128]{1,0:T(8,128)(2,1)S(1)} %bitcast.28), channel_id=1, source_target_pairs={{0,8},{8,16},{1,9},{9,17},{2,10},{10,18},{3,11},{11,19},{4,12},{12... | collective-permute-start | bytes 884744 | tf_op jit(solution)/shard_map/ppermute | solution.py:319
  39.6 33.3 %collective-permute-start.11 = (bf16[1152,128]{1,0:T(8,128)(2,1)S(1)}, bf16[1152,128]{1,0:T(8,128)(2,1)}, u32[]{:S(2)}, u32[]{:S(2)}) collective-permute-start(bf16[1152,128]{1,0:T(8,128)(2,1)S(1)} %bitcast_add_fusion.2), channel_id=1, source_target_pairs={{0,24},{8,0},{16,8},{24,16},{1,25},{9,1},{17,9},{25,17},{2,26},{10... | collective-permute-start | bytes 884744 | tf_op jit(solution)/shard_map/ppermute | solution.py:327
  52.3 20.6 %collective-permute-start.9 = (bf16[1152,128]{1,0:T(8,128)(2,1)S(1)}, bf16[1152,128]{1,0:T(8,128)(2,1)}, u32[]{:S(2)}, u32[]{:S(2)}) collective-permute-start(bf16[1152,128]{1,0:T(8,128)(2,1)S(1)} %bitcast_add_fusion.3), channel_id=1, source_target_pairs={{0,8},{8,16},{16,24},{24,0},{1,9},{9,17},{17,25},{25,1},{2,10},{10... | collective-permute-start | bytes 884744 | tf_op jit(solution)/shard_map/ppermute | solution.py:326
  53.1 13.2 %collective-permute-start.12 = (bf16[1152,128]{1,0:T(8,128)(2,1)S(1)}, bf16[1152,128]{1,0:T(8,128)(2,1)S(1)}, u32[]{:S(2)}, u32[]{:S(2)}) collective-permute-start(bf16[1152,128]{1,0:T(8,128)(2,1)S(1)} %bitcast.30), channel_id=1, source_target_pairs={{0,8},{8,16},{1,9},{9,17},{2,10},{10,18},{3,11},{11,19},{4,12},{12... | collective-permute-start | bytes 884744 | tf_op jit(solution)/shard_map/ppermute | solution.py:319
  57.2 27.3 %collective-permute-start.15 = (bf16[1152,128]{1,0:T(8,128)(2,1)S(1)}, bf16[1152,128]{1,0:T(8,128)(2,1)S(1)}, u32[]{:S(2)}, u32[]{:S(2)}) collective-permute-start(bf16[1152,128]{1,0:T(8,128)(2,1)S(1)} %bitcast_add_fusion), channel_id=1, source_target_pairs={{0,24},{8,0},{16,8},{24,16},{1,25},{9,1},{17,9},{25,17},{2,26},{10... | collective-permute-start | bytes 884744 | tf_op jit(solution)/shard_map/ppermute | solution.py:327
  66.4 18.2 %collective-permute-start.13 = (bf16[1152,128]{1,0:T(8,128)(2,1)S(1)}, bf16[1152,128]{1,0:T(8,128)(2,1)S(1)}, u32[]{:S(2)}, u32[]{:S(2)}) collective-permute-start(bf16[1152,128]{1,0:T(8,128)(2,1)S(1)} %bitcast_add_fusion.1), channel_id=1, source_target_pairs={{0,8},{8,16},{16,24},{24,0},{1,9},{9,17},{17,25},{25,1},{2,10},{10... | collective-permute-start | bytes 884744 | tf_op jit(solution)/shard_map/ppermute | solution.py:326
  69.5 15.1 %collective-permute-start.16 = (bf16[192,128]{1,0:T(8,128)(2,1)S(1)}, bf16[192,128]{1,0:T(8,128)(2,1)S(1)}, u32[]{:S(2)}, u32[]{:S(2)}) collective-permute-start(bf16[192,128]{1,0:T(8,128)(2,1)S(1)} %get-tuple-element.79), channel_id=1, source_target_pairs={{0,16},{8,24},{16,0},{24,8},{1,17},{9,25},{17,1},{25,9},{2,18},{10... | collective-permute-start | bytes 147464 | tf_op jit(solution)/shard_map/ppermute | solution.py:418
  90.8 10.5 %collective-permute-start.18 = (bf16[1184,128]{1,0:T(8,128)(2,1)}, bf16[1184,128]{1,0:T(8,128)(2,1)S(1)}, u32[]{:S(2)}, u32[]{:S(2)}) collective-permute-start(bf16[1184,128]{1,0:T(8,128)(2,1)} %get-tuple-element.81.near.refs_2_), channel_id=1, source_target_pairs={{0,24},{2,26},{4,28},{6,30},{8,0},{10,2},{12,4},{14,6},{16,8},{18,... | collective-permute-start | bytes 909320 | tf_op jit(solution)/shard_map/ppermute | solution.py:342
  90.8 12.7 %collective-permute-start.17 = (bf16[1184,128]{1,0:T(8,128)(2,1)}, bf16[1184,128]{1,0:T(8,128)(2,1)S(1)}, u32[]{:S(2)}, u32[]{:S(2)}) collective-permute-start(bf16[1184,128]{1,0:T(8,128)(2,1)} %get-tuple-element.81.near.refs_2_), channel_id=1, source_target_pairs={{0,8},{2,10},{4,12},{6,14},{8,16},{10,18},{12,20},{14,22},{16,24},... | collective-permute-start | bytes 909320 | tf_op jit(solution)/shard_map/ppermute | solution.py:341
  92.3 27.8 %collective-permute-start.21 = (bf16[1152,128]{1,0:T(8,128)(2,1)}, bf16[1152,128]{1,0:T(8,128)(2,1)S(1)}, u32[]{:S(2)}, u32[]{:S(2)}) collective-permute-start(bf16[1152,128]{1,0:T(8,128)(2,1)} %get-tuple-element.82), channel_id=1, source_target_pairs={{0,26},{2,24},{4,30},{6,28},{8,2},{10,0},{12,6},{14,4},{16,10},{18... | collective-permute-start | bytes 884744 | tf_op jit(solution)/shard_map/ppermute | solution.py:342
  96.6 24.8 %collective-permute-start.20 = (bf16[1152,128]{1,0:T(8,128)(2,1)}, bf16[1152,128]{1,0:T(8,128)(2,1)S(1)}, u32[]{:S(2)}, u32[]{:S(2)}) collective-permute-start(bf16[1152,128]{1,0:T(8,128)(2,1)} %get-tuple-element.82), channel_id=1, source_target_pairs={{0,10},{2,8},{4,14},{6,12},{8,18},{10,16},{12,22},{14,20},{16,26},... | collective-permute-start | bytes 884744 | tf_op jit(solution)/shard_map/ppermute | solution.py:341
  96.6 25.5 %collective-permute-start.19 = (bf16[1152,128]{1,0:T(8,128)(2,1)}, bf16[1152,128]{1,0:T(8,128)(2,1)S(1)}, u32[]{:S(2)}, u32[]{:S(2)}) collective-permute-start(bf16[1152,128]{1,0:T(8,128)(2,1)} %get-tuple-element.82), channel_id=1, source_target_pairs={{0,2},{2,0},{4,6},{6,4},{8,10},{10,8},{12,14},{14,12},{16,18},{18,... | collective-permute-start | bytes 884744 | tf_op jit(solution)/shard_map/ppermute | solution.py:343
  101.2 33.6 %collective-permute-start.23 = (bf16[1184,128]{1,0:T(8,128)(2,1)S(1)}, bf16[1184,128]{1,0:T(8,128)(2,1)S(1)}, u32[]{:S(2)}, u32[]{:S(2)}) collective-permute-start(bf16[1184,128]{1,0:T(8,128)(2,1)S(1)} %collective-permute-done.18.near_after.refs_4_), channel_id=1, source_target_pairs={{8,0},{16,8},{9,1},{17,9},{10,2},{18,10},{11,3},{19,11},{12,4},{20... | collective-permute-start | bytes 909320 | tf_op jit(solution)/shard_map/ppermute | solution.py:345
  103.6 31.3 %collective-permute-start.22 = (bf16[1184,128]{1,0:T(8,128)(2,1)S(1)}, bf16[1184,128]{1,0:T(8,128)(2,1)}, u32[]{:S(2)}, u32[]{:S(2)}) collective-permute-start(bf16[1184,128]{1,0:T(8,128)(2,1)S(1)} %collective-permute-done.17.near_before.refs_3_), channel_id=1, source_target_pairs={{8,16},{16,24},{9,17},{17,25},{10,18},{18,26},{11,19},{19,27},{12,... | collective-permute-start | bytes 909320 | tf_op jit(solution)/shard_map/ppermute | solution.py:344
  120.1 12.4 %collective-permute-start.25 = (bf16[1152,128]{1,0:T(8,128)(2,1)S(1)}, bf16[1152,128]{1,0:T(8,128)(2,1)S(1)}, u32[]{:S(2)}, u32[]{:S(2)}) collective-permute-start(bf16[1152,128]{1,0:T(8,128)(2,1)S(1)} %collective-permute-done.21.far_after), channel_id=1, source_target_pairs={{8,0},{16,8},{9,1},{17,9},{10,2},{18,10},{11,3},{19,11},{12,4},{20... | collective-permute-start | bytes 884744 | tf_op jit(solution)/shard_map/ppermute | solution.py:345
  121.4 11.2 %collective-permute-start.24 = (bf16[1152,128]{1,0:T(8,128)(2,1)S(1)}, bf16[1152,128]{1,0:T(8,128)(2,1)S(1)}, u32[]{:S(2)}, u32[]{:S(2)}) collective-permute-start(bf16[1152,128]{1,0:T(8,128)(2,1)S(1)} %collective-permute-done.20.far_before), channel_id=1, source_target_pairs={{8,16},{16,24},{9,17},{17,25},{10,18},{18,26},{11,19},{19,27},{12,... | collective-permute-start | bytes 884744 | tf_op jit(solution)/shard_map/ppermute | solution.py:344
  129.9 10.2 %collective-permute-start.29 = (bf16[192,128]{1,0:T(8,128)(2,1)S(1)}, bf16[192,128]{1,0:T(8,128)(2,1)S(1)}, u32[]{:S(2)}, u32[]{:S(2)}) collective-permute-start(bf16[192,128]{1,0:T(8,128)(2,1)S(1)} %copy-done.26), channel_id=1, source_target_pairs={{0,8},{8,16},{16,24},{24,0},{1,9},{9,17},{17,25},{25,1},{2,10},{10... | collective-permute-start | bytes 147464 | tf_op jit(solution)/shard_map/ppermute | solution.py:454
  140.8 14.7 %collective-permute-start.32 = (bf16[3,1152,128]{2,1,0:T(8,128)(2,1)S(1)}, bf16[3,1152,128]{2,1,0:T(8,128)(2,1)S(1)}, u32[]{:S(2)}, u32[]{:S(2)}) collective-permute-start(bf16[3,1152,128]{2,1,0:T(8,128)(2,1)S(1)} %get-tuple-element.100), channel_id=1, source_target_pairs={{0,2},{2,0},{4,6},{6,4},{1,3},{3,1},{5,7},{7,5},{8,10},{10,8},{12,... | collective-permute-start | bytes 2654216 | tf_op jit(solution)/shard_map/ppermute | solution.py:474
  144.1 10.3 %collective-permute-start.28 = (bf16[192,512]{1,0:T(8,128)(2,1)}, bf16[192,512]{1,0:T(8,128)(2,1)S(1)}, u32[]{:S(2)}, u32[]{:S(2)}) collective-permute-start(bf16[192,512]{1,0:T(8,128)(2,1)} %get-tuple-element.94), channel_id=1, source_target_pairs={{5,0},{4,1},{7,2},{6,3},{1,4},{0,5},{3,6},{2,7},{13,8},{12,9},{15,... | collective-permute-start | bytes 589832 | tf_op jit(solution)/shard_map/ppermute | solution.py:476
  155.4 11.2 %collective-permute-start.34 = (bf16[192,512]{1,0:T(8,128)(2,1)S(1)}, bf16[192,512]{1,0:T(8,128)(2,1)S(1)}, u32[]{:S(2)}, u32[]{:S(2)}) collective-permute-start(bf16[192,512]{1,0:T(8,128)(2,1)S(1)} %add_convert_fusion), channel_id=1, source_target_pairs={{0,0},{2,16},{4,8},{6,24},{8,2},{10,18},{12,10},{14,26},{16,4},{18... | collective-permute-start | bytes 589832 | tf_op jit(solution)/shard_map/ppermute | solution.py:481
  (42 other events, 395.1 us)

commit v13 on v11

--- a/solution.py
+++ b/solution.py
@@ -367,15 +367,14 @@
     moved = lax.ppermute(tokens, ("dp", "row"), swap)
     turn = [[(a, (a + ahead) % ndp) for a in range(ndp)] for ahead in range(ndp)]
     upstream = [*kernel_call(split_body, [shaped((rows, width), BF16)] * ndp)(grad_out)]
+    upstream[1] = lax.ppermute(upstream[1], "dp", turn[1])
     moved, upstream = lax.optimization_barrier((moved, upstream))
     near = [moved] + [lax.ppermute(moved, ("row", "col"), offset(*p)) for p in places[1:]]
-    for ahead in (1, 3):
+    for ahead in range(2, ndp):
         upstream[ahead] = lax.ppermute(upstream[ahead], "dp", turn[ahead])
-    upstream[1::2], near[1:] = lax.optimization_barrier((upstream[1::2], near[1:]))
+    upstream[2:], near[1:] = lax.optimization_barrier((upstream[2:], near[1:]))
     x0 = jnp.stack(near).reshape(nblocks, ncol, rows, dcol)
     x1 = lax.ppermute(x0, "row", partner)
-    upstream[2] = lax.ppermute(upstream[2], "dp", turn[2])
-    upstream[2], x1 = lax.optimization_barrier((upstream[2], x1))
 
     sf = lax.dynamic_slice_in_dim(short_filter, z * width, width, 2).reshape(3 * nshort, width)
     lf = lax.dynamic_slice_in_dim(long_filter, z * groups, groups, 0).astype(F32)

time: 164 us -> 165 us (level)
    ppermute x1, waiting for transfers between devices: 9.2 us -> 2.4 us  [move_activations(): moved = lax.ppermute(tokens, ('dp', 'row'), swap)]
    ppermute x2, starting transfers between devices: 5.97 us -> 11.6 us  [sum_over_line(): lax.ppermute(left + from_right, 'dp', [(a, (a - 1) % ndp) for a in range(...]
    ppermute x1, starting transfers between devices: 6.46 us -> 1.29 us  [move_activations(): upstream[1] = lax.ppermute(upstream[1], 'dp', turn[1])]
    ppermute x2, starting transfers between devices: 5.3 us -> 8.6 us  [sum_over_line(): from_left = lax.ppermute(far, 'dp', [(a, a + 1) for a in range(ndp // 2)])]
    ppermute x1, waiting for transfers between devices: 4.07 us -> 6.56 us  [move_activations(): upstream[1] = lax.ppermute(upstream[1], 'dp', turn[1])]
  transfers between devices with their start and end apart: 35 -> 35, of which waited for: 16 -> 17; matrix products, arithmetic and copies ran while one was open for 2% -> 2% of each run, Pallas kernels for 19% -> 19%
where the time goes in v13:
time: 165 us; the launch traced here: 164 us
  starting transfers between devices  61.2 us (37%)
  waiting for transfers between devices  59.8 us (36%)
  Pallas kernels  31.2 us (19%)
  local copies, waits for them, and re-layouts  8.34 us (5%)
  other arithmetic  2.19 us (1%)
    ppermute x2, starting transfers between devices, sum_over_line(): lax.ppermute(left + from_right, 'dp', [(a, (a - 1) % ndp) for a in range(...  11.6 us
    ppermute x2, waiting for transfers between devices, gather_over_line(): before = lax.ppermute(own, ('dp', 'row'), shift(1))  10.8 us
    ppermute x2, waiting for transfers between devices, gather_over_line(): after = lax.ppermute(own, ('dp', 'row'), shift(-1))  10.7 us
    ppermute x2, starting transfers between devices, sum_over_line(): from_left = lax.ppermute(far, 'dp', [(a, a + 1) for a in range(ndp // 2)])  8.6 us
    ppermute x3, waiting for transfers between devices, move_activations(): lax.ppermute(sent, ('row', 'col'), [(b, a) for a, b in offset(*p)])  8.32 us
    pallas_call x2, Pallas kernels, move_activations(): kernel_call(project_body, [shaped((3, chunk, width), BF16)] * ndp, grid=(...  7.93 us
    unnamed x59, local copies, waits for them, and re-layouts  7.65 us
    pallas_call x1, Pallas kernels, move_activations(): kernel_call(functools.partial(weight_grad_body, scale), [shaped((3, drow,...  7.06 us
  transfers between devices with their start and end apart: 35, of which 17 were waited for; matrix products, arithmetic and copies ran while one was open for 2% of the time, Pallas kernels for 19%

profile of v13, /device:TPU:1, one launch (start us, length us, event | category | flops | bytes accessed | tf_op | source)
XLA Modules:
  0.0 163.9 jit_solution(13494289479518670913)
XLA Ops:
  0.6 4.6 %collective-permute-start = (bf16[192,512]{1,0:T(8,128)(2,1)}, bf16[192,512]{1,0:T(8,128)(2,1)S(1)}, u32[]{:S(2)}, u32[]{:S(2)}) collective-permute-start(bf16[192,512]{1,0:T(8,128)(2,1)} %param.5), channel_id=1, source_target_pairs={{0,0},{16,2},{8,4},{24,6},{2,8},{18,10},{10,12},{26,14},{4,16},{20... | collective-permute-start | bytes 589832 | tf_op jit(solution)/shard_map/ppermute | solution.py:367
  7.5 6.6 %collective-permute-done.1.refs_10_ = bf16[192,128]{1,0:T(8,128)(2,1)S(1)} collective-permute-done((bf16[192,128]{1,0:T(8,128)(2,1)S(1)}, bf16[192,128]{1,0:T(8,128)(2,1)S(1)}, u32[]{:S(2)}, u32[]{:S(2)}) %collective-permute-start.1) | collective-permute-done | bytes 49184 | tf_op jit(solution)/shard_map/ppermute | solution.py:370
  27.9 3.8 %shard_map.93 = (bf16[3,384,128]{2,1,0:T(8,128)(2,1)S(1)}, bf16[3,384,128]{2,1,0:T(8,128)(2,1)S(1)}, bf16[3,384,128]{2,1,0:T(8,128)(2,1)S(1)}, bf16[3,384,128]{2,1,0:T(8,128)(2,1)S(1)}) custom-call(bf16[2,2,192,512]{3,2,1,0:T(8,128)(2,1)S(1)} %bitcast.20, bf16[3,1024,512]{2,1,0:T(8,128)(2,1)} %bitcast.5.w_ref.refs_4_), custom_call_target="tpu_custom_call" | custom-call | flops 1207959552 | bytes 5111808 | tf_op jit(solution)/shard_map/pallas_call | solution.py:395
  33.4 4.6 %collective-permute-start.8 = (bf16[1152,128]{1,0:T(8,128)(2,1)S(1)}, bf16[1152,128]{1,0:T(8,128)(2,1)S(1)}, u32[]{:S(2)}, u32[]{:S(2)}) collective-permute-start(bf16[1152,128]{1,0:T(8,128)(2,1)S(1)} %bitcast.23), channel_id=1, source_target_pairs={{0,8},{8,16},{1,9},{9,17},{2,10},{10,18},{3,11},{11,19},{4,12},{12... | collective-permute-start | bytes 884744 | tf_op jit(solution)/shard_map/ppermute | solution.py:318
  38.2 7.4 %collective-permute-start.11 = (bf16[1152,128]{1,0:T(8,128)(2,1)S(1)}, bf16[1152,128]{1,0:T(8,128)(2,1)}, u32[]{:S(2)}, u32[]{:S(2)}) collective-permute-start(bf16[1152,128]{1,0:T(8,128)(2,1)S(1)} %bitcast_add_fusion.2), channel_id=1, source_target_pairs={{0,24},{8,0},{16,8},{24,16},{1,25},{9,1},{17,9},{25,17},{2,26},{10... | collective-permute-start | bytes 884744 | tf_op jit(solution)/shard_map/ppermute | solution.py:321
  45.6 4.1 %shard_map.94 = (bf16[3,384,128]{2,1,0:T(8,128)(2,1)S(1)}, bf16[3,384,128]{2,1,0:T(8,128)(2,1)S(1)}, bf16[3,384,128]{2,1,0:T(8,128)(2,1)S(1)}, bf16[3,384,128]{2,1,0:T(8,128)(2,1)S(1)}) custom-call(bf16[2,2,192,512]{3,2,1,0:T(8,128)(2,1)S(1)} %collective-permute-done.7.x_ref.refs_1_, bf16[3,1024,512]{2,1,0:T(8,128)(2,1)} %bitcast.5.w_ref.refs_4_), custom_call_target="tpu_custom_call" | custom-call | flops 1207959552 | bytes 5111808 | tf_op jit(solution)/shard_map/pallas_call | solution.py:395
  51.4 4.0 %collective-permute-start.12 = (bf16[1152,128]{1,0:T(8,128)(2,1)S(1)}, bf16[1152,128]{1,0:T(8,128)(2,1)S(1)}, u32[]{:S(2)}, u32[]{:S(2)}) collective-permute-start(bf16[1152,128]{1,0:T(8,128)(2,1)S(1)} %bitcast.25), channel_id=1, source_target_pairs={{0,8},{8,16},{1,9},{9,17},{2,10},{10,18},{3,11},{11,19},{4,12},{12... | collective-permute-start | bytes 884744 | tf_op jit(solution)/shard_map/ppermute | solution.py:318
  55.5 4.2 %collective-permute-start.15 = (bf16[1152,128]{1,0:T(8,128)(2,1)S(1)}, bf16[1152,128]{1,0:T(8,128)(2,1)S(1)}, u32[]{:S(2)}, u32[]{:S(2)}) collective-permute-start(bf16[1152,128]{1,0:T(8,128)(2,1)S(1)} %bitcast_add_fusion), channel_id=1, source_target_pairs={{0,24},{8,0},{16,8},{24,16},{1,25},{9,1},{17,9},{25,17},{2,26},{10... | collective-permute-start | bytes 884744 | tf_op jit(solution)/shard_map/ppermute | solution.py:321
  59.6 4.9 %collective-permute-done.12 = bf16[1152,128]{1,0:T(8,128)(2,1)S(1)} collective-permute-done((bf16[1152,128]{1,0:T(8,128)(2,1)S(1)}, bf16[1152,128]{1,0:T(8,128)(2,1)S(1)}, u32[]{:S(2)}, u32[]{:S(2)}) %collective-permute-start.12) | collective-permute-done | bytes 294944 | tf_op jit(solution)/shard_map/ppermute | solution.py:318
  69.9 2.5 %collective-permute-done.15.refs_5_ = bf16[1152,128]{1,0:T(8,128)(2,1)S(1)} collective-permute-done((bf16[1152,128]{1,0:T(8,128)(2,1)S(1)}, bf16[1152,128]{1,0:T(8,128)(2,1)S(1)}, u32[]{:S(2)}, u32[]{:S(2)}) %collective-permute-start.15) | collective-permute-done | bytes 294944 | tf_op jit(solution)/shard_map/ppermute | solution.py:321
  72.5 6.8 %collective-permute-done.13.refs_4_ = bf16[1152,128]{1,0:T(8,128)(2,1)S(1)} collective-permute-done((bf16[1152,128]{1,0:T(8,128)(2,1)S(1)}, bf16[1152,128]{1,0:T(8,128)(2,1)S(1)}, u32[]{:S(2)}, u32[]{:S(2)}) %collective-permute-start.13) | collective-permute-done | bytes 294944 | tf_op jit(solution)/shard_map/ppermute | solution.py:320
  80.0 5.4 %shard_map.96 = (bf16[1184,128]{1,0:T(8,128)(2,1)}, bf16[1152,128]{1,0:T(8,128)(2,1)}, bf16[192,128]{1,0:T(8,128)(2,1)}, bf16[192,128]{1,0:T(8,128)(2,1)}, bf16[...) custom-call(bf16[1152,128]{1,0:T(8,128)(2,1)} %bitcast.26, bf16[1152,128]{1,0:T(8,128)(2,1)} %copy-done.17, ...), custom_call_target="tpu_custom_call" | custom-call | flops 1207959552 | bytes 2752512 | tf_op jit(solution)/shard_map/pallas_call | solution.py:414
  85.4 2.9 %collective-permute-start.20 = (bf16[1152,128]{1,0:T(8,128)(2,1)}, bf16[1152,128]{1,0:T(8,128)(2,1)S(1)}, u32[]{:S(2)}, u32[]{:S(2)}) collective-permute-start(bf16[1152,128]{1,0:T(8,128)(2,1)} %get-tuple-element.76), channel_id=1, source_target_pairs={{0,26},{2,24},{4,30},{6,28},{8,2},{10,0},{12,6},{14,4},{16,10},{18... | collective-permute-start | bytes 884744 | tf_op jit(solution)/shard_map/ppermute | solution.py:336
  89.8 5.7 %collective-permute-done.20.far_after = bf16[1152,128]{1,0:T(8,128)(2,1)S(1)} collective-permute-done((bf16[1152,128]{1,0:T(8,128)(2,1)}, bf16[1152,128]{1,0:T(8,128)(2,1)S(1)}, u32[]{:S(2)}, u32[]{:S(2)}) %collective-permute-start.20) | collective-permute-done | bytes 294944 | tf_op jit(solution)/shard_map/ppermute | solution.py:336
  96.9 5.0 %collective-permute-done.17.near_after.refs_4_ = bf16[1184,128]{1,0:T(8,128)(2,1)S(1)} collective-permute-done((bf16[1184,128]{1,0:T(8,128)(2,1)}, bf16[1184,128]{1,0:T(8,128)(2,1)S(1)}, u32[]{:S(2)}, u32[]{:S(2)}) %collective-permute-start.17) | collective-permute-done | bytes 303136 | tf_op jit(solution)/shard_map/ppermute | solution.py:336
  103.3 7.0 %collective-permute-done.16.near_before.refs_3_ = bf16[1184,128]{1,0:T(8,128)(2,1)S(1)} collective-permute-done((bf16[1184,128]{1,0:T(8,128)(2,1)}, bf16[1184,128]{1,0:T(8,128)(2,1)S(1)}, u32[]{:S(2)}, u32[]{:S(2)}) %collective-permute-start.16) | collective-permute-done | bytes 303136 | tf_op jit(solution)/shard_map/ppermute | solution.py:335
  110.9 3.8 %collective-permute-done.19.far_before = bf16[1152,128]{1,0:T(8,128)(2,1)S(1)} collective-permute-done((bf16[1152,128]{1,0:T(8,128)(2,1)}, bf16[1152,128]{1,0:T(8,128)(2,1)S(1)}, u32[]{:S(2)}, u32[]{:S(2)}) %collective-permute-start.19) | collective-permute-done | bytes 294944 | tf_op jit(solution)/shard_map/ppermute | solution.py:335
  116.8 4.1 %collective-permute-start.29 = (bf16[192,128]{1,0:T(8,128)(2,1)}, bf16[192,128]{1,0:T(8,128)(2,1)S(1)}, u32[]{:S(2)}, u32[]{:S(2)}) collective-permute-start(bf16[192,128]{1,0:T(8,128)(2,1)} %get-tuple-element.85), channel_id=1, source_target_pairs={{0,8},{8,16},{16,24},{24,0},{1,9},{9,17},{17,25},{25,1},{2,10},{10... | collective-permute-start | bytes 147464 | tf_op jit(solution)/shard_map/ppermute | solution.py:434
  121.8 5.5 %shard_map.97 = (f32[2,384,512]{2,1,0:T(8,128)S(1)}, bf16[3,1152,128]{2,1,0:T(8,128)(2,1)S(1)}) custom-call(bf16[1184,128]{1,0:T(8,128)(2,1)S(1)} %copy-done.6, bf16[1184,128]{1,0:T(8,128)(2,1)S(1)} %collective-permute-done.16.near_before.refs_3_, bf16[1184,128]{1,0:T(8,128)(2,1)S(1)} %collective-permute-done.17.near_after.refs_4_, ...), custom_call_target="tpu_custom_call" | custom-call | flops 2415919104 | bytes 10223616 | tf_op jit(solution)/shard_map/pallas_call | solution.py:441
  132.8 4.5 %shard_map.98 = (bf16[1184,128]{1,0:T(8,128)(2,1)}, bf16[1152,128]{1,0:T(8,128)(2,1)}, bf16[192,512]{1,0:T(8,128)(2,1)}, bf16[192,512]{1,0:T(8,128)(2,1)}, bf16[...) custom-call(f32[2,384,512]{2,1,0:T(8,128)} %copy-done.1, bf16[1184,128]{1,0:T(8,128)(2,1)} %copy-done.13, ...), custom_call_target="tpu_custom_call" | custom-call | flops 603979776 | bytes 2555904 | tf_op jit(solution)/shard_map/pallas_call | solution.py:450
  142.6 3.2 %collective-permute-done.26 = bf16[192,512]{1,0:T(8,128)(2,1)S(1)} collective-permute-done((bf16[192,512]{1,0:T(8,128)(2,1)}, bf16[192,512]{1,0:T(8,128)(2,1)S(1)}, u32[]{:S(2)}, u32[]{:S(2)}) %collective-permute-start.26) | collective-permute-done | bytes 196640 | tf_op jit(solution)/shard_map/ppermute | solution.py:469
  146.7 4.2 %collective-permute-done.28 = bf16[192,512]{1,0:T(8,128)(2,1)S(1)} collective-permute-done((bf16[192,512]{1,0:T(8,128)(2,1)}, bf16[192,512]{1,0:T(8,128)(2,1)S(1)}, u32[]{:S(2)}, u32[]{:S(2)}) %collective-permute-start.28) | collective-permute-done | bytes 196640 | tf_op jit(solution)/shard_map/ppermute | solution.py:469
  152.0 3.8 %collective-permute-start.34 = (bf16[192,512]{1,0:T(8,128)(2,1)S(1)}, bf16[192,512]{1,0:T(8,128)(2,1)S(1)}, u32[]{:S(2)}, u32[]{:S(2)}) collective-permute-start(bf16[192,512]{1,0:T(8,128)(2,1)S(1)} %add_convert_fusion), channel_id=1, source_target_pairs={{0,0},{2,16},{4,8},{6,24},{8,2},{10,18},{12,10},{14,26},{16,4},{18... | collective-permute-start | bytes 589832 | tf_op jit(solution)/shard_map/ppermute | solution.py:474
  155.8 7.1 %shard_map.99 = (f32[3,1024,512]{2,1,0:T(8,128)}, bf16[192,512]{1,0:T(8,128)(2,1)}, f32[32,128]{1,0:T(8,128)}, f32[3,3,512]{2,1,0:T(4,128)}) custom-call(bf16[2,2,192,512]{3,2,1,0:T(8,128)(2,1)} %bitcast.21, bf16[2,2,192,512]{3,2,1,0:T(8,128)(2,1)} %copy-done.5, bf16[1184,128]{1,0:T(8,128)(2,1)} %get-tuple-element.75.near.refs_2_, ...), custom_call_target="tpu_custom_call" | custom-call | flops 2415919104 | bytes 10223616 | tf_op jit(solution)/shard_map/pallas_call | solution.py:476
  (126 shorter events, 47.0 us)
Async XLA Ops:
  0.6 15.8 %collective-permute-start = (bf16[192,512]{1,0:T(8,128)(2,1)}, bf16[192,512]{1,0:T(8,128)(2,1)S(1)}, u32[]{:S(2)}, u32[]{:S(2)}) collective-permute-start(bf16[192,512]{1,0:T(8,128)(2,1)} %param.5), channel_id=1, source_target_pairs={{0,0},{16,2},{8,4},{24,6},{2,8},{18,10},{10,12},{26,14},{4,16},{20... | collective-permute-start | bytes 589832 | tf_op jit(solution)/shard_map/ppermute | solution.py:367
  16.5 10.9 %collective-permute-start.5 = (bf16[192,512]{1,0:T(8,128)(2,1)S(1)}, bf16[192,512]{1,0:T(8,128)(2,1)S(1)}, u32[]{:S(2)}, u32[]{:S(2)}) collective-permute-start(bf16[192,512]{1,0:T(8,128)(2,1)S(1)} %collective-permute-done), channel_id=1, source_target_pairs={{0,4},{1,5},{2,6},{3,7},{4,0},{5,1},{6,2},{7,3},{8,12},{9,13},{10,... | collective-permute-start | bytes 589832 | tf_op jit(solution)/shard_map/ppermute | solution.py:372
  27.5 18.1 %collective-permute-start.7 = (bf16[2,2,192,512]{3,2,1,0:T(8,128)(2,1)S(1)}, bf16[2,2,192,512]{3,2,1,0:T(8,128)(2,1)S(1)}, u32[]{:S(2)}, u32[]{:S(2)}) collective-permute-start(bf16[2,2,192,512]{3,2,1,0:T(8,128)(2,1)S(1)} %bitcast.19), channel_id=1, source_target_pairs={{0,2},{2,0},{4,6},{6,4},{1,3},{3,1},{5,7},{7,5},{8,10},{10,8},{12,... | collective-permute-start | bytes 2359304 | tf_op jit(solution)/shard_map/ppermute | solution.py:377
  33.2 83.6 %collective-permute-start.21 = (bf16[3,1024,512]{2,1,0:T(8,128)(2,1)}, bf16[3,1024,512]{2,1,0:T(8,128)(2,1)}, u32[]{:S(2)}, u32[]{:S(2)}) collective-permute-start(bf16[3,1024,512]{2,1,0:T(8,128)(2,1)} %bitcast.5.w_ref.refs_4_), channel_id=1, source_target_pairs={{0,2},{2,0},{4,6},{6,4},{1,3},{3,1},{5,7},{7,5},{8,10},{10,8},{12,... | collective-permute-start | bytes 9437192 | tf_op jit(solution)/shard_map/ppermute | solution.py:440
  33.4 17.0 %collective-permute-start.8 = (bf16[1152,128]{1,0:T(8,128)(2,1)S(1)}, bf16[1152,128]{1,0:T(8,128)(2,1)S(1)}, u32[]{:S(2)}, u32[]{:S(2)}) collective-permute-start(bf16[1152,128]{1,0:T(8,128)(2,1)S(1)} %bitcast.23), channel_id=1, source_target_pairs={{0,8},{8,16},{1,9},{9,17},{2,10},{10,18},{3,11},{11,19},{4,12},{12... | collective-permute-start | bytes 884744 | tf_op jit(solution)/shard_map/ppermute | solution.py:318
  38.2 31.8 %collective-permute-start.11 = (bf16[1152,128]{1,0:T(8,128)(2,1)S(1)}, bf16[1152,128]{1,0:T(8,128)(2,1)}, u32[]{:S(2)}, u32[]{:S(2)}) collective-permute-start(bf16[1152,128]{1,0:T(8,128)(2,1)S(1)} %bitcast_add_fusion.2), channel_id=1, source_target_pairs={{0,24},{8,0},{16,8},{24,16},{1,25},{9,1},{17,9},{25,17},{2,26},{10... | collective-permute-start | bytes 884744 | tf_op jit(solution)/shard_map/ppermute | solution.py:321
  50.5 19.4 %collective-permute-start.9 = (bf16[1152,128]{1,0:T(8,128)(2,1)S(1)}, bf16[1152,128]{1,0:T(8,128)(2,1)S(1)}, u32[]{:S(2)}, u32[]{:S(2)}) collective-permute-start(bf16[1152,128]{1,0:T(8,128)(2,1)S(1)} %bitcast_add_fusion.3), channel_id=1, source_target_pairs={{0,8},{8,16},{16,24},{24,0},{1,9},{9,17},{17,25},{25,1},{2,10},{10... | collective-permute-start | bytes 884744 | tf_op jit(solution)/shard_map/ppermute | solution.py:320
  51.4 13.1 %collective-permute-start.12 = (bf16[1152,128]{1,0:T(8,128)(2,1)S(1)}, bf16[1152,128]{1,0:T(8,128)(2,1)S(1)}, u32[]{:S(2)}, u32[]{:S(2)}) collective-permute-start(bf16[1152,128]{1,0:T(8,128)(2,1)S(1)} %bitcast.25), channel_id=1, source_target_pairs={{0,8},{8,16},{1,9},{9,17},{2,10},{10,18},{3,11},{11,19},{4,12},{12... | collective-permute-start | bytes 884744 | tf_op jit(solution)/shard_map/ppermute | solution.py:318
  55.5 17.0 %collective-permute-start.15 = (bf16[1152,128]{1,0:T(8,128)(2,1)S(1)}, bf16[1152,128]{1,0:T(8,128)(2,1)S(1)}, u32[]{:S(2)}, u32[]{:S(2)}) collective-permute-start(bf16[1152,128]{1,0:T(8,128)(2,1)S(1)} %bitcast_add_fusion), channel_id=1, source_target_pairs={{0,24},{8,0},{16,8},{24,16},{1,25},{9,1},{17,9},{25,17},{2,26},{10... | collective-permute-start | bytes 884744 | tf_op jit(solution)/shard_map/ppermute | solution.py:321
  64.6 14.7 %collective-permute-start.13 = (bf16[1152,128]{1,0:T(8,128)(2,1)S(1)}, bf16[1152,128]{1,0:T(8,128)(2,1)S(1)}, u32[]{:S(2)}, u32[]{:S(2)}) collective-permute-start(bf16[1152,128]{1,0:T(8,128)(2,1)S(1)} %bitcast_add_fusion.1), channel_id=1, source_target_pairs={{0,8},{8,16},{16,24},{24,0},{1,9},{9,17},{17,25},{25,1},{2,10},{10... | collective-permute-start | bytes 884744 | tf_op jit(solution)/shard_map/ppermute | solution.py:320
  85.4 10.0 %collective-permute-start.20 = (bf16[1152,128]{1,0:T(8,128)(2,1)}, bf16[1152,128]{1,0:T(8,128)(2,1)S(1)}, u32[]{:S(2)}, u32[]{:S(2)}) collective-permute-start(bf16[1152,128]{1,0:T(8,128)(2,1)} %get-tuple-element.76), channel_id=1, source_target_pairs={{0,26},{2,24},{4,30},{6,28},{8,2},{10,0},{12,6},{14,4},{16,10},{18... | collective-permute-start | bytes 884744 | tf_op jit(solution)/shard_map/ppermute | solution.py:336
  88.3 13.6 %collective-permute-start.17 = (bf16[1184,128]{1,0:T(8,128)(2,1)}, bf16[1184,128]{1,0:T(8,128)(2,1)S(1)}, u32[]{:S(2)}, u32[]{:S(2)}) collective-permute-start(bf16[1184,128]{1,0:T(8,128)(2,1)} %get-tuple-element.75.near.refs_2_), channel_id=1, source_target_pairs={{0,24},{2,26},{4,28},{6,30},{8,0},{10,2},{12,4},{14,6},{16,8},{18,... | collective-permute-start | bytes 909320 | tf_op jit(solution)/shard_map/ppermute | solution.py:336
  89.6 20.6 %collective-permute-start.16 = (bf16[1184,128]{1,0:T(8,128)(2,1)}, bf16[1184,128]{1,0:T(8,128)(2,1)S(1)}, u32[]{:S(2)}, u32[]{:S(2)}) collective-permute-start(bf16[1184,128]{1,0:T(8,128)(2,1)} %get-tuple-element.75.near.refs_2_), channel_id=1, source_target_pairs={{0,8},{2,10},{4,12},{6,14},{8,16},{10,18},{12,20},{14,22},{16,24},... | collective-permute-start | bytes 909320 | tf_op jit(solution)/shard_map/ppermute | solution.py:335
  89.8 25.0 %collective-permute-start.19 = (bf16[1152,128]{1,0:T(8,128)(2,1)}, bf16[1152,128]{1,0:T(8,128)(2,1)S(1)}, u32[]{:S(2)}, u32[]{:S(2)}) collective-permute-start(bf16[1152,128]{1,0:T(8,128)(2,1)} %get-tuple-element.76), channel_id=1, source_target_pairs={{0,10},{2,8},{4,14},{6,12},{8,18},{10,16},{12,22},{14,20},{16,26},... | collective-permute-start | bytes 884744 | tf_op jit(solution)/shard_map/ppermute | solution.py:335
  95.5 20.6 %collective-permute-start.18 = (bf16[1152,128]{1,0:T(8,128)(2,1)}, bf16[1152,128]{1,0:T(8,128)(2,1)S(1)}, u32[]{:S(2)}, u32[]{:S(2)}) collective-permute-start(bf16[1152,128]{1,0:T(8,128)(2,1)} %get-tuple-element.76), channel_id=1, source_target_pairs={{0,2},{2,0},{4,6},{6,4},{8,10},{10,8},{12,14},{14,12},{16,18},{18,... | collective-permute-start | bytes 884744 | tf_op jit(solution)/shard_map/ppermute | solution.py:337
  102.0 29.9 %collective-permute-start.23 = (bf16[1184,128]{1,0:T(8,128)(2,1)S(1)}, bf16[1184,128]{1,0:T(8,128)(2,1)S(1)}, u32[]{:S(2)}, u32[]{:S(2)}) collective-permute-start(bf16[1184,128]{1,0:T(8,128)(2,1)S(1)} %collective-permute-done.17.near_after.refs_4_), channel_id=1, source_target_pairs={{8,0},{16,8},{9,1},{17,9},{10,2},{18,10},{11,3},{19,11},{12,4},{20... | collective-permute-start | bytes 909320 | tf_op jit(solution)/shard_map/ppermute | solution.py:339
  110.3 21.7 %collective-permute-start.22 = (bf16[1184,128]{1,0:T(8,128)(2,1)S(1)}, bf16[1184,128]{1,0:T(8,128)(2,1)S(1)}, u32[]{:S(2)}, u32[]{:S(2)}) collective-permute-start(bf16[1184,128]{1,0:T(8,128)(2,1)S(1)} %collective-permute-done.16.near_before.refs_3_), channel_id=1, source_target_pairs={{8,16},{16,24},{9,17},{17,25},{10,18},{18,26},{11,19},{19,27},{12,... | collective-permute-start | bytes 909320 | tf_op jit(solution)/shard_map/ppermute | solution.py:338
  114.8 14.8 %collective-permute-start.25 = (bf16[1152,128]{1,0:T(8,128)(2,1)S(1)}, bf16[1152,128]{1,0:T(8,128)(2,1)S(1)}, u32[]{:S(2)}, u32[]{:S(2)}) collective-permute-start(bf16[1152,128]{1,0:T(8,128)(2,1)S(1)} %collective-permute-done.20.far_after), channel_id=1, source_target_pairs={{8,0},{16,8},{9,1},{17,9},{10,2},{18,10},{11,3},{19,11},{12,4},{20... | collective-permute-start | bytes 884744 | tf_op jit(solution)/shard_map/ppermute | solution.py:339
  116.1 13.5 %collective-permute-start.24 = (bf16[1152,128]{1,0:T(8,128)(2,1)S(1)}, bf16[1152,128]{1,0:T(8,128)(2,1)S(1)}, u32[]{:S(2)}, u32[]{:S(2)}) collective-permute-start(bf16[1152,128]{1,0:T(8,128)(2,1)S(1)} %collective-permute-done.19.far_before), channel_id=1, source_target_pairs={{8,16},{16,24},{9,17},{17,25},{10,18},{18,26},{11,19},{19,27},{12,... | collective-permute-start | bytes 884744 | tf_op jit(solution)/shard_map/ppermute | solution.py:338
  116.8 20.6 %collective-permute-start.29 = (bf16[192,128]{1,0:T(8,128)(2,1)}, bf16[192,128]{1,0:T(8,128)(2,1)S(1)}, u32[]{:S(2)}, u32[]{:S(2)}) collective-permute-start(bf16[192,128]{1,0:T(8,128)(2,1)} %get-tuple-element.85), channel_id=1, source_target_pairs={{0,8},{8,16},{16,24},{24,0},{1,9},{9,17},{17,25},{25,1},{2,10},{10... | collective-permute-start | bytes 147464 | tf_op jit(solution)/shard_map/ppermute | solution.py:434
  138.0 14.0 %collective-permute-start.32 = (bf16[3,1152,128]{2,1,0:T(8,128)(2,1)S(1)}, bf16[3,1152,128]{2,1,0:T(8,128)(2,1)S(1)}, u32[]{:S(2)}, u32[]{:S(2)}) collective-permute-start(bf16[3,1152,128]{2,1,0:T(8,128)(2,1)S(1)} %get-tuple-element.88), channel_id=1, source_target_pairs={{0,2},{2,0},{4,6},{6,4},{1,3},{3,1},{5,7},{7,5},{8,10},{10,8},{12,... | collective-permute-start | bytes 2654216 | tf_op jit(solution)/shard_map/ppermute | solution.py:467
  140.6 10.3 %collective-permute-start.28 = (bf16[192,512]{1,0:T(8,128)(2,1)}, bf16[192,512]{1,0:T(8,128)(2,1)S(1)}, u32[]{:S(2)}, u32[]{:S(2)}) collective-permute-start(bf16[192,512]{1,0:T(8,128)(2,1)} %get-tuple-element.82), channel_id=1, source_target_pairs={{5,0},{4,1},{7,2},{6,3},{1,4},{0,5},{3,6},{2,7},{13,8},{12,9},{15,... | collective-permute-start | bytes 589832 | tf_op jit(solution)/shard_map/ppermute | solution.py:469
  141.7 10.2 %collective-permute-start.33 = (bf16[1152,128]{1,0:T(8,128)(2,1)}, bf16[1152,128]{1,0:T(8,128)(2,1)S(1)}, u32[]{:S(2)}, u32[]{:S(2)}) collective-permute-start(bf16[1152,128]{1,0:T(8,128)(2,1)} %get-tuple-element.89), channel_id=1, source_target_pairs={{0,2},{2,0},{4,6},{6,4},{1,3},{3,1},{5,7},{7,5},{8,10},{10,8},{12,... | collective-permute-start | bytes 884744 | tf_op jit(solution)/shard_map/ppermute | solution.py:467
  152.0 11.2 %collective-permute-start.34 = (bf16[192,512]{1,0:T(8,128)(2,1)S(1)}, bf16[192,512]{1,0:T(8,128)(2,1)S(1)}, u32[]{:S(2)}, u32[]{:S(2)}) collective-permute-start(bf16[192,512]{1,0:T(8,128)(2,1)S(1)} %add_convert_fusion), channel_id=1, source_target_pairs={{0,0},{2,16},{4,8},{6,24},{8,2},{10,18},{12,10},{14,26},{16,4},{18... | collective-permute-start | bytes 589832 | tf_op jit(solution)/shard_map/ppermute | solution.py:474
  (40 other events, 373.7 us)

commit v14 on v12

--- a/solution.py
+++ b/solution.py
@@ -80,45 +80,45 @@
         out_ref[0] = held[wrapped(z + ahead, len(out_refs))]
 
 
-def first_grad_body(near, near_before, near_after, far, far_before, far_after, w_ref, partner_w_ref, out_ref, far_ref, held):
+def far_columns_body(w_ref, out_ref, sem):
+    ndp = lax.axis_size("dp")
+    width = out_ref.shape[2]
+    start = wrapped(lax.axis_index("dp") + ndp // 2, ndp) * width
+    copy = pltpu.make_async_copy(w_ref.at[:, :, pl.ds(pl.multiple_of(start, width), width)], out_ref, sem)
+    copy.start()
+    copy.wait()
+
+
+def first_grad_body(own, before, after, w_ref, out_ref, held):
     ndp, _, width = held.shape
     ncol, tokens, depth = out_ref.shape
     z, col = lax.axis_index("dp"), lax.axis_index("col")
-    far_ref[0], far_ref[1], far_ref[2] = far[...], far_before[...], far_after[...]
-    for pieces, weights, first in (
-        ((near, near_before, near_after), w_ref, True),
-        ((far, far_before, far_after), partner_w_ref, False),
-    ):
-        held[wrapped(z + ndp // 2, ndp)] = jnp.zeros(held.shape[1:], BF16)
-        for ahead, piece in zip((0, -1, 1), pieces):
-            held[wrapped(z + ahead, ndp)] = piece[: 3 * tokens]
-        for dx in range(ncol):
-            start = pl.multiple_of(wrapped(col - dx, ncol) * depth, depth)
-            total = jnp.zeros((tokens, depth), F32) if first else out_ref[dx]
-            for i in range(3):
-                rows = slice(i * tokens, (i + 1) * tokens)
-                total += lax.dot_general(
-                    jnp.concatenate([held[owner, rows] for owner in range(ndp)], axis=1),
-                    weights[i, pl.ds(start, depth), :],
-                    (((1,), (1,)), ((), ())),
-                    preferred_element_type=F32,
-                )
-            out_ref[dx] = total
-
-
-def second_grad_body(ndp, part_ref, *refs):
-    arrived, weights, refs = (refs[:2], refs[2:4]), refs[4:6], refs[6:]
+    held[wrapped(z + ndp // 2, ndp)] = jnp.zeros(held.shape[1:], BF16)
+    for ahead, piece in zip((0, -1, 1), (own, before, after)):
+        held[wrapped(z + ahead, ndp)] = piece[: 3 * tokens]
+    for dx in range(ncol):
+        start = pl.multiple_of(wrapped(col - dx, ncol) * depth, depth)
+        total = jnp.zeros((tokens, depth), F32)
+        for i in range(3):
+            rows = slice(i * tokens, (i + 1) * tokens)
+            total += lax.dot_general(
+                jnp.concatenate([held[owner, rows] for owner in range(ndp)], axis=1),
+                w_ref[i, pl.ds(start, depth), :],
+                (((1,), (1,)), ((), ())),
+                preferred_element_type=F32,
+            )
+        out_ref[dx] = total.astype(out_ref.dtype)
+
+
+def second_grad_body(ndp, *refs):
+    arrived, sources, refs = (refs[:2], refs[2:4]), refs[4:8], refs[8:]
     (near_ref, far_ref), refs = refs[:2], refs[2:]
-    *out_refs, held_w, held_part, sems = refs
+    *out_refs, held_w, held_partner_w, held_part, held_partner, sems = refs
+    held = (held_w, held_partner_w, held_part, held_partner)
     ncol, tokens, depth = held_part.shape
     rows = out_refs[0].shape[0]
-    width = near_ref.shape[1]
     z, col = lax.axis_index("dp"), lax.axis_index("col")
-    lanes = pl.ds(pl.multiple_of(wrapped(z + ndp // 2, ndp) * width, width), width)
-    copies = [
-        pltpu.make_async_copy(w_ref.at[:, :, lanes], held_w.at[k], sems.at[k]) for k, w_ref in enumerate(weights)
-    ]
-    copies.append(pltpu.make_async_copy(part_ref, held_part, sems.at[2]))
+    copies = [pltpu.make_async_copy(a, b, sems.at[k]) for k, (a, b) in enumerate(zip(sources, held))]
     for copy in copies:
         copy.start()
     for k, (pair, target) in enumerate(zip(arrived, (near_ref, far_ref))):
@@ -126,7 +126,7 @@
 
             @pl.when(here)
             def _(source=source, target=target, k=k):
-                copy = pltpu.make_async_copy(source, target, sems.at[3 + k])
+                copy = pltpu.make_async_copy(source, target, sems.at[4 + k])
                 copy.start()
                 copy.wait()
 
@@ -137,22 +137,17 @@
     )
     for dx in range(ncol):
         start = pl.multiple_of(wrapped(col - dx, ncol) * depth, depth)
-        right = jnp.concatenate([held_w[k, i, pl.ds(start, depth), :] for k in range(2) for i in range(3)], axis=1)
-        total = held_part[dx] + lax.dot_general(
-            left, right, (((1,), (1,)), ((), ())), preferred_element_type=F32
+        right = jnp.concatenate(
+            [w_ref[i, pl.ds(start, depth), :] for w_ref in (held_w, held_partner_w) for i in range(3)], axis=1
         )
+        total = held_part[dx] + held_partner[dx].astype(F32)
+        total += lax.dot_general(left, right, (((1,), (1,)), ((), ())), preferred_element_type=F32)
         for block in range(tokens // rows):
             out_refs[block * ncol + dx][...] = total[block * rows : (block + 1) * rows].astype(BF16)
 
 
 def weight_grad_body(scale, *refs):
-    (x0_ref, x1_ref), near_refs, (far_ref, far_last_ref), mixed_refs, refs = (
-        refs[:2],
-        refs[2:6],
-        refs[6:8],
-        refs[8:12],
-        refs[12:],
-    )
+    (x0_ref, x1_ref), near_refs, other_refs, mixed_refs, refs = refs[:2], refs[2:6], refs[6:10], refs[10:14], refs[14:]
     out_ref, mixed_ref, long_ref, short_ref, held, held_mixed = refs
     nblocks, ncol, rows, depth = x0_ref.shape
     _, ndp, _, width = held.shape
@@ -166,7 +161,7 @@
         for k, ahead in enumerate((0, -1, 1, 2)):
             owner = wrapped(z + ahead, ndp)
             held[0, owner] = near_refs[k][...]
-            held[1, owner, : 3 * tokens] = far_ref[k] if k < 3 else far_last_ref[...]
+            held[1, owner, : 3 * tokens] = other_refs[k][...]
         for back in range(ndp):
             held_mixed[wrapped(z - back, ndp)] = mixed_refs[back][...]
         for owner in range(ndp):
@@ -331,19 +326,18 @@
 def gather_over_line(own, across):
     ndp, nrow = lax.axis_size("dp"), lax.axis_size("row")
 
-    def shift(count):
+    def pairs(dps, count, across):
         return [
             (a * nrow + r, (a + count) % ndp * nrow + (r + 1 - 2 * (r % 2) if across else r))
-            for a in range(ndp)
+            for a in dps
             for r in range(nrow)
         ]
 
-    before = lax.ppermute(own, ("dp", "row"), shift(1))
-    after = lax.ppermute(own, ("dp", "row"), shift(-1))
-    here = lax.ppermute(own, ("dp", "row"), shift(0)) if across else own
-    far_before = lax.ppermute(before, "dp", [(a - 1, a) for a in range(ndp // 2, ndp)])
-    far_after = lax.ppermute(after, "dp", [(a + 1, a) for a in range(ndp // 2)])
-    return here, before, after, far_before, far_after
+    before = lax.ppermute(own, ("dp", "row"), pairs(range(ndp), 1, False))
+    after = lax.ppermute(own, ("dp", "row"), pairs(range(ndp), -1, False))
+    far_before = lax.ppermute(before, ("dp", "row"), pairs(range(ndp // 2 - 1, ndp - 1), 1, across))
+    far_after = lax.ppermute(after, ("dp", "row"), pairs(range(1, ndp // 2 + 1), -1, across))
+    return own, before, after, far_before, far_after
 
 
 def move_activations(tokens, in_weight, short_filter, long_filter, grad_out):
@@ -371,14 +365,21 @@
 
     w = jnp.transpose(in_weight, (1, 0, 2))
     moved = lax.ppermute(tokens, ("dp", "row"), swap)
+    far_w = kernel_call(
+        far_columns_body,
+        shaped((3, drow, width), BF16),
+        in_specs=[pl.BlockSpec(memory_space=pl.ANY)],
+        out_specs=pl.BlockSpec(memory_space=pltpu.VMEM),
+        scratch=[pltpu.SemaphoreType.DMA],
+    )(w)
     turn = [[(a, (a + ahead) % ndp) for a in range(ndp)] for ahead in range(ndp)]
     upstream = [*kernel_call(split_body, [shaped((rows, width), BF16)] * ndp)(grad_out)]
     upstream[1] = lax.ppermute(upstream[1], "dp", turn[1])
-    moved, upstream = lax.optimization_barrier((moved, upstream))
+    moved, upstream, far_w = lax.optimization_barrier((moved, upstream, far_w))
     near = [moved] + [lax.ppermute(moved, ("row", "col"), offset(*p)) for p in places[1:]]
-    upstream[3] = lax.ppermute(upstream[3], "dp", turn[3])
-    partner_w = lax.ppermute(w, "row", partner)
-    upstream[3], near[1:], partner_w = lax.optimization_barrier((upstream[3], near[1:], partner_w))
+    for ahead in range(2, ndp):
+        upstream[ahead] = lax.ppermute(upstream[ahead], "dp", turn[ahead])
+    upstream[2:], near[1:] = lax.optimization_barrier((upstream[2:], near[1:]))
     x0 = jnp.stack(near).reshape(nblocks, ncol, rows, dcol)
     x1 = lax.ppermute(x0, "row", partner)
 
@@ -396,7 +397,7 @@
 
     mm_flops = seq * drow * 3 * local
     mm_bytes = seq * drow + 6 * drow * local + 3 * seq * local
-    sums = []
+    shares, passed, sums = [], [], []
     for x in (x0, x1):
         parts = kernel_call(
             project_body,
@@ -411,12 +412,14 @@
             flops=mm_flops,
             nbytes=mm_bytes,
         )(x, w)
-        own, right, far, left = (p.reshape(3 * chunk, width) for p in parts)
-        passed = first_hop(far)
-        sums += [own, *second_hop(right, left, *passed)]
-    passed, upstream[2] = lax.optimization_barrier((passed, upstream[2]))
-    upstream[2] = lax.ppermute(upstream[2], "dp", turn[2])
-
+        shares.append([p.reshape(3 * chunk, width) for p in parts])
+        passed.append(first_hop(shares[-1][2]))
+    passed[0], shares[1] = lax.optimization_barrier((passed[0], shares[1]))
+    for (own, right, _, left), came in zip(shares, passed):
+        sums += [own, *second_hop(right, left, *came)]
+
+    partner_far_w = lax.ppermute(far_w, "row", partner)
+    sums, partner_far_w = lax.optimization_barrier((sums, partner_far_w))
     extra = -(-(groups + 3 * nshort) // 16) * 16
     half = pl.BlockSpec((groups, ntaps, 2 * ntaps), lambda i: (0, 0, 0))
     other = pl.BlockSpec((groups, ntaps, 2 * ntaps), lambda i: (1, 0, 0))
@@ -442,42 +445,47 @@
     )(*sums, sf, bands, bands, *upstream)
     *near, near_far_before, near_far_after = gather_over_line(grad_near, False)
     *far, far_far_before, far_far_after = gather_over_line(grad_other, True)
-    part, far_three = kernel_call(
-        first_grad_body,
-        [shaped((ncol, chunk, dcol), F32), shaped((3, 3 * chunk, width), BF16)],
-        scratch=[pltpu.VMEM((ndp, 3 * chunk, width), BF16)],
-        flops=2 * mm_flops,
-        nbytes=2 * mm_bytes,
-    )(*near, *far, w, partner_w)
-    part, mixed = lax.optimization_barrier((part, mixed))
+    near, far = lax.optimization_barrier((near, far))
+    parts = [
+        kernel_call(
+            first_grad_body,
+            shaped((ncol, chunk, dcol), dtype),
+            scratch=[pltpu.VMEM((ndp, 3 * chunk, width), BF16)],
+            flops=mm_flops,
+            nbytes=mm_bytes,
+        )(*pieces, w)
+        for pieces, dtype in ((far, BF16), (near, F32))
+    ]
     for ahead in range(1, ndp):
         mixed[ahead] = lax.ppermute(mixed[ahead], "dp", turn[ahead])
+    from_partner = lax.ppermute(parts[0], "row", partner)
     everywhere = pl.BlockSpec(memory_space=pl.ANY)
     in_vmem = pl.BlockSpec(memory_space=pltpu.VMEM)
     near_last, far_last, *blocks = kernel_call(
         functools.partial(second_grad_body, ndp),
         [shaped(grad_near.shape, BF16), shaped(grad_other.shape, BF16)]
         + [shaped((rows, dcol), BF16)] * len(places),
-        grid=(),
-        in_specs=[everywhere] * 7,
+        in_specs=[everywhere] * 8,
         out_specs=[in_vmem] * (2 + len(places)),
         scratch=[
-            pltpu.VMEM((2, 3, drow, width), BF16),
+            pltpu.VMEM(far_w.shape, BF16),
+            pltpu.VMEM(far_w.shape, BF16),
             pltpu.VMEM((ncol, chunk, dcol), F32),
-            pltpu.SemaphoreType.DMA((5,)),
+            pltpu.VMEM((ncol, chunk, dcol), BF16),
+            pltpu.SemaphoreType.DMA((6,)),
         ],
         flops=mm_flops // 2,
         nbytes=mm_bytes // 2,
         vmem=MOST_VMEM_BYTES,
-    )(part, near_far_before, near_far_after, far_far_before, far_far_after, w, partner_w)
-    far_three, far_last, mixed[1:] = lax.optimization_barrier((far_three, far_last, mixed[1:]))
-    far_three, far_last = (lax.ppermute(part, "row", partner) for part in (far_three, far_last))
+    )(near_far_before, near_far_after, far_far_before, far_far_after, far_w, partner_far_w, parts[1], from_partner)
+    blocks[1], mixed[1:] = lax.optimization_barrier((blocks[1], mixed[1:]))
+    far_last = lax.ppermute(far_last, "row", partner)
     arrivals = [
         lax.ppermute(sent, ("row", "col"), [(b, a) for a, b in offset(*p)])
         for p, sent in zip(places[1:], blocks[1:])
     ]
     arrived = sum((a.astype(F32) for a in arrivals), blocks[0].astype(F32)).astype(BF16)
-    arrived, far_three, far_last = lax.optimization_barrier((arrived, far_three, far_last))
+    arrived, far_last = lax.optimization_barrier((arrived, far_last))
     grad_in = lax.ppermute(arrived, ("dp", "row"), swap_back)
 
     grad_weight, mixed, grad_long, grad_short = kernel_call(
@@ -491,7 +499,7 @@
         grid=(3,),
         in_specs=[whole(nblocks, ncol, rows, dcol)] * 2
         + [whole(*grad_near.shape)] * 4
-        + [whole(*far_three.shape), whole(*far_last.shape)]
+        + [whole(*grad_other.shape)] * 4
         + [whole(rows, width)] * ndp,
         out_specs=[
             pl.BlockSpec((1, drow, local), lambda i: (i, 0, 0)),
@@ -506,7 +514,7 @@
         flops=2 * mm_flops,
         nbytes=2 * mm_bytes,
         vmem=MOST_VMEM_BYTES,
-    )(x0, x1, *near, near_last, far_three, far_last, *mixed)
+    )(x0, x1, *near, near_last, *far, far_last, *mixed)
     grad_weight = jnp.transpose(grad_weight, (1, 0, 2))
     return (mixed, grad_in, grad_weight, grad_long, grad_short)
 

time: 168 us -> 177 us (1.054)
  waiting for transfers between devices: 63.2 us -> 71.2 us
  local copies, waits for them, and re-layouts: 13.7 us -> 16.2 us
  Pallas kernels: 27.4 us -> 25.1 us
  other arithmetic: 2.19 us -> 4.04 us
    ppermute x2, waiting for transfers between devices: 0.01 us -> 12.4 us  [second_hop(): lax.ppermute(right + from_left, 'dp', [(a, (a + 1) % ndp) for a in range(...]
    ppermute x2, starting transfers between devices: 12.7 us -> 1.17 us  [second_hop(): lax.ppermute(left + from_right, 'dp', [(a, (a - 1) % ndp) for a in range(...]
    ppermute x2, waiting for transfers between devices: 0.01 us -> 6.36 us  [second_hop(): lax.ppermute(left + from_right, 'dp', [(a, (a - 1) % ndp) for a in range(...]
    ppermute x14 -> x13, starting transfers between devices: 14.5 us -> 19.7 us  [the longest x2 7.33 us: gather_over_line(): after = lax.ppermute(own, ('dp', 'row'), pairs(range(ndp), -1, False))]
    ppermute x1, waiting for transfers between devices: 7.21 us -> 3.94 us  [move_activations(): upstream[1] = lax.ppermute(upstream[1], 'dp', turn[1])]
    ppermute x3, waiting for transfers between devices: 8.28 us -> 5.51 us  [move_activations(): lax.ppermute(sent, ('row', 'col'), [(b, a) for a, b in offset(*p)])]
    unnamed x63 -> x79, local copies, waits for them, and re-layouts: 13 us -> 15.5 us
    pallas_call x1 -> x3, Pallas kernels: 5.54 us -> 3.05 us  [the longest x2 2.9 us: move_activations(): kernel_call(first_grad_body, shaped((ncol, chunk, dcol), dtype), scratch=...]
  transfers between devices with their start and end apart: 35 -> 34, of which waited for: 14 -> 16; matrix products, arithmetic and copies ran while one was open for 2% -> 3% of each run, Pallas kernels for 13% -> 10%
where the time goes in v14:
time: 177 us; the launch traced here: 176 us
  waiting for transfers between devices  71.2 us (40%)
  starting transfers between devices  58.5 us (33%)
  Pallas kernels  25.1 us (14%)
  local copies, waits for them, and re-layouts  16.2 us (9%)
  other arithmetic  4.04 us (2%)
    unnamed x79, local copies, waits for them, and re-layouts  15.5 us
    ppermute x2, waiting for transfers between devices, gather_over_line(): after = lax.ppermute(own, ('dp', 'row'), pairs(range(ndp), -1, False))  15.4 us
    ppermute x2, waiting for transfers between devices, second_hop(): lax.ppermute(right + from_left, 'dp', [(a, (a + 1) % ndp) for a in range(...  12.4 us
    ppermute x2, waiting for transfers between devices, gather_over_line(): lax.ppermute(after, ('dp', 'row'), pairs(range(1, ndp // 2 + 1), -1, acro...  10.5 us
    ppermute x2, starting transfers between devices, first_hop(): lax.ppermute(far, 'dp', [(a, a + 1) for a in range(ndp // 2)])  9.04 us
    ppermute x2, starting transfers between devices, gather_over_line(): after = lax.ppermute(own, ('dp', 'row'), pairs(range(ndp), -1, False))  7.33 us
    pallas_call x1, Pallas kernels, move_activations(): kernel_call(functools.partial(weight_grad_body, scale), [shaped((3, drow,...  7.03 us
    ppermute x2, waiting for transfers between devices, second_hop(): lax.ppermute(left + from_right, 'dp', [(a, (a - 1) % ndp) for a in range(...  6.36 us
  transfers between devices with their start and end apart: 34, of which 16 were waited for; matrix products, arithmetic and copies ran while one was open for 3% of the time, Pallas kernels for 10%

profile of v14, /device:TPU:1, one launch (start us, length us, event | category | flops | bytes accessed | tf_op | source)
XLA Modules:
  0.0 176.2 jit_solution(96604841294954671)
XLA Ops:
  0.6 4.6 %collective-permute-start = (bf16[192,512]{1,0:T(8,128)(2,1)}, bf16[192,512]{1,0:T(8,128)(2,1)S(1)}, u32[]{:S(2)}, u32[]{:S(2)}) collective-permute-start(bf16[192,512]{1,0:T(8,128)(2,1)} %param.5), channel_id=1, source_target_pairs={{0,0},{16,2},{8,4},{24,6},{2,8},{18,10},{10,12},{26,14},{4,16},{20... | collective-permute-start | bytes 589832 | tf_op jit(solution)/shard_map/ppermute | solution.py:367
  10.1 3.9 %collective-permute-done.1.refs_10_ = bf16[192,128]{1,0:T(8,128)(2,1)S(1)} collective-permute-done((bf16[192,128]{1,0:T(8,128)(2,1)S(1)}, bf16[192,128]{1,0:T(8,128)(2,1)S(1)}, u32[]{:S(2)}, u32[]{:S(2)}) %collective-permute-start.1) | collective-permute-done | bytes 49184 | tf_op jit(solution)/shard_map/ppermute | solution.py:377
  14.1 2.4 %collective-permute-done = bf16[192,512]{1,0:T(8,128)(2,1)S(1)} collective-permute-done((bf16[192,512]{1,0:T(8,128)(2,1)}, bf16[192,512]{1,0:T(8,128)(2,1)S(1)}, u32[]{:S(2)}, u32[]{:S(2)}) %collective-permute-start) | collective-permute-done | bytes 196640 | tf_op jit(solution)/shard_map/ppermute | solution.py:367
  19.1 2.9 %collective-permute-start.2 = (bf16[192,128]{1,0:T(8,128)(2,1)S(1)}, bf16[192,128]{1,0:T(8,128)(2,1)S(1)}, u32[]{:S(2)}, u32[]{:S(2)}) collective-permute-start(bf16[192,128]{1,0:T(8,128)(2,1)S(1)} %get-tuple-element.73), channel_id=1, source_target_pairs={{0,16},{8,24},{16,0},{24,8},{1,17},{9,25},{17,1},{25,9},{2,18},{10... | collective-permute-start | bytes 147464 | tf_op jit(solution)/shard_map/ppermute | solution.py:381
  25.4 2.6 %collective-permute-done.5 = bf16[192,512]{1,0:T(8,128)(2,1)S(1)} collective-permute-done((bf16[192,512]{1,0:T(8,128)(2,1)S(1)}, bf16[192,512]{1,0:T(8,128)(2,1)S(1)}, u32[]{:S(2)}, u32[]{:S(2)}) %collective-permute-start.5) | collective-permute-done | bytes 196640 | tf_op jit(solution)/shard_map/ppermute | solution.py:379
  32.8 4.6 %collective-permute-start.8 = (bf16[1152,128]{1,0:T(8,128)(2,1)S(1)}, bf16[1152,128]{1,0:T(8,128)(2,1)}, u32[]{:S(2)}, u32[]{:S(2)}) collective-permute-start(bf16[1152,128]{1,0:T(8,128)(2,1)S(1)} %bitcast.28), channel_id=1, source_target_pairs={{0,8},{8,16},{1,9},{9,17},{2,10},{10,18},{3,11},{11,19},{4,12},{12... | collective-permute-start | bytes 884744 | tf_op jit(solution)/shard_map/ppermute | solution.py:314
  44.4 4.5 %collective-permute-start.12 = (bf16[1152,128]{1,0:T(8,128)(2,1)S(1)}, bf16[1152,128]{1,0:T(8,128)(2,1)S(1)}, u32[]{:S(2)}, u32[]{:S(2)}) collective-permute-start(bf16[1152,128]{1,0:T(8,128)(2,1)S(1)} %bitcast.30), channel_id=1, source_target_pairs={{0,8},{8,16},{1,9},{9,17},{2,10},{10,18},{3,11},{11,19},{4,12},{12... | collective-permute-start | bytes 884744 | tf_op jit(solution)/shard_map/ppermute | solution.py:314
  55.2 2.3 %collective-permute-start.13 = (bf16[1152,128]{1,0:T(8,128)(2,1)S(1)}, bf16[1152,128]{1,0:T(8,128)(2,1)S(1)}, u32[]{:S(2)}, u32[]{:S(2)}) collective-permute-start(bf16[1152,128]{1,0:T(8,128)(2,1)S(1)} %add.31), channel_id=1, source_target_pairs={{0,8},{8,16},{16,24},{24,0},{1,9},{9,17},{17,25},{25,1},{2,10},{10... | collective-permute-start | bytes 884744 | tf_op jit(solution)/shard_map/ppermute | solution.py:321
  61.7 6.0 %collective-permute-done.10.refs_1_ = bf16[1152,128]{1,0:T(8,128)(2,1)S(1)} collective-permute-done((bf16[1152,128]{1,0:T(8,128)(2,1)S(1)}, bf16[1152,128]{1,0:T(8,128)(2,1)S(1)}, u32[]{:S(2)}, u32[]{:S(2)}) %collective-permute-start.10) | collective-permute-done | bytes 294944 | tf_op jit(solution)/shard_map/ppermute | solution.py:321
  67.8 6.3 %collective-permute-done.13.refs_4_ = bf16[1152,128]{1,0:T(8,128)(2,1)S(1)} collective-permute-done((bf16[1152,128]{1,0:T(8,128)(2,1)S(1)}, bf16[1152,128]{1,0:T(8,128)(2,1)S(1)}, u32[]{:S(2)}, u32[]{:S(2)}) %collective-permute-start.13) | collective-permute-done | bytes 294944 | tf_op jit(solution)/shard_map/ppermute | solution.py:321
  74.1 6.4 %collective-permute-done.15.refs_5_ = bf16[1152,128]{1,0:T(8,128)(2,1)S(1)} collective-permute-done((bf16[1152,128]{1,0:T(8,128)(2,1)S(1)}, bf16[1152,128]{1,0:T(8,128)(2,1)S(1)}, u32[]{:S(2)}, u32[]{:S(2)}) %collective-permute-start.15) | collective-permute-done | bytes 294944 | tf_op jit(solution)/shard_map/ppermute | solution.py:322
  81.2 5.4 %shard_map.97 = (bf16[1184,128]{1,0:T(8,128)(2,1)}, bf16[1152,128]{1,0:T(8,128)(2,1)}, bf16[192,128]{1,0:T(8,128)(2,1)}, bf16[192,128]{1,0:T(8,128)(2,1)}, bf16[...) custom-call(bf16[1152,128]{1,0:T(8,128)(2,1)} %bitcast.31, bf16[1152,128]{1,0:T(8,128)(2,1)} %copy-done.26, ...), custom_call_target="tpu_custom_call" | custom-call | flops 1207959552 | bytes 2752512 | tf_op jit(solution)/shard_map/pallas_call | solution.py:427
  86.6 4.1 %collective-permute-start.18 = (bf16[1184,128]{1,0:T(8,128)(2,1)}, bf16[1184,128]{1,0:T(8,128)(2,1)S(1)}, u32[]{:S(2)}, u32[]{:S(2)}) collective-permute-start(bf16[1184,128]{1,0:T(8,128)(2,1)} %get-tuple-element.104.own.refs_2_), channel_id=1, source_target_pairs={{0,24},{2,26},{4,28},{6,30},{8,0},{10,2},{12,4},{14,6},{16,8},{18,... | collective-permute-start | bytes 909320 | tf_op jit(solution)/shard_map/ppermute | solution.py:337
  90.7 3.3 %collective-permute-start.20 = (bf16[1152,128]{1,0:T(8,128)(2,1)}, bf16[1152,128]{1,0:T(8,128)(2,1)S(1)}, u32[]{:S(2)}, u32[]{:S(2)}) collective-permute-start(bf16[1152,128]{1,0:T(8,128)(2,1)} %get-tuple-element.108.own.refs_6_), channel_id=1, source_target_pairs={{0,24},{2,26},{4,28},{6,30},{8,0},{10,2},{12,4},{14,6},{16,8},{18,... | collective-permute-start | bytes 884744 | tf_op jit(solution)/shard_map/ppermute | solution.py:337
  93.9 15.4 %collective-permute-done.20.after.refs_8_ = bf16[1152,128]{1,0:T(8,128)(2,1)S(1)} collective-permute-done((bf16[1152,128]{1,0:T(8,128)(2,1)}, bf16[1152,128]{1,0:T(8,128)(2,1)S(1)}, u32[]{:S(2)}, u32[]{:S(2)}) %collective-permute-start.20) | collective-permute-done | bytes 294944 | tf_op jit(solution)/shard_map/ppermute | solution.py:337
  109.4 6.3 %collective-permute-done.19.before.refs_7_ = bf16[1152,128]{1,0:T(8,128)(2,1)S(1)} collective-permute-done((bf16[1152,128]{1,0:T(8,128)(2,1)}, bf16[1152,128]{1,0:T(8,128)(2,1)S(1)}, u32[]{:S(2)}, u32[]{:S(2)}) %collective-permute-start.19) | collective-permute-done | bytes 294944 | tf_op jit(solution)/shard_map/ppermute | solution.py:336
  120.2 2.6 %collective-permute-start.25 = (bf16[2,384,512]{2,1,0:T(8,128)(2,1)S(1)}, bf16[2,384,512]{2,1,0:T(8,128)(2,1)}, u32[]{:S(2)}, u32[]{:S(2)}) collective-permute-start(bf16[2,384,512]{2,1,0:T(8,128)(2,1)S(1)} %shard_map.99), channel_id=1, source_target_pairs={{0,2},{2,0},{4,6},{6,4},{1,3},{3,1},{5,7},{7,5},{8,10},{10,8},{12,... | collective-permute-start | bytes 2359304 | tf_op jit(solution)/shard_map/ppermute | solution.py:461
  129.4 10.5 %collective-permute-done.24.refs_3_ = bf16[1152,128]{1,0:T(8,128)(2,1)S(1)} collective-permute-done((bf16[1152,128]{1,0:T(8,128)(2,1)S(1)}, bf16[1152,128]{1,0:T(8,128)(2,1)S(1)}, u32[]{:S(2)}, u32[]{:S(2)}) %collective-permute-start.24) | collective-permute-done | bytes 294944 | tf_op jit(solution)/shard_map/ppermute | solution.py:339
  141.5 3.6 %collective-permute-start.27 = (bf16[192,128]{1,0:T(8,128)(2,1)S(1)}, bf16[192,128]{1,0:T(8,128)(2,1)S(1)}, u32[]{:S(2)}, u32[]{:S(2)}) collective-permute-start(bf16[192,128]{1,0:T(8,128)(2,1)S(1)} %copy-done.34), channel_id=1, source_target_pairs={{0,16},{8,24},{16,0},{24,8},{1,17},{9,25},{17,1},{25,9},{2,18},{10... | collective-permute-start | bytes 147464 | tf_op jit(solution)/shard_map/ppermute | solution.py:460
  146.0 4.8 %shard_map.100 = (bf16[1184,128]{1,0:T(8,128)(2,1)}, bf16[1152,128]{1,0:T(8,128)(2,1)}, bf16[192,512]{1,0:T(8,128)(2,1)}, bf16[192,512]{1,0:T(8,128)(2,1)}, bf16...) custom-call(bf16[1184,128]{1,0:T(8,128)(2,1)} %copy-done.22, bf16[1184,128]{1,0:T(8,128)(2,1)} %copy-done.21, ...), custom_call_target="tpu_custom_call" | custom-call | flops 603979776 | bytes 2555904 | tf_op jit(solution)/shard_map/pallas_call | solution.py:464
  153.6 2.2 %collective-permute-start.32 = (bf16[1152,128]{1,0:T(8,128)(2,1)}, bf16[1152,128]{1,0:T(8,128)(2,1)S(1)}, u32[]{:S(2)}, u32[]{:S(2)}) collective-permute-start(bf16[1152,128]{1,0:T(8,128)(2,1)} %get-tuple-element.120), channel_id=1, source_target_pairs={{0,2},{2,0},{4,6},{6,4},{1,3},{3,1},{5,7},{7,5},{8,10},{10,8},{12,... | collective-permute-start | bytes 884744 | tf_op jit(solution)/shard_map/ppermute | solution.py:482
  157.2 4.0 %collective-permute-done.31 = bf16[192,512]{1,0:T(8,128)(2,1)S(1)} collective-permute-done((bf16[192,512]{1,0:T(8,128)(2,1)}, bf16[192,512]{1,0:T(8,128)(2,1)S(1)}, u32[]{:S(2)}, u32[]{:S(2)}) %collective-permute-start.31) | collective-permute-done | bytes 196640 | tf_op jit(solution)/shard_map/ppermute | solution.py:484
  162.3 5.4 %collective-permute-start.33 = (bf16[192,512]{1,0:T(8,128)(2,1)S(1)}, bf16[192,512]{1,0:T(8,128)(2,1)S(1)}, u32[]{:S(2)}, u32[]{:S(2)}) collective-permute-start(bf16[192,512]{1,0:T(8,128)(2,1)S(1)} %add_convert_fusion), channel_id=1, source_target_pairs={{0,0},{2,16},{4,8},{6,24},{8,2},{10,18},{12,10},{14,26},{16,4},{18... | collective-permute-start | bytes 589832 | tf_op jit(solution)/shard_map/ppermute | solution.py:489
  167.7 7.0 %shard_map.101 = (f32[3,1024,512]{2,1,0:T(8,128)}, bf16[192,512]{1,0:T(8,128)(2,1)}, f32[32,128]{1,0:T(8,128)}, f32[3,3,512]{2,1,0:T(4,128)}) custom-call(bf16[2,2,192,512]{3,2,1,0:T(8,128)(2,1)} %bitcast.24, bf16[2,2,192,512]{3,2,1,0:T(8,128)(2,1)} %copy-done.16, bf16[1184,128]{1,0:T(8,128)(2,1)} %get-tuple-element.104.own.refs_2_, ...), custom_call_target="tpu_custom_call" | custom-call | flops 2415919104 | bytes 10223616 | tf_op jit(solution)/shard_map/pallas_call | solution.py:491
  (146 shorter events, 54.0 us)
Async XLA Ops:
  0.6 15.8 %collective-permute-start = (bf16[192,512]{1,0:T(8,128)(2,1)}, bf16[192,512]{1,0:T(8,128)(2,1)S(1)}, u32[]{:S(2)}, u32[]{:S(2)}) collective-permute-start(bf16[192,512]{1,0:T(8,128)(2,1)} %param.5), channel_id=1, source_target_pairs={{0,0},{16,2},{8,4},{24,6},{2,8},{18,10},{10,12},{26,14},{4,16},{20... | collective-permute-start | bytes 589832 | tf_op jit(solution)/shard_map/ppermute | solution.py:367
  16.8 11.1 %collective-permute-start.5 = (bf16[192,512]{1,0:T(8,128)(2,1)S(1)}, bf16[192,512]{1,0:T(8,128)(2,1)S(1)}, u32[]{:S(2)}, u32[]{:S(2)}) collective-permute-start(bf16[192,512]{1,0:T(8,128)(2,1)S(1)} %collective-permute-done), channel_id=1, source_target_pairs={{0,4},{1,5},{2,6},{3,7},{4,0},{5,1},{6,2},{7,3},{8,12},{9,13},{10,... | collective-permute-start | bytes 589832 | tf_op jit(solution)/shard_map/ppermute | solution.py:379
  28.1 9.6 %collective-permute-start.7 = (bf16[2,2,192,512]{3,2,1,0:T(8,128)(2,1)S(1)}, bf16[2,2,192,512]{3,2,1,0:T(8,128)(2,1)S(1)}, u32[]{:S(2)}, u32[]{:S(2)}) collective-permute-start(bf16[2,2,192,512]{3,2,1,0:T(8,128)(2,1)S(1)} %bitcast.22), channel_id=1, source_target_pairs={{0,2},{2,0},{4,6},{6,4},{1,3},{3,1},{5,7},{7,5},{8,10},{10,8},{12,... | collective-permute-start | bytes 2359304 | tf_op jit(solution)/shard_map/ppermute | solution.py:384
  31.4 17.5 %collective-permute-start.9 = (bf16[1152,128]{1,0:T(8,128)(2,1)S(1)}, bf16[1152,128]{1,0:T(8,128)(2,1)}, u32[]{:S(2)}, u32[]{:S(2)}) collective-permute-start(bf16[1152,128]{1,0:T(8,128)(2,1)S(1)} %bitcast.27), channel_id=1, source_target_pairs={{16,8},{24,16},{17,9},{25,17},{18,10},{26,18},{19,11},{27,19},{20,... | collective-permute-start | bytes 884744 | tf_op jit(solution)/shard_map/ppermute | solution.py:315
  32.8 16.1 %collective-permute-start.8 = (bf16[1152,128]{1,0:T(8,128)(2,1)S(1)}, bf16[1152,128]{1,0:T(8,128)(2,1)}, u32[]{:S(2)}, u32[]{:S(2)}) collective-permute-start(bf16[1152,128]{1,0:T(8,128)(2,1)S(1)} %bitcast.28), channel_id=1, source_target_pairs={{0,8},{8,16},{1,9},{9,17},{2,10},{10,18},{3,11},{11,19},{4,12},{12... | collective-permute-start | bytes 884744 | tf_op jit(solution)/shard_map/ppermute | solution.py:314
  37.3 24.4 %collective-permute-start.16 = (bf16[3,1024,128]{2,1,0:T(8,128)(2,1)S(1)}, bf16[3,1024,128]{2,1,0:T(8,128)(2,1)}, u32[]{:S(2)}, u32[]{:S(2)}) collective-permute-start(bf16[3,1024,128]{2,1,0:T(8,128)(2,1)S(1)} %shard_map.93.refs_4_), channel_id=1, source_target_pairs={{0,2},{2,0},{4,6},{6,4},{1,3},{3,1},{5,7},{7,5},{8,10},{10,8},{12,... | collective-permute-start | bytes 2359304 | tf_op jit(solution)/shard_map/ppermute | solution.py:421
  43.7 13.7 %collective-permute-start.14 = (bf16[1152,128]{1,0:T(8,128)(2,1)S(1)}, bf16[1152,128]{1,0:T(8,128)(2,1)S(1)}, u32[]{:S(2)}, u32[]{:S(2)}) collective-permute-start(bf16[1152,128]{1,0:T(8,128)(2,1)S(1)} %bitcast.29), channel_id=1, source_target_pairs={{16,8},{24,16},{17,9},{25,17},{18,10},{26,18},{19,11},{27,19},{20,... | collective-permute-start | bytes 884744 | tf_op jit(solution)/shard_map/ppermute | solution.py:315
  44.4 10.7 %collective-permute-start.12 = (bf16[1152,128]{1,0:T(8,128)(2,1)S(1)}, bf16[1152,128]{1,0:T(8,128)(2,1)S(1)}, u32[]{:S(2)}, u32[]{:S(2)}) collective-permute-start(bf16[1152,128]{1,0:T(8,128)(2,1)S(1)} %bitcast.30), channel_id=1, source_target_pairs={{0,8},{8,16},{1,9},{9,17},{2,10},{10,18},{3,11},{11,19},{4,12},{12... | collective-permute-start | bytes 884744 | tf_op jit(solution)/shard_map/ppermute | solution.py:314
  49.9 11.8 %collective-permute-start.11 = (bf16[1152,128]{1,0:T(8,128)(2,1)S(1)}, bf16[1152,128]{1,0:T(8,128)(2,1)S(1)}, u32[]{:S(2)}, u32[]{:S(2)}) collective-permute-start(bf16[1152,128]{1,0:T(8,128)(2,1)S(1)} %bitcast_add_fusion), channel_id=1, source_target_pairs={{0,24},{8,0},{16,8},{24,16},{1,25},{9,1},{17,9},{25,17},{2,26},{10... | collective-permute-start | bytes 884744 | tf_op jit(solution)/shard_map/ppermute | solution.py:322
  51.0 16.8 %collective-permute-start.10 = (bf16[1152,128]{1,0:T(8,128)(2,1)S(1)}, bf16[1152,128]{1,0:T(8,128)(2,1)S(1)}, u32[]{:S(2)}, u32[]{:S(2)}) collective-permute-start(bf16[1152,128]{1,0:T(8,128)(2,1)S(1)} %bitcast_add_fusion.1), channel_id=1, source_target_pairs={{0,8},{8,16},{16,24},{24,0},{1,9},{9,17},{17,25},{25,1},{2,10},{10... | collective-permute-start | bytes 884744 | tf_op jit(solution)/shard_map/ppermute | solution.py:321
  55.2 18.9 %collective-permute-start.13 = (bf16[1152,128]{1,0:T(8,128)(2,1)S(1)}, bf16[1152,128]{1,0:T(8,128)(2,1)S(1)}, u32[]{:S(2)}, u32[]{:S(2)}) collective-permute-start(bf16[1152,128]{1,0:T(8,128)(2,1)S(1)} %add.31), channel_id=1, source_target_pairs={{0,8},{8,16},{16,24},{24,0},{1,9},{9,17},{17,25},{25,1},{2,10},{10... | collective-permute-start | bytes 884744 | tf_op jit(solution)/shard_map/ppermute | solution.py:321
  57.5 22.9 %collective-permute-start.15 = (bf16[1152,128]{1,0:T(8,128)(2,1)S(1)}, bf16[1152,128]{1,0:T(8,128)(2,1)S(1)}, u32[]{:S(2)}, u32[]{:S(2)}) collective-permute-start(bf16[1152,128]{1,0:T(8,128)(2,1)S(1)} %add.32), channel_id=1, source_target_pairs={{0,24},{8,0},{16,8},{24,16},{1,25},{9,1},{17,9},{25,17},{2,26},{10... | collective-permute-start | bytes 884744 | tf_op jit(solution)/shard_map/ppermute | solution.py:322
  86.6 29.1 %collective-permute-start.18 = (bf16[1184,128]{1,0:T(8,128)(2,1)}, bf16[1184,128]{1,0:T(8,128)(2,1)S(1)}, u32[]{:S(2)}, u32[]{:S(2)}) collective-permute-start(bf16[1184,128]{1,0:T(8,128)(2,1)} %get-tuple-element.104.own.refs_2_), channel_id=1, source_target_pairs={{0,24},{2,26},{4,28},{6,30},{8,0},{10,2},{12,4},{14,6},{16,8},{18,... | collective-permute-start | bytes 909320 | tf_op jit(solution)/shard_map/ppermute | solution.py:337
  90.7 25.0 %collective-permute-start.17 = (bf16[1184,128]{1,0:T(8,128)(2,1)}, bf16[1184,128]{1,0:T(8,128)(2,1)S(1)}, u32[]{:S(2)}, u32[]{:S(2)}) collective-permute-start(bf16[1184,128]{1,0:T(8,128)(2,1)} %get-tuple-element.104.own.refs_2_), channel_id=1, source_target_pairs={{0,8},{2,10},{4,12},{6,14},{8,16},{10,18},{12,20},{14,22},{16,24},... | collective-permute-start | bytes 909320 | tf_op jit(solution)/shard_map/ppermute | solution.py:336
  90.7 18.7 %collective-permute-start.20 = (bf16[1152,128]{1,0:T(8,128)(2,1)}, bf16[1152,128]{1,0:T(8,128)(2,1)S(1)}, u32[]{:S(2)}, u32[]{:S(2)}) collective-permute-start(bf16[1152,128]{1,0:T(8,128)(2,1)} %get-tuple-element.108.own.refs_6_), channel_id=1, source_target_pairs={{0,24},{2,26},{4,28},{6,30},{8,0},{10,2},{12,4},{14,6},{16,8},{18,... | collective-permute-start | bytes 884744 | tf_op jit(solution)/shard_map/ppermute | solution.py:337
  93.9 21.8 %collective-permute-start.19 = (bf16[1152,128]{1,0:T(8,128)(2,1)}, bf16[1152,128]{1,0:T(8,128)(2,1)S(1)}, u32[]{:S(2)}, u32[]{:S(2)}) collective-permute-start(bf16[1152,128]{1,0:T(8,128)(2,1)} %get-tuple-element.108.own.refs_6_), channel_id=1, source_target_pairs={{0,8},{2,10},{4,12},{6,14},{8,16},{10,18},{12,20},{14,22},{16,24},... | collective-permute-start | bytes 884744 | tf_op jit(solution)/shard_map/ppermute | solution.py:336
  120.2 25.7 %collective-permute-start.25 = (bf16[2,384,512]{2,1,0:T(8,128)(2,1)S(1)}, bf16[2,384,512]{2,1,0:T(8,128)(2,1)}, u32[]{:S(2)}, u32[]{:S(2)}) collective-permute-start(bf16[2,384,512]{2,1,0:T(8,128)(2,1)S(1)} %shard_map.99), channel_id=1, source_target_pairs={{0,2},{2,0},{4,6},{6,4},{1,3},{3,1},{5,7},{7,5},{8,10},{10,8},{12,... | collective-permute-start | bytes 2359304 | tf_op jit(solution)/shard_map/ppermute | solution.py:461
  122.8 22.3 %collective-permute-start.22 = (bf16[1184,128]{1,0:T(8,128)(2,1)S(1)}, bf16[1184,128]{1,0:T(8,128)(2,1)S(1)}, u32[]{:S(2)}, u32[]{:S(2)}) collective-permute-start(bf16[1184,128]{1,0:T(8,128)(2,1)S(1)} %collective-permute-done.18.after.refs_4_), channel_id=1, source_target_pairs={{8,0},{10,2},{12,4},{14,6},{16,8},{18,10},{20,12},{22,14},{9,1},{1... | collective-permute-start | bytes 909320 | tf_op jit(solution)/shard_map/ppermute | solution.py:339
  124.1 21.0 %collective-permute-start.21 = (bf16[1184,128]{1,0:T(8,128)(2,1)S(1)}, bf16[1184,128]{1,0:T(8,128)(2,1)S(1)}, u32[]{:S(2)}, u32[]{:S(2)}) collective-permute-start(bf16[1184,128]{1,0:T(8,128)(2,1)S(1)} %collective-permute-done.17.before.refs_3_), channel_id=1, source_target_pairs={{8,16},{10,18},{12,20},{14,22},{16,24},{18,26},{20,28},{22,30},{9,... | collective-permute-start | bytes 909320 | tf_op jit(solution)/shard_map/ppermute | solution.py:338
  124.8 15.2 %collective-permute-start.24 = (bf16[1152,128]{1,0:T(8,128)(2,1)S(1)}, bf16[1152,128]{1,0:T(8,128)(2,1)S(1)}, u32[]{:S(2)}, u32[]{:S(2)}) collective-permute-start(bf16[1152,128]{1,0:T(8,128)(2,1)S(1)} %collective-permute-done.20.after.refs_8_), channel_id=1, source_target_pairs={{8,2},{10,0},{12,6},{14,4},{16,10},{18,8},{20,14},{22,12},{9,3},{1... | collective-permute-start | bytes 884744 | tf_op jit(solution)/shard_map/ppermute | solution.py:339
  126.1 15.3 %collective-permute-start.23 = (bf16[1152,128]{1,0:T(8,128)(2,1)S(1)}, bf16[1152,128]{1,0:T(8,128)(2,1)S(1)}, u32[]{:S(2)}, u32[]{:S(2)}) collective-permute-start(bf16[1152,128]{1,0:T(8,128)(2,1)S(1)} %collective-permute-done.19.before.refs_7_), channel_id=1, source_target_pairs={{8,18},{10,16},{12,22},{14,20},{16,26},{18,24},{20,30},{22,28},{9,... | collective-permute-start | bytes 884744 | tf_op jit(solution)/shard_map/ppermute | solution.py:338
  140.0 10.8 %collective-permute-start.26 = (bf16[192,128]{1,0:T(8,128)(2,1)S(1)}, bf16[192,128]{1,0:T(8,128)(2,1)S(1)}, u32[]{:S(2)}, u32[]{:S(2)}) collective-permute-start(bf16[192,128]{1,0:T(8,128)(2,1)S(1)} %copy-done.35), channel_id=1, source_target_pairs={{0,8},{8,16},{16,24},{24,0},{1,9},{9,17},{17,25},{25,1},{2,10},{10... | collective-permute-start | bytes 147464 | tf_op jit(solution)/shard_map/ppermute | solution.py:460
  141.5 9.3 %collective-permute-start.27 = (bf16[192,128]{1,0:T(8,128)(2,1)S(1)}, bf16[192,128]{1,0:T(8,128)(2,1)S(1)}, u32[]{:S(2)}, u32[]{:S(2)}) collective-permute-start(bf16[192,128]{1,0:T(8,128)(2,1)S(1)} %copy-done.34), channel_id=1, source_target_pairs={{0,16},{8,24},{16,0},{24,8},{1,17},{9,25},{17,1},{25,9},{2,18},{10... | collective-permute-start | bytes 147464 | tf_op jit(solution)/shard_map/ppermute | solution.py:460
  162.3 13.2 %collective-permute-start.33 = (bf16[192,512]{1,0:T(8,128)(2,1)S(1)}, bf16[192,512]{1,0:T(8,128)(2,1)S(1)}, u32[]{:S(2)}, u32[]{:S(2)}) collective-permute-start(bf16[192,512]{1,0:T(8,128)(2,1)S(1)} %add_convert_fusion), channel_id=1, source_target_pairs={{0,0},{2,16},{4,8},{6,24},{8,2},{10,18},{12,10},{14,26},{16,4},{18... | collective-permute-start | bytes 589832 | tf_op jit(solution)/shard_map/ppermute | solution.py:489
  (49 other events, 481.3 us)

commit v15 on v11

--- a/solution.py
+++ b/solution.py
@@ -80,11 +80,20 @@
         out_ref[0] = held[wrapped(z + ahead, len(out_refs))]
 
 
+def far_columns_body(w_ref, out_ref, sem):
+    ndp = lax.axis_size("dp")
+    width = out_ref.shape[2]
+    start = wrapped(lax.axis_index("dp") + ndp // 2, ndp) * width
+    copy = pltpu.make_async_copy(w_ref.at[:, :, pl.ds(pl.multiple_of(start, width), width)], out_ref, sem)
+    copy.start()
+    copy.wait()
+
+
 def first_grad_body(near, near_before, near_after, far, far_before, far_after, w_ref, partner_w_ref, out_ref, far_ref, held):
     ndp, _, width = held.shape
     ncol, tokens, depth = out_ref.shape
     z, col = lax.axis_index("dp"), lax.axis_index("col")
-    far_ref[0], far_ref[1], far_ref[2] = far[...], far_before[...], far_after[...]
+    far_ref[0], far_ref[1] = far_before[...], far_after[...]
     for pieces, weights, first in (
         ((near, near_before, near_after), w_ref, True),
         ((far, far_before, far_after), partner_w_ref, False),
@@ -107,7 +116,7 @@
 
 
 def second_grad_body(ndp, part_ref, *refs):
-    arrived, weights, refs = (refs[:2], refs[2:4]), refs[4:6], refs[6:]
+    arrived, (w_ref, partner_w_ref), refs = (refs[:2], refs[2:4]), refs[4:6], refs[6:]
     (near_ref, far_ref), refs = refs[:2], refs[2:]
     *out_refs, held_w, held_part, sems = refs
     ncol, tokens, depth = held_part.shape
@@ -116,7 +125,8 @@
     z, col = lax.axis_index("dp"), lax.axis_index("col")
     lanes = pl.ds(pl.multiple_of(wrapped(z + ndp // 2, ndp) * width, width), width)
     copies = [
-        pltpu.make_async_copy(w_ref.at[:, :, lanes], held_w.at[k], sems.at[k]) for k, w_ref in enumerate(weights)
+        pltpu.make_async_copy(w_ref, held_w.at[0], sems.at[0]),
+        pltpu.make_async_copy(partner_w_ref.at[:, :, lanes], held_w.at[1], sems.at[1]),
     ]
     copies.append(pltpu.make_async_copy(part_ref, held_part, sems.at[2]))
     for copy in copies:
@@ -146,13 +156,9 @@
 
 
 def weight_grad_body(scale, *refs):
-    (x0_ref, x1_ref), near_refs, (far_ref, far_last_ref), mixed_refs, refs = (
-        refs[:2],
-        refs[2:6],
-        refs[6:8],
-        refs[8:12],
-        refs[12:],
-    )
+    (x0_ref, x1_ref), near_refs, other_refs, mixed_refs, refs = refs[:2], refs[2:6], refs[6:9], refs[9:13], refs[13:]
+    own_ref, two_ref, last_ref = other_refs
+    other = (own_ref, two_ref.at[0], two_ref.at[1], last_ref)
     out_ref, mixed_ref, long_ref, short_ref, held, held_mixed = refs
     nblocks, ncol, rows, depth = x0_ref.shape
     _, ndp, _, width = held.shape
@@ -166,7 +172,7 @@
         for k, ahead in enumerate((0, -1, 1, 2)):
             owner = wrapped(z + ahead, ndp)
             held[0, owner] = near_refs[k][...]
-            held[1, owner, : 3 * tokens] = far_ref[k] if k < 3 else far_last_ref[...]
+            held[1, owner, : 3 * tokens] = other[k][...]
         for back in range(ndp):
             held_mixed[wrapped(z - back, ndp)] = mixed_refs[back][...]
         for owner in range(ndp):
@@ -365,9 +371,16 @@
 
     w = jnp.transpose(in_weight, (1, 0, 2))
     moved = lax.ppermute(tokens, ("dp", "row"), swap)
+    far_w = kernel_call(
+        far_columns_body,
+        shaped((3, drow, width), BF16),
+        in_specs=[pl.BlockSpec(memory_space=pl.ANY)],
+        out_specs=pl.BlockSpec(memory_space=pltpu.VMEM),
+        scratch=[pltpu.SemaphoreType.DMA],
+    )(w)
     turn = [[(a, (a + ahead) % ndp) for a in range(ndp)] for ahead in range(ndp)]
     upstream = [*kernel_call(split_body, [shaped((rows, width), BF16)] * ndp)(grad_out)]
-    moved, upstream = lax.optimization_barrier((moved, upstream))
+    moved, upstream, far_w = lax.optimization_barrier((moved, upstream, far_w))
     near = [moved] + [lax.ppermute(moved, ("row", "col"), offset(*p)) for p in places[1:]]
     for ahead in (1, 3):
         upstream[ahead] = lax.ppermute(upstream[ahead], "dp", turn[ahead])
@@ -439,9 +452,9 @@
     *near, near_far_before, near_far_after = gather_over_line(grad_near, False)
     *far, far_far_before, far_far_after = gather_over_line(grad_other, True)
     partner_w = lax.ppermute(w, "row", partner)
-    part, far_three = kernel_call(
+    part, far_two = kernel_call(
         first_grad_body,
-        [shaped((ncol, chunk, dcol), F32), shaped((3, 3 * chunk, width), BF16)],
+        [shaped((ncol, chunk, dcol), F32), shaped((2, 3 * chunk, width), BF16)],
         scratch=[pltpu.VMEM((ndp, 3 * chunk, width), BF16)],
         flops=2 * mm_flops,
         nbytes=2 * mm_bytes,
@@ -463,15 +476,15 @@
         flops=mm_flops // 2,
         nbytes=mm_bytes // 2,
         vmem=MOST_VMEM_BYTES,
-    )(part, near_far_before, near_far_after, far_far_before, far_far_after, w, partner_w)
-    far_three, far_last, mixed[1:] = lax.optimization_barrier((far_three, far_last, mixed[1:]))
-    far_three, far_last = (lax.ppermute(part, "row", partner) for part in (far_three, far_last))
+    )(part, near_far_before, near_far_after, far_far_before, far_far_after, far_w, partner_w)
+    far_two, far_last, mixed[1:] = lax.optimization_barrier((far_two, far_last, mixed[1:]))
+    far_two, far_last = (lax.ppermute(part, "row", partner) for part in (far_two, far_last))
     arrivals = [
         lax.ppermute(sent, ("row", "col"), [(b, a) for a, b in offset(*p)])
         for p, sent in zip(places[1:], blocks[1:])
     ]
     arrived = sum((a.astype(F32) for a in arrivals), blocks[0].astype(F32)).astype(BF16)
-    arrived, far_three, far_last = lax.optimization_barrier((arrived, far_three, far_last))
+    arrived, far_two, far_last = lax.optimization_barrier((arrived, far_two, far_last))
     grad_in = lax.ppermute(arrived, ("dp", "row"), swap_back)
 
     grad_weight, mixed, grad_long, grad_short = kernel_call(
@@ -485,7 +498,7 @@
         grid=(3,),
         in_specs=[whole(nblocks, ncol, rows, dcol)] * 2
         + [whole(*grad_near.shape)] * 4
-        + [whole(*far_three.shape), whole(*far_last.shape)]
+        + [whole(*grad_other.shape), whole(*far_two.shape), whole(*far_last.shape)]
         + [whole(rows, width)] * ndp,
         out_specs=[
             pl.BlockSpec((1, drow, local), lambda i: (i, 0, 0)),
@@ -500,7 +513,7 @@
         flops=2 * mm_flops,
         nbytes=2 * mm_bytes,
         vmem=MOST_VMEM_BYTES,
-    )(x0, x1, *near, near_last, far_three, far_last, *mixed)
+    )(x0, x1, *near, near_last, grad_other, far_two, far_last, *mixed)
     grad_weight = jnp.transpose(grad_weight, (1, 0, 2))
     return (mixed, grad_in, grad_weight, grad_long, grad_short)
 

time: 164 us -> 163 us (level)
  waiting for transfers between devices: 59.9 us -> 58.1 us
    ppermute x1, waiting for transfers between devices: 9.2 us -> 6.54 us  [move_activations(): moved = lax.ppermute(tokens, ('dp', 'row'), swap)]
    pallas_call x1 -> x2, Pallas kernels: 5.54 us -> 6.66 us  [the longest x1 5.52 us: move_activations(): kernel_call(first_grad_body, [shaped((ncol, chunk, dcol), F32), shaped((2...]
    unnamed x59 -> x61, local copies, waits for them, and re-layouts: 7.67 us -> 8.39 us
  transfers between devices with their start and end apart: 35 -> 35, of which waited for: 16 -> 17; matrix products, arithmetic and copies ran while one was open for 2% -> 2% of each run, Pallas kernels for 19% -> 20%
where the time goes in v15:
time: 163 us; the launch traced here: 162 us
  starting transfers between devices  59.4 us (36%)
  waiting for transfers between devices  58.1 us (36%)
  Pallas kernels  32.4 us (20%)
  local copies, waits for them, and re-layouts  9.08 us (6%)
  other arithmetic  2.19 us (1%)
    ppermute x2, waiting for transfers between devices, gather_over_line(): before = lax.ppermute(own, ('dp', 'row'), shift(1))  10.3 us
    ppermute x2, waiting for transfers between devices, gather_over_line(): after = lax.ppermute(own, ('dp', 'row'), shift(-1))  10.2 us
    unnamed x61, local copies, waits for them, and re-layouts  8.39 us
    ppermute x2, waiting for transfers between devices, sum_over_line(): lax.ppermute(right + from_left, 'dp', [(a, (a + 1) % ndp) for a in range(...  8.37 us
    ppermute x3, waiting for transfers between devices, move_activations(): lax.ppermute(sent, ('row', 'col'), [(b, a) for a, b in offset(*p)])  8.24 us
    pallas_call x2, Pallas kernels, move_activations(): kernel_call(project_body, [shaped((3, chunk, width), BF16)] * ndp, grid=(...  8.1 us
    ppermute x3, starting transfers between devices, move_activations(): lax.ppermute(part, 'dp', [(a, (a + ahead) % ndp) for a in range(ndp)])  7.22 us
    pallas_call x1, Pallas kernels, move_activations(): kernel_call(functools.partial(weight_grad_body, scale), [shaped((3, drow,...  7.04 us
  transfers between devices with their start and end apart: 35, of which 17 were waited for; matrix products, arithmetic and copies ran while one was open for 2% of the time, Pallas kernels for 20%

profile of v15, /device:TPU:1, one launch (start us, length us, event | category | flops | bytes accessed | tf_op | source)
XLA Modules:
  0.0 162.5 jit_solution(9901864668388600888)
XLA Ops:
  0.6 4.6 %collective-permute-start = (bf16[192,512]{1,0:T(8,128)(2,1)}, bf16[192,512]{1,0:T(8,128)(2,1)S(1)}, u32[]{:S(2)}, u32[]{:S(2)}) collective-permute-start(bf16[192,512]{1,0:T(8,128)(2,1)} %param.5), channel_id=1, source_target_pairs={{0,0},{16,2},{8,4},{24,6},{2,8},{18,10},{10,12},{26,14},{4,16},{20... | collective-permute-start | bytes 589832 | tf_op jit(solution)/shard_map/ppermute | solution.py:373
  8.9 6.5 %collective-permute-done = bf16[192,512]{1,0:T(8,128)(2,1)S(1)} collective-permute-done((bf16[192,512]{1,0:T(8,128)(2,1)}, bf16[192,512]{1,0:T(8,128)(2,1)S(1)}, u32[]{:S(2)}, u32[]{:S(2)}) %collective-permute-start) | collective-permute-done | bytes 196640 | tf_op jit(solution)/shard_map/ppermute | solution.py:373
  15.4 2.7 %collective-permute-start.4 = (bf16[192,512]{1,0:T(8,128)(2,1)S(1)}, bf16[192,512]{1,0:T(8,128)(2,1)S(1)}, u32[]{:S(2)}, u32[]{:S(2)}) collective-permute-start(bf16[192,512]{1,0:T(8,128)(2,1)S(1)} %collective-permute-done), channel_id=1, source_target_pairs={{0,4},{1,5},{2,6},{3,7},{4,0},{5,1},{6,2},{7,3},{8,12},{9,13},{10,... | collective-permute-start | bytes 589832 | tf_op jit(solution)/shard_map/ppermute | solution.py:384
  25.1 4.0 %shard_map.94 = (bf16[3,384,128]{2,1,0:T(8,128)(2,1)S(1)}, bf16[3,384,128]{2,1,0:T(8,128)(2,1)S(1)}, bf16[3,384,128]{2,1,0:T(8,128)(2,1)S(1)}, bf16[3,384,128]{2,1,0:T(8,128)(2,1)S(1)}) custom-call(bf16[2,2,192,512]{3,2,1,0:T(8,128)(2,1)S(1)} %bitcast.20, bf16[3,1024,512]{2,1,0:T(8,128)(2,1)} %bitcast.w_ref), custom_call_target="tpu_custom_call" | custom-call | flops 1207959552 | bytes 5111808 | tf_op jit(solution)/shard_map/pallas_call | solution.py:409
  30.1 6.5 %collective-permute-start.6 = (bf16[192,128]{1,0:T(8,128)(2,1)S(1)}, bf16[192,128]{1,0:T(8,128)(2,1)S(1)}, u32[]{:S(2)}, u32[]{:S(2)}) collective-permute-start(bf16[192,128]{1,0:T(8,128)(2,1)S(1)} %get-tuple-element.66), channel_id=1, source_target_pairs={{0,16},{8,24},{16,0},{24,8},{1,17},{9,25},{17,1},{25,9},{2,18},{10... | collective-permute-start | bytes 147464 | tf_op jit(solution)/shard_map/ppermute | solution.py:390
  40.6 4.1 %collective-permute-done.6.refs_11_ = bf16[192,128]{1,0:T(8,128)(2,1)S(1)} collective-permute-done((bf16[192,128]{1,0:T(8,128)(2,1)S(1)}, bf16[192,128]{1,0:T(8,128)(2,1)S(1)}, u32[]{:S(2)}, u32[]{:S(2)}) %collective-permute-start.6) | collective-permute-done | bytes 49184 | tf_op jit(solution)/shard_map/ppermute | solution.py:390
  45.3 4.1 %shard_map.95 = (bf16[3,384,128]{2,1,0:T(8,128)(2,1)S(1)}, bf16[3,384,128]{2,1,0:T(8,128)(2,1)S(1)}, bf16[3,384,128]{2,1,0:T(8,128)(2,1)S(1)}, bf16[3,384,128]{2,1,0:T(8,128)(2,1)S(1)}) custom-call(bf16[2,2,192,512]{3,2,1,0:T(8,128)(2,1)S(1)} %collective-permute-done.7.x_ref.refs_1_, bf16[3,1024,512]{2,1,0:T(8,128)(2,1)} %bitcast.w_ref), custom_call_target="tpu_custom_call" | custom-call | flops 1207959552 | bytes 5111808 | tf_op jit(solution)/shard_map/pallas_call | solution.py:409
  50.6 4.0 %collective-permute-start.12 = (bf16[1152,128]{1,0:T(8,128)(2,1)S(1)}, bf16[1152,128]{1,0:T(8,128)(2,1)S(1)}, u32[]{:S(2)}, u32[]{:S(2)}) collective-permute-start(bf16[1152,128]{1,0:T(8,128)(2,1)S(1)} %bitcast.25), channel_id=1, source_target_pairs={{0,8},{8,16},{1,9},{9,17},{2,10},{10,18},{3,11},{11,19},{4,12},{12... | collective-permute-start | bytes 884744 | tf_op jit(solution)/shard_map/ppermute | solution.py:324
  54.7 3.3 %collective-permute-start.15 = (bf16[1152,128]{1,0:T(8,128)(2,1)S(1)}, bf16[1152,128]{1,0:T(8,128)(2,1)S(1)}, u32[]{:S(2)}, u32[]{:S(2)}) collective-permute-start(bf16[1152,128]{1,0:T(8,128)(2,1)S(1)} %bitcast_add_fusion), channel_id=1, source_target_pairs={{0,24},{8,0},{16,8},{24,16},{1,25},{9,1},{17,9},{25,17},{2,26},{10... | collective-permute-start | bytes 884744 | tf_op jit(solution)/shard_map/ppermute | solution.py:327
  58.0 3.7 %collective-permute-done.12 = bf16[1152,128]{1,0:T(8,128)(2,1)S(1)} collective-permute-done((bf16[1152,128]{1,0:T(8,128)(2,1)S(1)}, bf16[1152,128]{1,0:T(8,128)(2,1)S(1)}, u32[]{:S(2)}, u32[]{:S(2)}) %collective-permute-start.12) | collective-permute-done | bytes 294944 | tf_op jit(solution)/shard_map/ppermute | solution.py:324
  69.3 8.4 %collective-permute-done.13.refs_4_ = bf16[1152,128]{1,0:T(8,128)(2,1)S(1)} collective-permute-done((bf16[1152,128]{1,0:T(8,128)(2,1)S(1)}, bf16[1152,128]{1,0:T(8,128)(2,1)S(1)}, u32[]{:S(2)}, u32[]{:S(2)}) %collective-permute-start.13) | collective-permute-done | bytes 294944 | tf_op jit(solution)/shard_map/ppermute | solution.py:326
  78.4 5.4 %shard_map.97 = (bf16[1184,128]{1,0:T(8,128)(2,1)}, bf16[1152,128]{1,0:T(8,128)(2,1)}, bf16[192,128]{1,0:T(8,128)(2,1)}, bf16[192,128]{1,0:T(8,128)(2,1)}, bf16[...) custom-call(bf16[1152,128]{1,0:T(8,128)(2,1)} %bitcast.26, bf16[1152,128]{1,0:T(8,128)(2,1)} %copy-done.18, ...), custom_call_target="tpu_custom_call" | custom-call | flops 1207959552 | bytes 2752512 | tf_op jit(solution)/shard_map/pallas_call | solution.py:428
  83.8 3.6 %collective-permute-start.20 = (bf16[1152,128]{1,0:T(8,128)(2,1)}, bf16[1152,128]{1,0:T(8,128)(2,1)S(1)}, u32[]{:S(2)}, u32[]{:S(2)}) collective-permute-start(bf16[1152,128]{1,0:T(8,128)(2,1)} %get-tuple-element.81.refs_6_), channel_id=1, source_target_pairs={{0,26},{2,24},{4,30},{6,28},{8,2},{10,0},{12,6},{14,4},{16,10},{18... | collective-permute-start | bytes 884744 | tf_op jit(solution)/shard_map/ppermute | solution.py:342
  89.2 5.4 %collective-permute-done.20.far_after = bf16[1152,128]{1,0:T(8,128)(2,1)S(1)} collective-permute-done((bf16[1152,128]{1,0:T(8,128)(2,1)}, bf16[1152,128]{1,0:T(8,128)(2,1)S(1)}, u32[]{:S(2)}, u32[]{:S(2)}) %collective-permute-start.20) | collective-permute-done | bytes 294944 | tf_op jit(solution)/shard_map/ppermute | solution.py:342
  96.2 4.9 %collective-permute-done.17.near_after.refs_4_ = bf16[1184,128]{1,0:T(8,128)(2,1)S(1)} collective-permute-done((bf16[1184,128]{1,0:T(8,128)(2,1)}, bf16[1184,128]{1,0:T(8,128)(2,1)S(1)}, u32[]{:S(2)}, u32[]{:S(2)}) %collective-permute-start.17) | collective-permute-done | bytes 303136 | tf_op jit(solution)/shard_map/ppermute | solution.py:342
  102.4 7.5 %collective-permute-done.16.near_before.refs_3_ = bf16[1184,128]{1,0:T(8,128)(2,1)S(1)} collective-permute-done((bf16[1184,128]{1,0:T(8,128)(2,1)}, bf16[1184,128]{1,0:T(8,128)(2,1)S(1)}, u32[]{:S(2)}, u32[]{:S(2)}) %collective-permute-start.16) | collective-permute-done | bytes 303136 | tf_op jit(solution)/shard_map/ppermute | solution.py:341
  110.6 2.8 %collective-permute-done.19.far_before = bf16[1152,128]{1,0:T(8,128)(2,1)S(1)} collective-permute-done((bf16[1152,128]{1,0:T(8,128)(2,1)}, bf16[1152,128]{1,0:T(8,128)(2,1)S(1)}, u32[]{:S(2)}, u32[]{:S(2)}) %collective-permute-start.19) | collective-permute-done | bytes 294944 | tf_op jit(solution)/shard_map/ppermute | solution.py:341
  115.4 4.8 %collective-permute-start.29 = (bf16[192,128]{1,0:T(8,128)(2,1)}, bf16[192,128]{1,0:T(8,128)(2,1)S(1)}, u32[]{:S(2)}, u32[]{:S(2)}) collective-permute-start(bf16[192,128]{1,0:T(8,128)(2,1)} %get-tuple-element.91), channel_id=1, source_target_pairs={{0,8},{8,16},{16,24},{24,0},{1,9},{9,17},{17,25},{25,1},{2,10},{10... | collective-permute-start | bytes 147464 | tf_op jit(solution)/shard_map/ppermute | solution.py:448
  121.2 5.5 %shard_map.98 = (f32[2,384,512]{2,1,0:T(8,128)S(1)}, bf16[2,1152,128]{2,1,0:T(8,128)(2,1)S(1)}) custom-call(bf16[1184,128]{1,0:T(8,128)(2,1)S(1)} %copy-done.7, bf16[1184,128]{1,0:T(8,128)(2,1)S(1)} %collective-permute-done.16.near_before.refs_3_, bf16[1184,128]{1,0:T(8,128)(2,1)S(1)} %collective-permute-done.17.near_after.refs_4_, ...), custom_call_target="tpu_custom_call" | custom-call | flops 2415919104 | bytes 10223616 | tf_op jit(solution)/shard_map/pallas_call | solution.py:455
  131.9 4.5 %shard_map.99 = (bf16[1184,128]{1,0:T(8,128)(2,1)}, bf16[1152,128]{1,0:T(8,128)(2,1)}, bf16[192,512]{1,0:T(8,128)(2,1)}, bf16[192,512]{1,0:T(8,128)(2,1)}, bf16[...) custom-call(f32[2,384,512]{2,1,0:T(8,128)} %copy-done.2, bf16[1184,128]{1,0:T(8,128)(2,1)} %copy-done.14, ...), custom_call_target="tpu_custom_call" | custom-call | flops 603979776 | bytes 2555904 | tf_op jit(solution)/shard_map/pallas_call | solution.py:464
  141.3 3.1 %collective-permute-done.26 = bf16[192,512]{1,0:T(8,128)(2,1)S(1)} collective-permute-done((bf16[192,512]{1,0:T(8,128)(2,1)}, bf16[192,512]{1,0:T(8,128)(2,1)S(1)}, u32[]{:S(2)}, u32[]{:S(2)}) %collective-permute-start.26) | collective-permute-done | bytes 196640 | tf_op jit(solution)/shard_map/ppermute | solution.py:483
  145.3 4.2 %collective-permute-done.28 = bf16[192,512]{1,0:T(8,128)(2,1)S(1)} collective-permute-done((bf16[192,512]{1,0:T(8,128)(2,1)}, bf16[192,512]{1,0:T(8,128)(2,1)S(1)}, u32[]{:S(2)}, u32[]{:S(2)}) %collective-permute-start.28) | collective-permute-done | bytes 196640 | tf_op jit(solution)/shard_map/ppermute | solution.py:483
  150.6 3.8 %collective-permute-start.34 = (bf16[192,512]{1,0:T(8,128)(2,1)S(1)}, bf16[192,512]{1,0:T(8,128)(2,1)S(1)}, u32[]{:S(2)}, u32[]{:S(2)}) collective-permute-start(bf16[192,512]{1,0:T(8,128)(2,1)S(1)} %add_convert_fusion), channel_id=1, source_target_pairs={{0,0},{2,16},{4,8},{6,24},{8,2},{10,18},{12,10},{14,26},{16,4},{18... | collective-permute-start | bytes 589832 | tf_op jit(solution)/shard_map/ppermute | solution.py:488
  154.4 7.0 %shard_map.100 = (f32[3,1024,512]{2,1,0:T(8,128)}, bf16[192,512]{1,0:T(8,128)(2,1)}, f32[32,128]{1,0:T(8,128)}, f32[3,3,512]{2,1,0:T(4,128)}) custom-call(bf16[2,2,192,512]{3,2,1,0:T(8,128)(2,1)} %bitcast.21, bf16[2,2,192,512]{3,2,1,0:T(8,128)(2,1)} %copy-done.6, bf16[1184,128]{1,0:T(8,128)(2,1)} %get-tuple-element.80.near.refs_2_, ...), custom_call_target="tpu_custom_call" | custom-call | flops 2415919104 | bytes 10223616 | tf_op jit(solution)/shard_map/pallas_call | solution.py:490
  (129 shorter events, 46.8 us)
Async XLA Ops:
  0.6 14.8 %collective-permute-start = (bf16[192,512]{1,0:T(8,128)(2,1)}, bf16[192,512]{1,0:T(8,128)(2,1)S(1)}, u32[]{:S(2)}, u32[]{:S(2)}) collective-permute-start(bf16[192,512]{1,0:T(8,128)(2,1)} %param.5), channel_id=1, source_target_pairs={{0,0},{16,2},{8,4},{24,6},{2,8},{18,10},{10,12},{26,14},{4,16},{20... | collective-permute-start | bytes 589832 | tf_op jit(solution)/shard_map/ppermute | solution.py:373
  25.0 20.4 %collective-permute-start.7 = (bf16[2,2,192,512]{3,2,1,0:T(8,128)(2,1)S(1)}, bf16[2,2,192,512]{3,2,1,0:T(8,128)(2,1)S(1)}, u32[]{:S(2)}, u32[]{:S(2)}) collective-permute-start(bf16[2,2,192,512]{3,2,1,0:T(8,128)(2,1)S(1)} %bitcast.19), channel_id=1, source_target_pairs={{0,2},{2,0},{4,6},{6,4},{1,3},{3,1},{5,7},{7,5},{8,10},{10,8},{12,... | collective-permute-start | bytes 2359304 | tf_op jit(solution)/shard_map/ppermute | solution.py:389
  29.8 85.6 %collective-permute-start.21 = (bf16[3,1024,512]{2,1,0:T(8,128)(2,1)}, bf16[3,1024,512]{2,1,0:T(8,128)(2,1)}, u32[]{:S(2)}, u32[]{:S(2)}) collective-permute-start(bf16[3,1024,512]{2,1,0:T(8,128)(2,1)} %bitcast.w_ref), channel_id=1, source_target_pairs={{0,2},{2,0},{4,6},{6,4},{1,3},{3,1},{5,7},{7,5},{8,10},{10,8},{12,... | collective-permute-start | bytes 9437192 | tf_op jit(solution)/shard_map/ppermute | solution.py:454
  30.1 14.6 %collective-permute-start.6 = (bf16[192,128]{1,0:T(8,128)(2,1)S(1)}, bf16[192,128]{1,0:T(8,128)(2,1)S(1)}, u32[]{:S(2)}, u32[]{:S(2)}) collective-permute-start(bf16[192,128]{1,0:T(8,128)(2,1)S(1)} %get-tuple-element.66), channel_id=1, source_target_pairs={{0,16},{8,24},{16,0},{24,8},{1,17},{9,25},{17,1},{25,9},{2,18},{10... | collective-permute-start | bytes 147464 | tf_op jit(solution)/shard_map/ppermute | solution.py:390
  36.6 13.6 %collective-permute-start.8 = (bf16[1152,128]{1,0:T(8,128)(2,1)S(1)}, bf16[1152,128]{1,0:T(8,128)(2,1)S(1)}, u32[]{:S(2)}, u32[]{:S(2)}) collective-permute-start(bf16[1152,128]{1,0:T(8,128)(2,1)S(1)} %bitcast.23), channel_id=1, source_target_pairs={{0,8},{8,16},{1,9},{9,17},{2,10},{10,18},{3,11},{11,19},{4,12},{12... | collective-permute-start | bytes 884744 | tf_op jit(solution)/shard_map/ppermute | solution.py:324
  38.0 29.1 %collective-permute-start.11 = (bf16[1152,128]{1,0:T(8,128)(2,1)S(1)}, bf16[1152,128]{1,0:T(8,128)(2,1)}, u32[]{:S(2)}, u32[]{:S(2)}) collective-permute-start(bf16[1152,128]{1,0:T(8,128)(2,1)S(1)} %bitcast_add_fusion.2), channel_id=1, source_target_pairs={{0,24},{8,0},{16,8},{24,16},{1,25},{9,1},{17,9},{25,17},{2,26},{10... | collective-permute-start | bytes 884744 | tf_op jit(solution)/shard_map/ppermute | solution.py:327
  50.2 16.9 %collective-permute-start.9 = (bf16[1152,128]{1,0:T(8,128)(2,1)S(1)}, bf16[1152,128]{1,0:T(8,128)(2,1)S(1)}, u32[]{:S(2)}, u32[]{:S(2)}) collective-permute-start(bf16[1152,128]{1,0:T(8,128)(2,1)S(1)} %bitcast_add_fusion.3), channel_id=1, source_target_pairs={{0,8},{8,16},{16,24},{24,0},{1,9},{9,17},{17,25},{25,1},{2,10},{10... | collective-permute-start | bytes 884744 | tf_op jit(solution)/shard_map/ppermute | solution.py:326
  50.6 11.1 %collective-permute-start.12 = (bf16[1152,128]{1,0:T(8,128)(2,1)S(1)}, bf16[1152,128]{1,0:T(8,128)(2,1)S(1)}, u32[]{:S(2)}, u32[]{:S(2)}) collective-permute-start(bf16[1152,128]{1,0:T(8,128)(2,1)S(1)} %bitcast.25), channel_id=1, source_target_pairs={{0,8},{8,16},{1,9},{9,17},{2,10},{10,18},{3,11},{11,19},{4,12},{12... | collective-permute-start | bytes 884744 | tf_op jit(solution)/shard_map/ppermute | solution.py:324
  54.7 14.6 %collective-permute-start.15 = (bf16[1152,128]{1,0:T(8,128)(2,1)S(1)}, bf16[1152,128]{1,0:T(8,128)(2,1)S(1)}, u32[]{:S(2)}, u32[]{:S(2)}) collective-permute-start(bf16[1152,128]{1,0:T(8,128)(2,1)S(1)} %bitcast_add_fusion), channel_id=1, source_target_pairs={{0,24},{8,0},{16,8},{24,16},{1,25},{9,1},{17,9},{25,17},{2,26},{10... | collective-permute-start | bytes 884744 | tf_op jit(solution)/shard_map/ppermute | solution.py:327
  61.8 15.9 %collective-permute-start.13 = (bf16[1152,128]{1,0:T(8,128)(2,1)S(1)}, bf16[1152,128]{1,0:T(8,128)(2,1)S(1)}, u32[]{:S(2)}, u32[]{:S(2)}) collective-permute-start(bf16[1152,128]{1,0:T(8,128)(2,1)S(1)} %bitcast_add_fusion.1), channel_id=1, source_target_pairs={{0,8},{8,16},{16,24},{24,0},{1,9},{9,17},{17,25},{25,1},{2,10},{10... | collective-permute-start | bytes 884744 | tf_op jit(solution)/shard_map/ppermute | solution.py:326
  83.8 10.8 %collective-permute-start.20 = (bf16[1152,128]{1,0:T(8,128)(2,1)}, bf16[1152,128]{1,0:T(8,128)(2,1)S(1)}, u32[]{:S(2)}, u32[]{:S(2)}) collective-permute-start(bf16[1152,128]{1,0:T(8,128)(2,1)} %get-tuple-element.81.refs_6_), channel_id=1, source_target_pairs={{0,26},{2,24},{4,30},{6,28},{8,2},{10,0},{12,6},{14,4},{16,10},{18... | collective-permute-start | bytes 884744 | tf_op jit(solution)/shard_map/ppermute | solution.py:342
  87.5 13.6 %collective-permute-start.17 = (bf16[1184,128]{1,0:T(8,128)(2,1)}, bf16[1184,128]{1,0:T(8,128)(2,1)S(1)}, u32[]{:S(2)}, u32[]{:S(2)}) collective-permute-start(bf16[1184,128]{1,0:T(8,128)(2,1)} %get-tuple-element.80.near.refs_2_), channel_id=1, source_target_pairs={{0,24},{2,26},{4,28},{6,30},{8,0},{10,2},{12,4},{14,6},{16,8},{18,... | collective-permute-start | bytes 909320 | tf_op jit(solution)/shard_map/ppermute | solution.py:342
  89.2 20.7 %collective-permute-start.16 = (bf16[1184,128]{1,0:T(8,128)(2,1)}, bf16[1184,128]{1,0:T(8,128)(2,1)S(1)}, u32[]{:S(2)}, u32[]{:S(2)}) collective-permute-start(bf16[1184,128]{1,0:T(8,128)(2,1)} %get-tuple-element.80.near.refs_2_), channel_id=1, source_target_pairs={{0,8},{2,10},{4,12},{6,14},{8,16},{10,18},{12,20},{14,22},{16,24},... | collective-permute-start | bytes 909320 | tf_op jit(solution)/shard_map/ppermute | solution.py:341
  89.2 24.2 %collective-permute-start.19 = (bf16[1152,128]{1,0:T(8,128)(2,1)}, bf16[1152,128]{1,0:T(8,128)(2,1)S(1)}, u32[]{:S(2)}, u32[]{:S(2)}) collective-permute-start(bf16[1152,128]{1,0:T(8,128)(2,1)} %get-tuple-element.81.refs_6_), channel_id=1, source_target_pairs={{0,10},{2,8},{4,14},{6,12},{8,18},{10,16},{12,22},{14,20},{16,26},... | collective-permute-start | bytes 884744 | tf_op jit(solution)/shard_map/ppermute | solution.py:341
  94.6 20.1 %collective-permute-start.18 = (bf16[1152,128]{1,0:T(8,128)(2,1)}, bf16[1152,128]{1,0:T(8,128)(2,1)S(1)}, u32[]{:S(2)}, u32[]{:S(2)}) collective-permute-start(bf16[1152,128]{1,0:T(8,128)(2,1)} %get-tuple-element.81.refs_6_), channel_id=1, source_target_pairs={{0,2},{2,0},{4,6},{6,4},{8,10},{10,8},{12,14},{14,12},{16,18},{18,... | collective-permute-start | bytes 884744 | tf_op jit(solution)/shard_map/ppermute | solution.py:343
  101.1 30.0 %collective-permute-start.23 = (bf16[1184,128]{1,0:T(8,128)(2,1)S(1)}, bf16[1184,128]{1,0:T(8,128)(2,1)S(1)}, u32[]{:S(2)}, u32[]{:S(2)}) collective-permute-start(bf16[1184,128]{1,0:T(8,128)(2,1)S(1)} %collective-permute-done.17.near_after.refs_4_), channel_id=1, source_target_pairs={{8,0},{16,8},{9,1},{17,9},{10,2},{18,10},{11,3},{19,11},{12,4},{20... | collective-permute-start | bytes 909320 | tf_op jit(solution)/shard_map/ppermute | solution.py:345
  109.9 21.2 %collective-permute-start.22 = (bf16[1184,128]{1,0:T(8,128)(2,1)S(1)}, bf16[1184,128]{1,0:T(8,128)(2,1)S(1)}, u32[]{:S(2)}, u32[]{:S(2)}) collective-permute-start(bf16[1184,128]{1,0:T(8,128)(2,1)S(1)} %collective-permute-done.16.near_before.refs_3_), channel_id=1, source_target_pairs={{8,16},{16,24},{9,17},{17,25},{10,18},{18,26},{11,19},{19,27},{12,... | collective-permute-start | bytes 909320 | tf_op jit(solution)/shard_map/ppermute | solution.py:344
  113.4 15.2 %collective-permute-start.25 = (bf16[1152,128]{1,0:T(8,128)(2,1)S(1)}, bf16[1152,128]{1,0:T(8,128)(2,1)S(1)}, u32[]{:S(2)}, u32[]{:S(2)}) collective-permute-start(bf16[1152,128]{1,0:T(8,128)(2,1)S(1)} %collective-permute-done.20.far_after), channel_id=1, source_target_pairs={{8,0},{16,8},{9,1},{17,9},{10,2},{18,10},{11,3},{19,11},{12,4},{20... | collective-permute-start | bytes 884744 | tf_op jit(solution)/shard_map/ppermute | solution.py:345
  114.7 14.0 %collective-permute-start.24 = (bf16[1152,128]{1,0:T(8,128)(2,1)S(1)}, bf16[1152,128]{1,0:T(8,128)(2,1)S(1)}, u32[]{:S(2)}, u32[]{:S(2)}) collective-permute-start(bf16[1152,128]{1,0:T(8,128)(2,1)S(1)} %collective-permute-done.19.far_before), channel_id=1, source_target_pairs={{8,16},{16,24},{9,17},{17,25},{10,18},{18,26},{11,19},{19,27},{12,... | collective-permute-start | bytes 884744 | tf_op jit(solution)/shard_map/ppermute | solution.py:344
  115.4 21.0 %collective-permute-start.29 = (bf16[192,128]{1,0:T(8,128)(2,1)}, bf16[192,128]{1,0:T(8,128)(2,1)S(1)}, u32[]{:S(2)}, u32[]{:S(2)}) collective-permute-start(bf16[192,128]{1,0:T(8,128)(2,1)} %get-tuple-element.91), channel_id=1, source_target_pairs={{0,8},{8,16},{16,24},{24,0},{1,9},{9,17},{17,25},{25,1},{2,10},{10... | collective-permute-start | bytes 147464 | tf_op jit(solution)/shard_map/ppermute | solution.py:448
  136.4 14.1 %collective-permute-start.32 = (bf16[2,1152,128]{2,1,0:T(8,128)(2,1)S(1)}, bf16[2,1152,128]{2,1,0:T(8,128)(2,1)S(1)}, u32[]{:S(2)}, u32[]{:S(2)}) collective-permute-start(bf16[2,1152,128]{2,1,0:T(8,128)(2,1)S(1)} %get-tuple-element.94), channel_id=1, source_target_pairs={{0,2},{2,0},{4,6},{6,4},{1,3},{3,1},{5,7},{7,5},{8,10},{10,8},{12,... | collective-permute-start | bytes 1769480 | tf_op jit(solution)/shard_map/ppermute | solution.py:481
  138.9 10.6 %collective-permute-start.28 = (bf16[192,512]{1,0:T(8,128)(2,1)}, bf16[192,512]{1,0:T(8,128)(2,1)S(1)}, u32[]{:S(2)}, u32[]{:S(2)}) collective-permute-start(bf16[192,512]{1,0:T(8,128)(2,1)} %get-tuple-element.88), channel_id=1, source_target_pairs={{5,0},{4,1},{7,2},{6,3},{1,4},{0,5},{3,6},{2,7},{13,8},{12,9},{15,... | collective-permute-start | bytes 589832 | tf_op jit(solution)/shard_map/ppermute | solution.py:483
  140.4 10.2 %collective-permute-start.33 = (bf16[1152,128]{1,0:T(8,128)(2,1)}, bf16[1152,128]{1,0:T(8,128)(2,1)S(1)}, u32[]{:S(2)}, u32[]{:S(2)}) collective-permute-start(bf16[1152,128]{1,0:T(8,128)(2,1)} %get-tuple-element.95), channel_id=1, source_target_pairs={{0,2},{2,0},{4,6},{6,4},{1,3},{3,1},{5,7},{7,5},{8,10},{10,8},{12,... | collective-permute-start | bytes 884744 | tf_op jit(solution)/shard_map/ppermute | solution.py:481
  150.6 11.2 %collective-permute-start.34 = (bf16[192,512]{1,0:T(8,128)(2,1)S(1)}, bf16[192,512]{1,0:T(8,128)(2,1)S(1)}, u32[]{:S(2)}, u32[]{:S(2)}) collective-permute-start(bf16[192,512]{1,0:T(8,128)(2,1)S(1)} %add_convert_fusion), channel_id=1, source_target_pairs={{0,0},{2,16},{4,8},{6,24},{8,2},{10,18},{12,10},{14,26},{16,4},{18... | collective-permute-start | bytes 589832 | tf_op jit(solution)/shard_map/ppermute | solution.py:488
  (41 other events, 393.3 us)

commit v16 on v15

--- a/solution.py
+++ b/solution.py
@@ -89,30 +89,37 @@
     copy.wait()
 
 
-def first_grad_body(near, near_before, near_after, far, far_before, far_after, w_ref, partner_w_ref, out_ref, far_ref, held):
-    ndp, _, width = held.shape
+def first_grad_body(
+    near, near_before, near_after, far, far_before, far_after, w_ref, partner_w_ref, out_ref, far_ref, held, held_w, sems
+):
+    _, ndp, _, width = held.shape
     ncol, tokens, depth = out_ref.shape
     z, col = lax.axis_index("dp"), lax.axis_index("col")
+    copies = []
+    for dx in range(ncol):
+        start = pl.multiple_of(wrapped(col - dx, ncol) * depth, depth)
+        for k, weights in enumerate((w_ref, partner_w_ref)):
+            copy = pltpu.make_async_copy(weights.at[:, pl.ds(start, depth)], held_w.at[k, dx], sems.at[k, dx])
+            copy.start()
+            copies.append(copy)
     far_ref[0], far_ref[1] = far_before[...], far_after[...]
-    for pieces, weights, first in (
-        ((near, near_before, near_after), w_ref, True),
-        ((far, far_before, far_after), partner_w_ref, False),
-    ):
-        held[wrapped(z + ndp // 2, ndp)] = jnp.zeros(held.shape[1:], BF16)
+    for k, pieces in enumerate(((near, near_before, near_after), (far, far_before, far_after))):
+        held[k, wrapped(z + ndp // 2, ndp)] = jnp.zeros(held.shape[2:], BF16)
         for ahead, piece in zip((0, -1, 1), pieces):
-            held[wrapped(z + ahead, ndp)] = piece[: 3 * tokens]
-        for dx in range(ncol):
-            start = pl.multiple_of(wrapped(col - dx, ncol) * depth, depth)
-            total = jnp.zeros((tokens, depth), F32) if first else out_ref[dx]
+            held[k, wrapped(z + ahead, ndp)] = piece[: 3 * tokens]
+    for dx in range(ncol):
+        total = jnp.zeros((tokens, depth), F32)
+        for k in range(2):
+            copies[2 * dx + k].wait()
             for i in range(3):
                 rows = slice(i * tokens, (i + 1) * tokens)
                 total += lax.dot_general(
-                    jnp.concatenate([held[owner, rows] for owner in range(ndp)], axis=1),
-                    weights[i, pl.ds(start, depth), :],
+                    jnp.concatenate([held[k, owner, rows] for owner in range(ndp)], axis=1),
+                    held_w[k, dx, i],
                     (((1,), (1,)), ((), ())),
                     preferred_element_type=F32,
                 )
-            out_ref[dx] = total
+        out_ref[dx] = total.astype(BF16)
 
 
 def second_grad_body(ndp, part_ref, *refs):
@@ -148,7 +155,7 @@
     for dx in range(ncol):
         start = pl.multiple_of(wrapped(col - dx, ncol) * depth, depth)
         right = jnp.concatenate([held_w[k, i, pl.ds(start, depth), :] for k in range(2) for i in range(3)], axis=1)
-        total = held_part[dx] + lax.dot_general(
+        total = held_part[dx].astype(F32) + lax.dot_general(
             left, right, (((1,), (1,)), ((), ())), preferred_element_type=F32
         )
         for block in range(tokens // rows):
@@ -452,15 +459,21 @@
     *near, near_far_before, near_far_after = gather_over_line(grad_near, False)
     *far, far_far_before, far_far_after = gather_over_line(grad_other, True)
     partner_w = lax.ppermute(w, "row", partner)
+    everywhere = pl.BlockSpec(memory_space=pl.ANY)
+    in_vmem = pl.BlockSpec(memory_space=pltpu.VMEM)
     part, far_two = kernel_call(
         first_grad_body,
-        [shaped((ncol, chunk, dcol), F32), shaped((2, 3 * chunk, width), BF16)],
-        scratch=[pltpu.VMEM((ndp, 3 * chunk, width), BF16)],
+        [shaped((ncol, chunk, dcol), BF16), shaped((2, 3 * chunk, width), BF16)],
+        in_specs=[in_vmem] * 6 + [everywhere] * 2,
+        out_specs=[in_vmem] * 2,
+        scratch=[
+            pltpu.VMEM((2, ndp, 3 * chunk, width), BF16),
+            pltpu.VMEM((2, ncol, 3, dcol, local), BF16),
+            pltpu.SemaphoreType.DMA((2, ncol)),
+        ],
         flops=2 * mm_flops,
         nbytes=2 * mm_bytes,
     )(*near, *far, w, partner_w)
-    everywhere = pl.BlockSpec(memory_space=pl.ANY)
-    in_vmem = pl.BlockSpec(memory_space=pltpu.VMEM)
     near_last, far_last, *blocks = kernel_call(
         functools.partial(second_grad_body, ndp),
         [shaped(grad_near.shape, BF16), shaped(grad_other.shape, BF16)]
@@ -470,7 +483,7 @@
         out_specs=[in_vmem] * (2 + len(places)),
         scratch=[
             pltpu.VMEM((2, 3, drow, width), BF16),
-            pltpu.VMEM((ncol, chunk, dcol), F32),
+            pltpu.VMEM((ncol, chunk, dcol), BF16),
             pltpu.SemaphoreType.DMA((5,)),
         ],
         flops=mm_flops // 2,

time: 163 us -> 163 us (level)
  waiting for transfers between devices: 58.1 us -> 59.9 us
  transfers between devices with their start and end apart: 35 -> 35, of which waited for: 17 -> 17; matrix products, arithmetic and copies ran while one was open for 2% -> 2% of each run, Pallas kernels for 20% -> 19%
where the time goes in v16:
time: 163 us; the launch traced here: 162 us
  waiting for transfers between devices  59.9 us (37%)
  starting transfers between devices  58.8 us (36%)
  Pallas kernels  31.3 us (19%)
  local copies, waits for them, and re-layouts  8.81 us (5%)
  other arithmetic  2.19 us (1%)
    ppermute x2, waiting for transfers between devices, gather_over_line(): before = lax.ppermute(own, ('dp', 'row'), shift(1))  10.3 us
    ppermute x2, waiting for transfers between devices, gather_over_line(): after = lax.ppermute(own, ('dp', 'row'), shift(-1))  10.2 us
    ppermute x2, waiting for transfers between devices, sum_over_line(): lax.ppermute(right + from_left, 'dp', [(a, (a + 1) % ndp) for a in range(...  8.37 us
    ppermute x3, waiting for transfers between devices, move_activations(): lax.ppermute(sent, ('row', 'col'), [(b, a) for a, b in offset(*p)])  8.25 us
    unnamed x61, local copies, waits for them, and re-layouts  8.13 us
    pallas_call x2, Pallas kernels, move_activations(): kernel_call(project_body, [shaped((3, chunk, width), BF16)] * ndp, grid=(...  8.1 us
    ppermute x3, starting transfers between devices, move_activations(): lax.ppermute(part, 'dp', [(a, (a + ahead) % ndp) for a in range(ndp)])  7.22 us
    pallas_call x1, Pallas kernels, move_activations(): kernel_call(functools.partial(weight_grad_body, scale), [shaped((3, drow,...  7.04 us
  transfers between devices with their start and end apart: 35, of which 17 were waited for; matrix products, arithmetic and copies ran while one was open for 2% of the time, Pallas kernels for 19%

profile of v16, /device:TPU:1, one launch (start us, length us, event | category | flops | bytes accessed | tf_op | source)
XLA Modules:
  0.0 162.1 jit_solution(15730590219220664212)
XLA Ops:
  0.6 4.6 %collective-permute-start = (bf16[192,512]{1,0:T(8,128)(2,1)}, bf16[192,512]{1,0:T(8,128)(2,1)S(1)}, u32[]{:S(2)}, u32[]{:S(2)}) collective-permute-start(bf16[192,512]{1,0:T(8,128)(2,1)} %param.5), channel_id=1, source_target_pairs={{0,0},{16,2},{8,4},{24,6},{2,8},{18,10},{10,12},{26,14},{4,16},{20... | collective-permute-start | bytes 589832 | tf_op jit(solution)/shard_map/ppermute | solution.py:380
  8.9 6.5 %collective-permute-done = bf16[192,512]{1,0:T(8,128)(2,1)S(1)} collective-permute-done((bf16[192,512]{1,0:T(8,128)(2,1)}, bf16[192,512]{1,0:T(8,128)(2,1)S(1)}, u32[]{:S(2)}, u32[]{:S(2)}) %collective-permute-start) | collective-permute-done | bytes 196640 | tf_op jit(solution)/shard_map/ppermute | solution.py:380
  15.4 2.7 %collective-permute-start.4 = (bf16[192,512]{1,0:T(8,128)(2,1)S(1)}, bf16[192,512]{1,0:T(8,128)(2,1)S(1)}, u32[]{:S(2)}, u32[]{:S(2)}) collective-permute-start(bf16[192,512]{1,0:T(8,128)(2,1)S(1)} %collective-permute-done), channel_id=1, source_target_pairs={{0,4},{1,5},{2,6},{3,7},{4,0},{5,1},{6,2},{7,3},{8,12},{9,13},{10,... | collective-permute-start | bytes 589832 | tf_op jit(solution)/shard_map/ppermute | solution.py:391
  25.1 4.0 %shard_map.94 = (bf16[3,384,128]{2,1,0:T(8,128)(2,1)S(1)}, bf16[3,384,128]{2,1,0:T(8,128)(2,1)S(1)}, bf16[3,384,128]{2,1,0:T(8,128)(2,1)S(1)}, bf16[3,384,128]{2,1,0:T(8,128)(2,1)S(1)}) custom-call(bf16[2,2,192,512]{3,2,1,0:T(8,128)(2,1)S(1)} %bitcast.20, bf16[3,1024,512]{2,1,0:T(8,128)(2,1)} %bitcast.w_ref), custom_call_target="tpu_custom_call" | custom-call | flops 1207959552 | bytes 5111808 | tf_op jit(solution)/shard_map/pallas_call | solution.py:416
  30.1 6.5 %collective-permute-start.6 = (bf16[192,128]{1,0:T(8,128)(2,1)S(1)}, bf16[192,128]{1,0:T(8,128)(2,1)S(1)}, u32[]{:S(2)}, u32[]{:S(2)}) collective-permute-start(bf16[192,128]{1,0:T(8,128)(2,1)S(1)} %get-tuple-element.66), channel_id=1, source_target_pairs={{0,16},{8,24},{16,0},{24,8},{1,17},{9,25},{17,1},{25,9},{2,18},{10... | collective-permute-start | bytes 147464 | tf_op jit(solution)/shard_map/ppermute | solution.py:397
  40.6 4.1 %collective-permute-done.6.refs_11_ = bf16[192,128]{1,0:T(8,128)(2,1)S(1)} collective-permute-done((bf16[192,128]{1,0:T(8,128)(2,1)S(1)}, bf16[192,128]{1,0:T(8,128)(2,1)S(1)}, u32[]{:S(2)}, u32[]{:S(2)}) %collective-permute-start.6) | collective-permute-done | bytes 49184 | tf_op jit(solution)/shard_map/ppermute | solution.py:397
  45.3 4.1 %shard_map.95 = (bf16[3,384,128]{2,1,0:T(8,128)(2,1)S(1)}, bf16[3,384,128]{2,1,0:T(8,128)(2,1)S(1)}, bf16[3,384,128]{2,1,0:T(8,128)(2,1)S(1)}, bf16[3,384,128]{2,1,0:T(8,128)(2,1)S(1)}) custom-call(bf16[2,2,192,512]{3,2,1,0:T(8,128)(2,1)S(1)} %collective-permute-done.7.x_ref.refs_1_, bf16[3,1024,512]{2,1,0:T(8,128)(2,1)} %bitcast.w_ref), custom_call_target="tpu_custom_call" | custom-call | flops 1207959552 | bytes 5111808 | tf_op jit(solution)/shard_map/pallas_call | solution.py:416
  50.6 4.0 %collective-permute-start.12 = (bf16[1152,128]{1,0:T(8,128)(2,1)S(1)}, bf16[1152,128]{1,0:T(8,128)(2,1)S(1)}, u32[]{:S(2)}, u32[]{:S(2)}) collective-permute-start(bf16[1152,128]{1,0:T(8,128)(2,1)S(1)} %bitcast.25), channel_id=1, source_target_pairs={{0,8},{8,16},{1,9},{9,17},{2,10},{10,18},{3,11},{11,19},{4,12},{12... | collective-permute-start | bytes 884744 | tf_op jit(solution)/shard_map/ppermute | solution.py:331
  54.7 3.3 %collective-permute-start.15 = (bf16[1152,128]{1,0:T(8,128)(2,1)S(1)}, bf16[1152,128]{1,0:T(8,128)(2,1)S(1)}, u32[]{:S(2)}, u32[]{:S(2)}) collective-permute-start(bf16[1152,128]{1,0:T(8,128)(2,1)S(1)} %bitcast_add_fusion), channel_id=1, source_target_pairs={{0,24},{8,0},{16,8},{24,16},{1,25},{9,1},{17,9},{25,17},{2,26},{10... | collective-permute-start | bytes 884744 | tf_op jit(solution)/shard_map/ppermute | solution.py:334
  58.0 3.7 %collective-permute-done.12 = bf16[1152,128]{1,0:T(8,128)(2,1)S(1)} collective-permute-done((bf16[1152,128]{1,0:T(8,128)(2,1)S(1)}, bf16[1152,128]{1,0:T(8,128)(2,1)S(1)}, u32[]{:S(2)}, u32[]{:S(2)}) %collective-permute-start.12) | collective-permute-done | bytes 294944 | tf_op jit(solution)/shard_map/ppermute | solution.py:331
  69.3 8.4 %collective-permute-done.13.refs_4_ = bf16[1152,128]{1,0:T(8,128)(2,1)S(1)} collective-permute-done((bf16[1152,128]{1,0:T(8,128)(2,1)S(1)}, bf16[1152,128]{1,0:T(8,128)(2,1)S(1)}, u32[]{:S(2)}, u32[]{:S(2)}) %collective-permute-start.13) | collective-permute-done | bytes 294944 | tf_op jit(solution)/shard_map/ppermute | solution.py:333
  78.4 5.4 %shard_map.97 = (bf16[1184,128]{1,0:T(8,128)(2,1)}, bf16[1152,128]{1,0:T(8,128)(2,1)}, bf16[192,128]{1,0:T(8,128)(2,1)}, bf16[192,128]{1,0:T(8,128)(2,1)}, bf16[...) custom-call(bf16[1152,128]{1,0:T(8,128)(2,1)} %bitcast.26, bf16[1152,128]{1,0:T(8,128)(2,1)} %copy-done.18, ...), custom_call_target="tpu_custom_call" | custom-call | flops 1207959552 | bytes 2752512 | tf_op jit(solution)/shard_map/pallas_call | solution.py:435
  83.8 3.6 %collective-permute-start.20 = (bf16[1152,128]{1,0:T(8,128)(2,1)}, bf16[1152,128]{1,0:T(8,128)(2,1)S(1)}, u32[]{:S(2)}, u32[]{:S(2)}) collective-permute-start(bf16[1152,128]{1,0:T(8,128)(2,1)} %get-tuple-element.81.refs_6_), channel_id=1, source_target_pairs={{0,26},{2,24},{4,30},{6,28},{8,2},{10,0},{12,6},{14,4},{16,10},{18... | collective-permute-start | bytes 884744 | tf_op jit(solution)/shard_map/ppermute | solution.py:349
  89.2 5.4 %collective-permute-done.20.far_after = bf16[1152,128]{1,0:T(8,128)(2,1)S(1)} collective-permute-done((bf16[1152,128]{1,0:T(8,128)(2,1)}, bf16[1152,128]{1,0:T(8,128)(2,1)S(1)}, u32[]{:S(2)}, u32[]{:S(2)}) %collective-permute-start.20) | collective-permute-done | bytes 294944 | tf_op jit(solution)/shard_map/ppermute | solution.py:349
  96.2 4.9 %collective-permute-done.17.near_after.refs_4_ = bf16[1184,128]{1,0:T(8,128)(2,1)S(1)} collective-permute-done((bf16[1184,128]{1,0:T(8,128)(2,1)}, bf16[1184,128]{1,0:T(8,128)(2,1)S(1)}, u32[]{:S(2)}, u32[]{:S(2)}) %collective-permute-start.17) | collective-permute-done | bytes 303136 | tf_op jit(solution)/shard_map/ppermute | solution.py:349
  102.4 7.5 %collective-permute-done.16.near_before.refs_3_ = bf16[1184,128]{1,0:T(8,128)(2,1)S(1)} collective-permute-done((bf16[1184,128]{1,0:T(8,128)(2,1)}, bf16[1184,128]{1,0:T(8,128)(2,1)S(1)}, u32[]{:S(2)}, u32[]{:S(2)}) %collective-permute-start.16) | collective-permute-done | bytes 303136 | tf_op jit(solution)/shard_map/ppermute | solution.py:348
  110.6 2.8 %collective-permute-done.19.far_before = bf16[1152,128]{1,0:T(8,128)(2,1)S(1)} collective-permute-done((bf16[1152,128]{1,0:T(8,128)(2,1)}, bf16[1152,128]{1,0:T(8,128)(2,1)S(1)}, u32[]{:S(2)}, u32[]{:S(2)}) %collective-permute-start.19) | collective-permute-done | bytes 294944 | tf_op jit(solution)/shard_map/ppermute | solution.py:348
  115.4 4.8 %collective-permute-start.29 = (bf16[192,128]{1,0:T(8,128)(2,1)}, bf16[192,128]{1,0:T(8,128)(2,1)S(1)}, u32[]{:S(2)}, u32[]{:S(2)}) collective-permute-start(bf16[192,128]{1,0:T(8,128)(2,1)} %get-tuple-element.91), channel_id=1, source_target_pairs={{0,8},{8,16},{16,24},{24,0},{1,9},{9,17},{17,25},{25,1},{2,10},{10... | collective-permute-start | bytes 147464 | tf_op jit(solution)/shard_map/ppermute | solution.py:455
  121.2 4.6 %shard_map.98 = (bf16[2,384,512]{2,1,0:T(8,128)(2,1)S(1)}, bf16[2,1152,128]{2,1,0:T(8,128)(2,1)S(1)}) custom-call(bf16[1184,128]{1,0:T(8,128)(2,1)S(1)} %copy-done.7, bf16[1184,128]{1,0:T(8,128)(2,1)S(1)} %collective-permute-done.16.near_before.refs_3_, bf16[1184,128]{1,0:T(8,128)(2,1)S(1)} %collective-permute-done.17.near_after.refs_4_, ...), custom_call_target="tpu_custom_call" | custom-call | flops 2415919104 | bytes 10223616 | tf_op jit(solution)/shard_map/pallas_call | solution.py:464
  131.9 4.3 %shard_map.99 = (bf16[1184,128]{1,0:T(8,128)(2,1)}, bf16[1152,128]{1,0:T(8,128)(2,1)}, bf16[192,512]{1,0:T(8,128)(2,1)}, bf16[192,512]{1,0:T(8,128)(2,1)}, bf16[...) custom-call(bf16[2,384,512]{2,1,0:T(8,128)(2,1)} %copy-done.4, bf16[1184,128]{1,0:T(8,128)(2,1)} %copy-done.14, ...), custom_call_target="tpu_custom_call" | custom-call | flops 603979776 | bytes 2555904 | tf_op jit(solution)/shard_map/pallas_call | solution.py:477
  140.9 3.1 %collective-permute-done.26 = bf16[192,512]{1,0:T(8,128)(2,1)S(1)} collective-permute-done((bf16[192,512]{1,0:T(8,128)(2,1)}, bf16[192,512]{1,0:T(8,128)(2,1)S(1)}, u32[]{:S(2)}, u32[]{:S(2)}) %collective-permute-start.26) | collective-permute-done | bytes 196640 | tf_op jit(solution)/shard_map/ppermute | solution.py:496
  144.9 4.2 %collective-permute-done.28 = bf16[192,512]{1,0:T(8,128)(2,1)S(1)} collective-permute-done((bf16[192,512]{1,0:T(8,128)(2,1)}, bf16[192,512]{1,0:T(8,128)(2,1)S(1)}, u32[]{:S(2)}, u32[]{:S(2)}) %collective-permute-start.28) | collective-permute-done | bytes 196640 | tf_op jit(solution)/shard_map/ppermute | solution.py:496
  150.2 3.2 %collective-permute-start.34 = (bf16[192,512]{1,0:T(8,128)(2,1)S(1)}, bf16[192,512]{1,0:T(8,128)(2,1)S(1)}, u32[]{:S(2)}, u32[]{:S(2)}) collective-permute-start(bf16[192,512]{1,0:T(8,128)(2,1)S(1)} %add_convert_fusion), channel_id=1, source_target_pairs={{0,0},{2,16},{4,8},{6,24},{8,2},{10,18},{12,10},{14,26},{16,4},{18... | collective-permute-start | bytes 589832 | tf_op jit(solution)/shard_map/ppermute | solution.py:501
  153.5 7.0 %shard_map.100 = (f32[3,1024,512]{2,1,0:T(8,128)}, bf16[192,512]{1,0:T(8,128)(2,1)}, f32[32,128]{1,0:T(8,128)}, f32[3,3,512]{2,1,0:T(4,128)}) custom-call(bf16[2,2,192,512]{3,2,1,0:T(8,128)(2,1)} %bitcast.21, bf16[2,2,192,512]{3,2,1,0:T(8,128)(2,1)} %copy-done.6, bf16[1184,128]{1,0:T(8,128)(2,1)} %get-tuple-element.80.near.refs_2_, ...), custom_call_target="tpu_custom_call" | custom-call | flops 2415919104 | bytes 10223616 | tf_op jit(solution)/shard_map/pallas_call | solution.py:503
  (129 shorter events, 48.1 us)
Async XLA Ops:
  0.6 14.8 %collective-permute-start = (bf16[192,512]{1,0:T(8,128)(2,1)}, bf16[192,512]{1,0:T(8,128)(2,1)S(1)}, u32[]{:S(2)}, u32[]{:S(2)}) collective-permute-start(bf16[192,512]{1,0:T(8,128)(2,1)} %param.5), channel_id=1, source_target_pairs={{0,0},{16,2},{8,4},{24,6},{2,8},{18,10},{10,12},{26,14},{4,16},{20... | collective-permute-start | bytes 589832 | tf_op jit(solution)/shard_map/ppermute | solution.py:380
  25.0 20.4 %collective-permute-start.7 = (bf16[2,2,192,512]{3,2,1,0:T(8,128)(2,1)S(1)}, bf16[2,2,192,512]{3,2,1,0:T(8,128)(2,1)S(1)}, u32[]{:S(2)}, u32[]{:S(2)}) collective-permute-start(bf16[2,2,192,512]{3,2,1,0:T(8,128)(2,1)S(1)} %bitcast.19), channel_id=1, source_target_pairs={{0,2},{2,0},{4,6},{6,4},{1,3},{3,1},{5,7},{7,5},{8,10},{10,8},{12,... | collective-permute-start | bytes 2359304 | tf_op jit(solution)/shard_map/ppermute | solution.py:396
  29.8 85.6 %collective-permute-start.21 = (bf16[3,1024,512]{2,1,0:T(8,128)(2,1)}, bf16[3,1024,512]{2,1,0:T(8,128)(2,1)}, u32[]{:S(2)}, u32[]{:S(2)}) collective-permute-start(bf16[3,1024,512]{2,1,0:T(8,128)(2,1)} %bitcast.w_ref), channel_id=1, source_target_pairs={{0,2},{2,0},{4,6},{6,4},{1,3},{3,1},{5,7},{7,5},{8,10},{10,8},{12,... | collective-permute-start | bytes 9437192 | tf_op jit(solution)/shard_map/ppermute | solution.py:461
  30.1 14.6 %collective-permute-start.6 = (bf16[192,128]{1,0:T(8,128)(2,1)S(1)}, bf16[192,128]{1,0:T(8,128)(2,1)S(1)}, u32[]{:S(2)}, u32[]{:S(2)}) collective-permute-start(bf16[192,128]{1,0:T(8,128)(2,1)S(1)} %get-tuple-element.66), channel_id=1, source_target_pairs={{0,16},{8,24},{16,0},{24,8},{1,17},{9,25},{17,1},{25,9},{2,18},{10... | collective-permute-start | bytes 147464 | tf_op jit(solution)/shard_map/ppermute | solution.py:397
  36.6 13.6 %collective-permute-start.8 = (bf16[1152,128]{1,0:T(8,128)(2,1)S(1)}, bf16[1152,128]{1,0:T(8,128)(2,1)S(1)}, u32[]{:S(2)}, u32[]{:S(2)}) collective-permute-start(bf16[1152,128]{1,0:T(8,128)(2,1)S(1)} %bitcast.23), channel_id=1, source_target_pairs={{0,8},{8,16},{1,9},{9,17},{2,10},{10,18},{3,11},{11,19},{4,12},{12... | collective-permute-start | bytes 884744 | tf_op jit(solution)/shard_map/ppermute | solution.py:331
  38.0 29.1 %collective-permute-start.11 = (bf16[1152,128]{1,0:T(8,128)(2,1)S(1)}, bf16[1152,128]{1,0:T(8,128)(2,1)}, u32[]{:S(2)}, u32[]{:S(2)}) collective-permute-start(bf16[1152,128]{1,0:T(8,128)(2,1)S(1)} %bitcast_add_fusion.2), channel_id=1, source_target_pairs={{0,24},{8,0},{16,8},{24,16},{1,25},{9,1},{17,9},{25,17},{2,26},{10... | collective-permute-start | bytes 884744 | tf_op jit(solution)/shard_map/ppermute | solution.py:334
  50.2 16.9 %collective-permute-start.9 = (bf16[1152,128]{1,0:T(8,128)(2,1)S(1)}, bf16[1152,128]{1,0:T(8,128)(2,1)S(1)}, u32[]{:S(2)}, u32[]{:S(2)}) collective-permute-start(bf16[1152,128]{1,0:T(8,128)(2,1)S(1)} %bitcast_add_fusion.3), channel_id=1, source_target_pairs={{0,8},{8,16},{16,24},{24,0},{1,9},{9,17},{17,25},{25,1},{2,10},{10... | collective-permute-start | bytes 884744 | tf_op jit(solution)/shard_map/ppermute | solution.py:333
  50.6 11.1 %collective-permute-start.12 = (bf16[1152,128]{1,0:T(8,128)(2,1)S(1)}, bf16[1152,128]{1,0:T(8,128)(2,1)S(1)}, u32[]{:S(2)}, u32[]{:S(2)}) collective-permute-start(bf16[1152,128]{1,0:T(8,128)(2,1)S(1)} %bitcast.25), channel_id=1, source_target_pairs={{0,8},{8,16},{1,9},{9,17},{2,10},{10,18},{3,11},{11,19},{4,12},{12... | collective-permute-start | bytes 884744 | tf_op jit(solution)/shard_map/ppermute | solution.py:331
  54.7 14.6 %collective-permute-start.15 = (bf16[1152,128]{1,0:T(8,128)(2,1)S(1)}, bf16[1152,128]{1,0:T(8,128)(2,1)S(1)}, u32[]{:S(2)}, u32[]{:S(2)}) collective-permute-start(bf16[1152,128]{1,0:T(8,128)(2,1)S(1)} %bitcast_add_fusion), channel_id=1, source_target_pairs={{0,24},{8,0},{16,8},{24,16},{1,25},{9,1},{17,9},{25,17},{2,26},{10... | collective-permute-start | bytes 884744 | tf_op jit(solution)/shard_map/ppermute | solution.py:334
  61.8 15.9 %collective-permute-start.13 = (bf16[1152,128]{1,0:T(8,128)(2,1)S(1)}, bf16[1152,128]{1,0:T(8,128)(2,1)S(1)}, u32[]{:S(2)}, u32[]{:S(2)}) collective-permute-start(bf16[1152,128]{1,0:T(8,128)(2,1)S(1)} %bitcast_add_fusion.1), channel_id=1, source_target_pairs={{0,8},{8,16},{16,24},{24,0},{1,9},{9,17},{17,25},{25,1},{2,10},{10... | collective-permute-start | bytes 884744 | tf_op jit(solution)/shard_map/ppermute | solution.py:333
  83.8 10.8 %collective-permute-start.20 = (bf16[1152,128]{1,0:T(8,128)(2,1)}, bf16[1152,128]{1,0:T(8,128)(2,1)S(1)}, u32[]{:S(2)}, u32[]{:S(2)}) collective-permute-start(bf16[1152,128]{1,0:T(8,128)(2,1)} %get-tuple-element.81.refs_6_), channel_id=1, source_target_pairs={{0,26},{2,24},{4,30},{6,28},{8,2},{10,0},{12,6},{14,4},{16,10},{18... | collective-permute-start | bytes 884744 | tf_op jit(solution)/shard_map/ppermute | solution.py:349
  87.5 13.6 %collective-permute-start.17 = (bf16[1184,128]{1,0:T(8,128)(2,1)}, bf16[1184,128]{1,0:T(8,128)(2,1)S(1)}, u32[]{:S(2)}, u32[]{:S(2)}) collective-permute-start(bf16[1184,128]{1,0:T(8,128)(2,1)} %get-tuple-element.80.near.refs_2_), channel_id=1, source_target_pairs={{0,24},{2,26},{4,28},{6,30},{8,0},{10,2},{12,4},{14,6},{16,8},{18,... | collective-permute-start | bytes 909320 | tf_op jit(solution)/shard_map/ppermute | solution.py:349
  89.2 20.7 %collective-permute-start.16 = (bf16[1184,128]{1,0:T(8,128)(2,1)}, bf16[1184,128]{1,0:T(8,128)(2,1)S(1)}, u32[]{:S(2)}, u32[]{:S(2)}) collective-permute-start(bf16[1184,128]{1,0:T(8,128)(2,1)} %get-tuple-element.80.near.refs_2_), channel_id=1, source_target_pairs={{0,8},{2,10},{4,12},{6,14},{8,16},{10,18},{12,20},{14,22},{16,24},... | collective-permute-start | bytes 909320 | tf_op jit(solution)/shard_map/ppermute | solution.py:348
  89.2 24.2 %collective-permute-start.19 = (bf16[1152,128]{1,0:T(8,128)(2,1)}, bf16[1152,128]{1,0:T(8,128)(2,1)S(1)}, u32[]{:S(2)}, u32[]{:S(2)}) collective-permute-start(bf16[1152,128]{1,0:T(8,128)(2,1)} %get-tuple-element.81.refs_6_), channel_id=1, source_target_pairs={{0,10},{2,8},{4,14},{6,12},{8,18},{10,16},{12,22},{14,20},{16,26},... | collective-permute-start | bytes 884744 | tf_op jit(solution)/shard_map/ppermute | solution.py:348
  94.6 20.1 %collective-permute-start.18 = (bf16[1152,128]{1,0:T(8,128)(2,1)}, bf16[1152,128]{1,0:T(8,128)(2,1)S(1)}, u32[]{:S(2)}, u32[]{:S(2)}) collective-permute-start(bf16[1152,128]{1,0:T(8,128)(2,1)} %get-tuple-element.81.refs_6_), channel_id=1, source_target_pairs={{0,2},{2,0},{4,6},{6,4},{8,10},{10,8},{12,14},{14,12},{16,18},{18,... | collective-permute-start | bytes 884744 | tf_op jit(solution)/shard_map/ppermute | solution.py:350
  101.1 30.0 %collective-permute-start.23 = (bf16[1184,128]{1,0:T(8,128)(2,1)S(1)}, bf16[1184,128]{1,0:T(8,128)(2,1)S(1)}, u32[]{:S(2)}, u32[]{:S(2)}) collective-permute-start(bf16[1184,128]{1,0:T(8,128)(2,1)S(1)} %collective-permute-done.17.near_after.refs_4_), channel_id=1, source_target_pairs={{8,0},{16,8},{9,1},{17,9},{10,2},{18,10},{11,3},{19,11},{12,4},{20... | collective-permute-start | bytes 909320 | tf_op jit(solution)/shard_map/ppermute | solution.py:352
  109.9 21.2 %collective-permute-start.22 = (bf16[1184,128]{1,0:T(8,128)(2,1)S(1)}, bf16[1184,128]{1,0:T(8,128)(2,1)S(1)}, u32[]{:S(2)}, u32[]{:S(2)}) collective-permute-start(bf16[1184,128]{1,0:T(8,128)(2,1)S(1)} %collective-permute-done.16.near_before.refs_3_), channel_id=1, source_target_pairs={{8,16},{16,24},{9,17},{17,25},{10,18},{18,26},{11,19},{19,27},{12,... | collective-permute-start | bytes 909320 | tf_op jit(solution)/shard_map/ppermute | solution.py:351
  113.4 15.2 %collective-permute-start.25 = (bf16[1152,128]{1,0:T(8,128)(2,1)S(1)}, bf16[1152,128]{1,0:T(8,128)(2,1)S(1)}, u32[]{:S(2)}, u32[]{:S(2)}) collective-permute-start(bf16[1152,128]{1,0:T(8,128)(2,1)S(1)} %collective-permute-done.20.far_after), channel_id=1, source_target_pairs={{8,0},{16,8},{9,1},{17,9},{10,2},{18,10},{11,3},{19,11},{12,4},{20... | collective-permute-start | bytes 884744 | tf_op jit(solution)/shard_map/ppermute | solution.py:352
  114.7 14.0 %collective-permute-start.24 = (bf16[1152,128]{1,0:T(8,128)(2,1)S(1)}, bf16[1152,128]{1,0:T(8,128)(2,1)S(1)}, u32[]{:S(2)}, u32[]{:S(2)}) collective-permute-start(bf16[1152,128]{1,0:T(8,128)(2,1)S(1)} %collective-permute-done.19.far_before), channel_id=1, source_target_pairs={{8,16},{16,24},{9,17},{17,25},{10,18},{18,26},{11,19},{19,27},{12,... | collective-permute-start | bytes 884744 | tf_op jit(solution)/shard_map/ppermute | solution.py:351
  115.4 20.8 %collective-permute-start.29 = (bf16[192,128]{1,0:T(8,128)(2,1)}, bf16[192,128]{1,0:T(8,128)(2,1)S(1)}, u32[]{:S(2)}, u32[]{:S(2)}) collective-permute-start(bf16[192,128]{1,0:T(8,128)(2,1)} %get-tuple-element.91), channel_id=1, source_target_pairs={{0,8},{8,16},{16,24},{24,0},{1,9},{9,17},{17,25},{25,1},{2,10},{10... | collective-permute-start | bytes 147464 | tf_op jit(solution)/shard_map/ppermute | solution.py:455
  136.2 14.0 %collective-permute-start.32 = (bf16[2,1152,128]{2,1,0:T(8,128)(2,1)S(1)}, bf16[2,1152,128]{2,1,0:T(8,128)(2,1)S(1)}, u32[]{:S(2)}, u32[]{:S(2)}) collective-permute-start(bf16[2,1152,128]{2,1,0:T(8,128)(2,1)S(1)} %get-tuple-element.94), channel_id=1, source_target_pairs={{0,2},{2,0},{4,6},{6,4},{1,3},{3,1},{5,7},{7,5},{8,10},{10,8},{12,... | collective-permute-start | bytes 1769480 | tf_op jit(solution)/shard_map/ppermute | solution.py:494
  138.6 10.6 %collective-permute-start.28 = (bf16[192,512]{1,0:T(8,128)(2,1)}, bf16[192,512]{1,0:T(8,128)(2,1)S(1)}, u32[]{:S(2)}, u32[]{:S(2)}) collective-permute-start(bf16[192,512]{1,0:T(8,128)(2,1)} %get-tuple-element.88), channel_id=1, source_target_pairs={{5,0},{4,1},{7,2},{6,3},{1,4},{0,5},{3,6},{2,7},{13,8},{12,9},{15,... | collective-permute-start | bytes 589832 | tf_op jit(solution)/shard_map/ppermute | solution.py:496
  140.0 10.2 %collective-permute-start.33 = (bf16[1152,128]{1,0:T(8,128)(2,1)}, bf16[1152,128]{1,0:T(8,128)(2,1)S(1)}, u32[]{:S(2)}, u32[]{:S(2)}) collective-permute-start(bf16[1152,128]{1,0:T(8,128)(2,1)} %get-tuple-element.95), channel_id=1, source_target_pairs={{0,2},{2,0},{4,6},{6,4},{1,3},{3,1},{5,7},{7,5},{8,10},{10,8},{12,... | collective-permute-start | bytes 884744 | tf_op jit(solution)/shard_map/ppermute | solution.py:494
  150.2 11.2 %collective-permute-start.34 = (bf16[192,512]{1,0:T(8,128)(2,1)S(1)}, bf16[192,512]{1,0:T(8,128)(2,1)S(1)}, u32[]{:S(2)}, u32[]{:S(2)}) collective-permute-start(bf16[192,512]{1,0:T(8,128)(2,1)S(1)} %add_convert_fusion), channel_id=1, source_target_pairs={{0,0},{2,16},{4,8},{6,24},{8,2},{10,18},{12,10},{14,26},{16,4},{18... | collective-permute-start | bytes 589832 | tf_op jit(solution)/shard_map/ppermute | solution.py:501
  (41 other events, 387.7 us)

commit v17 on v16

--- a/solution.py
+++ b/solution.py
@@ -162,47 +162,60 @@
             out_refs[block * ncol + dx][...] = total[block * rows : (block + 1) * rows].astype(BF16)
 
 
-def weight_grad_body(scale, *refs):
-    (x0_ref, x1_ref), near_refs, other_refs, mixed_refs, refs = refs[:2], refs[2:6], refs[6:9], refs[9:13], refs[13:]
-    own_ref, two_ref, last_ref = other_refs
-    other = (own_ref, two_ref.at[0], two_ref.at[1], last_ref)
-    out_ref, mixed_ref, long_ref, short_ref, held, held_mixed = refs
-    nblocks, ncol, rows, depth = x0_ref.shape
-    _, ndp, _, width = held.shape
-    tokens = nblocks * rows
-    i = pl.program_id(0)
-    z, col = lax.axis_index("dp"), lax.axis_index("col")
-
-    @pl.when(i == 0)
+def weight_products(x_ref, held, at, ncol):
+    ndp = held.shape[0]
+    nblocks, _, rows, depth = x_ref.shape
+    col = lax.axis_index("col")
+    gm = jnp.concatenate([held[owner, at, :] for owner in range(ndp)], axis=1)
+    for dx in range(ncol):
+        start = pl.multiple_of(wrapped(col - dx, ncol) * depth, depth)
+        x = x_ref[:, dx].reshape(nblocks * rows, depth)
+        yield pl.ds(start, depth), lax.dot_general(x, gm, (((0,), (0,)), ((), ())), preferred_element_type=F32)
+
+
+def own_weight_grad_body(x_ref, *refs):
+    pieces, (out_ref, long_ref, short_ref, held) = refs[:4], refs[4:]
+    ndp, _, width = held.shape
+    tokens = x_ref.shape[0] * x_ref.shape[2]
+    z = lax.axis_index("dp")
+
+    @pl.when(pl.program_id(0) == 0)
     def _():
         groups = long_ref.shape[0] // ndp
-        for k, ahead in enumerate((0, -1, 1, 2)):
-            owner = wrapped(z + ahead, ndp)
-            held[0, owner] = near_refs[k][...]
-            held[1, owner, : 3 * tokens] = other[k][...]
+        nshort, three, _ = short_ref.shape
+        for piece, ahead in zip(pieces, (0, -1, 1, 2)):
+            held[wrapped(z + ahead, ndp)] = piece[...]
+        for owner in range(ndp):
+            lanes = slice(owner * width, (owner + 1) * width)
+            small = held[owner, 3 * tokens :].astype(F32)
+            long_ref[owner * groups : (owner + 1) * groups] = small[:groups]
+            for j in range(nshort):
+                short_ref[j, :, lanes] = small[groups + three * j : groups + three * (j + 1)]
+
+    at = pl.ds(pl.multiple_of(pl.program_id(0) * tokens, 16), tokens)
+    for place, product in weight_products(x_ref, held, at, x_ref.shape[1]):
+        out_ref[0, place, :] = product.astype(BF16)
+
+
+def weight_grad_body(scale, x_ref, part_ref, *refs):
+    (own_ref, two_ref, last_ref), mixed_refs, refs = refs[:3], refs[3:7], refs[7:]
+    out_ref, mixed_ref, held, held_mixed = refs
+    ndp, _, width = held.shape
+    tokens = x_ref.shape[0] * x_ref.shape[2]
+    z = lax.axis_index("dp")
+
+    @pl.when(pl.program_id(0) == 0)
+    def _():
+        for piece, ahead in zip((own_ref, two_ref.at[0], two_ref.at[1], last_ref), (0, -1, 1, 2)):
+            held[wrapped(z + ahead, ndp)] = piece[...]
         for back in range(ndp):
             held_mixed[wrapped(z - back, ndp)] = mixed_refs[back][...]
         for owner in range(ndp):
-            lanes = slice(owner * width, (owner + 1) * width)
-            mixed_ref[:, lanes] = held_mixed[owner]
-            small = held[0, owner, 3 * tokens :].astype(F32)
-            long_ref[owner * groups : (owner + 1) * groups] = small[:groups]
-            nshort, three, _ = short_ref.shape
-            for j in range(nshort):
-                short_ref[j, :, lanes] = small[groups + three * j : groups + three * (j + 1)]
-
-    at = pl.ds(pl.multiple_of(i * tokens, 16), tokens)
-    gm = jnp.concatenate(
-        [jnp.concatenate([held[k, owner, at, :] for owner in range(ndp)], axis=1) for k in range(2)], axis=0
-    )
-    for dx in range(ncol):
-        start = pl.multiple_of(wrapped(col - dx, ncol) * depth, depth)
-        x = jnp.concatenate(
-            [x_ref[:, dx].reshape(tokens, depth) for x_ref in (x0_ref, x1_ref)], axis=0
-        )
-        out_ref[0, pl.ds(start, depth), :] = scale * lax.dot_general(
-            x, gm, (((0,), (0,)), ((), ())), preferred_element_type=F32
-        )
+            mixed_ref[:, owner * width : (owner + 1) * width] = held_mixed[owner]
+
+    at = pl.ds(pl.multiple_of(pl.program_id(0) * tokens, 16), tokens)
+    for place, product in weight_products(x_ref, held, at, x_ref.shape[1]):
+        out_ref[0, place, :] = scale * (part_ref[0, place, :].astype(F32) + product)
 
 
 def delayed(values, count):
@@ -497,36 +510,34 @@
         for p, sent in zip(places[1:], blocks[1:])
     ]
     arrived = sum((a.astype(F32) for a in arrivals), blocks[0].astype(F32)).astype(BF16)
-    arrived, far_two, far_last = lax.optimization_barrier((arrived, far_two, far_last))
+    one_of_three = pl.BlockSpec((1, drow, local), lambda i: (i, 0, 0))
+    own_part, grad_long, grad_short = kernel_call(
+        own_weight_grad_body,
+        [shaped((3, drow, local), BF16), shaped((ngroups, ntaps), F32), shaped((nshort, 3, local), F32)],
+        grid=(3,),
+        in_specs=[whole(nblocks, ncol, rows, dcol)] + [whole(*grad_near.shape)] * 4,
+        out_specs=[one_of_three, whole(ngroups, ntaps), whole(nshort, 3, local)],
+        scratch=[pltpu.VMEM((ndp, 3 * chunk + extra, width), BF16)],
+        flops=mm_flops,
+        nbytes=mm_bytes,
+        vmem=MOST_VMEM_BYTES,
+    )(x0, *near, near_last)
+    arrived, far_two, far_last, own_part = lax.optimization_barrier((arrived, far_two, far_last, own_part))
     grad_in = lax.ppermute(arrived, ("dp", "row"), swap_back)
 
-    grad_weight, mixed, grad_long, grad_short = kernel_call(
+    grad_weight, mixed = kernel_call(
         functools.partial(weight_grad_body, scale),
-        [
-            shaped((3, drow, local), F32),
-            shaped((rows, local), BF16),
-            shaped((ngroups, ntaps), F32),
-            shaped((nshort, 3, local), F32),
-        ],
+        [shaped((3, drow, local), F32), shaped((rows, local), BF16)],
         grid=(3,),
-        in_specs=[whole(nblocks, ncol, rows, dcol)] * 2
-        + [whole(*grad_near.shape)] * 4
+        in_specs=[whole(nblocks, ncol, rows, dcol), one_of_three]
         + [whole(*grad_other.shape), whole(*far_two.shape), whole(*far_last.shape)]
         + [whole(rows, width)] * ndp,
-        out_specs=[
-            pl.BlockSpec((1, drow, local), lambda i: (i, 0, 0)),
-            whole(rows, local),
-            whole(ngroups, ntaps),
-            whole(nshort, 3, local),
-        ],
-        scratch=[
-            pltpu.VMEM((2, ndp, 3 * chunk + extra, width), BF16),
-            pltpu.VMEM((ndp, rows, width), BF16),
-        ],
-        flops=2 * mm_flops,
-        nbytes=2 * mm_bytes,
+        out_specs=[one_of_three, whole(rows, local)],
+        scratch=[pltpu.VMEM((ndp, 3 * chunk, width), BF16), pltpu.VMEM((ndp, rows, width), BF16)],
+        flops=mm_flops,
+        nbytes=mm_bytes,
         vmem=MOST_VMEM_BYTES,
-    )(x0, x1, *near, near_last, grad_other, far_two, far_last, *mixed)
+    )(x1, own_part, grad_other, far_two, far_last, *mixed)
     grad_weight = jnp.transpose(grad_weight, (1, 0, 2))
     return (mixed, grad_in, grad_weight, grad_long, grad_short)
 

time: 163 us -> 163 us (level)
  waiting for transfers between devices: 59.9 us -> 53.8 us
  Pallas kernels: 31.3 us -> 36.2 us
    ppermute x3, waiting for transfers between devices: 8.25 us -> 2.3 us  [move_activations(): lax.ppermute(sent, ('row', 'col'), [(b, a) for a, b in offset(*p)])]
    pallas_call x0 -> x1, Pallas kernels: none -> 5.01 us  [move_activations(): kernel_call(own_weight_grad_body, [shaped((3, drow, local), BF16), shaped...]
    unnamed x61 -> x63, local copies, waits for them, and re-layouts: 8.13 us -> 8.12 us
  transfers between devices with their start and end apart: 35 -> 35, of which waited for: 17 -> 15; matrix products, arithmetic and copies ran while one was open for 2% -> 2% of each run, Pallas kernels for 19% -> 22%
where the time goes in v17:
time: 163 us
  starting transfers between devices  59.8 us (37%)
  waiting for transfers between devices  53.8 us (33%)
  Pallas kernels  36.2 us (22%)
  local copies, waits for them, and re-layouts  8.8 us (5%)
  other arithmetic  2.96 us (2%)
    ppermute x2, waiting for transfers between devices, gather_over_line(): before = lax.ppermute(own, ('dp', 'row'), shift(1))  10.3 us
    ppermute x2, waiting for transfers between devices, gather_over_line(): after = lax.ppermute(own, ('dp', 'row'), shift(-1))  10.2 us
    ppermute x2, waiting for transfers between devices, sum_over_line(): lax.ppermute(right + from_left, 'dp', [(a, (a + 1) % ndp) for a in range(...  8.35 us
    unnamed x63, local copies, waits for them, and re-layouts  8.12 us
    pallas_call x2, Pallas kernels, move_activations(): kernel_call(project_body, [shaped((3, chunk, width), BF16)] * ndp, grid=(...  8.1 us
    ppermute x3, starting transfers between devices, move_activations(): lax.ppermute(part, 'dp', [(a, (a + ahead) % ndp) for a in range(ndp)])  7.22 us
    pallas_call x1, Pallas kernels, move_activations(): kernel_call(functools.partial(weight_grad_body, scale), [shaped((3, drow,...  6.86 us
    ppermute x1, waiting for transfers between devices, move_activations(): moved = lax.ppermute(tokens, ('dp', 'row'), swap)  6.56 us
  transfers between devices with their start and end apart: 35, of which 15 were waited for; matrix products, arithmetic and copies ran while one was open for 2% of the time, Pallas kernels for 22%

profile of v17, /device:TPU:1, one launch (start us, length us, event | category | flops | bytes accessed | tf_op | source)
XLA Modules:
  0.0 162.6 jit_solution(8487980046748727590)
XLA Ops:
  0.6 4.6 %collective-permute-start = (bf16[192,512]{1,0:T(8,128)(2,1)}, bf16[192,512]{1,0:T(8,128)(2,1)S(1)}, u32[]{:S(2)}, u32[]{:S(2)}) collective-permute-start(bf16[192,512]{1,0:T(8,128)(2,1)} %param.5), channel_id=1, source_target_pairs={{0,0},{16,2},{8,4},{24,6},{2,8},{18,10},{10,12},{26,14},{4,16},{20... | collective-permute-start | bytes 589832 | tf_op jit(solution)/shard_map/ppermute | solution.py:393
  8.9 6.6 %collective-permute-done = bf16[192,512]{1,0:T(8,128)(2,1)S(1)} collective-permute-done((bf16[192,512]{1,0:T(8,128)(2,1)}, bf16[192,512]{1,0:T(8,128)(2,1)S(1)}, u32[]{:S(2)}, u32[]{:S(2)}) %collective-permute-start) | collective-permute-done | bytes 196640 | tf_op jit(solution)/shard_map/ppermute | solution.py:393
  15.4 2.7 %collective-permute-start.5 = (bf16[192,512]{1,0:T(8,128)(2,1)S(1)}, bf16[192,512]{1,0:T(8,128)(2,1)S(1)}, u32[]{:S(2)}, u32[]{:S(2)}) collective-permute-start(bf16[192,512]{1,0:T(8,128)(2,1)S(1)} %collective-permute-done), channel_id=1, source_target_pairs={{0,4},{1,5},{2,6},{3,7},{4,0},{5,1},{6,2},{7,3},{8,12},{9,13},{10,... | collective-permute-start | bytes 589832 | tf_op jit(solution)/shard_map/ppermute | solution.py:404
  25.1 4.0 %shard_map.94 = (bf16[3,384,128]{2,1,0:T(8,128)(2,1)S(1)}, bf16[3,384,128]{2,1,0:T(8,128)(2,1)S(1)}, bf16[3,384,128]{2,1,0:T(8,128)(2,1)S(1)}, bf16[3,384,128]{2,1,0:T(8,128)(2,1)S(1)}) custom-call(bf16[2,2,192,512]{3,2,1,0:T(8,128)(2,1)S(1)} %bitcast.20, bf16[3,1024,512]{2,1,0:T(8,128)(2,1)} %bitcast.w_ref), custom_call_target="tpu_custom_call" | custom-call | flops 1207959552 | bytes 5111808 | tf_op jit(solution)/shard_map/pallas_call | solution.py:429
  30.1 6.5 %collective-permute-start.1 = (bf16[192,128]{1,0:T(8,128)(2,1)S(1)}, bf16[192,128]{1,0:T(8,128)(2,1)S(1)}, u32[]{:S(2)}, u32[]{:S(2)}) collective-permute-start(bf16[192,128]{1,0:T(8,128)(2,1)S(1)} %get-tuple-element.62), channel_id=1, source_target_pairs={{0,16},{8,24},{16,0},{24,8},{1,17},{9,25},{17,1},{25,9},{2,18},{10... | collective-permute-start | bytes 147464 | tf_op jit(solution)/shard_map/ppermute | solution.py:410
  38.0 2.7 %collective-permute-start.11 = (bf16[1152,128]{1,0:T(8,128)(2,1)S(1)}, bf16[1152,128]{1,0:T(8,128)(2,1)}, u32[]{:S(2)}, u32[]{:S(2)}) collective-permute-start(bf16[1152,128]{1,0:T(8,128)(2,1)S(1)} %bitcast_add_fusion.2), channel_id=1, source_target_pairs={{0,24},{8,0},{16,8},{24,16},{1,25},{9,1},{17,9},{25,17},{2,26},{10... | collective-permute-start | bytes 884744 | tf_op jit(solution)/shard_map/ppermute | solution.py:347
  40.6 4.1 %collective-permute-done.1.refs_11_ = bf16[192,128]{1,0:T(8,128)(2,1)S(1)} collective-permute-done((bf16[192,128]{1,0:T(8,128)(2,1)S(1)}, bf16[192,128]{1,0:T(8,128)(2,1)S(1)}, u32[]{:S(2)}, u32[]{:S(2)}) %collective-permute-start.1) | collective-permute-done | bytes 49184 | tf_op jit(solution)/shard_map/ppermute | solution.py:410
  45.3 4.1 %shard_map.95 = (bf16[3,384,128]{2,1,0:T(8,128)(2,1)S(1)}, bf16[3,384,128]{2,1,0:T(8,128)(2,1)S(1)}, bf16[3,384,128]{2,1,0:T(8,128)(2,1)S(1)}, bf16[3,384,128]{2,1,0:T(8,128)(2,1)S(1)}) custom-call(bf16[2,2,192,512]{3,2,1,0:T(8,128)(2,1)S(1)} %collective-permute-done.7.x_ref, bf16[3,1024,512]{2,1,0:T(8,128)(2,1)} %bitcast.w_ref), custom_call_target="tpu_custom_call" | custom-call | flops 1207959552 | bytes 5111808 | tf_op jit(solution)/shard_map/pallas_call | solution.py:429
  50.6 4.0 %collective-permute-start.12 = (bf16[1152,128]{1,0:T(8,128)(2,1)S(1)}, bf16[1152,128]{1,0:T(8,128)(2,1)S(1)}, u32[]{:S(2)}, u32[]{:S(2)}) collective-permute-start(bf16[1152,128]{1,0:T(8,128)(2,1)S(1)} %bitcast.25), channel_id=1, source_target_pairs={{0,8},{8,16},{1,9},{9,17},{2,10},{10,18},{3,11},{11,19},{4,12},{12... | collective-permute-start | bytes 884744 | tf_op jit(solution)/shard_map/ppermute | solution.py:344
  54.7 3.3 %collective-permute-start.15 = (bf16[1152,128]{1,0:T(8,128)(2,1)S(1)}, bf16[1152,128]{1,0:T(8,128)(2,1)S(1)}, u32[]{:S(2)}, u32[]{:S(2)}) collective-permute-start(bf16[1152,128]{1,0:T(8,128)(2,1)S(1)} %bitcast_add_fusion), channel_id=1, source_target_pairs={{0,24},{8,0},{16,8},{24,16},{1,25},{9,1},{17,9},{25,17},{2,26},{10... | collective-permute-start | bytes 884744 | tf_op jit(solution)/shard_map/ppermute | solution.py:347
  58.0 3.6 %collective-permute-done.12 = bf16[1152,128]{1,0:T(8,128)(2,1)S(1)} collective-permute-done((bf16[1152,128]{1,0:T(8,128)(2,1)S(1)}, bf16[1152,128]{1,0:T(8,128)(2,1)S(1)}, u32[]{:S(2)}, u32[]{:S(2)}) %collective-permute-start.12) | collective-permute-done | bytes 294944 | tf_op jit(solution)/shard_map/ppermute | solution.py:344
  69.3 8.3 %collective-permute-done.13.refs_4_ = bf16[1152,128]{1,0:T(8,128)(2,1)S(1)} collective-permute-done((bf16[1152,128]{1,0:T(8,128)(2,1)S(1)}, bf16[1152,128]{1,0:T(8,128)(2,1)S(1)}, u32[]{:S(2)}, u32[]{:S(2)}) %collective-permute-start.13) | collective-permute-done | bytes 294944 | tf_op jit(solution)/shard_map/ppermute | solution.py:346
  78.4 5.4 %shard_map.97 = (bf16[1184,128]{1,0:T(8,128)(2,1)}, bf16[1152,128]{1,0:T(8,128)(2,1)}, bf16[192,128]{1,0:T(8,128)(2,1)}, bf16[192,128]{1,0:T(8,128)(2,1)}, bf16[...) custom-call(bf16[1152,128]{1,0:T(8,128)(2,1)} %bitcast.26, bf16[1152,128]{1,0:T(8,128)(2,1)} %copy-done.23, ...), custom_call_target="tpu_custom_call" | custom-call | flops 1207959552 | bytes 2752512 | tf_op jit(solution)/shard_map/pallas_call | solution.py:448
  83.8 3.6 %collective-permute-start.20 = (bf16[1152,128]{1,0:T(8,128)(2,1)}, bf16[1152,128]{1,0:T(8,128)(2,1)S(1)}, u32[]{:S(2)}, u32[]{:S(2)}) collective-permute-start(bf16[1152,128]{1,0:T(8,128)(2,1)} %get-tuple-element.83.refs_0_), channel_id=1, source_target_pairs={{0,26},{2,24},{4,30},{6,28},{8,2},{10,0},{12,6},{14,4},{16,10},{18... | collective-permute-start | bytes 884744 | tf_op jit(solution)/shard_map/ppermute | solution.py:362
  89.2 5.4 %collective-permute-done.20.far_after = bf16[1152,128]{1,0:T(8,128)(2,1)S(1)} collective-permute-done((bf16[1152,128]{1,0:T(8,128)(2,1)}, bf16[1152,128]{1,0:T(8,128)(2,1)S(1)}, u32[]{:S(2)}, u32[]{:S(2)}) %collective-permute-start.20) | collective-permute-done | bytes 294944 | tf_op jit(solution)/shard_map/ppermute | solution.py:362
  96.2 4.9 %collective-permute-done.17.near_after.refs_2_ = bf16[1184,128]{1,0:T(8,128)(2,1)S(1)} collective-permute-done((bf16[1184,128]{1,0:T(8,128)(2,1)}, bf16[1184,128]{1,0:T(8,128)(2,1)S(1)}, u32[]{:S(2)}, u32[]{:S(2)}) %collective-permute-start.17) | collective-permute-done | bytes 303136 | tf_op jit(solution)/shard_map/ppermute | solution.py:362
  102.4 7.5 %collective-permute-done.16.near_before.refs_1_ = bf16[1184,128]{1,0:T(8,128)(2,1)S(1)} collective-permute-done((bf16[1184,128]{1,0:T(8,128)(2,1)}, bf16[1184,128]{1,0:T(8,128)(2,1)S(1)}, u32[]{:S(2)}, u32[]{:S(2)}) %collective-permute-start.16) | collective-permute-done | bytes 303136 | tf_op jit(solution)/shard_map/ppermute | solution.py:361
  110.5 2.8 %collective-permute-done.19.far_before = bf16[1152,128]{1,0:T(8,128)(2,1)S(1)} collective-permute-done((bf16[1152,128]{1,0:T(8,128)(2,1)}, bf16[1152,128]{1,0:T(8,128)(2,1)S(1)}, u32[]{:S(2)}, u32[]{:S(2)}) %collective-permute-start.19) | collective-permute-done | bytes 294944 | tf_op jit(solution)/shard_map/ppermute | solution.py:361
  115.4 4.8 %collective-permute-start.29 = (bf16[192,128]{1,0:T(8,128)(2,1)}, bf16[192,128]{1,0:T(8,128)(2,1)S(1)}, u32[]{:S(2)}, u32[]{:S(2)}) collective-permute-start(bf16[192,128]{1,0:T(8,128)(2,1)} %get-tuple-element.92), channel_id=1, source_target_pairs={{0,8},{8,16},{16,24},{24,0},{1,9},{9,17},{17,25},{25,1},{2,10},{10... | collective-permute-start | bytes 147464 | tf_op jit(solution)/shard_map/ppermute | solution.py:468
  121.2 4.6 %shard_map.98 = (bf16[2,384,512]{2,1,0:T(8,128)(2,1)S(1)}, bf16[2,1152,128]{2,1,0:T(8,128)(2,1)S(1)}) custom-call(bf16[1184,128]{1,0:T(8,128)(2,1)S(1)} %copy-done.7, bf16[1184,128]{1,0:T(8,128)(2,1)S(1)} %collective-permute-done.16.near_before.refs_1_, bf16[1184,128]{1,0:T(8,128)(2,1)S(1)} %collective-permute-done.17.near_after.refs_2_, ...), custom_call_target="tpu_custom_call" | custom-call | flops 2415919104 | bytes 10223616 | tf_op jit(solution)/shard_map/pallas_call | solution.py:477
  131.9 4.3 %shard_map.99 = (bf16[1184,128]{1,0:T(8,128)(2,1)}, bf16[1152,128]{1,0:T(8,128)(2,1)}, bf16[192,512]{1,0:T(8,128)(2,1)}, bf16[192,512]{1,0:T(8,128)(2,1)}, bf16[...) custom-call(bf16[2,384,512]{2,1,0:T(8,128)(2,1)} %copy-done.5, bf16[1184,128]{1,0:T(8,128)(2,1)} %copy-done.15, ...), custom_call_target="tpu_custom_call" | custom-call | flops 603979776 | bytes 2555904 | tf_op jit(solution)/shard_map/pallas_call | solution.py:490
  141.4 5.0 %shard_map.100 = (bf16[3,1024,512]{2,1,0:T(8,128)(2,1)}, f32[32,128]{1,0:T(8,128)}, f32[3,3,512]{2,1,0:T(4,128)}) custom-call(bf16[2,2,192,512]{3,2,1,0:T(8,128)(2,1)} %bitcast.21, bf16[1184,128]{1,0:T(8,128)(2,1)} %get-tuple-element.82.near.refs_0_, bf16[1184,128]{1,0:T(8,128)(2,1)} %copy-done.9, bf16[1184,128]{1,0:T(8,128)(2,1)} %copy-done.8, ...), custom_call_target="tpu_custom_call" | custom-call | flops 1207959552 | bytes 5111808 | tf_op jit(solution)/shard_map/pallas_call | solution.py:514
  150.5 3.8 %collective-permute-start.34 = (bf16[192,512]{1,0:T(8,128)(2,1)}, bf16[192,512]{1,0:T(8,128)(2,1)S(1)}, u32[]{:S(2)}, u32[]{:S(2)}) collective-permute-start(bf16[192,512]{1,0:T(8,128)(2,1)} %add_convert_fusion), channel_id=1, source_target_pairs={{0,0},{2,16},{4,8},{6,24},{8,2},{10,18},{12,10},{14,26},{16,4},{18... | collective-permute-start | bytes 589832 | tf_op jit(solution)/shard_map/ppermute | solution.py:526
  154.4 6.9 %shard_map.101 = (f32[3,1024,512]{2,1,0:T(8,128)}, bf16[192,512]{1,0:T(8,128)(2,1)}) custom-call(bf16[2,2,192,512]{3,2,1,0:T(8,128)(2,1)} %copy-done.4, bf16[3,1024,512]{2,1,0:T(8,128)(2,1)} %get-tuple-element.99.part_ref, bf16[1152,128]{1,0:T(8,128)(2,1)} %get-tuple-element.83.refs_0_, bf16[2,1152,128]{2,1,0:T(8,128)(2,1)} %copy-done.13, ...), custom_call_target="tpu_custom_call" | custom-call | flops 1207959552 | bytes 5111808 | tf_op jit(solution)/shard_map/pallas_call | solution.py:528
  (132 shorter events, 48.0 us)
Async XLA Ops:
  0.6 14.8 %collective-permute-start = (bf16[192,512]{1,0:T(8,128)(2,1)}, bf16[192,512]{1,0:T(8,128)(2,1)S(1)}, u32[]{:S(2)}, u32[]{:S(2)}) collective-permute-start(bf16[192,512]{1,0:T(8,128)(2,1)} %param.5), channel_id=1, source_target_pairs={{0,0},{16,2},{8,4},{24,6},{2,8},{18,10},{10,12},{26,14},{4,16},{20... | collective-permute-start | bytes 589832 | tf_op jit(solution)/shard_map/ppermute | solution.py:393
  25.0 20.4 %collective-permute-start.7 = (bf16[2,2,192,512]{3,2,1,0:T(8,128)(2,1)S(1)}, bf16[2,2,192,512]{3,2,1,0:T(8,128)(2,1)S(1)}, u32[]{:S(2)}, u32[]{:S(2)}) collective-permute-start(bf16[2,2,192,512]{3,2,1,0:T(8,128)(2,1)S(1)} %bitcast.19), channel_id=1, source_target_pairs={{0,2},{2,0},{4,6},{6,4},{1,3},{3,1},{5,7},{7,5},{8,10},{10,8},{12,... | collective-permute-start | bytes 2359304 | tf_op jit(solution)/shard_map/ppermute | solution.py:409
  29.8 85.6 %collective-permute-start.21 = (bf16[3,1024,512]{2,1,0:T(8,128)(2,1)}, bf16[3,1024,512]{2,1,0:T(8,128)(2,1)}, u32[]{:S(2)}, u32[]{:S(2)}) collective-permute-start(bf16[3,1024,512]{2,1,0:T(8,128)(2,1)} %bitcast.w_ref), channel_id=1, source_target_pairs={{0,2},{2,0},{4,6},{6,4},{1,3},{3,1},{5,7},{7,5},{8,10},{10,8},{12,... | collective-permute-start | bytes 9437192 | tf_op jit(solution)/shard_map/ppermute | solution.py:474
  30.1 14.6 %collective-permute-start.1 = (bf16[192,128]{1,0:T(8,128)(2,1)S(1)}, bf16[192,128]{1,0:T(8,128)(2,1)S(1)}, u32[]{:S(2)}, u32[]{:S(2)}) collective-permute-start(bf16[192,128]{1,0:T(8,128)(2,1)S(1)} %get-tuple-element.62), channel_id=1, source_target_pairs={{0,16},{8,24},{16,0},{24,8},{1,17},{9,25},{17,1},{25,9},{2,18},{10... | collective-permute-start | bytes 147464 | tf_op jit(solution)/shard_map/ppermute | solution.py:410
  36.6 13.6 %collective-permute-start.8 = (bf16[1152,128]{1,0:T(8,128)(2,1)S(1)}, bf16[1152,128]{1,0:T(8,128)(2,1)S(1)}, u32[]{:S(2)}, u32[]{:S(2)}) collective-permute-start(bf16[1152,128]{1,0:T(8,128)(2,1)S(1)} %bitcast.23), channel_id=1, source_target_pairs={{0,8},{8,16},{1,9},{9,17},{2,10},{10,18},{3,11},{11,19},{4,12},{12... | collective-permute-start | bytes 884744 | tf_op jit(solution)/shard_map/ppermute | solution.py:344
  38.0 29.1 %collective-permute-start.11 = (bf16[1152,128]{1,0:T(8,128)(2,1)S(1)}, bf16[1152,128]{1,0:T(8,128)(2,1)}, u32[]{:S(2)}, u32[]{:S(2)}) collective-permute-start(bf16[1152,128]{1,0:T(8,128)(2,1)S(1)} %bitcast_add_fusion.2), channel_id=1, source_target_pairs={{0,24},{8,0},{16,8},{24,16},{1,25},{9,1},{17,9},{25,17},{2,26},{10... | collective-permute-start | bytes 884744 | tf_op jit(solution)/shard_map/ppermute | solution.py:347
  50.2 16.9 %collective-permute-start.9 = (bf16[1152,128]{1,0:T(8,128)(2,1)S(1)}, bf16[1152,128]{1,0:T(8,128)(2,1)S(1)}, u32[]{:S(2)}, u32[]{:S(2)}) collective-permute-start(bf16[1152,128]{1,0:T(8,128)(2,1)S(1)} %bitcast_add_fusion.3), channel_id=1, source_target_pairs={{0,8},{8,16},{16,24},{24,0},{1,9},{9,17},{17,25},{25,1},{2,10},{10... | collective-permute-start | bytes 884744 | tf_op jit(solution)/shard_map/ppermute | solution.py:346
  50.6 11.1 %collective-permute-start.12 = (bf16[1152,128]{1,0:T(8,128)(2,1)S(1)}, bf16[1152,128]{1,0:T(8,128)(2,1)S(1)}, u32[]{:S(2)}, u32[]{:S(2)}) collective-permute-start(bf16[1152,128]{1,0:T(8,128)(2,1)S(1)} %bitcast.25), channel_id=1, source_target_pairs={{0,8},{8,16},{1,9},{9,17},{2,10},{10,18},{3,11},{11,19},{4,12},{12... | collective-permute-start | bytes 884744 | tf_op jit(solution)/shard_map/ppermute | solution.py:344
  54.7 14.6 %collective-permute-start.15 = (bf16[1152,128]{1,0:T(8,128)(2,1)S(1)}, bf16[1152,128]{1,0:T(8,128)(2,1)S(1)}, u32[]{:S(2)}, u32[]{:S(2)}) collective-permute-start(bf16[1152,128]{1,0:T(8,128)(2,1)S(1)} %bitcast_add_fusion), channel_id=1, source_target_pairs={{0,24},{8,0},{16,8},{24,16},{1,25},{9,1},{17,9},{25,17},{2,26},{10... | collective-permute-start | bytes 884744 | tf_op jit(solution)/shard_map/ppermute | solution.py:347
  61.7 15.9 %collective-permute-start.13 = (bf16[1152,128]{1,0:T(8,128)(2,1)S(1)}, bf16[1152,128]{1,0:T(8,128)(2,1)S(1)}, u32[]{:S(2)}, u32[]{:S(2)}) collective-permute-start(bf16[1152,128]{1,0:T(8,128)(2,1)S(1)} %bitcast_add_fusion.1), channel_id=1, source_target_pairs={{0,8},{8,16},{16,24},{24,0},{1,9},{9,17},{17,25},{25,1},{2,10},{10... | collective-permute-start | bytes 884744 | tf_op jit(solution)/shard_map/ppermute | solution.py:346
  83.8 10.8 %collective-permute-start.20 = (bf16[1152,128]{1,0:T(8,128)(2,1)}, bf16[1152,128]{1,0:T(8,128)(2,1)S(1)}, u32[]{:S(2)}, u32[]{:S(2)}) collective-permute-start(bf16[1152,128]{1,0:T(8,128)(2,1)} %get-tuple-element.83.refs_0_), channel_id=1, source_target_pairs={{0,26},{2,24},{4,30},{6,28},{8,2},{10,0},{12,6},{14,4},{16,10},{18... | collective-permute-start | bytes 884744 | tf_op jit(solution)/shard_map/ppermute | solution.py:362
  87.5 13.6 %collective-permute-start.17 = (bf16[1184,128]{1,0:T(8,128)(2,1)}, bf16[1184,128]{1,0:T(8,128)(2,1)S(1)}, u32[]{:S(2)}, u32[]{:S(2)}) collective-permute-start(bf16[1184,128]{1,0:T(8,128)(2,1)} %get-tuple-element.82.near.refs_0_), channel_id=1, source_target_pairs={{0,24},{2,26},{4,28},{6,30},{8,0},{10,2},{12,4},{14,6},{16,8},{18,... | collective-permute-start | bytes 909320 | tf_op jit(solution)/shard_map/ppermute | solution.py:362
  89.2 20.7 %collective-permute-start.16 = (bf16[1184,128]{1,0:T(8,128)(2,1)}, bf16[1184,128]{1,0:T(8,128)(2,1)S(1)}, u32[]{:S(2)}, u32[]{:S(2)}) collective-permute-start(bf16[1184,128]{1,0:T(8,128)(2,1)} %get-tuple-element.82.near.refs_0_), channel_id=1, source_target_pairs={{0,8},{2,10},{4,12},{6,14},{8,16},{10,18},{12,20},{14,22},{16,24},... | collective-permute-start | bytes 909320 | tf_op jit(solution)/shard_map/ppermute | solution.py:361
  89.2 24.2 %collective-permute-start.19 = (bf16[1152,128]{1,0:T(8,128)(2,1)}, bf16[1152,128]{1,0:T(8,128)(2,1)S(1)}, u32[]{:S(2)}, u32[]{:S(2)}) collective-permute-start(bf16[1152,128]{1,0:T(8,128)(2,1)} %get-tuple-element.83.refs_0_), channel_id=1, source_target_pairs={{0,10},{2,8},{4,14},{6,12},{8,18},{10,16},{12,22},{14,20},{16,26},... | collective-permute-start | bytes 884744 | tf_op jit(solution)/shard_map/ppermute | solution.py:361
  94.6 20.1 %collective-permute-start.18 = (bf16[1152,128]{1,0:T(8,128)(2,1)}, bf16[1152,128]{1,0:T(8,128)(2,1)S(1)}, u32[]{:S(2)}, u32[]{:S(2)}) collective-permute-start(bf16[1152,128]{1,0:T(8,128)(2,1)} %get-tuple-element.83.refs_0_), channel_id=1, source_target_pairs={{0,2},{2,0},{4,6},{6,4},{8,10},{10,8},{12,14},{14,12},{16,18},{18,... | collective-permute-start | bytes 884744 | tf_op jit(solution)/shard_map/ppermute | solution.py:363
  101.1 30.0 %collective-permute-start.23 = (bf16[1184,128]{1,0:T(8,128)(2,1)S(1)}, bf16[1184,128]{1,0:T(8,128)(2,1)S(1)}, u32[]{:S(2)}, u32[]{:S(2)}) collective-permute-start(bf16[1184,128]{1,0:T(8,128)(2,1)S(1)} %collective-permute-done.17.near_after.refs_2_), channel_id=1, source_target_pairs={{8,0},{16,8},{9,1},{17,9},{10,2},{18,10},{11,3},{19,11},{12,4},{20... | collective-permute-start | bytes 909320 | tf_op jit(solution)/shard_map/ppermute | solution.py:365
  109.9 21.2 %collective-permute-start.22 = (bf16[1184,128]{1,0:T(8,128)(2,1)S(1)}, bf16[1184,128]{1,0:T(8,128)(2,1)S(1)}, u32[]{:S(2)}, u32[]{:S(2)}) collective-permute-start(bf16[1184,128]{1,0:T(8,128)(2,1)S(1)} %collective-permute-done.16.near_before.refs_1_), channel_id=1, source_target_pairs={{8,16},{16,24},{9,17},{17,25},{10,18},{18,26},{11,19},{19,27},{12,... | collective-permute-start | bytes 909320 | tf_op jit(solution)/shard_map/ppermute | solution.py:364
  113.4 15.2 %collective-permute-start.25 = (bf16[1152,128]{1,0:T(8,128)(2,1)S(1)}, bf16[1152,128]{1,0:T(8,128)(2,1)S(1)}, u32[]{:S(2)}, u32[]{:S(2)}) collective-permute-start(bf16[1152,128]{1,0:T(8,128)(2,1)S(1)} %collective-permute-done.20.far_after), channel_id=1, source_target_pairs={{8,0},{16,8},{9,1},{17,9},{10,2},{18,10},{11,3},{19,11},{12,4},{20... | collective-permute-start | bytes 884744 | tf_op jit(solution)/shard_map/ppermute | solution.py:365
  114.7 14.0 %collective-permute-start.24 = (bf16[1152,128]{1,0:T(8,128)(2,1)S(1)}, bf16[1152,128]{1,0:T(8,128)(2,1)S(1)}, u32[]{:S(2)}, u32[]{:S(2)}) collective-permute-start(bf16[1152,128]{1,0:T(8,128)(2,1)S(1)} %collective-permute-done.19.far_before), channel_id=1, source_target_pairs={{8,16},{16,24},{9,17},{17,25},{10,18},{18,26},{11,19},{19,27},{12,... | collective-permute-start | bytes 884744 | tf_op jit(solution)/shard_map/ppermute | solution.py:364
  115.4 20.8 %collective-permute-start.29 = (bf16[192,128]{1,0:T(8,128)(2,1)}, bf16[192,128]{1,0:T(8,128)(2,1)S(1)}, u32[]{:S(2)}, u32[]{:S(2)}) collective-permute-start(bf16[192,128]{1,0:T(8,128)(2,1)} %get-tuple-element.92), channel_id=1, source_target_pairs={{0,8},{8,16},{16,24},{24,0},{1,9},{9,17},{17,25},{25,1},{2,10},{10... | collective-permute-start | bytes 147464 | tf_op jit(solution)/shard_map/ppermute | solution.py:468
  136.2 14.3 %collective-permute-start.32 = (bf16[2,1152,128]{2,1,0:T(8,128)(2,1)S(1)}, bf16[2,1152,128]{2,1,0:T(8,128)(2,1)S(1)}, u32[]{:S(2)}, u32[]{:S(2)}) collective-permute-start(bf16[2,1152,128]{2,1,0:T(8,128)(2,1)S(1)} %get-tuple-element.95), channel_id=1, source_target_pairs={{0,2},{2,0},{4,6},{6,4},{1,3},{3,1},{5,7},{7,5},{8,10},{10,8},{12,... | collective-permute-start | bytes 1769480 | tf_op jit(solution)/shard_map/ppermute | solution.py:507
  138.6 10.1 %collective-permute-start.28 = (bf16[192,512]{1,0:T(8,128)(2,1)}, bf16[192,512]{1,0:T(8,128)(2,1)}, u32[]{:S(2)}, u32[]{:S(2)}) collective-permute-start(bf16[192,512]{1,0:T(8,128)(2,1)} %get-tuple-element.89), channel_id=1, source_target_pairs={{5,0},{4,1},{7,2},{6,3},{1,4},{0,5},{3,6},{2,7},{13,8},{12,9},{15,... | collective-permute-start | bytes 589832 | tf_op jit(solution)/shard_map/ppermute | solution.py:509
  140.0 10.5 %collective-permute-start.33 = (bf16[1152,128]{1,0:T(8,128)(2,1)}, bf16[1152,128]{1,0:T(8,128)(2,1)S(1)}, u32[]{:S(2)}, u32[]{:S(2)}) collective-permute-start(bf16[1152,128]{1,0:T(8,128)(2,1)} %get-tuple-element.96), channel_id=1, source_target_pairs={{0,2},{2,0},{4,6},{6,4},{1,3},{3,1},{5,7},{7,5},{8,10},{10,8},{12,... | collective-permute-start | bytes 884744 | tf_op jit(solution)/shard_map/ppermute | solution.py:507
  150.5 11.4 %collective-permute-start.34 = (bf16[192,512]{1,0:T(8,128)(2,1)}, bf16[192,512]{1,0:T(8,128)(2,1)S(1)}, u32[]{:S(2)}, u32[]{:S(2)}) collective-permute-start(bf16[192,512]{1,0:T(8,128)(2,1)} %add_convert_fusion), channel_id=1, source_target_pairs={{0,0},{2,16},{4,8},{6,24},{8,2},{10,18},{12,10},{14,26},{16,4},{18... | collective-permute-start | bytes 589832 | tf_op jit(solution)/shard_map/ppermute | solution.py:526
  (42 other events, 400.6 us)

commit v18 on v16

--- a/solution.py
+++ b/solution.py
@@ -173,7 +173,7 @@
     i = pl.program_id(0)
     z, col = lax.axis_index("dp"), lax.axis_index("col")
 
-    @pl.when(i == 0)
+    @pl.when((i == 0) & (pl.program_id(1) == 0))
     def _():
         groups = long_ref.shape[0] // ndp
         for k, ahead in enumerate((0, -1, 1, 2)):
@@ -195,14 +195,9 @@
     gm = jnp.concatenate(
         [jnp.concatenate([held[k, owner, at, :] for owner in range(ndp)], axis=1) for k in range(2)], axis=0
     )
-    for dx in range(ncol):
-        start = pl.multiple_of(wrapped(col - dx, ncol) * depth, depth)
-        x = jnp.concatenate(
-            [x_ref[:, dx].reshape(tokens, depth) for x_ref in (x0_ref, x1_ref)], axis=0
-        )
-        out_ref[0, pl.ds(start, depth), :] = scale * lax.dot_general(
-            x, gm, (((0,), (0,)), ((), ())), preferred_element_type=F32
-        )
+    dx = wrapped(col - pl.program_id(1), ncol)
+    x = jnp.concatenate([x_ref[:, dx].reshape(tokens, depth) for x_ref in (x0_ref, x1_ref)], axis=0)
+    out_ref[0] = scale * lax.dot_general(x, gm, (((0,), (0,)), ((), ())), preferred_element_type=F32)
 
 
 def delayed(values, count):
@@ -326,13 +321,19 @@
     near_ref[3 * tokens // 2 :] = small.astype(BF16)
 
 
-def sum_over_line(own, right, far, left):
+def first_hop(far):
     ndp = lax.axis_size("dp")
-    from_left = lax.ppermute(far, "dp", [(a, a + 1) for a in range(ndp // 2)])
-    from_right = lax.ppermute(far, "dp", [(a, a - 1) for a in range(ndp // 2, ndp)])
+    return (
+        lax.ppermute(far, "dp", [(a, a + 1) for a in range(ndp // 2)]),
+        lax.ppermute(far, "dp", [(a, a - 1) for a in range(ndp // 2, ndp)]),
+    )
+
+
+def second_hop(right, left, from_left, from_right):
+    ndp = lax.axis_size("dp")
     rightward = lax.ppermute(right + from_left, "dp", [(a, (a + 1) % ndp) for a in range(ndp)])
     leftward = lax.ppermute(left + from_right, "dp", [(a, (a - 1) % ndp) for a in range(ndp)])
-    return own, rightward, leftward
+    return rightward, leftward
 
 
 def gather_over_line(own, across):
@@ -395,7 +396,6 @@
     x0 = jnp.stack(near).reshape(nblocks, ncol, rows, dcol)
     x1 = lax.ppermute(x0, "row", partner)
     upstream[2] = lax.ppermute(upstream[2], "dp", turn[2])
-    upstream[2], x1 = lax.optimization_barrier((upstream[2], x1))
 
     sf = lax.dynamic_slice_in_dim(short_filter, z * width, width, 2).reshape(3 * nshort, width)
     lf = lax.dynamic_slice_in_dim(long_filter, z * groups, groups, 0).astype(F32)
@@ -411,7 +411,7 @@
 
     mm_flops = seq * drow * 3 * local
     mm_bytes = seq * drow + 6 * drow * local + 3 * seq * local
-    sums = []
+    shares, passed, sums = [], [], []
     for x in (x0, x1):
         parts = kernel_call(
             project_body,
@@ -426,7 +426,11 @@
             flops=mm_flops,
             nbytes=mm_bytes,
         )(x, w)
-        sums += sum_over_line(*(p.reshape(3 * chunk, width) for p in parts))
+        shares.append([p.reshape(3 * chunk, width) for p in parts])
+        passed.append(first_hop(shares[-1][2]))
+    passed[0], shares[1], upstream[2], later_w = lax.optimization_barrier((passed[0], shares[1], upstream[2], w))
+    for (own, right, _, left), came in zip(shares, passed):
+        sums += [own, *second_hop(right, left, *came)]
 
     extra = -(-(groups + 3 * nshort) // 16) * 16
     half = pl.BlockSpec((groups, ntaps, 2 * ntaps), lambda i: (0, 0, 0))
@@ -458,7 +462,7 @@
     ]
     *near, near_far_before, near_far_after = gather_over_line(grad_near, False)
     *far, far_far_before, far_far_after = gather_over_line(grad_other, True)
-    partner_w = lax.ppermute(w, "row", partner)
+    partner_w = lax.ppermute(later_w, "row", partner)
     everywhere = pl.BlockSpec(memory_space=pl.ANY)
     in_vmem = pl.BlockSpec(memory_space=pltpu.VMEM)
     part, far_two = kernel_call(
@@ -500,6 +504,7 @@
     arrived, far_two, far_last = lax.optimization_barrier((arrived, far_two, far_last))
     grad_in = lax.ppermute(arrived, ("dp", "row"), swap_back)
 
+    each = lambda *shape: pl.BlockSpec(shape, lambda i, e: (0,) * len(shape))
     grad_weight, mixed, grad_long, grad_short = kernel_call(
         functools.partial(weight_grad_body, scale),
         [
@@ -508,16 +513,16 @@
             shaped((ngroups, ntaps), F32),
             shaped((nshort, 3, local), F32),
         ],
-        grid=(3,),
-        in_specs=[whole(nblocks, ncol, rows, dcol)] * 2
-        + [whole(*grad_near.shape)] * 4
-        + [whole(*grad_other.shape), whole(*far_two.shape), whole(*far_last.shape)]
-        + [whole(rows, width)] * ndp,
+        grid=(3, ncol),
+        in_specs=[each(nblocks, ncol, rows, dcol)] * 2
+        + [each(*grad_near.shape)] * 4
+        + [each(*grad_other.shape), each(*far_two.shape), each(*far_last.shape)]
+        + [each(rows, width)] * ndp,
         out_specs=[
-            pl.BlockSpec((1, drow, local), lambda i: (i, 0, 0)),
-            whole(rows, local),
-            whole(ngroups, ntaps),
-            whole(nshort, 3, local),
+            pl.BlockSpec((1, dcol, local), lambda i, e: (i, e, 0)),
+            each(rows, local),
+            each(ngroups, ntaps),
+            each(nshort, 3, local),
         ],
         scratch=[
             pltpu.VMEM((2, ndp, 3 * chunk + extra, width), BF16),

time: 163 us -> 170 us (1.043)
  waiting for transfers between devices: 59.9 us -> 67.2 us
    ppermute x9, starting transfers between devices: 15.6 us -> 23 us  [the longest x2 9.92 us: first_hop(): lax.ppermute(far, 'dp', [(a, a + 1) for a in range(ndp // 2)])]
    ppermute x9, waiting for transfers between devices: 14.2 us -> 20.1 us  [the longest x2 9.66 us: second_hop(): lax.ppermute(right + from_left, 'dp', [(a, (a + 1) % ndp) for a in range(...]
    ppermute x1, starting transfers between devices: 6.46 us -> 1.23 us  [move_activations(): upstream[2] = lax.ppermute(upstream[2], 'dp', turn[2])]
    ppermute x2, waiting for transfers between devices: 10.2 us -> 12.2 us  [gather_over_line(): after = lax.ppermute(own, ('dp', 'row'), shift(-1))]
    ppermute x2, waiting for transfers between devices: 10.3 us -> 12.2 us  [gather_over_line(): before = lax.ppermute(own, ('dp', 'row'), shift(1))]
    unnamed x61 -> x63, local copies, waits for them, and re-layouts: 8.13 us -> 8.93 us
  transfers between devices with their start and end apart: 35 -> 35, of which waited for: 17 -> 18; matrix products, arithmetic and copies ran while one was open for 2% -> 2% of each run, Pallas kernels for 19% -> 19%
where the time goes in v18:
time: 170 us
  waiting for transfers between devices  67.2 us (40%)
  starting transfers between devices  57.6 us (34%)
  Pallas kernels  31.9 us (19%)
  local copies, waits for them, and re-layouts  9.62 us (6%)
  other arithmetic  2.2 us (1%)
    ppermute x2, waiting for transfers between devices, gather_over_line(): before = lax.ppermute(own, ('dp', 'row'), shift(1))  12.2 us
    ppermute x2, waiting for transfers between devices, gather_over_line(): after = lax.ppermute(own, ('dp', 'row'), shift(-1))  12.2 us
    ppermute x2, starting transfers between devices, first_hop(): lax.ppermute(far, 'dp', [(a, a + 1) for a in range(ndp // 2)])  9.92 us
    ppermute x2, waiting for transfers between devices, second_hop(): lax.ppermute(right + from_left, 'dp', [(a, (a + 1) % ndp) for a in range(...  9.66 us
    unnamed x63, local copies, waits for them, and re-layouts  8.93 us
    ppermute x2, starting transfers between devices, second_hop(): lax.ppermute(right + from_left, 'dp', [(a, (a + 1) % ndp) for a in range(...  8.37 us
    ppermute x3, waiting for transfers between devices, move_activations(): lax.ppermute(sent, ('row', 'col'), [(b, a) for a, b in offset(*p)])  8.24 us
    pallas_call x2, Pallas kernels, move_activations(): kernel_call(project_body, [shaped((3, chunk, width), BF16)] * ndp, grid=(...  7.93 us
  transfers between devices with their start and end apart: 35, of which 18 were waited for; matrix products, arithmetic and copies ran while one was open for 2% of the time, Pallas kernels for 19%

profile of v18, /device:TPU:1, one launch (start us, length us, event | category | flops | bytes accessed | tf_op | source)
XLA Modules:
  0.0 169.6 jit_solution(5564873945466196284)
XLA Ops:
  0.6 4.6 %collective-permute-start = (bf16[192,512]{1,0:T(8,128)(2,1)}, bf16[192,512]{1,0:T(8,128)(2,1)S(1)}, u32[]{:S(2)}, u32[]{:S(2)}) collective-permute-start(bf16[192,512]{1,0:T(8,128)(2,1)} %param.5), channel_id=1, source_target_pairs={{0,0},{16,2},{8,4},{24,6},{2,8},{18,10},{10,12},{26,14},{4,16},{20... | collective-permute-start | bytes 589832 | tf_op jit(solution)/shard_map/ppermute | solution.py:381
  8.9 6.5 %collective-permute-done = bf16[192,512]{1,0:T(8,128)(2,1)S(1)} collective-permute-done((bf16[192,512]{1,0:T(8,128)(2,1)}, bf16[192,512]{1,0:T(8,128)(2,1)S(1)}, u32[]{:S(2)}, u32[]{:S(2)}) %collective-permute-start) | collective-permute-done | bytes 196640 | tf_op jit(solution)/shard_map/ppermute | solution.py:381
  25.7 3.8 %shard_map.94 = (bf16[3,384,128]{2,1,0:T(8,128)(2,1)S(1)}, bf16[3,384,128]{2,1,0:T(8,128)(2,1)S(1)}, bf16[3,384,128]{2,1,0:T(8,128)(2,1)S(1)}, bf16[3,384,128]{2,1,0:T(8,128)(2,1)S(1)}) custom-call(bf16[2,2,192,512]{3,2,1,0:T(8,128)(2,1)S(1)} %bitcast.18, bf16[3,1024,512]{2,1,0:T(8,128)(2,1)} %bitcast.w_ref), custom_call_target="tpu_custom_call" | custom-call | flops 1207959552 | bytes 5111808 | tf_op jit(solution)/shard_map/pallas_call | solution.py:416
  30.9 5.9 %collective-permute-start.7 = (bf16[1152,128]{1,0:T(8,128)(2,1)S(1)}, bf16[1152,128]{1,0:T(8,128)(2,1)S(1)}, u32[]{:S(2)}, u32[]{:S(2)}) collective-permute-start(bf16[1152,128]{1,0:T(8,128)(2,1)S(1)} %bitcast.25), channel_id=1, source_target_pairs={{0,8},{8,16},{1,9},{9,17},{2,10},{10,18},{3,11},{11,19},{4,12},{12... | collective-permute-start | bytes 884744 | tf_op jit(solution)/shard_map/ppermute | solution.py:327
  38.1 4.1 %shard_map.95 = (bf16[3,384,128]{2,1,0:T(8,128)(2,1)S(1)}, bf16[3,384,128]{2,1,0:T(8,128)(2,1)S(1)}, bf16[3,384,128]{2,1,0:T(8,128)(2,1)S(1)}, bf16[3,384,128]{2,1,0:T(8,128)(2,1)S(1)}) custom-call(bf16[2,2,192,512]{3,2,1,0:T(8,128)(2,1)S(1)} %collective-permute-done.6.x_ref.refs_1_, bf16[3,1024,512]{2,1,0:T(8,128)(2,1)} %bitcast.w_ref), custom_call_target="tpu_custom_call" | custom-call | flops 1207959552 | bytes 5111808 | tf_op jit(solution)/shard_map/pallas_call | solution.py:416
  47.5 4.0 %collective-permute-start.12 = (bf16[1152,128]{1,0:T(8,128)(2,1)S(1)}, bf16[1152,128]{1,0:T(8,128)(2,1)S(1)}, u32[]{:S(2)}, u32[]{:S(2)}) collective-permute-start(bf16[1152,128]{1,0:T(8,128)(2,1)S(1)} %bitcast.23), channel_id=1, source_target_pairs={{0,8},{8,16},{1,9},{9,17},{2,10},{10,18},{3,11},{11,19},{4,12},{12... | collective-permute-start | bytes 884744 | tf_op jit(solution)/shard_map/ppermute | solution.py:327
  54.0 3.9 %collective-permute-done.12 = bf16[1152,128]{1,0:T(8,128)(2,1)S(1)} collective-permute-done((bf16[1152,128]{1,0:T(8,128)(2,1)S(1)}, bf16[1152,128]{1,0:T(8,128)(2,1)S(1)}, u32[]{:S(2)}, u32[]{:S(2)}) %collective-permute-start.12) | collective-permute-done | bytes 294944 | tf_op jit(solution)/shard_map/ppermute | solution.py:327
  57.9 8.0 %collective-permute-start.13 = (bf16[1152,128]{1,0:T(8,128)(2,1)S(1)}, bf16[1152,128]{1,0:T(8,128)(2,1)S(1)}, u32[]{:S(2)}, u32[]{:S(2)}) collective-permute-start(bf16[1152,128]{1,0:T(8,128)(2,1)S(1)} %add.31), channel_id=1, source_target_pairs={{0,8},{8,16},{16,24},{24,0},{1,9},{9,17},{17,25},{25,1},{2,10},{10... | collective-permute-start | bytes 884744 | tf_op jit(solution)/shard_map/ppermute | solution.py:334
  69.2 3.3 %collective-permute-done.10.refs_1_ = bf16[1152,128]{1,0:T(8,128)(2,1)S(1)} collective-permute-done((bf16[1152,128]{1,0:T(8,128)(2,1)S(1)}, bf16[1152,128]{1,0:T(8,128)(2,1)S(1)}, u32[]{:S(2)}, u32[]{:S(2)}) %collective-permute-start.10) | collective-permute-done | bytes 294944 | tf_op jit(solution)/shard_map/ppermute | solution.py:334
  72.5 6.4 %collective-permute-done.13.refs_4_ = bf16[1152,128]{1,0:T(8,128)(2,1)S(1)} collective-permute-done((bf16[1152,128]{1,0:T(8,128)(2,1)S(1)}, bf16[1152,128]{1,0:T(8,128)(2,1)S(1)}, u32[]{:S(2)}, u32[]{:S(2)}) %collective-permute-start.13) | collective-permute-done | bytes 294944 | tf_op jit(solution)/shard_map/ppermute | solution.py:334
  78.8 6.5 %collective-permute-done.15.refs_5_ = bf16[1152,128]{1,0:T(8,128)(2,1)S(1)} collective-permute-done((bf16[1152,128]{1,0:T(8,128)(2,1)S(1)}, bf16[1152,128]{1,0:T(8,128)(2,1)S(1)}, u32[]{:S(2)}, u32[]{:S(2)}) %collective-permute-start.15) | collective-permute-done | bytes 294944 | tf_op jit(solution)/shard_map/ppermute | solution.py:335
  86.1 5.4 %shard_map.97 = (bf16[1184,128]{1,0:T(8,128)(2,1)}, bf16[1152,128]{1,0:T(8,128)(2,1)}, bf16[192,128]{1,0:T(8,128)(2,1)}, bf16[192,128]{1,0:T(8,128)(2,1)}, bf16[...) custom-call(bf16[1152,128]{1,0:T(8,128)(2,1)} %bitcast.26, bf16[1152,128]{1,0:T(8,128)(2,1)} %copy-done.19, ...), custom_call_target="tpu_custom_call" | custom-call | flops 1207959552 | bytes 2752512 | tf_op jit(solution)/shard_map/pallas_call | solution.py:439
  91.5 2.7 %collective-permute-start.20 = (bf16[1152,128]{1,0:T(8,128)(2,1)}, bf16[1152,128]{1,0:T(8,128)(2,1)S(1)}, u32[]{:S(2)}, u32[]{:S(2)}) collective-permute-start(bf16[1152,128]{1,0:T(8,128)(2,1)} %get-tuple-element.90.refs_6_), channel_id=1, source_target_pairs={{0,26},{2,24},{4,30},{6,28},{8,2},{10,0},{12,6},{14,4},{16,10},{18... | collective-permute-start | bytes 884744 | tf_op jit(solution)/shard_map/ppermute | solution.py:350
  95.7 5.7 %collective-permute-done.20.far_after = bf16[1152,128]{1,0:T(8,128)(2,1)S(1)} collective-permute-done((bf16[1152,128]{1,0:T(8,128)(2,1)}, bf16[1152,128]{1,0:T(8,128)(2,1)S(1)}, u32[]{:S(2)}, u32[]{:S(2)}) %collective-permute-start.20) | collective-permute-done | bytes 294944 | tf_op jit(solution)/shard_map/ppermute | solution.py:350
  101.5 6.4 %collective-permute-done.17.near_after.refs_4_ = bf16[1184,128]{1,0:T(8,128)(2,1)S(1)} collective-permute-done((bf16[1184,128]{1,0:T(8,128)(2,1)}, bf16[1184,128]{1,0:T(8,128)(2,1)S(1)}, u32[]{:S(2)}, u32[]{:S(2)}) %collective-permute-start.17) | collective-permute-done | bytes 303136 | tf_op jit(solution)/shard_map/ppermute | solution.py:350
  109.2 7.0 %collective-permute-done.16.near_before.refs_3_ = bf16[1184,128]{1,0:T(8,128)(2,1)S(1)} collective-permute-done((bf16[1184,128]{1,0:T(8,128)(2,1)}, bf16[1184,128]{1,0:T(8,128)(2,1)S(1)}, u32[]{:S(2)}, u32[]{:S(2)}) %collective-permute-start.16) | collective-permute-done | bytes 303136 | tf_op jit(solution)/shard_map/ppermute | solution.py:349
  116.9 5.3 %collective-permute-done.19.far_before = bf16[1152,128]{1,0:T(8,128)(2,1)S(1)} collective-permute-done((bf16[1152,128]{1,0:T(8,128)(2,1)}, bf16[1152,128]{1,0:T(8,128)(2,1)S(1)}, u32[]{:S(2)}, u32[]{:S(2)}) %collective-permute-start.19) | collective-permute-done | bytes 294944 | tf_op jit(solution)/shard_map/ppermute | solution.py:349
  124.1 3.7 %collective-permute-start.29 = (bf16[192,128]{1,0:T(8,128)(2,1)}, bf16[192,128]{1,0:T(8,128)(2,1)S(1)}, u32[]{:S(2)}, u32[]{:S(2)}) collective-permute-start(bf16[192,128]{1,0:T(8,128)(2,1)} %get-tuple-element.101), channel_id=1, source_target_pairs={{0,8},{8,16},{16,24},{24,0},{1,9},{9,17},{17,25},{25,1},{2,10},{10... | collective-permute-start | bytes 147464 | tf_op jit(solution)/shard_map/ppermute | solution.py:459
  128.8 4.6 %shard_map.98 = (bf16[2,384,512]{2,1,0:T(8,128)(2,1)S(1)}, bf16[2,1152,128]{2,1,0:T(8,128)(2,1)S(1)}) custom-call(bf16[1184,128]{1,0:T(8,128)(2,1)S(1)} %copy-done.7, bf16[1184,128]{1,0:T(8,128)(2,1)S(1)} %collective-permute-done.16.near_before.refs_3_, bf16[1184,128]{1,0:T(8,128)(2,1)S(1)} %collective-permute-done.17.near_after.refs_4_, ...), custom_call_target="tpu_custom_call" | custom-call | flops 2415919104 | bytes 10223616 | tf_op jit(solution)/shard_map/pallas_call | solution.py:468
  139.4 4.3 %shard_map.99 = (bf16[1184,128]{1,0:T(8,128)(2,1)}, bf16[1152,128]{1,0:T(8,128)(2,1)}, bf16[192,512]{1,0:T(8,128)(2,1)}, bf16[192,512]{1,0:T(8,128)(2,1)}, bf16[...) custom-call(bf16[2,384,512]{2,1,0:T(8,128)(2,1)} %copy-done.4, bf16[1184,128]{1,0:T(8,128)(2,1)} %copy-done.14, ...), custom_call_target="tpu_custom_call" | custom-call | flops 603979776 | bytes 2555904 | tf_op jit(solution)/shard_map/pallas_call | solution.py:481
  148.4 3.1 %collective-permute-done.26 = bf16[192,512]{1,0:T(8,128)(2,1)S(1)} collective-permute-done((bf16[192,512]{1,0:T(8,128)(2,1)}, bf16[192,512]{1,0:T(8,128)(2,1)S(1)}, u32[]{:S(2)}, u32[]{:S(2)}) %collective-permute-start.26) | collective-permute-done | bytes 196640 | tf_op jit(solution)/shard_map/ppermute | solution.py:500
  152.5 4.2 %collective-permute-done.28 = bf16[192,512]{1,0:T(8,128)(2,1)S(1)} collective-permute-done((bf16[192,512]{1,0:T(8,128)(2,1)}, bf16[192,512]{1,0:T(8,128)(2,1)S(1)}, u32[]{:S(2)}, u32[]{:S(2)}) %collective-permute-start.28) | collective-permute-done | bytes 196640 | tf_op jit(solution)/shard_map/ppermute | solution.py:500
  157.8 3.2 %collective-permute-start.34 = (bf16[192,512]{1,0:T(8,128)(2,1)S(1)}, bf16[192,512]{1,0:T(8,128)(2,1)S(1)}, u32[]{:S(2)}, u32[]{:S(2)}) collective-permute-start(bf16[192,512]{1,0:T(8,128)(2,1)S(1)} %add_convert_fusion), channel_id=1, source_target_pairs={{0,0},{2,16},{4,8},{6,24},{8,2},{10,18},{12,10},{14,26},{16,4},{18... | collective-permute-start | bytes 589832 | tf_op jit(solution)/shard_map/ppermute | solution.py:505
  161.1 7.8 %shard_map.100 = (f32[3,1024,512]{2,1,0:T(8,128)}, bf16[192,512]{1,0:T(8,128)(2,1)}, f32[32,128]{1,0:T(8,128)}, f32[3,3,512]{2,1,0:T(4,128)}) custom-call(bf16[2,2,192,512]{3,2,1,0:T(8,128)(2,1)} %bitcast.19, bf16[2,2,192,512]{3,2,1,0:T(8,128)(2,1)} %copy-done.6, bf16[1184,128]{1,0:T(8,128)(2,1)} %get-tuple-element.89.near.refs_2_, ...), custom_call_target="tpu_custom_call" | custom-call | flops 2415919104 | bytes 10223616 | tf_op jit(solution)/shard_map/pallas_call | solution.py:508
  (131 shorter events, 48.0 us)
Async XLA Ops:
  0.6 14.8 %collective-permute-start = (bf16[192,512]{1,0:T(8,128)(2,1)}, bf16[192,512]{1,0:T(8,128)(2,1)S(1)}, u32[]{:S(2)}, u32[]{:S(2)}) collective-permute-start(bf16[192,512]{1,0:T(8,128)(2,1)} %param.5), channel_id=1, source_target_pairs={{0,0},{16,2},{8,4},{24,6},{2,8},{18,10},{10,12},{26,14},{4,16},{20... | collective-permute-start | bytes 589832 | tf_op jit(solution)/shard_map/ppermute | solution.py:381
  25.0 13.1 %collective-permute-start.6 = (bf16[2,2,192,512]{3,2,1,0:T(8,128)(2,1)S(1)}, bf16[2,2,192,512]{3,2,1,0:T(8,128)(2,1)S(1)}, u32[]{:S(2)}, u32[]{:S(2)}) collective-permute-start(bf16[2,2,192,512]{3,2,1,0:T(8,128)(2,1)S(1)} %bitcast.17), channel_id=1, source_target_pairs={{0,2},{2,0},{4,6},{6,4},{1,3},{3,1},{5,7},{7,5},{8,10},{10,8},{12,... | collective-permute-start | bytes 2359304 | tf_op jit(solution)/shard_map/ppermute | solution.py:397
  30.2 15.2 %collective-permute-start.8 = (bf16[1152,128]{1,0:T(8,128)(2,1)S(1)}, bf16[1152,128]{1,0:T(8,128)(2,1)S(1)}, u32[]{:S(2)}, u32[]{:S(2)}) collective-permute-start(bf16[1152,128]{1,0:T(8,128)(2,1)S(1)} %bitcast.24), channel_id=1, source_target_pairs={{16,8},{24,16},{17,9},{25,17},{18,10},{26,18},{19,11},{27,19},{20,... | collective-permute-start | bytes 884744 | tf_op jit(solution)/shard_map/ppermute | solution.py:328
  30.9 14.5 %collective-permute-start.7 = (bf16[1152,128]{1,0:T(8,128)(2,1)S(1)}, bf16[1152,128]{1,0:T(8,128)(2,1)S(1)}, u32[]{:S(2)}, u32[]{:S(2)}) collective-permute-start(bf16[1152,128]{1,0:T(8,128)(2,1)S(1)} %bitcast.25), channel_id=1, source_target_pairs={{0,8},{8,16},{1,9},{9,17},{2,10},{10,18},{3,11},{11,19},{4,12},{12... | collective-permute-start | bytes 884744 | tf_op jit(solution)/shard_map/ppermute | solution.py:327
  45.4 78.7 %collective-permute-start.21 = (bf16[3,1024,512]{2,1,0:T(8,128)(2,1)}, bf16[3,1024,512]{2,1,0:T(8,128)(2,1)}, u32[]{:S(2)}, u32[]{:S(2)}) collective-permute-start(bf16[3,1024,512]{2,1,0:T(8,128)(2,1)} %bitcast.w_ref), channel_id=1, source_target_pairs={{0,2},{2,0},{4,6},{6,4},{1,3},{3,1},{5,7},{7,5},{8,10},{10,8},{12,... | collective-permute-start | bytes 9437192 | tf_op jit(solution)/shard_map/ppermute | solution.py:465
  46.8 19.1 %collective-permute-start.14 = (bf16[1152,128]{1,0:T(8,128)(2,1)S(1)}, bf16[1152,128]{1,0:T(8,128)(2,1)S(1)}, u32[]{:S(2)}, u32[]{:S(2)}) collective-permute-start(bf16[1152,128]{1,0:T(8,128)(2,1)S(1)} %bitcast.22), channel_id=1, source_target_pairs={{16,8},{24,16},{17,9},{25,17},{18,10},{26,18},{19,11},{27,19},{20,... | collective-permute-start | bytes 884744 | tf_op jit(solution)/shard_map/ppermute | solution.py:328
  47.5 10.4 %collective-permute-start.12 = (bf16[1152,128]{1,0:T(8,128)(2,1)S(1)}, bf16[1152,128]{1,0:T(8,128)(2,1)S(1)}, u32[]{:S(2)}, u32[]{:S(2)}) collective-permute-start(bf16[1152,128]{1,0:T(8,128)(2,1)S(1)} %bitcast.23), channel_id=1, source_target_pairs={{0,8},{8,16},{1,9},{9,17},{2,10},{10,18},{3,11},{11,19},{4,12},{12... | collective-permute-start | bytes 884744 | tf_op jit(solution)/shard_map/ppermute | solution.py:327
  51.6 17.6 %collective-permute-start.11 = (bf16[1152,128]{1,0:T(8,128)(2,1)S(1)}, bf16[1152,128]{1,0:T(8,128)(2,1)S(1)}, u32[]{:S(2)}, u32[]{:S(2)}) collective-permute-start(bf16[1152,128]{1,0:T(8,128)(2,1)S(1)} %bitcast_add_fusion), channel_id=1, source_target_pairs={{0,24},{8,0},{16,8},{24,16},{1,25},{9,1},{17,9},{25,17},{2,26},{10... | collective-permute-start | bytes 884744 | tf_op jit(solution)/shard_map/ppermute | solution.py:335
  53.6 18.9 %collective-permute-start.10 = (bf16[1152,128]{1,0:T(8,128)(2,1)S(1)}, bf16[1152,128]{1,0:T(8,128)(2,1)S(1)}, u32[]{:S(2)}, u32[]{:S(2)}) collective-permute-start(bf16[1152,128]{1,0:T(8,128)(2,1)S(1)} %bitcast_add_fusion.1), channel_id=1, source_target_pairs={{0,8},{8,16},{16,24},{24,0},{1,9},{9,17},{17,25},{25,1},{2,10},{10... | collective-permute-start | bytes 884744 | tf_op jit(solution)/shard_map/ppermute | solution.py:334
  57.9 20.9 %collective-permute-start.13 = (bf16[1152,128]{1,0:T(8,128)(2,1)S(1)}, bf16[1152,128]{1,0:T(8,128)(2,1)S(1)}, u32[]{:S(2)}, u32[]{:S(2)}) collective-permute-start(bf16[1152,128]{1,0:T(8,128)(2,1)S(1)} %add.31), channel_id=1, source_target_pairs={{0,8},{8,16},{16,24},{24,0},{1,9},{9,17},{17,25},{25,1},{2,10},{10... | collective-permute-start | bytes 884744 | tf_op jit(solution)/shard_map/ppermute | solution.py:334
  66.0 19.4 %collective-permute-start.15 = (bf16[1152,128]{1,0:T(8,128)(2,1)S(1)}, bf16[1152,128]{1,0:T(8,128)(2,1)S(1)}, u32[]{:S(2)}, u32[]{:S(2)}) collective-permute-start(bf16[1152,128]{1,0:T(8,128)(2,1)S(1)} %add.32), channel_id=1, source_target_pairs={{0,24},{8,0},{16,8},{24,16},{1,25},{9,1},{17,9},{25,17},{2,26},{10... | collective-permute-start | bytes 884744 | tf_op jit(solution)/shard_map/ppermute | solution.py:335
  94.2 13.7 %collective-permute-start.17 = (bf16[1184,128]{1,0:T(8,128)(2,1)}, bf16[1184,128]{1,0:T(8,128)(2,1)S(1)}, u32[]{:S(2)}, u32[]{:S(2)}) collective-permute-start(bf16[1184,128]{1,0:T(8,128)(2,1)} %get-tuple-element.89.near.refs_2_), channel_id=1, source_target_pairs={{0,24},{2,26},{4,28},{6,30},{8,0},{10,2},{12,4},{14,6},{16,8},{18,... | collective-permute-start | bytes 909320 | tf_op jit(solution)/shard_map/ppermute | solution.py:350
  95.6 20.6 %collective-permute-start.16 = (bf16[1184,128]{1,0:T(8,128)(2,1)}, bf16[1184,128]{1,0:T(8,128)(2,1)S(1)}, u32[]{:S(2)}, u32[]{:S(2)}) collective-permute-start(bf16[1184,128]{1,0:T(8,128)(2,1)} %get-tuple-element.89.near.refs_2_), channel_id=1, source_target_pairs={{0,8},{2,10},{4,12},{6,14},{8,16},{10,18},{12,20},{14,22},{16,24},... | collective-permute-start | bytes 909320 | tf_op jit(solution)/shard_map/ppermute | solution.py:349
  95.7 26.4 %collective-permute-start.19 = (bf16[1152,128]{1,0:T(8,128)(2,1)}, bf16[1152,128]{1,0:T(8,128)(2,1)S(1)}, u32[]{:S(2)}, u32[]{:S(2)}) collective-permute-start(bf16[1152,128]{1,0:T(8,128)(2,1)} %get-tuple-element.90.refs_6_), channel_id=1, source_target_pairs={{0,10},{2,8},{4,14},{6,12},{8,18},{10,16},{12,22},{14,20},{16,26},... | collective-permute-start | bytes 884744 | tf_op jit(solution)/shard_map/ppermute | solution.py:349
  101.4 22.0 %collective-permute-start.18 = (bf16[1152,128]{1,0:T(8,128)(2,1)}, bf16[1152,128]{1,0:T(8,128)(2,1)S(1)}, u32[]{:S(2)}, u32[]{:S(2)}) collective-permute-start(bf16[1152,128]{1,0:T(8,128)(2,1)} %get-tuple-element.90.refs_6_), channel_id=1, source_target_pairs={{0,2},{2,0},{4,6},{6,4},{8,10},{10,8},{12,14},{14,12},{16,18},{18,... | collective-permute-start | bytes 884744 | tf_op jit(solution)/shard_map/ppermute | solution.py:351
  107.9 30.7 %collective-permute-start.23 = (bf16[1184,128]{1,0:T(8,128)(2,1)S(1)}, bf16[1184,128]{1,0:T(8,128)(2,1)S(1)}, u32[]{:S(2)}, u32[]{:S(2)}) collective-permute-start(bf16[1184,128]{1,0:T(8,128)(2,1)S(1)} %collective-permute-done.17.near_after.refs_4_), channel_id=1, source_target_pairs={{8,0},{16,8},{9,1},{17,9},{10,2},{18,10},{11,3},{19,11},{12,4},{20... | collective-permute-start | bytes 909320 | tf_op jit(solution)/shard_map/ppermute | solution.py:353
  116.2 22.4 %collective-permute-start.22 = (bf16[1184,128]{1,0:T(8,128)(2,1)S(1)}, bf16[1184,128]{1,0:T(8,128)(2,1)S(1)}, u32[]{:S(2)}, u32[]{:S(2)}) collective-permute-start(bf16[1184,128]{1,0:T(8,128)(2,1)S(1)} %collective-permute-done.16.near_before.refs_3_), channel_id=1, source_target_pairs={{8,16},{16,24},{9,17},{17,25},{10,18},{18,26},{11,19},{19,27},{12,... | collective-permute-start | bytes 909320 | tf_op jit(solution)/shard_map/ppermute | solution.py:352
  122.1 14.0 %collective-permute-start.25 = (bf16[1152,128]{1,0:T(8,128)(2,1)S(1)}, bf16[1152,128]{1,0:T(8,128)(2,1)S(1)}, u32[]{:S(2)}, u32[]{:S(2)}) collective-permute-start(bf16[1152,128]{1,0:T(8,128)(2,1)S(1)} %collective-permute-done.20.far_after), channel_id=1, source_target_pairs={{8,0},{16,8},{9,1},{17,9},{10,2},{18,10},{11,3},{19,11},{12,4},{20... | collective-permute-start | bytes 884744 | tf_op jit(solution)/shard_map/ppermute | solution.py:353
  123.4 12.8 %collective-permute-start.24 = (bf16[1152,128]{1,0:T(8,128)(2,1)S(1)}, bf16[1152,128]{1,0:T(8,128)(2,1)S(1)}, u32[]{:S(2)}, u32[]{:S(2)}) collective-permute-start(bf16[1152,128]{1,0:T(8,128)(2,1)S(1)} %collective-permute-done.19.far_before), channel_id=1, source_target_pairs={{8,16},{16,24},{9,17},{17,25},{10,18},{18,26},{11,19},{19,27},{12,... | collective-permute-start | bytes 884744 | tf_op jit(solution)/shard_map/ppermute | solution.py:352
  124.1 19.6 %collective-permute-start.29 = (bf16[192,128]{1,0:T(8,128)(2,1)}, bf16[192,128]{1,0:T(8,128)(2,1)S(1)}, u32[]{:S(2)}, u32[]{:S(2)}) collective-permute-start(bf16[192,128]{1,0:T(8,128)(2,1)} %get-tuple-element.101), channel_id=1, source_target_pairs={{0,8},{8,16},{16,24},{24,0},{1,9},{9,17},{17,25},{25,1},{2,10},{10... | collective-permute-start | bytes 147464 | tf_op jit(solution)/shard_map/ppermute | solution.py:459
  143.8 14.0 %collective-permute-start.32 = (bf16[2,1152,128]{2,1,0:T(8,128)(2,1)S(1)}, bf16[2,1152,128]{2,1,0:T(8,128)(2,1)S(1)}, u32[]{:S(2)}, u32[]{:S(2)}) collective-permute-start(bf16[2,1152,128]{2,1,0:T(8,128)(2,1)S(1)} %get-tuple-element.104), channel_id=1, source_target_pairs={{0,2},{2,0},{4,6},{6,4},{1,3},{3,1},{5,7},{7,5},{8,10},{10,8},{12,... | collective-permute-start | bytes 1769480 | tf_op jit(solution)/shard_map/ppermute | solution.py:498
  146.4 10.3 %collective-permute-start.28 = (bf16[192,512]{1,0:T(8,128)(2,1)}, bf16[192,512]{1,0:T(8,128)(2,1)S(1)}, u32[]{:S(2)}, u32[]{:S(2)}) collective-permute-start(bf16[192,512]{1,0:T(8,128)(2,1)} %get-tuple-element.98), channel_id=1, source_target_pairs={{5,0},{4,1},{7,2},{6,3},{1,4},{0,5},{3,6},{2,7},{13,8},{12,9},{15,... | collective-permute-start | bytes 589832 | tf_op jit(solution)/shard_map/ppermute | solution.py:500
  147.5 10.2 %collective-permute-start.33 = (bf16[1152,128]{1,0:T(8,128)(2,1)}, bf16[1152,128]{1,0:T(8,128)(2,1)S(1)}, u32[]{:S(2)}, u32[]{:S(2)}) collective-permute-start(bf16[1152,128]{1,0:T(8,128)(2,1)} %get-tuple-element.105), channel_id=1, source_target_pairs={{0,2},{2,0},{4,6},{6,4},{1,3},{3,1},{5,7},{7,5},{8,10},{10,8},{12,... | collective-permute-start | bytes 884744 | tf_op jit(solution)/shard_map/ppermute | solution.py:498
  157.8 11.2 %collective-permute-start.34 = (bf16[192,512]{1,0:T(8,128)(2,1)S(1)}, bf16[192,512]{1,0:T(8,128)(2,1)S(1)}, u32[]{:S(2)}, u32[]{:S(2)}) collective-permute-start(bf16[192,512]{1,0:T(8,128)(2,1)S(1)} %add_convert_fusion), channel_id=1, source_target_pairs={{0,0},{2,16},{4,8},{6,24},{8,2},{10,18},{12,10},{14,26},{16,4},{18... | collective-permute-start | bytes 589832 | tf_op jit(solution)/shard_map/ppermute | solution.py:505
  (42 other events, 374.8 us)

commit v19 on v16

--- a/solution.py
+++ b/solution.py
@@ -162,16 +162,25 @@
             out_refs[block * ncol + dx][...] = total[block * rows : (block + 1) * rows].astype(BF16)
 
 
+def transpose_body(x0_ref, x1_ref, out_ref):
+    nblocks, ncol, rows, depth = x0_ref.shape
+    tokens = nblocks * rows
+    col = lax.axis_index("col")
+    for dx in range(ncol):
+        start = pl.multiple_of(wrapped(col - dx, ncol) * depth, depth)
+        for k, x_ref in enumerate((x0_ref, x1_ref)):
+            out_ref[pl.ds(start, depth), k * tokens : (k + 1) * tokens] = x_ref[:, dx].reshape(tokens, depth).T
+
+
 def weight_grad_body(scale, *refs):
-    (x0_ref, x1_ref), near_refs, other_refs, mixed_refs, refs = refs[:2], refs[2:6], refs[6:9], refs[9:13], refs[13:]
+    xt_ref, near_refs, other_refs, mixed_refs, refs = refs[0], refs[1:5], refs[5:8], refs[8:12], refs[12:]
     own_ref, two_ref, last_ref = other_refs
     other = (own_ref, two_ref.at[0], two_ref.at[1], last_ref)
     out_ref, mixed_ref, long_ref, short_ref, held, held_mixed = refs
-    nblocks, ncol, rows, depth = x0_ref.shape
     _, ndp, _, width = held.shape
-    tokens = nblocks * rows
+    tokens = xt_ref.shape[1] // 2
     i = pl.program_id(0)
-    z, col = lax.axis_index("dp"), lax.axis_index("col")
+    z = lax.axis_index("dp")
 
     @pl.when(i == 0)
     def _():
@@ -195,14 +204,7 @@
     gm = jnp.concatenate(
         [jnp.concatenate([held[k, owner, at, :] for owner in range(ndp)], axis=1) for k in range(2)], axis=0
     )
-    for dx in range(ncol):
-        start = pl.multiple_of(wrapped(col - dx, ncol) * depth, depth)
-        x = jnp.concatenate(
-            [x_ref[:, dx].reshape(tokens, depth) for x_ref in (x0_ref, x1_ref)], axis=0
-        )
-        out_ref[0, pl.ds(start, depth), :] = scale * lax.dot_general(
-            x, gm, (((0,), (0,)), ((), ())), preferred_element_type=F32
-        )
+    out_ref[0] = scale * jnp.dot(xt_ref[...], gm, preferred_element_type=F32)
 
 
 def delayed(values, count):
@@ -428,6 +430,8 @@
         )(x, w)
         sums += sum_over_line(*(p.reshape(3 * chunk, width) for p in parts))
 
+    xt = kernel_call(transpose_body, shaped((drow, 2 * chunk), BF16))(x0, x1)
+    sums, xt = lax.optimization_barrier((sums, xt))
     extra = -(-(groups + 3 * nshort) // 16) * 16
     half = pl.BlockSpec((groups, ntaps, 2 * ntaps), lambda i: (0, 0, 0))
     other = pl.BlockSpec((groups, ntaps, 2 * ntaps), lambda i: (1, 0, 0))
@@ -509,7 +513,7 @@
             shaped((nshort, 3, local), F32),
         ],
         grid=(3,),
-        in_specs=[whole(nblocks, ncol, rows, dcol)] * 2
+        in_specs=[whole(drow, 2 * chunk)]
         + [whole(*grad_near.shape)] * 4
         + [whole(*grad_other.shape), whole(*far_two.shape), whole(*far_last.shape)]
         + [whole(rows, width)] * ndp,
@@ -526,7 +530,7 @@
         flops=2 * mm_flops,
         nbytes=2 * mm_bytes,
         vmem=MOST_VMEM_BYTES,
-    )(x0, x1, *near, near_last, grad_other, far_two, far_last, *mixed)
+    )(xt, *near, near_last, grad_other, far_two, far_last, *mixed)
     grad_weight = jnp.transpose(grad_weight, (1, 0, 2))
     return (mixed, grad_in, grad_weight, grad_long, grad_short)
 

time: 163 us -> 167 us (1.025)
  starting transfers between devices: 58.8 us -> 66.9 us
  waiting for transfers between devices: 59.9 us -> 56.6 us
    ppermute x3, starting transfers between devices: 7.22 us -> 13.4 us  [move_activations(): lax.ppermute(part, 'dp', [(a, (a + ahead) % ndp) for a in range(ndp)])]
    ppermute x2, waiting for transfers between devices: 1.89 us -> 0.01 us  [gather_over_line(): far_after = lax.ppermute(after, 'dp', [(a + 1, a) for a in range(ndp // 2)])]
    ppermute x2, waiting for transfers between devices: 10.3 us -> 8.5 us  [gather_over_line(): before = lax.ppermute(own, ('dp', 'row'), shift(1))]
    ppermute x2, waiting for transfers between devices: 10.2 us -> 12 us  [gather_over_line(): after = lax.ppermute(own, ('dp', 'row'), shift(-1))]
    ppermute x2, waiting for transfers between devices: 8.37 us -> 6.67 us  [sum_over_line(): lax.ppermute(right + from_left, 'dp', [(a, (a + 1) % ndp) for a in range(...]
    unnamed x61 -> x57, local copies, waits for them, and re-layouts: 8.13 us -> 7.76 us
  transfers between devices with their start and end apart: 35 -> 35, of which waited for: 17 -> 15; matrix products, arithmetic and copies ran while one was open for 2% -> 2% of each run, Pallas kernels for 19% -> 19%
where the time goes in v19:
time: 167 us
  starting transfers between devices  66.9 us (40%)
  waiting for transfers between devices  56.6 us (34%)
  Pallas kernels  31.3 us (19%)
  local copies, waits for them, and re-layouts  8.45 us (5%)
  other arithmetic  2.19 us (1%)
    ppermute x3, starting transfers between devices, move_activations(): lax.ppermute(part, 'dp', [(a, (a + ahead) % ndp) for a in range(ndp)])  13.4 us
    ppermute x2, waiting for transfers between devices, gather_over_line(): after = lax.ppermute(own, ('dp', 'row'), shift(-1))  12 us
    ppermute x2, waiting for transfers between devices, gather_over_line(): before = lax.ppermute(own, ('dp', 'row'), shift(1))  8.5 us
    ppermute x3, waiting for transfers between devices, move_activations(): lax.ppermute(sent, ('row', 'col'), [(b, a) for a, b in offset(*p)])  8.11 us
    unnamed x57, local copies, waits for them, and re-layouts  7.76 us
    pallas_call x2, Pallas kernels, move_activations(): kernel_call(project_body, [shaped((3, chunk, width), BF16)] * ndp, grid=(...  7.66 us
    ppermute x1, waiting for transfers between devices, move_activations(): moved = lax.ppermute(tokens, ('dp', 'row'), swap)  7.43 us
    pallas_call x1, Pallas kernels, move_activations(): kernel_call(functools.partial(weight_grad_body, scale), [shaped((3, drow,...  6.99 us
  transfers between devices with their start and end apart: 35, of which 15 were waited for; matrix products, arithmetic and copies ran while one was open for 2% of the time, Pallas kernels for 19%

profile of v19, /device:TPU:1, one launch (start us, length us, event | category | flops | bytes accessed | tf_op | source)
XLA Modules:
  0.0 166.5 jit_solution(8953594433864918895)
XLA Ops:
  0.6 4.6 %collective-permute-start = (bf16[192,512]{1,0:T(8,128)(2,1)}, bf16[192,512]{1,0:T(8,128)(2,1)S(1)}, u32[]{:S(2)}, u32[]{:S(2)}) collective-permute-start(bf16[192,512]{1,0:T(8,128)(2,1)} %param.5), channel_id=1, source_target_pairs={{0,0},{16,2},{8,4},{24,6},{2,8},{18,10},{10,12},{26,14},{4,16},{20... | collective-permute-start | bytes 589832 | tf_op jit(solution)/shard_map/ppermute | solution.py:382
  8.0 7.4 %collective-permute-done = bf16[192,512]{1,0:T(8,128)(2,1)S(1)} collective-permute-done((bf16[192,512]{1,0:T(8,128)(2,1)}, bf16[192,512]{1,0:T(8,128)(2,1)S(1)}, u32[]{:S(2)}, u32[]{:S(2)}) %collective-permute-start) | collective-permute-done | bytes 196640 | tf_op jit(solution)/shard_map/ppermute | solution.py:382
  25.1 3.8 %shard_map.94 = (bf16[3,384,128]{2,1,0:T(8,128)(2,1)S(1)}, bf16[3,384,128]{2,1,0:T(8,128)(2,1)S(1)}, bf16[3,384,128]{2,1,0:T(8,128)(2,1)S(1)}, bf16[3,384,128]{2,1,0:T(8,128)(2,1)S(1)}) custom-call(bf16[2,2,192,512]{3,2,1,0:T(8,128)(2,1)S(1)} %bitcast.20, bf16[3,1024,512]{2,1,0:T(8,128)(2,1)} %bitcast.w_ref), custom_call_target="tpu_custom_call" | custom-call | flops 1207959552 | bytes 5111808 | tf_op jit(solution)/shard_map/pallas_call | solution.py:418
  30.8 6.2 %collective-permute-start.10 = (bf16[192,128]{1,0:T(8,128)(2,1)S(1)}, bf16[192,128]{1,0:T(8,128)(2,1)S(1)}, u32[]{:S(2)}, u32[]{:S(2)}) collective-permute-start(bf16[192,128]{1,0:T(8,128)(2,1)S(1)} %get-tuple-element.77), channel_id=1, source_target_pairs={{0,16},{8,24},{16,0},{24,8},{1,17},{9,25},{17,1},{25,9},{2,18},{10... | collective-permute-start | bytes 147464 | tf_op jit(solution)/shard_map/ppermute | solution.py:399
  38.5 3.1 %collective-permute-start.9 = (bf16[1152,128]{1,0:T(8,128)(2,1)S(1)}, bf16[1152,128]{1,0:T(8,128)(2,1)S(1)}, u32[]{:S(2)}, u32[]{:S(2)}) collective-permute-start(bf16[1152,128]{1,0:T(8,128)(2,1)S(1)} %bitcast_add_fusion.2), channel_id=1, source_target_pairs={{0,24},{8,0},{16,8},{24,16},{1,25},{9,1},{17,9},{25,17},{2,26},{10... | collective-permute-start | bytes 884744 | tf_op jit(solution)/shard_map/ppermute | solution.py:336
  41.6 4.4 %collective-permute-done.10.refs_11_ = bf16[192,128]{1,0:T(8,128)(2,1)S(1)} collective-permute-done((bf16[192,128]{1,0:T(8,128)(2,1)S(1)}, bf16[192,128]{1,0:T(8,128)(2,1)S(1)}, u32[]{:S(2)}, u32[]{:S(2)}) %collective-permute-start.10) | collective-permute-done | bytes 49184 | tf_op jit(solution)/shard_map/ppermute | solution.py:399
  46.0 3.8 %shard_map.95 = (bf16[3,384,128]{2,1,0:T(8,128)(2,1)S(1)}, bf16[3,384,128]{2,1,0:T(8,128)(2,1)S(1)}, bf16[3,384,128]{2,1,0:T(8,128)(2,1)S(1)}, bf16[3,384,128]{2,1,0:T(8,128)(2,1)S(1)}) custom-call(bf16[2,2,192,512]{3,2,1,0:T(8,128)(2,1)S(1)} %collective-permute-done.11.x_ref.x1_ref, bf16[3,1024,512]{2,1,0:T(8,128)(2,1)} %bitcast.w_ref), custom_call_target="tpu_custom_call" | custom-call | flops 1207959552 | bytes 5111808 | tf_op jit(solution)/shard_map/pallas_call | solution.py:418
  50.7 4.0 %collective-permute-start.12 = (bf16[1152,128]{1,0:T(8,128)(2,1)S(1)}, bf16[1152,128]{1,0:T(8,128)(2,1)S(1)}, u32[]{:S(2)}, u32[]{:S(2)}) collective-permute-start(bf16[1152,128]{1,0:T(8,128)(2,1)S(1)} %bitcast.25), channel_id=1, source_target_pairs={{0,8},{8,16},{1,9},{9,17},{2,10},{10,18},{3,11},{11,19},{4,12},{12... | collective-permute-start | bytes 884744 | tf_op jit(solution)/shard_map/ppermute | solution.py:333
  54.8 3.7 %collective-permute-start.15 = (bf16[1152,128]{1,0:T(8,128)(2,1)S(1)}, bf16[1152,128]{1,0:T(8,128)(2,1)}, u32[]{:S(2)}, u32[]{:S(2)}) collective-permute-start(bf16[1152,128]{1,0:T(8,128)(2,1)S(1)} %bitcast_add_fusion), channel_id=1, source_target_pairs={{0,24},{8,0},{16,8},{24,16},{1,25},{9,1},{17,9},{25,17},{2,26},{10... | collective-permute-start | bytes 884744 | tf_op jit(solution)/shard_map/ppermute | solution.py:336
  58.4 4.3 %collective-permute-done.12 = bf16[1152,128]{1,0:T(8,128)(2,1)S(1)} collective-permute-done((bf16[1152,128]{1,0:T(8,128)(2,1)S(1)}, bf16[1152,128]{1,0:T(8,128)(2,1)S(1)}, u32[]{:S(2)}, u32[]{:S(2)}) %collective-permute-start.12) | collective-permute-done | bytes 294944 | tf_op jit(solution)/shard_map/ppermute | solution.py:333
  71.5 6.7 %collective-permute-done.13.refs_4_ = bf16[1152,128]{1,0:T(8,128)(2,1)} collective-permute-done((bf16[1152,128]{1,0:T(8,128)(2,1)S(1)}, bf16[1152,128]{1,0:T(8,128)(2,1)}, u32[]{:S(2)}, u32[]{:S(2)}) %collective-permute-start.13) | collective-permute-done | bytes 294944 | tf_op jit(solution)/shard_map/ppermute | solution.py:335
  78.1 5.4 %shard_map.98 = (bf16[1184,128]{1,0:T(8,128)(2,1)}, bf16[1152,128]{1,0:T(8,128)(2,1)}, bf16[192,128]{1,0:T(8,128)(2,1)}, bf16[192,128]{1,0:T(8,128)(2,1)}, bf16[...) custom-call(bf16[1152,128]{1,0:T(8,128)(2,1)} %bitcast.26, bf16[1152,128]{1,0:T(8,128)(2,1)} %copy-done.18, ...), custom_call_target="tpu_custom_call" | custom-call | flops 1207959552 | bytes 2752512 | tf_op jit(solution)/shard_map/pallas_call | solution.py:439
  83.6 2.9 %collective-permute-start.20 = (bf16[1152,128]{1,0:T(8,128)(2,1)}, bf16[1152,128]{1,0:T(8,128)(2,1)S(1)}, u32[]{:S(2)}, u32[]{:S(2)}) collective-permute-start(bf16[1152,128]{1,0:T(8,128)(2,1)} %get-tuple-element.95.refs_5_), channel_id=1, source_target_pairs={{0,26},{2,24},{4,30},{6,28},{8,2},{10,0},{12,6},{14,4},{16,10},{18... | collective-permute-start | bytes 884744 | tf_op jit(solution)/shard_map/ppermute | solution.py:351
  88.5 5.3 %collective-permute-done.20.far_after = bf16[1152,128]{1,0:T(8,128)(2,1)S(1)} collective-permute-done((bf16[1152,128]{1,0:T(8,128)(2,1)}, bf16[1152,128]{1,0:T(8,128)(2,1)S(1)}, u32[]{:S(2)}, u32[]{:S(2)}) %collective-permute-start.20) | collective-permute-done | bytes 294944 | tf_op jit(solution)/shard_map/ppermute | solution.py:351
  95.5 6.7 %collective-permute-done.17.near_after.refs_3_ = bf16[1184,128]{1,0:T(8,128)(2,1)S(1)} collective-permute-done((bf16[1184,128]{1,0:T(8,128)(2,1)}, bf16[1184,128]{1,0:T(8,128)(2,1)S(1)}, u32[]{:S(2)}, u32[]{:S(2)}) %collective-permute-start.17) | collective-permute-done | bytes 303136 | tf_op jit(solution)/shard_map/ppermute | solution.py:351
  103.6 5.3 %collective-permute-done.16.near_before.refs_2_ = bf16[1184,128]{1,0:T(8,128)(2,1)S(1)} collective-permute-done((bf16[1184,128]{1,0:T(8,128)(2,1)}, bf16[1184,128]{1,0:T(8,128)(2,1)S(1)}, u32[]{:S(2)}, u32[]{:S(2)}) %collective-permute-start.16) | collective-permute-done | bytes 303136 | tf_op jit(solution)/shard_map/ppermute | solution.py:350
  109.5 3.2 %collective-permute-done.19.far_before = bf16[1152,128]{1,0:T(8,128)(2,1)S(1)} collective-permute-done((bf16[1152,128]{1,0:T(8,128)(2,1)}, bf16[1152,128]{1,0:T(8,128)(2,1)S(1)}, u32[]{:S(2)}, u32[]{:S(2)}) %collective-permute-start.19) | collective-permute-done | bytes 294944 | tf_op jit(solution)/shard_map/ppermute | solution.py:350
  114.7 10.7 %collective-permute-start.29 = (bf16[192,128]{1,0:T(8,128)(2,1)}, bf16[192,128]{1,0:T(8,128)(2,1)S(1)}, u32[]{:S(2)}, u32[]{:S(2)}) collective-permute-start(bf16[192,128]{1,0:T(8,128)(2,1)} %get-tuple-element.105), channel_id=1, source_target_pairs={{0,8},{8,16},{16,24},{24,0},{1,9},{9,17},{17,25},{25,1},{2,10},{10... | collective-permute-start | bytes 147464 | tf_op jit(solution)/shard_map/ppermute | solution.py:459
  126.4 4.6 %shard_map.99 = (bf16[2,384,512]{2,1,0:T(8,128)(2,1)S(1)}, bf16[2,1152,128]{2,1,0:T(8,128)(2,1)S(1)}) custom-call(bf16[1184,128]{1,0:T(8,128)(2,1)S(1)} %copy-done.6, bf16[1184,128]{1,0:T(8,128)(2,1)S(1)} %collective-permute-done.16.near_before.refs_2_, bf16[1184,128]{1,0:T(8,128)(2,1)S(1)} %collective-permute-done.17.near_after.refs_3_, ...), custom_call_target="tpu_custom_call" | custom-call | flops 2415919104 | bytes 10223616 | tf_op jit(solution)/shard_map/pallas_call | solution.py:468
  135.5 4.3 %shard_map.100 = (bf16[1184,128]{1,0:T(8,128)(2,1)}, bf16[1152,128]{1,0:T(8,128)(2,1)}, bf16[192,512]{1,0:T(8,128)(2,1)}, bf16[192,512]{1,0:T(8,128)(2,1)}, bf16...) custom-call(bf16[2,384,512]{2,1,0:T(8,128)(2,1)} %copy-done.4, bf16[1184,128]{1,0:T(8,128)(2,1)} %copy-done.13, ...), custom_call_target="tpu_custom_call" | custom-call | flops 603979776 | bytes 2555904 | tf_op jit(solution)/shard_map/pallas_call | solution.py:481
  145.1 3.1 %collective-permute-done.26 = bf16[192,512]{1,0:T(8,128)(2,1)S(1)} collective-permute-done((bf16[192,512]{1,0:T(8,128)(2,1)}, bf16[192,512]{1,0:T(8,128)(2,1)S(1)}, u32[]{:S(2)}, u32[]{:S(2)}) %collective-permute-start.26) | collective-permute-done | bytes 196640 | tf_op jit(solution)/shard_map/ppermute | solution.py:500
  149.2 3.9 %collective-permute-done.28 = bf16[192,512]{1,0:T(8,128)(2,1)S(1)} collective-permute-done((bf16[192,512]{1,0:T(8,128)(2,1)}, bf16[192,512]{1,0:T(8,128)(2,1)S(1)}, u32[]{:S(2)}, u32[]{:S(2)}) %collective-permute-start.28) | collective-permute-done | bytes 196640 | tf_op jit(solution)/shard_map/ppermute | solution.py:500
  154.2 4.6 %collective-permute-start.34 = (bf16[192,512]{1,0:T(8,128)(2,1)S(1)}, bf16[192,512]{1,0:T(8,128)(2,1)S(1)}, u32[]{:S(2)}, u32[]{:S(2)}) collective-permute-start(bf16[192,512]{1,0:T(8,128)(2,1)S(1)} %add_convert_fusion), channel_id=1, source_target_pairs={{0,0},{2,16},{4,8},{6,24},{8,2},{10,18},{12,10},{14,26},{16,4},{18... | collective-permute-start | bytes 589832 | tf_op jit(solution)/shard_map/ppermute | solution.py:505
  158.9 7.0 %shard_map.101 = (f32[3,1024,512]{2,1,0:T(8,128)}, bf16[192,512]{1,0:T(8,128)(2,1)}, f32[32,128]{1,0:T(8,128)}, f32[3,3,512]{2,1,0:T(4,128)}) custom-call(bf16[1024,768]{1,0:T(8,128)(2,1)} %copy-done.2, bf16[1184,128]{1,0:T(8,128)(2,1)} %get-tuple-element.94.near.refs_1_, bf16[1184,128]{1,0:T(8,128)(2,1)} %copy-done.8, bf16[1184,128]{1,0:T(8,128)(2,1)} %copy-done.7, ...), custom_call_target="tpu_custom_call" | custom-call | flops 2415919104 | bytes 10223616 | tf_op jit(solution)/shard_map/pallas_call | solution.py:507
  (126 shorter events, 46.3 us)
Async XLA Ops:
  0.6 14.8 %collective-permute-start = (bf16[192,512]{1,0:T(8,128)(2,1)}, bf16[192,512]{1,0:T(8,128)(2,1)S(1)}, u32[]{:S(2)}, u32[]{:S(2)}) collective-permute-start(bf16[192,512]{1,0:T(8,128)(2,1)} %param.5), channel_id=1, source_target_pairs={{0,0},{16,2},{8,4},{24,6},{2,8},{18,10},{10,12},{26,14},{4,16},{20... | collective-permute-start | bytes 589832 | tf_op jit(solution)/shard_map/ppermute | solution.py:382
  25.0 21.0 %collective-permute-start.11 = (bf16[2,2,192,512]{3,2,1,0:T(8,128)(2,1)S(1)}, bf16[2,2,192,512]{3,2,1,0:T(8,128)(2,1)S(1)}, u32[]{:S(2)}, u32[]{:S(2)}) collective-permute-start(bf16[2,2,192,512]{3,2,1,0:T(8,128)(2,1)S(1)} %bitcast.19), channel_id=1, source_target_pairs={{0,2},{2,0},{4,6},{6,4},{1,3},{3,1},{5,7},{7,5},{8,10},{10,8},{12,... | collective-permute-start | bytes 2359304 | tf_op jit(solution)/shard_map/ppermute | solution.py:398
  30.3 84.4 %collective-permute-start.21 = (bf16[3,1024,512]{2,1,0:T(8,128)(2,1)}, bf16[3,1024,512]{2,1,0:T(8,128)(2,1)}, u32[]{:S(2)}, u32[]{:S(2)}) collective-permute-start(bf16[3,1024,512]{2,1,0:T(8,128)(2,1)} %bitcast.w_ref), channel_id=1, source_target_pairs={{0,2},{2,0},{4,6},{6,4},{1,3},{3,1},{5,7},{7,5},{8,10},{10,8},{12,... | collective-permute-start | bytes 9437192 | tf_op jit(solution)/shard_map/ppermute | solution.py:465
  30.8 15.1 %collective-permute-start.10 = (bf16[192,128]{1,0:T(8,128)(2,1)S(1)}, bf16[192,128]{1,0:T(8,128)(2,1)S(1)}, u32[]{:S(2)}, u32[]{:S(2)}) collective-permute-start(bf16[192,128]{1,0:T(8,128)(2,1)S(1)} %get-tuple-element.77), channel_id=1, source_target_pairs={{0,16},{8,24},{16,0},{24,8},{1,17},{9,25},{17,1},{25,9},{2,18},{10... | collective-permute-start | bytes 147464 | tf_op jit(solution)/shard_map/ppermute | solution.py:399
  37.1 13.4 %collective-permute-start.6 = (bf16[1152,128]{1,0:T(8,128)(2,1)S(1)}, bf16[1152,128]{1,0:T(8,128)(2,1)S(1)}, u32[]{:S(2)}, u32[]{:S(2)}) collective-permute-start(bf16[1152,128]{1,0:T(8,128)(2,1)S(1)} %bitcast.23), channel_id=1, source_target_pairs={{0,8},{8,16},{1,9},{9,17},{2,10},{10,18},{3,11},{11,19},{4,12},{12... | collective-permute-start | bytes 884744 | tf_op jit(solution)/shard_map/ppermute | solution.py:333
  38.5 31.3 %collective-permute-start.9 = (bf16[1152,128]{1,0:T(8,128)(2,1)S(1)}, bf16[1152,128]{1,0:T(8,128)(2,1)S(1)}, u32[]{:S(2)}, u32[]{:S(2)}) collective-permute-start(bf16[1152,128]{1,0:T(8,128)(2,1)S(1)} %bitcast_add_fusion.2), channel_id=1, source_target_pairs={{0,24},{8,0},{16,8},{24,16},{1,25},{9,1},{17,9},{25,17},{2,26},{10... | collective-permute-start | bytes 884744 | tf_op jit(solution)/shard_map/ppermute | solution.py:336
  50.6 19.2 %collective-permute-start.7 = (bf16[1152,128]{1,0:T(8,128)(2,1)S(1)}, bf16[1152,128]{1,0:T(8,128)(2,1)S(1)}, u32[]{:S(2)}, u32[]{:S(2)}) collective-permute-start(bf16[1152,128]{1,0:T(8,128)(2,1)S(1)} %bitcast_add_fusion.3), channel_id=1, source_target_pairs={{0,8},{8,16},{16,24},{24,0},{1,9},{9,17},{17,25},{25,1},{2,10},{10... | collective-permute-start | bytes 884744 | tf_op jit(solution)/shard_map/ppermute | solution.py:335
  50.7 12.1 %collective-permute-start.12 = (bf16[1152,128]{1,0:T(8,128)(2,1)S(1)}, bf16[1152,128]{1,0:T(8,128)(2,1)S(1)}, u32[]{:S(2)}, u32[]{:S(2)}) collective-permute-start(bf16[1152,128]{1,0:T(8,128)(2,1)S(1)} %bitcast.25), channel_id=1, source_target_pairs={{0,8},{8,16},{1,9},{9,17},{2,10},{10,18},{3,11},{11,19},{4,12},{12... | collective-permute-start | bytes 884744 | tf_op jit(solution)/shard_map/ppermute | solution.py:333
  54.8 16.7 %collective-permute-start.15 = (bf16[1152,128]{1,0:T(8,128)(2,1)S(1)}, bf16[1152,128]{1,0:T(8,128)(2,1)}, u32[]{:S(2)}, u32[]{:S(2)}) collective-permute-start(bf16[1152,128]{1,0:T(8,128)(2,1)S(1)} %bitcast_add_fusion), channel_id=1, source_target_pairs={{0,24},{8,0},{16,8},{24,16},{1,25},{9,1},{17,9},{25,17},{2,26},{10... | collective-permute-start | bytes 884744 | tf_op jit(solution)/shard_map/ppermute | solution.py:336
  62.8 15.3 %collective-permute-start.13 = (bf16[1152,128]{1,0:T(8,128)(2,1)S(1)}, bf16[1152,128]{1,0:T(8,128)(2,1)}, u32[]{:S(2)}, u32[]{:S(2)}) collective-permute-start(bf16[1152,128]{1,0:T(8,128)(2,1)S(1)} %bitcast_add_fusion.1), channel_id=1, source_target_pairs={{0,8},{8,16},{16,24},{24,0},{1,9},{9,17},{17,25},{25,1},{2,10},{10... | collective-permute-start | bytes 884744 | tf_op jit(solution)/shard_map/ppermute | solution.py:335
  83.6 10.1 %collective-permute-start.20 = (bf16[1152,128]{1,0:T(8,128)(2,1)}, bf16[1152,128]{1,0:T(8,128)(2,1)S(1)}, u32[]{:S(2)}, u32[]{:S(2)}) collective-permute-start(bf16[1152,128]{1,0:T(8,128)(2,1)} %get-tuple-element.95.refs_5_), channel_id=1, source_target_pairs={{0,26},{2,24},{4,30},{6,28},{8,2},{10,0},{12,6},{14,4},{16,10},{18... | collective-permute-start | bytes 884744 | tf_op jit(solution)/shard_map/ppermute | solution.py:351
  86.5 15.8 %collective-permute-start.17 = (bf16[1184,128]{1,0:T(8,128)(2,1)}, bf16[1184,128]{1,0:T(8,128)(2,1)S(1)}, u32[]{:S(2)}, u32[]{:S(2)}) collective-permute-start(bf16[1184,128]{1,0:T(8,128)(2,1)} %get-tuple-element.94.near.refs_1_), channel_id=1, source_target_pairs={{0,24},{2,26},{4,28},{6,30},{8,0},{10,2},{12,4},{14,6},{16,8},{18,... | collective-permute-start | bytes 909320 | tf_op jit(solution)/shard_map/ppermute | solution.py:351
  88.2 20.6 %collective-permute-start.16 = (bf16[1184,128]{1,0:T(8,128)(2,1)}, bf16[1184,128]{1,0:T(8,128)(2,1)S(1)}, u32[]{:S(2)}, u32[]{:S(2)}) collective-permute-start(bf16[1184,128]{1,0:T(8,128)(2,1)} %get-tuple-element.94.near.refs_1_), channel_id=1, source_target_pairs={{0,8},{2,10},{4,12},{6,14},{8,16},{10,18},{12,20},{14,22},{16,24},... | collective-permute-start | bytes 909320 | tf_op jit(solution)/shard_map/ppermute | solution.py:350
  88.2 24.5 %collective-permute-start.19 = (bf16[1152,128]{1,0:T(8,128)(2,1)}, bf16[1152,128]{1,0:T(8,128)(2,1)S(1)}, u32[]{:S(2)}, u32[]{:S(2)}) collective-permute-start(bf16[1152,128]{1,0:T(8,128)(2,1)} %get-tuple-element.95.refs_5_), channel_id=1, source_target_pairs={{0,10},{2,8},{4,14},{6,12},{8,18},{10,16},{12,22},{14,20},{16,26},... | collective-permute-start | bytes 884744 | tf_op jit(solution)/shard_map/ppermute | solution.py:350
  93.7 20.3 %collective-permute-start.18 = (bf16[1152,128]{1,0:T(8,128)(2,1)}, bf16[1152,128]{1,0:T(8,128)(2,1)S(1)}, u32[]{:S(2)}, u32[]{:S(2)}) collective-permute-start(bf16[1152,128]{1,0:T(8,128)(2,1)} %get-tuple-element.95.refs_5_), channel_id=1, source_target_pairs={{0,2},{2,0},{4,6},{6,4},{8,10},{10,8},{12,14},{14,12},{16,18},{18,... | collective-permute-start | bytes 884744 | tf_op jit(solution)/shard_map/ppermute | solution.py:352
  102.3 32.4 %collective-permute-start.23 = (bf16[1184,128]{1,0:T(8,128)(2,1)S(1)}, bf16[1184,128]{1,0:T(8,128)(2,1)S(1)}, u32[]{:S(2)}, u32[]{:S(2)}) collective-permute-start(bf16[1184,128]{1,0:T(8,128)(2,1)S(1)} %collective-permute-done.17.near_after.refs_3_), channel_id=1, source_target_pairs={{8,0},{16,8},{9,1},{17,9},{10,2},{18,10},{11,3},{19,11},{12,4},{20... | collective-permute-start | bytes 909320 | tf_op jit(solution)/shard_map/ppermute | solution.py:354
  108.9 25.9 %collective-permute-start.22 = (bf16[1184,128]{1,0:T(8,128)(2,1)S(1)}, bf16[1184,128]{1,0:T(8,128)(2,1)S(1)}, u32[]{:S(2)}, u32[]{:S(2)}) collective-permute-start(bf16[1184,128]{1,0:T(8,128)(2,1)S(1)} %collective-permute-done.16.near_before.refs_2_), channel_id=1, source_target_pairs={{8,16},{16,24},{9,17},{17,25},{10,18},{18,26},{11,19},{19,27},{12,... | collective-permute-start | bytes 909320 | tf_op jit(solution)/shard_map/ppermute | solution.py:353
  112.7 19.2 %collective-permute-start.25 = (bf16[1152,128]{1,0:T(8,128)(2,1)S(1)}, bf16[1152,128]{1,0:T(8,128)(2,1)S(1)}, u32[]{:S(2)}, u32[]{:S(2)}) collective-permute-start(bf16[1152,128]{1,0:T(8,128)(2,1)S(1)} %collective-permute-done.20.far_after), channel_id=1, source_target_pairs={{8,0},{16,8},{9,1},{17,9},{10,2},{18,10},{11,3},{19,11},{12,4},{20... | collective-permute-start | bytes 884744 | tf_op jit(solution)/shard_map/ppermute | solution.py:354
  114.0 18.0 %collective-permute-start.24 = (bf16[1152,128]{1,0:T(8,128)(2,1)S(1)}, bf16[1152,128]{1,0:T(8,128)(2,1)S(1)}, u32[]{:S(2)}, u32[]{:S(2)}) collective-permute-start(bf16[1152,128]{1,0:T(8,128)(2,1)S(1)} %collective-permute-done.19.far_before), channel_id=1, source_target_pairs={{8,16},{16,24},{9,17},{17,25},{10,18},{18,26},{11,19},{19,27},{12,... | collective-permute-start | bytes 884744 | tf_op jit(solution)/shard_map/ppermute | solution.py:353
  114.7 25.1 %collective-permute-start.29 = (bf16[192,128]{1,0:T(8,128)(2,1)}, bf16[192,128]{1,0:T(8,128)(2,1)S(1)}, u32[]{:S(2)}, u32[]{:S(2)}) collective-permute-start(bf16[192,128]{1,0:T(8,128)(2,1)} %get-tuple-element.105), channel_id=1, source_target_pairs={{0,8},{8,16},{16,24},{24,0},{1,9},{9,17},{17,25},{25,1},{2,10},{10... | collective-permute-start | bytes 147464 | tf_op jit(solution)/shard_map/ppermute | solution.py:459
  139.9 14.4 %collective-permute-start.32 = (bf16[2,1152,128]{2,1,0:T(8,128)(2,1)S(1)}, bf16[2,1152,128]{2,1,0:T(8,128)(2,1)S(1)}, u32[]{:S(2)}, u32[]{:S(2)}) collective-permute-start(bf16[2,1152,128]{2,1,0:T(8,128)(2,1)S(1)} %get-tuple-element.108), channel_id=1, source_target_pairs={{0,2},{2,0},{4,6},{6,4},{1,3},{3,1},{5,7},{7,5},{8,10},{10,8},{12,... | collective-permute-start | bytes 1769480 | tf_op jit(solution)/shard_map/ppermute | solution.py:498
  142.7 10.4 %collective-permute-start.28 = (bf16[192,512]{1,0:T(8,128)(2,1)}, bf16[192,512]{1,0:T(8,128)(2,1)S(1)}, u32[]{:S(2)}, u32[]{:S(2)}) collective-permute-start(bf16[192,512]{1,0:T(8,128)(2,1)} %get-tuple-element.102), channel_id=1, source_target_pairs={{5,0},{4,1},{7,2},{6,3},{1,4},{0,5},{3,6},{2,7},{13,8},{12,9},{15,... | collective-permute-start | bytes 589832 | tf_op jit(solution)/shard_map/ppermute | solution.py:500
  144.2 10.0 %collective-permute-start.33 = (bf16[1152,128]{1,0:T(8,128)(2,1)}, bf16[1152,128]{1,0:T(8,128)(2,1)S(1)}, u32[]{:S(2)}, u32[]{:S(2)}) collective-permute-start(bf16[1152,128]{1,0:T(8,128)(2,1)} %get-tuple-element.109), channel_id=1, source_target_pairs={{0,2},{2,0},{4,6},{6,4},{1,3},{3,1},{5,7},{7,5},{8,10},{10,8},{12,... | collective-permute-start | bytes 884744 | tf_op jit(solution)/shard_map/ppermute | solution.py:498
  154.2 11.6 %collective-permute-start.34 = (bf16[192,512]{1,0:T(8,128)(2,1)S(1)}, bf16[192,512]{1,0:T(8,128)(2,1)S(1)}, u32[]{:S(2)}, u32[]{:S(2)}) collective-permute-start(bf16[192,512]{1,0:T(8,128)(2,1)S(1)} %add_convert_fusion), channel_id=1, source_target_pairs={{0,0},{2,16},{4,8},{6,24},{8,2},{10,18},{12,10},{14,26},{16,4},{18... | collective-permute-start | bytes 589832 | tf_op jit(solution)/shard_map/ppermute | solution.py:505
  (39 other events, 375.9 us)

commit v20 on v16

--- a/solution.py
+++ b/solution.py
@@ -525,7 +525,6 @@
         ],
         flops=2 * mm_flops,
         nbytes=2 * mm_bytes,
-        vmem=MOST_VMEM_BYTES,
     )(x0, x1, *near, near_last, grad_other, far_two, far_last, *mixed)
     grad_weight = jnp.transpose(grad_weight, (1, 0, 2))
     return (mixed, grad_in, grad_weight, grad_long, grad_short)

time: 163 us -> 166 us (1.018)
  local copies, waits for them, and re-layouts: 8.81 us -> 14.9 us
  Pallas kernels: 31.3 us -> 29.5 us
    unnamed x61 -> x55, local copies, waits for them, and re-layouts: 8.13 us -> 14.2 us
  transfers between devices with their start and end apart: 35 -> 35, of which waited for: 17 -> 16; matrix products, arithmetic and copies ran while one was open for 2% -> 2% of each run, Pallas kernels for 19% -> 18%
where the time goes in v20:
time: 166 us; the launch traced here: 165 us
  waiting for transfers between devices  58.8 us (35%)
  starting transfers between devices  58.4 us (35%)
  Pallas kernels  29.5 us (18%)
  local copies, waits for them, and re-layouts  14.9 us (9%)
  other arithmetic  2.19 us (1%)
    unnamed x55, local copies, waits for them, and re-layouts  14.2 us
    ppermute x2, waiting for transfers between devices, gather_over_line(): after = lax.ppermute(own, ('dp', 'row'), shift(-1))  10.4 us
    ppermute x2, waiting for transfers between devices, gather_over_line(): before = lax.ppermute(own, ('dp', 'row'), shift(1))  10.3 us
    ppermute x3, waiting for transfers between devices, move_activations(): lax.ppermute(sent, ('row', 'col'), [(b, a) for a, b in offset(*p)])  8.09 us
    pallas_call x2, Pallas kernels, move_activations(): kernel_call(project_body, [shaped((3, chunk, width), BF16)] * ndp, grid=(...  7.64 us
    ppermute x2, waiting for transfers between devices, sum_over_line(): lax.ppermute(right + from_left, 'dp', [(a, (a + 1) % ndp) for a in range(...  7.62 us
    ppermute x3, starting transfers between devices, move_activations(): lax.ppermute(part, 'dp', [(a, (a + ahead) % ndp) for a in range(ndp)])  6.97 us
    ppermute x2, starting transfers between devices, sum_over_line(): lax.ppermute(left + from_right, 'dp', [(a, (a - 1) % ndp) for a in range(...  6.76 us
  transfers between devices with their start and end apart: 35, of which 16 were waited for; matrix products, arithmetic and copies ran while one was open for 2% of the time, Pallas kernels for 18%

profile of v20, /device:TPU:1, one launch (start us, length us, event | category | flops | bytes accessed | tf_op | source)
XLA Modules:
  0.0 164.8 jit_solution(197039547990074925)
XLA Ops:
  0.6 4.6 %collective-permute-start = (bf16[192,512]{1,0:T(8,128)(2,1)}, bf16[192,512]{1,0:T(8,128)(2,1)S(1)}, u32[]{:S(2)}, u32[]{:S(2)}) collective-permute-start(bf16[192,512]{1,0:T(8,128)(2,1)} %param.5), channel_id=1, source_target_pairs={{0,0},{16,2},{8,4},{24,6},{2,8},{18,10},{10,12},{26,14},{4,16},{20... | collective-permute-start | bytes 589832 | tf_op jit(solution)/shard_map/ppermute | solution.py:380
  8.9 6.5 %collective-permute-done = bf16[192,512]{1,0:T(8,128)(2,1)S(1)} collective-permute-done((bf16[192,512]{1,0:T(8,128)(2,1)}, bf16[192,512]{1,0:T(8,128)(2,1)S(1)}, u32[]{:S(2)}, u32[]{:S(2)}) %collective-permute-start) | collective-permute-done | bytes 196640 | tf_op jit(solution)/shard_map/ppermute | solution.py:380
  25.1 3.8 %shard_map.94 = (bf16[3,384,128]{2,1,0:T(8,128)(2,1)S(1)}, bf16[3,384,128]{2,1,0:T(8,128)(2,1)S(1)}, bf16[3,384,128]{2,1,0:T(8,128)(2,1)S(1)}, bf16[3,384,128]{2,1,0:T(8,128)(2,1)S(1)}) custom-call(bf16[2,2,192,512]{3,2,1,0:T(8,128)(2,1)S(1)} %bitcast.20, bf16[3,1024,512]{2,1,0:T(8,128)(2,1)} %bitcast.w_ref), custom_call_target="tpu_custom_call" | custom-call | flops 1207959552 | bytes 5111808 | tf_op jit(solution)/shard_map/pallas_call | solution.py:416
  30.8 6.2 %collective-permute-start.6 = (bf16[192,128]{1,0:T(8,128)(2,1)S(1)}, bf16[192,128]{1,0:T(8,128)(2,1)S(1)}, u32[]{:S(2)}, u32[]{:S(2)}) collective-permute-start(bf16[192,128]{1,0:T(8,128)(2,1)S(1)} %get-tuple-element.66), channel_id=1, source_target_pairs={{0,16},{8,24},{16,0},{24,8},{1,17},{9,25},{17,1},{25,9},{2,18},{10... | collective-permute-start | bytes 147464 | tf_op jit(solution)/shard_map/ppermute | solution.py:397
  38.5 3.1 %collective-permute-start.11 = (bf16[1152,128]{1,0:T(8,128)(2,1)S(1)}, bf16[1152,128]{1,0:T(8,128)(2,1)S(1)}, u32[]{:S(2)}, u32[]{:S(2)}) collective-permute-start(bf16[1152,128]{1,0:T(8,128)(2,1)S(1)} %bitcast_add_fusion.2), channel_id=1, source_target_pairs={{0,24},{8,0},{16,8},{24,16},{1,25},{9,1},{17,9},{25,17},{2,26},{10... | collective-permute-start | bytes 884744 | tf_op jit(solution)/shard_map/ppermute | solution.py:334
  41.6 4.4 %collective-permute-done.6.refs_11_ = bf16[192,128]{1,0:T(8,128)(2,1)S(1)} collective-permute-done((bf16[192,128]{1,0:T(8,128)(2,1)S(1)}, bf16[192,128]{1,0:T(8,128)(2,1)S(1)}, u32[]{:S(2)}, u32[]{:S(2)}) %collective-permute-start.6) | collective-permute-done | bytes 49184 | tf_op jit(solution)/shard_map/ppermute | solution.py:397
  46.5 3.8 %shard_map.95 = (bf16[3,384,128]{2,1,0:T(8,128)(2,1)S(1)}, bf16[3,384,128]{2,1,0:T(8,128)(2,1)S(1)}, bf16[3,384,128]{2,1,0:T(8,128)(2,1)S(1)}, bf16[3,384,128]{2,1,0:T(8,128)(2,1)S(1)}) custom-call(bf16[2,2,192,512]{3,2,1,0:T(8,128)(2,1)S(1)} %collective-permute-done.7.x_ref.refs_1_, bf16[3,1024,512]{2,1,0:T(8,128)(2,1)} %bitcast.w_ref), custom_call_target="tpu_custom_call" | custom-call | flops 1207959552 | bytes 5111808 | tf_op jit(solution)/shard_map/pallas_call | solution.py:416
  51.2 4.0 %collective-permute-start.12 = (bf16[1152,128]{1,0:T(8,128)(2,1)S(1)}, bf16[1152,128]{1,0:T(8,128)(2,1)S(1)}, u32[]{:S(2)}, u32[]{:S(2)}) collective-permute-start(bf16[1152,128]{1,0:T(8,128)(2,1)S(1)} %bitcast.25), channel_id=1, source_target_pairs={{0,8},{8,16},{1,9},{9,17},{2,10},{10,18},{3,11},{11,19},{4,12},{12... | collective-permute-start | bytes 884744 | tf_op jit(solution)/shard_map/ppermute | solution.py:331
  55.3 3.7 %collective-permute-start.15 = (bf16[1152,128]{1,0:T(8,128)(2,1)S(1)}, bf16[1152,128]{1,0:T(8,128)(2,1)}, u32[]{:S(2)}, u32[]{:S(2)}) collective-permute-start(bf16[1152,128]{1,0:T(8,128)(2,1)S(1)} %bitcast_add_fusion), channel_id=1, source_target_pairs={{0,24},{8,0},{16,8},{24,16},{1,25},{9,1},{17,9},{25,17},{2,26},{10... | collective-permute-start | bytes 884744 | tf_op jit(solution)/shard_map/ppermute | solution.py:334
  59.0 3.7 %collective-permute-done.12 = bf16[1152,128]{1,0:T(8,128)(2,1)S(1)} collective-permute-done((bf16[1152,128]{1,0:T(8,128)(2,1)S(1)}, bf16[1152,128]{1,0:T(8,128)(2,1)S(1)}, u32[]{:S(2)}, u32[]{:S(2)}) %collective-permute-start.12) | collective-permute-done | bytes 294944 | tf_op jit(solution)/shard_map/ppermute | solution.py:331
  68.1 3.0 %collective-permute-done.15.refs_5_ = bf16[1152,128]{1,0:T(8,128)(2,1)} collective-permute-done((bf16[1152,128]{1,0:T(8,128)(2,1)S(1)}, bf16[1152,128]{1,0:T(8,128)(2,1)}, u32[]{:S(2)}, u32[]{:S(2)}) %collective-permute-start.15) | collective-permute-done | bytes 294944 | tf_op jit(solution)/shard_map/ppermute | solution.py:334
  71.1 7.6 %collective-permute-done.13.refs_4_ = bf16[1152,128]{1,0:T(8,128)(2,1)} collective-permute-done((bf16[1152,128]{1,0:T(8,128)(2,1)S(1)}, bf16[1152,128]{1,0:T(8,128)(2,1)}, u32[]{:S(2)}, u32[]{:S(2)}) %collective-permute-start.13) | collective-permute-done | bytes 294944 | tf_op jit(solution)/shard_map/ppermute | solution.py:333
  78.7 5.4 %shard_map.97 = (bf16[1184,128]{1,0:T(8,128)(2,1)}, bf16[1152,128]{1,0:T(8,128)(2,1)}, bf16[192,128]{1,0:T(8,128)(2,1)}, bf16[192,128]{1,0:T(8,128)(2,1)}, bf16[...) custom-call(bf16[1152,128]{1,0:T(8,128)(2,1)} %bitcast.26, bf16[1152,128]{1,0:T(8,128)(2,1)} %copy-done.23, ...), custom_call_target="tpu_custom_call" | custom-call | flops 1207959552 | bytes 2752512 | tf_op jit(solution)/shard_map/pallas_call | solution.py:435
  84.1 3.4 %collective-permute-start.20 = (bf16[1152,128]{1,0:T(8,128)(2,1)}, bf16[1152,128]{1,0:T(8,128)(2,1)S(1)}, u32[]{:S(2)}, u32[]{:S(2)}) collective-permute-start(bf16[1152,128]{1,0:T(8,128)(2,1)} %get-tuple-element.81.refs_6_), channel_id=1, source_target_pairs={{0,26},{2,24},{4,30},{6,28},{8,2},{10,0},{12,6},{14,4},{16,10},{18... | collective-permute-start | bytes 884744 | tf_op jit(solution)/shard_map/ppermute | solution.py:349
  89.2 5.4 %collective-permute-done.20.far_after = bf16[1152,128]{1,0:T(8,128)(2,1)S(1)} collective-permute-done((bf16[1152,128]{1,0:T(8,128)(2,1)}, bf16[1152,128]{1,0:T(8,128)(2,1)S(1)}, u32[]{:S(2)}, u32[]{:S(2)}) %collective-permute-start.20) | collective-permute-done | bytes 294944 | tf_op jit(solution)/shard_map/ppermute | solution.py:349
  96.2 5.0 %collective-permute-done.17.near_after.refs_4_ = bf16[1184,128]{1,0:T(8,128)(2,1)S(1)} collective-permute-done((bf16[1184,128]{1,0:T(8,128)(2,1)}, bf16[1184,128]{1,0:T(8,128)(2,1)S(1)}, u32[]{:S(2)}, u32[]{:S(2)}) %collective-permute-start.17) | collective-permute-done | bytes 303136 | tf_op jit(solution)/shard_map/ppermute | solution.py:349
  102.4 7.5 %collective-permute-done.16.near_before.refs_3_ = bf16[1184,128]{1,0:T(8,128)(2,1)S(1)} collective-permute-done((bf16[1184,128]{1,0:T(8,128)(2,1)}, bf16[1184,128]{1,0:T(8,128)(2,1)S(1)}, u32[]{:S(2)}, u32[]{:S(2)}) %collective-permute-start.16) | collective-permute-done | bytes 303136 | tf_op jit(solution)/shard_map/ppermute | solution.py:348
  115.4 4.7 %collective-permute-start.29 = (bf16[192,128]{1,0:T(8,128)(2,1)}, bf16[192,128]{1,0:T(8,128)(2,1)S(1)}, u32[]{:S(2)}, u32[]{:S(2)}) collective-permute-start(bf16[192,128]{1,0:T(8,128)(2,1)} %get-tuple-element.91), channel_id=1, source_target_pairs={{0,8},{8,16},{16,24},{24,0},{1,9},{9,17},{17,25},{25,1},{2,10},{10... | collective-permute-start | bytes 147464 | tf_op jit(solution)/shard_map/ppermute | solution.py:455
  121.0 4.6 %shard_map.98 = (bf16[2,384,512]{2,1,0:T(8,128)(2,1)S(1)}, bf16[2,1152,128]{2,1,0:T(8,128)(2,1)S(1)}) custom-call(bf16[1184,128]{1,0:T(8,128)(2,1)S(1)} %copy-done.6, bf16[1184,128]{1,0:T(8,128)(2,1)S(1)} %collective-permute-done.16.near_before.refs_3_, bf16[1184,128]{1,0:T(8,128)(2,1)S(1)} %collective-permute-done.17.near_after.refs_4_, ...), custom_call_target="tpu_custom_call" | custom-call | flops 2415919104 | bytes 10223616 | tf_op jit(solution)/shard_map/pallas_call | solution.py:464
  132.5 4.3 %shard_map.99 = (bf16[1184,128]{1,0:T(8,128)(2,1)}, bf16[1152,128]{1,0:T(8,128)(2,1)}, bf16[192,512]{1,0:T(8,128)(2,1)}, bf16[192,512]{1,0:T(8,128)(2,1)}, bf16[...) custom-call(bf16[2,384,512]{2,1,0:T(8,128)(2,1)} %copy-done.3, bf16[1184,128]{1,0:T(8,128)(2,1)} %copy-done.19, ...), custom_call_target="tpu_custom_call" | custom-call | flops 603979776 | bytes 2555904 | tf_op jit(solution)/shard_map/pallas_call | solution.py:477
  141.5 3.1 %collective-permute-done.26 = bf16[192,512]{1,0:T(8,128)(2,1)S(1)} collective-permute-done((bf16[192,512]{1,0:T(8,128)(2,1)}, bf16[192,512]{1,0:T(8,128)(2,1)S(1)}, u32[]{:S(2)}, u32[]{:S(2)}) %collective-permute-start.26) | collective-permute-done | bytes 196640 | tf_op jit(solution)/shard_map/ppermute | solution.py:496
  145.7 4.0 %collective-permute-done.28 = bf16[192,512]{1,0:T(8,128)(2,1)S(1)} collective-permute-done((bf16[192,512]{1,0:T(8,128)(2,1)}, bf16[192,512]{1,0:T(8,128)(2,1)S(1)}, u32[]{:S(2)}, u32[]{:S(2)}) %collective-permute-start.28) | collective-permute-done | bytes 196640 | tf_op jit(solution)/shard_map/ppermute | solution.py:496
  150.7 3.1 %collective-permute-start.34 = (bf16[192,512]{1,0:T(8,128)(2,1)S(1)}, bf16[192,512]{1,0:T(8,128)(2,1)S(1)}, u32[]{:S(2)}, u32[]{:S(2)}) collective-permute-start(bf16[192,512]{1,0:T(8,128)(2,1)S(1)} %add_convert_fusion), channel_id=1, source_target_pairs={{0,0},{2,16},{4,8},{6,24},{8,2},{10,18},{12,10},{14,26},{16,4},{18... | collective-permute-start | bytes 589832 | tf_op jit(solution)/shard_map/ppermute | solution.py:501
  158.4 5.7 %shard_map.100 = (f32[3,1024,512]{2,1,0:T(8,128)}, bf16[192,512]{1,0:T(8,128)(2,1)}, f32[32,128]{1,0:T(8,128)}, f32[3,3,512]{2,1,0:T(4,128)}) custom-call(bf16[2,2,192,512]{3,2,1,0:T(8,128)(2,1)S(1)} %bitcast.21, bf16[2,2,192,512]{3,2,1,0:T(8,128)(2,1)S(1)} %collective-permute-done.7.x_ref.refs_1_, bf16[1184,128]{1,0:T(8,128)(2,1)S(1)} %copy-done.7, ...), custom_call_target="tpu_custom_call" | custom-call | flops 2415919104 | bytes 10223616 | tf_op jit(solution)/shard_map/pallas_call | solution.py:503
  (123 shorter events, 53.2 us)
Async XLA Ops:
  0.6 14.8 %collective-permute-start = (bf16[192,512]{1,0:T(8,128)(2,1)}, bf16[192,512]{1,0:T(8,128)(2,1)S(1)}, u32[]{:S(2)}, u32[]{:S(2)}) collective-permute-start(bf16[192,512]{1,0:T(8,128)(2,1)} %param.5), channel_id=1, source_target_pairs={{0,0},{16,2},{8,4},{24,6},{2,8},{18,10},{10,12},{26,14},{4,16},{20... | collective-permute-start | bytes 589832 | tf_op jit(solution)/shard_map/ppermute | solution.py:380
  24.9 21.6 %collective-permute-start.7 = (bf16[2,2,192,512]{3,2,1,0:T(8,128)(2,1)S(1)}, bf16[2,2,192,512]{3,2,1,0:T(8,128)(2,1)S(1)}, u32[]{:S(2)}, u32[]{:S(2)}) collective-permute-start(bf16[2,2,192,512]{3,2,1,0:T(8,128)(2,1)S(1)} %bitcast.19), channel_id=1, source_target_pairs={{0,2},{2,0},{4,6},{6,4},{1,3},{3,1},{5,7},{7,5},{8,10},{10,8},{12,... | collective-permute-start | bytes 2359304 | tf_op jit(solution)/shard_map/ppermute | solution.py:396
  30.3 85.1 %collective-permute-start.21 = (bf16[3,1024,512]{2,1,0:T(8,128)(2,1)}, bf16[3,1024,512]{2,1,0:T(8,128)(2,1)}, u32[]{:S(2)}, u32[]{:S(2)}) collective-permute-start(bf16[3,1024,512]{2,1,0:T(8,128)(2,1)} %bitcast.w_ref), channel_id=1, source_target_pairs={{0,2},{2,0},{4,6},{6,4},{1,3},{3,1},{5,7},{7,5},{8,10},{10,8},{12,... | collective-permute-start | bytes 9437192 | tf_op jit(solution)/shard_map/ppermute | solution.py:461
  30.8 15.1 %collective-permute-start.6 = (bf16[192,128]{1,0:T(8,128)(2,1)S(1)}, bf16[192,128]{1,0:T(8,128)(2,1)S(1)}, u32[]{:S(2)}, u32[]{:S(2)}) collective-permute-start(bf16[192,128]{1,0:T(8,128)(2,1)S(1)} %get-tuple-element.66), channel_id=1, source_target_pairs={{0,16},{8,24},{16,0},{24,8},{1,17},{9,25},{17,1},{25,9},{2,18},{10... | collective-permute-start | bytes 147464 | tf_op jit(solution)/shard_map/ppermute | solution.py:397
  37.0 14.0 %collective-permute-start.8 = (bf16[1152,128]{1,0:T(8,128)(2,1)S(1)}, bf16[1152,128]{1,0:T(8,128)(2,1)S(1)}, u32[]{:S(2)}, u32[]{:S(2)}) collective-permute-start(bf16[1152,128]{1,0:T(8,128)(2,1)S(1)} %bitcast.23), channel_id=1, source_target_pairs={{0,8},{8,16},{1,9},{9,17},{2,10},{10,18},{3,11},{11,19},{4,12},{12... | collective-permute-start | bytes 884744 | tf_op jit(solution)/shard_map/ppermute | solution.py:331
  38.5 29.6 %collective-permute-start.11 = (bf16[1152,128]{1,0:T(8,128)(2,1)S(1)}, bf16[1152,128]{1,0:T(8,128)(2,1)S(1)}, u32[]{:S(2)}, u32[]{:S(2)}) collective-permute-start(bf16[1152,128]{1,0:T(8,128)(2,1)S(1)} %bitcast_add_fusion.2), channel_id=1, source_target_pairs={{0,24},{8,0},{16,8},{24,16},{1,25},{9,1},{17,9},{25,17},{2,26},{10... | collective-permute-start | bytes 884744 | tf_op jit(solution)/shard_map/ppermute | solution.py:334
  51.2 16.9 %collective-permute-start.9 = (bf16[1152,128]{1,0:T(8,128)(2,1)S(1)}, bf16[1152,128]{1,0:T(8,128)(2,1)S(1)}, u32[]{:S(2)}, u32[]{:S(2)}) collective-permute-start(bf16[1152,128]{1,0:T(8,128)(2,1)S(1)} %bitcast_add_fusion.3), channel_id=1, source_target_pairs={{0,8},{8,16},{16,24},{24,0},{1,9},{9,17},{17,25},{25,1},{2,10},{10... | collective-permute-start | bytes 884744 | tf_op jit(solution)/shard_map/ppermute | solution.py:333
  51.2 11.4 %collective-permute-start.12 = (bf16[1152,128]{1,0:T(8,128)(2,1)S(1)}, bf16[1152,128]{1,0:T(8,128)(2,1)S(1)}, u32[]{:S(2)}, u32[]{:S(2)}) collective-permute-start(bf16[1152,128]{1,0:T(8,128)(2,1)S(1)} %bitcast.25), channel_id=1, source_target_pairs={{0,8},{8,16},{1,9},{9,17},{2,10},{10,18},{3,11},{11,19},{4,12},{12... | collective-permute-start | bytes 884744 | tf_op jit(solution)/shard_map/ppermute | solution.py:331
  55.3 15.8 %collective-permute-start.15 = (bf16[1152,128]{1,0:T(8,128)(2,1)S(1)}, bf16[1152,128]{1,0:T(8,128)(2,1)}, u32[]{:S(2)}, u32[]{:S(2)}) collective-permute-start(bf16[1152,128]{1,0:T(8,128)(2,1)S(1)} %bitcast_add_fusion), channel_id=1, source_target_pairs={{0,24},{8,0},{16,8},{24,16},{1,25},{9,1},{17,9},{25,17},{2,26},{10... | collective-permute-start | bytes 884744 | tf_op jit(solution)/shard_map/ppermute | solution.py:334
  62.7 16.0 %collective-permute-start.13 = (bf16[1152,128]{1,0:T(8,128)(2,1)S(1)}, bf16[1152,128]{1,0:T(8,128)(2,1)}, u32[]{:S(2)}, u32[]{:S(2)}) collective-permute-start(bf16[1152,128]{1,0:T(8,128)(2,1)S(1)} %bitcast_add_fusion.1), channel_id=1, source_target_pairs={{0,8},{8,16},{16,24},{24,0},{1,9},{9,17},{17,25},{25,1},{2,10},{10... | collective-permute-start | bytes 884744 | tf_op jit(solution)/shard_map/ppermute | solution.py:333
  84.1 10.5 %collective-permute-start.20 = (bf16[1152,128]{1,0:T(8,128)(2,1)}, bf16[1152,128]{1,0:T(8,128)(2,1)S(1)}, u32[]{:S(2)}, u32[]{:S(2)}) collective-permute-start(bf16[1152,128]{1,0:T(8,128)(2,1)} %get-tuple-element.81.refs_6_), channel_id=1, source_target_pairs={{0,26},{2,24},{4,30},{6,28},{8,2},{10,0},{12,6},{14,4},{16,10},{18... | collective-permute-start | bytes 884744 | tf_op jit(solution)/shard_map/ppermute | solution.py:349
  87.5 13.6 %collective-permute-start.17 = (bf16[1184,128]{1,0:T(8,128)(2,1)}, bf16[1184,128]{1,0:T(8,128)(2,1)S(1)}, u32[]{:S(2)}, u32[]{:S(2)}) collective-permute-start(bf16[1184,128]{1,0:T(8,128)(2,1)} %get-tuple-element.80.near.refs_2_), channel_id=1, source_target_pairs={{0,24},{2,26},{4,28},{6,30},{8,0},{10,2},{12,4},{14,6},{16,8},{18,... | collective-permute-start | bytes 909320 | tf_op jit(solution)/shard_map/ppermute | solution.py:349
  89.2 20.7 %collective-permute-start.16 = (bf16[1184,128]{1,0:T(8,128)(2,1)}, bf16[1184,128]{1,0:T(8,128)(2,1)S(1)}, u32[]{:S(2)}, u32[]{:S(2)}) collective-permute-start(bf16[1184,128]{1,0:T(8,128)(2,1)} %get-tuple-element.80.near.refs_2_), channel_id=1, source_target_pairs={{0,8},{2,10},{4,12},{6,14},{8,16},{10,18},{12,20},{14,22},{16,24},... | collective-permute-start | bytes 909320 | tf_op jit(solution)/shard_map/ppermute | solution.py:348
  89.2 24.2 %collective-permute-start.19 = (bf16[1152,128]{1,0:T(8,128)(2,1)}, bf16[1152,128]{1,0:T(8,128)(2,1)S(1)}, u32[]{:S(2)}, u32[]{:S(2)}) collective-permute-start(bf16[1152,128]{1,0:T(8,128)(2,1)} %get-tuple-element.81.refs_6_), channel_id=1, source_target_pairs={{0,10},{2,8},{4,14},{6,12},{8,18},{10,16},{12,22},{14,20},{16,26},... | collective-permute-start | bytes 884744 | tf_op jit(solution)/shard_map/ppermute | solution.py:348
  94.6 20.1 %collective-permute-start.18 = (bf16[1152,128]{1,0:T(8,128)(2,1)}, bf16[1152,128]{1,0:T(8,128)(2,1)S(1)}, u32[]{:S(2)}, u32[]{:S(2)}) collective-permute-start(bf16[1152,128]{1,0:T(8,128)(2,1)} %get-tuple-element.81.refs_6_), channel_id=1, source_target_pairs={{0,2},{2,0},{4,6},{6,4},{8,10},{10,8},{12,14},{14,12},{16,18},{18,... | collective-permute-start | bytes 884744 | tf_op jit(solution)/shard_map/ppermute | solution.py:350
  101.1 29.9 %collective-permute-start.23 = (bf16[1184,128]{1,0:T(8,128)(2,1)S(1)}, bf16[1184,128]{1,0:T(8,128)(2,1)S(1)}, u32[]{:S(2)}, u32[]{:S(2)}) collective-permute-start(bf16[1184,128]{1,0:T(8,128)(2,1)S(1)} %collective-permute-done.17.near_after.refs_4_), channel_id=1, source_target_pairs={{8,0},{16,8},{9,1},{17,9},{10,2},{18,10},{11,3},{19,11},{12,4},{20... | collective-permute-start | bytes 909320 | tf_op jit(solution)/shard_map/ppermute | solution.py:352
  109.9 21.1 %collective-permute-start.22 = (bf16[1184,128]{1,0:T(8,128)(2,1)S(1)}, bf16[1184,128]{1,0:T(8,128)(2,1)S(1)}, u32[]{:S(2)}, u32[]{:S(2)}) collective-permute-start(bf16[1184,128]{1,0:T(8,128)(2,1)S(1)} %collective-permute-done.16.near_before.refs_3_), channel_id=1, source_target_pairs={{8,16},{16,24},{9,17},{17,25},{10,18},{18,26},{11,19},{19,27},{12,... | collective-permute-start | bytes 909320 | tf_op jit(solution)/shard_map/ppermute | solution.py:351
  113.4 15.3 %collective-permute-start.25 = (bf16[1152,128]{1,0:T(8,128)(2,1)S(1)}, bf16[1152,128]{1,0:T(8,128)(2,1)S(1)}, u32[]{:S(2)}, u32[]{:S(2)}) collective-permute-start(bf16[1152,128]{1,0:T(8,128)(2,1)S(1)} %collective-permute-done.20.far_after), channel_id=1, source_target_pairs={{8,0},{16,8},{9,1},{17,9},{10,2},{18,10},{11,3},{19,11},{12,4},{20... | collective-permute-start | bytes 884744 | tf_op jit(solution)/shard_map/ppermute | solution.py:352
  114.7 14.0 %collective-permute-start.24 = (bf16[1152,128]{1,0:T(8,128)(2,1)S(1)}, bf16[1152,128]{1,0:T(8,128)(2,1)S(1)}, u32[]{:S(2)}, u32[]{:S(2)}) collective-permute-start(bf16[1152,128]{1,0:T(8,128)(2,1)S(1)} %collective-permute-done.19.far_before), channel_id=1, source_target_pairs={{8,16},{16,24},{9,17},{17,25},{10,18},{18,26},{11,19},{19,27},{12,... | collective-permute-start | bytes 884744 | tf_op jit(solution)/shard_map/ppermute | solution.py:351
  115.4 21.4 %collective-permute-start.29 = (bf16[192,128]{1,0:T(8,128)(2,1)}, bf16[192,128]{1,0:T(8,128)(2,1)S(1)}, u32[]{:S(2)}, u32[]{:S(2)}) collective-permute-start(bf16[192,128]{1,0:T(8,128)(2,1)} %get-tuple-element.91), channel_id=1, source_target_pairs={{0,8},{8,16},{16,24},{24,0},{1,9},{9,17},{17,25},{25,1},{2,10},{10... | collective-permute-start | bytes 147464 | tf_op jit(solution)/shard_map/ppermute | solution.py:455
  136.8 13.8 %collective-permute-start.32 = (bf16[2,1152,128]{2,1,0:T(8,128)(2,1)}, bf16[2,1152,128]{2,1,0:T(8,128)(2,1)S(1)}, u32[]{:S(2)}, u32[]{:S(2)}) collective-permute-start(bf16[2,1152,128]{2,1,0:T(8,128)(2,1)} %copy-done.5), channel_id=1, source_target_pairs={{0,2},{2,0},{4,6},{6,4},{1,3},{3,1},{5,7},{7,5},{8,10},{10,8},{12,... | collective-permute-start | bytes 1769480 | tf_op jit(solution)/shard_map/ppermute | solution.py:494
  139.2 10.5 %collective-permute-start.28 = (bf16[192,512]{1,0:T(8,128)(2,1)}, bf16[192,512]{1,0:T(8,128)(2,1)S(1)}, u32[]{:S(2)}, u32[]{:S(2)}) collective-permute-start(bf16[192,512]{1,0:T(8,128)(2,1)} %get-tuple-element.88), channel_id=1, source_target_pairs={{5,0},{4,1},{7,2},{6,3},{1,4},{0,5},{3,6},{2,7},{13,8},{12,9},{15,... | collective-permute-start | bytes 589832 | tf_op jit(solution)/shard_map/ppermute | solution.py:496
  140.6 10.0 %collective-permute-start.33 = (bf16[1152,128]{1,0:T(8,128)(2,1)}, bf16[1152,128]{1,0:T(8,128)(2,1)S(1)}, u32[]{:S(2)}, u32[]{:S(2)}) collective-permute-start(bf16[1152,128]{1,0:T(8,128)(2,1)} %get-tuple-element.95), channel_id=1, source_target_pairs={{0,2},{2,0},{4,6},{6,4},{1,3},{3,1},{5,7},{7,5},{8,10},{10,8},{12,... | collective-permute-start | bytes 884744 | tf_op jit(solution)/shard_map/ppermute | solution.py:494
  150.7 13.4 %collective-permute-start.34 = (bf16[192,512]{1,0:T(8,128)(2,1)S(1)}, bf16[192,512]{1,0:T(8,128)(2,1)S(1)}, u32[]{:S(2)}, u32[]{:S(2)}) collective-permute-start(bf16[192,512]{1,0:T(8,128)(2,1)S(1)} %add_convert_fusion), channel_id=1, source_target_pairs={{0,0},{2,16},{4,8},{6,24},{8,2},{10,18},{12,10},{14,26},{16,4},{18... | collective-permute-start | bytes 589832 | tf_op jit(solution)/shard_map/ppermute | solution.py:501
  (38 other events, 284.8 us)

commit v21 on v16

--- a/solution.py
+++ b/solution.py
@@ -326,13 +326,14 @@
     near_ref[3 * tokens // 2 :] = small.astype(BF16)
 
 
-def sum_over_line(own, right, far, left):
+def sum_over_line(own, right, far, left, later):
     ndp = lax.axis_size("dp")
     from_left = lax.ppermute(far, "dp", [(a, a + 1) for a in range(ndp // 2)])
     from_right = lax.ppermute(far, "dp", [(a, a - 1) for a in range(ndp // 2, ndp)])
+    from_right, later = lax.optimization_barrier((from_right, later))
     rightward = lax.ppermute(right + from_left, "dp", [(a, (a + 1) % ndp) for a in range(ndp)])
     leftward = lax.ppermute(left + from_right, "dp", [(a, (a - 1) % ndp) for a in range(ndp)])
-    return own, rightward, leftward
+    return [own, rightward, leftward], later
 
 
 def gather_over_line(own, across):
@@ -411,7 +412,7 @@
 
     mm_flops = seq * drow * 3 * local
     mm_bytes = seq * drow + 6 * drow * local + 3 * seq * local
-    sums = []
+    sums, first_w = [], None
     for x in (x0, x1):
         parts = kernel_call(
             project_body,
@@ -426,7 +427,8 @@
             flops=mm_flops,
             nbytes=mm_bytes,
         )(x, w)
-        sums += sum_over_line(*(p.reshape(3 * chunk, width) for p in parts))
+        three, later_w = sum_over_line(*(p.reshape(3 * chunk, width) for p in parts), w)
+        sums, first_w = sums + three, later_w if x is x0 else first_w
 
     extra = -(-(groups + 3 * nshort) // 16) * 16
     half = pl.BlockSpec((groups, ntaps, 2 * ntaps), lambda i: (0, 0, 0))
@@ -458,7 +460,7 @@
     ]
     *near, near_far_before, near_far_after = gather_over_line(grad_near, False)
     *far, far_far_before, far_far_after = gather_over_line(grad_other, True)
-    partner_w = lax.ppermute(w, "row", partner)
+    partner_w = lax.ppermute(first_w, "row", partner)
     everywhere = pl.BlockSpec(memory_space=pl.ANY)
     in_vmem = pl.BlockSpec(memory_space=pltpu.VMEM)
     part, far_two = kernel_call(

time: 163 us -> 166 us (1.018)
    ppermute x2, starting transfers between devices: 5.97 us -> 8.84 us  [sum_over_line(): lax.ppermute(left + from_right, 'dp', [(a, (a - 1) % ndp) for a in range(...]
    ppermute x2, waiting for transfers between devices: 8.37 us -> 6.36 us  [sum_over_line(): lax.ppermute(right + from_left, 'dp', [(a, (a + 1) % ndp) for a in range(...]
    ppermute x2, waiting for transfers between devices: 2.16 us -> 4.12 us  [sum_over_line(): lax.ppermute(left + from_right, 'dp', [(a, (a - 1) % ndp) for a in range(...]
    ppermute x2, waiting for transfers between devices: 10.2 us -> 12 us  [gather_over_line(): after = lax.ppermute(own, ('dp', 'row'), shift(-1))]
where the time goes in v21:
time: 166 us; the launch traced here: 165 us
  waiting for transfers between devices  61.4 us (37%)
  starting transfers between devices  59.9 us (36%)
  Pallas kernels  31.3 us (19%)
  local copies, waits for them, and re-layouts  8.81 us (5%)
  other arithmetic  2.19 us (1%)
    ppermute x2, waiting for transfers between devices, gather_over_line(): after = lax.ppermute(own, ('dp', 'row'), shift(-1))  12 us
    ppermute x2, waiting for transfers between devices, gather_over_line(): before = lax.ppermute(own, ('dp', 'row'), shift(1))  10.6 us
    ppermute x2, starting transfers between devices, sum_over_line(): lax.ppermute(left + from_right, 'dp', [(a, (a - 1) % ndp) for a in range(...  8.84 us
    ppermute x3, waiting for transfers between devices, move_activations(): lax.ppermute(sent, ('row', 'col'), [(b, a) for a, b in offset(*p)])  8.25 us
    unnamed x61, local copies, waits for them, and re-layouts  8.13 us
    pallas_call x2, Pallas kernels, move_activations(): kernel_call(project_body, [shaped((3, chunk, width), BF16)] * ndp, grid=(...  8.1 us
    pallas_call x1, Pallas kernels, move_activations(): kernel_call(functools.partial(weight_grad_body, scale), [shaped((3, drow,...  7.04 us
    ppermute x1, waiting for transfers between devices, move_activations(): moved = lax.ppermute(tokens, ('dp', 'row'), swap)  6.54 us
  transfers between devices with their start and end apart: 35, of which 17 were waited for; matrix products, arithmetic and copies ran while one was open for 2% of the time, Pallas kernels for 19%

profile of v21, /device:TPU:1, one launch (start us, length us, event | category | flops | bytes accessed | tf_op | source)
XLA Modules:
  0.0 164.8 jit_solution(11514983420110243270)
XLA Ops:
  0.6 4.6 %collective-permute-start = (bf16[192,512]{1,0:T(8,128)(2,1)}, bf16[192,512]{1,0:T(8,128)(2,1)S(1)}, u32[]{:S(2)}, u32[]{:S(2)}) collective-permute-start(bf16[192,512]{1,0:T(8,128)(2,1)} %param.5), channel_id=1, source_target_pairs={{0,0},{16,2},{8,4},{24,6},{2,8},{18,10},{10,12},{26,14},{4,16},{20... | collective-permute-start | bytes 589832 | tf_op jit(solution)/shard_map/ppermute | solution.py:381
  8.9 6.5 %collective-permute-done = bf16[192,512]{1,0:T(8,128)(2,1)S(1)} collective-permute-done((bf16[192,512]{1,0:T(8,128)(2,1)}, bf16[192,512]{1,0:T(8,128)(2,1)S(1)}, u32[]{:S(2)}, u32[]{:S(2)}) %collective-permute-start) | collective-permute-done | bytes 196640 | tf_op jit(solution)/shard_map/ppermute | solution.py:381
  25.1 4.0 %shard_map.94 = (bf16[3,384,128]{2,1,0:T(8,128)(2,1)S(1)}, bf16[3,384,128]{2,1,0:T(8,128)(2,1)S(1)}, bf16[3,384,128]{2,1,0:T(8,128)(2,1)S(1)}, bf16[3,384,128]{2,1,0:T(8,128)(2,1)S(1)}) custom-call(bf16[2,2,192,512]{3,2,1,0:T(8,128)(2,1)S(1)} %bitcast.20, bf16[3,1024,512]{2,1,0:T(8,128)(2,1)} %bitcast.w_ref), custom_call_target="tpu_custom_call" | custom-call | flops 1207959552 | bytes 5111808 | tf_op jit(solution)/shard_map/pallas_call | solution.py:417
  29.8 6.3 %collective-permute-start.6 = (bf16[192,128]{1,0:T(8,128)(2,1)S(1)}, bf16[192,128]{1,0:T(8,128)(2,1)S(1)}, u32[]{:S(2)}, u32[]{:S(2)}) collective-permute-start(bf16[192,128]{1,0:T(8,128)(2,1)S(1)} %get-tuple-element.69), channel_id=1, source_target_pairs={{0,16},{8,24},{16,0},{24,8},{1,17},{9,25},{17,1},{25,9},{2,18},{10... | collective-permute-start | bytes 147464 | tf_op jit(solution)/shard_map/ppermute | solution.py:398
  38.3 3.9 %collective-permute-start.11 = (bf16[1152,128]{1,0:T(8,128)(2,1)S(1)}, bf16[1152,128]{1,0:T(8,128)(2,1)}, u32[]{:S(2)}, u32[]{:S(2)}) collective-permute-start(bf16[1152,128]{1,0:T(8,128)(2,1)S(1)} %bitcast_add_fusion.2), channel_id=1, source_target_pairs={{0,24},{8,0},{16,8},{24,16},{1,25},{9,1},{17,9},{25,17},{2,26},{10... | collective-permute-start | bytes 884744 | tf_op jit(solution)/shard_map/ppermute | solution.py:335
  45.3 4.1 %shard_map.95 = (bf16[3,384,128]{2,1,0:T(8,128)(2,1)S(1)}, bf16[3,384,128]{2,1,0:T(8,128)(2,1)S(1)}, bf16[3,384,128]{2,1,0:T(8,128)(2,1)S(1)}, bf16[3,384,128]{2,1,0:T(8,128)(2,1)S(1)}) custom-call(bf16[2,2,192,512]{3,2,1,0:T(8,128)(2,1)S(1)} %collective-permute-done.7.x_ref.refs_1_, bf16[3,1024,512]{2,1,0:T(8,128)(2,1)} %bitcast.w_ref), custom_call_target="tpu_custom_call" | custom-call | flops 1207959552 | bytes 5111808 | tf_op jit(solution)/shard_map/pallas_call | solution.py:417
  52.2 4.0 %collective-permute-start.12 = (bf16[1152,128]{1,0:T(8,128)(2,1)S(1)}, bf16[1152,128]{1,0:T(8,128)(2,1)S(1)}, u32[]{:S(2)}, u32[]{:S(2)}) collective-permute-start(bf16[1152,128]{1,0:T(8,128)(2,1)S(1)} %bitcast.25), channel_id=1, source_target_pairs={{0,8},{8,16},{1,9},{9,17},{2,10},{10,18},{3,11},{11,19},{4,12},{12... | collective-permute-start | bytes 884744 | tf_op jit(solution)/shard_map/ppermute | solution.py:331
  56.3 5.0 %collective-permute-start.15 = (bf16[1152,128]{1,0:T(8,128)(2,1)S(1)}, bf16[1152,128]{1,0:T(8,128)(2,1)S(1)}, u32[]{:S(2)}, u32[]{:S(2)}) collective-permute-start(bf16[1152,128]{1,0:T(8,128)(2,1)S(1)} %bitcast_add_fusion), channel_id=1, source_target_pairs={{0,24},{8,0},{16,8},{24,16},{1,25},{9,1},{17,9},{25,17},{2,26},{10... | collective-permute-start | bytes 884744 | tf_op jit(solution)/shard_map/ppermute | solution.py:335
  61.2 3.7 %collective-permute-done.12 = bf16[1152,128]{1,0:T(8,128)(2,1)S(1)} collective-permute-done((bf16[1152,128]{1,0:T(8,128)(2,1)S(1)}, bf16[1152,128]{1,0:T(8,128)(2,1)S(1)}, u32[]{:S(2)}, u32[]{:S(2)}) %collective-permute-start.12) | collective-permute-done | bytes 294944 | tf_op jit(solution)/shard_map/ppermute | solution.py:331
  70.4 4.1 %collective-permute-done.15.refs_5_ = bf16[1152,128]{1,0:T(8,128)(2,1)S(1)} collective-permute-done((bf16[1152,128]{1,0:T(8,128)(2,1)S(1)}, bf16[1152,128]{1,0:T(8,128)(2,1)S(1)}, u32[]{:S(2)}, u32[]{:S(2)}) %collective-permute-start.15) | collective-permute-done | bytes 294944 | tf_op jit(solution)/shard_map/ppermute | solution.py:335
  74.5 6.4 %collective-permute-done.13.refs_4_ = bf16[1152,128]{1,0:T(8,128)(2,1)S(1)} collective-permute-done((bf16[1152,128]{1,0:T(8,128)(2,1)S(1)}, bf16[1152,128]{1,0:T(8,128)(2,1)S(1)}, u32[]{:S(2)}, u32[]{:S(2)}) %collective-permute-start.13) | collective-permute-done | bytes 294944 | tf_op jit(solution)/shard_map/ppermute | solution.py:334
  81.6 5.4 %shard_map.97 = (bf16[1184,128]{1,0:T(8,128)(2,1)}, bf16[1152,128]{1,0:T(8,128)(2,1)}, bf16[192,128]{1,0:T(8,128)(2,1)}, bf16[192,128]{1,0:T(8,128)(2,1)}, bf16[...) custom-call(bf16[1152,128]{1,0:T(8,128)(2,1)} %bitcast.26, bf16[1152,128]{1,0:T(8,128)(2,1)} %copy-done.18, ...), custom_call_target="tpu_custom_call" | custom-call | flops 1207959552 | bytes 2752512 | tf_op jit(solution)/shard_map/pallas_call | solution.py:437
  87.0 3.1 %collective-permute-start.20 = (bf16[1152,128]{1,0:T(8,128)(2,1)}, bf16[1152,128]{1,0:T(8,128)(2,1)S(1)}, u32[]{:S(2)}, u32[]{:S(2)}) collective-permute-start(bf16[1152,128]{1,0:T(8,128)(2,1)} %get-tuple-element.86.refs_6_), channel_id=1, source_target_pairs={{0,26},{2,24},{4,30},{6,28},{8,2},{10,0},{12,6},{14,4},{16,10},{18... | collective-permute-start | bytes 884744 | tf_op jit(solution)/shard_map/ppermute | solution.py:350
  91.6 5.8 %collective-permute-done.20.far_after = bf16[1152,128]{1,0:T(8,128)(2,1)S(1)} collective-permute-done((bf16[1152,128]{1,0:T(8,128)(2,1)}, bf16[1152,128]{1,0:T(8,128)(2,1)S(1)}, u32[]{:S(2)}, u32[]{:S(2)}) %collective-permute-start.20) | collective-permute-done | bytes 294944 | tf_op jit(solution)/shard_map/ppermute | solution.py:350
  97.6 6.2 %collective-permute-done.17.near_after.refs_4_ = bf16[1184,128]{1,0:T(8,128)(2,1)S(1)} collective-permute-done((bf16[1184,128]{1,0:T(8,128)(2,1)}, bf16[1184,128]{1,0:T(8,128)(2,1)S(1)}, u32[]{:S(2)}, u32[]{:S(2)}) %collective-permute-start.17) | collective-permute-done | bytes 303136 | tf_op jit(solution)/shard_map/ppermute | solution.py:350
  105.1 7.1 %collective-permute-done.16.near_before.refs_3_ = bf16[1184,128]{1,0:T(8,128)(2,1)S(1)} collective-permute-done((bf16[1184,128]{1,0:T(8,128)(2,1)}, bf16[1184,128]{1,0:T(8,128)(2,1)S(1)}, u32[]{:S(2)}, u32[]{:S(2)}) %collective-permute-start.16) | collective-permute-done | bytes 303136 | tf_op jit(solution)/shard_map/ppermute | solution.py:349
  112.9 3.5 %collective-permute-done.19.far_before = bf16[1152,128]{1,0:T(8,128)(2,1)S(1)} collective-permute-done((bf16[1152,128]{1,0:T(8,128)(2,1)}, bf16[1152,128]{1,0:T(8,128)(2,1)S(1)}, u32[]{:S(2)}, u32[]{:S(2)}) %collective-permute-start.19) | collective-permute-done | bytes 294944 | tf_op jit(solution)/shard_map/ppermute | solution.py:349
  118.4 3.5 %collective-permute-start.29 = (bf16[192,128]{1,0:T(8,128)(2,1)}, bf16[192,128]{1,0:T(8,128)(2,1)S(1)}, u32[]{:S(2)}, u32[]{:S(2)}) collective-permute-start(bf16[192,128]{1,0:T(8,128)(2,1)} %get-tuple-element.97), channel_id=1, source_target_pairs={{0,8},{8,16},{16,24},{24,0},{1,9},{9,17},{17,25},{25,1},{2,10},{10... | collective-permute-start | bytes 147464 | tf_op jit(solution)/shard_map/ppermute | solution.py:457
  122.8 4.6 %shard_map.98 = (bf16[2,384,512]{2,1,0:T(8,128)(2,1)S(1)}, bf16[2,1152,128]{2,1,0:T(8,128)(2,1)S(1)}) custom-call(bf16[1184,128]{1,0:T(8,128)(2,1)S(1)} %copy-done.7, bf16[1184,128]{1,0:T(8,128)(2,1)S(1)} %collective-permute-done.16.near_before.refs_3_, bf16[1184,128]{1,0:T(8,128)(2,1)S(1)} %collective-permute-done.17.near_after.refs_4_, ...), custom_call_target="tpu_custom_call" | custom-call | flops 2415919104 | bytes 10223616 | tf_op jit(solution)/shard_map/pallas_call | solution.py:466
  134.5 4.3 %shard_map.99 = (bf16[1184,128]{1,0:T(8,128)(2,1)}, bf16[1152,128]{1,0:T(8,128)(2,1)}, bf16[192,512]{1,0:T(8,128)(2,1)}, bf16[192,512]{1,0:T(8,128)(2,1)}, bf16[...) custom-call(bf16[2,384,512]{2,1,0:T(8,128)(2,1)} %copy-done.4, bf16[1184,128]{1,0:T(8,128)(2,1)} %copy-done.14, ...), custom_call_target="tpu_custom_call" | custom-call | flops 603979776 | bytes 2555904 | tf_op jit(solution)/shard_map/pallas_call | solution.py:479
  143.6 3.1 %collective-permute-done.26 = bf16[192,512]{1,0:T(8,128)(2,1)S(1)} collective-permute-done((bf16[192,512]{1,0:T(8,128)(2,1)}, bf16[192,512]{1,0:T(8,128)(2,1)S(1)}, u32[]{:S(2)}, u32[]{:S(2)}) %collective-permute-start.26) | collective-permute-done | bytes 196640 | tf_op jit(solution)/shard_map/ppermute | solution.py:498
  147.6 4.2 %collective-permute-done.28 = bf16[192,512]{1,0:T(8,128)(2,1)S(1)} collective-permute-done((bf16[192,512]{1,0:T(8,128)(2,1)}, bf16[192,512]{1,0:T(8,128)(2,1)S(1)}, u32[]{:S(2)}, u32[]{:S(2)}) %collective-permute-start.28) | collective-permute-done | bytes 196640 | tf_op jit(solution)/shard_map/ppermute | solution.py:498
  152.9 3.2 %collective-permute-start.34 = (bf16[192,512]{1,0:T(8,128)(2,1)S(1)}, bf16[192,512]{1,0:T(8,128)(2,1)S(1)}, u32[]{:S(2)}, u32[]{:S(2)}) collective-permute-start(bf16[192,512]{1,0:T(8,128)(2,1)S(1)} %add_convert_fusion), channel_id=1, source_target_pairs={{0,0},{2,16},{4,8},{6,24},{8,2},{10,18},{12,10},{14,26},{16,4},{18... | collective-permute-start | bytes 589832 | tf_op jit(solution)/shard_map/ppermute | solution.py:503
  156.2 7.0 %shard_map.100 = (f32[3,1024,512]{2,1,0:T(8,128)}, bf16[192,512]{1,0:T(8,128)(2,1)}, f32[32,128]{1,0:T(8,128)}, f32[3,3,512]{2,1,0:T(4,128)}) custom-call(bf16[2,2,192,512]{3,2,1,0:T(8,128)(2,1)} %bitcast.21, bf16[2,2,192,512]{3,2,1,0:T(8,128)(2,1)} %copy-done.6, bf16[1184,128]{1,0:T(8,128)(2,1)} %get-tuple-element.85.near.refs_2_, ...), custom_call_target="tpu_custom_call" | custom-call | flops 2415919104 | bytes 10223616 | tf_op jit(solution)/shard_map/pallas_call | solution.py:505
  (129 shorter events, 50.0 us)
Async XLA Ops:
  0.6 14.8 %collective-permute-start = (bf16[192,512]{1,0:T(8,128)(2,1)}, bf16[192,512]{1,0:T(8,128)(2,1)S(1)}, u32[]{:S(2)}, u32[]{:S(2)}) collective-permute-start(bf16[192,512]{1,0:T(8,128)(2,1)} %param.5), channel_id=1, source_target_pairs={{0,0},{16,2},{8,4},{24,6},{2,8},{18,10},{10,12},{26,14},{4,16},{20... | collective-permute-start | bytes 589832 | tf_op jit(solution)/shard_map/ppermute | solution.py:381
  25.0 20.4 %collective-permute-start.7 = (bf16[2,2,192,512]{3,2,1,0:T(8,128)(2,1)S(1)}, bf16[2,2,192,512]{3,2,1,0:T(8,128)(2,1)S(1)}, u32[]{:S(2)}, u32[]{:S(2)}) collective-permute-start(bf16[2,2,192,512]{3,2,1,0:T(8,128)(2,1)S(1)} %bitcast.19), channel_id=1, source_target_pairs={{0,2},{2,0},{4,6},{6,4},{1,3},{3,1},{5,7},{7,5},{8,10},{10,8},{12,... | collective-permute-start | bytes 2359304 | tf_op jit(solution)/shard_map/ppermute | solution.py:397
  29.8 14.9 %collective-permute-start.6 = (bf16[192,128]{1,0:T(8,128)(2,1)S(1)}, bf16[192,128]{1,0:T(8,128)(2,1)S(1)}, u32[]{:S(2)}, u32[]{:S(2)}) collective-permute-start(bf16[192,128]{1,0:T(8,128)(2,1)S(1)} %get-tuple-element.69), channel_id=1, source_target_pairs={{0,16},{8,24},{16,0},{24,8},{1,17},{9,25},{17,1},{25,9},{2,18},{10... | collective-permute-start | bytes 147464 | tf_op jit(solution)/shard_map/ppermute | solution.py:398
  36.1 14.1 %collective-permute-start.8 = (bf16[1152,128]{1,0:T(8,128)(2,1)S(1)}, bf16[1152,128]{1,0:T(8,128)(2,1)S(1)}, u32[]{:S(2)}, u32[]{:S(2)}) collective-permute-start(bf16[1152,128]{1,0:T(8,128)(2,1)S(1)} %bitcast.23), channel_id=1, source_target_pairs={{0,8},{8,16},{1,9},{9,17},{2,10},{10,18},{3,11},{11,19},{4,12},{12... | collective-permute-start | bytes 884744 | tf_op jit(solution)/shard_map/ppermute | solution.py:331
  37.4 81.0 %collective-permute-start.21 = (bf16[3,1024,512]{2,1,0:T(8,128)(2,1)}, bf16[3,1024,512]{2,1,0:T(8,128)(2,1)}, u32[]{:S(2)}, u32[]{:S(2)}) collective-permute-start(bf16[3,1024,512]{2,1,0:T(8,128)(2,1)} %bitcast.w_ref), channel_id=1, source_target_pairs={{0,2},{2,0},{4,6},{6,4},{1,3},{3,1},{5,7},{7,5},{8,10},{10,8},{12,... | collective-permute-start | bytes 9437192 | tf_op jit(solution)/shard_map/ppermute | solution.py:463
  38.3 32.0 %collective-permute-start.11 = (bf16[1152,128]{1,0:T(8,128)(2,1)S(1)}, bf16[1152,128]{1,0:T(8,128)(2,1)}, u32[]{:S(2)}, u32[]{:S(2)}) collective-permute-start(bf16[1152,128]{1,0:T(8,128)(2,1)S(1)} %bitcast_add_fusion.2), channel_id=1, source_target_pairs={{0,24},{8,0},{16,8},{24,16},{1,25},{9,1},{17,9},{25,17},{2,26},{10... | collective-permute-start | bytes 884744 | tf_op jit(solution)/shard_map/ppermute | solution.py:335
  50.2 20.1 %collective-permute-start.9 = (bf16[1152,128]{1,0:T(8,128)(2,1)S(1)}, bf16[1152,128]{1,0:T(8,128)(2,1)S(1)}, u32[]{:S(2)}, u32[]{:S(2)}) collective-permute-start(bf16[1152,128]{1,0:T(8,128)(2,1)S(1)} %bitcast_add_fusion.3), channel_id=1, source_target_pairs={{0,8},{8,16},{16,24},{24,0},{1,9},{9,17},{17,25},{25,1},{2,10},{10... | collective-permute-start | bytes 884744 | tf_op jit(solution)/shard_map/ppermute | solution.py:334
  52.2 12.8 %collective-permute-start.12 = (bf16[1152,128]{1,0:T(8,128)(2,1)S(1)}, bf16[1152,128]{1,0:T(8,128)(2,1)S(1)}, u32[]{:S(2)}, u32[]{:S(2)}) collective-permute-start(bf16[1152,128]{1,0:T(8,128)(2,1)S(1)} %bitcast.25), channel_id=1, source_target_pairs={{0,8},{8,16},{1,9},{9,17},{2,10},{10,18},{3,11},{11,19},{4,12},{12... | collective-permute-start | bytes 884744 | tf_op jit(solution)/shard_map/ppermute | solution.py:331
  56.3 18.2 %collective-permute-start.15 = (bf16[1152,128]{1,0:T(8,128)(2,1)S(1)}, bf16[1152,128]{1,0:T(8,128)(2,1)S(1)}, u32[]{:S(2)}, u32[]{:S(2)}) collective-permute-start(bf16[1152,128]{1,0:T(8,128)(2,1)S(1)} %bitcast_add_fusion), channel_id=1, source_target_pairs={{0,24},{8,0},{16,8},{24,16},{1,25},{9,1},{17,9},{25,17},{2,26},{10... | collective-permute-start | bytes 884744 | tf_op jit(solution)/shard_map/ppermute | solution.py:335
  65.0 15.8 %collective-permute-start.13 = (bf16[1152,128]{1,0:T(8,128)(2,1)S(1)}, bf16[1152,128]{1,0:T(8,128)(2,1)S(1)}, u32[]{:S(2)}, u32[]{:S(2)}) collective-permute-start(bf16[1152,128]{1,0:T(8,128)(2,1)S(1)} %bitcast_add_fusion.1), channel_id=1, source_target_pairs={{0,8},{8,16},{16,24},{24,0},{1,9},{9,17},{17,25},{25,1},{2,10},{10... | collective-permute-start | bytes 884744 | tf_op jit(solution)/shard_map/ppermute | solution.py:334
  87.0 10.3 %collective-permute-start.20 = (bf16[1152,128]{1,0:T(8,128)(2,1)}, bf16[1152,128]{1,0:T(8,128)(2,1)S(1)}, u32[]{:S(2)}, u32[]{:S(2)}) collective-permute-start(bf16[1152,128]{1,0:T(8,128)(2,1)} %get-tuple-element.86.refs_6_), channel_id=1, source_target_pairs={{0,26},{2,24},{4,30},{6,28},{8,2},{10,0},{12,6},{14,4},{16,10},{18... | collective-permute-start | bytes 884744 | tf_op jit(solution)/shard_map/ppermute | solution.py:350
  90.1 13.7 %collective-permute-start.17 = (bf16[1184,128]{1,0:T(8,128)(2,1)}, bf16[1184,128]{1,0:T(8,128)(2,1)S(1)}, u32[]{:S(2)}, u32[]{:S(2)}) collective-permute-start(bf16[1184,128]{1,0:T(8,128)(2,1)} %get-tuple-element.85.near.refs_2_), channel_id=1, source_target_pairs={{0,24},{2,26},{4,28},{6,30},{8,0},{10,2},{12,4},{14,6},{16,8},{18,... | collective-permute-start | bytes 909320 | tf_op jit(solution)/shard_map/ppermute | solution.py:350
  91.6 20.6 %collective-permute-start.16 = (bf16[1184,128]{1,0:T(8,128)(2,1)}, bf16[1184,128]{1,0:T(8,128)(2,1)S(1)}, u32[]{:S(2)}, u32[]{:S(2)}) collective-permute-start(bf16[1184,128]{1,0:T(8,128)(2,1)} %get-tuple-element.85.near.refs_2_), channel_id=1, source_target_pairs={{0,8},{2,10},{4,12},{6,14},{8,16},{10,18},{12,20},{14,22},{16,24},... | collective-permute-start | bytes 909320 | tf_op jit(solution)/shard_map/ppermute | solution.py:349
  91.6 24.8 %collective-permute-start.19 = (bf16[1152,128]{1,0:T(8,128)(2,1)}, bf16[1152,128]{1,0:T(8,128)(2,1)S(1)}, u32[]{:S(2)}, u32[]{:S(2)}) collective-permute-start(bf16[1152,128]{1,0:T(8,128)(2,1)} %get-tuple-element.86.refs_6_), channel_id=1, source_target_pairs={{0,10},{2,8},{4,14},{6,12},{8,18},{10,16},{12,22},{14,20},{16,26},... | collective-permute-start | bytes 884744 | tf_op jit(solution)/shard_map/ppermute | solution.py:349
  97.3 20.3 %collective-permute-start.18 = (bf16[1152,128]{1,0:T(8,128)(2,1)}, bf16[1152,128]{1,0:T(8,128)(2,1)S(1)}, u32[]{:S(2)}, u32[]{:S(2)}) collective-permute-start(bf16[1152,128]{1,0:T(8,128)(2,1)} %get-tuple-element.86.refs_6_), channel_id=1, source_target_pairs={{0,2},{2,0},{4,6},{6,4},{8,10},{10,8},{12,14},{14,12},{16,18},{18,... | collective-permute-start | bytes 884744 | tf_op jit(solution)/shard_map/ppermute | solution.py:351
  103.8 29.9 %collective-permute-start.23 = (bf16[1184,128]{1,0:T(8,128)(2,1)S(1)}, bf16[1184,128]{1,0:T(8,128)(2,1)S(1)}, u32[]{:S(2)}, u32[]{:S(2)}) collective-permute-start(bf16[1184,128]{1,0:T(8,128)(2,1)S(1)} %collective-permute-done.17.near_after.refs_4_), channel_id=1, source_target_pairs={{8,0},{16,8},{9,1},{17,9},{10,2},{18,10},{11,3},{19,11},{12,4},{20... | collective-permute-start | bytes 909320 | tf_op jit(solution)/shard_map/ppermute | solution.py:353
  112.2 21.5 %collective-permute-start.22 = (bf16[1184,128]{1,0:T(8,128)(2,1)S(1)}, bf16[1184,128]{1,0:T(8,128)(2,1)S(1)}, u32[]{:S(2)}, u32[]{:S(2)}) collective-permute-start(bf16[1184,128]{1,0:T(8,128)(2,1)S(1)} %collective-permute-done.16.near_before.refs_3_), channel_id=1, source_target_pairs={{8,16},{16,24},{9,17},{17,25},{10,18},{18,26},{11,19},{19,27},{12,... | collective-permute-start | bytes 909320 | tf_op jit(solution)/shard_map/ppermute | solution.py:352
  116.4 15.0 %collective-permute-start.25 = (bf16[1152,128]{1,0:T(8,128)(2,1)S(1)}, bf16[1152,128]{1,0:T(8,128)(2,1)S(1)}, u32[]{:S(2)}, u32[]{:S(2)}) collective-permute-start(bf16[1152,128]{1,0:T(8,128)(2,1)S(1)} %collective-permute-done.20.far_after), channel_id=1, source_target_pairs={{8,0},{16,8},{9,1},{17,9},{10,2},{18,10},{11,3},{19,11},{12,4},{20... | collective-permute-start | bytes 884744 | tf_op jit(solution)/shard_map/ppermute | solution.py:353
  117.7 13.7 %collective-permute-start.24 = (bf16[1152,128]{1,0:T(8,128)(2,1)S(1)}, bf16[1152,128]{1,0:T(8,128)(2,1)S(1)}, u32[]{:S(2)}, u32[]{:S(2)}) collective-permute-start(bf16[1152,128]{1,0:T(8,128)(2,1)S(1)} %collective-permute-done.19.far_before), channel_id=1, source_target_pairs={{8,16},{16,24},{9,17},{17,25},{10,18},{18,26},{11,19},{19,27},{12,... | collective-permute-start | bytes 884744 | tf_op jit(solution)/shard_map/ppermute | solution.py:352
  118.4 20.4 %collective-permute-start.29 = (bf16[192,128]{1,0:T(8,128)(2,1)}, bf16[192,128]{1,0:T(8,128)(2,1)S(1)}, u32[]{:S(2)}, u32[]{:S(2)}) collective-permute-start(bf16[192,128]{1,0:T(8,128)(2,1)} %get-tuple-element.97), channel_id=1, source_target_pairs={{0,8},{8,16},{16,24},{24,0},{1,9},{9,17},{17,25},{25,1},{2,10},{10... | collective-permute-start | bytes 147464 | tf_op jit(solution)/shard_map/ppermute | solution.py:457
  138.9 14.0 %collective-permute-start.32 = (bf16[2,1152,128]{2,1,0:T(8,128)(2,1)S(1)}, bf16[2,1152,128]{2,1,0:T(8,128)(2,1)S(1)}, u32[]{:S(2)}, u32[]{:S(2)}) collective-permute-start(bf16[2,1152,128]{2,1,0:T(8,128)(2,1)S(1)} %get-tuple-element.100), channel_id=1, source_target_pairs={{0,2},{2,0},{4,6},{6,4},{1,3},{3,1},{5,7},{7,5},{8,10},{10,8},{12,... | collective-permute-start | bytes 1769480 | tf_op jit(solution)/shard_map/ppermute | solution.py:496
  141.5 10.3 %collective-permute-start.28 = (bf16[192,512]{1,0:T(8,128)(2,1)}, bf16[192,512]{1,0:T(8,128)(2,1)S(1)}, u32[]{:S(2)}, u32[]{:S(2)}) collective-permute-start(bf16[192,512]{1,0:T(8,128)(2,1)} %get-tuple-element.94), channel_id=1, source_target_pairs={{5,0},{4,1},{7,2},{6,3},{1,4},{0,5},{3,6},{2,7},{13,8},{12,9},{15,... | collective-permute-start | bytes 589832 | tf_op jit(solution)/shard_map/ppermute | solution.py:498
  142.7 10.2 %collective-permute-start.33 = (bf16[1152,128]{1,0:T(8,128)(2,1)}, bf16[1152,128]{1,0:T(8,128)(2,1)S(1)}, u32[]{:S(2)}, u32[]{:S(2)}) collective-permute-start(bf16[1152,128]{1,0:T(8,128)(2,1)} %get-tuple-element.101), channel_id=1, source_target_pairs={{0,2},{2,0},{4,6},{6,4},{1,3},{3,1},{5,7},{7,5},{8,10},{10,8},{12,... | collective-permute-start | bytes 884744 | tf_op jit(solution)/shard_map/ppermute | solution.py:496
  152.9 11.2 %collective-permute-start.34 = (bf16[192,512]{1,0:T(8,128)(2,1)S(1)}, bf16[192,512]{1,0:T(8,128)(2,1)S(1)}, u32[]{:S(2)}, u32[]{:S(2)}) collective-permute-start(bf16[192,512]{1,0:T(8,128)(2,1)S(1)} %add_convert_fusion), channel_id=1, source_target_pairs={{0,0},{2,16},{4,8},{6,24},{8,2},{10,18},{12,10},{14,26},{16,4},{18... | collective-permute-start | bytes 589832 | tf_op jit(solution)/shard_map/ppermute | solution.py:503
  (41 other events, 397.2 us)

commit v22 on v16

--- a/solution.py
+++ b/solution.py
@@ -473,6 +473,7 @@
         ],
         flops=2 * mm_flops,
         nbytes=2 * mm_bytes,
+        vmem=MOST_VMEM_BYTES,
     )(*near, *far, w, partner_w)
     near_last, far_last, *blocks = kernel_call(
         functools.partial(second_grad_body, ndp),

time: 163 us -> 163 us (level)
  Pallas kernels: 31.3 us -> 33.5 us
  local copies, waits for them, and re-layouts: 8.81 us -> 6.99 us
    pallas_call x1, Pallas kernels: 4.63 us -> 6.81 us  [move_activations(): kernel_call(first_grad_body, [shaped((ncol, chunk, dcol), BF16), shaped((...]
    unnamed x61 -> x55, local copies, waits for them, and re-layouts: 8.13 us -> 6.3 us
  transfers between devices with their start and end apart: 35 -> 35, of which waited for: 17 -> 17; matrix products, arithmetic and copies ran while one was open for 2% -> 2% of each run, Pallas kernels for 19% -> 21%
where the time goes in v22:
time: 163 us; the launch traced here: 162 us
  waiting for transfers between devices  59.9 us (37%)
  starting transfers between devices  58.4 us (36%)
  Pallas kernels  33.5 us (21%)
  local copies, waits for them, and re-layouts  6.99 us (4%)
  other arithmetic  2.19 us (1%)
    ppermute x2, waiting for transfers between devices, gather_over_line(): before = lax.ppermute(own, ('dp', 'row'), shift(1))  10.4 us
    ppermute x2, waiting for transfers between devices, gather_over_line(): after = lax.ppermute(own, ('dp', 'row'), shift(-1))  10.1 us
    ppermute x2, waiting for transfers between devices, sum_over_line(): lax.ppermute(right + from_left, 'dp', [(a, (a + 1) % ndp) for a in range(...  8.37 us
    ppermute x3, waiting for transfers between devices, move_activations(): lax.ppermute(sent, ('row', 'col'), [(b, a) for a, b in offset(*p)])  8.23 us
    pallas_call x2, Pallas kernels, move_activations(): kernel_call(project_body, [shaped((3, chunk, width), BF16)] * ndp, grid=(...  8.1 us
    ppermute x3, starting transfers between devices, move_activations(): lax.ppermute(part, 'dp', [(a, (a + ahead) % ndp) for a in range(ndp)])  7.23 us
    pallas_call x1, Pallas kernels, move_activations(): kernel_call(functools.partial(weight_grad_body, scale), [shaped((3, drow,...  7.05 us
    pallas_call x1, Pallas kernels, move_activations(): kernel_call(first_grad_body, [shaped((ncol, chunk, dcol), BF16), shaped((...  6.81 us
  transfers between devices with their start and end apart: 35, of which 17 were waited for; matrix products, arithmetic and copies ran while one was open for 2% of the time, Pallas kernels for 21%

profile of v22, /device:TPU:1, one launch (start us, length us, event | category | flops | bytes accessed | tf_op | source)
XLA Modules:
  0.0 162.1 jit_solution(2324557279247726147)
XLA Ops:
  0.6 4.6 %collective-permute-start = (bf16[192,512]{1,0:T(8,128)(2,1)}, bf16[192,512]{1,0:T(8,128)(2,1)S(1)}, u32[]{:S(2)}, u32[]{:S(2)}) collective-permute-start(bf16[192,512]{1,0:T(8,128)(2,1)} %param.5), channel_id=1, source_target_pairs={{0,0},{16,2},{8,4},{24,6},{2,8},{18,10},{10,12},{26,14},{4,16},{20... | collective-permute-start | bytes 589832 | tf_op jit(solution)/shard_map/ppermute | solution.py:380
  8.9 6.5 %collective-permute-done = bf16[192,512]{1,0:T(8,128)(2,1)S(1)} collective-permute-done((bf16[192,512]{1,0:T(8,128)(2,1)}, bf16[192,512]{1,0:T(8,128)(2,1)S(1)}, u32[]{:S(2)}, u32[]{:S(2)}) %collective-permute-start) | collective-permute-done | bytes 196640 | tf_op jit(solution)/shard_map/ppermute | solution.py:380
  15.4 2.7 %collective-permute-start.4 = (bf16[192,512]{1,0:T(8,128)(2,1)S(1)}, bf16[192,512]{1,0:T(8,128)(2,1)S(1)}, u32[]{:S(2)}, u32[]{:S(2)}) collective-permute-start(bf16[192,512]{1,0:T(8,128)(2,1)S(1)} %collective-permute-done), channel_id=1, source_target_pairs={{0,4},{1,5},{2,6},{3,7},{4,0},{5,1},{6,2},{7,3},{8,12},{9,13},{10,... | collective-permute-start | bytes 589832 | tf_op jit(solution)/shard_map/ppermute | solution.py:391
  25.1 4.0 %shard_map.94 = (bf16[3,384,128]{2,1,0:T(8,128)(2,1)S(1)}, bf16[3,384,128]{2,1,0:T(8,128)(2,1)S(1)}, bf16[3,384,128]{2,1,0:T(8,128)(2,1)S(1)}, bf16[3,384,128]{2,1,0:T(8,128)(2,1)S(1)}) custom-call(bf16[2,2,192,512]{3,2,1,0:T(8,128)(2,1)S(1)} %bitcast.20, bf16[3,1024,512]{2,1,0:T(8,128)(2,1)} %bitcast.w_ref), custom_call_target="tpu_custom_call" | custom-call | flops 1207959552 | bytes 5111808 | tf_op jit(solution)/shard_map/pallas_call | solution.py:416
  30.1 6.5 %collective-permute-start.6 = (bf16[192,128]{1,0:T(8,128)(2,1)S(1)}, bf16[192,128]{1,0:T(8,128)(2,1)S(1)}, u32[]{:S(2)}, u32[]{:S(2)}) collective-permute-start(bf16[192,128]{1,0:T(8,128)(2,1)S(1)} %get-tuple-element.66), channel_id=1, source_target_pairs={{0,16},{8,24},{16,0},{24,8},{1,17},{9,25},{17,1},{25,9},{2,18},{10... | collective-permute-start | bytes 147464 | tf_op jit(solution)/shard_map/ppermute | solution.py:397
  40.6 4.1 %collective-permute-done.6.refs_11_ = bf16[192,128]{1,0:T(8,128)(2,1)S(1)} collective-permute-done((bf16[192,128]{1,0:T(8,128)(2,1)S(1)}, bf16[192,128]{1,0:T(8,128)(2,1)S(1)}, u32[]{:S(2)}, u32[]{:S(2)}) %collective-permute-start.6) | collective-permute-done | bytes 49184 | tf_op jit(solution)/shard_map/ppermute | solution.py:397
  45.4 4.1 %shard_map.95 = (bf16[3,384,128]{2,1,0:T(8,128)(2,1)S(1)}, bf16[3,384,128]{2,1,0:T(8,128)(2,1)S(1)}, bf16[3,384,128]{2,1,0:T(8,128)(2,1)S(1)}, bf16[3,384,128]{2,1,0:T(8,128)(2,1)S(1)}) custom-call(bf16[2,2,192,512]{3,2,1,0:T(8,128)(2,1)S(1)} %collective-permute-done.7.x_ref.refs_1_, bf16[3,1024,512]{2,1,0:T(8,128)(2,1)} %bitcast.w_ref), custom_call_target="tpu_custom_call" | custom-call | flops 1207959552 | bytes 5111808 | tf_op jit(solution)/shard_map/pallas_call | solution.py:416
  50.6 4.0 %collective-permute-start.12 = (bf16[1152,128]{1,0:T(8,128)(2,1)S(1)}, bf16[1152,128]{1,0:T(8,128)(2,1)S(1)}, u32[]{:S(2)}, u32[]{:S(2)}) collective-permute-start(bf16[1152,128]{1,0:T(8,128)(2,1)S(1)} %bitcast.25), channel_id=1, source_target_pairs={{0,8},{8,16},{1,9},{9,17},{2,10},{10,18},{3,11},{11,19},{4,12},{12... | collective-permute-start | bytes 884744 | tf_op jit(solution)/shard_map/ppermute | solution.py:331
  54.7 3.3 %collective-permute-start.15 = (bf16[1152,128]{1,0:T(8,128)(2,1)S(1)}, bf16[1152,128]{1,0:T(8,128)(2,1)S(1)}, u32[]{:S(2)}, u32[]{:S(2)}) collective-permute-start(bf16[1152,128]{1,0:T(8,128)(2,1)S(1)} %bitcast_add_fusion), channel_id=1, source_target_pairs={{0,24},{8,0},{16,8},{24,16},{1,25},{9,1},{17,9},{25,17},{2,26},{10... | collective-permute-start | bytes 884744 | tf_op jit(solution)/shard_map/ppermute | solution.py:334
  58.0 3.7 %collective-permute-done.12 = bf16[1152,128]{1,0:T(8,128)(2,1)S(1)} collective-permute-done((bf16[1152,128]{1,0:T(8,128)(2,1)S(1)}, bf16[1152,128]{1,0:T(8,128)(2,1)S(1)}, u32[]{:S(2)}, u32[]{:S(2)}) %collective-permute-start.12) | collective-permute-done | bytes 294944 | tf_op jit(solution)/shard_map/ppermute | solution.py:331
  69.3 8.4 %collective-permute-done.13.refs_4_ = bf16[1152,128]{1,0:T(8,128)(2,1)S(1)} collective-permute-done((bf16[1152,128]{1,0:T(8,128)(2,1)S(1)}, bf16[1152,128]{1,0:T(8,128)(2,1)S(1)}, u32[]{:S(2)}, u32[]{:S(2)}) %collective-permute-start.13) | collective-permute-done | bytes 294944 | tf_op jit(solution)/shard_map/ppermute | solution.py:333
  78.4 5.4 %shard_map.97 = (bf16[1184,128]{1,0:T(8,128)(2,1)}, bf16[1152,128]{1,0:T(8,128)(2,1)}, bf16[192,128]{1,0:T(8,128)(2,1)}, bf16[192,128]{1,0:T(8,128)(2,1)}, bf16[...) custom-call(bf16[1152,128]{1,0:T(8,128)(2,1)} %bitcast.26, bf16[1152,128]{1,0:T(8,128)(2,1)} %copy-done.15, ...), custom_call_target="tpu_custom_call" | custom-call | flops 1207959552 | bytes 2752512 | tf_op jit(solution)/shard_map/pallas_call | solution.py:435
  83.8 3.6 %collective-permute-start.20 = (bf16[1152,128]{1,0:T(8,128)(2,1)}, bf16[1152,128]{1,0:T(8,128)(2,1)}, u32[]{:S(2)}, u32[]{:S(2)}) collective-permute-start(bf16[1152,128]{1,0:T(8,128)(2,1)} %get-tuple-element.81.refs_6_), channel_id=1, source_target_pairs={{0,26},{2,24},{4,30},{6,28},{8,2},{10,0},{12,6},{14,4},{16,10},{18... | collective-permute-start | bytes 884744 | tf_op jit(solution)/shard_map/ppermute | solution.py:349
  89.2 5.4 %collective-permute-done.20.far_after = bf16[1152,128]{1,0:T(8,128)(2,1)} collective-permute-done((bf16[1152,128]{1,0:T(8,128)(2,1)}, bf16[1152,128]{1,0:T(8,128)(2,1)}, u32[]{:S(2)}, u32[]{:S(2)}) %collective-permute-start.20) | collective-permute-done | bytes 294944 | tf_op jit(solution)/shard_map/ppermute | solution.py:349
  96.3 4.8 %collective-permute-done.17.near_after.refs_4_ = bf16[1184,128]{1,0:T(8,128)(2,1)} collective-permute-done((bf16[1184,128]{1,0:T(8,128)(2,1)}, bf16[1184,128]{1,0:T(8,128)(2,1)}, u32[]{:S(2)}, u32[]{:S(2)}) %collective-permute-start.17) | collective-permute-done | bytes 303136 | tf_op jit(solution)/shard_map/ppermute | solution.py:349
  102.3 7.6 %collective-permute-done.16.near_before.refs_3_ = bf16[1184,128]{1,0:T(8,128)(2,1)} collective-permute-done((bf16[1184,128]{1,0:T(8,128)(2,1)}, bf16[1184,128]{1,0:T(8,128)(2,1)}, u32[]{:S(2)}, u32[]{:S(2)}) %collective-permute-start.16) | collective-permute-done | bytes 303136 | tf_op jit(solution)/shard_map/ppermute | solution.py:348
  110.6 2.8 %collective-permute-done.19.far_before = bf16[1152,128]{1,0:T(8,128)(2,1)} collective-permute-done((bf16[1152,128]{1,0:T(8,128)(2,1)}, bf16[1152,128]{1,0:T(8,128)(2,1)}, u32[]{:S(2)}, u32[]{:S(2)}) %collective-permute-start.19) | collective-permute-done | bytes 294944 | tf_op jit(solution)/shard_map/ppermute | solution.py:348
  115.5 4.8 %collective-permute-start.29 = (bf16[192,128]{1,0:T(8,128)(2,1)}, bf16[192,128]{1,0:T(8,128)(2,1)S(1)}, u32[]{:S(2)}, u32[]{:S(2)}) collective-permute-start(bf16[192,128]{1,0:T(8,128)(2,1)} %get-tuple-element.91), channel_id=1, source_target_pairs={{0,8},{8,16},{16,24},{24,0},{1,9},{9,17},{17,25},{25,1},{2,10},{10... | collective-permute-start | bytes 147464 | tf_op jit(solution)/shard_map/ppermute | solution.py:455
  120.3 6.8 %shard_map.98 = (bf16[2,384,512]{2,1,0:T(8,128)(2,1)}, bf16[2,1152,128]{2,1,0:T(8,128)(2,1)}) custom-call(bf16[1184,128]{1,0:T(8,128)(2,1)} %get-tuple-element.80.near.refs_2_, bf16[1184,128]{1,0:T(8,128)(2,1)} %collective-permute-done.16.near_before.refs_3_, bf16[1184,128]{1,0:T(8,128)(2,1)} %collective-permute-done.17.near_after.refs_4_, ...), custom_call_target="tpu_custom_call" | custom-call | flops 2415919104 | bytes 10223616 | tf_op jit(solution)/shard_map/pallas_call | solution.py:464
  131.8 4.3 %shard_map.99 = (bf16[1184,128]{1,0:T(8,128)(2,1)}, bf16[1152,128]{1,0:T(8,128)(2,1)}, bf16[192,512]{1,0:T(8,128)(2,1)}, bf16[192,512]{1,0:T(8,128)(2,1)}, bf16[...) custom-call(bf16[2,384,512]{2,1,0:T(8,128)(2,1)} %get-tuple-element.82.part_ref, bf16[1184,128]{1,0:T(8,128)(2,1)} %copy-done.10, ...), custom_call_target="tpu_custom_call" | custom-call | flops 603979776 | bytes 2555904 | tf_op jit(solution)/shard_map/pallas_call | solution.py:478
  140.9 3.1 %collective-permute-done.26 = bf16[192,512]{1,0:T(8,128)(2,1)S(1)} collective-permute-done((bf16[192,512]{1,0:T(8,128)(2,1)}, bf16[192,512]{1,0:T(8,128)(2,1)S(1)}, u32[]{:S(2)}, u32[]{:S(2)}) %collective-permute-start.26) | collective-permute-done | bytes 196640 | tf_op jit(solution)/shard_map/ppermute | solution.py:497
  144.9 4.2 %collective-permute-done.28 = bf16[192,512]{1,0:T(8,128)(2,1)S(1)} collective-permute-done((bf16[192,512]{1,0:T(8,128)(2,1)}, bf16[192,512]{1,0:T(8,128)(2,1)S(1)}, u32[]{:S(2)}, u32[]{:S(2)}) %collective-permute-start.28) | collective-permute-done | bytes 196640 | tf_op jit(solution)/shard_map/ppermute | solution.py:497
  150.2 2.7 %collective-permute-start.34 = (bf16[192,512]{1,0:T(8,128)(2,1)S(1)}, bf16[192,512]{1,0:T(8,128)(2,1)S(1)}, u32[]{:S(2)}, u32[]{:S(2)}) collective-permute-start(bf16[192,512]{1,0:T(8,128)(2,1)S(1)} %add_convert_fusion), channel_id=1, source_target_pairs={{0,0},{2,16},{4,8},{6,24},{8,2},{10,18},{12,10},{14,26},{16,4},{18... | collective-permute-start | bytes 589832 | tf_op jit(solution)/shard_map/ppermute | solution.py:502
  153.0 7.1 %shard_map.100 = (f32[3,1024,512]{2,1,0:T(8,128)}, bf16[192,512]{1,0:T(8,128)(2,1)}, f32[32,128]{1,0:T(8,128)}, f32[3,3,512]{2,1,0:T(4,128)}) custom-call(bf16[2,2,192,512]{3,2,1,0:T(8,128)(2,1)} %bitcast.21, bf16[2,2,192,512]{3,2,1,0:T(8,128)(2,1)} %copy-done.5, bf16[1184,128]{1,0:T(8,128)(2,1)} %get-tuple-element.80.near.refs_2_, ...), custom_call_target="tpu_custom_call" | custom-call | flops 2415919104 | bytes 10223616 | tf_op jit(solution)/shard_map/pallas_call | solution.py:504
  (123 shorter events, 46.5 us)
Async XLA Ops:
  0.6 14.8 %collective-permute-start = (bf16[192,512]{1,0:T(8,128)(2,1)}, bf16[192,512]{1,0:T(8,128)(2,1)S(1)}, u32[]{:S(2)}, u32[]{:S(2)}) collective-permute-start(bf16[192,512]{1,0:T(8,128)(2,1)} %param.5), channel_id=1, source_target_pairs={{0,0},{16,2},{8,4},{24,6},{2,8},{18,10},{10,12},{26,14},{4,16},{20... | collective-permute-start | bytes 589832 | tf_op jit(solution)/shard_map/ppermute | solution.py:380
  25.0 20.4 %collective-permute-start.7 = (bf16[2,2,192,512]{3,2,1,0:T(8,128)(2,1)S(1)}, bf16[2,2,192,512]{3,2,1,0:T(8,128)(2,1)S(1)}, u32[]{:S(2)}, u32[]{:S(2)}) collective-permute-start(bf16[2,2,192,512]{3,2,1,0:T(8,128)(2,1)S(1)} %bitcast.19), channel_id=1, source_target_pairs={{0,2},{2,0},{4,6},{6,4},{1,3},{3,1},{5,7},{7,5},{8,10},{10,8},{12,... | collective-permute-start | bytes 2359304 | tf_op jit(solution)/shard_map/ppermute | solution.py:396
  29.8 85.7 %collective-permute-start.21 = (bf16[3,1024,512]{2,1,0:T(8,128)(2,1)}, bf16[3,1024,512]{2,1,0:T(8,128)(2,1)}, u32[]{:S(2)}, u32[]{:S(2)}) collective-permute-start(bf16[3,1024,512]{2,1,0:T(8,128)(2,1)} %bitcast.w_ref), channel_id=1, source_target_pairs={{0,2},{2,0},{4,6},{6,4},{1,3},{3,1},{5,7},{7,5},{8,10},{10,8},{12,... | collective-permute-start | bytes 9437192 | tf_op jit(solution)/shard_map/ppermute | solution.py:461
  30.1 14.6 %collective-permute-start.6 = (bf16[192,128]{1,0:T(8,128)(2,1)S(1)}, bf16[192,128]{1,0:T(8,128)(2,1)S(1)}, u32[]{:S(2)}, u32[]{:S(2)}) collective-permute-start(bf16[192,128]{1,0:T(8,128)(2,1)S(1)} %get-tuple-element.66), channel_id=1, source_target_pairs={{0,16},{8,24},{16,0},{24,8},{1,17},{9,25},{17,1},{25,9},{2,18},{10... | collective-permute-start | bytes 147464 | tf_op jit(solution)/shard_map/ppermute | solution.py:397
  36.6 13.6 %collective-permute-start.8 = (bf16[1152,128]{1,0:T(8,128)(2,1)S(1)}, bf16[1152,128]{1,0:T(8,128)(2,1)S(1)}, u32[]{:S(2)}, u32[]{:S(2)}) collective-permute-start(bf16[1152,128]{1,0:T(8,128)(2,1)S(1)} %bitcast.23), channel_id=1, source_target_pairs={{0,8},{8,16},{1,9},{9,17},{2,10},{10,18},{3,11},{11,19},{4,12},{12... | collective-permute-start | bytes 884744 | tf_op jit(solution)/shard_map/ppermute | solution.py:331
  38.0 29.1 %collective-permute-start.11 = (bf16[1152,128]{1,0:T(8,128)(2,1)S(1)}, bf16[1152,128]{1,0:T(8,128)(2,1)}, u32[]{:S(2)}, u32[]{:S(2)}) collective-permute-start(bf16[1152,128]{1,0:T(8,128)(2,1)S(1)} %bitcast_add_fusion.2), channel_id=1, source_target_pairs={{0,24},{8,0},{16,8},{24,16},{1,25},{9,1},{17,9},{25,17},{2,26},{10... | collective-permute-start | bytes 884744 | tf_op jit(solution)/shard_map/ppermute | solution.py:334
  50.3 16.9 %collective-permute-start.9 = (bf16[1152,128]{1,0:T(8,128)(2,1)S(1)}, bf16[1152,128]{1,0:T(8,128)(2,1)S(1)}, u32[]{:S(2)}, u32[]{:S(2)}) collective-permute-start(bf16[1152,128]{1,0:T(8,128)(2,1)S(1)} %bitcast_add_fusion.3), channel_id=1, source_target_pairs={{0,8},{8,16},{16,24},{24,0},{1,9},{9,17},{17,25},{25,1},{2,10},{10... | collective-permute-start | bytes 884744 | tf_op jit(solution)/shard_map/ppermute | solution.py:333
  50.6 11.1 %collective-permute-start.12 = (bf16[1152,128]{1,0:T(8,128)(2,1)S(1)}, bf16[1152,128]{1,0:T(8,128)(2,1)S(1)}, u32[]{:S(2)}, u32[]{:S(2)}) collective-permute-start(bf16[1152,128]{1,0:T(8,128)(2,1)S(1)} %bitcast.25), channel_id=1, source_target_pairs={{0,8},{8,16},{1,9},{9,17},{2,10},{10,18},{3,11},{11,19},{4,12},{12... | collective-permute-start | bytes 884744 | tf_op jit(solution)/shard_map/ppermute | solution.py:331
  54.7 14.6 %collective-permute-start.15 = (bf16[1152,128]{1,0:T(8,128)(2,1)S(1)}, bf16[1152,128]{1,0:T(8,128)(2,1)S(1)}, u32[]{:S(2)}, u32[]{:S(2)}) collective-permute-start(bf16[1152,128]{1,0:T(8,128)(2,1)S(1)} %bitcast_add_fusion), channel_id=1, source_target_pairs={{0,24},{8,0},{16,8},{24,16},{1,25},{9,1},{17,9},{25,17},{2,26},{10... | collective-permute-start | bytes 884744 | tf_op jit(solution)/shard_map/ppermute | solution.py:334
  61.8 15.9 %collective-permute-start.13 = (bf16[1152,128]{1,0:T(8,128)(2,1)S(1)}, bf16[1152,128]{1,0:T(8,128)(2,1)S(1)}, u32[]{:S(2)}, u32[]{:S(2)}) collective-permute-start(bf16[1152,128]{1,0:T(8,128)(2,1)S(1)} %bitcast_add_fusion.1), channel_id=1, source_target_pairs={{0,8},{8,16},{16,24},{24,0},{1,9},{9,17},{17,25},{25,1},{2,10},{10... | collective-permute-start | bytes 884744 | tf_op jit(solution)/shard_map/ppermute | solution.py:333
  83.8 10.8 %collective-permute-start.20 = (bf16[1152,128]{1,0:T(8,128)(2,1)}, bf16[1152,128]{1,0:T(8,128)(2,1)}, u32[]{:S(2)}, u32[]{:S(2)}) collective-permute-start(bf16[1152,128]{1,0:T(8,128)(2,1)} %get-tuple-element.81.refs_6_), channel_id=1, source_target_pairs={{0,26},{2,24},{4,30},{6,28},{8,2},{10,0},{12,6},{14,4},{16,10},{18... | collective-permute-start | bytes 884744 | tf_op jit(solution)/shard_map/ppermute | solution.py:349
  87.4 13.6 %collective-permute-start.17 = (bf16[1184,128]{1,0:T(8,128)(2,1)}, bf16[1184,128]{1,0:T(8,128)(2,1)}, u32[]{:S(2)}, u32[]{:S(2)}) collective-permute-start(bf16[1184,128]{1,0:T(8,128)(2,1)} %get-tuple-element.80.near.refs_2_), channel_id=1, source_target_pairs={{0,24},{2,26},{4,28},{6,30},{8,0},{10,2},{12,4},{14,6},{16,8},{18,... | collective-permute-start | bytes 909320 | tf_op jit(solution)/shard_map/ppermute | solution.py:349
  89.2 20.8 %collective-permute-start.16 = (bf16[1184,128]{1,0:T(8,128)(2,1)}, bf16[1184,128]{1,0:T(8,128)(2,1)}, u32[]{:S(2)}, u32[]{:S(2)}) collective-permute-start(bf16[1184,128]{1,0:T(8,128)(2,1)} %get-tuple-element.80.near.refs_2_), channel_id=1, source_target_pairs={{0,8},{2,10},{4,12},{6,14},{8,16},{10,18},{12,20},{14,22},{16,24},... | collective-permute-start | bytes 909320 | tf_op jit(solution)/shard_map/ppermute | solution.py:348
  89.2 24.3 %collective-permute-start.19 = (bf16[1152,128]{1,0:T(8,128)(2,1)}, bf16[1152,128]{1,0:T(8,128)(2,1)}, u32[]{:S(2)}, u32[]{:S(2)}) collective-permute-start(bf16[1152,128]{1,0:T(8,128)(2,1)} %get-tuple-element.81.refs_6_), channel_id=1, source_target_pairs={{0,10},{2,8},{4,14},{6,12},{8,18},{10,16},{12,22},{14,20},{16,26},... | collective-permute-start | bytes 884744 | tf_op jit(solution)/shard_map/ppermute | solution.py:348
  94.5 20.2 %collective-permute-start.18 = (bf16[1152,128]{1,0:T(8,128)(2,1)}, bf16[1152,128]{1,0:T(8,128)(2,1)S(1)}, u32[]{:S(2)}, u32[]{:S(2)}) collective-permute-start(bf16[1152,128]{1,0:T(8,128)(2,1)} %get-tuple-element.81.refs_6_), channel_id=1, source_target_pairs={{0,2},{2,0},{4,6},{6,4},{8,10},{10,8},{12,14},{14,12},{16,18},{18,... | collective-permute-start | bytes 884744 | tf_op jit(solution)/shard_map/ppermute | solution.py:350
  101.0 30.0 %collective-permute-start.23 = (bf16[1184,128]{1,0:T(8,128)(2,1)}, bf16[1184,128]{1,0:T(8,128)(2,1)S(1)}, u32[]{:S(2)}, u32[]{:S(2)}) collective-permute-start(bf16[1184,128]{1,0:T(8,128)(2,1)} %collective-permute-done.17.near_after.refs_4_), channel_id=1, source_target_pairs={{8,0},{16,8},{9,1},{17,9},{10,2},{18,10},{11,3},{19,11},{12,4},{20... | collective-permute-start | bytes 909320 | tf_op jit(solution)/shard_map/ppermute | solution.py:352
  109.9 21.1 %collective-permute-start.22 = (bf16[1184,128]{1,0:T(8,128)(2,1)}, bf16[1184,128]{1,0:T(8,128)(2,1)S(1)}, u32[]{:S(2)}, u32[]{:S(2)}) collective-permute-start(bf16[1184,128]{1,0:T(8,128)(2,1)} %collective-permute-done.16.near_before.refs_3_), channel_id=1, source_target_pairs={{8,16},{16,24},{9,17},{17,25},{10,18},{18,26},{11,19},{19,27},{12,... | collective-permute-start | bytes 909320 | tf_op jit(solution)/shard_map/ppermute | solution.py:351
  113.5 15.1 %collective-permute-start.25 = (bf16[1152,128]{1,0:T(8,128)(2,1)}, bf16[1152,128]{1,0:T(8,128)(2,1)S(1)}, u32[]{:S(2)}, u32[]{:S(2)}) collective-permute-start(bf16[1152,128]{1,0:T(8,128)(2,1)} %collective-permute-done.20.far_after), channel_id=1, source_target_pairs={{8,0},{16,8},{9,1},{17,9},{10,2},{18,10},{11,3},{19,11},{12,4},{20... | collective-permute-start | bytes 884744 | tf_op jit(solution)/shard_map/ppermute | solution.py:352
  114.8 13.8 %collective-permute-start.24 = (bf16[1152,128]{1,0:T(8,128)(2,1)}, bf16[1152,128]{1,0:T(8,128)(2,1)S(1)}, u32[]{:S(2)}, u32[]{:S(2)}) collective-permute-start(bf16[1152,128]{1,0:T(8,128)(2,1)} %collective-permute-done.19.far_before), channel_id=1, source_target_pairs={{8,16},{16,24},{9,17},{17,25},{10,18},{18,26},{11,19},{19,27},{12,... | collective-permute-start | bytes 884744 | tf_op jit(solution)/shard_map/ppermute | solution.py:351
  115.5 20.7 %collective-permute-start.29 = (bf16[192,128]{1,0:T(8,128)(2,1)}, bf16[192,128]{1,0:T(8,128)(2,1)S(1)}, u32[]{:S(2)}, u32[]{:S(2)}) collective-permute-start(bf16[192,128]{1,0:T(8,128)(2,1)} %get-tuple-element.91), channel_id=1, source_target_pairs={{0,8},{8,16},{16,24},{24,0},{1,9},{9,17},{17,25},{25,1},{2,10},{10... | collective-permute-start | bytes 147464 | tf_op jit(solution)/shard_map/ppermute | solution.py:455
  136.2 14.0 %collective-permute-start.32 = (bf16[2,1152,128]{2,1,0:T(8,128)(2,1)S(1)}, bf16[2,1152,128]{2,1,0:T(8,128)(2,1)S(1)}, u32[]{:S(2)}, u32[]{:S(2)}) collective-permute-start(bf16[2,1152,128]{2,1,0:T(8,128)(2,1)S(1)} %copy-done.13), channel_id=1, source_target_pairs={{0,2},{2,0},{4,6},{6,4},{1,3},{3,1},{5,7},{7,5},{8,10},{10,8},{12,... | collective-permute-start | bytes 1769480 | tf_op jit(solution)/shard_map/ppermute | solution.py:495
  138.5 10.6 %collective-permute-start.28 = (bf16[192,512]{1,0:T(8,128)(2,1)}, bf16[192,512]{1,0:T(8,128)(2,1)S(1)}, u32[]{:S(2)}, u32[]{:S(2)}) collective-permute-start(bf16[192,512]{1,0:T(8,128)(2,1)} %get-tuple-element.88), channel_id=1, source_target_pairs={{5,0},{4,1},{7,2},{6,3},{1,4},{0,5},{3,6},{2,7},{13,8},{12,9},{15,... | collective-permute-start | bytes 589832 | tf_op jit(solution)/shard_map/ppermute | solution.py:497
  140.0 10.2 %collective-permute-start.33 = (bf16[1152,128]{1,0:T(8,128)(2,1)}, bf16[1152,128]{1,0:T(8,128)(2,1)S(1)}, u32[]{:S(2)}, u32[]{:S(2)}) collective-permute-start(bf16[1152,128]{1,0:T(8,128)(2,1)} %get-tuple-element.95), channel_id=1, source_target_pairs={{0,2},{2,0},{4,6},{6,4},{1,3},{3,1},{5,7},{7,5},{8,10},{10,8},{12,... | collective-permute-start | bytes 884744 | tf_op jit(solution)/shard_map/ppermute | solution.py:495
  150.2 11.2 %collective-permute-start.34 = (bf16[192,512]{1,0:T(8,128)(2,1)S(1)}, bf16[192,512]{1,0:T(8,128)(2,1)S(1)}, u32[]{:S(2)}, u32[]{:S(2)}) collective-permute-start(bf16[192,512]{1,0:T(8,128)(2,1)S(1)} %add_convert_fusion), channel_id=1, source_target_pairs={{0,0},{2,16},{4,8},{6,24},{8,2},{10,18},{12,10},{14,26},{16,4},{18... | collective-permute-start | bytes 589832 | tf_op jit(solution)/shard_map/ppermute | solution.py:502
  (38 other events, 352.0 us)
